TPU v7x, 32 devices: a whole 2x2x4 slice. The times are simulated.
32 devices in a mesh: dp: 2 (over core), tm: 4 (over z), space: 4 (over y, x).
Axes of the slice: x: 2, y: 2, z: 4, core: 2. Of those that a mesh axis runs over, the one named last changes fastest.
Arguments:
- patches: bfloat16 [2, 8, 256, 1152], P('dp', 'tm', 'space'), may hold values from -4 to 4
- query_s: bfloat16 [2, 8, 256, 1152], P('dp', 'tm', 'space'), may hold values from -8 to 8
- key_s: bfloat16 [2, 8, 256, 1152], P('dp', 'tm', 'space'), may hold values from -8 to 8
- value_s: bfloat16 [2, 8, 256, 1152], P('dp', 'tm', 'space'), may hold values from -6 to 6
- query_t: bfloat16 [2, 8, 256, 1152], P('dp', 'tm', 'space'), may hold values from -8 to 8
- key_t: bfloat16 [2, 8, 256, 1152], P('dp', 'tm', 'space'), may hold values from -8 to 8
- value_t: bfloat16 [2, 8, 256, 1152], P('dp', 'tm', 'space'), may hold values from -6 to 6
- adapters_a: bfloat16 [4, 1152, 16], replicated, may hold values from -0.1875 to 0.1875
- adapters_b: bfloat16 [4, 16, 1152], replicated, may hold values from -1.5 to 1.5
- cotangent: bfloat16 [2, 8, 256, 1152], P('dp', 'tm', 'space'), may hold values from -6 to 6
Outputs:
- mixed: bfloat16 [2, 8, 256, 1152], P('dp', 'tm', 'space')
- grads_a: float32 [4, 1152, 16], replicated
- grads_b: float32 [4, 16, 1152], replicated
All inputs are finite; a program needn't handle non-finite values.
Results may differ from a plain program's by a relative error of at most 0.018.
The roundings to bfloat16 on the way count: a program that leaves them out, or rounds other values in their place, can miss the bound.
Values may be sent and summed in bfloat16 or wider, within the bound.
No kernel may reach another device: no remote copies, remote signals or barrier semaphores. Data moves between devices by JAX's collectives and lax.ppermute only.
A program may use at most 64 MiB of HBM per device.

v0:
```python
import jax
import jax.numpy as jnp
from jax import lax
from jax.sharding import PartitionSpec as P

HEAD_DIM = 72


def softmax_probs(query, keys):
    length, columns = query.shape
    heads_here = columns // HEAD_DIM
    heads_q = query.reshape(length, heads_here, HEAD_DIM)
    heads_k = keys.reshape(keys.shape[0], heads_here, HEAD_DIM)
    scores = jnp.einsum(
        "qhd,khd->hqk", heads_q, heads_k, preferred_element_type=jnp.float32
    ) * HEAD_DIM ** (-0.5)
    peak = jnp.max(scores, axis=-1, keepdims=True)
    weights = jnp.exp(scores - peak)
    return weights / jnp.sum(weights, axis=-1, keepdims=True)


def attend_forward(query, keys, values):
    length, columns = query.shape
    heads_here = columns // HEAD_DIM
    probs_low = softmax_probs(query, keys).astype(jnp.bfloat16)
    heads_v = values.reshape(values.shape[0], heads_here, HEAD_DIM)
    output = jnp.einsum("hqk,khd->qhd", probs_low, heads_v, preferred_element_type=jnp.float32)
    return output.reshape(length, columns).astype(jnp.bfloat16)


def attend_backward(query, keys, values, grad):
    length, columns = query.shape
    count = keys.shape[0]
    heads_here = columns // HEAD_DIM
    probs = softmax_probs(query, keys)
    probs_low = probs.astype(jnp.bfloat16)
    heads_g = grad.reshape(length, heads_here, HEAD_DIM)
    heads_v = values.reshape(count, heads_here, HEAD_DIM)
    heads_k = keys.reshape(count, heads_here, HEAD_DIM)
    dvals = jnp.einsum("hqk,qhd->khd", probs_low, heads_g, preferred_element_type=jnp.float32)
    dprob = jnp.einsum("qhd,khd->hqk", heads_g, heads_v, preferred_element_type=jnp.float32)
    inner = jnp.sum(probs * dprob, axis=-1, keepdims=True)
    dscore = (probs * (dprob - inner) * HEAD_DIM ** (-0.5)).astype(jnp.bfloat16)
    dquery = jnp.einsum("hqk,khd->qhd", dscore, heads_k, preferred_element_type=jnp.float32)
    return (
        dquery.reshape(length, columns).astype(jnp.bfloat16),
        dvals.reshape(count, columns).astype(jnp.bfloat16),
    )


def per_device(
    patches, query_s, key_s, value_s, query_t, key_t, value_t, adapters_a, adapters_b, cotangent
):
    inputs = patches[0]
    frames_dev, patch_dev, width = inputs.shape

    def encode(source, index):
        return jnp.dot(
            source.reshape(-1, width), adapters_a[index], preferred_element_type=jnp.float32
        ).astype(jnp.bfloat16)

    def adapted(base, codes, index):
        lifted = base.reshape(-1, width).astype(jnp.float32) + jnp.dot(
            codes, adapters_b[index], preferred_element_type=jnp.float32
        )
        return lifted.astype(jnp.bfloat16).reshape(frames_dev, patch_dev, width)

    def token_grads(codes, dproj, index):
        flat_dproj = dproj.reshape(-1, width)
        grad_b = jnp.dot(codes.T, flat_dproj, preferred_element_type=jnp.float32)
        dcodes = jnp.dot(
            flat_dproj, adapters_b[index].T, preferred_element_type=jnp.float32
        ).astype(jnp.bfloat16)
        return (grad_b, dcodes)

    def down_grad(source, dcodes):
        return jnp.dot(source.reshape(-1, width).T, dcodes, preferred_element_type=jnp.float32)

    codes_sq = encode(inputs, 0)
    codes_sv = encode(inputs, 1)
    q_s = adapted(query_s[0], codes_sq, 0)
    v_s = adapted(value_s[0], codes_sv, 1)
    space_q, space_k, space_v = (
        lax.all_to_all(q_s, "space", split_axis=2, concat_axis=1, tiled=True),
        lax.all_to_all(key_s[0], "space", split_axis=2, concat_axis=1, tiled=True),
        lax.all_to_all(v_s, "space", split_axis=2, concat_axis=1, tiled=True),
    )
    out_s = lax.map(
        lambda trio: attend_forward(trio[0], trio[1], trio[2]), (space_q, space_k, space_v)
    )
    back_s = lax.all_to_all(out_s, "space", split_axis=1, concat_axis=2, tiled=True)
    hidden = (inputs.astype(jnp.float32) + back_s.astype(jnp.float32)).astype(jnp.bfloat16)
    codes_tq = encode(hidden, 2)
    codes_tv = encode(hidden, 3)
    q_t = adapted(query_t[0], codes_tq, 2)
    v_t = adapted(value_t[0], codes_tv, 3)
    time_q, time_k, time_v = (
        lax.all_to_all(q_t, "tm", split_axis=2, concat_axis=0, tiled=True),
        lax.all_to_all(key_t[0], "tm", split_axis=2, concat_axis=0, tiled=True),
        lax.all_to_all(v_t, "tm", split_axis=2, concat_axis=0, tiled=True),
    )
    out_t = jax.vmap(attend_forward, in_axes=1, out_axes=1)(time_q, time_k, time_v)
    back_t = lax.all_to_all(out_t, "tm", split_axis=0, concat_axis=2, tiled=True)
    mixed = (hidden.astype(jnp.float32) + back_t.astype(jnp.float32)).astype(jnp.bfloat16)
    grad = cotangent[0]
    grad_time = lax.all_to_all(grad, "tm", split_axis=2, concat_axis=0, tiled=True)
    dq_time, dv_time = jax.vmap(attend_backward, in_axes=1, out_axes=1)(
        time_q, time_k, time_v, grad_time
    )
    dq_t, dv_t = (
        lax.all_to_all(dq_time, "tm", split_axis=0, concat_axis=2, tiled=True),
        lax.all_to_all(dv_time, "tm", split_axis=0, concat_axis=2, tiled=True),
    )
    gb_tq, dcodes_tq = token_grads(codes_tq, dq_t, 2)
    gb_tv, dcodes_tv = token_grads(codes_tv, dv_t, 3)
    ga_tq = down_grad(hidden, dcodes_tq)
    ga_tv = down_grad(hidden, dcodes_tv)
    factor = (
        frames_dev * patch_dev * lax.axis_size("dp") * lax.axis_size("tm") * lax.axis_size("space")
    ) ** (-0.5)
    dhidden = grad.reshape(-1, width).astype(jnp.float32)
    dhidden = dhidden + jnp.dot(dcodes_tq, adapters_a[2].T, preferred_element_type=jnp.float32)
    dhidden = dhidden + jnp.dot(dcodes_tv, adapters_a[3].T, preferred_element_type=jnp.float32)
    dhidden = dhidden.astype(jnp.bfloat16).reshape(frames_dev, patch_dev, width)
    grad_space = lax.all_to_all(dhidden, "space", split_axis=2, concat_axis=1, tiled=True)
    dq_space, dv_space = lax.map(
        lambda quad: attend_backward(quad[0], quad[1], quad[2], quad[3]),
        (space_q, space_k, space_v, grad_space),
    )
    dq_s, dv_s = (
        lax.all_to_all(dq_space, "space", split_axis=1, concat_axis=2, tiled=True),
        lax.all_to_all(dv_space, "space", split_axis=1, concat_axis=2, tiled=True),
    )
    gb_sq, dcodes_sq = token_grads(codes_sq, dq_s, 0)
    gb_sv, dcodes_sv = token_grads(codes_sv, dv_s, 1)
    ga_sq = down_grad(inputs, dcodes_sq)
    ga_sv = down_grad(inputs, dcodes_sv)
    total_a, total_b = lax.psum(
        (jnp.stack([ga_sq, ga_sv, ga_tq, ga_tv]), jnp.stack([gb_sq, gb_sv, gb_tq, gb_tv])),
        ("dp", "tm", "space"),
    )
    grads_a = total_a * factor
    grads_b = total_b * factor
    return (mixed[None], grads_a, grads_b)


def solution(mesh):
    in_specs = (
        P("dp", "tm", "space", None),
        P("dp", "tm", "space", None),
        P("dp", "tm", "space", None),
        P("dp", "tm", "space", None),
        P("dp", "tm", "space", None),
        P("dp", "tm", "space", None),
        P("dp", "tm", "space", None),
        P(),
        P(),
        P("dp", "tm", "space", None),
    )
    out_specs = (P("dp", "tm", "space", None), P(), P())
    return jax.shard_map(
        per_device, mesh=mesh, in_specs=in_specs, out_specs=out_specs, check_vma=False
    )
```

profile of v0, /device:TPU:0, one launch (start us, length us, event | category | flops | bytes accessed | tf_op | source)
XLA Modules:
  0.0 344.0 jit_solution(10725607579424361705)
XLA Ops:
  11.5 5.3 %all-to-all-start = ((bf16[4,2,18432]{2,1,0:T(2,128)(2,1)}), bf16[4,2,18432]{2,1,0:T(2,128)(2,1)S(1)}, u32[]{:S(2)}, u32[]{:S(2)}) async-start(bf16[4,2,18432]{2,1,0:T(2,128)(2,1)} %reshape.212), calls=%async_computation | async-start | bytes 589824 | tf_op jit(solution)/shard_map/all_to_all | solution.py:86
  22.4 3.5 %all-to-all-start.1 = ((bf16[4,2,18432]{2,1,0:T(2,128)(2,1)}), bf16[4,2,18432]{2,1,0:T(2,128)(2,1)S(1)}, u32[]{:S(2)}, u32[]{:S(2)}) async-start(bf16[4,2,18432]{2,1,0:T(2,128)(2,1)} %reshape.214), calls=%async_computation.1 | async-start | bytes 589824 | tf_op jit(solution)/shard_map/all_to_all | solution.py:84
  27.5 3.8 %all-to-all-done.1 = bf16[4,2,18432]{2,1,0:T(2,128)(2,1)S(1)} async-done(((bf16[4,2,18432]{2,1,0:T(2,128)(2,1)}), bf16[4,2,18432]{2,1,0:T(2,128)(2,1)S(1)}, u32[]{:S(2)}, u32[]{:S(2)}) %all-to-all-start.1) | async-done | bytes 294944 | tf_op jit(solution)/shard_map/all_to_all | solution.py:84
  31.3 3.5 %all-to-all-start.2 = ((bf16[4,2,18432]{2,1,0:T(2,128)(2,1)}), bf16[4,2,18432]{2,1,0:T(2,128)(2,1)S(1)}, u32[]{:S(2)}, u32[]{:S(2)}) async-start(bf16[4,2,18432]{2,1,0:T(2,128)(2,1)} %reshape.216), calls=%async_computation.2 | async-start | bytes 589824 | tf_op jit(solution)/shard_map/all_to_all | solution.py:85
  41.3 5.3 %while.22 = (s32[]{:T(128)}, bf16[2,256,288]{1,2,0:T(8,128)(2,1)S(1)}, bf16[2,256,288]{1,2,0:T(8,128)(2,1)S(1)}, bf16[2,256,288]{1,2,0:T(8,128)(2,1)S(1)}, bf16[2,256,288]{1,2,0:T(8,128)(2,1)S(1)}, /*index=5*/s32[]{:T(128)}) while((s32[]{:T(128)}, bf16[2,256,288]{1,2,0:T(8,128)(2,1)S(1)}, bf16[2,256,288]{1,2,0:T(8,128)(2,1)S(1)}, ...), condition=%wide.region_3.4_spmd, body=%wide.region_0.3_spmd.sunk | while | flops 115156480 | bytes 4169817 | solution.py:88
  47.7 3.5 %all-to-all-start.3 = ((bf16[2,256,288]{2,0,1:T(2,128)(2,1)}), bf16[2,256,288]{2,0,1:T(2,128)(2,1)S(1)}, u32[]{:S(2)}, u32[]{:S(2)}) async-start(bf16[2,256,288]{2,0,1:T(2,128)(2,1)} %copy.117), calls=%async_computation.3 | async-start | bytes 786432 | tf_op jit(solution)/shard_map/all_to_all | solution.py:91
  52.8 4.2 %all-to-all-done.3 = bf16[2,256,288]{2,0,1:T(2,128)(2,1)S(1)} async-done(((bf16[2,256,288]{2,0,1:T(2,128)(2,1)}), bf16[2,256,288]{2,0,1:T(2,128)(2,1)S(1)}, u32[]{:S(2)}, u32[]{:S(2)}) %all-to-all-start.3) | async-done | bytes 294944 | tf_op jit(solution)/shard_map/all_to_all | solution.py:91
  57.0 4.9 %all-to-all-start.6 = ((bf16[4,2,18432]{2,1,0:T(2,128)(2,1)}), bf16[4,2,18432]{2,1,0:T(2,128)(2,1)S(1)}, u32[]{:S(2)}, u32[]{:S(2)}) async-start(bf16[4,2,18432]{2,1,0:T(2,128)(2,1)} %reshape.222), calls=%async_computation.6 | async-start | bytes 589824 | tf_op jit(solution)/shard_map/all_to_all | solution.py:99
  66.9 2.0 all-to-all-done.6
  68.9 4.1 %all-to-all-start.4 = ((bf16[4,2,18432]{2,1,0:T(2,128)(2,1)}), bf16[4,2,18432]{2,1,0:T(2,128)(2,1)}, u32[]{:S(2)}, u32[]{:S(2)}) async-start(bf16[4,2,18432]{2,1,0:T(2,128)(2,1)} %reshape.218), calls=%async_computation.4 | async-start | bytes 589824 | tf_op jit(solution)/shard_map/all_to_all | solution.py:100
  77.0 3.2 all-to-all-done.4
  80.2 4.3 %all-to-all-start.5 = ((bf16[4,2,18432]{2,1,0:T(2,128)(2,1)}), bf16[4,2,18432]{2,1,0:T(2,128)(2,1)}, u32[]{:S(2)}, u32[]{:S(2)}) async-start(bf16[4,2,18432]{2,1,0:T(2,128)(2,1)} %reshape.220), calls=%async_computation.5 | async-start | bytes 589824 | tf_op jit(solution)/shard_map/all_to_all | solution.py:98
  92.7 4.8 %all-to-all-start.8 = ((bf16[4,2,18432]{2,1,0:T(2,128)(2,1)}), bf16[4,2,18432]{2,1,0:T(2,128)(2,1)S(1)}, u32[]{:S(2)}, u32[]{:S(2)}) async-start(bf16[4,2,18432]{2,1,0:T(2,128)(2,1)} %reshape.224), calls=%async_computation.8 | async-start | bytes 589824 | tf_op jit(solution)/shard_map/all_to_all | solution.py:106
  102.9 3.3 fusion.97
  111.7 5.1 %all-to-all-start.7 = ((bf16[8,64,288]{2,1,0:T(8,128)(2,1)}), bf16[8,64,288]{2,1,0:T(8,128)(2,1)}, u32[]{:S(2)}, u32[]{:S(2)}) async-start(bf16[8,64,288]{2,1,0:T(8,128)(2,1)} %copy.137), calls=%async_computation.7 | async-start | bytes 786432 | tf_op jit(solution)/shard_map/all_to_all | solution.py:103
  124.4 3.0 all-to-all-done.7
  127.4 4.7 %all-to-all-start.10 = ((bf16[8,64,288]{2,1,0:T(8,128)(2,1)}), bf16[8,64,288]{2,1,0:T(8,128)(2,1)}, u32[]{:S(2)}, u32[]{:S(2)}) async-start(bf16[8,64,288]{2,1,0:T(8,128)(2,1)} %copy.152), calls=%async_computation.10 | async-start | bytes 786432 | tf_op jit(solution)/shard_map/all_to_all | solution.py:112
  133.7 3.3 fusion.37
  138.3 6.6 %all-to-all-done.10 = bf16[8,64,288]{2,1,0:T(8,128)(2,1)} async-done(((bf16[8,64,288]{2,1,0:T(8,128)(2,1)}), bf16[8,64,288]{2,1,0:T(8,128)(2,1)}, u32[]{:S(2)}, u32[]{:S(2)}) %all-to-all-start.10) | async-done | bytes 294944 | tf_op jit(solution)/shard_map/all_to_all | solution.py:112
  145.0 3.7 %all-to-all-start.9 = ((bf16[8,64,288]{2,1,0:T(8,128)(2,1)}), bf16[8,64,288]{2,1,0:T(8,128)(2,1)S(1)}, u32[]{:S(2)}, u32[]{:S(2)}) async-start(bf16[8,64,288]{2,1,0:T(8,128)(2,1)} %copy.148), calls=%async_computation.9 | async-start | bytes 786432 | tf_op jit(solution)/shard_map/all_to_all | solution.py:111
  153.8 3.5 %all-to-all-done.9 = bf16[8,64,288]{2,1,0:T(8,128)(2,1)S(1)} async-done(((bf16[8,64,288]{2,1,0:T(8,128)(2,1)}), bf16[8,64,288]{2,1,0:T(8,128)(2,1)S(1)}, u32[]{:S(2)}, u32[]{:S(2)}) %all-to-all-start.9) | async-done | bytes 294944 | tf_op jit(solution)/shard_map/all_to_all | solution.py:111
  161.4 3.5 %all-to-all-start.11 = ((bf16[4,2,18432]{2,1,0:T(2,128)(2,1)}), bf16[4,2,18432]{2,1,0:T(2,128)(2,1)S(1)}, u32[]{:S(2)}, u32[]{:S(2)}) async-start(bf16[4,2,18432]{2,1,0:T(2,128)(2,1)} %reshape.226), calls=%async_computation.11 | async-start | bytes 589824 | tf_op jit(solution)/shard_map/all_to_all | solution.py:125
  166.5 3.8 %all-to-all-done.11 = bf16[4,2,18432]{2,1,0:T(2,128)(2,1)S(1)} async-done(((bf16[4,2,18432]{2,1,0:T(2,128)(2,1)}), bf16[4,2,18432]{2,1,0:T(2,128)(2,1)S(1)}, u32[]{:S(2)}, u32[]{:S(2)}) %all-to-all-start.11) | async-done | bytes 294944 | tf_op jit(solution)/shard_map/all_to_all | solution.py:125
  173.2 10.8 %while.23 = (s32[]{:T(128)}, bf16[2,256,288]{1,2,0:T(8,128)(2,1)}, bf16[2,256,288]{1,2,0:T(8,128)(2,1)}, bf16[2,256,288]{1,2,0:T(8,128)(2,1)S(1)}, bf16[2,256,28...) while((s32[]{:T(128)}, bf16[2,256,288]{1,2,0:T(8,128)(2,1)}, ...), condition=%wide.region_11.12_spmd, body=%wide.region_7.11_spmd.sunk | while | flops 192563968 | bytes 7467149 | solution.py:126
  175.8 2.0 fusion.184
  181.3 2.0 fusion.184
  184.0 1.9 copy.164
  185.9 3.6 %all-to-all-start.13 = ((bf16[2,256,288]{2,0,1:T(2,128)(2,1)}), bf16[2,256,288]{2,0,1:T(2,128)(2,1)S(1)}, u32[]{:S(2)}, u32[]{:S(2)}) async-start(bf16[2,256,288]{2,0,1:T(2,128)(2,1)} %copy.164), calls=%async_computation.13 | async-start | bytes 786432 | tf_op jit(solution)/shard_map/all_to_all | solution.py:132
  191.7 3.6 %all-to-all-done.13 = bf16[2,256,288]{2,0,1:T(2,128)(2,1)S(1)} async-done(((bf16[2,256,288]{2,0,1:T(2,128)(2,1)}), bf16[2,256,288]{2,0,1:T(2,128)(2,1)S(1)}, u32[]{:S(2)}, u32[]{:S(2)}) %all-to-all-start.13) | async-done | bytes 294944 | tf_op jit(solution)/shard_map/all_to_all | solution.py:132
  195.4 3.5 %all-to-all-start.12 = ((bf16[2,256,288]{2,0,1:T(2,128)(2,1)}), bf16[2,256,288]{2,0,1:T(2,128)(2,1)S(1)}, u32[]{:S(2)}, u32[]{:S(2)}) async-start(bf16[2,256,288]{2,0,1:T(2,128)(2,1)} %copy.161), calls=%async_computation.12 | async-start | bytes 786432 | tf_op jit(solution)/shard_map/all_to_all | solution.py:131
  201.3 3.4 all-to-all-done.12
  209.6 125.0 %all-reduce.3.cloned.1.call-done = (f32[4,1152,16]{1,2,0:T(8,128)}, f32[4,16,1152]{2,1,0:T(8,128)}) async-done(((f32[4,1152,16]{1,2,0:T(8,128)}, f32[4,16,1152]{2,1,0:T(8,128)}), (f32[4,1152,16]{1,2,0:T(8,128)}, f32[4,16,1152]{2,1,0:T(8,128)})) %all-reduce.3.cloned.1.call-update) | async-done | bytes 589840 | tf_op jit(solution)/shard_map/psum | solution.py:138
  (216 shorter events, 96.5 us)
Async XLA Ops:
  7.2 1.2 copy-start.11
  8.3 1.3 copy-start.25
  11.5 5.3 %copy-start = (bf16[1,2,64,1152]{3,2,1,0:T(8,128)(2,1)S(1)}, bf16[1,2,64,1152]{3,2,1,0:T(8,128)(2,1)}, u32[]{:S(2)}) copy-start(bf16[1,2,64,1152]{3,2,1,0:T(8,128)(2,1)} %param.14) | copy-start | bytes 884740
  11.5 10.9 %all-to-all-start = ((bf16[4,2,18432]{2,1,0:T(2,128)(2,1)}), bf16[4,2,18432]{2,1,0:T(2,128)(2,1)S(1)}, u32[]{:S(2)}, u32[]{:S(2)}) async-start(bf16[4,2,18432]{2,1,0:T(2,128)(2,1)} %reshape.212), calls=%async_computation | async-start | bytes 589824 | tf_op jit(solution)/shard_map/all_to_all | solution.py:86
  19.1 1.2 copy-start.15
  22.4 8.9 %all-to-all-start.1 = ((bf16[4,2,18432]{2,1,0:T(2,128)(2,1)}), bf16[4,2,18432]{2,1,0:T(2,128)(2,1)S(1)}, u32[]{:S(2)}, u32[]{:S(2)}) async-start(bf16[4,2,18432]{2,1,0:T(2,128)(2,1)} %reshape.214), calls=%async_computation.1 | async-start | bytes 589824 | tf_op jit(solution)/shard_map/all_to_all | solution.py:84
  27.5 7.3 %copy-start.16 = (bf16[1,2,64,1152]{3,2,1,0:T(8,128)(2,1)S(1)}, bf16[1,2,64,1152]{3,2,1,0:T(8,128)(2,1)}, u32[]{:S(2)}) copy-start(bf16[1,2,64,1152]{3,2,1,0:T(8,128)(2,1)} %param.19) | copy-start | bytes 884740
  31.3 8.9 %all-to-all-start.2 = ((bf16[4,2,18432]{2,1,0:T(2,128)(2,1)}), bf16[4,2,18432]{2,1,0:T(2,128)(2,1)S(1)}, u32[]{:S(2)}, u32[]{:S(2)}) async-start(bf16[4,2,18432]{2,1,0:T(2,128)(2,1)} %reshape.216), calls=%async_computation.2 | async-start | bytes 589824 | tf_op jit(solution)/shard_map/all_to_all | solution.py:85
  47.7 9.3 %all-to-all-start.3 = ((bf16[2,256,288]{2,0,1:T(2,128)(2,1)}), bf16[2,256,288]{2,0,1:T(2,128)(2,1)S(1)}, u32[]{:S(2)}, u32[]{:S(2)}) async-start(bf16[2,256,288]{2,0,1:T(2,128)(2,1)} %copy.117), calls=%async_computation.3 | async-start | bytes 786432 | tf_op jit(solution)/shard_map/all_to_all | solution.py:91
  57.0 11.9 %all-to-all-start.6 = ((bf16[4,2,18432]{2,1,0:T(2,128)(2,1)}), bf16[4,2,18432]{2,1,0:T(2,128)(2,1)S(1)}, u32[]{:S(2)}, u32[]{:S(2)}) async-start(bf16[4,2,18432]{2,1,0:T(2,128)(2,1)} %reshape.222), calls=%async_computation.6 | async-start | bytes 589824 | tf_op jit(solution)/shard_map/all_to_all | solution.py:99
  63.9 1.1 copy-start.27
  68.9 5.1 %copy-start.8 = (bf16[4,2,18432]{2,1,0:T(2,128)(2,1)}, bf16[4,2,18432]{2,1,0:T(2,128)(2,1)S(1)}, u32[]{:S(2)}) copy-start(bf16[4,2,18432]{2,1,0:T(2,128)(2,1)S(1)} %all-to-all-done.6) | copy-start | bytes 884740
  68.9 11.3 %all-to-all-start.4 = ((bf16[4,2,18432]{2,1,0:T(2,128)(2,1)}), bf16[4,2,18432]{2,1,0:T(2,128)(2,1)}, u32[]{:S(2)}, u32[]{:S(2)}) async-start(bf16[4,2,18432]{2,1,0:T(2,128)(2,1)} %reshape.218), calls=%async_computation.4 | async-start | bytes 589824 | tf_op jit(solution)/shard_map/all_to_all | solution.py:100
  74.0 1.1 copy-start.29
  77.0 7.5 %copy-start.6 = (bf16[1,2,64,1152]{3,2,1,0:T(8,128)(2,1)S(1)}, bf16[1,2,64,1152]{3,2,1,0:T(8,128)(2,1)}, u32[]{:S(2)}) copy-start(bf16[1,2,64,1152]{3,2,1,0:T(8,128)(2,1)} %param.23) | copy-start | bytes 884740
  80.2 12.5 %all-to-all-start.5 = ((bf16[4,2,18432]{2,1,0:T(2,128)(2,1)}), bf16[4,2,18432]{2,1,0:T(2,128)(2,1)}, u32[]{:S(2)}, u32[]{:S(2)}) async-start(bf16[4,2,18432]{2,1,0:T(2,128)(2,1)} %reshape.220), calls=%async_computation.5 | async-start | bytes 589824 | tf_op jit(solution)/shard_map/all_to_all | solution.py:98
  92.7 19.1 %all-to-all-start.8 = ((bf16[4,2,18432]{2,1,0:T(2,128)(2,1)}), bf16[4,2,18432]{2,1,0:T(2,128)(2,1)S(1)}, u32[]{:S(2)}, u32[]{:S(2)}) async-start(bf16[4,2,18432]{2,1,0:T(2,128)(2,1)} %reshape.224), calls=%async_computation.8 | async-start | bytes 589824 | tf_op jit(solution)/shard_map/all_to_all | solution.py:106
  111.7 15.7 %all-to-all-start.7 = ((bf16[8,64,288]{2,1,0:T(8,128)(2,1)}), bf16[8,64,288]{2,1,0:T(8,128)(2,1)}, u32[]{:S(2)}, u32[]{:S(2)}) async-start(bf16[8,64,288]{2,1,0:T(8,128)(2,1)} %copy.137), calls=%async_computation.7 | async-start | bytes 786432 | tf_op jit(solution)/shard_map/all_to_all | solution.py:103
  120.1 1.1 copy-start.33
  124.4 7.7 %copy-start.5 = (bf16[64,8,4,72]{3,2,0,1:T(4,128)(2,1)S(1)}, bf16[64,8,4,72]{3,2,0,1:T(4,128)(2,1)}, u32[]{:S(2)}) copy-start(bf16[64,8,4,72]{3,2,0,1:T(4,128)(2,1)} %copy-done.4) | copy-start | bytes 884740
  127.4 17.6 %all-to-all-start.10 = ((bf16[8,64,288]{2,1,0:T(8,128)(2,1)}), bf16[8,64,288]{2,1,0:T(8,128)(2,1)}, u32[]{:S(2)}, u32[]{:S(2)}) async-start(bf16[8,64,288]{2,1,0:T(8,128)(2,1)} %copy.152), calls=%async_computation.10 | async-start | bytes 786432 | tf_op jit(solution)/shard_map/all_to_all | solution.py:112
  145.0 12.3 %all-to-all-start.9 = ((bf16[8,64,288]{2,1,0:T(8,128)(2,1)}), bf16[8,64,288]{2,1,0:T(8,128)(2,1)S(1)}, u32[]{:S(2)}, u32[]{:S(2)}) async-start(bf16[8,64,288]{2,1,0:T(8,128)(2,1)} %copy.148), calls=%async_computation.9 | async-start | bytes 786432 | tf_op jit(solution)/shard_map/all_to_all | solution.py:111
  157.9 1.4 copy-start.1
  161.4 8.9 %all-to-all-start.11 = ((bf16[4,2,18432]{2,1,0:T(2,128)(2,1)}), bf16[4,2,18432]{2,1,0:T(2,128)(2,1)S(1)}, u32[]{:S(2)}, u32[]{:S(2)}) async-start(bf16[4,2,18432]{2,1,0:T(2,128)(2,1)} %reshape.226), calls=%async_computation.11 | async-start | bytes 589824 | tf_op jit(solution)/shard_map/all_to_all | solution.py:125
  185.9 3.6 %copy-start.28 = (bf16[128,16]{0,1:T(8,128)(2,1)S(1)}, bf16[128,16]{0,1:T(8,128)(2,1)}, u32[]{:S(2)}) copy-start(bf16[128,16]{0,1:T(8,128)(2,1)} %copy-done.27) | copy-start | bytes 12292
  185.9 3.8 %copy-start.30 = (bf16[128,16]{0,1:T(8,128)(2,1)S(1)}, bf16[128,16]{0,1:T(8,128)(2,1)}, u32[]{:S(2)}) copy-start(bf16[128,16]{0,1:T(8,128)(2,1)} %copy-done.29) | copy-start | bytes 12292
  185.9 9.4 %all-to-all-start.13 = ((bf16[2,256,288]{2,0,1:T(2,128)(2,1)}), bf16[2,256,288]{2,0,1:T(2,128)(2,1)S(1)}, u32[]{:S(2)}, u32[]{:S(2)}) async-start(bf16[2,256,288]{2,0,1:T(2,128)(2,1)} %copy.164), calls=%async_computation.13 | async-start | bytes 786432 | tf_op jit(solution)/shard_map/all_to_all | solution.py:132
  189.5 1.1 copy-start.10
  195.4 9.3 %all-to-all-start.12 = ((bf16[2,256,288]{2,0,1:T(2,128)(2,1)}), bf16[2,256,288]{2,0,1:T(2,128)(2,1)S(1)}, u32[]{:S(2)}, u32[]{:S(2)}) async-start(bf16[2,256,288]{2,0,1:T(2,128)(2,1)} %copy.161), calls=%async_computation.12 | async-start | bytes 786432 | tf_op jit(solution)/shard_map/all_to_all | solution.py:131
  198.8 135.8 %all-reduce.3.cloned.1.call-start = ((), (), s32[]{:S(2)}) async-start(), calls=%async_computation.14 | async-start | bytes 1179648 | tf_op jit(solution)/shard_map/psum | solution.py:138
  207.7 1.2 copy-start.3
  334.6 1.7 copy-start.22
  (18 other events, 15.6 us)
Sparse Core Ops, SparseCore 0:
  208.5 126.0 all-reduce.2
where the time goes:
time: 346 us; the launch traced here: 344 us
  waiting for transfers between devices  166 us (48%)
  local copies, waits for them, and re-layouts  62.1 us (18%)
  starting transfers between devices  57.7 us (17%)
  matrix products  37.5 us (11%)
  between operations  14.9 us (4%)
  other arithmetic  5.94 us (2%)
    psum x1, waiting for transfers between devices, per_device(): lax.psum((jnp.stack([ga_sq, ga_sv, ga_tq, ga_tv]), jnp.stack([gb_sq, gb_s...  125 us
    unnamed x88, local copies, waits for them, and re-layouts  25.3 us
    sub x5, matrix products, softmax_probs(): weights = jnp.exp(scores - peak)  8.53 us
    dot_general x3, matrix products, attend_backward(): jnp.einsum('hqk,khd->qhd', dscore, heads_k, preferred_element_type=jnp.fl...  7.27 us
  transfers between devices with their start and end apart: 15, of which 13 were waited for; matrix products, arithmetic and copies ran while one was open for 18% of the time, Pallas kernels for 0%

commit v1 on v0

v1 whole, which is shorter than its diff:
```python
import functools

import jax
import jax.numpy as jnp
from jax import lax
from jax.experimental import pallas as pl
from jax.experimental.pallas import tpu as pltpu
from jax.sharding import PartitionSpec as P

HEAD_DIM = 72
RANK = 16
SCALE = HEAD_DIM ** (-0.5)
F32 = jnp.float32
BF16 = jnp.bfloat16
NN = (((1,), (0,)), ((), ()))
NT = (((1,), (1,)), ((), ()))
TN = (((0,), (0,)), ((), ()))


def mm(a, b, dims=NN):
    return lax.dot_general(a, b, dims, preferred_element_type=F32)


def call(kernel, out_shape, *args, flops=0):
    vmem = pl.BlockSpec(memory_space=pltpu.VMEM)
    single = not isinstance(out_shape, (tuple, list))
    outs = (out_shape,) if single else tuple(out_shape)
    moved = sum(a.size * a.dtype.itemsize for a in args)
    moved += sum(o.size * o.dtype.itemsize for o in outs)
    result = pl.pallas_call(
        kernel,
        out_shape=outs,
        in_specs=[vmem] * len(args),
        out_specs=tuple(vmem for _ in outs),
        compiler_params=pltpu.CompilerParams(vmem_limit_bytes=48 * 1024 * 1024),
        cost_estimate=pl.CostEstimate(flops=flops, bytes_accessed=moved, transcendentals=0),
    )(*args)
    return result[0] if single else result


def shape(dims, dtype):
    return jax.ShapeDtypeStruct(tuple(dims), dtype)


def probs_of(keys, q_t, mask):
    scores = mm(keys, q_t) * SCALE
    if mask is not None:
        scores = jnp.where(mask, scores, -1e30)
    peak = jnp.max(scores, axis=0, keepdims=True)
    weights = jnp.exp(scores - peak)
    return weights / jnp.sum(weights, axis=0, keepdims=True)


def head_forward(q_t, k_t, v_t, mask=None):
    probs = probs_of(k_t.T, q_t, mask)
    return mm(v_t, probs.astype(BF16))


def head_backward(q_t, k_t, v_t, g_t, mask=None, forward=False):
    probs = probs_of(k_t.T, q_t, mask)
    low = probs.astype(BF16)
    dvals = mm(g_t, low, NT)
    dprob = mm(v_t.T, g_t)
    inner = jnp.sum(probs * dprob, axis=0, keepdims=True)
    dscore = (probs * (dprob - inner) * SCALE).astype(BF16)
    dquery = mm(k_t, dscore)
    out = mm(v_t, low) if forward else None
    return dquery, dvals, out


def rows_of(array, head):
    return array[head * HEAD_DIM : (head + 1) * HEAD_DIM]


def pack_time_kernel(n_t, sub, q_ref, k_ref, v_ref, g_ref, out_ref):
    for index, ref in enumerate((q_ref, k_ref, v_ref, g_ref)):
        frames = ref.shape[1]
        for i in range(n_t):
            for f in range(frames):
                out_ref[i, index, f * sub : (f + 1) * sub] = ref[0, f, i * sub : (i + 1) * sub]


def pack_space_kernel(n_s, p_ref, q_ref, k_ref, v_ref, g_ref, at_ref, b_ref, first_ref, second_ref):
    tokens, width = first_ref.shape[3], p_ref.shape[3]
    d_s = width // n_s

    def flat(ref):
        return ref[0].reshape(tokens, width)

    patches = flat(p_ref)
    downs = jnp.concatenate([at_ref[0], at_ref[1]], axis=0)
    codes_q = mm(patches, at_ref[0], NT).astype(BF16)
    codes_v = mm(patches, at_ref[1], NT).astype(BF16)
    codes_t = mm(downs, patches, NT).astype(BF16)
    query = (flat(q_ref).astype(F32) + mm(codes_q, b_ref[0])).astype(BF16)
    value = (flat(v_ref).astype(F32) + mm(codes_v, b_ref[1])).astype(BF16)
    for index, array in enumerate((query, flat(k_ref), value)):
        turned = array.T
        for j in range(n_s):
            first_ref[j, index] = turned[j * d_s : (j + 1) * d_s]
    for index, array in enumerate((patches, flat(g_ref))):
        turned = array.T
        for j in range(n_s):
            second_ref[j, index * d_s : (index + 1) * d_s] = turned[j * d_s : (j + 1) * d_s]
    for j in range(n_s):
        second_ref[j, 2 * d_s :] = codes_t


def frame_rows(pieces, f, patch_dev):
    return jnp.concatenate([x[:, f * patch_dev : (f + 1) * patch_dev] for x in pieces], axis=1)


def space_forward_kernel(frames, first_ref, qkv_ref, out_ref):
    n_s, _, d_s, tokens = first_ref.shape
    patch_dev = tokens // frames
    total = n_s * patch_dev
    step = min(total, 256)
    for index in range(3):
        pieces = [first_ref[j, index] for j in range(n_s)]
        for f in range(frames):
            qkv_ref[index, f] = frame_rows(pieces, f, patch_dev)
    for f in range(frames):
        query = qkv_ref[0, f].astype(F32)
        keys = qkv_ref[1, f].astype(F32)
        vals = qkv_ref[2, f].astype(F32)
        heads = []
        for h in range(d_s // HEAD_DIM):
            k_h = rows_of(keys, h).astype(BF16)
            v_h = rows_of(vals, h).astype(BF16)
            q_h = rows_of(query, h).astype(BF16)
            parts = [
                head_forward(q_h[:, s : s + step], k_h, v_h) for s in range(0, total, step)
            ]
            heads.append(parts[0] if len(parts) == 1 else jnp.concatenate(parts, axis=1))
        out = jnp.concatenate(heads, axis=0).astype(BF16)
        for j in range(n_s):
            out_ref[j, :, f * patch_dev : (f + 1) * patch_dev] = out[
                :, j * patch_dev : (j + 1) * patch_dev
            ]


def lane_block(rows):
    return lax.broadcasted_iota(jnp.int32, (rows, 128), 1) // (2 * RANK)


def fold(token_rows):
    block = lane_block(8)
    result = token_rows[0:8]
    for k in range(1, 4):
        result = jnp.where(block == k, token_rows[8 * k : 8 * k + 8], result)
    return result


def unfold(folded):
    pieces = [folded]
    for k in range(1, 4):
        pieces.append(pltpu.roll(folded, 128 - 2 * RANK * k, 1))
    return jnp.concatenate(pieces, axis=0)


def hidden_kernel(n_t, frames, out_ref, second_ref, at_ref, hidden_ref, send_ref):
    n_s, d_s, tokens = out_ref.shape
    patch_dev = tokens // frames
    sub = patch_dev // n_t
    downs = jnp.concatenate([at_ref[2], at_ref[3]] * 4, axis=0)
    for j in range(n_s):
        hidden = (second_ref[j, :d_s].astype(F32) + out_ref[j].astype(F32)).astype(BF16)
        hidden_ref[j] = hidden
        codes = mm(downs, hidden).T
        for i in range(n_t):
            rows = jnp.concatenate(
                [
                    codes[f * patch_dev + i * sub : f * patch_dev + (i + 1) * sub]
                    for f in range(frames)
                ],
                axis=0,
            )
            send_ref[i * n_s + j] = fold(rows)


def turn_kernel(time_ref, out_ref):
    n_t = time_ref.shape[0]
    for index in range(4):
        rows = jnp.concatenate([time_ref[i, index] for i in range(n_t)], axis=0)
        out_ref[index] = rows.T


def time_kernel(n_s, sub, x_ref, codes_ref, b_ref, out_ref, send_ref, grad_b_ref):
    _, width, tokens = x_ref.shape
    n_t = codes_ref.shape[0] // n_s
    pieces = []
    for i in range(n_t):
        total = codes_ref[i * n_s]
        for j in range(1, n_s):
            total = total + codes_ref[i * n_s + j]
        pieces.append(unfold(total))
    codes = jnp.concatenate(pieces, axis=0).T
    codes_q = codes[:RANK].astype(BF16)
    codes_v = codes[RANK : 2 * RANK].astype(BF16)
    query = (x_ref[0].astype(F32) + mm(b_ref[2], codes_q, TN)).astype(BF16).astype(F32)
    vals = (x_ref[2].astype(F32) + mm(b_ref[3], codes_v, TN)).astype(BF16).astype(F32)
    keys = x_ref[1].astype(F32)
    grad = x_ref[3].astype(F32)
    row = lax.broadcasted_iota(jnp.int32, (tokens, tokens), 0)
    col = lax.broadcasted_iota(jnp.int32, (tokens, tokens), 1)
    mask = lax.rem(row, sub) == lax.rem(col, sub)
    outs, d_query, d_vals = [], [], []
    for h in range(width // HEAD_DIM):
        dq, dv, out = head_backward(
            rows_of(query, h).astype(BF16),
            rows_of(keys, h).astype(BF16),
            rows_of(vals, h).astype(BF16),
            rows_of(grad, h).astype(BF16),
            mask,
            True,
        )
        outs.append(out)
        d_query.append(dq)
        d_vals.append(dv)
    out = jnp.concatenate(outs, axis=0).astype(BF16).T
    per = tokens // n_t
    for i in range(n_t):
        out_ref[i] = out[i * per : (i + 1) * per]
    d_query = jnp.concatenate(d_query, axis=0).astype(BF16)
    d_vals = jnp.concatenate(d_vals, axis=0).astype(BF16)
    grad_b_ref[:RANK] = mm(codes_q, d_query, NT)
    grad_b_ref[RANK:] = mm(codes_v, d_vals, NT)
    d_codes = jnp.concatenate([mm(b_ref[2], d_query), mm(b_ref[3], d_vals)] * 4, axis=0)
    d_codes = d_codes.astype(BF16).astype(F32).T
    for i in range(n_t):
        folded = fold(d_codes[i * per : (i + 1) * per])
        for j in range(n_s):
            send_ref[i * n_s + j] = folded


def space_backward_kernel(
    frames, qkv_ref, hidden_ref, second_ref, codes_ref, grad_b_ref, at_ref, b_ref, send_ref, part_ref
):
    n_s, d_s, tokens = hidden_ref.shape
    n_t = codes_ref.shape[0] // n_s
    patch_dev = tokens // frames
    sub = patch_dev // n_t
    total = n_s * patch_dev
    step = min(total, 256)
    ups = jnp.concatenate([at_ref[2], at_ref[3]], axis=0).T
    grads, grad_a = [], None
    for j in range(n_s):
        chunks = [unfold(codes_ref[i * n_s + j]) for i in range(n_t)]
        rows = jnp.concatenate(
            [chunks[i][f * sub : (f + 1) * sub] for f in range(frames) for i in range(n_t)], axis=0
        )
        d_codes = rows.T[: 2 * RANK].astype(BF16)
        term = mm(d_codes, hidden_ref[j], NT)
        grad_a = term if grad_a is None else grad_a + term
        cot = second_ref[j, d_s : 2 * d_s].astype(F32)
        grads.append((cot + mm(ups, d_codes)).astype(BF16))
    part_ref[: 2 * RANK] = grad_a
    grad_b_q = grad_b_v = None
    codes = [second_ref[j, 2 * d_s :] for j in range(n_s)]
    for f in range(frames):
        query = qkv_ref[0, f].astype(F32)
        keys = qkv_ref[1, f].astype(F32)
        vals = qkv_ref[2, f].astype(F32)
        grad = frame_rows(grads, f, patch_dev).astype(F32)
        d_query, d_vals = [], []
        for h in range(d_s // HEAD_DIM):
            k_h = rows_of(keys, h).astype(BF16)
            v_h = rows_of(vals, h).astype(BF16)
            q_h = rows_of(query, h).astype(BF16)
            g_h = rows_of(grad, h).astype(BF16)
            dq_parts, dv_sum = [], None
            for s in range(0, total, step):
                dq, dv, _ = head_backward(q_h[:, s : s + step], k_h, v_h, g_h[:, s : s + step])
                dq_parts.append(dq)
                dv_sum = dv if dv_sum is None else dv_sum + dv
            d_query.append(
                dq_parts[0] if len(dq_parts) == 1 else jnp.concatenate(dq_parts, axis=1)
            )
            d_vals.append(dv_sum)
        d_query = jnp.concatenate(d_query, axis=0).astype(BF16)
        d_vals = jnp.concatenate(d_vals, axis=0).astype(BF16)
        partial = jnp.concatenate([mm(b_ref[0], d_query), mm(b_ref[1], d_vals)], axis=0)
        for j in range(n_s):
            send_ref[j, :, f * total : (f + 1) * total] = partial.astype(BF16)
        frame_codes = frame_rows(codes, f, patch_dev)
        term_q = mm(frame_codes[:RANK], d_query, NT)
        term_v = mm(frame_codes[RANK:], d_vals, NT)
        grad_b_q = term_q if grad_b_q is None else grad_b_q + term_q
        grad_b_v = term_v if grad_b_v is None else grad_b_v + term_v
    part_ref[2 * RANK : 3 * RANK] = grad_b_q
    part_ref[3 * RANK :] = grad_b_v
    time_grad = grad_b_ref[...].astype(BF16)
    for j in range(n_s):
        send_ref[j, :, frames * total : frames * total + d_s] = time_grad[
            :, j * d_s : (j + 1) * d_s
        ]


def merge_kernel(frames, n_out, second_ref, recv_ref, part_ref, send_ref):
    n_s, _, tokens = second_ref.shape
    d_s = part_ref.shape[1]
    patch_dev = tokens // frames
    total = n_s * patch_dev
    patches = [second_ref[j, :d_s] for j in range(n_s)]
    grad_a = None
    for f in range(frames):
        codes = None
        for j in range(n_s):
            term = recv_ref[j, :, f * total : (f + 1) * total].astype(F32)
            codes = term if codes is None else codes + term
        term = mm(codes.astype(BF16), frame_rows(patches, f, patch_dev), NT)
        grad_a = term if grad_a is None else grad_a + term
    time_grad = None
    for j in range(n_s):
        term = recv_ref[j, :, frames * total : frames * total + d_s].astype(F32)
        time_grad = term if time_grad is None else time_grad + term
    rows = jnp.concatenate([grad_a, part_ref[...], time_grad], axis=0)
    per = rows.shape[0] // n_out
    for i in range(n_out):
        send_ref[i] = rows[i * per : (i + 1) * per].astype(send_ref.dtype)


def total_kernel(recv_ref, send_ref):
    total = recv_ref[0].astype(F32)
    for i in range(1, recv_ref.shape[0]):
        total = total + recv_ref[i].astype(F32)
    for i in range(send_ref.shape[0]):
        send_ref[i] = total.astype(send_ref.dtype)


def final_kernel(factor, n_s, recv_ref, a_ref, b_ref):
    count, per, d_s = recv_ref.shape
    blocks = count // n_s
    half = blocks // 2
    for block in range(blocks):
        rows = jnp.concatenate([recv_ref[block * n_s + j] for j in range(n_s)], axis=1)
        rows = rows.astype(F32) * factor
        target = a_ref if block < half else b_ref
        start = (block % half) * per
        target[start // RANK, start % RANK : start % RANK + per] = rows


def mixed_kernel(frames, hidden_ref, out_ref, mixed_ref):
    n_s, d_s, tokens = hidden_ref.shape
    n_t = out_ref.shape[0]
    patch_dev = tokens // frames
    sub = patch_dev // n_t
    hidden = hidden_ref[...].reshape(n_s * d_s, tokens).T
    for f in range(frames):
        for i in range(n_t):
            start = f * patch_dev + i * sub
            total = hidden[start : start + sub].astype(F32)
            total = total + out_ref[i, f * sub : (f + 1) * sub].astype(F32)
            mixed_ref[0, f, i * sub : (i + 1) * sub] = total.astype(BF16)


def swap(array, axes):
    return lax.all_to_all(array, axes, split_axis=0, concat_axis=0, tiled=True)


def per_device(
    patches, query_s, key_s, value_s, query_t, key_t, value_t, adapters_a, adapters_b, cotangent
):
    _, frames, patch_dev, width = patches.shape
    n_d, n_t, n_s = (lax.axis_size(name) for name in ("dp", "tm", "space"))
    tokens = frames * patch_dev
    sub = patch_dev // n_t
    d_s = width // n_s
    n_out = n_d * n_t
    total = n_s * patch_dev
    factor = (tokens * n_d * n_t * n_s) ** (-0.5)
    here = lax.axis_index("space") * d_s
    downs = jnp.swapaxes(adapters_a, 1, 2)
    downs_here = lax.dynamic_slice_in_dim(downs, here, d_s, 2)
    ups_here = lax.dynamic_slice_in_dim(adapters_b, here, d_s, 2)

    time_send = call(
        functools.partial(pack_time_kernel, n_t, sub),
        shape((n_t, 4, frames * sub, width), BF16),
        query_t, key_t, value_t, cotangent,
    )
    time_recv = swap(time_send, "tm")
    first, second = call(
        functools.partial(pack_space_kernel, n_s),
        (shape((n_s, 3, d_s, tokens), BF16), shape((n_s, 2 * d_s + 2 * RANK, tokens), BF16)),
        patches, query_s, key_s, value_s, cotangent, downs, adapters_b,
    )
    first = swap(first, "space")
    second = swap(second, "space")
    qkv, out_s = call(
        functools.partial(space_forward_kernel, frames),
        (shape((3, frames, d_s, total), BF16), shape((n_s, d_s, tokens), BF16)),
        first,
    )
    hidden, codes_send = call(
        functools.partial(hidden_kernel, n_t, frames),
        (shape((n_s, d_s, tokens), BF16), shape((n_t * n_s, 8, 128), F32)),
        out_s, second, downs_here,
    )
    codes_recv = swap(codes_send, ("tm", "space"))
    turned = call(turn_kernel, shape((4, width, n_t * frames * sub), BF16), time_recv)
    out_t, dcodes_send, time_grad_b = call(
        functools.partial(time_kernel, n_s, sub),
        (
            shape((n_t, frames * sub, width), BF16),
            shape((n_t * n_s, 8, 128), F32),
            shape((2 * RANK, width), F32),
        ),
        turned, codes_recv, adapters_b,
    )
    dcodes_recv = swap(dcodes_send, ("tm", "space"))
    part_lanes = frames * total + -(-d_s // 128) * 128
    partial_send, part = call(
        functools.partial(space_backward_kernel, frames),
        (shape((n_s, 2 * RANK, part_lanes), BF16), shape((4 * RANK, d_s), F32)),
        qkv, hidden, second, dcodes_recv, time_grad_b, downs_here, ups_here,
    )
    partial_recv = swap(partial_send, "space")
    sums_send = call(
        functools.partial(merge_kernel, frames, n_out),
        shape((n_out, 8 * RANK // n_out, d_s), F32),
        second, partial_recv, part,
    )
    sums_recv = swap(sums_send, ("dp", "tm"))
    all_send = call(total_kernel, shape((n_out * n_s, 8 * RANK // n_out, d_s), F32), sums_recv)
    all_recv = swap(all_send, ("dp", "tm", "space"))
    grads_a, grads_b = call(
        functools.partial(final_kernel, factor, n_s),
        (shape((4, RANK, width), F32), shape((4, RANK, width), F32)),
        all_recv,
    )
    mixed = call(
        functools.partial(mixed_kernel, frames),
        shape(patches.shape, BF16),
        swap(hidden, "space"), swap(out_t, "tm"),
    )
    return (mixed, jnp.swapaxes(grads_a, 1, 2), grads_b)


def solution(mesh):
    token = P("dp", "tm", "space", None)
    return jax.shard_map(
        per_device,
        mesh=mesh,
        in_specs=(token,) * 7 + (P(), P(), token),
        out_specs=(token, P(), P()),
        check_vma=False,
    )
```

time: 346 us -> 172 us (0.50)
  waiting for transfers between devices: 166 us -> 82.1 us
  local copies, waits for them, and re-layouts: 62.1 us -> 8.57 us
  matrix products: 37.5 us -> 0 us
  blocking collectives: 0 us -> 32.9 us
  starting transfers between devices: 57.7 us -> 25.1 us
  Pallas kernels: 0 us -> 22 us
  between operations: 14.9 us -> 0.79 us
  other arithmetic: 5.94 us -> 0 us
    psum x1 -> x0, waiting for transfers between devices: 125 us -> none  [per_device(): lax.psum((jnp.stack([ga_sq, ga_sv, ga_tq, ga_tv]), jnp.stack([gb_sq, gb_s...]
    all_to_all x14 -> x7, waiting for transfers between devices: 40.5 us -> 82.1 us  [swap(): return lax.all_to_all(array, axes, split_axis=0, concat_axis=0, tiled=True)]
    all_to_all x0 -> x3, blocking collectives: none -> 32.9 us  [swap(): return lax.all_to_all(array, axes, split_axis=0, concat_axis=0, tiled=True)]
    all_to_all x14 -> x7, starting transfers between devices: 57.7 us -> 25.1 us  [swap(): return lax.all_to_all(array, axes, split_axis=0, concat_axis=0, tiled=True)]
    dot_general x34 -> x0, matrix products: 29 us -> none  [the longest x3 7.27 us: attend_backward(): jnp.einsum('hqk,khd->qhd', dscore, heads_k, preferred_element_type=jnp.fl...]
    pallas_call x0 -> x11, Pallas kernels: none -> 22 us  [call(): pl.pallas_call(kernel, out_shape=outs, in_specs=[vmem] * len(args), out_s...]
    unnamed x88 -> x28, local copies, waits for them, and re-layouts: 25.3 us -> 7.55 us
    all_to_all x22 -> x0, local copies, waits for them, and re-layouts: 12.5 us -> none  [the longest x2 2.81 us: per_device(): lax.all_to_all(q_t, 'tm', split_axis=2, concat_axis=0, tiled=True)]
  transfers between devices with their start and end apart: 15 -> 7, of which waited for: 13 -> 7; matrix products, arithmetic and copies ran while one was open for 18% -> 1% of each run, Pallas kernels for 0% -> 4%
where the time goes in v1:
time: 172 us; the launch traced here: 171 us
  waiting for transfers between devices  82.1 us (48%)
  blocking collectives  32.9 us (19%)
  starting transfers between devices  25.1 us (15%)
  Pallas kernels  22 us (13%)
  local copies, waits for them, and re-layouts  8.57 us (5%)
    all_to_all x7, waiting for transfers between devices, swap(): return lax.all_to_all(array, axes, split_axis=0, concat_axis=0, tiled=True)  82.1 us
    all_to_all x3, blocking collectives, swap(): return lax.all_to_all(array, axes, split_axis=0, concat_axis=0, tiled=True)  32.9 us
    all_to_all x7, starting transfers between devices, swap(): return lax.all_to_all(array, axes, split_axis=0, concat_axis=0, tiled=True)  25.1 us
    pallas_call x11, Pallas kernels, call(): pl.pallas_call(kernel, out_shape=outs, in_specs=[vmem] * len(args), out_s...  22 us
    unnamed x28, local copies, waits for them, and re-layouts  7.55 us
  transfers between devices with their start and end apart: 7, of which 7 were waited for; matrix products, arithmetic and copies ran while one was open for 1% of the time, Pallas kernels for 4%

profile of v1, /device:TPU:0, one launch (start us, length us, event | category | flops | bytes accessed | tf_op | source)
XLA Modules:
  0.0 171.4 jit_solution(8851036744536889263)
XLA Ops:
  0.6 1.0 copy-done
  1.6 0.9 copy-done.4
  2.5 1.0 copy-done.9
  3.5 1.0 copy-done.10
  4.4 1.0 copy-done.11
  5.4 1.0 copy-done.12
  7.3 1.5 shard_map.121
  8.8 14.6 %all_to_all.50.second_ref = bf16[4,608,128]{2,1,0:T(8,128)(2,1)S(1)} all-to-all(bf16[4,608,128]{2,1,0:T(8,128)(2,1)S(1)} %get-tuple-element.18), channel_id=1, replica_groups=mesh['dp'=2,'tm'=4,'space'=4] {'space'}, dimensions={0} | all-to-all | bytes 1245184 | tf_op jit(solution)/shard_map/all_to_all | solution.py:358
  23.4 3.6 %all-to-all-start = ((bf16[4,3,288,128]{3,2,1,0:T(8,128)(2,1)}), bf16[4,3,288,128]{3,2,1,0:T(8,128)(2,1)S(1)}, u32[]{:S(2)}, u32[]{:S(2)}) async-start(bf16[4,3,288,128]{3,2,1,0:T(8,128)(2,1)} %get-tuple-element.16), calls=%async_computation | async-start | bytes 1769472 | tf_op jit(solution)/shard_map/all_to_all | solution.py:358
  27.1 1.1 shard_map.124
  28.2 9.5 %all-to-all-done.first_ref = bf16[4,3,288,128]{3,2,1,0:T(8,128)(2,1)S(1)} async-done(((bf16[4,3,288,128]{3,2,1,0:T(8,128)(2,1)}), bf16[4,3,288,128]{3,2,1,0:T(8,128)(2,1)S(1)}, u32[]{:S(2)}, u32[]{:S(2)}) %all-to-all-start) | async-done | bytes 884768 | tf_op jit(solution)/shard_map/all_to_all | solution.py:358
  37.8 4.9 %all-to-all-start.3 = ((bf16[4,4,32,1152]{3,2,1,0:T(8,128)(2,1)}), bf16[4,4,32,1152]{3,2,1,0:T(8,128)(2,1)S(1)}, u32[]{:S(2)}, u32[]{:S(2)}) async-start(bf16[4,4,32,1152]{3,2,1,0:T(8,128)(2,1)} %shard_map.124), calls=%async_computation.3 | async-start | bytes 2359296 | tf_op jit(solution)/shard_map/all_to_all | solution.py:358
  42.6 0.9 dynamic-slice_bitcast_fusion.at_ref
  43.6 2.9 %shard_map.122 = (bf16[3,2,288,256]{3,2,1,0:T(8,128)(2,1)S(1)}, bf16[4,288,128]{2,1,0:T(8,128)(2,1)S(1)}) custom-call(bf16[4,3,288,128]{3,2,1,0:T(8,128)(2,1)S(1)} %all-to-all-done.first_ref), custom_call_target="tpu_custom_call" | custom-call | bytes 2064384 | tf_op jit(solution)/shard_map/pallas_call | solution.py:30
  47.3 1.0 shard_map.123
  48.3 22.0 %all-to-all-done.3.time_ref = bf16[4,4,32,1152]{3,2,1,0:T(8,128)(2,1)S(1)} async-done(((bf16[4,4,32,1152]{3,2,1,0:T(8,128)(2,1)}), bf16[4,4,32,1152]{3,2,1,0:T(8,128)(2,1)S(1)}, u32[]{:S(2)}, u32[]{:S(2)}) %all-to-all-start.3) | async-done | bytes 1179680 | tf_op jit(solution)/shard_map/all_to_all | solution.py:358
  70.3 3.5 %all-to-all-start.4 = ((f32[16,8,128]{2,1,0:T(8,128)}), f32[16,8,128]{2,1,0:T(8,128)S(1)}, u32[]{:S(2)}, u32[]{:S(2)}) async-start(f32[16,8,128]{2,1,0:T(8,128)} %get-tuple-element.20), calls=%async_computation.4 | async-start | bytes 131072 | tf_op jit(solution)/shard_map/all_to_all | solution.py:358
  74.2 7.1 %all-to-all-done.4.codes_ref = f32[16,8,128]{2,1,0:T(8,128)S(1)} async-done(((f32[16,8,128]{2,1,0:T(8,128)}), f32[16,8,128]{2,1,0:T(8,128)S(1)}, u32[]{:S(2)}, u32[]{:S(2)}) %all-to-all-start.4) | async-done | bytes 65568 | tf_op jit(solution)/shard_map/all_to_all | solution.py:358
  81.3 5.6 %shard_map.126 = (bf16[4,32,1152]{2,1,0:T(8,128)(2,1)}, f32[16,8,128]{2,1,0:T(8,128)}, f32[32,1152]{1,0:T(8,128)S(1)}) custom-call(bf16[4,1152,128]{2,1,0:T(8,128)(2,1)S(1)} %shard_map.125.x_ref, f32[16,8,128]{2,1,0:T(8,128)S(1)} %all-to-all-done.4.codes_ref, bf16[4,16,1152]{2,1,0:T(8,128)(2,1)S(1)} %copy-done.5), custom_call_target="tpu_custom_call" | custom-call | bytes 1900544 | tf_op jit(solution)/shard_map/pallas_call | solution.py:30
  87.0 3.5 %all-to-all-start.6 = ((f32[16,8,128]{2,1,0:T(8,128)}), f32[16,8,128]{2,1,0:T(8,128)S(1)}, u32[]{:S(2)}, u32[]{:S(2)}) async-start(f32[16,8,128]{2,1,0:T(8,128)} %get-tuple-element.23), calls=%async_computation.6 | async-start | bytes 131072 | tf_op jit(solution)/shard_map/all_to_all | solution.py:358
  90.6 7.4 %all-to-all-done.6.codes_ref = f32[16,8,128]{2,1,0:T(8,128)S(1)} async-done(((f32[16,8,128]{2,1,0:T(8,128)}), f32[16,8,128]{2,1,0:T(8,128)S(1)}, u32[]{:S(2)}, u32[]{:S(2)}) %all-to-all-start.6) | async-done | bytes 65568 | tf_op jit(solution)/shard_map/all_to_all | solution.py:358
  98.0 6.4 %shard_map.128 = (bf16[4,32,896]{2,1,0:T(8,128)(2,1)S(1)}, f32[64,288]{1,0:T(8,128)S(1)}) custom-call(bf16[3,2,288,256]{3,2,1,0:T(8,128)(2,1)S(1)} %copy-done.3, bf16[4,288,128]{2,1,0:T(8,128)(2,1)} %get-tuple-element.19.hidden_ref, bf16[4,608,128]{2,1,0:T(8,128)(2,1)S(1)} %all_to_all.50.second_ref, f32[16,8,128]{2,1,0:T(8,128)S(1)} %all-to-all-done.6.codes_ref, ...), custom_call_target="tpu_custom_call" | custom-call | bytes 2392064 | tf_op jit(solution)/shard_map/pallas_call | solution.py:30
  104.5 8.0 %all_to_all.51.recv_ref = bf16[4,32,896]{2,1,0:T(8,128)(2,1)S(1)} all-to-all(bf16[4,32,896]{2,1,0:T(8,128)(2,1)S(1)} %get-tuple-element.25), channel_id=1, replica_groups=mesh['dp'=2,'tm'=4,'space'=4] {'space'}, dimensions={0} | all-to-all | bytes 458752 | tf_op jit(solution)/shard_map/all_to_all | solution.py:358
  112.5 3.5 %all-to-all-start.2 = ((bf16[4,288,128]{2,1,0:T(8,128)(2,1)}), bf16[4,288,128]{2,1,0:T(8,128)(2,1)S(1)}, u32[]{:S(2)}, u32[]{:S(2)}) async-start(bf16[4,288,128]{2,1,0:T(8,128)(2,1)} %get-tuple-element.19.hidden_ref), calls=%async_computation.2 | async-start | bytes 589824 | tf_op jit(solution)/shard_map/all_to_all | solution.py:358
  116.2 5.2 %all-to-all-done.2.hidden_ref = bf16[4,288,128]{2,1,0:T(8,128)(2,1)S(1)} async-done(((bf16[4,288,128]{2,1,0:T(8,128)(2,1)}), bf16[4,288,128]{2,1,0:T(8,128)(2,1)S(1)}, u32[]{:S(2)}, u32[]{:S(2)}) %all-to-all-start.2) | async-done | bytes 294944 | tf_op jit(solution)/shard_map/all_to_all | solution.py:358
  121.4 10.3 %all_to_all.52.recv_ref = f32[8,16,288]{2,1,0:T(8,128)S(1)} all-to-all(f32[8,16,288]{2,1,0:T(8,128)S(1)} %shard_map.129), channel_id=1, replica_groups=mesh['dp'=2,'tm'=4,'space'=4] {'dp','tm'}, dimensions={0} | all-to-all | bytes 294912 | tf_op jit(solution)/shard_map/all_to_all | solution.py:358
  131.7 3.5 %all-to-all-start.5 = ((bf16[4,32,1152]{2,1,0:T(8,128)(2,1)}), bf16[4,32,1152]{2,1,0:T(8,128)(2,1)S(1)}, u32[]{:S(2)}, u32[]{:S(2)}) async-start(bf16[4,32,1152]{2,1,0:T(8,128)(2,1)} %get-tuple-element.21), calls=%async_computation.5 | async-start | bytes 589824 | tf_op jit(solution)/shard_map/all_to_all | solution.py:358
  135.1 1.0 shard_map.130
  136.1 9.2 %all-to-all-done.5.out_ref = bf16[4,32,1152]{2,1,0:T(8,128)(2,1)S(1)} async-done(((bf16[4,32,1152]{2,1,0:T(8,128)(2,1)}), bf16[4,32,1152]{2,1,0:T(8,128)(2,1)S(1)}, u32[]{:S(2)}, u32[]{:S(2)}) %all-to-all-start.5) | async-done | bytes 294944 | tf_op jit(solution)/shard_map/all_to_all | solution.py:358
  145.3 2.6 %all-to-all-start.9 = ((f32[32,16,288]{2,1,0:T(8,128)}), f32[32,16,288]{2,1,0:T(8,128)S(1)}, u32[]{:S(2)}, u32[]{:S(2)}) async-start(f32[32,16,288]{2,1,0:T(8,128)} %shard_map.130), calls=%async_computation.9 | async-start | bytes 1572864 | tf_op jit(solution)/shard_map/all_to_all | solution.py:358
  148.8 21.6 %all-to-all-done.9.recv_ref = f32[32,16,288]{2,1,0:T(8,128)S(1)} async-done(((f32[32,16,288]{2,1,0:T(8,128)}), f32[32,16,288]{2,1,0:T(8,128)S(1)}, u32[]{:S(2)}, u32[]{:S(2)}) %all-to-all-start.9) | async-done | bytes 589856 | tf_op jit(solution)/shard_map/all_to_all | solution.py:358
  170.4 1.0 shard_map.131
  (26 shorter events, 3.4 us)
Async XLA Ops:
  0.6 1.0 copy-start
  1.6 0.9 copy-start.4
  2.5 1.0 copy-start.9
  3.5 1.0 copy-start.10
  4.4 1.0 copy-start.11
  5.4 1.0 copy-start.12
  6.4 0.9 copy-start.13
  23.4 3.7 %copy-start.1 = (bf16[1,2,64,1152]{3,2,1,0:T(8,128)(2,1)S(1)}, bf16[1,2,64,1152]{3,2,1,0:T(8,128)(2,1)}, u32[]{:S(2)}) copy-start(bf16[1,2,64,1152]{3,2,1,0:T(8,128)(2,1)} %g_ref.3) | copy-start | bytes 884740
  23.4 3.7 %copy-start.6 = (bf16[1,2,64,1152]{3,2,1,0:T(8,128)(2,1)S(1)}, bf16[1,2,64,1152]{3,2,1,0:T(8,128)(2,1)}, u32[]{:S(2)}) copy-start(bf16[1,2,64,1152]{3,2,1,0:T(8,128)(2,1)} %q_ref.3) | copy-start | bytes 884740
  23.4 3.7 %copy-start.7 = (bf16[1,2,64,1152]{3,2,1,0:T(8,128)(2,1)S(1)}, bf16[1,2,64,1152]{3,2,1,0:T(8,128)(2,1)}, u32[]{:S(2)}) copy-start(bf16[1,2,64,1152]{3,2,1,0:T(8,128)(2,1)} %k_ref.3) | copy-start | bytes 884740
  23.4 3.7 %copy-start.8 = (bf16[1,2,64,1152]{3,2,1,0:T(8,128)(2,1)S(1)}, bf16[1,2,64,1152]{3,2,1,0:T(8,128)(2,1)}, u32[]{:S(2)}) copy-start(bf16[1,2,64,1152]{3,2,1,0:T(8,128)(2,1)} %v_ref.3) | copy-start | bytes 884740
  23.4 14.3 %all-to-all-start = ((bf16[4,3,288,128]{3,2,1,0:T(8,128)(2,1)}), bf16[4,3,288,128]{3,2,1,0:T(8,128)(2,1)S(1)}, u32[]{:S(2)}, u32[]{:S(2)}) async-start(bf16[4,3,288,128]{3,2,1,0:T(8,128)(2,1)} %get-tuple-element.16), calls=%async_computation | async-start | bytes 1769472 | tf_op jit(solution)/shard_map/all_to_all | solution.py:358
  37.8 32.6 %all-to-all-start.3 = ((bf16[4,4,32,1152]{3,2,1,0:T(8,128)(2,1)}), bf16[4,4,32,1152]{3,2,1,0:T(8,128)(2,1)S(1)}, u32[]{:S(2)}, u32[]{:S(2)}) async-start(bf16[4,4,32,1152]{3,2,1,0:T(8,128)(2,1)} %shard_map.124), calls=%async_computation.3 | async-start | bytes 2359296 | tf_op jit(solution)/shard_map/all_to_all | solution.py:358
  46.4 0.9 copy-start.2
  70.3 11.0 %all-to-all-start.4 = ((f32[16,8,128]{2,1,0:T(8,128)}), f32[16,8,128]{2,1,0:T(8,128)S(1)}, u32[]{:S(2)}, u32[]{:S(2)}) async-start(f32[16,8,128]{2,1,0:T(8,128)} %get-tuple-element.20), calls=%async_computation.4 | async-start | bytes 131072 | tf_op jit(solution)/shard_map/all_to_all | solution.py:358
  73.8 7.5 %copy-start.5 = (bf16[4,16,1152]{2,1,0:T(8,128)(2,1)S(1)}, bf16[4,16,1152]{2,1,0:T(8,128)(2,1)}, u32[]{:S(2)}) copy-start(bf16[4,16,1152]{2,1,0:T(8,128)(2,1)} %b_ref.3) | copy-start | bytes 442372
  74.2 23.8 %copy-start.3 = (bf16[3,2,288,256]{3,2,1,0:T(8,128)(2,1)S(1)}, bf16[3,2,288,256]{3,2,1,0:T(8,128)(2,1)}, u32[]{:S(2)}) copy-start(bf16[3,2,288,256]{3,2,1,0:T(8,128)(2,1)} %copy-done.2) | copy-start | bytes 2654212
  87.0 11.0 %all-to-all-start.6 = ((f32[16,8,128]{2,1,0:T(8,128)}), f32[16,8,128]{2,1,0:T(8,128)S(1)}, u32[]{:S(2)}, u32[]{:S(2)}) async-start(f32[16,8,128]{2,1,0:T(8,128)} %get-tuple-element.23), calls=%async_computation.6 | async-start | bytes 131072 | tf_op jit(solution)/shard_map/all_to_all | solution.py:358
  112.5 8.9 %all-to-all-start.2 = ((bf16[4,288,128]{2,1,0:T(8,128)(2,1)}), bf16[4,288,128]{2,1,0:T(8,128)(2,1)S(1)}, u32[]{:S(2)}, u32[]{:S(2)}) async-start(bf16[4,288,128]{2,1,0:T(8,128)(2,1)} %get-tuple-element.19.hidden_ref), calls=%async_computation.2 | async-start | bytes 589824 | tf_op jit(solution)/shard_map/all_to_all | solution.py:358
  131.7 13.7 %all-to-all-start.5 = ((bf16[4,32,1152]{2,1,0:T(8,128)(2,1)}), bf16[4,32,1152]{2,1,0:T(8,128)(2,1)S(1)}, u32[]{:S(2)}, u32[]{:S(2)}) async-start(bf16[4,32,1152]{2,1,0:T(8,128)(2,1)} %get-tuple-element.21), calls=%async_computation.5 | async-start | bytes 589824 | tf_op jit(solution)/shard_map/all_to_all | solution.py:358
  145.3 25.1 %all-to-all-start.9 = ((f32[32,16,288]{2,1,0:T(8,128)}), f32[32,16,288]{2,1,0:T(8,128)S(1)}, u32[]{:S(2)}, u32[]{:S(2)}) async-start(f32[32,16,288]{2,1,0:T(8,128)} %shard_map.130), calls=%async_computation.9 | async-start | bytes 1572864 | tf_op jit(solution)/shard_map/all_to_all | solution.py:358

commit v2 on v1

v2 whole, which is shorter than its diff:
```python
import functools

import jax
import jax.numpy as jnp
from jax import lax
from jax.experimental import pallas as pl
from jax.experimental.pallas import tpu as pltpu
from jax.sharding import PartitionSpec as P

HEAD_DIM = 72
RANK = 16
SCALE = HEAD_DIM ** (-0.5)
F32 = jnp.float32
BF16 = jnp.bfloat16
NN = (((1,), (0,)), ((), ()))
NT = (((1,), (1,)), ((), ()))
TN = (((0,), (0,)), ((), ()))


def mm(a, b, dims=NN):
    return lax.dot_general(a, b, dims, preferred_element_type=F32)


def call(kernel, out_shape, *args, scratch=(), anywhere=False):
    vmem = pl.BlockSpec(memory_space=pltpu.VMEM)
    single = not isinstance(out_shape, (tuple, list))
    outs = (out_shape,) if single else tuple(out_shape)
    result = pl.pallas_call(
        kernel,
        out_shape=outs,
        in_specs=[pl.BlockSpec(memory_space=pl.ANY) if anywhere else vmem] * len(args),
        out_specs=tuple(vmem for _ in outs),
        scratch_shapes=list(scratch),
        compiler_params=pltpu.CompilerParams(vmem_limit_bytes=48 * 1024 * 1024),
    )(*args)
    return result[0] if single else list(result)


def shape(dims, dtype):
    return jax.ShapeDtypeStruct(tuple(dims), dtype)


def probs_of(keys, q_t, mask):
    scores = mm(keys, q_t) * SCALE
    if mask is not None:
        scores = jnp.where(mask, scores, -1e30)
    peak = jnp.max(scores, axis=0, keepdims=True)
    weights = jnp.exp(scores - peak)
    return weights / jnp.sum(weights, axis=0, keepdims=True)


def head_forward(q_t, k_t, v_t, mask=None):
    probs = probs_of(k_t.T, q_t, mask)
    return mm(v_t, probs.astype(BF16))


def head_backward(q_t, k_t, v_t, g_t, mask=None, forward=False):
    probs = probs_of(k_t.T, q_t, mask)
    low = probs.astype(BF16)
    dvals = mm(g_t, low, NT)
    dprob = mm(v_t.T, g_t)
    inner = jnp.sum(probs * dprob, axis=0, keepdims=True)
    dscore = (probs * (dprob - inner) * SCALE).astype(BF16)
    dquery = mm(k_t, dscore)
    out = mm(v_t, low) if forward else None
    return dquery, dvals, out


def rows_of(array, head):
    return array[head * HEAD_DIM : (head + 1) * HEAD_DIM]


def peer(axis, distance):
    return lax.axis_index(axis) ^ distance


def load_all(refs, buffers, sems):
    copies = [
        pltpu.make_async_copy(ref, buffer, sems.at[index])
        for index, (ref, buffer) in enumerate(zip(refs, buffers))
    ]
    for copy in copies:
        copy.start()
    return copies


def pack_time_kernel(n_t, sub, q_ref, k_ref, v_ref, g_ref, *rest):
    outs, sems = rest[:n_t], rest[n_t]
    frames = q_ref.shape[1]
    copies = []
    for k in range(n_t):
        start = pl.multiple_of(peer("tm", k) * sub, sub)
        for index, ref in enumerate((q_ref, k_ref, v_ref, g_ref)):
            for f in range(frames):
                copy = pltpu.make_async_copy(
                    ref.at[0, f, pl.ds(start, sub)],
                    outs[k].at[index, f * sub : (f + 1) * sub],
                    sems.at[len(copies)],
                )
                copy.start()
                copies.append(copy)
    for copy in copies:
        copy.wait()


def pack_space_kernel(n_s, *refs):
    ins, refs = refs[:7], refs[7:]
    firsts, seconds, buffers = refs[:n_s], refs[n_s : 2 * n_s], refs[2 * n_s : 2 * n_s + 7]
    turned_ref, sems = refs[2 * n_s + 7 :]
    p_buf, at_buf, b_buf, q_buf, v_buf, k_buf, g_buf = buffers
    copies = load_all(ins, buffers, sems)
    d_s, tokens = firsts[0].shape[1:]

    def flat(ref):
        return ref[0].reshape(tokens, ref.shape[3])

    def send(array, targets, index):
        turned = array.T
        for j in range(n_s):
            turned_ref[index, j] = turned[j * d_s : (j + 1) * d_s]
        for k in range(n_s):
            targets(k)[...] = turned_ref[index, peer("space", k)]

    copies[0].wait()
    copies[1].wait()
    copies[2].wait()
    patches = flat(p_buf)
    codes_q = mm(patches, at_buf[0], NT).astype(BF16)
    codes_v = mm(patches, at_buf[1], NT).astype(BF16)
    codes_t = jnp.concatenate([codes_q, codes_v], axis=1).T
    copies[3].wait()
    query = (flat(q_buf).astype(F32) + mm(codes_q, b_buf[0])).astype(BF16)
    send(query, lambda k: firsts[k].at[0], 0)
    copies[4].wait()
    value = (flat(v_buf).astype(F32) + mm(codes_v, b_buf[1])).astype(BF16)
    send(value, lambda k: firsts[k].at[2], 1)
    copies[5].wait()
    send(flat(k_buf), lambda k: firsts[k].at[1], 2)
    send(patches, lambda k: seconds[k].at[:d_s], 3)
    copies[6].wait()
    send(flat(g_buf), lambda k: seconds[k].at[d_s : 2 * d_s], 4)
    for k in range(n_s):
        seconds[k][2 * d_s :] = codes_t


def frame_rows(pieces, f, patch_dev):
    return jnp.concatenate([x[:, f * patch_dev : (f + 1) * patch_dev] for x in pieces], axis=1)


def space_forward_kernel(frames, n_s, *refs):
    firsts, qkv_ref, outs = refs[:n_s], refs[n_s], refs[n_s + 1 :]
    _, d_s, tokens = firsts[0].shape
    patch_dev = tokens // frames
    total = n_s * patch_dev
    step = min(total, 256)
    for index in range(3):
        pieces = [first[index] for first in firsts]
        for f in range(frames):
            qkv_ref[index, f] = frame_rows(pieces, f, patch_dev)
    for f in range(frames):
        query = qkv_ref[0, f].astype(F32)
        keys = qkv_ref[1, f].astype(F32)
        vals = qkv_ref[2, f].astype(F32)
        heads = []
        for h in range(d_s // HEAD_DIM):
            k_h = rows_of(keys, h).astype(BF16)
            v_h = rows_of(vals, h).astype(BF16)
            q_h = rows_of(query, h).astype(BF16)
            parts = [
                head_forward(q_h[:, s : s + step], k_h, v_h) for s in range(0, total, step)
            ]
            heads.append(parts[0] if len(parts) == 1 else jnp.concatenate(parts, axis=1))
        out = jnp.concatenate(heads, axis=0).astype(BF16)
        for k in range(n_s):
            outs[k][:, f * patch_dev : (f + 1) * patch_dev] = out[
                :, k * patch_dev : (k + 1) * patch_dev
            ]


def lane_block(rows):
    return lax.broadcasted_iota(jnp.int32, (rows, 128), 1) // (2 * RANK)


def fold(token_rows):
    block = lane_block(8)
    result = token_rows[0:8]
    for k in range(1, 4):
        result = jnp.where(block == k, token_rows[8 * k : 8 * k + 8], result)
    return result


def unfold(folded):
    pieces = [folded]
    for k in range(1, 4):
        pieces.append(pltpu.roll(folded, 128 - 2 * RANK * k, 1))
    return jnp.concatenate(pieces, axis=0)


def hidden_kernel(n_t, n_s, *refs):
    pieces, refs = refs[:n_s], refs[n_s:]
    p_ref, at_ref, hidden_ref = refs[:3]
    sends = refs[3 : 3 + n_t]
    out_buf, codes_buf = refs[3 + n_t :]
    _, frames, patch_dev, width = p_ref.shape
    tokens = frames * patch_dev
    sub = patch_dev // n_t
    for k in range(n_s):
        out_buf[peer("space", k)] = pieces[k][...]
    out = out_buf[...].reshape(width, tokens).T
    hidden = (p_ref[0].reshape(tokens, width).astype(F32) + out.astype(F32)).astype(BF16)
    hidden_ref[...] = hidden
    downs = jnp.concatenate([at_ref[2], at_ref[3]] * 4, axis=0)
    codes_buf[...] = mm(hidden, downs, NT).astype(BF16).astype(F32)
    for k in range(n_t):
        rows = [
            codes_buf[pl.ds(pl.multiple_of(f * patch_dev + peer("tm", k) * sub, sub), sub)]
            for f in range(frames)
        ]
        sends[k][...] = fold(jnp.concatenate(rows, axis=0))


def turn_kernel(*refs):
    pieces, out_ref = refs[:-1], refs[-1]
    for index in range(4):
        rows = jnp.concatenate([piece[index] for piece in pieces], axis=0)
        out_ref[index] = rows.T


def time_kernel(n_t, sub, x_ref, b_ref, *refs):
    codes_refs, refs = refs[:n_t], refs[n_t:]
    outs, sends, grad_b_ref = refs[:n_t], refs[n_t : 2 * n_t], refs[2 * n_t]
    _, width, tokens = x_ref.shape
    codes = jnp.concatenate([unfold(ref[...]) for ref in codes_refs], axis=0).T
    codes_q = codes[:RANK].astype(BF16)
    codes_v = codes[RANK : 2 * RANK].astype(BF16)
    query = (x_ref[0].astype(F32) + mm(b_ref[2], codes_q, TN)).astype(BF16).astype(F32)
    vals = (x_ref[2].astype(F32) + mm(b_ref[3], codes_v, TN)).astype(BF16).astype(F32)
    keys = x_ref[1].astype(F32)
    grad = x_ref[3].astype(F32)
    row = lax.broadcasted_iota(jnp.int32, (tokens, tokens), 0)
    col = lax.broadcasted_iota(jnp.int32, (tokens, tokens), 1)
    mask = lax.rem(row, sub) == lax.rem(col, sub)
    outs_h, d_query, d_vals = [], [], []
    for h in range(width // HEAD_DIM):
        dq, dv, out = head_backward(
            rows_of(query, h).astype(BF16),
            rows_of(keys, h).astype(BF16),
            rows_of(vals, h).astype(BF16),
            rows_of(grad, h).astype(BF16),
            mask,
            True,
        )
        outs_h.append(out)
        d_query.append(dq)
        d_vals.append(dv)
    d_query = jnp.concatenate(d_query, axis=0).astype(BF16)
    d_vals = jnp.concatenate(d_vals, axis=0).astype(BF16)
    d_codes = jnp.concatenate([mm(b_ref[2], d_query), mm(b_ref[3], d_vals)] * 4, axis=0)
    d_codes = d_codes.astype(BF16).astype(F32).T
    per = tokens // n_t
    for k in range(n_t):
        sends[k][...] = fold(d_codes[k * per : (k + 1) * per])
    out = jnp.concatenate(outs_h, axis=0).astype(BF16).T
    for k in range(n_t):
        outs[k][...] = out[k * per : (k + 1) * per]
    grad_b_ref[:RANK] = mm(codes_q, d_query, NT)
    grad_b_ref[RANK:] = mm(codes_v, d_vals, NT)


def place_codes_kernel(frames, sub, *refs):
    pieces, (out_ref, buf) = refs[:-2], refs[-2:]
    patch_dev = sub * len(pieces)
    for k, piece in enumerate(pieces):
        rows = unfold(piece[...])
        for f in range(frames):
            start = pl.multiple_of(f * patch_dev + peer("tm", k) * sub, sub)
            buf[pl.ds(start, sub)] = rows[f * sub : (f + 1) * sub]
    out_ref[...] = buf[...].T[: 2 * RANK].astype(BF16)


def space_backward_kernel(frames, n_s, qkv_ref, hidden_ref, grad_b_ref, at_ref, at_here_ref, b_here_ref, *refs):
    seconds, dcodes, sends = refs[:n_s], refs[n_s : 2 * n_s], refs[2 * n_s : 3 * n_s]
    part_ref, cut_buf = refs[3 * n_s :]
    d_s = part_ref.shape[1]
    tokens = hidden_ref.shape[0]
    patch_dev = tokens // frames
    total = n_s * patch_dev
    step = min(total, 256)
    ups = jnp.concatenate([at_here_ref[2], at_here_ref[3]], axis=0).T
    grads = []
    for k in range(n_s):
        cot = seconds[k][d_s : 2 * d_s].astype(F32)
        grads.append((cot + mm(ups, dcodes[k][...])).astype(BF16))
    grad_b_q = grad_b_v = None
    codes = [second[2 * d_s :] for second in seconds]
    for f in range(frames):
        query = qkv_ref[0, f].astype(F32)
        keys = qkv_ref[1, f].astype(F32)
        vals = qkv_ref[2, f].astype(F32)
        grad = frame_rows(grads, f, patch_dev).astype(F32)
        d_query, d_vals = [], []
        for h in range(d_s // HEAD_DIM):
            k_h = rows_of(keys, h).astype(BF16)
            v_h = rows_of(vals, h).astype(BF16)
            q_h = rows_of(query, h).astype(BF16)
            g_h = rows_of(grad, h).astype(BF16)
            dq_parts, dv_sum = [], None
            for s in range(0, total, step):
                dq, dv, _ = head_backward(q_h[:, s : s + step], k_h, v_h, g_h[:, s : s + step])
                dq_parts.append(dq)
                dv_sum = dv if dv_sum is None else dv_sum + dv
            d_query.append(
                dq_parts[0] if len(dq_parts) == 1 else jnp.concatenate(dq_parts, axis=1)
            )
            d_vals.append(dv_sum)
        d_query = jnp.concatenate(d_query, axis=0).astype(BF16)
        d_vals = jnp.concatenate(d_vals, axis=0).astype(BF16)
        partial = jnp.concatenate([mm(b_here_ref[0], d_query), mm(b_here_ref[1], d_vals)], axis=0)
        partial = partial.astype(BF16)
        blocks = [partial[:, m * patch_dev : (m + 1) * patch_dev] for m in range(n_s)]
        for k in range(n_s):
            turned = jnp.concatenate([blocks[m ^ k] for m in range(n_s)], axis=1)
            sends[k][:, f * total : (f + 1) * total] = turned
        frame_codes = frame_rows(codes, f, patch_dev)
        term_q = mm(frame_codes[:RANK], d_query, NT)
        term_v = mm(frame_codes[RANK:], d_vals, NT)
        grad_b_q = term_q if grad_b_q is None else grad_b_q + term_q
        grad_b_v = term_v if grad_b_v is None else grad_b_v + term_v
    part_ref[:RANK] = grad_b_q
    part_ref[RANK:] = grad_b_v
    grad_a = mm(dcodes[0][...], hidden_ref[...])
    pad = -(-d_s // 128) * 128
    for j in range(n_s):
        cut_buf[j, 0, :, :d_s] = grad_a[:, j * d_s : (j + 1) * d_s].astype(BF16)
        cut_buf[j, 1, :, :d_s] = grad_b_ref[:, j * d_s : (j + 1) * d_s].astype(BF16)
    for k in range(n_s):
        for index in range(2):
            start = frames * total + index * pad
            sends[k][:, start : start + pad] = cut_buf[peer("space", k), index]


def add_up(terms):
    result = None
    for term in terms:
        result = term if result is None else result + term
    return result


def merge_kernel(frames, n_s, n_d, part_ref, *refs):
    seconds, recvs, refs = refs[:n_s], refs[n_s : 2 * n_s], refs[2 * n_s :]
    sends, buf = refs[:n_d], refs[n_d]
    d_s = part_ref.shape[1]
    tokens = seconds[0].shape[1]
    patch_dev = tokens // frames
    total = n_s * patch_dev
    pad = -(-d_s // 128) * 128
    patches = [second[:d_s] for second in seconds]
    terms = []
    for f in range(frames):
        codes = [recv[:, f * total : (f + 1) * total].astype(F32) for recv in recvs]
        terms.append(mm(add_up(codes).astype(BF16), frame_rows(patches, f, patch_dev), NT))
    start = frames * total
    time_a = add_up([recv[:, start : start + d_s].astype(F32) for recv in recvs])
    time_b = add_up([recv[:, start + pad : start + pad + d_s].astype(F32) for recv in recvs])
    rows = jnp.concatenate([add_up(terms), time_a, part_ref[...], time_b], axis=0)
    per = rows.shape[0] // n_d
    for d in range(n_d):
        buf[d] = rows[d * per : (d + 1) * per]
    for k in range(n_d):
        sends[k][...] = buf[peer("dp", k)]


def total_kernel(*refs):
    refs[-1][...] = add_up([ref[...].astype(F32) for ref in refs[:-1]]).astype(refs[-1].dtype)


def join_kernel(*refs):
    pieces, (out_ref, buf) = refs[:-2], refs[-2:]
    for k, piece in enumerate(pieces):
        buf[peer("space", k)] = piece[...]
    out_ref[...] = jnp.concatenate([buf[j] for j in range(len(pieces))], axis=1)


def final_kernel(factor, n_d, *refs):
    pieces, (a_ref, b_ref, buf) = refs[:n_d], refs[n_d:]
    for k, piece in enumerate(pieces):
        buf[peer("dp", k)] = piece[...]
    per = pieces[0].shape[0]
    half = n_d // 2
    for d in range(n_d):
        rows = buf[d].astype(F32) * factor
        target = a_ref if d < half else b_ref
        for r in range(0, per, min(per, RANK)):
            start = (d % half) * per + r
            size = min(per, RANK)
            target[start // RANK, start % RANK : start % RANK + size] = rows[r : r + size]


def mixed_kernel(frames, hidden_ref, *refs):
    pieces, (mixed_ref, buf) = refs[:-2], refs[-2:]
    n_t = len(pieces)
    tokens, width = hidden_ref.shape
    patch_dev = tokens // frames
    sub = patch_dev // n_t
    for k, piece in enumerate(pieces):
        for f in range(frames):
            start = pl.multiple_of(f * patch_dev + peer("tm", k) * sub, sub)
            buf[pl.ds(start, sub)] = piece[f * sub : (f + 1) * sub]
    total = hidden_ref[...].astype(F32) + buf[...].astype(F32)
    mixed_ref[0] = total.astype(BF16).reshape(frames, patch_dev, width)


def exchange(pieces, axis):
    size = lax.axis_size(axis)
    return [pieces[0]] + [
        lax.ppermute(pieces[k], axis, [(i, i ^ k) for i in range(size)]) for k in range(1, size)
    ]


def share(array, axis):
    return exchange([array] * lax.axis_size(axis), axis)


def per_device(
    patches, query_s, key_s, value_s, query_t, key_t, value_t, adapters_a, adapters_b, cotangent
):
    _, frames, patch_dev, width = patches.shape
    n_d, n_t, n_s = (lax.axis_size(name) for name in ("dp", "tm", "space"))
    tokens = frames * patch_dev
    sub = patch_dev // n_t
    d_s = width // n_s
    total = n_s * patch_dev
    factor = (tokens * n_d * n_t * n_s) ** (-0.5)
    here = lax.axis_index("space") * d_s
    downs = jnp.swapaxes(adapters_a, 1, 2)
    downs_here = lax.dynamic_slice_in_dim(downs, here, d_s, 2)
    ups_here = lax.dynamic_slice_in_dim(adapters_b, here, d_s, 2)
    dma = pltpu.SemaphoreType.DMA
    pad = -(-d_s // 128) * 128

    time_pieces = exchange(
        call(
            functools.partial(pack_time_kernel, n_t, sub),
            [shape((4, frames * sub, width), BF16)] * n_t,
            query_t, key_t, value_t, cotangent,
            scratch=[dma((4 * frames * n_t,))],
            anywhere=True,
        ),
        "tm",
    )
    packed = call(
        functools.partial(pack_space_kernel, n_s),
        [shape((3, d_s, tokens), BF16)] * n_s + [shape((2 * d_s + 2 * RANK, tokens), BF16)] * n_s,
        patches, downs, adapters_b, query_s, value_s, key_s, cotangent,
        scratch=[
            pltpu.VMEM(x.shape, BF16)
            for x in (patches, downs, adapters_b, query_s, value_s, key_s, cotangent)
        ]
        + [pltpu.VMEM((5, n_s, d_s, tokens), BF16), dma((7,))],
        anywhere=True,
    )
    firsts = exchange(packed[:n_s], "space")
    seconds = exchange(packed[n_s:], "space")
    qkv, *out_s = call(
        functools.partial(space_forward_kernel, frames, n_s),
        [shape((3, frames, d_s, total), BF16)] + [shape((d_s, tokens), BF16)] * n_s,
        *firsts,
    )
    out_s = exchange(out_s, "space")
    hidden, *codes = call(
        functools.partial(hidden_kernel, n_t, n_s),
        [shape((tokens, width), BF16)] + [shape((8, 128), F32)] * n_t,
        *out_s, patches, downs,
        scratch=[pltpu.VMEM((n_s, d_s, tokens), BF16), pltpu.VMEM((tokens, 128), F32)],
    )
    codes = exchange(codes, "tm")
    turned = call(turn_kernel, shape((4, width, n_t * frames * sub), BF16), *time_pieces)
    timed = call(
        functools.partial(time_kernel, n_t, sub),
        [shape((frames * sub, width), BF16)] * n_t
        + [shape((8, 128), F32)] * n_t
        + [shape((2 * RANK, width), F32)],
        turned, adapters_b, *codes,
    )
    out_t, dcodes, time_grad_b = timed[:n_t], timed[n_t : 2 * n_t], timed[2 * n_t]
    dcodes = exchange(dcodes, "tm")
    dcodes = call(
        functools.partial(place_codes_kernel, frames, sub),
        shape((2 * RANK, tokens), BF16),
        *dcodes,
        scratch=[pltpu.VMEM((tokens, 128), F32)],
    )
    dcodes = share(dcodes, "space")
    *partial, part = call(
        functools.partial(space_backward_kernel, frames, n_s),
        [shape((2 * RANK, frames * total + 2 * pad), BF16)] * n_s + [shape((2 * RANK, d_s), F32)],
        qkv, hidden, time_grad_b, downs, downs_here, ups_here, *seconds, *dcodes,
        scratch=[pltpu.VMEM((n_s, 2, 2 * RANK, pad), BF16)],
    )
    partial = exchange(partial, "space")
    rows = 8 * RANK // n_d
    sums = call(
        functools.partial(merge_kernel, frames, n_s, n_d),
        [shape((rows, d_s), F32)] * n_d,
        part, *seconds, *partial,
        scratch=[pltpu.VMEM((n_d, rows, d_s), F32)],
    )
    sums = call(total_kernel, shape((rows, d_s), BF16), *exchange(sums, "dp"))
    sums = call(total_kernel, shape((rows, d_s), BF16), *share(sums, "tm"))
    sums = call(
        join_kernel,
        shape((rows, width), BF16),
        *share(sums, "space"),
        scratch=[pltpu.VMEM((n_s, rows, d_s), BF16)],
    )
    grads_a, grads_b = call(
        functools.partial(final_kernel, factor, n_d),
        [shape((4, RANK, width), F32)] * 2,
        *share(sums, "dp"),
        scratch=[pltpu.VMEM((n_d, rows, width), BF16)],
    )
    mixed = call(
        functools.partial(mixed_kernel, frames),
        shape(patches.shape, BF16),
        hidden, *exchange(out_t, "tm"),
        scratch=[pltpu.VMEM((tokens, width), BF16)],
    )
    return (mixed, jnp.swapaxes(grads_a, 1, 2), grads_b)


def solution(mesh):
    token = P("dp", "tm", "space", None)
    return jax.shard_map(
        per_device,
        mesh=mesh,
        in_specs=(token,) * 7 + (P(), P(), token),
        out_specs=(token, P(), P()),
        check_vma=False,
    )
```

time: 172 us -> 111 us (0.65)
  waiting for transfers between devices: 82.1 us -> 32.2 us
  blocking collectives: 32.9 us -> 0 us
  starting transfers between devices: 25.1 us -> 50.5 us
  local copies, waits for them, and re-layouts: 8.57 us -> 6.82 us
    all_to_all x7 -> x0, waiting for transfers between devices: 82.1 us -> none  [swap(): return lax.all_to_all(array, axes, split_axis=0, concat_axis=0, tiled=True)]
    ppermute x0 -> x35, starting transfers between devices: none -> 50.5 us  [exchange(): lax.ppermute(pieces[k], axis, [(i, i ^ k) for i in range(size)])]
    all_to_all x3 -> x0, blocking collectives: 32.9 us -> none  [swap(): return lax.all_to_all(array, axes, split_axis=0, concat_axis=0, tiled=True)]
    ppermute x0 -> x35, waiting for transfers between devices: none -> 32.2 us  [exchange(): lax.ppermute(pieces[k], axis, [(i, i ^ k) for i in range(size)])]
    all_to_all x7 -> x0, starting transfers between devices: 25.1 us -> none  [swap(): return lax.all_to_all(array, axes, split_axis=0, concat_axis=0, tiled=True)]
    pallas_call x11 -> x14, Pallas kernels: 22 us -> 20.3 us  [call(): pl.pallas_call(kernel, out_shape=outs, in_specs=[pl.BlockSpec(memory_spac...]
  transfers between devices with their start and end apart: 7 -> 35, of which waited for: 7 -> 21; matrix products, arithmetic and copies ran while one was open for 1% -> 0% of each run, Pallas kernels for 4% -> 10%
where the time goes in v2:
time: 111 us
  starting transfers between devices  50.5 us (45%)
  waiting for transfers between devices  32.2 us (29%)
  Pallas kernels  20.3 us (18%)
  local copies, waits for them, and re-layouts  6.82 us (6%)
    ppermute x35, starting transfers between devices, exchange(): lax.ppermute(pieces[k], axis, [(i, i ^ k) for i in range(size)])  50.5 us
    ppermute x35, waiting for transfers between devices, exchange(): lax.ppermute(pieces[k], axis, [(i, i ^ k) for i in range(size)])  32.2 us
    pallas_call x14, Pallas kernels, call(): pl.pallas_call(kernel, out_shape=outs, in_specs=[pl.BlockSpec(memory_spac...  20.3 us
    unnamed x28, local copies, waits for them, and re-layouts  6.65 us
  transfers between devices with their start and end apart: 35, of which 21 were waited for; matrix products, arithmetic and copies ran while one was open for 0% of the time, Pallas kernels for 10%

profile of v2, /device:TPU:0, one launch (start us, length us, event | category | flops | bytes accessed | tf_op | source)
XLA Modules:
  0.0 110.6 jit_solution(10578238383922568393)
XLA Ops:
  7.3 2.2 %shard_map.121 = (bf16[3,288,128]{2,1,0:T(8,128)(2,1)S(1)}, bf16[3,288,128]{2,1,0:T(8,128)(2,1)S(1)}, bf16[3,288,128]{2,1,0:T(8,128)(2,1)S(1)}, bf16[3,288,128]{...) custom-call(bf16[1,2,64,1152]{3,2,1,0:T(8,128)(2,1)S(1)} %copy-done., ...), custom_call_target="tpu_custom_call" | custom-call | tf_op jit(solution)/shard_map/pallas_call | solution.py:28
  9.6 3.0 %collective-permute-start = (bf16[3,288,128]{2,1,0:T(8,128)(2,1)S(1)}, bf16[3,288,128]{2,1,0:T(8,128)(2,1)S(1)}, u32[]{:S(2)}, u32[]{:S(2)}) collective-permute-start(bf16[3,288,128]{2,1,0:T(8,128)(2,1)S(1)} %get-tuple-element.44), channel_id=1, source_target_pairs={{0,1},{1,0},{2,3},{3,2},{4,5},{5,4},{6,7},{7,6},{8,9},{9,8},{10,11... | collective-permute-start | bytes 663560 | tf_op jit(solution)/shard_map/ppermute | solution.py:416
  12.6 1.6 %collective-permute-start.1 = (bf16[3,288,128]{2,1,0:T(8,128)(2,1)S(1)}, bf16[3,288,128]{2,1,0:T(8,128)(2,1)S(1)}, u32[]{:S(2)}, u32[]{:S(2)}) collective-permute-start(bf16[3,288,128]{2,1,0:T(8,128)(2,1)S(1)} %get-tuple-element.45), channel_id=1, source_target_pairs={{0,2},{1,3},{2,0},{3,1},{4,6},{5,7},{6,4},{7,5},{8,10},{9,11},{10,... | collective-permute-start | bytes 663560 | tf_op jit(solution)/shard_map/ppermute | solution.py:416
  14.2 1.9 %shard_map.124 = (bf16[4,32,1152]{2,1,0:T(8,128)(2,1)S(1)}, bf16[4,32,1152]{2,1,0:T(8,128)(2,1)S(1)}, bf16[4,32,1152]{2,1,0:T(8,128)(2,1)S(1)}, bf16[4,32,1152]{2,1,0:T(8,128)(2,1)S(1)}) custom-call(bf16[1,2,64,1152]{3,2,1,0:T(8,128)(2,1)S(1)} %copy-done.11, bf16[1,2,64,1152]{3,2,1,0:T(8,128)(2,1)S(1)} %copy-done.12, ...), custom_call_target="tpu_custom_call" | custom-call | tf_op jit(solution)/shard_map/pallas_call | solution.py:28
  16.1 2.0 %collective-permute-start.6 = (bf16[4,32,1152]{2,1,0:T(8,128)(2,1)S(1)}, bf16[4,32,1152]{2,1,0:T(8,128)(2,1)S(1)}, u32[]{:S(2)}, u32[]{:S(2)}) collective-permute-start(bf16[4,32,1152]{2,1,0:T(8,128)(2,1)S(1)} %get-tuple-element.53), channel_id=1, source_target_pairs={{0,4},{4,0},{8,12},{12,8},{1,5},{5,1},{9,13},{13,9},{2,6},{6,2},{1... | collective-permute-start | bytes 884744 | tf_op jit(solution)/shard_map/ppermute | solution.py:416
  18.1 2.6 %collective-permute-start.7 = (bf16[4,32,1152]{2,1,0:T(8,128)(2,1)S(1)}, bf16[4,32,1152]{2,1,0:T(8,128)(2,1)S(1)}, u32[]{:S(2)}, u32[]{:S(2)}) collective-permute-start(bf16[4,32,1152]{2,1,0:T(8,128)(2,1)S(1)} %get-tuple-element.54), channel_id=1, source_target_pairs={{0,8},{4,12},{8,0},{12,4},{1,9},{5,13},{9,1},{13,5},{2,10},{6,14},... | collective-permute-start | bytes 884744 | tf_op jit(solution)/shard_map/ppermute | solution.py:416
  20.7 2.3 %collective-permute-start.8 = (bf16[4,32,1152]{2,1,0:T(8,128)(2,1)S(1)}, bf16[4,32,1152]{2,1,0:T(8,128)(2,1)S(1)}, u32[]{:S(2)}, u32[]{:S(2)}) collective-permute-start(bf16[4,32,1152]{2,1,0:T(8,128)(2,1)S(1)} %get-tuple-element.55), channel_id=1, source_target_pairs={{0,12},{4,8},{8,4},{12,0},{1,13},{5,9},{9,5},{13,1},{2,14},{6,10},... | collective-permute-start | bytes 884744 | tf_op jit(solution)/shard_map/ppermute | solution.py:416
  24.2 2.9 %shard_map.122 = (bf16[3,2,288,256]{3,2,1,0:T(8,128)(2,1)S(1)}, bf16[288,128]{1,0:T(8,128)(2,1)S(1)}, bf16[288,128]{1,0:T(8,128)(2,1)S(1)}, bf16[288,128]{1,0:T(8,128)(2,1)S(1)}, bf16[288,128]{1,0:T(8,128)(2,1)S(1)}) custom-call(bf16[3,288,128]{2,1,0:T(8,128)(2,1)S(1)} %get-tuple-element.43.refs_0_, bf16[3,288,128]{2,1,0:T(8,128)(2,1)S(1)} %collective-permute-done.refs_1_, ...), custom_call_target="tpu_custom_call" | custom-call | tf_op jit(solution)/shard_map/pallas_call | solution.py:28
  29.2 2.3 %collective-permute-done.3.refs_1_ = bf16[288,128]{1,0:T(8,128)(2,1)S(1)} collective-permute-done((bf16[288,128]{1,0:T(8,128)(2,1)S(1)}, bf16[288,128]{1,0:T(8,128)(2,1)S(1)}, u32[]{:S(2)}, u32[]{:S(2)}) %collective-permute-start.3) | collective-permute-done | bytes 73760 | tf_op jit(solution)/shard_map/ppermute | solution.py:416
  31.5 1.5 %collective-permute-start.5 = (bf16[288,128]{1,0:T(8,128)(2,1)S(1)}, bf16[288,128]{1,0:T(8,128)(2,1)S(1)}, u32[]{:S(2)}, u32[]{:S(2)}) collective-permute-start(bf16[288,128]{1,0:T(8,128)(2,1)S(1)} %get-tuple-element.50), channel_id=1, source_target_pairs={{0,3},{1,2},{2,1},{3,0},{4,7},{5,6},{6,5},{7,4},{8,11},{9,10},{10,... | collective-permute-start | bytes 221192 | tf_op jit(solution)/shard_map/ppermute | solution.py:416
  33.0 1.6 %collective-permute-start.15 = (bf16[608,128]{1,0:T(8,128)(2,1)S(1)}, bf16[608,128]{1,0:T(8,128)(2,1)S(1)}, u32[]{:S(2)}, u32[]{:S(2)}) collective-permute-start(bf16[608,128]{1,0:T(8,128)(2,1)S(1)} %get-tuple-element.67), channel_id=1, source_target_pairs={{0,1},{1,0},{2,3},{3,2},{4,5},{5,4},{6,7},{7,6},{8,9},{9,8},{10,11... | collective-permute-start | bytes 466952 | tf_op jit(solution)/shard_map/ppermute | solution.py:416
  34.5 2.2 %collective-permute-done.5.refs_3_ = bf16[288,128]{1,0:T(8,128)(2,1)S(1)} collective-permute-done((bf16[288,128]{1,0:T(8,128)(2,1)S(1)}, bf16[288,128]{1,0:T(8,128)(2,1)S(1)}, u32[]{:S(2)}, u32[]{:S(2)}) %collective-permute-start.5) | collective-permute-done | bytes 73760 | tf_op jit(solution)/shard_map/ppermute | solution.py:416
  37.1 1.6 %collective-permute-start.9 = (f32[8,128]{1,0:T(8,128)S(1)}, f32[8,128]{1,0:T(8,128)S(1)}, u32[]{:S(2)}, u32[]{:S(2)}) collective-permute-start(f32[8,128]{1,0:T(8,128)S(1)} %get-tuple-element.57), channel_id=1, source_target_pairs={{0,4},{4,0},{8,12},{12,8},{1,5},{5,1},{9,13},{13,9},{2,6},{6,2},{1... | collective-permute-start | bytes 12296 | tf_op jit(solution)/shard_map/ppermute | solution.py:416
  38.7 2.6 %collective-permute-start.10 = (f32[8,128]{1,0:T(8,128)S(1)}, f32[8,128]{1,0:T(8,128)S(1)}, u32[]{:S(2)}, u32[]{:S(2)}) collective-permute-start(f32[8,128]{1,0:T(8,128)S(1)} %get-tuple-element.58), channel_id=1, source_target_pairs={{0,8},{4,12},{8,0},{12,4},{1,9},{5,13},{9,1},{13,5},{2,10},{6,14},... | collective-permute-start | bytes 12296 | tf_op jit(solution)/shard_map/ppermute | solution.py:416
  41.6 2.5 %collective-permute-start.11 = (f32[8,128]{1,0:T(8,128)S(1)}, f32[8,128]{1,0:T(8,128)S(1)}, u32[]{:S(2)}, u32[]{:S(2)}) collective-permute-start(f32[8,128]{1,0:T(8,128)S(1)} %get-tuple-element.59), channel_id=1, source_target_pairs={{0,12},{4,8},{8,4},{12,0},{1,13},{5,9},{9,5},{13,1},{2,14},{6,10},... | collective-permute-start | bytes 12296 | tf_op jit(solution)/shard_map/ppermute | solution.py:416
  47.0 4.9 %shard_map.126 = (bf16[32,1152]{1,0:T(8,128)(2,1)S(1)}, bf16[32,1152]{1,0:T(8,128)(2,1)S(1)}, bf16[32,1152]{1,0:T(8,128)(2,1)S(1)}, bf16[32,1152]{1,0:T(8,128)(2...) custom-call(bf16[4,1152,128]{2,1,0:T(8,128)(2,1)S(1)} %shard_map.125, ...), custom_call_target="tpu_custom_call" | custom-call | tf_op jit(solution)/shard_map/pallas_call | solution.py:28
  52.3 1.5 %collective-permute-start.16 = (bf16[608,128]{1,0:T(8,128)(2,1)S(1)}, bf16[608,128]{1,0:T(8,128)(2,1)S(1)}, u32[]{:S(2)}, u32[]{:S(2)}) collective-permute-start(bf16[608,128]{1,0:T(8,128)(2,1)S(1)} %get-tuple-element.68), channel_id=1, source_target_pairs={{0,2},{1,3},{2,0},{3,1},{4,6},{5,7},{6,4},{7,5},{8,10},{9,11},{10,... | collective-permute-start | bytes 466952 | tf_op jit(solution)/shard_map/ppermute | solution.py:416
  55.3 2.8 %collective-permute-start.19 = (f32[8,128]{1,0:T(8,128)S(1)}, f32[8,128]{1,0:T(8,128)S(1)}, u32[]{:S(2)}, u32[]{:S(2)}) collective-permute-start(f32[8,128]{1,0:T(8,128)S(1)} %get-tuple-element.72), channel_id=1, source_target_pairs={{0,8},{4,12},{8,0},{12,4},{1,9},{5,13},{9,1},{13,5},{2,10},{6,14},... | collective-permute-start | bytes 12296 | tf_op jit(solution)/shard_map/ppermute | solution.py:416
  59.8 3.7 %collective-permute-done.20.refs_3_ = f32[8,128]{1,0:T(8,128)S(1)} collective-permute-done((f32[8,128]{1,0:T(8,128)S(1)}, f32[8,128]{1,0:T(8,128)S(1)}, u32[]{:S(2)}, u32[]{:S(2)}) %collective-permute-start.20) | collective-permute-done | bytes 4128 | tf_op jit(solution)/shard_map/ppermute | solution.py:416
  63.6 1.5 %collective-permute-start.23 = (bf16[32,128]{1,0:T(8,128)(2,1)S(1)}, bf16[32,128]{1,0:T(8,128)(2,1)S(1)}, u32[]{:S(2)}, u32[]{:S(2)}) collective-permute-start(bf16[32,128]{1,0:T(8,128)(2,1)S(1)} %shard_map.128.refs_4_), channel_id=1, source_target_pairs={{0,3},{1,2},{2,1},{3,0},{4,7},{5,6},{6,5},{7,4},{8,11},{9,10},{10,... | collective-permute-start | bytes 24584 | tf_op jit(solution)/shard_map/ppermute | solution.py:416
  65.6 1.5 %collective-permute-start.21 = (bf16[32,128]{1,0:T(8,128)(2,1)S(1)}, bf16[32,128]{1,0:T(8,128)(2,1)S(1)}, u32[]{:S(2)}, u32[]{:S(2)}) collective-permute-start(bf16[32,128]{1,0:T(8,128)(2,1)S(1)} %shard_map.128.refs_4_), channel_id=1, source_target_pairs={{0,1},{1,0},{2,3},{3,2},{4,5},{5,4},{6,7},{7,6},{8,9},{9,8},{10,11... | collective-permute-start | bytes 24584 | tf_op jit(solution)/shard_map/ppermute | solution.py:416
  69.3 5.3 %shard_map.129 = (bf16[32,1280]{1,0:T(8,128)(2,1)S(1)}, bf16[32,1280]{1,0:T(8,128)(2,1)S(1)}, bf16[32,1280]{1,0:T(8,128)(2,1)S(1)}, bf16[32,1280]{1,0:T(8,128)(2,1)S(1)}, f32[32,288]{1,0:T(8,128)S(1)}) custom-call(bf16[3,2,288,256]{3,2,1,0:T(8,128)(2,1)S(1)} %get-tuple-element.64.qkv_ref, bf16[128,1152]{1,0:T(8,128)(2,1)S(1)} %get-tuple-element.51.hidden_ref, ...), custom_call_target="tpu_custom_call" | custom-call | tf_op jit(solution)/shard_map/pallas_call | solution.py:28
  74.6 1.6 %collective-permute-start.24 = (bf16[32,1280]{1,0:T(8,128)(2,1)S(1)}, bf16[32,1280]{1,0:T(8,128)(2,1)S(1)}, u32[]{:S(2)}, u32[]{:S(2)}) collective-permute-start(bf16[32,1280]{1,0:T(8,128)(2,1)S(1)} %get-tuple-element.76), channel_id=1, source_target_pairs={{0,1},{1,0},{2,3},{3,2},{4,5},{5,4},{6,7},{7,6},{8,9},{9,8},{10,11... | collective-permute-start | bytes 245768 | tf_op jit(solution)/shard_map/ppermute | solution.py:416
  76.2 1.6 %collective-permute-start.25 = (bf16[32,1280]{1,0:T(8,128)(2,1)S(1)}, bf16[32,1280]{1,0:T(8,128)(2,1)S(1)}, u32[]{:S(2)}, u32[]{:S(2)}) collective-permute-start(bf16[32,1280]{1,0:T(8,128)(2,1)S(1)} %get-tuple-element.77), channel_id=1, source_target_pairs={{0,2},{1,3},{2,0},{3,1},{4,6},{5,7},{6,4},{7,5},{8,10},{9,11},{10,... | collective-permute-start | bytes 245768 | tf_op jit(solution)/shard_map/ppermute | solution.py:416
  80.6 2.5 %collective-permute-done.26.refs_7_ = bf16[32,1280]{1,0:T(8,128)(2,1)S(1)} collective-permute-done((bf16[32,1280]{1,0:T(8,128)(2,1)S(1)}, bf16[32,1280]{1,0:T(8,128)(2,1)S(1)}, u32[]{:S(2)}, u32[]{:S(2)}) %collective-permute-start.26) | collective-permute-done | bytes 81952 | tf_op jit(solution)/shard_map/ppermute | solution.py:416
  86.2 3.0 %collective-permute-start.28 = (bf16[64,288]{1,0:T(8,128)(2,1)S(1)}, bf16[64,288]{1,0:T(8,128)(2,1)S(1)}, u32[]{:S(2)}, u32[]{:S(2)}) collective-permute-start(bf16[64,288]{1,0:T(8,128)(2,1)S(1)} %shard_map.131.refs_0_), channel_id=1, source_target_pairs={{0,4},{4,0},{8,12},{12,8},{1,5},{5,1},{9,13},{13,9},{2,6},{6,2},{1... | collective-permute-start | bytes 110600 | tf_op jit(solution)/shard_map/ppermute | solution.py:416
  89.2 2.0 %collective-permute-done.30.refs_3_ = bf16[64,288]{1,0:T(8,128)(2,1)S(1)} collective-permute-done((bf16[64,288]{1,0:T(8,128)(2,1)S(1)}, bf16[64,288]{1,0:T(8,128)(2,1)S(1)}, u32[]{:S(2)}, u32[]{:S(2)}) %collective-permute-start.30) | collective-permute-done | bytes 36896 | tf_op jit(solution)/shard_map/ppermute | solution.py:416
  93.0 1.5 %collective-permute-start.32 = (bf16[64,288]{1,0:T(8,128)(2,1)S(1)}, bf16[64,288]{1,0:T(8,128)(2,1)S(1)}, u32[]{:S(2)}, u32[]{:S(2)}) collective-permute-start(bf16[64,288]{1,0:T(8,128)(2,1)S(1)} %shard_map.132.refs_0_), channel_id=1, source_target_pairs={{0,2},{1,3},{2,0},{3,1},{4,6},{5,7},{6,4},{7,5},{8,10},{9,11},{10,... | collective-permute-start | bytes 110600 | tf_op jit(solution)/shard_map/ppermute | solution.py:416
  94.6 1.6 %collective-permute-start.31 = (bf16[64,288]{1,0:T(8,128)(2,1)S(1)}, bf16[64,288]{1,0:T(8,128)(2,1)S(1)}, u32[]{:S(2)}, u32[]{:S(2)}) collective-permute-start(bf16[64,288]{1,0:T(8,128)(2,1)S(1)} %shard_map.132.refs_0_), channel_id=1, source_target_pairs={{0,1},{1,0},{2,3},{3,2},{4,5},{5,4},{6,7},{7,6},{8,9},{9,8},{10,11... | collective-permute-start | bytes 110600 | tf_op jit(solution)/shard_map/ppermute | solution.py:416
  96.1 1.6 %collective-permute-done.33.refs_3_ = bf16[64,288]{1,0:T(8,128)(2,1)S(1)} collective-permute-done((bf16[64,288]{1,0:T(8,128)(2,1)S(1)}, bf16[64,288]{1,0:T(8,128)(2,1)S(1)}, u32[]{:S(2)}, u32[]{:S(2)}) %collective-permute-start.33) | collective-permute-done | bytes 36896 | tf_op jit(solution)/shard_map/ppermute | solution.py:416
  100.9 2.5 %collective-permute-start.14 = (bf16[32,1152]{1,0:T(8,128)(2,1)S(1)}, bf16[32,1152]{1,0:T(8,128)(2,1)S(1)}, u32[]{:S(2)}, u32[]{:S(2)}) collective-permute-start(bf16[32,1152]{1,0:T(8,128)(2,1)S(1)} %get-tuple-element.63), channel_id=1, source_target_pairs={{0,12},{4,8},{8,4},{12,0},{1,13},{5,9},{9,5},{13,1},{2,14},{6,10},... | collective-permute-start | bytes 221192 | tf_op jit(solution)/shard_map/ppermute | solution.py:416
  104.3 4.5 %collective-permute-done.13.refs_2_ = bf16[32,1152]{1,0:T(8,128)(2,1)S(1)} collective-permute-done((bf16[32,1152]{1,0:T(8,128)(2,1)S(1)}, bf16[32,1152]{1,0:T(8,128)(2,1)S(1)}, u32[]{:S(2)}, u32[]{:S(2)}) %collective-permute-start.13) | collective-permute-done | bytes 73760 | tf_op jit(solution)/shard_map/ppermute | solution.py:416
  (82 shorter events, 33.4 us)
Async XLA Ops:
  9.6 11.1 %collective-permute-start = (bf16[3,288,128]{2,1,0:T(8,128)(2,1)S(1)}, bf16[3,288,128]{2,1,0:T(8,128)(2,1)S(1)}, u32[]{:S(2)}, u32[]{:S(2)}) collective-permute-start(bf16[3,288,128]{2,1,0:T(8,128)(2,1)S(1)} %get-tuple-element.44), channel_id=1, source_target_pairs={{0,1},{1,0},{2,3},{3,2},{4,5},{5,4},{6,7},{7,6},{8,9},{9,8},{10,11... | collective-permute-start | bytes 663560 | tf_op jit(solution)/shard_map/ppermute | solution.py:416
  12.6 11.6 %collective-permute-start.1 = (bf16[3,288,128]{2,1,0:T(8,128)(2,1)S(1)}, bf16[3,288,128]{2,1,0:T(8,128)(2,1)S(1)}, u32[]{:S(2)}, u32[]{:S(2)}) collective-permute-start(bf16[3,288,128]{2,1,0:T(8,128)(2,1)S(1)} %get-tuple-element.45), channel_id=1, source_target_pairs={{0,2},{1,3},{2,0},{3,1},{4,6},{5,7},{6,4},{7,5},{8,10},{9,11},{10,... | collective-permute-start | bytes 663560 | tf_op jit(solution)/shard_map/ppermute | solution.py:416
  14.1 10.0 %collective-permute-start.2 = (bf16[3,288,128]{2,1,0:T(8,128)(2,1)S(1)}, bf16[3,288,128]{2,1,0:T(8,128)(2,1)S(1)}, u32[]{:S(2)}, u32[]{:S(2)}) collective-permute-start(bf16[3,288,128]{2,1,0:T(8,128)(2,1)S(1)} %get-tuple-element.46), channel_id=1, source_target_pairs={{0,3},{1,2},{2,1},{3,0},{4,7},{5,6},{6,5},{7,4},{8,11},{9,10},{10,... | collective-permute-start | bytes 663560 | tf_op jit(solution)/shard_map/ppermute | solution.py:416
  16.1 22.7 %collective-permute-start.6 = (bf16[4,32,1152]{2,1,0:T(8,128)(2,1)S(1)}, bf16[4,32,1152]{2,1,0:T(8,128)(2,1)S(1)}, u32[]{:S(2)}, u32[]{:S(2)}) collective-permute-start(bf16[4,32,1152]{2,1,0:T(8,128)(2,1)S(1)} %get-tuple-element.53), channel_id=1, source_target_pairs={{0,4},{4,0},{8,12},{12,8},{1,5},{5,1},{9,13},{13,9},{2,6},{6,2},{1... | collective-permute-start | bytes 884744 | tf_op jit(solution)/shard_map/ppermute | solution.py:416
  18.1 23.5 %collective-permute-start.7 = (bf16[4,32,1152]{2,1,0:T(8,128)(2,1)S(1)}, bf16[4,32,1152]{2,1,0:T(8,128)(2,1)S(1)}, u32[]{:S(2)}, u32[]{:S(2)}) collective-permute-start(bf16[4,32,1152]{2,1,0:T(8,128)(2,1)S(1)} %get-tuple-element.54), channel_id=1, source_target_pairs={{0,8},{4,12},{8,0},{12,4},{1,9},{5,13},{9,1},{13,5},{2,10},{6,14},... | collective-permute-start | bytes 884744 | tf_op jit(solution)/shard_map/ppermute | solution.py:416
  20.7 23.5 %collective-permute-start.8 = (bf16[4,32,1152]{2,1,0:T(8,128)(2,1)S(1)}, bf16[4,32,1152]{2,1,0:T(8,128)(2,1)S(1)}, u32[]{:S(2)}, u32[]{:S(2)}) collective-permute-start(bf16[4,32,1152]{2,1,0:T(8,128)(2,1)S(1)} %get-tuple-element.55), channel_id=1, source_target_pairs={{0,12},{4,8},{8,4},{12,0},{1,13},{5,9},{9,5},{13,1},{2,14},{6,10},... | collective-permute-start | bytes 884744 | tf_op jit(solution)/shard_map/ppermute | solution.py:416
  27.1 4.4 %collective-permute-start.3 = (bf16[288,128]{1,0:T(8,128)(2,1)S(1)}, bf16[288,128]{1,0:T(8,128)(2,1)S(1)}, u32[]{:S(2)}, u32[]{:S(2)}) collective-permute-start(bf16[288,128]{1,0:T(8,128)(2,1)S(1)} %get-tuple-element.48), channel_id=1, source_target_pairs={{0,1},{1,0},{2,3},{3,2},{4,5},{5,4},{6,7},{7,6},{8,9},{9,8},{10,11... | collective-permute-start | bytes 221192 | tf_op jit(solution)/shard_map/ppermute | solution.py:416
  28.4 4.6 %collective-permute-start.4 = (bf16[288,128]{1,0:T(8,128)(2,1)S(1)}, bf16[288,128]{1,0:T(8,128)(2,1)S(1)}, u32[]{:S(2)}, u32[]{:S(2)}) collective-permute-start(bf16[288,128]{1,0:T(8,128)(2,1)S(1)} %get-tuple-element.49), channel_id=1, source_target_pairs={{0,2},{1,3},{2,0},{3,1},{4,6},{5,7},{6,4},{7,5},{8,10},{9,11},{10,... | collective-permute-start | bytes 221192 | tf_op jit(solution)/shard_map/ppermute | solution.py:416
  31.5 5.3 %collective-permute-start.5 = (bf16[288,128]{1,0:T(8,128)(2,1)S(1)}, bf16[288,128]{1,0:T(8,128)(2,1)S(1)}, u32[]{:S(2)}, u32[]{:S(2)}) collective-permute-start(bf16[288,128]{1,0:T(8,128)(2,1)S(1)} %get-tuple-element.50), channel_id=1, source_target_pairs={{0,3},{1,2},{2,1},{3,0},{4,7},{5,6},{6,5},{7,4},{8,11},{9,10},{10,... | collective-permute-start | bytes 221192 | tf_op jit(solution)/shard_map/ppermute | solution.py:416
  33.0 32.7 %collective-permute-start.15 = (bf16[608,128]{1,0:T(8,128)(2,1)S(1)}, bf16[608,128]{1,0:T(8,128)(2,1)S(1)}, u32[]{:S(2)}, u32[]{:S(2)}) collective-permute-start(bf16[608,128]{1,0:T(8,128)(2,1)S(1)} %get-tuple-element.67), channel_id=1, source_target_pairs={{0,1},{1,0},{2,3},{3,2},{4,5},{5,4},{6,7},{7,6},{8,9},{9,8},{10,11... | collective-permute-start | bytes 466952 | tf_op jit(solution)/shard_map/ppermute | solution.py:416
  37.1 7.5 %collective-permute-start.9 = (f32[8,128]{1,0:T(8,128)S(1)}, f32[8,128]{1,0:T(8,128)S(1)}, u32[]{:S(2)}, u32[]{:S(2)}) collective-permute-start(f32[8,128]{1,0:T(8,128)S(1)} %get-tuple-element.57), channel_id=1, source_target_pairs={{0,4},{4,0},{8,12},{12,8},{1,5},{5,1},{9,13},{13,9},{2,6},{6,2},{1... | collective-permute-start | bytes 12296 | tf_op jit(solution)/shard_map/ppermute | solution.py:416
  38.7 7.2 %collective-permute-start.10 = (f32[8,128]{1,0:T(8,128)S(1)}, f32[8,128]{1,0:T(8,128)S(1)}, u32[]{:S(2)}, u32[]{:S(2)}) collective-permute-start(f32[8,128]{1,0:T(8,128)S(1)} %get-tuple-element.58), channel_id=1, source_target_pairs={{0,8},{4,12},{8,0},{12,4},{1,9},{5,13},{9,1},{13,5},{2,10},{6,14},... | collective-permute-start | bytes 12296 | tf_op jit(solution)/shard_map/ppermute | solution.py:416
  41.6 5.4 %collective-permute-start.11 = (f32[8,128]{1,0:T(8,128)S(1)}, f32[8,128]{1,0:T(8,128)S(1)}, u32[]{:S(2)}, u32[]{:S(2)}) collective-permute-start(f32[8,128]{1,0:T(8,128)S(1)} %get-tuple-element.59), channel_id=1, source_target_pairs={{0,12},{4,8},{8,4},{12,0},{1,13},{5,9},{9,5},{13,1},{2,14},{6,10},... | collective-permute-start | bytes 12296 | tf_op jit(solution)/shard_map/ppermute | solution.py:416
  52.0 6.1 %collective-permute-start.18 = (f32[8,128]{1,0:T(8,128)S(1)}, f32[8,128]{1,0:T(8,128)S(1)}, u32[]{:S(2)}, u32[]{:S(2)}) collective-permute-start(f32[8,128]{1,0:T(8,128)S(1)} %get-tuple-element.71), channel_id=1, source_target_pairs={{0,4},{4,0},{8,12},{12,8},{1,5},{5,1},{9,13},{13,9},{2,6},{6,2},{1... | collective-permute-start | bytes 12296 | tf_op jit(solution)/shard_map/ppermute | solution.py:416
  52.3 14.9 %collective-permute-start.16 = (bf16[608,128]{1,0:T(8,128)(2,1)S(1)}, bf16[608,128]{1,0:T(8,128)(2,1)S(1)}, u32[]{:S(2)}, u32[]{:S(2)}) collective-permute-start(bf16[608,128]{1,0:T(8,128)(2,1)S(1)} %get-tuple-element.68), channel_id=1, source_target_pairs={{0,2},{1,3},{2,0},{3,1},{4,6},{5,7},{6,4},{7,5},{8,10},{9,11},{10,... | collective-permute-start | bytes 466952 | tf_op jit(solution)/shard_map/ppermute | solution.py:416
  53.8 13.4 %collective-permute-start.17 = (bf16[608,128]{1,0:T(8,128)(2,1)S(1)}, bf16[608,128]{1,0:T(8,128)(2,1)S(1)}, u32[]{:S(2)}, u32[]{:S(2)}) collective-permute-start(bf16[608,128]{1,0:T(8,128)(2,1)S(1)} %get-tuple-element.69), channel_id=1, source_target_pairs={{0,3},{1,2},{2,1},{3,0},{4,7},{5,6},{6,5},{7,4},{8,11},{9,10},{10,... | collective-permute-start | bytes 466952 | tf_op jit(solution)/shard_map/ppermute | solution.py:416
  55.3 4.5 %collective-permute-start.19 = (f32[8,128]{1,0:T(8,128)S(1)}, f32[8,128]{1,0:T(8,128)S(1)}, u32[]{:S(2)}, u32[]{:S(2)}) collective-permute-start(f32[8,128]{1,0:T(8,128)S(1)} %get-tuple-element.72), channel_id=1, source_target_pairs={{0,8},{4,12},{8,0},{12,4},{1,9},{5,13},{9,1},{13,5},{2,10},{6,14},... | collective-permute-start | bytes 12296 | tf_op jit(solution)/shard_map/ppermute | solution.py:416
  58.1 5.4 %collective-permute-start.20 = (f32[8,128]{1,0:T(8,128)S(1)}, f32[8,128]{1,0:T(8,128)S(1)}, u32[]{:S(2)}, u32[]{:S(2)}) collective-permute-start(f32[8,128]{1,0:T(8,128)S(1)} %get-tuple-element.73), channel_id=1, source_target_pairs={{0,12},{4,8},{8,4},{12,0},{1,13},{5,9},{9,5},{13,1},{2,14},{6,10},... | collective-permute-start | bytes 12296 | tf_op jit(solution)/shard_map/ppermute | solution.py:416
  63.6 4.6 %collective-permute-start.23 = (bf16[32,128]{1,0:T(8,128)(2,1)S(1)}, bf16[32,128]{1,0:T(8,128)(2,1)S(1)}, u32[]{:S(2)}, u32[]{:S(2)}) collective-permute-start(bf16[32,128]{1,0:T(8,128)(2,1)S(1)} %shard_map.128.refs_4_), channel_id=1, source_target_pairs={{0,3},{1,2},{2,1},{3,0},{4,7},{5,6},{6,5},{7,4},{8,11},{9,10},{10,... | collective-permute-start | bytes 24584 | tf_op jit(solution)/shard_map/ppermute | solution.py:416
  74.6 4.5 %collective-permute-start.24 = (bf16[32,1280]{1,0:T(8,128)(2,1)S(1)}, bf16[32,1280]{1,0:T(8,128)(2,1)S(1)}, u32[]{:S(2)}, u32[]{:S(2)}) collective-permute-start(bf16[32,1280]{1,0:T(8,128)(2,1)S(1)} %get-tuple-element.76), channel_id=1, source_target_pairs={{0,1},{1,0},{2,3},{3,2},{4,5},{5,4},{6,7},{7,6},{8,9},{9,8},{10,11... | collective-permute-start | bytes 245768 | tf_op jit(solution)/shard_map/ppermute | solution.py:416
  76.2 4.4 %collective-permute-start.25 = (bf16[32,1280]{1,0:T(8,128)(2,1)S(1)}, bf16[32,1280]{1,0:T(8,128)(2,1)S(1)}, u32[]{:S(2)}, u32[]{:S(2)}) collective-permute-start(bf16[32,1280]{1,0:T(8,128)(2,1)S(1)} %get-tuple-element.77), channel_id=1, source_target_pairs={{0,2},{1,3},{2,0},{3,1},{4,6},{5,7},{6,4},{7,5},{8,10},{9,11},{10,... | collective-permute-start | bytes 245768 | tf_op jit(solution)/shard_map/ppermute | solution.py:416
  77.8 5.3 %collective-permute-start.26 = (bf16[32,1280]{1,0:T(8,128)(2,1)S(1)}, bf16[32,1280]{1,0:T(8,128)(2,1)S(1)}, u32[]{:S(2)}, u32[]{:S(2)}) collective-permute-start(bf16[32,1280]{1,0:T(8,128)(2,1)S(1)} %get-tuple-element.78), channel_id=1, source_target_pairs={{0,3},{1,2},{2,1},{3,0},{4,7},{5,6},{6,5},{7,4},{8,11},{9,10},{10,... | collective-permute-start | bytes 245768 | tf_op jit(solution)/shard_map/ppermute | solution.py:416
  84.8 6.5 %collective-permute-start.30 = (bf16[64,288]{1,0:T(8,128)(2,1)S(1)}, bf16[64,288]{1,0:T(8,128)(2,1)S(1)}, u32[]{:S(2)}, u32[]{:S(2)}) collective-permute-start(bf16[64,288]{1,0:T(8,128)(2,1)S(1)} %shard_map.131.refs_0_), channel_id=1, source_target_pairs={{0,12},{4,8},{8,4},{12,0},{1,13},{5,9},{9,5},{13,1},{2,14},{6,10},... | collective-permute-start | bytes 110600 | tf_op jit(solution)/shard_map/ppermute | solution.py:416
  86.2 6.4 %collective-permute-start.29 = (bf16[64,288]{1,0:T(8,128)(2,1)S(1)}, bf16[64,288]{1,0:T(8,128)(2,1)S(1)}, u32[]{:S(2)}, u32[]{:S(2)}) collective-permute-start(bf16[64,288]{1,0:T(8,128)(2,1)S(1)} %shard_map.131.refs_0_), channel_id=1, source_target_pairs={{0,8},{4,12},{8,0},{12,4},{1,9},{5,13},{9,1},{13,5},{2,10},{6,14},... | collective-permute-start | bytes 110600 | tf_op jit(solution)/shard_map/ppermute | solution.py:416
  86.2 6.4 %collective-permute-start.28 = (bf16[64,288]{1,0:T(8,128)(2,1)S(1)}, bf16[64,288]{1,0:T(8,128)(2,1)S(1)}, u32[]{:S(2)}, u32[]{:S(2)}) collective-permute-start(bf16[64,288]{1,0:T(8,128)(2,1)S(1)} %shard_map.131.refs_0_), channel_id=1, source_target_pairs={{0,4},{4,0},{8,12},{12,8},{1,5},{5,1},{9,13},{13,9},{2,6},{6,2},{1... | collective-permute-start | bytes 110600 | tf_op jit(solution)/shard_map/ppermute | solution.py:416
  92.6 5.2 %collective-permute-start.33 = (bf16[64,288]{1,0:T(8,128)(2,1)S(1)}, bf16[64,288]{1,0:T(8,128)(2,1)S(1)}, u32[]{:S(2)}, u32[]{:S(2)}) collective-permute-start(bf16[64,288]{1,0:T(8,128)(2,1)S(1)} %shard_map.132.refs_0_), channel_id=1, source_target_pairs={{0,3},{1,2},{2,1},{3,0},{4,7},{5,6},{6,5},{7,4},{8,11},{9,10},{10,... | collective-permute-start | bytes 110600 | tf_op jit(solution)/shard_map/ppermute | solution.py:416
  93.0 4.7 %collective-permute-start.32 = (bf16[64,288]{1,0:T(8,128)(2,1)S(1)}, bf16[64,288]{1,0:T(8,128)(2,1)S(1)}, u32[]{:S(2)}, u32[]{:S(2)}) collective-permute-start(bf16[64,288]{1,0:T(8,128)(2,1)S(1)} %shard_map.132.refs_0_), channel_id=1, source_target_pairs={{0,2},{1,3},{2,0},{3,1},{4,6},{5,7},{6,4},{7,5},{8,10},{9,11},{10,... | collective-permute-start | bytes 110600 | tf_op jit(solution)/shard_map/ppermute | solution.py:416
  94.6 4.1 %collective-permute-start.31 = (bf16[64,288]{1,0:T(8,128)(2,1)S(1)}, bf16[64,288]{1,0:T(8,128)(2,1)S(1)}, u32[]{:S(2)}, u32[]{:S(2)}) collective-permute-start(bf16[64,288]{1,0:T(8,128)(2,1)S(1)} %shard_map.132.refs_0_), channel_id=1, source_target_pairs={{0,1},{1,0},{2,3},{3,2},{4,5},{5,4},{6,7},{7,6},{8,9},{9,8},{10,11... | collective-permute-start | bytes 110600 | tf_op jit(solution)/shard_map/ppermute | solution.py:416
  98.8 10.9 %collective-permute-start.34 = (bf16[64,1152]{1,0:T(8,128)(2,1)S(1)}, bf16[64,1152]{1,0:T(8,128)(2,1)S(1)}, u32[]{:S(2)}, u32[]{:S(2)}) collective-permute-start(bf16[64,1152]{1,0:T(8,128)(2,1)S(1)} %shard_map.133.refs_0_), channel_id=1, source_target_pairs={{0,16},{16,0},{1,17},{17,1},{2,18},{18,2},{3,19},{19,3},{4,20},{20... | collective-permute-start | bytes 442376 | tf_op jit(solution)/shard_map/ppermute | solution.py:416
  98.9 5.5 %collective-permute-start.12 = (bf16[32,1152]{1,0:T(8,128)(2,1)S(1)}, bf16[32,1152]{1,0:T(8,128)(2,1)S(1)}, u32[]{:S(2)}, u32[]{:S(2)}) collective-permute-start(bf16[32,1152]{1,0:T(8,128)(2,1)S(1)} %get-tuple-element.61), channel_id=1, source_target_pairs={{0,4},{4,0},{8,12},{12,8},{1,5},{5,1},{9,13},{13,9},{2,6},{6,2},{1... | collective-permute-start | bytes 221192 | tf_op jit(solution)/shard_map/ppermute | solution.py:416
  99.7 9.2 %collective-permute-start.13 = (bf16[32,1152]{1,0:T(8,128)(2,1)S(1)}, bf16[32,1152]{1,0:T(8,128)(2,1)S(1)}, u32[]{:S(2)}, u32[]{:S(2)}) collective-permute-start(bf16[32,1152]{1,0:T(8,128)(2,1)S(1)} %get-tuple-element.62), channel_id=1, source_target_pairs={{0,8},{4,12},{8,0},{12,4},{1,9},{5,13},{9,1},{13,5},{2,10},{6,14},... | collective-permute-start | bytes 221192 | tf_op jit(solution)/shard_map/ppermute | solution.py:416
  100.9 8.0 %collective-permute-start.14 = (bf16[32,1152]{1,0:T(8,128)(2,1)S(1)}, bf16[32,1152]{1,0:T(8,128)(2,1)S(1)}, u32[]{:S(2)}, u32[]{:S(2)}) collective-permute-start(bf16[32,1152]{1,0:T(8,128)(2,1)S(1)} %get-tuple-element.63), channel_id=1, source_target_pairs={{0,12},{4,8},{8,4},{12,0},{1,13},{5,9},{9,5},{13,1},{2,14},{6,10},... | collective-permute-start | bytes 221192 | tf_op jit(solution)/shard_map/ppermute | solution.py:416
  (17 other events, 100.1 us)

commit v3 on v2

--- a/solution.py
+++ b/solution.py
@@ -21,19 +21,28 @@
     return lax.dot_general(a, b, dims, preferred_element_type=F32)
 
 
-def call(kernel, out_shape, *args, scratch=(), anywhere=False):
+def call(kernel, out_shape, *args, scratch=(), hbm=False, limit=48, after=(), carry=()):
     vmem = pl.BlockSpec(memory_space=pltpu.VMEM)
+    anywhere = pl.BlockSpec(memory_space=pl.ANY)
+    main = pl.BlockSpec(memory_space=pltpu.HBM) if hbm else vmem
     single = not isinstance(out_shape, (tuple, list))
     outs = (out_shape,) if single else tuple(out_shape)
+    used, extra = len(args), len(after) + len(carry)
+
+    def body(*refs):
+        inside = refs[:used] + refs[used + extra : used + extra + len(outs)]
+        kernel(*inside, *refs[used + extra + len(outs) + len(carry) :])
+
     result = pl.pallas_call(
-        kernel,
-        out_shape=outs,
-        in_specs=[pl.BlockSpec(memory_space=pl.ANY) if anywhere else vmem] * len(args),
-        out_specs=tuple(vmem for _ in outs),
+        body,
+        out_shape=outs + tuple(shape(x.shape, x.dtype) for x in carry),
+        in_specs=[main] * used + [anywhere] * extra,
+        out_specs=(vmem,) * len(outs) + (anywhere,) * len(carry),
         scratch_shapes=list(scratch),
-        compiler_params=pltpu.CompilerParams(vmem_limit_bytes=48 * 1024 * 1024),
-    )(*args)
-    return result[0] if single else list(result)
+        input_output_aliases={used + len(after) + i: len(outs) + i for i in range(len(carry))},
+        compiler_params=pltpu.CompilerParams(vmem_limit_bytes=limit * 1024 * 1024),
+    )(*args, *after, *carry)
+    return result[0] if single and not carry else list(result)
 
 
 def shape(dims, dtype):
@@ -105,21 +114,20 @@
 
 def pack_space_kernel(n_s, *refs):
     ins, refs = refs[:7], refs[7:]
-    firsts, seconds, buffers = refs[:n_s], refs[n_s : 2 * n_s], refs[2 * n_s : 2 * n_s + 7]
-    turned_ref, sems = refs[2 * n_s + 7 :]
+    outs, buffers, (turned_ref, sems) = refs[:n_s], refs[n_s : n_s + 7], refs[n_s + 7 :]
     p_buf, at_buf, b_buf, q_buf, v_buf, k_buf, g_buf = buffers
     copies = load_all(ins, buffers, sems)
-    d_s, tokens = firsts[0].shape[1:]
+    d_s, tokens = turned_ref.shape[2:]
 
     def flat(ref):
         return ref[0].reshape(tokens, ref.shape[3])
 
-    def send(array, targets, index):
+    def send(array, index):
         turned = array.T
         for j in range(n_s):
             turned_ref[index, j] = turned[j * d_s : (j + 1) * d_s]
         for k in range(n_s):
-            targets(k)[...] = turned_ref[index, peer("space", k)]
+            outs[k][index * d_s : (index + 1) * d_s] = turned_ref[index, peer("space", k)]
 
     copies[0].wait()
     copies[1].wait()
@@ -130,17 +138,17 @@
     codes_t = jnp.concatenate([codes_q, codes_v], axis=1).T
     copies[3].wait()
     query = (flat(q_buf).astype(F32) + mm(codes_q, b_buf[0])).astype(BF16)
-    send(query, lambda k: firsts[k].at[0], 0)
+    send(query, 0)
     copies[4].wait()
     value = (flat(v_buf).astype(F32) + mm(codes_v, b_buf[1])).astype(BF16)
-    send(value, lambda k: firsts[k].at[2], 1)
+    send(value, 2)
     copies[5].wait()
-    send(flat(k_buf), lambda k: firsts[k].at[1], 2)
-    send(patches, lambda k: seconds[k].at[:d_s], 3)
+    send(flat(k_buf), 1)
+    send(patches, 3)
     copies[6].wait()
-    send(flat(g_buf), lambda k: seconds[k].at[d_s : 2 * d_s], 4)
+    send(flat(g_buf), 4)
     for k in range(n_s):
-        seconds[k][2 * d_s :] = codes_t
+        outs[k][5 * d_s :] = codes_t
 
 
 def frame_rows(pieces, f, patch_dev):
@@ -148,13 +156,13 @@
 
 
 def space_forward_kernel(frames, n_s, *refs):
-    firsts, qkv_ref, outs = refs[:n_s], refs[n_s], refs[n_s + 1 :]
-    _, d_s, tokens = firsts[0].shape
+    packed, qkv_ref, outs = refs[:n_s], refs[n_s], refs[n_s + 1 :]
+    d_s, tokens = outs[0].shape
     patch_dev = tokens // frames
     total = n_s * patch_dev
     step = min(total, 256)
     for index in range(3):
-        pieces = [first[index] for first in firsts]
+        pieces = [x[index * d_s : (index + 1) * d_s] for x in packed]
         for f in range(frames):
             qkv_ref[index, f] = frame_rows(pieces, f, patch_dev)
     for f in range(frames):
@@ -279,7 +287,7 @@
 
 
 def space_backward_kernel(frames, n_s, qkv_ref, hidden_ref, grad_b_ref, at_ref, at_here_ref, b_here_ref, *refs):
-    seconds, dcodes, sends = refs[:n_s], refs[n_s : 2 * n_s], refs[2 * n_s : 3 * n_s]
+    packed, dcodes, sends = refs[:n_s], refs[n_s : 2 * n_s], refs[2 * n_s : 3 * n_s]
     part_ref, cut_buf = refs[3 * n_s :]
     d_s = part_ref.shape[1]
     tokens = hidden_ref.shape[0]
@@ -289,10 +297,10 @@
     ups = jnp.concatenate([at_here_ref[2], at_here_ref[3]], axis=0).T
     grads = []
     for k in range(n_s):
-        cot = seconds[k][d_s : 2 * d_s].astype(F32)
+        cot = packed[k][4 * d_s : 5 * d_s].astype(F32)
         grads.append((cot + mm(ups, dcodes[k][...])).astype(BF16))
     grad_b_q = grad_b_v = None
-    codes = [second[2 * d_s :] for second in seconds]
+    codes = [x[5 * d_s :] for x in packed]
     for f in range(frames):
         query = qkv_ref[0, f].astype(F32)
         keys = qkv_ref[1, f].astype(F32)
@@ -347,14 +355,14 @@
 
 
 def merge_kernel(frames, n_s, n_d, part_ref, *refs):
-    seconds, recvs, refs = refs[:n_s], refs[n_s : 2 * n_s], refs[2 * n_s :]
+    packed, recvs, refs = refs[:n_s], refs[n_s : 2 * n_s], refs[2 * n_s :]
     sends, buf = refs[:n_d], refs[n_d]
     d_s = part_ref.shape[1]
-    tokens = seconds[0].shape[1]
+    tokens = packed[0].shape[1]
     patch_dev = tokens // frames
     total = n_s * patch_dev
     pad = -(-d_s // 128) * 128
-    patches = [second[:d_s] for second in seconds]
+    patches = [x[3 * d_s : 4 * d_s] for x in packed]
     terms = []
     for f in range(frames):
         codes = [recv[:, f * total : (f + 1) * total].astype(F32) for recv in recvs]
@@ -438,33 +446,30 @@
     dma = pltpu.SemaphoreType.DMA
     pad = -(-d_s // 128) * 128
 
-    time_pieces = exchange(
-        call(
-            functools.partial(pack_time_kernel, n_t, sub),
-            [shape((4, frames * sub, width), BF16)] * n_t,
-            query_t, key_t, value_t, cotangent,
-            scratch=[dma((4 * frames * n_t,))],
-            anywhere=True,
-        ),
-        "tm",
-    )
+    time_pieces = call(
+        functools.partial(pack_time_kernel, n_t, sub),
+        [shape((4, frames * sub, width), BF16)] * n_t,
+        query_t, key_t, value_t, cotangent,
+        scratch=[dma((4 * frames * n_t,))],
+        hbm=True, limit=54,
+    )
+    time_pieces = exchange(time_pieces, "tm")
     packed = call(
         functools.partial(pack_space_kernel, n_s),
-        [shape((3, d_s, tokens), BF16)] * n_s + [shape((2 * d_s + 2 * RANK, tokens), BF16)] * n_s,
+        [shape((5 * d_s + 2 * RANK, tokens), BF16)] * n_s,
         patches, downs, adapters_b, query_s, value_s, key_s, cotangent,
         scratch=[
             pltpu.VMEM(x.shape, BF16)
             for x in (patches, downs, adapters_b, query_s, value_s, key_s, cotangent)
         ]
         + [pltpu.VMEM((5, n_s, d_s, tokens), BF16), dma((7,))],
-        anywhere=True,
-    )
-    firsts = exchange(packed[:n_s], "space")
-    seconds = exchange(packed[n_s:], "space")
+        hbm=True, limit=54,
+    )
+    packed = exchange(packed, "space")
     qkv, *out_s = call(
         functools.partial(space_forward_kernel, frames, n_s),
         [shape((3, frames, d_s, total), BF16)] + [shape((d_s, tokens), BF16)] * n_s,
-        *firsts,
+        *packed,
     )
     out_s = exchange(out_s, "space")
     hidden, *codes = call(
@@ -491,22 +496,29 @@
         scratch=[pltpu.VMEM((tokens, 128), F32)],
     )
     dcodes = share(dcodes, "space")
-    *partial, part = call(
+    backward = call(
         functools.partial(space_backward_kernel, frames, n_s),
         [shape((2 * RANK, frames * total + 2 * pad), BF16)] * n_s + [shape((2 * RANK, d_s), F32)],
-        qkv, hidden, time_grad_b, downs, downs_here, ups_here, *seconds, *dcodes,
+        qkv, hidden, time_grad_b, downs, downs_here, ups_here, *packed, *dcodes,
         scratch=[pltpu.VMEM((n_s, 2, 2 * RANK, pad), BF16)],
-    )
+        carry=out_t,
+    )
+    partial, part, out_t = backward[:n_s], backward[n_s], backward[n_s + 1 :]
     partial = exchange(partial, "space")
+    out_t = exchange(out_t, "tm")
     rows = 8 * RANK // n_d
     sums = call(
         functools.partial(merge_kernel, frames, n_s, n_d),
         [shape((rows, d_s), F32)] * n_d,
-        part, *seconds, *partial,
+        part, *packed, *partial,
         scratch=[pltpu.VMEM((n_d, rows, d_s), F32)],
     )
-    sums = call(total_kernel, shape((rows, d_s), BF16), *exchange(sums, "dp"))
-    sums = call(total_kernel, shape((rows, d_s), BF16), *share(sums, "tm"))
+    sums = call(total_kernel, shape((rows, d_s), BF16), *exchange(sums, "dp"), after=out_t[1:])
+    step = 1
+    while step < n_t:
+        other = lax.ppermute(sums, "tm", [(i, i ^ step) for i in range(n_t)])
+        sums = call(total_kernel, shape((rows, d_s), BF16), sums, other)
+        step *= 2
     sums = call(
         join_kernel,
         shape((rows, width), BF16),
@@ -522,7 +534,7 @@
     mixed = call(
         functools.partial(mixed_kernel, frames),
         shape(patches.shape, BF16),
-        hidden, *exchange(out_t, "tm"),
+        hidden, *out_t,
         scratch=[pltpu.VMEM((tokens, width), BF16)],
     )
     return (mixed, jnp.swapaxes(grads_a, 1, 2), grads_b)

time: 111 us -> 104 us (0.937)
  starting transfers between devices: 50.5 us -> 41.5 us
  local copies, waits for them, and re-layouts: 6.82 us -> 0.2 us
  waiting for transfers between devices: 32.2 us -> 37.6 us
  Pallas kernels: 20.3 us -> 23.5 us
    ppermute x35 -> x29, starting transfers between devices: 50.5 us -> 41.1 us  [exchange(): lax.ppermute(pieces[k], axis, [(i, i ^ k) for i in range(size)])]
    ppermute x0 -> x2, waiting for transfers between devices: none -> 9.01 us  [per_device(): other = lax.ppermute(sums, 'tm', [(i, i ^ step) for i in range(n_t)])]
    unnamed x28 -> x10, local copies, waits for them, and re-layouts: 6.65 us -> 0.02 us
    ppermute x35 -> x29, waiting for transfers between devices: 32.2 us -> 28.6 us  [exchange(): lax.ppermute(pieces[k], axis, [(i, i ^ k) for i in range(size)])]
    pallas_call x14 -> x15, Pallas kernels: 20.3 us -> 23.5 us  [call(): pl.pallas_call(body, out_shape=outs + tuple((shape(x.shape, x.dtype) for...]
  transfers between devices with their start and end apart: 35 -> 31, of which waited for: 21 -> 19; matrix products, arithmetic and copies ran while one was open for 0% -> 0% of each run, Pallas kernels for 10% -> 8%
where the time goes in v3:
time: 104 us
  starting transfers between devices  41.5 us (40%)
  waiting for transfers between devices  37.6 us (36%)
  Pallas kernels  23.5 us (23%)
    ppermute x29, starting transfers between devices, exchange(): lax.ppermute(pieces[k], axis, [(i, i ^ k) for i in range(size)])  41.1 us
    ppermute x29, waiting for transfers between devices, exchange(): lax.ppermute(pieces[k], axis, [(i, i ^ k) for i in range(size)])  28.6 us
    pallas_call x15, Pallas kernels, call(): pl.pallas_call(body, out_shape=outs + tuple((shape(x.shape, x.dtype) for...  23.5 us
    ppermute x2, waiting for transfers between devices, per_device(): other = lax.ppermute(sums, 'tm', [(i, i ^ step) for i in range(n_t)])  9.01 us
  transfers between devices with their start and end apart: 31, of which 19 were waited for; matrix products, arithmetic and copies ran while one was open for 0% of the time, Pallas kernels for 8%

profile of v3, /device:TPU:0, one launch (start us, length us, event | category | flops | bytes accessed | tf_op | source)
XLA Modules:
  0.0 103.7 jit_solution(12170837609127700575)
XLA Ops:
  0.6 3.8 %shard_map.121 = (bf16[1472,128]{1,0:T(8,128)(2,1)}, bf16[1472,128]{1,0:T(8,128)(2,1)}, bf16[1472,128]{1,0:T(8,128)(2,1)}, bf16[1472,128]{1,0:T(8,128)(2,1)}) custom-call(bf16[1,2,64,1152]{3,2,1,0:T(8,128)(2,1)} %refs_4_.3, bf16[4,16,1152]{2,1,0:T(8,128)(2,1)} %bitcast.4, bf16[4,16,1152]{2,1,0:T(8,128)(2,1)} %refs_1_.3, bf16[1,2,64,1152]{3,2,1,0:T(8,128)(2,1)} %refs_3_.2, ...), custom_call_target="tpu_custom_call" | custom-call | tf_op jit(solution)/shard_map/pallas_call | solution.py:36
  4.4 3.0 %collective-permute-start = (bf16[1472,128]{1,0:T(8,128)(2,1)}, bf16[1472,128]{1,0:T(8,128)(2,1)S(1)}, u32[]{:S(2)}, u32[]{:S(2)}) collective-permute-start(bf16[1472,128]{1,0:T(8,128)(2,1)} %get-tuple-element.44), channel_id=1, source_target_pairs={{0,1},{1,0},{2,3},{3,2},{4,5},{5,4},{6,7},{7,6},{8,9},{9,8},{10,11... | collective-permute-start | bytes 1130504 | tf_op jit(solution)/shard_map/ppermute | solution.py:424
  7.4 1.6 %collective-permute-start.1 = (bf16[1472,128]{1,0:T(8,128)(2,1)}, bf16[1472,128]{1,0:T(8,128)(2,1)S(1)}, u32[]{:S(2)}, u32[]{:S(2)}) collective-permute-start(bf16[1472,128]{1,0:T(8,128)(2,1)} %get-tuple-element.45), channel_id=1, source_target_pairs={{0,2},{1,3},{2,0},{3,1},{4,6},{5,7},{6,4},{7,5},{8,10},{9,11},{10,... | collective-permute-start | bytes 1130504 | tf_op jit(solution)/shard_map/ppermute | solution.py:424
  9.0 2.5 %shard_map.124 = (bf16[4,32,1152]{2,1,0:T(8,128)(2,1)}, bf16[4,32,1152]{2,1,0:T(8,128)(2,1)}, bf16[4,32,1152]{2,1,0:T(8,128)(2,1)}, bf16[4,32,1152]{2,1,0:T(8,128)(2,1)}) custom-call(bf16[1,2,64,1152]{3,2,1,0:T(8,128)(2,1)} %refs_0_.3, bf16[1,2,64,1152]{3,2,1,0:T(8,128)(2,1)} %refs_1_.2, bf16[1,2,64,1152]{3,2,1,0:T(8,128)(2,1)} %refs_2_.3, ...), custom_call_target="tpu_custom_call" | custom-call | tf_op jit(solution)/shard_map/pallas_call | solution.py:36
  11.6 2.0 %collective-permute-start.6 = (bf16[4,32,1152]{2,1,0:T(8,128)(2,1)}, bf16[4,32,1152]{2,1,0:T(8,128)(2,1)S(1)}, u32[]{:S(2)}, u32[]{:S(2)}) collective-permute-start(bf16[4,32,1152]{2,1,0:T(8,128)(2,1)} %get-tuple-element.54), channel_id=1, source_target_pairs={{0,4},{4,0},{8,12},{12,8},{1,5},{5,1},{9,13},{13,9},{2,6},{6,2},{1... | collective-permute-start | bytes 884744 | tf_op jit(solution)/shard_map/ppermute | solution.py:424
  13.6 2.6 %collective-permute-start.7 = (bf16[4,32,1152]{2,1,0:T(8,128)(2,1)}, bf16[4,32,1152]{2,1,0:T(8,128)(2,1)}, u32[]{:S(2)}, u32[]{:S(2)}) collective-permute-start(bf16[4,32,1152]{2,1,0:T(8,128)(2,1)} %get-tuple-element.55), channel_id=1, source_target_pairs={{0,8},{4,12},{8,0},{12,4},{1,9},{5,13},{9,1},{13,5},{2,10},{6,14},... | collective-permute-start | bytes 884744 | tf_op jit(solution)/shard_map/ppermute | solution.py:424
  17.2 4.2 %collective-permute-start.8 = (bf16[4,32,1152]{2,1,0:T(8,128)(2,1)}, bf16[4,32,1152]{2,1,0:T(8,128)(2,1)}, u32[]{:S(2)}, u32[]{:S(2)}) collective-permute-start(bf16[4,32,1152]{2,1,0:T(8,128)(2,1)} %get-tuple-element.56), channel_id=1, source_target_pairs={{0,12},{4,8},{8,4},{12,0},{1,13},{5,9},{9,5},{13,1},{2,14},{6,10},... | collective-permute-start | bytes 884744 | tf_op jit(solution)/shard_map/ppermute | solution.py:424
  21.4 4.5 %collective-permute-done.1.refs_2_.refs_8_.refs_3_ = bf16[1472,128]{1,0:T(8,128)(2,1)S(1)} collective-permute-done((bf16[1472,128]{1,0:T(8,128)(2,1)}, bf16[1472,128]{1,0:T(8,128)(2,1)S(1)}, u32[]{:S(2)}, u32[]{:S(2)}) %collective-permute-start.1) | collective-permute-done | bytes 376864 | tf_op jit(solution)/shard_map/ppermute | solution.py:424
  25.9 2.9 %shard_map.122 = (bf16[3,2,288,256]{3,2,1,0:T(8,128)(2,1)S(1)}, bf16[288,128]{1,0:T(8,128)(2,1)S(1)}, bf16[288,128]{1,0:T(8,128)(2,1)S(1)}, bf16[288,128]{1,0:T(8,128)(2,1)S(1)}, bf16[288,128]{1,0:T(8,128)(2,1)S(1)}) custom-call(bf16[1472,128]{1,0:T(8,128)(2,1)S(1)} %copy-done, bf16[1472,128]{1,0:T(8,128)(2,1)S(1)} %collective-permute-done.refs_1_.refs_7_.refs_2_, ...), custom_call_target="tpu_custom_call" | custom-call | tf_op jit(solution)/shard_map/pallas_call | solution.py:36
  28.8 1.3 %collective-permute-start.3 = (bf16[288,128]{1,0:T(8,128)(2,1)S(1)}, bf16[288,128]{1,0:T(8,128)(2,1)S(1)}, u32[]{:S(2)}, u32[]{:S(2)}) collective-permute-start(bf16[288,128]{1,0:T(8,128)(2,1)S(1)} %get-tuple-element.48), channel_id=1, source_target_pairs={{0,1},{1,0},{2,3},{3,2},{4,5},{5,4},{6,7},{7,6},{8,9},{9,8},{10,11... | collective-permute-start | bytes 221192 | tf_op jit(solution)/shard_map/ppermute | solution.py:424
  30.9 2.3 %collective-permute-done.3.refs_1_ = bf16[288,128]{1,0:T(8,128)(2,1)S(1)} collective-permute-done((bf16[288,128]{1,0:T(8,128)(2,1)S(1)}, bf16[288,128]{1,0:T(8,128)(2,1)S(1)}, u32[]{:S(2)}, u32[]{:S(2)}) %collective-permute-start.3) | collective-permute-done | bytes 73760 | tf_op jit(solution)/shard_map/ppermute | solution.py:424
  33.2 1.5 %collective-permute-start.5 = (bf16[288,128]{1,0:T(8,128)(2,1)S(1)}, bf16[288,128]{1,0:T(8,128)(2,1)S(1)}, u32[]{:S(2)}, u32[]{:S(2)}) collective-permute-start(bf16[288,128]{1,0:T(8,128)(2,1)S(1)} %get-tuple-element.50), channel_id=1, source_target_pairs={{0,3},{1,2},{2,1},{3,0},{4,7},{5,6},{6,5},{7,4},{8,11},{9,10},{10,... | collective-permute-start | bytes 221192 | tf_op jit(solution)/shard_map/ppermute | solution.py:424
  34.7 3.8 %collective-permute-done.5.refs_3_ = bf16[288,128]{1,0:T(8,128)(2,1)S(1)} collective-permute-done((bf16[288,128]{1,0:T(8,128)(2,1)S(1)}, bf16[288,128]{1,0:T(8,128)(2,1)S(1)}, u32[]{:S(2)}, u32[]{:S(2)}) %collective-permute-start.5) | collective-permute-done | bytes 73760 | tf_op jit(solution)/shard_map/ppermute | solution.py:424
  38.8 1.6 %collective-permute-start.9 = (f32[8,128]{1,0:T(8,128)S(1)}, f32[8,128]{1,0:T(8,128)S(1)}, u32[]{:S(2)}, u32[]{:S(2)}) collective-permute-start(f32[8,128]{1,0:T(8,128)S(1)} %get-tuple-element.58), channel_id=1, source_target_pairs={{0,4},{4,0},{8,12},{12,8},{1,5},{5,1},{9,13},{13,9},{2,6},{6,2},{1... | collective-permute-start | bytes 12296 | tf_op jit(solution)/shard_map/ppermute | solution.py:424
  40.5 2.6 %collective-permute-start.10 = (f32[8,128]{1,0:T(8,128)S(1)}, f32[8,128]{1,0:T(8,128)S(1)}, u32[]{:S(2)}, u32[]{:S(2)}) collective-permute-start(f32[8,128]{1,0:T(8,128)S(1)} %get-tuple-element.59), channel_id=1, source_target_pairs={{0,8},{4,12},{8,0},{12,4},{1,9},{5,13},{9,1},{13,5},{2,10},{6,14},... | collective-permute-start | bytes 12296 | tf_op jit(solution)/shard_map/ppermute | solution.py:424
  43.3 1.4 %shard_map.125.refs_0_ = bf16[4,1152,128]{2,1,0:T(8,128)(2,1)S(1)} custom-call(bf16[4,32,1152]{2,1,0:T(8,128)(2,1)S(1)} %copy-done.4, bf16[4,32,1152]{2,1,0:T(8,128)(2,1)S(1)} %collective-permute-done.6.refs_1_, bf16[4,32,1152]{2,1,0:T(8,128)(2,1)} %collective-permute-done.7.refs_2_, bf16[4,32,1152]{2,1,0:T(8,128)(2,1)} %collective-permute-done.8.refs_3_), custom_call_target="tpu_custom_call" | custom-call | tf_op jit(solution)/shard_map/pallas_call | solution.py:36
  45.0 3.5 %collective-permute-done.11.refs_5_ = f32[8,128]{1,0:T(8,128)S(1)} collective-permute-done((f32[8,128]{1,0:T(8,128)S(1)}, f32[8,128]{1,0:T(8,128)S(1)}, u32[]{:S(2)}, u32[]{:S(2)}) %collective-permute-start.11) | collective-permute-done | bytes 4128 | tf_op jit(solution)/shard_map/ppermute | solution.py:424
  48.5 4.9 %shard_map.126 = (bf16[32,1152]{1,0:T(8,128)(2,1)S(1)}, bf16[32,1152]{1,0:T(8,128)(2,1)S(1)}, bf16[32,1152]{1,0:T(8,128)(2,1)S(1)}, bf16[32,1152]{1,0:T(8,128)(2...) custom-call(bf16[4,1152,128]{2,1,0:T(8,128)(2,1)S(1)} %shard_map.125, ...), custom_call_target="tpu_custom_call" | custom-call | tf_op jit(solution)/shard_map/pallas_call | solution.py:36
  54.2 3.6 %collective-permute-start.14 = (f32[8,128]{1,0:T(8,128)S(1)}, f32[8,128]{1,0:T(8,128)S(1)}, u32[]{:S(2)}, u32[]{:S(2)}) collective-permute-start(f32[8,128]{1,0:T(8,128)S(1)} %get-tuple-element.65), channel_id=1, source_target_pairs={{0,12},{4,8},{8,4},{12,0},{1,13},{5,9},{9,5},{13,1},{2,14},{6,10},... | collective-permute-start | bytes 12296 | tf_op jit(solution)/shard_map/ppermute | solution.py:424
  58.0 1.6 %collective-permute-done.14.refs_3_ = f32[8,128]{1,0:T(8,128)S(1)} collective-permute-done((f32[8,128]{1,0:T(8,128)S(1)}, f32[8,128]{1,0:T(8,128)S(1)}, u32[]{:S(2)}, u32[]{:S(2)}) %collective-permute-start.14) | collective-permute-done | bytes 4128 | tf_op jit(solution)/shard_map/ppermute | solution.py:424
  59.8 1.5 %collective-permute-start.17 = (bf16[32,128]{1,0:T(8,128)(2,1)S(1)}, bf16[32,128]{1,0:T(8,128)(2,1)S(1)}, u32[]{:S(2)}, u32[]{:S(2)}) collective-permute-start(bf16[32,128]{1,0:T(8,128)(2,1)S(1)} %shard_map.127.refs_10_), channel_id=1, source_target_pairs={{0,3},{1,2},{2,1},{3,0},{4,7},{5,6},{6,5},{7,4},{8,11},{9,10},{10,... | collective-permute-start | bytes 24584 | tf_op jit(solution)/shard_map/ppermute | solution.py:424
  61.3 1.3 %collective-permute-start.16 = (bf16[32,128]{1,0:T(8,128)(2,1)S(1)}, bf16[32,128]{1,0:T(8,128)(2,1)S(1)}, u32[]{:S(2)}, u32[]{:S(2)}) collective-permute-start(bf16[32,128]{1,0:T(8,128)(2,1)S(1)} %shard_map.127.refs_10_), channel_id=1, source_target_pairs={{0,2},{1,3},{2,0},{3,1},{4,6},{5,7},{6,4},{7,5},{8,10},{9,11},{10,... | collective-permute-start | bytes 24584 | tf_op jit(solution)/shard_map/ppermute | solution.py:424
  66.2 5.3 %shard_map.128 = (bf16[32,1280]{1,0:T(8,128)(2,1)S(1)}, bf16[32,1280]{1,0:T(8,128)(2,1)S(1)}, bf16[32,1280]{1,0:T(8,128)(2,1)S(1)}, bf16[32,1280]{1,0:T(8,128)(2...) custom-call(bf16[3,2,288,256]{3,2,1,0:T(8,128)(2,1)S(1)} %get-tuple-, ...), custom_call_target="tpu_custom_call", output_to_operand_aliasing={{5}: (14, {}), {6}: (15, {}), {7}: (16, {}), {8}: (17, {})} | custom-call | tf_op jit(solution)/shard_map/pallas_call | solution.py:36
  72.3 1.7 %collective-permute-start.22 = (bf16[32,1280]{1,0:T(8,128)(2,1)S(1)}, bf16[32,1280]{1,0:T(8,128)(2,1)S(1)}, u32[]{:S(2)}, u32[]{:S(2)}) collective-permute-start(bf16[32,1280]{1,0:T(8,128)(2,1)S(1)} %get-tuple-element.77), channel_id=1, source_target_pairs={{0,2},{1,3},{2,0},{3,1},{4,6},{5,7},{6,4},{7,5},{8,10},{9,11},{10,... | collective-permute-start | bytes 245768 | tf_op jit(solution)/shard_map/ppermute | solution.py:424
  75.4 3.8 %collective-permute-start.19 = (bf16[32,1152]{1,0:T(8,128)(2,1)S(1)}, bf16[32,1152]{1,0:T(8,128)(2,1)S(1)}, u32[]{:S(2)}, u32[]{:S(2)}) collective-permute-start(bf16[32,1152]{1,0:T(8,128)(2,1)S(1)} %get-tuple-element.72), channel_id=1, source_target_pairs={{0,8},{4,12},{8,0},{12,4},{1,9},{5,13},{9,1},{13,5},{2,10},{6,14},... | collective-permute-start | bytes 221192 | tf_op jit(solution)/shard_map/ppermute | solution.py:424
  80.0 2.3 %collective-permute-done.19.refs_3_ = bf16[32,1152]{1,0:T(8,128)(2,1)S(1)} collective-permute-done((bf16[32,1152]{1,0:T(8,128)(2,1)S(1)}, bf16[32,1152]{1,0:T(8,128)(2,1)S(1)}, u32[]{:S(2)}, u32[]{:S(2)}) %collective-permute-start.19) | collective-permute-done | bytes 73760 | tf_op jit(solution)/shard_map/ppermute | solution.py:424
  82.3 3.1 %collective-permute-done.20.refs_4_ = bf16[32,1152]{1,0:T(8,128)(2,1)S(1)} collective-permute-done((bf16[32,1152]{1,0:T(8,128)(2,1)S(1)}, bf16[32,1152]{1,0:T(8,128)(2,1)S(1)}, u32[]{:S(2)}, u32[]{:S(2)}) %collective-permute-start.20) | collective-permute-done | bytes 73760 | tf_op jit(solution)/shard_map/ppermute | solution.py:424
  85.5 4.1 %collective-permute-done.25.refs_1_ = bf16[64,288]{1,0:T(8,128)(2,1)S(1)} collective-permute-done((bf16[64,288]{1,0:T(8,128)(2,1)S(1)}, bf16[64,288]{1,0:T(8,128)(2,1)S(1)}, u32[]{:S(2)}, u32[]{:S(2)}) %collective-permute-start.25) | collective-permute-done | bytes 36896 | tf_op jit(solution)/shard_map/ppermute | solution.py:519
  89.9 4.9 %collective-permute-done.26.refs_1_ = bf16[64,288]{1,0:T(8,128)(2,1)S(1)} collective-permute-done((bf16[64,288]{1,0:T(8,128)(2,1)S(1)}, bf16[64,288]{1,0:T(8,128)(2,1)S(1)}, u32[]{:S(2)}, u32[]{:S(2)}) %collective-permute-start.26) | collective-permute-done | bytes 36896 | tf_op jit(solution)/shard_map/ppermute | solution.py:519
  94.9 1.9 %collective-permute-start.29 = (bf16[64,288]{1,0:T(8,128)(2,1)S(1)}, bf16[64,288]{1,0:T(8,128)(2,1)S(1)}, u32[]{:S(2)}, u32[]{:S(2)}) collective-permute-start(bf16[64,288]{1,0:T(8,128)(2,1)S(1)} %shard_map.133.refs_0_), channel_id=1, source_target_pairs={{0,3},{1,2},{2,1},{3,0},{4,7},{5,6},{6,5},{7,4},{8,11},{9,10},{10,... | collective-permute-start | bytes 110600 | tf_op jit(solution)/shard_map/ppermute | solution.py:424
  97.1 1.3 %collective-permute-start.27 = (bf16[64,288]{1,0:T(8,128)(2,1)S(1)}, bf16[64,288]{1,0:T(8,128)(2,1)S(1)}, u32[]{:S(2)}, u32[]{:S(2)}) collective-permute-start(bf16[64,288]{1,0:T(8,128)(2,1)S(1)} %shard_map.133.refs_0_), channel_id=1, source_target_pairs={{0,1},{1,0},{2,3},{3,2},{4,5},{5,4},{6,7},{7,6},{8,9},{9,8},{10,11... | collective-permute-start | bytes 110600 | tf_op jit(solution)/shard_map/ppermute | solution.py:424
  98.4 1.5 %collective-permute-done.29.refs_3_ = bf16[64,288]{1,0:T(8,128)(2,1)S(1)} collective-permute-done((bf16[64,288]{1,0:T(8,128)(2,1)S(1)}, bf16[64,288]{1,0:T(8,128)(2,1)S(1)}, u32[]{:S(2)}, u32[]{:S(2)}) %collective-permute-start.29) | collective-permute-done | bytes 36896 | tf_op jit(solution)/shard_map/ppermute | solution.py:424
  (57 shorter events, 15.0 us)
Async XLA Ops:
  4.4 12.8 %collective-permute-start = (bf16[1472,128]{1,0:T(8,128)(2,1)}, bf16[1472,128]{1,0:T(8,128)(2,1)S(1)}, u32[]{:S(2)}, u32[]{:S(2)}) collective-permute-start(bf16[1472,128]{1,0:T(8,128)(2,1)} %get-tuple-element.44), channel_id=1, source_target_pairs={{0,1},{1,0},{2,3},{3,2},{4,5},{5,4},{6,7},{7,6},{8,9},{9,8},{10,11... | collective-permute-start | bytes 1130504 | tf_op jit(solution)/shard_map/ppermute | solution.py:424
  7.4 18.5 %collective-permute-start.1 = (bf16[1472,128]{1,0:T(8,128)(2,1)}, bf16[1472,128]{1,0:T(8,128)(2,1)S(1)}, u32[]{:S(2)}, u32[]{:S(2)}) collective-permute-start(bf16[1472,128]{1,0:T(8,128)(2,1)} %get-tuple-element.45), channel_id=1, source_target_pairs={{0,2},{1,3},{2,0},{3,1},{4,6},{5,7},{6,4},{7,5},{8,10},{9,11},{10,... | collective-permute-start | bytes 1130504 | tf_op jit(solution)/shard_map/ppermute | solution.py:424
  9.0 16.9 %collective-permute-start.2 = (bf16[1472,128]{1,0:T(8,128)(2,1)}, bf16[1472,128]{1,0:T(8,128)(2,1)S(1)}, u32[]{:S(2)}, u32[]{:S(2)}) collective-permute-start(bf16[1472,128]{1,0:T(8,128)(2,1)} %get-tuple-element.46), channel_id=1, source_target_pairs={{0,3},{1,2},{2,1},{3,0},{4,7},{5,6},{6,5},{7,4},{8,11},{9,10},{10,... | collective-permute-start | bytes 1130504 | tf_op jit(solution)/shard_map/ppermute | solution.py:424
  11.6 31.7 %copy-start.4 = (bf16[4,32,1152]{2,1,0:T(8,128)(2,1)S(1)}, bf16[4,32,1152]{2,1,0:T(8,128)(2,1)}, u32[]{:S(2)}) copy-start(bf16[4,32,1152]{2,1,0:T(8,128)(2,1)} %get-tuple-element.53.refs_0_) | copy-start | bytes 884740
  11.6 31.5 %collective-permute-start.6 = (bf16[4,32,1152]{2,1,0:T(8,128)(2,1)}, bf16[4,32,1152]{2,1,0:T(8,128)(2,1)S(1)}, u32[]{:S(2)}, u32[]{:S(2)}) collective-permute-start(bf16[4,32,1152]{2,1,0:T(8,128)(2,1)} %get-tuple-element.54), channel_id=1, source_target_pairs={{0,4},{4,0},{8,12},{12,8},{1,5},{5,1},{9,13},{13,9},{2,6},{6,2},{1... | collective-permute-start | bytes 884744 | tf_op jit(solution)/shard_map/ppermute | solution.py:424
  13.6 29.7 %collective-permute-start.7 = (bf16[4,32,1152]{2,1,0:T(8,128)(2,1)}, bf16[4,32,1152]{2,1,0:T(8,128)(2,1)}, u32[]{:S(2)}, u32[]{:S(2)}) collective-permute-start(bf16[4,32,1152]{2,1,0:T(8,128)(2,1)} %get-tuple-element.55), channel_id=1, source_target_pairs={{0,8},{4,12},{8,0},{12,4},{1,9},{5,13},{9,1},{13,5},{2,10},{6,14},... | collective-permute-start | bytes 884744 | tf_op jit(solution)/shard_map/ppermute | solution.py:424
  17.2 26.1 %collective-permute-start.8 = (bf16[4,32,1152]{2,1,0:T(8,128)(2,1)}, bf16[4,32,1152]{2,1,0:T(8,128)(2,1)}, u32[]{:S(2)}, u32[]{:S(2)}) collective-permute-start(bf16[4,32,1152]{2,1,0:T(8,128)(2,1)} %get-tuple-element.56), channel_id=1, source_target_pairs={{0,12},{4,8},{8,4},{12,0},{1,13},{5,9},{9,5},{13,1},{2,14},{6,10},... | collective-permute-start | bytes 884744 | tf_op jit(solution)/shard_map/ppermute | solution.py:424
  28.8 4.4 %collective-permute-start.3 = (bf16[288,128]{1,0:T(8,128)(2,1)S(1)}, bf16[288,128]{1,0:T(8,128)(2,1)S(1)}, u32[]{:S(2)}, u32[]{:S(2)}) collective-permute-start(bf16[288,128]{1,0:T(8,128)(2,1)S(1)} %get-tuple-element.48), channel_id=1, source_target_pairs={{0,1},{1,0},{2,3},{3,2},{4,5},{5,4},{6,7},{7,6},{8,9},{9,8},{10,11... | collective-permute-start | bytes 221192 | tf_op jit(solution)/shard_map/ppermute | solution.py:424
  30.2 4.6 %collective-permute-start.4 = (bf16[288,128]{1,0:T(8,128)(2,1)S(1)}, bf16[288,128]{1,0:T(8,128)(2,1)S(1)}, u32[]{:S(2)}, u32[]{:S(2)}) collective-permute-start(bf16[288,128]{1,0:T(8,128)(2,1)S(1)} %get-tuple-element.49), channel_id=1, source_target_pairs={{0,2},{1,3},{2,0},{3,1},{4,6},{5,7},{6,4},{7,5},{8,10},{9,11},{10,... | collective-permute-start | bytes 221192 | tf_op jit(solution)/shard_map/ppermute | solution.py:424
  33.2 5.3 %collective-permute-start.5 = (bf16[288,128]{1,0:T(8,128)(2,1)S(1)}, bf16[288,128]{1,0:T(8,128)(2,1)S(1)}, u32[]{:S(2)}, u32[]{:S(2)}) collective-permute-start(bf16[288,128]{1,0:T(8,128)(2,1)S(1)} %get-tuple-element.50), channel_id=1, source_target_pairs={{0,3},{1,2},{2,1},{3,0},{4,7},{5,6},{6,5},{7,4},{8,11},{9,10},{10,... | collective-permute-start | bytes 221192 | tf_op jit(solution)/shard_map/ppermute | solution.py:424
  38.8 5.9 %collective-permute-start.9 = (f32[8,128]{1,0:T(8,128)S(1)}, f32[8,128]{1,0:T(8,128)S(1)}, u32[]{:S(2)}, u32[]{:S(2)}) collective-permute-start(f32[8,128]{1,0:T(8,128)S(1)} %get-tuple-element.58), channel_id=1, source_target_pairs={{0,4},{4,0},{8,12},{12,8},{1,5},{5,1},{9,13},{13,9},{2,6},{6,2},{1... | collective-permute-start | bytes 12296 | tf_op jit(solution)/shard_map/ppermute | solution.py:424
  40.5 4.5 %collective-permute-start.10 = (f32[8,128]{1,0:T(8,128)S(1)}, f32[8,128]{1,0:T(8,128)S(1)}, u32[]{:S(2)}, u32[]{:S(2)}) collective-permute-start(f32[8,128]{1,0:T(8,128)S(1)} %get-tuple-element.59), channel_id=1, source_target_pairs={{0,8},{4,12},{8,0},{12,4},{1,9},{5,13},{9,1},{13,5},{2,10},{6,14},... | collective-permute-start | bytes 12296 | tf_op jit(solution)/shard_map/ppermute | solution.py:424
  43.1 5.4 %collective-permute-start.11 = (f32[8,128]{1,0:T(8,128)S(1)}, f32[8,128]{1,0:T(8,128)S(1)}, u32[]{:S(2)}, u32[]{:S(2)}) collective-permute-start(f32[8,128]{1,0:T(8,128)S(1)} %get-tuple-element.60), channel_id=1, source_target_pairs={{0,12},{4,8},{8,4},{12,0},{1,13},{5,9},{9,5},{13,1},{2,14},{6,10},... | collective-permute-start | bytes 12296 | tf_op jit(solution)/shard_map/ppermute | solution.py:424
  53.4 4.5 %collective-permute-start.12 = (f32[8,128]{1,0:T(8,128)S(1)}, f32[8,128]{1,0:T(8,128)S(1)}, u32[]{:S(2)}, u32[]{:S(2)}) collective-permute-start(f32[8,128]{1,0:T(8,128)S(1)} %get-tuple-element.63), channel_id=1, source_target_pairs={{0,4},{4,0},{8,12},{12,8},{1,5},{5,1},{9,13},{13,9},{2,6},{6,2},{1... | collective-permute-start | bytes 12296 | tf_op jit(solution)/shard_map/ppermute | solution.py:424
  53.4 4.6 %collective-permute-start.13 = (f32[8,128]{1,0:T(8,128)S(1)}, f32[8,128]{1,0:T(8,128)S(1)}, u32[]{:S(2)}, u32[]{:S(2)}) collective-permute-start(f32[8,128]{1,0:T(8,128)S(1)} %get-tuple-element.64), channel_id=1, source_target_pairs={{0,8},{4,12},{8,0},{12,4},{1,9},{5,13},{9,1},{13,5},{2,10},{6,14},... | collective-permute-start | bytes 12296 | tf_op jit(solution)/shard_map/ppermute | solution.py:424
  54.2 5.4 %collective-permute-start.14 = (f32[8,128]{1,0:T(8,128)S(1)}, f32[8,128]{1,0:T(8,128)S(1)}, u32[]{:S(2)}, u32[]{:S(2)}) collective-permute-start(f32[8,128]{1,0:T(8,128)S(1)} %get-tuple-element.65), channel_id=1, source_target_pairs={{0,12},{4,8},{8,4},{12,0},{1,13},{5,9},{9,5},{13,1},{2,14},{6,10},... | collective-permute-start | bytes 12296 | tf_op jit(solution)/shard_map/ppermute | solution.py:424
  59.8 4.6 %collective-permute-start.17 = (bf16[32,128]{1,0:T(8,128)(2,1)S(1)}, bf16[32,128]{1,0:T(8,128)(2,1)S(1)}, u32[]{:S(2)}, u32[]{:S(2)}) collective-permute-start(bf16[32,128]{1,0:T(8,128)(2,1)S(1)} %shard_map.127.refs_10_), channel_id=1, source_target_pairs={{0,3},{1,2},{2,1},{3,0},{4,7},{5,6},{6,5},{7,4},{8,11},{9,10},{10,... | collective-permute-start | bytes 24584 | tf_op jit(solution)/shard_map/ppermute | solution.py:424
  61.3 3.7 %collective-permute-start.16 = (bf16[32,128]{1,0:T(8,128)(2,1)S(1)}, bf16[32,128]{1,0:T(8,128)(2,1)S(1)}, u32[]{:S(2)}, u32[]{:S(2)}) collective-permute-start(bf16[32,128]{1,0:T(8,128)(2,1)S(1)} %shard_map.127.refs_10_), channel_id=1, source_target_pairs={{0,2},{1,3},{2,0},{3,1},{4,6},{5,7},{6,4},{7,5},{8,10},{9,11},{10,... | collective-permute-start | bytes 24584 | tf_op jit(solution)/shard_map/ppermute | solution.py:424
  62.5 3.7 %collective-permute-start.15 = (bf16[32,128]{1,0:T(8,128)(2,1)S(1)}, bf16[32,128]{1,0:T(8,128)(2,1)S(1)}, u32[]{:S(2)}, u32[]{:S(2)}) collective-permute-start(bf16[32,128]{1,0:T(8,128)(2,1)S(1)} %shard_map.127.refs_10_), channel_id=1, source_target_pairs={{0,1},{1,0},{2,3},{3,2},{4,5},{5,4},{6,7},{7,6},{8,9},{9,8},{10,11... | collective-permute-start | bytes 24584 | tf_op jit(solution)/shard_map/ppermute | solution.py:424
  71.5 7.7 %collective-permute-start.21 = (bf16[32,1280]{1,0:T(8,128)(2,1)S(1)}, bf16[32,1280]{1,0:T(8,128)(2,1)S(1)}, u32[]{:S(2)}, u32[]{:S(2)}) collective-permute-start(bf16[32,1280]{1,0:T(8,128)(2,1)S(1)} %get-tuple-element.76), channel_id=1, source_target_pairs={{0,1},{1,0},{2,3},{3,2},{4,5},{5,4},{6,7},{7,6},{8,9},{9,8},{10,11... | collective-permute-start | bytes 245768 | tf_op jit(solution)/shard_map/ppermute | solution.py:424
  72.3 7.3 %collective-permute-start.22 = (bf16[32,1280]{1,0:T(8,128)(2,1)S(1)}, bf16[32,1280]{1,0:T(8,128)(2,1)S(1)}, u32[]{:S(2)}, u32[]{:S(2)}) collective-permute-start(bf16[32,1280]{1,0:T(8,128)(2,1)S(1)} %get-tuple-element.77), channel_id=1, source_target_pairs={{0,2},{1,3},{2,0},{3,1},{4,6},{5,7},{6,4},{7,5},{8,10},{9,11},{10,... | collective-permute-start | bytes 245768 | tf_op jit(solution)/shard_map/ppermute | solution.py:424
  74.0 5.6 %collective-permute-start.23 = (bf16[32,1280]{1,0:T(8,128)(2,1)S(1)}, bf16[32,1280]{1,0:T(8,128)(2,1)S(1)}, u32[]{:S(2)}, u32[]{:S(2)}) collective-permute-start(bf16[32,1280]{1,0:T(8,128)(2,1)S(1)} %get-tuple-element.78), channel_id=1, source_target_pairs={{0,3},{1,2},{2,1},{3,0},{4,7},{5,6},{6,5},{7,4},{8,11},{9,10},{10,... | collective-permute-start | bytes 245768 | tf_op jit(solution)/shard_map/ppermute | solution.py:424
  75.1 4.9 %collective-permute-start.18 = (bf16[32,1152]{1,0:T(8,128)(2,1)S(1)}, bf16[32,1152]{1,0:T(8,128)(2,1)S(1)}, u32[]{:S(2)}, u32[]{:S(2)}) collective-permute-start(bf16[32,1152]{1,0:T(8,128)(2,1)S(1)} %get-tuple-element.71), channel_id=1, source_target_pairs={{0,4},{4,0},{8,12},{12,8},{1,5},{5,1},{9,13},{13,9},{2,6},{6,2},{1... | collective-permute-start | bytes 221192 | tf_op jit(solution)/shard_map/ppermute | solution.py:424
  75.4 6.9 %collective-permute-start.19 = (bf16[32,1152]{1,0:T(8,128)(2,1)S(1)}, bf16[32,1152]{1,0:T(8,128)(2,1)S(1)}, u32[]{:S(2)}, u32[]{:S(2)}) collective-permute-start(bf16[32,1152]{1,0:T(8,128)(2,1)S(1)} %get-tuple-element.72), channel_id=1, source_target_pairs={{0,8},{4,12},{8,0},{12,4},{1,9},{5,13},{9,1},{13,5},{2,10},{6,14},... | collective-permute-start | bytes 221192 | tf_op jit(solution)/shard_map/ppermute | solution.py:424
  79.2 6.2 %collective-permute-start.20 = (bf16[32,1152]{1,0:T(8,128)(2,1)S(1)}, bf16[32,1152]{1,0:T(8,128)(2,1)S(1)}, u32[]{:S(2)}, u32[]{:S(2)}) collective-permute-start(bf16[32,1152]{1,0:T(8,128)(2,1)S(1)} %get-tuple-element.73), channel_id=1, source_target_pairs={{0,12},{4,8},{8,4},{12,0},{1,13},{5,9},{9,5},{13,1},{2,14},{6,10},... | collective-permute-start | bytes 221192 | tf_op jit(solution)/shard_map/ppermute | solution.py:424
  79.9 5.5 %collective-permute-start.24 = (f32[64,288]{1,0:T(8,128)S(1)}, f32[64,288]{1,0:T(8,128)S(1)}, u32[]{:S(2)}, u32[]{:S(2)}) collective-permute-start(f32[64,288]{1,0:T(8,128)S(1)} %get-tuple-element.80), channel_id=1, source_target_pairs={{0,16},{16,0},{1,17},{17,1},{2,18},{18,2},{3,19},{19,3},{4,20},{20... | collective-permute-start | bytes 221192 | tf_op jit(solution)/shard_map/ppermute | solution.py:424
  85.4 4.2 %collective-permute-start.25 = (bf16[64,288]{1,0:T(8,128)(2,1)S(1)}, bf16[64,288]{1,0:T(8,128)(2,1)S(1)}, u32[]{:S(2)}, u32[]{:S(2)}) collective-permute-start(bf16[64,288]{1,0:T(8,128)(2,1)S(1)} %shard_map.131.refs_0_), channel_id=1, source_target_pairs={{0,4},{4,0},{8,12},{12,8},{1,5},{5,1},{9,13},{13,9},{2,6},{6,2},{1... | collective-permute-start | bytes 110600 | tf_op jit(solution)/shard_map/ppermute | solution.py:519
  89.6 5.2 %collective-permute-start.26 = (bf16[64,288]{1,0:T(8,128)(2,1)S(1)}, bf16[64,288]{1,0:T(8,128)(2,1)S(1)}, u32[]{:S(2)}, u32[]{:S(2)}) collective-permute-start(bf16[64,288]{1,0:T(8,128)(2,1)S(1)} %shard_map.132.refs_0_), channel_id=1, source_target_pairs={{0,8},{4,12},{8,0},{12,4},{1,9},{5,13},{9,1},{13,5},{2,10},{6,14},... | collective-permute-start | bytes 110600 | tf_op jit(solution)/shard_map/ppermute | solution.py:519
  94.9 5.1 %collective-permute-start.29 = (bf16[64,288]{1,0:T(8,128)(2,1)S(1)}, bf16[64,288]{1,0:T(8,128)(2,1)S(1)}, u32[]{:S(2)}, u32[]{:S(2)}) collective-permute-start(bf16[64,288]{1,0:T(8,128)(2,1)S(1)} %shard_map.133.refs_0_), channel_id=1, source_target_pairs={{0,3},{1,2},{2,1},{3,0},{4,7},{5,6},{6,5},{7,4},{8,11},{9,10},{10,... | collective-permute-start | bytes 110600 | tf_op jit(solution)/shard_map/ppermute | solution.py:424
  96.7 4.1 %collective-permute-start.28 = (bf16[64,288]{1,0:T(8,128)(2,1)S(1)}, bf16[64,288]{1,0:T(8,128)(2,1)S(1)}, u32[]{:S(2)}, u32[]{:S(2)}) collective-permute-start(bf16[64,288]{1,0:T(8,128)(2,1)S(1)} %shard_map.133.refs_0_), channel_id=1, source_target_pairs={{0,2},{1,3},{2,0},{3,1},{4,6},{5,7},{6,4},{7,5},{8,10},{9,11},{10,... | collective-permute-start | bytes 110600 | tf_op jit(solution)/shard_map/ppermute | solution.py:424
  97.1 4.1 %collective-permute-start.27 = (bf16[64,288]{1,0:T(8,128)(2,1)S(1)}, bf16[64,288]{1,0:T(8,128)(2,1)S(1)}, u32[]{:S(2)}, u32[]{:S(2)}) collective-permute-start(bf16[64,288]{1,0:T(8,128)(2,1)S(1)} %shard_map.133.refs_0_), channel_id=1, source_target_pairs={{0,1},{1,0},{2,3},{3,2},{4,5},{5,4},{6,7},{7,6},{8,9},{9,8},{10,11... | collective-permute-start | bytes 110600 | tf_op jit(solution)/shard_map/ppermute | solution.py:424
  101.4 1.4 %collective-permute-start.30 = (bf16[64,1152]{1,0:T(8,128)(2,1)S(1)}, bf16[64,1152]{1,0:T(8,128)(2,1)S(1)}, u32[]{:S(2)}, u32[]{:S(2)}) collective-permute-start(bf16[64,1152]{1,0:T(8,128)(2,1)S(1)} %shard_map.134.refs_0_), channel_id=1, source_target_pairs={{0,16},{16,0},{1,17},{17,1},{2,18},{18,2},{3,19},{19,3},{4,20},{20... | collective-permute-start | bytes 442376 | tf_op jit(solution)/shard_map/ppermute | solution.py:424
  (4 other events, 85.7 us)

commit v4 on v3

--- a/solution.py
+++ b/solution.py
@@ -113,21 +113,21 @@
 
 
 def pack_space_kernel(n_s, *refs):
-    ins, refs = refs[:7], refs[7:]
-    outs, buffers, (turned_ref, sems) = refs[:n_s], refs[n_s : n_s + 7], refs[n_s + 7 :]
+    ins, outs, refs = refs[:7], refs[7:9], refs[9:]
+    buffers, sems = refs[:7], refs[7]
+    send_ref, side_ref = outs
     p_buf, at_buf, b_buf, q_buf, v_buf, k_buf, g_buf = buffers
     copies = load_all(ins, buffers, sems)
-    d_s, tokens = turned_ref.shape[2:]
+    tokens = send_ref.shape[2]
+    d_s = send_ref.shape[1] // 4
 
     def flat(ref):
         return ref[0].reshape(tokens, ref.shape[3])
 
-    def send(array, index):
+    def send(array, target, index):
         turned = array.T
         for j in range(n_s):
-            turned_ref[index, j] = turned[j * d_s : (j + 1) * d_s]
-        for k in range(n_s):
-            outs[k][index * d_s : (index + 1) * d_s] = turned_ref[index, peer("space", k)]
+            target[j, index * d_s : (index + 1) * d_s] = turned[j * d_s : (j + 1) * d_s]
 
     copies[0].wait()
     copies[1].wait()
@@ -135,34 +135,33 @@
     patches = flat(p_buf)
     codes_q = mm(patches, at_buf[0], NT).astype(BF16)
     codes_v = mm(patches, at_buf[1], NT).astype(BF16)
-    codes_t = jnp.concatenate([codes_q, codes_v], axis=1).T
+    send(patches, send_ref, 3)
     copies[3].wait()
     query = (flat(q_buf).astype(F32) + mm(codes_q, b_buf[0])).astype(BF16)
-    send(query, 0)
+    send(query, send_ref, 0)
     copies[4].wait()
     value = (flat(v_buf).astype(F32) + mm(codes_v, b_buf[1])).astype(BF16)
-    send(value, 2)
+    send(value, send_ref, 2)
     copies[5].wait()
-    send(flat(k_buf), 1)
-    send(patches, 3)
+    send(flat(k_buf), send_ref, 1)
     copies[6].wait()
-    send(flat(g_buf), 4)
-    for k in range(n_s):
-        outs[k][5 * d_s :] = codes_t
+    send(flat(g_buf), side_ref, 0)
+    codes_t = jnp.concatenate([codes_q, codes_v], axis=1).T
+    for j in range(n_s):
+        side_ref[j, d_s:] = codes_t
 
 
 def frame_rows(pieces, f, patch_dev):
     return jnp.concatenate([x[:, f * patch_dev : (f + 1) * patch_dev] for x in pieces], axis=1)
 
 
-def space_forward_kernel(frames, n_s, *refs):
-    packed, qkv_ref, outs = refs[:n_s], refs[n_s], refs[n_s + 1 :]
-    d_s, tokens = outs[0].shape
+def space_forward_kernel(frames, packed_ref, qkv_ref, out_ref):
+    n_s, d_s, tokens = out_ref.shape
     patch_dev = tokens // frames
     total = n_s * patch_dev
     step = min(total, 256)
     for index in range(3):
-        pieces = [x[index * d_s : (index + 1) * d_s] for x in packed]
+        pieces = [packed_ref[j, index * d_s : (index + 1) * d_s] for j in range(n_s)]
         for f in range(frames):
             qkv_ref[index, f] = frame_rows(pieces, f, patch_dev)
     for f in range(frames):
@@ -179,9 +178,9 @@
             ]
             heads.append(parts[0] if len(parts) == 1 else jnp.concatenate(parts, axis=1))
         out = jnp.concatenate(heads, axis=0).astype(BF16)
-        for k in range(n_s):
-            outs[k][:, f * patch_dev : (f + 1) * patch_dev] = out[
-                :, k * patch_dev : (k + 1) * patch_dev
+        for j in range(n_s):
+            out_ref[j, :, f * patch_dev : (f + 1) * patch_dev] = out[
+                :, j * patch_dev : (j + 1) * patch_dev
             ]
 
 
@@ -204,27 +203,31 @@
     return jnp.concatenate(pieces, axis=0)
 
 
-def hidden_kernel(n_t, n_s, *refs):
-    pieces, refs = refs[:n_s], refs[n_s:]
-    p_ref, at_ref, hidden_ref = refs[:3]
-    sends = refs[3 : 3 + n_t]
-    out_buf, codes_buf = refs[3 + n_t :]
-    _, frames, patch_dev, width = p_ref.shape
-    tokens = frames * patch_dev
+def hidden_kernel(n_t, frames, out_ref, packed_ref, at_ref, hidden_ref, send_ref):
+    n_s, d_s, tokens = out_ref.shape
+    patch_dev = tokens // frames
     sub = patch_dev // n_t
-    for k in range(n_s):
-        out_buf[peer("space", k)] = pieces[k][...]
-    out = out_buf[...].reshape(width, tokens).T
-    hidden = (p_ref[0].reshape(tokens, width).astype(F32) + out.astype(F32)).astype(BF16)
-    hidden_ref[...] = hidden
     downs = jnp.concatenate([at_ref[2], at_ref[3]] * 4, axis=0)
-    codes_buf[...] = mm(hidden, downs, NT).astype(BF16).astype(F32)
-    for k in range(n_t):
-        rows = [
-            codes_buf[pl.ds(pl.multiple_of(f * patch_dev + peer("tm", k) * sub, sub), sub)]
-            for f in range(frames)
-        ]
-        sends[k][...] = fold(jnp.concatenate(rows, axis=0))
+    for j in range(n_s):
+        hidden = (packed_ref[j, 3 * d_s :].astype(F32) + out_ref[j].astype(F32)).astype(BF16)
+        hidden_ref[j] = hidden
+        codes = mm(downs, hidden).T
+        for i in range(n_t):
+            rows = jnp.concatenate(
+                [
+                    codes[f * patch_dev + i * sub : f * patch_dev + (i + 1) * sub]
+                    for f in range(frames)
+                ],
+                axis=0,
+            )
+            send_ref[i * n_s + j] = fold(rows)
+
+
+def side_kernel(hidden_ref, side_ref, *outs):
+    d_s = hidden_ref.shape[1]
+    for k, out in enumerate(outs):
+        out[:d_s] = hidden_ref[peer("space", k)]
+        out[d_s:] = side_ref[peer("space", k)]
 
 
 def turn_kernel(*refs):
@@ -234,11 +237,20 @@
         out_ref[index] = rows.T
 
 
-def time_kernel(n_t, sub, x_ref, b_ref, *refs):
-    codes_refs, refs = refs[:n_t], refs[n_t:]
-    outs, sends, grad_b_ref = refs[:n_t], refs[n_t : 2 * n_t], refs[2 * n_t]
+def add_up(terms):
+    result = None
+    for term in terms:
+        result = term if result is None else result + term
+    return result
+
+
+def time_kernel(n_t, n_s, sub, x_ref, b_ref, codes_ref, send_ref, grad_b_ref, *outs):
     _, width, tokens = x_ref.shape
-    codes = jnp.concatenate([unfold(ref[...]) for ref in codes_refs], axis=0).T
+    pieces = []
+    for k in range(n_t):
+        start = peer("tm", k) * n_s
+        pieces.append(unfold(add_up([codes_ref[start + j] for j in range(n_s)])))
+    codes = jnp.concatenate(pieces, axis=0).T
     codes_q = codes[:RANK].astype(BF16)
     codes_v = codes[RANK : 2 * RANK].astype(BF16)
     query = (x_ref[0].astype(F32) + mm(b_ref[2], codes_q, TN)).astype(BF16).astype(F32)
@@ -267,7 +279,10 @@
     d_codes = d_codes.astype(BF16).astype(F32).T
     per = tokens // n_t
     for k in range(n_t):
-        sends[k][...] = fold(d_codes[k * per : (k + 1) * per])
+        folded = fold(d_codes[k * per : (k + 1) * per])
+        start = peer("tm", k) * n_s
+        for j in range(n_s):
+            send_ref[start + j] = folded
     out = jnp.concatenate(outs_h, axis=0).astype(BF16).T
     for k in range(n_t):
         outs[k][...] = out[k * per : (k + 1) * per]
@@ -275,32 +290,31 @@
     grad_b_ref[RANK:] = mm(codes_v, d_vals, NT)
 
 
-def place_codes_kernel(frames, sub, *refs):
-    pieces, (out_ref, buf) = refs[:-2], refs[-2:]
-    patch_dev = sub * len(pieces)
-    for k, piece in enumerate(pieces):
-        rows = unfold(piece[...])
-        for f in range(frames):
-            start = pl.multiple_of(f * patch_dev + peer("tm", k) * sub, sub)
-            buf[pl.ds(start, sub)] = rows[f * sub : (f + 1) * sub]
-    out_ref[...] = buf[...].T[: 2 * RANK].astype(BF16)
-
-
-def space_backward_kernel(frames, n_s, qkv_ref, hidden_ref, grad_b_ref, at_ref, at_here_ref, b_here_ref, *refs):
-    packed, dcodes, sends = refs[:n_s], refs[n_s : 2 * n_s], refs[2 * n_s : 3 * n_s]
-    part_ref, cut_buf = refs[3 * n_s :]
-    d_s = part_ref.shape[1]
-    tokens = hidden_ref.shape[0]
+def space_backward_kernel(frames, n_s, qkv_ref, hidden_ref, grad_b_ref, codes_ref, at_ref, b_ref, *refs):
+    sides, sends, (part_ref, cut_buf, side_buf) = refs[:n_s], refs[n_s : 2 * n_s], refs[2 * n_s :]
+    n_s, d_s, tokens = hidden_ref.shape
+    n_t = codes_ref.shape[0] // n_s
     patch_dev = tokens // frames
+    sub = patch_dev // n_t
     total = n_s * patch_dev
     step = min(total, 256)
-    ups = jnp.concatenate([at_here_ref[2], at_here_ref[3]], axis=0).T
-    grads = []
     for k in range(n_s):
-        cot = packed[k][4 * d_s : 5 * d_s].astype(F32)
-        grads.append((cot + mm(ups, dcodes[k][...])).astype(BF16))
+        side_buf[peer("space", k)] = sides[k][d_s:]
+    ups = jnp.concatenate([at_ref[2], at_ref[3]], axis=0).T
+    grads, grad_a = [], None
+    for j in range(n_s):
+        chunks = [unfold(codes_ref[i * n_s + j]) for i in range(n_t)]
+        rows = jnp.concatenate(
+            [chunks[i][f * sub : (f + 1) * sub] for f in range(frames) for i in range(n_t)], axis=0
+        )
+        d_codes = rows.T[: 2 * RANK].astype(BF16)
+        term = mm(d_codes, hidden_ref[j], NT)
+        grad_a = term if grad_a is None else grad_a + term
+        cot = side_buf[j, :d_s].astype(F32)
+        grads.append((cot + mm(ups, d_codes)).astype(BF16))
+    part_ref[: 2 * RANK] = grad_a
     grad_b_q = grad_b_v = None
-    codes = [x[5 * d_s :] for x in packed]
+    codes = [side_buf[j, d_s:] for j in range(n_s)]
     for f in range(frames):
         query = qkv_ref[0, f].astype(F32)
         keys = qkv_ref[1, f].astype(F32)
@@ -323,54 +337,36 @@
             d_vals.append(dv_sum)
         d_query = jnp.concatenate(d_query, axis=0).astype(BF16)
         d_vals = jnp.concatenate(d_vals, axis=0).astype(BF16)
-        partial = jnp.concatenate([mm(b_here_ref[0], d_query), mm(b_here_ref[1], d_vals)], axis=0)
-        partial = partial.astype(BF16)
-        blocks = [partial[:, m * patch_dev : (m + 1) * patch_dev] for m in range(n_s)]
+        partial = jnp.concatenate([mm(b_ref[0], d_query), mm(b_ref[1], d_vals)], axis=0)
         for k in range(n_s):
-            turned = jnp.concatenate([blocks[m ^ k] for m in range(n_s)], axis=1)
-            sends[k][:, f * total : (f + 1) * total] = turned
+            sends[k][:, f * total : (f + 1) * total] = partial.astype(BF16)
         frame_codes = frame_rows(codes, f, patch_dev)
         term_q = mm(frame_codes[:RANK], d_query, NT)
         term_v = mm(frame_codes[RANK:], d_vals, NT)
         grad_b_q = term_q if grad_b_q is None else grad_b_q + term_q
         grad_b_v = term_v if grad_b_v is None else grad_b_v + term_v
-    part_ref[:RANK] = grad_b_q
-    part_ref[RANK:] = grad_b_v
-    grad_a = mm(dcodes[0][...], hidden_ref[...])
-    pad = -(-d_s // 128) * 128
+    part_ref[2 * RANK : 3 * RANK] = grad_b_q
+    part_ref[3 * RANK :] = grad_b_v
     for j in range(n_s):
-        cut_buf[j, 0, :, :d_s] = grad_a[:, j * d_s : (j + 1) * d_s].astype(BF16)
-        cut_buf[j, 1, :, :d_s] = grad_b_ref[:, j * d_s : (j + 1) * d_s].astype(BF16)
+        cut_buf[j, :, :d_s] = grad_b_ref[:, j * d_s : (j + 1) * d_s].astype(BF16)
     for k in range(n_s):
-        for index in range(2):
-            start = frames * total + index * pad
-            sends[k][:, start : start + pad] = cut_buf[peer("space", k), index]
-
-
-def add_up(terms):
-    result = None
-    for term in terms:
-        result = term if result is None else result + term
-    return result
-
-
-def merge_kernel(frames, n_s, n_d, part_ref, *refs):
-    packed, recvs, refs = refs[:n_s], refs[n_s : 2 * n_s], refs[2 * n_s :]
-    sends, buf = refs[:n_d], refs[n_d]
+        sends[k][:, frames * total :] = cut_buf[peer("space", k)]
+
+
+def merge_kernel(frames, n_s, n_d, part_ref, packed_ref, *refs):
+    recvs, sends, buf = refs[:n_s], refs[n_s : n_s + n_d], refs[n_s + n_d]
     d_s = part_ref.shape[1]
-    tokens = packed[0].shape[1]
+    tokens = packed_ref.shape[2]
     patch_dev = tokens // frames
     total = n_s * patch_dev
-    pad = -(-d_s // 128) * 128
-    patches = [x[3 * d_s : 4 * d_s] for x in packed]
+    patches = [packed_ref[j, 3 * d_s :] for j in range(n_s)]
     terms = []
     for f in range(frames):
         codes = [recv[:, f * total : (f + 1) * total].astype(F32) for recv in recvs]
         terms.append(mm(add_up(codes).astype(BF16), frame_rows(patches, f, patch_dev), NT))
     start = frames * total
-    time_a = add_up([recv[:, start : start + d_s].astype(F32) for recv in recvs])
-    time_b = add_up([recv[:, start + pad : start + pad + d_s].astype(F32) for recv in recvs])
-    rows = jnp.concatenate([add_up(terms), time_a, part_ref[...], time_b], axis=0)
+    time_b = add_up([recv[:, start : start + d_s].astype(F32) for recv in recvs])
+    rows = jnp.concatenate([add_up(terms), part_ref[...], time_b], axis=0)
     per = rows.shape[0] // n_d
     for d in range(n_d):
         buf[d] = rows[d * per : (d + 1) * per]
@@ -379,7 +375,10 @@
 
 
 def total_kernel(*refs):
-    refs[-1][...] = add_up([ref[...].astype(F32) for ref in refs[:-1]]).astype(refs[-1].dtype)
+    terms = [ref[...].astype(F32) for ref in refs[:-1]]
+    while len(terms) > 1:
+        terms = [terms[i] + terms[i + 1] for i in range(0, len(terms), 2)]
+    refs[-1][...] = terms[0].astype(refs[-1].dtype)
 
 
 def join_kernel(*refs):
@@ -404,18 +403,26 @@
             target[start // RANK, start % RANK : start % RANK + size] = rows[r : r + size]
 
 
-def mixed_kernel(frames, hidden_ref, *refs):
-    pieces, (mixed_ref, buf) = refs[:-2], refs[-2:]
+def mixed_kernel(frames, n_s, *refs):
+    sides, pieces = refs[:n_s], refs[n_s:-3]
+    mixed_ref, hidden_buf, buf = refs[-3:]
     n_t = len(pieces)
-    tokens, width = hidden_ref.shape
+    _, d_s, tokens = hidden_buf.shape
     patch_dev = tokens // frames
     sub = patch_dev // n_t
+    for k in range(n_s):
+        hidden_buf[peer("space", k)] = sides[k][:d_s]
     for k, piece in enumerate(pieces):
         for f in range(frames):
             start = pl.multiple_of(f * patch_dev + peer("tm", k) * sub, sub)
             buf[pl.ds(start, sub)] = piece[f * sub : (f + 1) * sub]
-    total = hidden_ref[...].astype(F32) + buf[...].astype(F32)
-    mixed_ref[0] = total.astype(BF16).reshape(frames, patch_dev, width)
+    hidden = hidden_buf[...].reshape(n_s * d_s, tokens).T
+    total = hidden.astype(F32) + buf[...].astype(F32)
+    mixed_ref[0] = total.astype(BF16).reshape(frames, patch_dev, n_s * d_s)
+
+
+def swap(array, axes):
+    return lax.all_to_all(array, axes, split_axis=0, concat_axis=0, tiled=True)
 
 
 def exchange(pieces, axis):
@@ -446,6 +453,17 @@
     dma = pltpu.SemaphoreType.DMA
     pad = -(-d_s // 128) * 128
 
+    packed, side = call(
+        functools.partial(pack_space_kernel, n_s),
+        [shape((n_s, 4 * d_s, tokens), BF16), shape((n_s, d_s + 2 * RANK, tokens), BF16)],
+        patches, downs, adapters_b, query_s, value_s, key_s, cotangent,
+        scratch=[
+            pltpu.VMEM(x.shape, BF16)
+            for x in (patches, downs, adapters_b, query_s, value_s, key_s, cotangent)
+        ]
+        + [dma((7,))],
+        hbm=True, limit=54,
+    )
     time_pieces = call(
         functools.partial(pack_time_kernel, n_t, sub),
         [shape((4, frames * sub, width), BF16)] * n_t,
@@ -453,72 +471,53 @@
         scratch=[dma((4 * frames * n_t,))],
         hbm=True, limit=54,
     )
+    packed = swap(packed, "space")
     time_pieces = exchange(time_pieces, "tm")
-    packed = call(
-        functools.partial(pack_space_kernel, n_s),
-        [shape((5 * d_s + 2 * RANK, tokens), BF16)] * n_s,
-        patches, downs, adapters_b, query_s, value_s, key_s, cotangent,
+    qkv, out_s = call(
+        functools.partial(space_forward_kernel, frames),
+        [shape((3, frames, d_s, total), BF16), shape((n_s, d_s, tokens), BF16)],
+        packed,
+    )
+    hidden, codes = call(
+        functools.partial(hidden_kernel, n_t, frames),
+        [shape((n_s, d_s, tokens), BF16), shape((n_t * n_s, 8, 128), F32)],
+        out_s, packed, downs_here,
+    )
+    codes = swap(codes, ("tm", "space"))
+    sides = call(
+        side_kernel, [shape((2 * d_s + 2 * RANK, tokens), BF16)] * n_s, hidden, side
+    )
+    sides = exchange(sides, "space")
+    turned = call(turn_kernel, shape((4, width, n_t * frames * sub), BF16), *time_pieces)
+    dcodes, time_grad_b, *out_t = call(
+        functools.partial(time_kernel, n_t, n_s, sub),
+        [shape((n_t * n_s, 8, 128), F32), shape((2 * RANK, width), F32)]
+        + [shape((frames * sub, width), BF16)] * n_t,
+        turned, adapters_b, codes,
+        after=sides[1:],
+    )
+    dcodes = swap(dcodes, ("tm", "space"))
+    out_t = exchange(out_t, "tm")
+    *partial, part = call(
+        functools.partial(space_backward_kernel, frames, n_s),
+        [shape((2 * RANK, frames * total + pad), BF16)] * n_s + [shape((4 * RANK, d_s), F32)],
+        qkv, hidden, time_grad_b, dcodes, downs_here, ups_here, *sides,
         scratch=[
-            pltpu.VMEM(x.shape, BF16)
-            for x in (patches, downs, adapters_b, query_s, value_s, key_s, cotangent)
-        ]
-        + [pltpu.VMEM((5, n_s, d_s, tokens), BF16), dma((7,))],
-        hbm=True, limit=54,
-    )
-    packed = exchange(packed, "space")
-    qkv, *out_s = call(
-        functools.partial(space_forward_kernel, frames, n_s),
-        [shape((3, frames, d_s, total), BF16)] + [shape((d_s, tokens), BF16)] * n_s,
-        *packed,
-    )
-    out_s = exchange(out_s, "space")
-    hidden, *codes = call(
-        functools.partial(hidden_kernel, n_t, n_s),
-        [shape((tokens, width), BF16)] + [shape((8, 128), F32)] * n_t,
-        *out_s, patches, downs,
-        scratch=[pltpu.VMEM((n_s, d_s, tokens), BF16), pltpu.VMEM((tokens, 128), F32)],
-    )
-    codes = exchange(codes, "tm")
-    turned = call(turn_kernel, shape((4, width, n_t * frames * sub), BF16), *time_pieces)
-    timed = call(
-        functools.partial(time_kernel, n_t, sub),
-        [shape((frames * sub, width), BF16)] * n_t
-        + [shape((8, 128), F32)] * n_t
-        + [shape((2 * RANK, width), F32)],
-        turned, adapters_b, *codes,
-    )
-    out_t, dcodes, time_grad_b = timed[:n_t], timed[n_t : 2 * n_t], timed[2 * n_t]
-    dcodes = exchange(dcodes, "tm")
-    dcodes = call(
-        functools.partial(place_codes_kernel, frames, sub),
-        shape((2 * RANK, tokens), BF16),
-        *dcodes,
-        scratch=[pltpu.VMEM((tokens, 128), F32)],
-    )
-    dcodes = share(dcodes, "space")
-    backward = call(
-        functools.partial(space_backward_kernel, frames, n_s),
-        [shape((2 * RANK, frames * total + 2 * pad), BF16)] * n_s + [shape((2 * RANK, d_s), F32)],
-        qkv, hidden, time_grad_b, downs, downs_here, ups_here, *packed, *dcodes,
-        scratch=[pltpu.VMEM((n_s, 2, 2 * RANK, pad), BF16)],
-        carry=out_t,
-    )
-    partial, part, out_t = backward[:n_s], backward[n_s], backward[n_s + 1 :]
+            pltpu.VMEM((n_s, 2 * RANK, pad), BF16),
+            pltpu.VMEM((n_s, d_s + 2 * RANK, tokens), BF16),
+        ],
+    )
     partial = exchange(partial, "space")
-    out_t = exchange(out_t, "tm")
     rows = 8 * RANK // n_d
     sums = call(
         functools.partial(merge_kernel, frames, n_s, n_d),
         [shape((rows, d_s), F32)] * n_d,
-        part, *packed, *partial,
+        part, packed, *partial,
         scratch=[pltpu.VMEM((n_d, rows, d_s), F32)],
-    )
-    sums = call(total_kernel, shape((rows, d_s), BF16), *exchange(sums, "dp"), after=out_t[1:])
-    step = 1
-    while step < n_t:
-        other = lax.ppermute(sums, "tm", [(i, i ^ step) for i in range(n_t)])
-        sums = call(total_kernel, shape((rows, d_s), BF16), sums, other)
-        step *= 2
+        after=out_t[1:],
+    )
+    sums = call(total_kernel, shape((rows, d_s), BF16), *exchange(sums, "dp"))
+    sums = call(total_kernel, shape((rows, d_s), BF16), *share(sums, "tm"))
     sums = call(
         join_kernel,
         shape((rows, width), BF16),
@@ -532,10 +531,10 @@
         scratch=[pltpu.VMEM((n_d, rows, width), BF16)],
     )
     mixed = call(
-        functools.partial(mixed_kernel, frames),
+        functools.partial(mixed_kernel, frames, n_s),
         shape(patches.shape, BF16),
-        hidden, *out_t,
-        scratch=[pltpu.VMEM((tokens, width), BF16)],
+        *sides, *out_t,
+        scratch=[pltpu.VMEM((n_s, d_s, tokens), BF16), pltpu.VMEM((tokens, width), BF16)],
     )
     return (mixed, jnp.swapaxes(grads_a, 1, 2), grads_b)
 

time: 104 us -> 102 us (0.981)
  waiting for transfers between devices: 37.6 us -> 24.4 us
  local copies, waits for them, and re-layouts: 0.2 us -> 12.1 us
  starting transfers between devices: 41.5 us -> 39.5 us
    ppermute x29 -> x20, waiting for transfers between devices: 28.6 us -> 11.5 us  [exchange(): lax.ppermute(pieces[k], axis, [(i, i ^ k) for i in range(size)])]
    ppermute x29 -> x20, starting transfers between devices: 41.1 us -> 24 us  [exchange(): lax.ppermute(pieces[k], axis, [(i, i ^ k) for i in range(size)])]
    all_to_all x0 -> x3, starting transfers between devices: none -> 15.5 us  [swap(): return lax.all_to_all(array, axes, split_axis=0, concat_axis=0, tiled=True)]
    all_to_all x0 -> x3, waiting for transfers between devices: none -> 12.9 us  [swap(): return lax.all_to_all(array, axes, split_axis=0, concat_axis=0, tiled=True)]
    unnamed x10 -> x34, local copies, waits for them, and re-layouts: 0.02 us -> 11.1 us
    ppermute x2 -> x0, waiting for transfers between devices: 9.01 us -> none  [per_device(): other = lax.ppermute(sums, 'tm', [(i, i ^ step) for i in range(n_t)])]
    pallas_call x15 -> x14, Pallas kernels: 23.5 us -> 24.5 us  [call(): pl.pallas_call(body, out_shape=outs + tuple((shape(x.shape, x.dtype) for...]
  transfers between devices with their start and end apart: 31 -> 23, of which waited for: 19 -> 13; matrix products, arithmetic and copies ran while one was open for 0% -> 1% of each run, Pallas kernels for 8% -> 15%
where the time goes in v4:
time: 102 us; the launch traced here: 101 us
  starting transfers between devices  39.5 us (39%)
  Pallas kernels  24.5 us (24%)
  waiting for transfers between devices  24.4 us (24%)
  local copies, waits for them, and re-layouts  12.1 us (12%)
    pallas_call x14, Pallas kernels, call(): pl.pallas_call(body, out_shape=outs + tuple((shape(x.shape, x.dtype) for...  24.5 us
    ppermute x20, starting transfers between devices, exchange(): lax.ppermute(pieces[k], axis, [(i, i ^ k) for i in range(size)])  24 us
    all_to_all x3, starting transfers between devices, swap(): return lax.all_to_all(array, axes, split_axis=0, concat_axis=0, tiled=True)  15.5 us
    all_to_all x3, waiting for transfers between devices, swap(): return lax.all_to_all(array, axes, split_axis=0, concat_axis=0, tiled=True)  12.9 us
    ppermute x20, waiting for transfers between devices, exchange(): lax.ppermute(pieces[k], axis, [(i, i ^ k) for i in range(size)])  11.5 us
    unnamed x34, local copies, waits for them, and re-layouts  11.1 us
  transfers between devices with their start and end apart: 23, of which 13 were waited for; matrix products, arithmetic and copies ran while one was open for 1% of the time, Pallas kernels for 15%

profile of v4, /device:TPU:0, one launch (start us, length us, event | category | flops | bytes accessed | tf_op | source)
XLA Modules:
  0.0 101.4 jit_solution(14728314173794580901)
XLA Ops:
  0.6 3.3 %shard_map.121 = (bf16[4,1152,128]{2,1,0:T(8,128)(2,1)}, bf16[4,320,128]{2,1,0:T(8,128)(2,1)}) custom-call(bf16[1,2,64,1152]{3,2,1,0:T(8,128)(2,1)} %refs_0_.2, bf16[4,16,1152]{2,1,0:T(8,128)(2,1)} %bitcast.4, bf16[4,16,1152]{2,1,0:T(8,128)(2,1)} %refs_1_.3, bf16[1,2,64,1152]{3,2,1,0:T(8,128)(2,1)} %refs_3_.2, bf16[1,2,64,1152]{3,2,1,0:T(8,128)(2,1)} %refs_4_.1, ...), custom_call_target="tpu_custom_call" | custom-call | tf_op jit(solution)/shard_map/pallas_call | solution.py:36
  3.9 5.2 %all-to-all-start = ((bf16[4,1152,128]{2,1,0:T(8,128)(2,1)}), bf16[4,1152,128]{2,1,0:T(8,128)(2,1)S(1)}, u32[]{:S(2)}, u32[]{:S(2)}) async-start(bf16[4,1152,128]{2,1,0:T(8,128)(2,1)} %get-tuple-element.32), calls=%async_computation | async-start | bytes 2359296 | tf_op jit(solution)/shard_map/all_to_all | solution.py:425
  9.1 2.5 %shard_map.125 = (bf16[4,32,1152]{2,1,0:T(8,128)(2,1)}, bf16[4,32,1152]{2,1,0:T(8,128)(2,1)}, bf16[4,32,1152]{2,1,0:T(8,128)(2,1)}, bf16[4,32,1152]{2,1,0:T(8,128)(2,1)}) custom-call(bf16[1,2,64,1152]{3,2,1,0:T(8,128)(2,1)} %refs_0_.3, bf16[1,2,64,1152]{3,2,1,0:T(8,128)(2,1)} %refs_1_.2, bf16[1,2,64,1152]{3,2,1,0:T(8,128)(2,1)} %refs_2_.3, ...), custom_call_target="tpu_custom_call" | custom-call | tf_op jit(solution)/shard_map/pallas_call | solution.py:36
  11.6 1.6 %collective-permute-start.3 = (bf16[4,32,1152]{2,1,0:T(8,128)(2,1)}, bf16[4,32,1152]{2,1,0:T(8,128)(2,1)S(1)}, u32[]{:S(2)}, u32[]{:S(2)}) collective-permute-start(bf16[4,32,1152]{2,1,0:T(8,128)(2,1)} %get-tuple-element.41), channel_id=1, source_target_pairs={{0,4},{4,0},{8,12},{12,8},{1,5},{5,1},{9,13},{13,9},{2,6},{6,2},{1... | collective-permute-start | bytes 884744 | tf_op jit(solution)/shard_map/ppermute | solution.py:431
  13.3 2.6 %collective-permute-start.4 = (bf16[4,32,1152]{2,1,0:T(8,128)(2,1)}, bf16[4,32,1152]{2,1,0:T(8,128)(2,1)S(1)}, u32[]{:S(2)}, u32[]{:S(2)}) collective-permute-start(bf16[4,32,1152]{2,1,0:T(8,128)(2,1)} %get-tuple-element.42), channel_id=1, source_target_pairs={{0,8},{4,12},{8,0},{12,4},{1,9},{5,13},{9,1},{13,5},{2,10},{6,14},... | collective-permute-start | bytes 884744 | tf_op jit(solution)/shard_map/ppermute | solution.py:431
  17.0 7.1 %all-to-all-done.refs_0_.refs_1_ = bf16[4,1152,128]{2,1,0:T(8,128)(2,1)S(1)} async-done(((bf16[4,1152,128]{2,1,0:T(8,128)(2,1)}), bf16[4,1152,128]{2,1,0:T(8,128)(2,1)S(1)}, u32[]{:S(2)}, u32[]{:S(2)}) %all-to-all-start) | async-done | bytes 1179680 | tf_op jit(solution)/shard_map/all_to_all | solution.py:425
  24.2 2.9 %shard_map.122 = (bf16[3,2,288,256]{3,2,1,0:T(8,128)(2,1)S(1)}, bf16[4,288,128]{2,1,0:T(8,128)(2,1)S(1)}) custom-call(bf16[4,1152,128]{2,1,0:T(8,128)(2,1)S(1)} %all-to-all-done.refs_0_.refs_1_), custom_call_target="tpu_custom_call" | custom-call | tf_op jit(solution)/shard_map/pallas_call | solution.py:36
  28.0 1.0 shard_map.123
  29.8 1.4 %collective-permute-start = (bf16[608,128]{1,0:T(8,128)(2,1)}, bf16[608,128]{1,0:T(8,128)(2,1)S(1)}, u32[]{:S(2)}, u32[]{:S(2)}) collective-permute-start(bf16[608,128]{1,0:T(8,128)(2,1)} %get-tuple-element.37), channel_id=1, source_target_pairs={{0,1},{1,0},{2,3},{3,2},{4,5},{5,4},{6,7},{7,6},{8,9},{9,8},{10,11... | collective-permute-start | bytes 466952 | tf_op jit(solution)/shard_map/ppermute | solution.py:431
  32.5 1.5 %collective-permute-start.2 = (bf16[608,128]{1,0:T(8,128)(2,1)}, bf16[608,128]{1,0:T(8,128)(2,1)S(1)}, u32[]{:S(2)}, u32[]{:S(2)}) collective-permute-start(bf16[608,128]{1,0:T(8,128)(2,1)} %get-tuple-element.39), channel_id=1, source_target_pairs={{0,3},{1,2},{2,1},{3,0},{4,7},{5,6},{6,5},{7,4},{8,11},{9,10},{10,... | collective-permute-start | bytes 466952 | tf_op jit(solution)/shard_map/ppermute | solution.py:431
  34.0 5.9 %all-to-all-start.1 = ((f32[16,8,128]{2,1,0:T(8,128)}), f32[16,8,128]{2,1,0:T(8,128)S(1)}, u32[]{:S(2)}, u32[]{:S(2)}) async-start(f32[16,8,128]{2,1,0:T(8,128)} %get-tuple-element.44), calls=%async_computation.1 | async-start | bytes 131072 | tf_op jit(solution)/shard_map/all_to_all | solution.py:425
  43.5 1.4 %shard_map.126.refs_0_ = bf16[4,1152,128]{2,1,0:T(8,128)(2,1)S(1)} custom-call(bf16[4,32,1152]{2,1,0:T(8,128)(2,1)S(1)} %copy-done.4, bf16[4,32,1152]{2,1,0:T(8,128)(2,1)S(1)} %copy-done.6, bf16[4,32,1152]{2,1,0:T(8,128)(2,1)S(1)} %copy-done.8, bf16[4,32,1152]{2,1,0:T(8,128)(2,1)} %collective-permute-done.5.refs_3_), custom_call_target="tpu_custom_call" | custom-call | tf_op jit(solution)/shard_map/pallas_call | solution.py:36
  44.9 2.6 %all-to-all-done.1.refs_2_ = f32[16,8,128]{2,1,0:T(8,128)S(1)} async-done(((f32[16,8,128]{2,1,0:T(8,128)}), f32[16,8,128]{2,1,0:T(8,128)S(1)}, u32[]{:S(2)}, u32[]{:S(2)}) %all-to-all-start.1) | async-done | bytes 65568 | tf_op jit(solution)/shard_map/all_to_all | solution.py:425
  47.5 5.0 %shard_map.127 = (f32[16,8,128]{2,1,0:T(8,128)S(1)}, f32[32,1152]{1,0:T(8,128)S(1)}, bf16[32,1152]{1,0:T(8,128)(2,1)S(1)}, bf16[32,1152]{1,0:T(8,128)(2,1)S(1)},...) custom-call(bf16[4,1152,128]{2,1,0:T(8,128)(2,1)S(1)} %shard_map.126.refs_0_, ...), custom_call_target="tpu_custom_call" | custom-call | tf_op jit(solution)/shard_map/pallas_call | solution.py:36
  56.2 4.4 %all-to-all-start.2 = ((f32[16,8,128]{2,1,0:T(8,128)}), f32[16,8,128]{2,1,0:T(8,128)S(1)}, u32[]{:S(2)}, u32[]{:S(2)}) async-start(f32[16,8,128]{2,1,0:T(8,128)} %copy-done.13), calls=%async_computation.2 | async-start | bytes 131072 | tf_op jit(solution)/shard_map/all_to_all | solution.py:425
  60.6 2.0 %collective-permute-start.6 = (bf16[32,1152]{1,0:T(8,128)(2,1)}, bf16[32,1152]{1,0:T(8,128)(2,1)S(1)}, u32[]{:S(2)}, u32[]{:S(2)}) collective-permute-start(bf16[32,1152]{1,0:T(8,128)(2,1)} %copy-done.16), channel_id=1, source_target_pairs={{0,4},{4,0},{8,12},{12,8},{1,5},{5,1},{9,13},{13,9},{2,6},{6,2},{1... | collective-permute-start | bytes 221192 | tf_op jit(solution)/shard_map/ppermute | solution.py:431
  62.6 2.4 %collective-permute-start.7 = (bf16[32,1152]{1,0:T(8,128)(2,1)}, bf16[32,1152]{1,0:T(8,128)(2,1)S(1)}, u32[]{:S(2)}, u32[]{:S(2)}) collective-permute-start(bf16[32,1152]{1,0:T(8,128)(2,1)} %copy-done.15), channel_id=1, source_target_pairs={{0,8},{4,12},{8,0},{12,4},{1,9},{5,13},{9,1},{13,5},{2,10},{6,14},... | collective-permute-start | bytes 221192 | tf_op jit(solution)/shard_map/ppermute | solution.py:431
  65.2 3.2 %all-to-all-done.2.refs_3_ = f32[16,8,128]{2,1,0:T(8,128)S(1)} async-done(((f32[16,8,128]{2,1,0:T(8,128)}), f32[16,8,128]{2,1,0:T(8,128)S(1)}, u32[]{:S(2)}, u32[]{:S(2)}) %all-to-all-start.2) | async-done | bytes 65568 | tf_op jit(solution)/shard_map/all_to_all | solution.py:425
  68.4 1.2 %copy-done.1 = bf16[3,2,288,256]{3,2,1,0:T(8,128)(2,1)S(1)} copy-done((bf16[3,2,288,256]{3,2,1,0:T(8,128)(2,1)S(1)}, bf16[3,2,288,256]{3,2,1,0:T(8,128)(2,1)}, u32[]{:S(2)}) %copy-start.1) | copy-done | bytes 884760
  70.5 5.5 %shard_map.129 = (bf16[32,896]{1,0:T(8,128)(2,1)S(1)}, bf16[32,896]{1,0:T(8,128)(2,1)S(1)}, bf16[32,896]{1,0:T(8,128)(2,1)S(1)}, bf16[32,896]{1,0:T(8,128)(2,1)S(1)}, f32[64,288]{1,0:T(8,128)S(1)}) custom-call(bf16[3,2,288,256]{3,2,1,0:T(8,128)(2,1)S(1)} %copy-done.1, bf16[4,288,128]{2,1,0:T(8,128)(2,1)S(1)} %get-tuple-element.34.refs_0_.refs_1_, ...), custom_call_target="tpu_custom_call" | custom-call | tf_op jit(solution)/shard_map/pallas_call | solution.py:36
  76.0 1.1 %collective-permute-start.9 = (bf16[32,896]{1,0:T(8,128)(2,1)S(1)}, bf16[32,896]{1,0:T(8,128)(2,1)S(1)}, u32[]{:S(2)}, u32[]{:S(2)}) collective-permute-start(bf16[32,896]{1,0:T(8,128)(2,1)S(1)} %get-tuple-element.54), channel_id=1, source_target_pairs={{0,1},{1,0},{2,3},{3,2},{4,5},{5,4},{6,7},{7,6},{8,9},{9,8},{10,11... | collective-permute-start | bytes 172040 | tf_op jit(solution)/shard_map/ppermute | solution.py:431
  77.3 2.2 %collective-permute-start.11 = (bf16[32,896]{1,0:T(8,128)(2,1)S(1)}, bf16[32,896]{1,0:T(8,128)(2,1)S(1)}, u32[]{:S(2)}, u32[]{:S(2)}) collective-permute-start(bf16[32,896]{1,0:T(8,128)(2,1)S(1)} %get-tuple-element.56), channel_id=1, source_target_pairs={{0,3},{1,2},{2,1},{3,0},{4,7},{5,6},{6,5},{7,4},{8,11},{9,10},{10,... | collective-permute-start | bytes 172040 | tf_op jit(solution)/shard_map/ppermute | solution.py:431
  80.2 1.1 %collective-permute-done.10.refs_4_ = bf16[32,896]{1,0:T(8,128)(2,1)S(1)} collective-permute-done((bf16[32,896]{1,0:T(8,128)(2,1)S(1)}, bf16[32,896]{1,0:T(8,128)(2,1)S(1)}, u32[]{:S(2)}, u32[]{:S(2)}) %collective-permute-start.10) | collective-permute-done | bytes 57376 | tf_op jit(solution)/shard_map/ppermute | solution.py:431
  81.3 1.1 %collective-permute-done.11.refs_5_ = bf16[32,896]{1,0:T(8,128)(2,1)S(1)} collective-permute-done((bf16[32,896]{1,0:T(8,128)(2,1)S(1)}, bf16[32,896]{1,0:T(8,128)(2,1)S(1)}, u32[]{:S(2)}, u32[]{:S(2)}) %collective-permute-start.11) | collective-permute-done | bytes 57376 | tf_op jit(solution)/shard_map/ppermute | solution.py:431
  82.8 1.3 %collective-permute-done.12.refs_1_ = f32[64,288]{1,0:T(8,128)S(1)} collective-permute-done((f32[64,288]{1,0:T(8,128)S(1)}, f32[64,288]{1,0:T(8,128)S(1)}, u32[]{:S(2)}, u32[]{:S(2)}) %collective-permute-start.12) | collective-permute-done | bytes 73760 | tf_op jit(solution)/shard_map/ppermute | solution.py:431
  84.1 2.2 %collective-permute-start.15 = (bf16[64,288]{1,0:T(8,128)(2,1)S(1)}, bf16[64,288]{1,0:T(8,128)(2,1)S(1)}, u32[]{:S(2)}, u32[]{:S(2)}) collective-permute-start(bf16[64,288]{1,0:T(8,128)(2,1)S(1)} %shard_map.131.refs_0_), channel_id=1, source_target_pairs={{0,12},{4,8},{8,4},{12,0},{1,13},{5,9},{9,5},{13,1},{2,14},{6,10},... | collective-permute-start | bytes 110600 | tf_op jit(solution)/shard_map/ppermute | solution.py:431
  86.3 2.2 %collective-permute-start.13 = (bf16[64,288]{1,0:T(8,128)(2,1)S(1)}, bf16[64,288]{1,0:T(8,128)(2,1)S(1)}, u32[]{:S(2)}, u32[]{:S(2)}) collective-permute-start(bf16[64,288]{1,0:T(8,128)(2,1)S(1)} %shard_map.131.refs_0_), channel_id=1, source_target_pairs={{0,4},{4,0},{8,12},{12,8},{1,5},{5,1},{9,13},{13,9},{2,6},{6,2},{1... | collective-permute-start | bytes 110600 | tf_op jit(solution)/shard_map/ppermute | solution.py:431
  88.5 1.8 %collective-permute-done.15.refs_3_ = bf16[64,288]{1,0:T(8,128)(2,1)S(1)} collective-permute-done((bf16[64,288]{1,0:T(8,128)(2,1)S(1)}, bf16[64,288]{1,0:T(8,128)(2,1)S(1)}, u32[]{:S(2)}, u32[]{:S(2)}) %collective-permute-start.15) | collective-permute-done | bytes 36896 | tf_op jit(solution)/shard_map/ppermute | solution.py:431
  90.3 1.5 %collective-permute-done.14.refs_2_ = bf16[64,288]{1,0:T(8,128)(2,1)S(1)} collective-permute-done((bf16[64,288]{1,0:T(8,128)(2,1)S(1)}, bf16[64,288]{1,0:T(8,128)(2,1)S(1)}, u32[]{:S(2)}, u32[]{:S(2)}) %collective-permute-start.14) | collective-permute-done | bytes 36896 | tf_op jit(solution)/shard_map/ppermute | solution.py:431
  91.9 2.3 %collective-permute-start.18 = (bf16[64,288]{1,0:T(8,128)(2,1)S(1)}, bf16[64,288]{1,0:T(8,128)(2,1)S(1)}, u32[]{:S(2)}, u32[]{:S(2)}) collective-permute-start(bf16[64,288]{1,0:T(8,128)(2,1)S(1)} %shard_map.132.refs_0_), channel_id=1, source_target_pairs={{0,3},{1,2},{2,1},{3,0},{4,7},{5,6},{6,5},{7,4},{8,11},{9,10},{10,... | collective-permute-start | bytes 110600 | tf_op jit(solution)/shard_map/ppermute | solution.py:431
  95.4 1.5 %collective-permute-done.18.refs_3_ = bf16[64,288]{1,0:T(8,128)(2,1)S(1)} collective-permute-done((bf16[64,288]{1,0:T(8,128)(2,1)S(1)}, bf16[64,288]{1,0:T(8,128)(2,1)S(1)}, u32[]{:S(2)}, u32[]{:S(2)}) %collective-permute-start.18) | collective-permute-done | bytes 36896 | tf_op jit(solution)/shard_map/ppermute | solution.py:431
  97.0 1.2 %collective-permute-done.17.refs_2_ = bf16[64,288]{1,0:T(8,128)(2,1)S(1)} collective-permute-done((bf16[64,288]{1,0:T(8,128)(2,1)S(1)}, bf16[64,288]{1,0:T(8,128)(2,1)S(1)}, u32[]{:S(2)}, u32[]{:S(2)}) %collective-permute-start.17) | collective-permute-done | bytes 36896 | tf_op jit(solution)/shard_map/ppermute | solution.py:431
  (64 shorter events, 18.5 us)
Async XLA Ops:
  3.9 20.2 %all-to-all-start = ((bf16[4,1152,128]{2,1,0:T(8,128)(2,1)}), bf16[4,1152,128]{2,1,0:T(8,128)(2,1)S(1)}, u32[]{:S(2)}, u32[]{:S(2)}) async-start(bf16[4,1152,128]{2,1,0:T(8,128)(2,1)} %get-tuple-element.32), calls=%async_computation | async-start | bytes 2359296 | tf_op jit(solution)/shard_map/all_to_all | solution.py:425
  11.6 20.1 %collective-permute-start.3 = (bf16[4,32,1152]{2,1,0:T(8,128)(2,1)}, bf16[4,32,1152]{2,1,0:T(8,128)(2,1)S(1)}, u32[]{:S(2)}, u32[]{:S(2)}) collective-permute-start(bf16[4,32,1152]{2,1,0:T(8,128)(2,1)} %get-tuple-element.41), channel_id=1, source_target_pairs={{0,4},{4,0},{8,12},{12,8},{1,5},{5,1},{9,13},{13,9},{2,6},{6,2},{1... | collective-permute-start | bytes 884744 | tf_op jit(solution)/shard_map/ppermute | solution.py:431
  13.3 26.6 %collective-permute-start.4 = (bf16[4,32,1152]{2,1,0:T(8,128)(2,1)}, bf16[4,32,1152]{2,1,0:T(8,128)(2,1)S(1)}, u32[]{:S(2)}, u32[]{:S(2)}) collective-permute-start(bf16[4,32,1152]{2,1,0:T(8,128)(2,1)} %get-tuple-element.42), channel_id=1, source_target_pairs={{0,8},{4,12},{8,0},{12,4},{1,9},{5,13},{9,1},{13,5},{2,10},{6,14},... | collective-permute-start | bytes 884744 | tf_op jit(solution)/shard_map/ppermute | solution.py:431
  15.9 24.8 %collective-permute-start.5 = (bf16[4,32,1152]{2,1,0:T(8,128)(2,1)}, bf16[4,32,1152]{2,1,0:T(8,128)(2,1)}, u32[]{:S(2)}, u32[]{:S(2)}) collective-permute-start(bf16[4,32,1152]{2,1,0:T(8,128)(2,1)} %get-tuple-element.43), channel_id=1, source_target_pairs={{0,12},{4,8},{8,4},{12,0},{1,13},{5,9},{9,5},{13,1},{2,14},{6,10},... | collective-permute-start | bytes 884744 | tf_op jit(solution)/shard_map/ppermute | solution.py:431
  17.0 11.9 %copy-start.3 = (bf16[4,320,128]{2,1,0:T(8,128)(2,1)S(1)}, bf16[4,320,128]{2,1,0:T(8,128)(2,1)}, u32[]{:S(2)}) copy-start(bf16[4,320,128]{2,1,0:T(8,128)(2,1)} %get-tuple-element.35.refs_1_) | copy-start | bytes 983044
  27.0 0.9 copy-start
  29.8 17.7 %collective-permute-start = (bf16[608,128]{1,0:T(8,128)(2,1)}, bf16[608,128]{1,0:T(8,128)(2,1)S(1)}, u32[]{:S(2)}, u32[]{:S(2)}) collective-permute-start(bf16[608,128]{1,0:T(8,128)(2,1)} %get-tuple-element.37), channel_id=1, source_target_pairs={{0,1},{1,0},{2,3},{3,2},{4,5},{5,4},{6,7},{7,6},{8,9},{9,8},{10,11... | collective-permute-start | bytes 466952 | tf_op jit(solution)/shard_map/ppermute | solution.py:431
  31.2 16.3 %collective-permute-start.1 = (bf16[608,128]{1,0:T(8,128)(2,1)}, bf16[608,128]{1,0:T(8,128)(2,1)S(1)}, u32[]{:S(2)}, u32[]{:S(2)}) collective-permute-start(bf16[608,128]{1,0:T(8,128)(2,1)} %get-tuple-element.38), channel_id=1, source_target_pairs={{0,2},{1,3},{2,0},{3,1},{4,6},{5,7},{6,4},{7,5},{8,10},{9,11},{10,... | collective-permute-start | bytes 466952 | tf_op jit(solution)/shard_map/ppermute | solution.py:431
  32.5 15.0 %collective-permute-start.2 = (bf16[608,128]{1,0:T(8,128)(2,1)}, bf16[608,128]{1,0:T(8,128)(2,1)S(1)}, u32[]{:S(2)}, u32[]{:S(2)}) collective-permute-start(bf16[608,128]{1,0:T(8,128)(2,1)} %get-tuple-element.39), channel_id=1, source_target_pairs={{0,3},{1,2},{2,1},{3,0},{4,7},{5,6},{6,5},{7,4},{8,11},{9,10},{10,... | collective-permute-start | bytes 466952 | tf_op jit(solution)/shard_map/ppermute | solution.py:431
  34.0 13.5 %all-to-all-start.1 = ((f32[16,8,128]{2,1,0:T(8,128)}), f32[16,8,128]{2,1,0:T(8,128)S(1)}, u32[]{:S(2)}, u32[]{:S(2)}) async-start(f32[16,8,128]{2,1,0:T(8,128)} %get-tuple-element.44), calls=%async_computation.1 | async-start | bytes 131072 | tf_op jit(solution)/shard_map/all_to_all | solution.py:425
  40.6 1.0 copy-start.4
  41.6 1.0 copy-start.6
  42.6 1.0 copy-start.8
  43.5 3.9 %copy-start.2 = (bf16[4,16,1152]{2,1,0:T(8,128)(2,1)S(1)}, bf16[4,16,1152]{2,1,0:T(8,128)(2,1)}, u32[]{:S(2)}) copy-start(bf16[4,16,1152]{2,1,0:T(8,128)(2,1)} %refs_1_.3) | copy-start | bytes 442372
  56.2 12.2 %all-to-all-start.2 = ((f32[16,8,128]{2,1,0:T(8,128)}), f32[16,8,128]{2,1,0:T(8,128)S(1)}, u32[]{:S(2)}, u32[]{:S(2)}) async-start(f32[16,8,128]{2,1,0:T(8,128)} %copy-done.13), calls=%async_computation.2 | async-start | bytes 131072 | tf_op jit(solution)/shard_map/all_to_all | solution.py:425
  60.6 16.7 %collective-permute-start.6 = (bf16[32,1152]{1,0:T(8,128)(2,1)}, bf16[32,1152]{1,0:T(8,128)(2,1)S(1)}, u32[]{:S(2)}, u32[]{:S(2)}) collective-permute-start(bf16[32,1152]{1,0:T(8,128)(2,1)} %copy-done.16), channel_id=1, source_target_pairs={{0,4},{4,0},{8,12},{12,8},{1,5},{5,1},{9,13},{13,9},{2,6},{6,2},{1... | collective-permute-start | bytes 221192 | tf_op jit(solution)/shard_map/ppermute | solution.py:431
  62.6 16.9 %collective-permute-start.7 = (bf16[32,1152]{1,0:T(8,128)(2,1)}, bf16[32,1152]{1,0:T(8,128)(2,1)S(1)}, u32[]{:S(2)}, u32[]{:S(2)}) collective-permute-start(bf16[32,1152]{1,0:T(8,128)(2,1)} %copy-done.15), channel_id=1, source_target_pairs={{0,8},{4,12},{8,0},{12,4},{1,9},{5,13},{9,1},{13,5},{2,10},{6,14},... | collective-permute-start | bytes 221192 | tf_op jit(solution)/shard_map/ppermute | solution.py:431
  65.0 14.5 %collective-permute-start.8 = (bf16[32,1152]{1,0:T(8,128)(2,1)}, bf16[32,1152]{1,0:T(8,128)(2,1)S(1)}, u32[]{:S(2)}, u32[]{:S(2)}) collective-permute-start(bf16[32,1152]{1,0:T(8,128)(2,1)} %copy-done.14), channel_id=1, source_target_pairs={{0,12},{4,8},{8,4},{12,0},{1,13},{5,9},{9,5},{13,1},{2,14},{6,10},... | collective-permute-start | bytes 221192 | tf_op jit(solution)/shard_map/ppermute | solution.py:431
  68.4 1.2 %copy-start.1 = (bf16[3,2,288,256]{3,2,1,0:T(8,128)(2,1)S(1)}, bf16[3,2,288,256]{3,2,1,0:T(8,128)(2,1)}, u32[]{:S(2)}) copy-start(bf16[3,2,288,256]{3,2,1,0:T(8,128)(2,1)} %copy-done) | copy-start | bytes 2654212
  69.6 0.9 copy-start.10
  76.0 4.2 %collective-permute-start.9 = (bf16[32,896]{1,0:T(8,128)(2,1)S(1)}, bf16[32,896]{1,0:T(8,128)(2,1)S(1)}, u32[]{:S(2)}, u32[]{:S(2)}) collective-permute-start(bf16[32,896]{1,0:T(8,128)(2,1)S(1)} %get-tuple-element.54), channel_id=1, source_target_pairs={{0,1},{1,0},{2,3},{3,2},{4,5},{5,4},{6,7},{7,6},{8,9},{9,8},{10,11... | collective-permute-start | bytes 172040 | tf_op jit(solution)/shard_map/ppermute | solution.py:431
  77.1 4.2 %collective-permute-start.10 = (bf16[32,896]{1,0:T(8,128)(2,1)S(1)}, bf16[32,896]{1,0:T(8,128)(2,1)S(1)}, u32[]{:S(2)}, u32[]{:S(2)}) collective-permute-start(bf16[32,896]{1,0:T(8,128)(2,1)S(1)} %get-tuple-element.55), channel_id=1, source_target_pairs={{0,2},{1,3},{2,0},{3,1},{4,6},{5,7},{6,4},{7,5},{8,10},{9,11},{10,... | collective-permute-start | bytes 172040 | tf_op jit(solution)/shard_map/ppermute | solution.py:431
  77.3 5.1 %collective-permute-start.11 = (bf16[32,896]{1,0:T(8,128)(2,1)S(1)}, bf16[32,896]{1,0:T(8,128)(2,1)S(1)}, u32[]{:S(2)}, u32[]{:S(2)}) collective-permute-start(bf16[32,896]{1,0:T(8,128)(2,1)S(1)} %get-tuple-element.56), channel_id=1, source_target_pairs={{0,3},{1,2},{2,1},{3,0},{4,7},{5,6},{6,5},{7,4},{8,11},{9,10},{10,... | collective-permute-start | bytes 172040 | tf_op jit(solution)/shard_map/ppermute | solution.py:431
  82.4 16.8 %copy-start.12 = (bf16[32,1152]{1,0:T(8,128)(2,1)S(1)}, bf16[32,1152]{1,0:T(8,128)(2,1)}, u32[]{:S(2)}) copy-start(bf16[32,1152]{1,0:T(8,128)(2,1)} %copy-done.11) | copy-start | bytes 221188
  82.7 1.4 %collective-permute-start.12 = (f32[64,288]{1,0:T(8,128)S(1)}, f32[64,288]{1,0:T(8,128)S(1)}, u32[]{:S(2)}, u32[]{:S(2)}) collective-permute-start(f32[64,288]{1,0:T(8,128)S(1)} %get-tuple-element.58), channel_id=1, source_target_pairs={{0,16},{16,0},{1,17},{17,1},{2,18},{18,2},{3,19},{19,3},{4,20},{20... | collective-permute-start | bytes 221192 | tf_op jit(solution)/shard_map/ppermute | solution.py:431
  84.1 6.3 %collective-permute-start.15 = (bf16[64,288]{1,0:T(8,128)(2,1)S(1)}, bf16[64,288]{1,0:T(8,128)(2,1)S(1)}, u32[]{:S(2)}, u32[]{:S(2)}) collective-permute-start(bf16[64,288]{1,0:T(8,128)(2,1)S(1)} %shard_map.131.refs_0_), channel_id=1, source_target_pairs={{0,12},{4,8},{8,4},{12,0},{1,13},{5,9},{9,5},{13,1},{2,14},{6,10},... | collective-permute-start | bytes 110600 | tf_op jit(solution)/shard_map/ppermute | solution.py:431
  86.3 5.5 %collective-permute-start.14 = (bf16[64,288]{1,0:T(8,128)(2,1)S(1)}, bf16[64,288]{1,0:T(8,128)(2,1)S(1)}, u32[]{:S(2)}, u32[]{:S(2)}) collective-permute-start(bf16[64,288]{1,0:T(8,128)(2,1)S(1)} %shard_map.131.refs_0_), channel_id=1, source_target_pairs={{0,8},{4,12},{8,0},{12,4},{1,9},{5,13},{9,1},{13,5},{2,10},{6,14},... | collective-permute-start | bytes 110600 | tf_op jit(solution)/shard_map/ppermute | solution.py:431
  86.3 5.5 %collective-permute-start.13 = (bf16[64,288]{1,0:T(8,128)(2,1)S(1)}, bf16[64,288]{1,0:T(8,128)(2,1)S(1)}, u32[]{:S(2)}, u32[]{:S(2)}) collective-permute-start(bf16[64,288]{1,0:T(8,128)(2,1)S(1)} %shard_map.131.refs_0_), channel_id=1, source_target_pairs={{0,4},{4,0},{8,12},{12,8},{1,5},{5,1},{9,13},{13,9},{2,6},{6,2},{1... | collective-permute-start | bytes 110600 | tf_op jit(solution)/shard_map/ppermute | solution.py:431
  91.9 5.1 %collective-permute-start.18 = (bf16[64,288]{1,0:T(8,128)(2,1)S(1)}, bf16[64,288]{1,0:T(8,128)(2,1)S(1)}, u32[]{:S(2)}, u32[]{:S(2)}) collective-permute-start(bf16[64,288]{1,0:T(8,128)(2,1)S(1)} %shard_map.132.refs_0_), channel_id=1, source_target_pairs={{0,3},{1,2},{2,1},{3,0},{4,7},{5,6},{6,5},{7,4},{8,11},{9,10},{10,... | collective-permute-start | bytes 110600 | tf_op jit(solution)/shard_map/ppermute | solution.py:431
  94.1 4.1 %collective-permute-start.17 = (bf16[64,288]{1,0:T(8,128)(2,1)S(1)}, bf16[64,288]{1,0:T(8,128)(2,1)S(1)}, u32[]{:S(2)}, u32[]{:S(2)}) collective-permute-start(bf16[64,288]{1,0:T(8,128)(2,1)S(1)} %shard_map.132.refs_0_), channel_id=1, source_target_pairs={{0,2},{1,3},{2,0},{3,1},{4,6},{5,7},{6,4},{7,5},{8,10},{9,11},{10,... | collective-permute-start | bytes 110600 | tf_op jit(solution)/shard_map/ppermute | solution.py:431
  94.9 4.1 %collective-permute-start.16 = (bf16[64,288]{1,0:T(8,128)(2,1)S(1)}, bf16[64,288]{1,0:T(8,128)(2,1)S(1)}, u32[]{:S(2)}, u32[]{:S(2)}) collective-permute-start(bf16[64,288]{1,0:T(8,128)(2,1)S(1)} %shard_map.132.refs_0_), channel_id=1, source_target_pairs={{0,1},{1,0},{2,3},{3,2},{4,5},{5,4},{6,7},{7,6},{8,9},{9,8},{10,11... | collective-permute-start | bytes 110600 | tf_op jit(solution)/shard_map/ppermute | solution.py:431
  99.1 1.4 %collective-permute-start.19 = (bf16[64,1152]{1,0:T(8,128)(2,1)S(1)}, bf16[64,1152]{1,0:T(8,128)(2,1)S(1)}, u32[]{:S(2)}, u32[]{:S(2)}) collective-permute-start(bf16[64,1152]{1,0:T(8,128)(2,1)S(1)} %shard_map.133.refs_0_), channel_id=1, source_target_pairs={{0,16},{16,0},{1,17},{17,1},{2,18},{18,2},{3,19},{19,3},{4,20},{20... | collective-permute-start | bytes 442376 | tf_op jit(solution)/shard_map/ppermute | solution.py:431
  (8 other events, 5.2 us)

commit v5 on v3

--- a/solution.py
+++ b/solution.py
@@ -21,7 +21,7 @@
     return lax.dot_general(a, b, dims, preferred_element_type=F32)
 
 
-def call(kernel, out_shape, *args, scratch=(), hbm=False, limit=48, after=(), carry=()):
+def call(kernel, out_shape, *args, scratch=(), hbm=False, limit=24, after=(), carry=()):
     vmem = pl.BlockSpec(memory_space=pltpu.VMEM)
     anywhere = pl.BlockSpec(memory_space=pl.ANY)
     main = pl.BlockSpec(memory_space=pltpu.HBM) if hbm else vmem
@@ -37,7 +37,7 @@
         body,
         out_shape=outs + tuple(shape(x.shape, x.dtype) for x in carry),
         in_specs=[main] * used + [anywhere] * extra,
-        out_specs=(vmem,) * len(outs) + (anywhere,) * len(carry),
+        out_specs=(anywhere if hbm else vmem,) * len(outs) + (anywhere,) * len(carry),
         scratch_shapes=list(scratch),
         input_output_aliases={used + len(after) + i: len(outs) + i for i in range(len(carry))},
         compiler_params=pltpu.CompilerParams(vmem_limit_bytes=limit * 1024 * 1024),
@@ -55,16 +55,10 @@
         scores = jnp.where(mask, scores, -1e30)
     peak = jnp.max(scores, axis=0, keepdims=True)
     weights = jnp.exp(scores - peak)
-    return weights / jnp.sum(weights, axis=0, keepdims=True)
-
-
-def head_forward(q_t, k_t, v_t, mask=None):
-    probs = probs_of(k_t.T, q_t, mask)
-    return mm(v_t, probs.astype(BF16))
-
-
-def head_backward(q_t, k_t, v_t, g_t, mask=None, forward=False):
-    probs = probs_of(k_t.T, q_t, mask)
+    return weights * (1.0 / jnp.sum(weights, axis=0, keepdims=True))
+
+
+def head_backward(probs, k_t, v_t, g_t, forward=False):
     low = probs.astype(BF16)
     dvals = mm(g_t, low, NT)
     dprob = mm(v_t.T, g_t)
@@ -83,86 +77,91 @@
     return lax.axis_index(axis) ^ distance
 
 
-def load_all(refs, buffers, sems):
+def pack_kernel(n_t, n_s, sub, *refs):
+    time_ins, ins, refs = refs[:4], refs[4:11], refs[11:]
+    send_ref, sides, times = refs[0], refs[1 : 1 + n_s], refs[1 + n_s : 1 + n_s + n_t]
+    refs = refs[1 + n_s + n_t :]
+    buffers, (turned_ref, codes_ref, sems, out_sems) = refs[:7], refs[7:]
+    k_buf, p_buf, at_buf, b_buf, q_buf, v_buf, g_buf = buffers
     copies = [
         pltpu.make_async_copy(ref, buffer, sems.at[index])
-        for index, (ref, buffer) in enumerate(zip(refs, buffers))
+        for index, (ref, buffer) in enumerate(zip(ins, buffers))
     ]
     for copy in copies:
         copy.start()
-    return copies
-
-
-def pack_time_kernel(n_t, sub, q_ref, k_ref, v_ref, g_ref, *rest):
-    outs, sems = rest[:n_t], rest[n_t]
-    frames = q_ref.shape[1]
-    copies = []
+    sent = []
+
+    def start_copy(source, target):
+        copy = pltpu.make_async_copy(source, target, out_sems.at[len(sent)])
+        copy.start()
+        sent.append(copy)
+
+    frames = time_ins[0].shape[1]
     for k in range(n_t):
         start = pl.multiple_of(peer("tm", k) * sub, sub)
-        for index, ref in enumerate((q_ref, k_ref, v_ref, g_ref)):
+        for index, ref in enumerate(time_ins):
             for f in range(frames):
-                copy = pltpu.make_async_copy(
+                start_copy(
                     ref.at[0, f, pl.ds(start, sub)],
-                    outs[k].at[index, f * sub : (f + 1) * sub],
-                    sems.at[len(copies)],
+                    times[k].at[index, f * sub : (f + 1) * sub],
                 )
-                copy.start()
-                copies.append(copy)
-    for copy in copies:
-        copy.wait()
-
-
-def pack_space_kernel(n_s, *refs):
-    ins, refs = refs[:7], refs[7:]
-    outs, buffers, (turned_ref, sems) = refs[:n_s], refs[n_s : n_s + 7], refs[n_s + 7 :]
-    p_buf, at_buf, b_buf, q_buf, v_buf, k_buf, g_buf = buffers
-    copies = load_all(ins, buffers, sems)
     d_s, tokens = turned_ref.shape[2:]
 
     def flat(ref):
         return ref[0].reshape(tokens, ref.shape[3])
 
-    def send(array, index):
+    def turn(array, index):
         turned = array.T
         for j in range(n_s):
             turned_ref[index, j] = turned[j * d_s : (j + 1) * d_s]
+
+    def send(array, index):
+        turn(array, index)
+        for j in range(n_s):
+            start_copy(turned_ref.at[index, j], send_ref.at[j, index * d_s : (index + 1) * d_s])
+
+    def side(array, index):
+        turn(array, index)
         for k in range(n_s):
-            outs[k][index * d_s : (index + 1) * d_s] = turned_ref[index, peer("space", k)]
+            place = (index - 3) * d_s
+            start_copy(turned_ref.at[index, peer("space", k)], sides[k].at[place : place + d_s])
 
     copies[0].wait()
+    send(flat(k_buf), 1)
     copies[1].wait()
+    patches = flat(p_buf)
     copies[2].wait()
-    patches = flat(p_buf)
+    copies[3].wait()
     codes_q = mm(patches, at_buf[0], NT).astype(BF16)
     codes_v = mm(patches, at_buf[1], NT).astype(BF16)
-    codes_t = jnp.concatenate([codes_q, codes_v], axis=1).T
-    copies[3].wait()
+    copies[4].wait()
     query = (flat(q_buf).astype(F32) + mm(codes_q, b_buf[0])).astype(BF16)
     send(query, 0)
-    copies[4].wait()
+    copies[5].wait()
     value = (flat(v_buf).astype(F32) + mm(codes_v, b_buf[1])).astype(BF16)
     send(value, 2)
-    copies[5].wait()
-    send(flat(k_buf), 1)
-    send(patches, 3)
+    side(patches, 3)
+    codes_ref[...] = jnp.concatenate([codes_q, codes_v], axis=1).T
+    for k in range(n_s):
+        start_copy(codes_ref, sides[k].at[2 * d_s : 2 * d_s + 2 * RANK])
     copies[6].wait()
-    send(flat(g_buf), 4)
-    for k in range(n_s):
-        outs[k][5 * d_s :] = codes_t
+    side(flat(g_buf), 4)
+    for copy in sent:
+        copy.wait()
 
 
 def frame_rows(pieces, f, patch_dev):
     return jnp.concatenate([x[:, f * patch_dev : (f + 1) * patch_dev] for x in pieces], axis=1)
 
 
-def space_forward_kernel(frames, n_s, *refs):
-    packed, qkv_ref, outs = refs[:n_s], refs[n_s], refs[n_s + 1 :]
-    d_s, tokens = outs[0].shape
+def space_forward_kernel(frames, packed_ref, qkv_ref, probs_ref, *refs):
+    *outs, out_buf = refs
+    n_s, d_s, tokens = out_buf.shape
     patch_dev = tokens // frames
     total = n_s * patch_dev
     step = min(total, 256)
     for index in range(3):
-        pieces = [x[index * d_s : (index + 1) * d_s] for x in packed]
+        pieces = [packed_ref[j, index * d_s : (index + 1) * d_s] for j in range(n_s)]
         for f in range(frames):
             qkv_ref[index, f] = frame_rows(pieces, f, patch_dev)
     for f in range(frames):
@@ -174,15 +173,19 @@
             k_h = rows_of(keys, h).astype(BF16)
             v_h = rows_of(vals, h).astype(BF16)
             q_h = rows_of(query, h).astype(BF16)
-            parts = [
-                head_forward(q_h[:, s : s + step], k_h, v_h) for s in range(0, total, step)
-            ]
+            parts = []
+            for s in range(0, total, step):
+                probs = probs_of(k_h.T, q_h[:, s : s + step], None)
+                probs_ref[f, h, :, s : s + step] = probs
+                parts.append(mm(v_h, probs.astype(BF16)))
             heads.append(parts[0] if len(parts) == 1 else jnp.concatenate(parts, axis=1))
         out = jnp.concatenate(heads, axis=0).astype(BF16)
-        for k in range(n_s):
-            outs[k][:, f * patch_dev : (f + 1) * patch_dev] = out[
-                :, k * patch_dev : (k + 1) * patch_dev
+        for j in range(n_s):
+            out_buf[j, :, f * patch_dev : (f + 1) * patch_dev] = out[
+                :, j * patch_dev : (j + 1) * patch_dev
             ]
+    for k in range(n_s):
+        outs[k][...] = out_buf[peer("space", k)]
 
 
 def lane_block(rows):
@@ -207,8 +210,7 @@
 def hidden_kernel(n_t, n_s, *refs):
     pieces, refs = refs[:n_s], refs[n_s:]
     p_ref, at_ref, hidden_ref = refs[:3]
-    sends = refs[3 : 3 + n_t]
-    out_buf, codes_buf = refs[3 + n_t :]
+    *sends, out_buf, codes_buf = refs[3:]
     _, frames, patch_dev, width = p_ref.shape
     tokens = frames * patch_dev
     sub = patch_dev // n_t
@@ -236,9 +238,10 @@
 
 def time_kernel(n_t, sub, x_ref, b_ref, *refs):
     codes_refs, refs = refs[:n_t], refs[n_t:]
-    outs, sends, grad_b_ref = refs[:n_t], refs[n_t : 2 * n_t], refs[2 * n_t]
+    outs, sends, grad_b_ref = refs[:n_t], refs[n_t : n_t + 2], refs[n_t + 2]
     _, width, tokens = x_ref.shape
-    codes = jnp.concatenate([unfold(ref[...]) for ref in codes_refs], axis=0).T
+    codes = [unfold(ref[...]) for ref in codes_refs]
+    codes = jnp.concatenate(codes, axis=0).T
     codes_q = codes[:RANK].astype(BF16)
     codes_v = codes[RANK : 2 * RANK].astype(BF16)
     query = (x_ref[0].astype(F32) + mm(b_ref[2], codes_q, TN)).astype(BF16).astype(F32)
@@ -250,14 +253,10 @@
     mask = lax.rem(row, sub) == lax.rem(col, sub)
     outs_h, d_query, d_vals = [], [], []
     for h in range(width // HEAD_DIM):
-        dq, dv, out = head_backward(
-            rows_of(query, h).astype(BF16),
-            rows_of(keys, h).astype(BF16),
-            rows_of(vals, h).astype(BF16),
-            rows_of(grad, h).astype(BF16),
-            mask,
-            True,
-        )
+        k_h = rows_of(keys, h).astype(BF16)
+        v_h = rows_of(vals, h).astype(BF16)
+        probs = probs_of(k_h.T, rows_of(query, h).astype(BF16), mask)
+        dq, dv, out = head_backward(probs, k_h, v_h, rows_of(grad, h).astype(BF16), True)
         outs_h.append(out)
         d_query.append(dq)
         d_vals.append(dv)
@@ -267,7 +266,7 @@
     d_codes = d_codes.astype(BF16).astype(F32).T
     per = tokens // n_t
     for k in range(n_t):
-        sends[k][...] = fold(d_codes[k * per : (k + 1) * per])
+        sends[k % 2][k // 2] = fold(d_codes[k * per : (k + 1) * per])
     out = jnp.concatenate(outs_h, axis=0).astype(BF16).T
     for k in range(n_t):
         outs[k][...] = out[k * per : (k + 1) * per]
@@ -275,34 +274,37 @@
     grad_b_ref[RANK:] = mm(codes_v, d_vals, NT)
 
 
-def place_codes_kernel(frames, sub, *refs):
+def place_codes_kernel(frames, sub, places, *refs):
     pieces, (out_ref, buf) = refs[:-2], refs[-2:]
     patch_dev = sub * len(pieces)
     for k, piece in enumerate(pieces):
-        rows = unfold(piece[...])
+        rows = unfold(piece[places[k]])
         for f in range(frames):
             start = pl.multiple_of(f * patch_dev + peer("tm", k) * sub, sub)
             buf[pl.ds(start, sub)] = rows[f * sub : (f + 1) * sub]
     out_ref[...] = buf[...].T[: 2 * RANK].astype(BF16)
 
 
-def space_backward_kernel(frames, n_s, qkv_ref, hidden_ref, grad_b_ref, at_ref, at_here_ref, b_here_ref, *refs):
-    packed, dcodes, sends = refs[:n_s], refs[n_s : 2 * n_s], refs[2 * n_s : 3 * n_s]
-    part_ref, cut_buf = refs[3 * n_s :]
+def space_backward_kernel(
+    frames, n_s, qkv_ref, probs_ref, hidden_ref, grad_b_ref, dcodes_ref, at_ref, at_here_ref, b_here_ref, *refs
+):
+    sides, sends, (part_ref, cut_buf, side_buf, dcodes_buf) = refs[:n_s], refs[n_s : 2 * n_s], refs[2 * n_s :]
     d_s = part_ref.shape[1]
     tokens = hidden_ref.shape[0]
     patch_dev = tokens // frames
     total = n_s * patch_dev
     step = min(total, 256)
+    for k in range(n_s):
+        side_buf[peer("space", k)] = sides[k][d_s:]
+        dcodes_buf[peer("space", k)] = dcodes_ref[k]
     ups = jnp.concatenate([at_here_ref[2], at_here_ref[3]], axis=0).T
     grads = []
-    for k in range(n_s):
-        cot = packed[k][4 * d_s : 5 * d_s].astype(F32)
-        grads.append((cot + mm(ups, dcodes[k][...])).astype(BF16))
+    for j in range(n_s):
+        cot = side_buf[j, :d_s].astype(F32)
+        grads.append((cot + mm(ups, dcodes_buf[j])).astype(BF16))
+    codes = [side_buf[j, d_s:] for j in range(n_s)]
     grad_b_q = grad_b_v = None
-    codes = [x[5 * d_s :] for x in packed]
     for f in range(frames):
-        query = qkv_ref[0, f].astype(F32)
         keys = qkv_ref[1, f].astype(F32)
         vals = qkv_ref[2, f].astype(F32)
         grad = frame_rows(grads, f, patch_dev).astype(F32)
@@ -310,11 +312,11 @@
         for h in range(d_s // HEAD_DIM):
             k_h = rows_of(keys, h).astype(BF16)
             v_h = rows_of(vals, h).astype(BF16)
-            q_h = rows_of(query, h).astype(BF16)
             g_h = rows_of(grad, h).astype(BF16)
             dq_parts, dv_sum = [], None
             for s in range(0, total, step):
-                dq, dv, _ = head_backward(q_h[:, s : s + step], k_h, v_h, g_h[:, s : s + step])
+                probs = probs_ref[f, h, :, s : s + step]
+                dq, dv, _ = head_backward(probs, k_h, v_h, g_h[:, s : s + step])
                 dq_parts.append(dq)
                 dv_sum = dv if dv_sum is None else dv_sum + dv
             d_query.append(
@@ -324,11 +326,8 @@
         d_query = jnp.concatenate(d_query, axis=0).astype(BF16)
         d_vals = jnp.concatenate(d_vals, axis=0).astype(BF16)
         partial = jnp.concatenate([mm(b_here_ref[0], d_query), mm(b_here_ref[1], d_vals)], axis=0)
-        partial = partial.astype(BF16)
-        blocks = [partial[:, m * patch_dev : (m + 1) * patch_dev] for m in range(n_s)]
         for k in range(n_s):
-            turned = jnp.concatenate([blocks[m ^ k] for m in range(n_s)], axis=1)
-            sends[k][:, f * total : (f + 1) * total] = turned
+            sends[k][:, f * total : (f + 1) * total] = partial.astype(BF16)
         frame_codes = frame_rows(codes, f, patch_dev)
         term_q = mm(frame_codes[:RANK], d_query, NT)
         term_v = mm(frame_codes[RANK:], d_vals, NT)
@@ -336,7 +335,7 @@
         grad_b_v = term_v if grad_b_v is None else grad_b_v + term_v
     part_ref[:RANK] = grad_b_q
     part_ref[RANK:] = grad_b_v
-    grad_a = mm(dcodes[0][...], hidden_ref[...])
+    grad_a = mm(dcodes_ref[0], hidden_ref[...])
     pad = -(-d_s // 128) * 128
     for j in range(n_s):
         cut_buf[j, 0, :, :d_s] = grad_a[:, j * d_s : (j + 1) * d_s].astype(BF16)
@@ -355,14 +354,16 @@
 
 
 def merge_kernel(frames, n_s, n_d, part_ref, *refs):
-    packed, recvs, refs = refs[:n_s], refs[n_s : 2 * n_s], refs[2 * n_s :]
-    sends, buf = refs[:n_d], refs[n_d]
+    sides, recvs, refs = refs[:n_s], refs[n_s : 2 * n_s], refs[2 * n_s :]
+    sends, (buf, patches_buf) = refs[:n_d], refs[n_d:]
     d_s = part_ref.shape[1]
-    tokens = packed[0].shape[1]
+    tokens = sides[0].shape[1]
+    for k in range(n_s):
+        patches_buf[peer("space", k)] = sides[k][:d_s]
     patch_dev = tokens // frames
     total = n_s * patch_dev
     pad = -(-d_s // 128) * 128
-    patches = [x[3 * d_s : 4 * d_s] for x in packed]
+    patches = [patches_buf[j] for j in range(n_s)]
     terms = []
     for f in range(frames):
         codes = [recv[:, f * total : (f + 1) * total].astype(F32) for recv in recvs]
@@ -379,7 +380,10 @@
 
 
 def total_kernel(*refs):
-    refs[-1][...] = add_up([ref[...].astype(F32) for ref in refs[:-1]]).astype(refs[-1].dtype)
+    terms = [ref[...].astype(F32) for ref in refs[:-1]]
+    while len(terms) > 1:
+        terms = [terms[i] + terms[i + 1] for i in range(0, len(terms), 2)]
+    refs[-1][...] = terms[0].astype(refs[-1].dtype)
 
 
 def join_kernel(*refs):
@@ -423,6 +427,51 @@
     return [pieces[0]] + [
         lax.ppermute(pieces[k], axis, [(i, i ^ k) for i in range(size)]) for k in range(1, size)
     ]
+
+
+def swap(array, axes):
+    return lax.all_to_all(array, axes, split_axis=0, concat_axis=0, tiled=True)
+
+
+def stack_kernel(places, *refs):
+    for index, (ref, place) in enumerate(zip(refs[:-1], places)):
+        refs[-1][index] = ref[place]
+
+
+def exchange_steps(even, odd, axis):
+    size = lax.axis_size(axis)
+    held = [((even, odd)[k % 2], k // 2) for k in range(size)]
+    step = 1
+    while step < size:
+        moving = [k for k in range(size) if k & step]
+        sent = odd
+        if step > 1:
+            arrays, places = zip(*[held[k] for k in moving])
+            sent = call(
+                functools.partial(stack_kernel, places), shape(odd.shape, odd.dtype), *arrays
+            )
+        got = lax.ppermute(sent, axis, [(i, i ^ step) for i in range(size)])
+        for index, k in enumerate(moving):
+            held[k] = (got, index)
+        step *= 2
+    return [array for array, _ in held], [place for _, place in held]
+
+
+def double_kernel(own_ref, got_ref, out_ref):
+    size = own_ref.shape[0]
+    out_ref[:size] = own_ref[...]
+    out_ref[size:] = got_ref[...]
+
+
+def share_steps(array, axis):
+    size = lax.axis_size(axis)
+    held = array[None]
+    step = 1
+    while step < size:
+        got = lax.ppermute(held, axis, [(i, i ^ step) for i in range(size)])
+        held = call(double_kernel, shape((2 * step,) + array.shape, array.dtype), held, got)
+        step *= 2
+    return held
 
 
 def share(array, axis):
@@ -446,30 +495,31 @@
     dma = pltpu.SemaphoreType.DMA
     pad = -(-d_s // 128) * 128
 
-    time_pieces = call(
-        functools.partial(pack_time_kernel, n_t, sub),
-        [shape((4, frames * sub, width), BF16)] * n_t,
-        query_t, key_t, value_t, cotangent,
-        scratch=[dma((4 * frames * n_t,))],
+    spatial = (key_s, patches, downs, adapters_b, query_s, value_s, cotangent)
+    send, *pieces = call(
+        functools.partial(pack_kernel, n_t, n_s, sub),
+        [shape((n_s, 3 * d_s, tokens), BF16)]
+        + [shape((2 * d_s + 2 * RANK, tokens), BF16)] * n_s
+        + [shape((4, frames * sub, width), BF16)] * n_t,
+        query_t, key_t, value_t, cotangent, *spatial,
+        scratch=[pltpu.VMEM(x.shape, BF16) for x in spatial]
+        + [
+            pltpu.VMEM((5, n_s, d_s, tokens), BF16),
+            pltpu.VMEM((2 * RANK, tokens), BF16),
+            dma((7,)),
+            dma((6 * n_s + 4 * frames * n_t,)),
+        ],
         hbm=True, limit=54,
     )
-    time_pieces = exchange(time_pieces, "tm")
-    packed = call(
-        functools.partial(pack_space_kernel, n_s),
-        [shape((5 * d_s + 2 * RANK, tokens), BF16)] * n_s,
-        patches, downs, adapters_b, query_s, value_s, key_s, cotangent,
-        scratch=[
-            pltpu.VMEM(x.shape, BF16)
-            for x in (patches, downs, adapters_b, query_s, value_s, key_s, cotangent)
-        ]
-        + [pltpu.VMEM((5, n_s, d_s, tokens), BF16), dma((7,))],
-        hbm=True, limit=54,
-    )
-    packed = exchange(packed, "space")
-    qkv, *out_s = call(
-        functools.partial(space_forward_kernel, frames, n_s),
-        [shape((3, frames, d_s, total), BF16)] + [shape((d_s, tokens), BF16)] * n_s,
-        *packed,
+    time_pieces = exchange(pieces[n_s:], "tm")
+    packed = swap(send, "space")
+    sides = exchange(pieces[:n_s], "space")
+    qkv, probs, *out_s = call(
+        functools.partial(space_forward_kernel, frames),
+        [shape((3, frames, d_s, total), BF16), shape((frames, d_s // HEAD_DIM, total, total), F32)]
+        + [shape((d_s, tokens), BF16)] * n_s,
+        packed,
+        scratch=[pltpu.VMEM((n_s, d_s, tokens), BF16)],
     )
     out_s = exchange(out_s, "space")
     hidden, *codes = call(
@@ -483,42 +533,52 @@
     timed = call(
         functools.partial(time_kernel, n_t, sub),
         [shape((frames * sub, width), BF16)] * n_t
-        + [shape((8, 128), F32)] * n_t
+        + [shape((n_t // 2, 8, 128), F32)] * 2
         + [shape((2 * RANK, width), F32)],
         turned, adapters_b, *codes,
-    )
-    out_t, dcodes, time_grad_b = timed[:n_t], timed[n_t : 2 * n_t], timed[2 * n_t]
-    dcodes = exchange(dcodes, "tm")
+        after=sides[1:],
+    )
+    out_t, (even, odd, time_grad_b) = timed[:n_t], timed[n_t:]
+    dcodes, places = exchange_steps(even, odd, "tm")
     dcodes = call(
-        functools.partial(place_codes_kernel, frames, sub),
+        functools.partial(place_codes_kernel, frames, sub, places),
         shape((2 * RANK, tokens), BF16),
         *dcodes,
         scratch=[pltpu.VMEM((tokens, 128), F32)],
     )
-    dcodes = share(dcodes, "space")
+    dcodes = share_steps(dcodes, "space")
+
+    def late(k):
+        return lax.ppermute(out_t[k], "tm", [(i, i ^ k) for i in range(n_t)])
+
+    out_t[1] = late(1)
     backward = call(
         functools.partial(space_backward_kernel, frames, n_s),
         [shape((2 * RANK, frames * total + 2 * pad), BF16)] * n_s + [shape((2 * RANK, d_s), F32)],
-        qkv, hidden, time_grad_b, downs, downs_here, ups_here, *packed, *dcodes,
-        scratch=[pltpu.VMEM((n_s, 2, 2 * RANK, pad), BF16)],
-        carry=out_t,
-    )
-    partial, part, out_t = backward[:n_s], backward[n_s], backward[n_s + 1 :]
+        qkv, probs, hidden, time_grad_b, dcodes, downs, downs_here, ups_here, *sides,
+        scratch=[
+            pltpu.VMEM((n_s, 2, 2 * RANK, pad), BF16),
+            pltpu.VMEM((n_s, d_s + 2 * RANK, tokens), BF16),
+            pltpu.VMEM((n_s, 2 * RANK, tokens), BF16),
+        ],
+        after=[out_t[1]],
+        carry=[out_t[2]],
+    )
+    partial, part, out_t[2] = backward[:n_s], backward[n_s], backward[n_s + 1]
     partial = exchange(partial, "space")
-    out_t = exchange(out_t, "tm")
+    out_t[2] = late(2)
     rows = 8 * RANK // n_d
-    sums = call(
+    *sums, out_t[3] = call(
         functools.partial(merge_kernel, frames, n_s, n_d),
         [shape((rows, d_s), F32)] * n_d,
-        part, *packed, *partial,
-        scratch=[pltpu.VMEM((n_d, rows, d_s), F32)],
-    )
-    sums = call(total_kernel, shape((rows, d_s), BF16), *exchange(sums, "dp"), after=out_t[1:])
-    step = 1
-    while step < n_t:
-        other = lax.ppermute(sums, "tm", [(i, i ^ step) for i in range(n_t)])
-        sums = call(total_kernel, shape((rows, d_s), BF16), sums, other)
-        step *= 2
+        part, *sides, *partial,
+        scratch=[pltpu.VMEM((n_d, rows, d_s), F32), pltpu.VMEM((n_s, d_s, tokens), BF16)],
+        after=[out_t[2]],
+        carry=[out_t[3]],
+    )
+    out_t[3] = late(3)
+    sums = call(total_kernel, shape((rows, d_s), BF16), *exchange(sums, "dp"))
+    sums = call(total_kernel, shape((rows, d_s), BF16), *share(sums, "tm"), after=[out_t[3]])
     sums = call(
         join_kernel,
         shape((rows, width), BF16),

time: 104 us -> 149 us (1.43)
  Pallas kernels: 23.5 us -> 51.2 us
  waiting for transfers between devices: 37.6 us -> 46.1 us
  local copies, waits for them, and re-layouts: 0.2 us -> 6.42 us
  starting transfers between devices: 41.5 us -> 44.4 us
    pallas_call x15 -> x16, Pallas kernels: 23.5 us -> 51.2 us  [call(): pl.pallas_call(body, out_shape=outs + tuple((shape(x.shape, x.dtype) for...]
    ppermute x29 -> x23, starting transfers between devices: 41.1 us -> 25.2 us  [exchange(): lax.ppermute(pieces[k], axis, [(i, i ^ k) for i in range(size)])]
    ppermute x2 -> x7, starting transfers between devices: 0.37 us -> 14 us  [the longest x3 7.37 us: late(): return lax.ppermute(out_t[k], 'tm', [(i, i ^ k) for i in range(n_t)])]
    all_to_all x0 -> x1, waiting for transfers between devices: none -> 11.3 us  [swap(): return lax.all_to_all(array, axes, split_axis=0, concat_axis=0, tiled=True)]
    unnamed x10 -> x26, local copies, waits for them, and re-layouts: 0.02 us -> 6.25 us
    all_to_all x0 -> x1, starting transfers between devices: none -> 5.18 us  [swap(): return lax.all_to_all(array, axes, split_axis=0, concat_axis=0, tiled=True)]
    ppermute x29 -> x23, waiting for transfers between devices: 28.6 us -> 25.4 us  [exchange(): lax.ppermute(pieces[k], axis, [(i, i ^ k) for i in range(size)])]
    ppermute x2 -> x7, waiting for transfers between devices: 9.01 us -> 9.43 us  [the longest x2 3.58 us: share_steps(): got = lax.ppermute(held, axis, [(i, i ^ step) for i in range(size)])]
  transfers between devices with their start and end apart: 31 -> 31, of which waited for: 19 -> 16; matrix products, arithmetic and copies ran while one was open for 0% -> 0% of each run, Pallas kernels for 8% -> 3%
where the time goes in v5:
time: 149 us
  Pallas kernels  51.2 us (34%)
  waiting for transfers between devices  46.1 us (31%)
  starting transfers between devices  44.4 us (30%)
  local copies, waits for them, and re-layouts  6.42 us (4%)
    pallas_call x16, Pallas kernels, call(): pl.pallas_call(body, out_shape=outs + tuple((shape(x.shape, x.dtype) for...  51.2 us
    ppermute x23, waiting for transfers between devices, exchange(): lax.ppermute(pieces[k], axis, [(i, i ^ k) for i in range(size)])  25.4 us
    ppermute x23, starting transfers between devices, exchange(): lax.ppermute(pieces[k], axis, [(i, i ^ k) for i in range(size)])  25.2 us
    all_to_all x1, waiting for transfers between devices, swap(): return lax.all_to_all(array, axes, split_axis=0, concat_axis=0, tiled=True)  11.3 us
    ppermute x3, starting transfers between devices, late(): return lax.ppermute(out_t[k], 'tm', [(i, i ^ k) for i in range(n_t)])  7.37 us
    unnamed x26, local copies, waits for them, and re-layouts  6.25 us
    all_to_all x1, starting transfers between devices, swap(): return lax.all_to_all(array, axes, split_axis=0, concat_axis=0, tiled=True)  5.18 us
    ppermute x2, starting transfers between devices, exchange_steps(): got = lax.ppermute(sent, axis, [(i, i ^ step) for i in range(size)])  4.94 us
  transfers between devices with their start and end apart: 31, of which 16 were waited for; matrix products, arithmetic and copies ran while one was open for 0% of the time, Pallas kernels for 3%

profile of v5, /device:TPU:0, one launch (start us, length us, event | category | flops | bytes accessed | tf_op | source)
XLA Modules:
  0.0 149.0 jit_solution(11738872340406555439)
XLA Ops:
  0.6 37.5 %shard_map.121 = (bf16[4,864,128]{2,1,0:T(8,128)(2,1)}, bf16[608,128]{1,0:T(8,128)(2,1)}, bf16[608,128]{1,0:T(8,128)(2,1)}, bf16[608,128]{1,0:T(8,128)(2,1)}, bf...) custom-call(bf16[1,2,64,1152]{3,2,1,0:T(8,128)(2,1)} %refs_0_.1, ...), custom_call_target="tpu_custom_call" | custom-call | tf_op jit(solution)/shard_map/pallas_call | solution.py:36
  38.1 5.2 %all-to-all-start = ((bf16[4,864,128]{2,1,0:T(8,128)(2,1)}), bf16[4,864,128]{2,1,0:T(8,128)(2,1)S(1)}, u32[]{:S(2)}, u32[]{:S(2)}) async-start(bf16[4,864,128]{2,1,0:T(8,128)(2,1)} %get-tuple-element.41), calls=%async_computation | async-start | bytes 1769472 | tf_op jit(solution)/shard_map/all_to_all | solution.py:433
  43.3 2.0 %collective-permute-start.9 = (bf16[608,128]{1,0:T(8,128)(2,1)}, bf16[608,128]{1,0:T(8,128)(2,1)S(1)}, u32[]{:S(2)}, u32[]{:S(2)}) collective-permute-start(bf16[608,128]{1,0:T(8,128)(2,1)} %get-tuple-element.55), channel_id=1, source_target_pairs={{0,1},{1,0},{2,3},{3,2},{4,5},{5,4},{6,7},{7,6},{8,9},{9,8},{10,11... | collective-permute-start | bytes 466952 | tf_op jit(solution)/shard_map/ppermute | solution.py:428
  45.3 11.3 %all-to-all-done.refs_0_ = bf16[4,864,128]{2,1,0:T(8,128)(2,1)S(1)} async-done(((bf16[4,864,128]{2,1,0:T(8,128)(2,1)}), bf16[4,864,128]{2,1,0:T(8,128)(2,1)S(1)}, u32[]{:S(2)}, u32[]{:S(2)}) %all-to-all-start) | async-done | bytes 884768 | tf_op jit(solution)/shard_map/all_to_all | solution.py:433
  56.6 2.9 %shard_map.122 = (bf16[3,2,288,256]{3,2,1,0:T(8,128)(2,1)S(1)}, f32[2,4,256,256]{3,2,1,0:T(8,128)S(1)}, bf16[288,128]{1,0:T(8,128)(2,1)S(1)}, bf16[288,128]{1,0:...) custom-call(bf16[4,864,128]{2,1,0:T(8,128)(2,1)S(1)} %all-to-all-done.refs_0_), custom_call_target="tpu_custom_call" | custom-call | tf_op jit(solution)/shard_map/pallas_call | solution.py:36
  60.5 1.5 collective-permute-start
  61.9 1.6 %collective-permute-start.3 = (bf16[4,32,1152]{2,1,0:T(8,128)(2,1)}, bf16[4,32,1152]{2,1,0:T(8,128)(2,1)S(1)}, u32[]{:S(2)}, u32[]{:S(2)}) collective-permute-start(bf16[4,32,1152]{2,1,0:T(8,128)(2,1)} %get-tuple-element.48), channel_id=1, source_target_pairs={{0,4},{4,0},{8,12},{12,8},{1,5},{5,1},{9,13},{13,9},{2,6},{6,2},{1... | collective-permute-start | bytes 884744 | tf_op jit(solution)/shard_map/ppermute | solution.py:428
  63.5 2.6 %collective-permute-start.4 = (bf16[4,32,1152]{2,1,0:T(8,128)(2,1)}, bf16[4,32,1152]{2,1,0:T(8,128)(2,1)S(1)}, u32[]{:S(2)}, u32[]{:S(2)}) collective-permute-start(bf16[4,32,1152]{2,1,0:T(8,128)(2,1)} %get-tuple-element.49), channel_id=1, source_target_pairs={{0,8},{4,12},{8,0},{12,4},{1,9},{5,13},{9,1},{13,5},{2,10},{6,14},... | collective-permute-start | bytes 884744 | tf_op jit(solution)/shard_map/ppermute | solution.py:428
  66.4 2.0 %collective-permute-start.2 = (bf16[288,128]{1,0:T(8,128)(2,1)S(1)}, bf16[288,128]{1,0:T(8,128)(2,1)S(1)}, u32[]{:S(2)}, u32[]{:S(2)}) collective-permute-start(bf16[288,128]{1,0:T(8,128)(2,1)S(1)} %get-tuple-element.45), channel_id=1, source_target_pairs={{0,3},{1,2},{2,1},{3,0},{4,7},{5,6},{6,5},{7,4},{8,11},{9,10},{10,... | collective-permute-start | bytes 221192 | tf_op jit(solution)/shard_map/ppermute | solution.py:428
  68.4 5.1 %collective-permute-done.1.refs_2_ = bf16[288,128]{1,0:T(8,128)(2,1)S(1)} collective-permute-done((bf16[288,128]{1,0:T(8,128)(2,1)S(1)}, bf16[288,128]{1,0:T(8,128)(2,1)S(1)}, u32[]{:S(2)}, u32[]{:S(2)}) %collective-permute-start.1) | collective-permute-done | bytes 73760 | tf_op jit(solution)/shard_map/ppermute | solution.py:428
  76.5 9.7 %collective-permute-done.4.refs_2_ = bf16[4,32,1152]{2,1,0:T(8,128)(2,1)S(1)} collective-permute-done((bf16[4,32,1152]{2,1,0:T(8,128)(2,1)}, bf16[4,32,1152]{2,1,0:T(8,128)(2,1)S(1)}, u32[]{:S(2)}, u32[]{:S(2)}) %collective-permute-start.4) | collective-permute-done | bytes 294944 | tf_op jit(solution)/shard_map/ppermute | solution.py:428
  86.2 1.9 %collective-permute-start.8 = (f32[8,128]{1,0:T(8,128)S(1)}, f32[8,128]{1,0:T(8,128)S(1)}, u32[]{:S(2)}, u32[]{:S(2)}) collective-permute-start(f32[8,128]{1,0:T(8,128)S(1)} %get-tuple-element.54), channel_id=1, source_target_pairs={{0,12},{4,8},{8,4},{12,0},{1,13},{5,9},{9,5},{13,1},{2,14},{6,10},... | collective-permute-start | bytes 12296 | tf_op jit(solution)/shard_map/ppermute | solution.py:428
  89.5 1.2 collective-permute-done.7.refs_4_
  91.6 5.0 %shard_map.125 = (bf16[32,1152]{1,0:T(8,128)(2,1)S(1)}, bf16[32,1152]{1,0:T(8,128)(2,1)S(1)}, bf16[32,1152]{1,0:T(8,128)(2,1)S(1)}, bf16[32,1152]{1,0:T(8,128)(2...) custom-call(bf16[4,1152,128]{2,1,0:T(8,128)(2,1)S(1)} %shard_map.124.refs_0_, ...), custom_call_target="tpu_custom_call" | custom-call | tf_op jit(solution)/shard_map/pallas_call | solution.py:36
  97.9 2.0 %collective-permute-start.13 = (f32[2,8,128]{2,1,0:T(8,128)S(1)}, f32[2,8,128]{2,1,0:T(8,128)S(1)}, u32[]{:S(2)}, u32[]{:S(2)}) collective-permute-start(f32[2,8,128]{2,1,0:T(8,128)S(1)} %get-tuple-element.64), channel_id=1, source_target_pairs={{0,4},{4,0},{8,12},{12,8},{1,5},{5,1},{9,13},{13,9},{2,6},{6,2},{1... | collective-permute-start | bytes 24584 | tf_op jit(solution)/shard_map/ppermute | solution.py:453
  99.8 1.7 %collective-permute-done.13.refs_1_ = f32[2,8,128]{2,1,0:T(8,128)S(1)} collective-permute-done((f32[2,8,128]{2,1,0:T(8,128)S(1)}, f32[2,8,128]{2,1,0:T(8,128)S(1)}, u32[]{:S(2)}, u32[]{:S(2)}) %collective-permute-start.13) | collective-permute-done | bytes 8224 | tf_op jit(solution)/shard_map/ppermute | solution.py:453
  101.5 3.0 %collective-permute-start.14 = (f32[2,8,128]{2,1,0:T(8,128)S(1)}, f32[2,8,128]{2,1,0:T(8,128)S(1)}, u32[]{:S(2)}, u32[]{:S(2)}) collective-permute-start(f32[2,8,128]{2,1,0:T(8,128)S(1)} %shard_map.126), channel_id=1, source_target_pairs={{0,8},{4,12},{8,0},{12,4},{1,9},{5,13},{9,1},{13,5},{2,10},{6,14},... | collective-permute-start | bytes 24584 | tf_op jit(solution)/shard_map/ppermute | solution.py:453
  104.5 1.6 %collective-permute-done.14.refs_2_.refs_3_ = f32[2,8,128]{2,1,0:T(8,128)S(1)} collective-permute-done((f32[2,8,128]{2,1,0:T(8,128)S(1)}, f32[2,8,128]{2,1,0:T(8,128)S(1)}, u32[]{:S(2)}, u32[]{:S(2)}) %collective-permute-start.14) | collective-permute-done | bytes 8224 | tf_op jit(solution)/shard_map/ppermute | solution.py:453
  107.3 2.0 %collective-permute-start.12 = (bf16[32,1152]{1,0:T(8,128)(2,1)}, bf16[32,1152]{1,0:T(8,128)(2,1)S(1)}, u32[]{:S(2)}, u32[]{:S(2)}) collective-permute-start(bf16[32,1152]{1,0:T(8,128)(2,1)} %copy-done.12), channel_id=1, source_target_pairs={{0,4},{4,0},{8,12},{12,8},{1,5},{5,1},{9,13},{13,9},{2,6},{6,2},{1... | collective-permute-start | bytes 221192 | tf_op jit(solution)/shard_map/ppermute | solution.py:552
  110.7 3.0 %collective-permute-done.16.refs_1_ = bf16[2,32,128]{2,1,0:T(8,128)(2,1)S(1)} collective-permute-done((bf16[2,32,128]{2,1,0:T(8,128)(2,1)S(1)}, bf16[2,32,128]{2,1,0:T(8,128)(2,1)S(1)}, u32[]{:S(2)}, u32[]{:S(2)}) %collective-permute-start.16) | collective-permute-done | bytes 16416 | tf_op jit(solution)/shard_map/ppermute | solution.py:471
  115.8 2.8 %shard_map.130 = (bf16[32,1280]{1,0:T(8,128)(2,1)S(1)}, bf16[32,1280]{1,0:T(8,128)(2,1)S(1)}, bf16[32,1280]{1,0:T(8,128)(2,1)S(1)}, bf16[32,1280]{1,0:T(8,128)(2...) custom-call(bf16[3,2,288,256]{3,2,1,0:T(8,128)(2,1)S(1)} %copy-done.3, ...), custom_call_target="tpu_custom_call", output_to_operand_aliasing={{5}: (13, {})} | custom-call | tf_op jit(solution)/shard_map/pallas_call | solution.py:36
  119.7 1.2 collective-permute-start.19
  120.9 1.3 collective-permute-start.20
  122.2 2.9 %collective-permute-start.17 = (bf16[32,1152]{1,0:T(8,128)(2,1)}, bf16[32,1152]{1,0:T(8,128)(2,1)S(1)}, u32[]{:S(2)}, u32[]{:S(2)}) collective-permute-start(bf16[32,1152]{1,0:T(8,128)(2,1)} %copy-done.11), channel_id=1, source_target_pairs={{0,8},{4,12},{8,0},{12,4},{1,9},{5,13},{9,1},{13,5},{2,10},{6,14},... | collective-permute-start | bytes 221192 | tf_op jit(solution)/shard_map/ppermute | solution.py:552
  125.1 2.5 %collective-permute-done.17.refs_9_.refs_3_ = bf16[32,1152]{1,0:T(8,128)(2,1)S(1)} collective-permute-done((bf16[32,1152]{1,0:T(8,128)(2,1)}, bf16[32,1152]{1,0:T(8,128)(2,1)S(1)}, u32[]{:S(2)}, u32[]{:S(2)}) %collective-permute-start.17) | collective-permute-done | bytes 73760 | tf_op jit(solution)/shard_map/ppermute | solution.py:552
  128.1 2.4 %collective-permute-start.21 = (bf16[32,1152]{1,0:T(8,128)(2,1)S(1)}, bf16[32,1152]{1,0:T(8,128)(2,1)S(1)}, u32[]{:S(2)}, u32[]{:S(2)}) collective-permute-start(bf16[32,1152]{1,0:T(8,128)(2,1)S(1)} %get-tuple-element.74), channel_id=1, source_target_pairs={{0,12},{4,8},{8,4},{12,0},{1,13},{5,9},{9,5},{13,1},{2,14},{6,10},... | collective-permute-start | bytes 221192 | tf_op jit(solution)/shard_map/ppermute | solution.py:552
  130.5 1.5 %collective-permute-start.25 = (bf16[64,288]{1,0:T(8,128)(2,1)S(1)}, bf16[64,288]{1,0:T(8,128)(2,1)S(1)}, u32[]{:S(2)}, u32[]{:S(2)}) collective-permute-start(bf16[64,288]{1,0:T(8,128)(2,1)S(1)} %shard_map.133.refs_0_), channel_id=1, source_target_pairs={{0,12},{4,8},{8,4},{12,0},{1,13},{5,9},{9,5},{13,1},{2,14},{6,10},... | collective-permute-start | bytes 110600 | tf_op jit(solution)/shard_map/ppermute | solution.py:428
  133.2 1.8 %collective-permute-start.23 = (bf16[64,288]{1,0:T(8,128)(2,1)S(1)}, bf16[64,288]{1,0:T(8,128)(2,1)S(1)}, u32[]{:S(2)}, u32[]{:S(2)}) collective-permute-start(bf16[64,288]{1,0:T(8,128)(2,1)S(1)} %shard_map.133.refs_0_), channel_id=1, source_target_pairs={{0,4},{4,0},{8,12},{12,8},{1,5},{5,1},{9,13},{13,9},{2,6},{6,2},{1... | collective-permute-start | bytes 110600 | tf_op jit(solution)/shard_map/ppermute | solution.py:428
  135.0 2.0 %collective-permute-done.25.refs_3_ = bf16[64,288]{1,0:T(8,128)(2,1)S(1)} collective-permute-done((bf16[64,288]{1,0:T(8,128)(2,1)S(1)}, bf16[64,288]{1,0:T(8,128)(2,1)S(1)}, u32[]{:S(2)}, u32[]{:S(2)}) %collective-permute-start.25) | collective-permute-done | bytes 36896 | tf_op jit(solution)/shard_map/ppermute | solution.py:428
  137.0 2.9 %collective-permute-done.24.refs_2_ = bf16[64,288]{1,0:T(8,128)(2,1)S(1)} collective-permute-done((bf16[64,288]{1,0:T(8,128)(2,1)S(1)}, bf16[64,288]{1,0:T(8,128)(2,1)S(1)}, u32[]{:S(2)}, u32[]{:S(2)}) %collective-permute-start.24) | collective-permute-done | bytes 36896 | tf_op jit(solution)/shard_map/ppermute | solution.py:428
  140.0 1.6 %collective-permute-start.28 = (bf16[64,288]{1,0:T(8,128)(2,1)S(1)}, bf16[64,288]{1,0:T(8,128)(2,1)S(1)}, u32[]{:S(2)}, u32[]{:S(2)}) collective-permute-start(bf16[64,288]{1,0:T(8,128)(2,1)S(1)} %shard_map.134.refs_0_), channel_id=1, source_target_pairs={{0,3},{1,2},{2,1},{3,0},{4,7},{5,6},{6,5},{7,4},{8,11},{9,10},{10,... | collective-permute-start | bytes 110600 | tf_op jit(solution)/shard_map/ppermute | solution.py:428
  143.5 1.7 %collective-permute-done.28.refs_3_ = bf16[64,288]{1,0:T(8,128)(2,1)S(1)} collective-permute-done((bf16[64,288]{1,0:T(8,128)(2,1)S(1)}, bf16[64,288]{1,0:T(8,128)(2,1)S(1)}, u32[]{:S(2)}, u32[]{:S(2)}) %collective-permute-start.28) | collective-permute-done | bytes 36896 | tf_op jit(solution)/shard_map/ppermute | solution.py:428
  (74 shorter events, 20.6 us)
Async XLA Ops:
  0.6 73.8 %copy-start = (bf16[4,1152,16]{1,2,0:T(8,128)(2,1)S(1)}, bf16[4,1152,16]{1,2,0:T(8,128)(2,1)}, u32[]{:S(2)}) copy-start(bf16[4,1152,16]{1,2,0:T(8,128)(2,1)} %param.17) | copy-start | bytes 442372
  38.1 18.5 %all-to-all-start = ((bf16[4,864,128]{2,1,0:T(8,128)(2,1)}), bf16[4,864,128]{2,1,0:T(8,128)(2,1)S(1)}, u32[]{:S(2)}, u32[]{:S(2)}) async-start(bf16[4,864,128]{2,1,0:T(8,128)(2,1)} %get-tuple-element.41), calls=%async_computation | async-start | bytes 1769472 | tf_op jit(solution)/shard_map/all_to_all | solution.py:433
  43.3 23.0 %collective-permute-start.9 = (bf16[608,128]{1,0:T(8,128)(2,1)}, bf16[608,128]{1,0:T(8,128)(2,1)S(1)}, u32[]{:S(2)}, u32[]{:S(2)}) collective-permute-start(bf16[608,128]{1,0:T(8,128)(2,1)} %get-tuple-element.55), channel_id=1, source_target_pairs={{0,1},{1,0},{2,3},{3,2},{4,5},{5,4},{6,7},{7,6},{8,9},{9,8},{10,11... | collective-permute-start | bytes 466952 | tf_op jit(solution)/shard_map/ppermute | solution.py:428
  60.5 5.9 %collective-permute-start = (bf16[288,128]{1,0:T(8,128)(2,1)S(1)}, bf16[288,128]{1,0:T(8,128)(2,1)S(1)}, u32[]{:S(2)}, u32[]{:S(2)}) collective-permute-start(bf16[288,128]{1,0:T(8,128)(2,1)S(1)} %get-tuple-element.43), channel_id=1, source_target_pairs={{0,1},{1,0},{2,3},{3,2},{4,5},{5,4},{6,7},{7,6},{8,9},{9,8},{10,11... | collective-permute-start | bytes 221192 | tf_op jit(solution)/shard_map/ppermute | solution.py:428
  61.9 13.8 %collective-permute-start.3 = (bf16[4,32,1152]{2,1,0:T(8,128)(2,1)}, bf16[4,32,1152]{2,1,0:T(8,128)(2,1)S(1)}, u32[]{:S(2)}, u32[]{:S(2)}) collective-permute-start(bf16[4,32,1152]{2,1,0:T(8,128)(2,1)} %get-tuple-element.48), channel_id=1, source_target_pairs={{0,4},{4,0},{8,12},{12,8},{1,5},{5,1},{9,13},{13,9},{2,6},{6,2},{1... | collective-permute-start | bytes 884744 | tf_op jit(solution)/shard_map/ppermute | solution.py:428
  63.5 22.7 %collective-permute-start.4 = (bf16[4,32,1152]{2,1,0:T(8,128)(2,1)}, bf16[4,32,1152]{2,1,0:T(8,128)(2,1)S(1)}, u32[]{:S(2)}, u32[]{:S(2)}) collective-permute-start(bf16[4,32,1152]{2,1,0:T(8,128)(2,1)} %get-tuple-element.49), channel_id=1, source_target_pairs={{0,8},{4,12},{8,0},{12,4},{1,9},{5,13},{9,1},{13,5},{2,10},{6,14},... | collective-permute-start | bytes 884744 | tf_op jit(solution)/shard_map/ppermute | solution.py:428
  66.1 20.1 %collective-permute-start.5 = (bf16[4,32,1152]{2,1,0:T(8,128)(2,1)}, bf16[4,32,1152]{2,1,0:T(8,128)(2,1)S(1)}, u32[]{:S(2)}, u32[]{:S(2)}) collective-permute-start(bf16[4,32,1152]{2,1,0:T(8,128)(2,1)} %get-tuple-element.50), channel_id=1, source_target_pairs={{0,12},{4,8},{8,4},{12,0},{1,13},{5,9},{9,5},{13,1},{2,14},{6,10},... | collective-permute-start | bytes 884744 | tf_op jit(solution)/shard_map/ppermute | solution.py:428
  66.3 7.1 %collective-permute-start.1 = (bf16[288,128]{1,0:T(8,128)(2,1)S(1)}, bf16[288,128]{1,0:T(8,128)(2,1)S(1)}, u32[]{:S(2)}, u32[]{:S(2)}) collective-permute-start(bf16[288,128]{1,0:T(8,128)(2,1)S(1)} %get-tuple-element.44), channel_id=1, source_target_pairs={{0,2},{1,3},{2,0},{3,1},{4,6},{5,7},{6,4},{7,5},{8,10},{9,11},{10,... | collective-permute-start | bytes 221192 | tf_op jit(solution)/shard_map/ppermute | solution.py:428
  66.4 7.1 %collective-permute-start.2 = (bf16[288,128]{1,0:T(8,128)(2,1)S(1)}, bf16[288,128]{1,0:T(8,128)(2,1)S(1)}, u32[]{:S(2)}, u32[]{:S(2)}) collective-permute-start(bf16[288,128]{1,0:T(8,128)(2,1)S(1)} %get-tuple-element.45), channel_id=1, source_target_pairs={{0,3},{1,2},{2,1},{3,0},{4,7},{5,6},{6,5},{7,4},{8,11},{9,10},{10,... | collective-permute-start | bytes 221192 | tf_op jit(solution)/shard_map/ppermute | solution.py:428
  73.4 16.0 %collective-permute-start.10 = (bf16[608,128]{1,0:T(8,128)(2,1)}, bf16[608,128]{1,0:T(8,128)(2,1)S(1)}, u32[]{:S(2)}, u32[]{:S(2)}) collective-permute-start(bf16[608,128]{1,0:T(8,128)(2,1)} %get-tuple-element.56), channel_id=1, source_target_pairs={{0,2},{1,3},{2,0},{3,1},{4,6},{5,7},{6,4},{7,5},{8,10},{9,11},{10,... | collective-permute-start | bytes 466952 | tf_op jit(solution)/shard_map/ppermute | solution.py:428
  73.5 16.0 %collective-permute-start.11 = (bf16[608,128]{1,0:T(8,128)(2,1)}, bf16[608,128]{1,0:T(8,128)(2,1)S(1)}, u32[]{:S(2)}, u32[]{:S(2)}) collective-permute-start(bf16[608,128]{1,0:T(8,128)(2,1)} %get-tuple-element.57), channel_id=1, source_target_pairs={{0,3},{1,2},{2,1},{3,0},{4,7},{5,6},{6,5},{7,4},{8,11},{9,10},{10,... | collective-permute-start | bytes 466952 | tf_op jit(solution)/shard_map/ppermute | solution.py:428
  75.8 13.7 %collective-permute-start.6 = (f32[8,128]{1,0:T(8,128)S(1)}, f32[8,128]{1,0:T(8,128)S(1)}, u32[]{:S(2)}, u32[]{:S(2)}) collective-permute-start(f32[8,128]{1,0:T(8,128)S(1)} %get-tuple-element.52), channel_id=1, source_target_pairs={{0,4},{4,0},{8,12},{12,8},{1,5},{5,1},{9,13},{13,9},{2,6},{6,2},{1... | collective-permute-start | bytes 12296 | tf_op jit(solution)/shard_map/ppermute | solution.py:428
  86.2 4.5 %collective-permute-start.7 = (f32[8,128]{1,0:T(8,128)S(1)}, f32[8,128]{1,0:T(8,128)S(1)}, u32[]{:S(2)}, u32[]{:S(2)}) collective-permute-start(f32[8,128]{1,0:T(8,128)S(1)} %get-tuple-element.53), channel_id=1, source_target_pairs={{0,8},{4,12},{8,0},{12,4},{1,9},{5,13},{9,1},{13,5},{2,10},{6,14},... | collective-permute-start | bytes 12296 | tf_op jit(solution)/shard_map/ppermute | solution.py:428
  86.2 5.4 %collective-permute-start.8 = (f32[8,128]{1,0:T(8,128)S(1)}, f32[8,128]{1,0:T(8,128)S(1)}, u32[]{:S(2)}, u32[]{:S(2)}) collective-permute-start(f32[8,128]{1,0:T(8,128)S(1)} %get-tuple-element.54), channel_id=1, source_target_pairs={{0,12},{4,8},{8,4},{12,0},{1,13},{5,9},{9,5},{13,1},{2,14},{6,10},... | collective-permute-start | bytes 12296 | tf_op jit(solution)/shard_map/ppermute | solution.py:428
  97.9 3.7 %collective-permute-start.13 = (f32[2,8,128]{2,1,0:T(8,128)S(1)}, f32[2,8,128]{2,1,0:T(8,128)S(1)}, u32[]{:S(2)}, u32[]{:S(2)}) collective-permute-start(f32[2,8,128]{2,1,0:T(8,128)S(1)} %get-tuple-element.64), channel_id=1, source_target_pairs={{0,4},{4,0},{8,12},{12,8},{1,5},{5,1},{9,13},{13,9},{2,6},{6,2},{1... | collective-permute-start | bytes 24584 | tf_op jit(solution)/shard_map/ppermute | solution.py:453
  101.5 4.6 %collective-permute-start.14 = (f32[2,8,128]{2,1,0:T(8,128)S(1)}, f32[2,8,128]{2,1,0:T(8,128)S(1)}, u32[]{:S(2)}, u32[]{:S(2)}) collective-permute-start(f32[2,8,128]{2,1,0:T(8,128)S(1)} %shard_map.126), channel_id=1, source_target_pairs={{0,8},{4,12},{8,0},{12,4},{1,9},{5,13},{9,1},{13,5},{2,10},{6,14},... | collective-permute-start | bytes 24584 | tf_op jit(solution)/shard_map/ppermute | solution.py:453
  106.3 3.7 %collective-permute-start.15 = (bf16[1,32,128]{2,1,0:T(8,128)(2,1)S(1)}, bf16[1,32,128]{2,1,0:T(8,128)(2,1)S(1)}, u32[]{:S(2)}, u32[]{:S(2)}) collective-permute-start(bf16[1,32,128]{2,1,0:T(8,128)(2,1)S(1)} %bitcast.8), channel_id=1, source_target_pairs={{0,1},{1,0},{2,3},{3,2},{4,5},{5,4},{6,7},{7,6},{8,9},{9,8},{10,11... | collective-permute-start | bytes 24584 | tf_op jit(solution)/shard_map/ppermute | solution.py:471
  107.3 6.4 %collective-permute-start.12 = (bf16[32,1152]{1,0:T(8,128)(2,1)}, bf16[32,1152]{1,0:T(8,128)(2,1)S(1)}, u32[]{:S(2)}, u32[]{:S(2)}) collective-permute-start(bf16[32,1152]{1,0:T(8,128)(2,1)} %copy-done.12), channel_id=1, source_target_pairs={{0,4},{4,0},{8,12},{12,8},{1,5},{5,1},{9,13},{13,9},{2,6},{6,2},{1... | collective-permute-start | bytes 221192 | tf_op jit(solution)/shard_map/ppermute | solution.py:552
  110.0 3.7 %collective-permute-start.16 = (bf16[2,32,128]{2,1,0:T(8,128)(2,1)S(1)}, bf16[2,32,128]{2,1,0:T(8,128)(2,1)S(1)}, u32[]{:S(2)}, u32[]{:S(2)}) collective-permute-start(bf16[2,32,128]{2,1,0:T(8,128)(2,1)S(1)} %shard_map.128.refs_0_), channel_id=1, source_target_pairs={{0,2},{1,3},{2,0},{3,1},{4,6},{5,7},{6,4},{7,5},{8,10},{9,11},{10,... | collective-permute-start | bytes 49160 | tf_op jit(solution)/shard_map/ppermute | solution.py:471
  118.6 9.0 %collective-permute-start.18 = (bf16[32,1280]{1,0:T(8,128)(2,1)S(1)}, bf16[32,1280]{1,0:T(8,128)(2,1)S(1)}, u32[]{:S(2)}, u32[]{:S(2)}) collective-permute-start(bf16[32,1280]{1,0:T(8,128)(2,1)S(1)} %get-tuple-element.70), channel_id=1, source_target_pairs={{0,1},{1,0},{2,3},{3,2},{4,5},{5,4},{6,7},{7,6},{8,9},{9,8},{10,11... | collective-permute-start | bytes 245768 | tf_op jit(solution)/shard_map/ppermute | solution.py:428
  119.7 8.0 %collective-permute-start.19 = (bf16[32,1280]{1,0:T(8,128)(2,1)S(1)}, bf16[32,1280]{1,0:T(8,128)(2,1)S(1)}, u32[]{:S(2)}, u32[]{:S(2)}) collective-permute-start(bf16[32,1280]{1,0:T(8,128)(2,1)S(1)} %get-tuple-element.71), channel_id=1, source_target_pairs={{0,2},{1,3},{2,0},{3,1},{4,6},{5,7},{6,4},{7,5},{8,10},{9,11},{10,... | collective-permute-start | bytes 245768 | tf_op jit(solution)/shard_map/ppermute | solution.py:428
  120.9 6.8 %collective-permute-start.20 = (bf16[32,1280]{1,0:T(8,128)(2,1)S(1)}, bf16[32,1280]{1,0:T(8,128)(2,1)S(1)}, u32[]{:S(2)}, u32[]{:S(2)}) collective-permute-start(bf16[32,1280]{1,0:T(8,128)(2,1)S(1)} %get-tuple-element.72), channel_id=1, source_target_pairs={{0,3},{1,2},{2,1},{3,0},{4,7},{5,6},{6,5},{7,4},{8,11},{9,10},{10,... | collective-permute-start | bytes 245768 | tf_op jit(solution)/shard_map/ppermute | solution.py:428
  122.2 5.5 %collective-permute-start.17 = (bf16[32,1152]{1,0:T(8,128)(2,1)}, bf16[32,1152]{1,0:T(8,128)(2,1)S(1)}, u32[]{:S(2)}, u32[]{:S(2)}) collective-permute-start(bf16[32,1152]{1,0:T(8,128)(2,1)} %copy-done.11), channel_id=1, source_target_pairs={{0,8},{4,12},{8,0},{12,4},{1,9},{5,13},{9,1},{13,5},{2,10},{6,14},... | collective-permute-start | bytes 221192 | tf_op jit(solution)/shard_map/ppermute | solution.py:552
  128.0 2.5 %collective-permute-start.22 = (f32[64,288]{1,0:T(8,128)S(1)}, f32[64,288]{1,0:T(8,128)S(1)}, u32[]{:S(2)}, u32[]{:S(2)}) collective-permute-start(f32[64,288]{1,0:T(8,128)S(1)} %get-tuple-element.76), channel_id=1, source_target_pairs={{0,16},{16,0},{1,17},{17,1},{2,18},{18,2},{3,19},{19,3},{4,20},{20... | collective-permute-start | bytes 221192 | tf_op jit(solution)/shard_map/ppermute | solution.py:428
  128.1 6.9 %collective-permute-start.21 = (bf16[32,1152]{1,0:T(8,128)(2,1)S(1)}, bf16[32,1152]{1,0:T(8,128)(2,1)S(1)}, u32[]{:S(2)}, u32[]{:S(2)}) collective-permute-start(bf16[32,1152]{1,0:T(8,128)(2,1)S(1)} %get-tuple-element.74), channel_id=1, source_target_pairs={{0,12},{4,8},{8,4},{12,0},{1,13},{5,9},{9,5},{13,1},{2,14},{6,10},... | collective-permute-start | bytes 221192 | tf_op jit(solution)/shard_map/ppermute | solution.py:552
  130.5 6.5 %collective-permute-start.25 = (bf16[64,288]{1,0:T(8,128)(2,1)S(1)}, bf16[64,288]{1,0:T(8,128)(2,1)S(1)}, u32[]{:S(2)}, u32[]{:S(2)}) collective-permute-start(bf16[64,288]{1,0:T(8,128)(2,1)S(1)} %shard_map.133.refs_0_), channel_id=1, source_target_pairs={{0,12},{4,8},{8,4},{12,0},{1,13},{5,9},{9,5},{13,1},{2,14},{6,10},... | collective-permute-start | bytes 110600 | tf_op jit(solution)/shard_map/ppermute | solution.py:428
  132.1 7.8 %collective-permute-start.24 = (bf16[64,288]{1,0:T(8,128)(2,1)S(1)}, bf16[64,288]{1,0:T(8,128)(2,1)S(1)}, u32[]{:S(2)}, u32[]{:S(2)}) collective-permute-start(bf16[64,288]{1,0:T(8,128)(2,1)S(1)} %shard_map.133.refs_0_), channel_id=1, source_target_pairs={{0,8},{4,12},{8,0},{12,4},{1,9},{5,13},{9,1},{13,5},{2,10},{6,14},... | collective-permute-start | bytes 110600 | tf_op jit(solution)/shard_map/ppermute | solution.py:428
  133.2 6.7 %collective-permute-start.23 = (bf16[64,288]{1,0:T(8,128)(2,1)S(1)}, bf16[64,288]{1,0:T(8,128)(2,1)S(1)}, u32[]{:S(2)}, u32[]{:S(2)}) collective-permute-start(bf16[64,288]{1,0:T(8,128)(2,1)S(1)} %shard_map.133.refs_0_), channel_id=1, source_target_pairs={{0,4},{4,0},{8,12},{12,8},{1,5},{5,1},{9,13},{13,9},{2,6},{6,2},{1... | collective-permute-start | bytes 110600 | tf_op jit(solution)/shard_map/ppermute | solution.py:428
  140.0 5.3 %collective-permute-start.28 = (bf16[64,288]{1,0:T(8,128)(2,1)S(1)}, bf16[64,288]{1,0:T(8,128)(2,1)S(1)}, u32[]{:S(2)}, u32[]{:S(2)}) collective-permute-start(bf16[64,288]{1,0:T(8,128)(2,1)S(1)} %shard_map.134.refs_0_), channel_id=1, source_target_pairs={{0,3},{1,2},{2,1},{3,0},{4,7},{5,6},{6,5},{7,4},{8,11},{9,10},{10,... | collective-permute-start | bytes 110600 | tf_op jit(solution)/shard_map/ppermute | solution.py:428
  141.6 4.1 %collective-permute-start.27 = (bf16[64,288]{1,0:T(8,128)(2,1)S(1)}, bf16[64,288]{1,0:T(8,128)(2,1)S(1)}, u32[]{:S(2)}, u32[]{:S(2)}) collective-permute-start(bf16[64,288]{1,0:T(8,128)(2,1)S(1)} %shard_map.134.refs_0_), channel_id=1, source_target_pairs={{0,2},{1,3},{2,0},{3,1},{4,6},{5,7},{6,4},{7,5},{8,10},{9,11},{10,... | collective-permute-start | bytes 110600 | tf_op jit(solution)/shard_map/ppermute | solution.py:428
  142.5 4.1 %collective-permute-start.26 = (bf16[64,288]{1,0:T(8,128)(2,1)S(1)}, bf16[64,288]{1,0:T(8,128)(2,1)S(1)}, u32[]{:S(2)}, u32[]{:S(2)}) collective-permute-start(bf16[64,288]{1,0:T(8,128)(2,1)S(1)} %shard_map.134.refs_0_), channel_id=1, source_target_pairs={{0,1},{1,0},{2,3},{3,2},{4,5},{5,4},{6,7},{7,6},{8,9},{9,8},{10,11... | collective-permute-start | bytes 110600 | tf_op jit(solution)/shard_map/ppermute | solution.py:428
  146.7 1.4 collective-permute-start.29
  (12 other events, 101.3 us)

commit v6 on v5

--- a/solution.py
+++ b/solution.py
@@ -79,13 +79,13 @@
 
 def pack_kernel(n_t, n_s, sub, *refs):
     time_ins, ins, refs = refs[:4], refs[4:11], refs[11:]
-    send_ref, sides, times = refs[0], refs[1 : 1 + n_s], refs[1 + n_s : 1 + n_s + n_t]
-    refs = refs[1 + n_s + n_t :]
-    buffers, (turned_ref, codes_ref, sems, out_sems) = refs[:7], refs[7:]
+    firsts, sides, times = refs[:n_s], refs[n_s : 2 * n_s], refs[2 * n_s : 2 * n_s + n_t]
+    refs = refs[2 * n_s + n_t :]
+    time_bufs, buffers, (turned_ref, codes_ref, sems, out_sems) = refs[:4], refs[4:11], refs[11:]
     k_buf, p_buf, at_buf, b_buf, q_buf, v_buf, g_buf = buffers
     copies = [
         pltpu.make_async_copy(ref, buffer, sems.at[index])
-        for index, (ref, buffer) in enumerate(zip(ins, buffers))
+        for index, (ref, buffer) in enumerate(zip(ins + time_ins, buffers + time_bufs))
     ]
     for copy in copies:
         copy.start()
@@ -96,15 +96,6 @@
         copy.start()
         sent.append(copy)
 
-    frames = time_ins[0].shape[1]
-    for k in range(n_t):
-        start = pl.multiple_of(peer("tm", k) * sub, sub)
-        for index, ref in enumerate(time_ins):
-            for f in range(frames):
-                start_copy(
-                    ref.at[0, f, pl.ds(start, sub)],
-                    times[k].at[index, f * sub : (f + 1) * sub],
-                )
     d_s, tokens = turned_ref.shape[2:]
 
     def flat(ref):
@@ -117,14 +108,12 @@
 
     def send(array, index):
         turn(array, index)
-        for j in range(n_s):
-            start_copy(turned_ref.at[index, j], send_ref.at[j, index * d_s : (index + 1) * d_s])
-
-    def side(array, index):
-        turn(array, index)
         for k in range(n_s):
-            place = (index - 3) * d_s
-            start_copy(turned_ref.at[index, peer("space", k)], sides[k].at[place : place + d_s])
+            targets, place = (firsts, index) if index < 3 else (sides, index - 3)
+            start_copy(
+                turned_ref.at[index, peer("space", k)],
+                targets[k].at[place * d_s : (place + 1) * d_s],
+            )
 
     copies[0].wait()
     send(flat(k_buf), 1)
@@ -140,12 +129,22 @@
     copies[5].wait()
     value = (flat(v_buf).astype(F32) + mm(codes_v, b_buf[1])).astype(BF16)
     send(value, 2)
-    side(patches, 3)
+    send(patches, 3)
     codes_ref[...] = jnp.concatenate([codes_q, codes_v], axis=1).T
     for k in range(n_s):
         start_copy(codes_ref, sides[k].at[2 * d_s : 2 * d_s + 2 * RANK])
+    frames = time_ins[0].shape[1]
+    for index, buffer in enumerate(time_bufs):
+        copies[7 + index].wait()
+        for k in range(n_t):
+            start = pl.multiple_of(peer("tm", k) * sub, sub)
+            for f in range(frames):
+                start_copy(
+                    buffer.at[0, f, pl.ds(start, sub)],
+                    times[k].at[index, f * sub : (f + 1) * sub],
+                )
     copies[6].wait()
-    side(flat(g_buf), 4)
+    send(flat(g_buf), 4)
     for copy in sent:
         copy.wait()
 
@@ -154,14 +153,14 @@
     return jnp.concatenate([x[:, f * patch_dev : (f + 1) * patch_dev] for x in pieces], axis=1)
 
 
-def space_forward_kernel(frames, packed_ref, qkv_ref, probs_ref, *refs):
-    *outs, out_buf = refs
-    n_s, d_s, tokens = out_buf.shape
+def space_forward_kernel(frames, n_s, *refs):
+    packed, (qkv_ref, probs_ref, *outs) = refs[:n_s], refs[n_s:]
+    d_s, tokens = outs[0].shape
     patch_dev = tokens // frames
     total = n_s * patch_dev
     step = min(total, 256)
     for index in range(3):
-        pieces = [packed_ref[j, index * d_s : (index + 1) * d_s] for j in range(n_s)]
+        pieces = [x[index * d_s : (index + 1) * d_s] for x in packed]
         for f in range(frames):
             qkv_ref[index, f] = frame_rows(pieces, f, patch_dev)
     for f in range(frames):
@@ -180,12 +179,10 @@
                 parts.append(mm(v_h, probs.astype(BF16)))
             heads.append(parts[0] if len(parts) == 1 else jnp.concatenate(parts, axis=1))
         out = jnp.concatenate(heads, axis=0).astype(BF16)
-        for j in range(n_s):
-            out_buf[j, :, f * patch_dev : (f + 1) * patch_dev] = out[
-                :, j * patch_dev : (j + 1) * patch_dev
+        for k in range(n_s):
+            outs[k][:, f * patch_dev : (f + 1) * patch_dev] = out[
+                :, k * patch_dev : (k + 1) * patch_dev
             ]
-    for k in range(n_s):
-        outs[k][...] = out_buf[peer("space", k)]
 
 
 def lane_block(rows):
@@ -288,21 +285,18 @@
 def space_backward_kernel(
     frames, n_s, qkv_ref, probs_ref, hidden_ref, grad_b_ref, dcodes_ref, at_ref, at_here_ref, b_here_ref, *refs
 ):
-    sides, sends, (part_ref, cut_buf, side_buf, dcodes_buf) = refs[:n_s], refs[n_s : 2 * n_s], refs[2 * n_s :]
+    sides, sends, (part_ref, cut_buf) = refs[:n_s], refs[n_s : 2 * n_s], refs[2 * n_s :]
     d_s = part_ref.shape[1]
     tokens = hidden_ref.shape[0]
     patch_dev = tokens // frames
     total = n_s * patch_dev
     step = min(total, 256)
-    for k in range(n_s):
-        side_buf[peer("space", k)] = sides[k][d_s:]
-        dcodes_buf[peer("space", k)] = dcodes_ref[k]
     ups = jnp.concatenate([at_here_ref[2], at_here_ref[3]], axis=0).T
     grads = []
-    for j in range(n_s):
-        cot = side_buf[j, :d_s].astype(F32)
-        grads.append((cot + mm(ups, dcodes_buf[j])).astype(BF16))
-    codes = [side_buf[j, d_s:] for j in range(n_s)]
+    for k in range(n_s):
+        cot = sides[k][d_s : 2 * d_s].astype(F32)
+        grads.append((cot + mm(ups, dcodes_ref[k])).astype(BF16))
+    codes = [x[2 * d_s :] for x in sides]
     grad_b_q = grad_b_v = None
     for f in range(frames):
         keys = qkv_ref[1, f].astype(F32)
@@ -326,8 +320,11 @@
         d_query = jnp.concatenate(d_query, axis=0).astype(BF16)
         d_vals = jnp.concatenate(d_vals, axis=0).astype(BF16)
         partial = jnp.concatenate([mm(b_here_ref[0], d_query), mm(b_here_ref[1], d_vals)], axis=0)
+        partial = partial.astype(BF16)
+        blocks = [partial[:, m * patch_dev : (m + 1) * patch_dev] for m in range(n_s)]
         for k in range(n_s):
-            sends[k][:, f * total : (f + 1) * total] = partial.astype(BF16)
+            turned = jnp.concatenate([blocks[m ^ k] for m in range(n_s)], axis=1)
+            sends[k][:, f * total : (f + 1) * total] = turned
         frame_codes = frame_rows(codes, f, patch_dev)
         term_q = mm(frame_codes[:RANK], d_query, NT)
         term_v = mm(frame_codes[RANK:], d_vals, NT)
@@ -355,15 +352,13 @@
 
 def merge_kernel(frames, n_s, n_d, part_ref, *refs):
     sides, recvs, refs = refs[:n_s], refs[n_s : 2 * n_s], refs[2 * n_s :]
-    sends, (buf, patches_buf) = refs[:n_d], refs[n_d:]
+    sends, buf = refs[:n_d], refs[n_d]
     d_s = part_ref.shape[1]
     tokens = sides[0].shape[1]
-    for k in range(n_s):
-        patches_buf[peer("space", k)] = sides[k][:d_s]
     patch_dev = tokens // frames
     total = n_s * patch_dev
     pad = -(-d_s // 128) * 128
-    patches = [patches_buf[j] for j in range(n_s)]
+    patches = [x[:d_s] for x in sides]
     terms = []
     for f in range(frames):
         codes = [recv[:, f * total : (f + 1) * total].astype(F32) for recv in recvs]
@@ -423,14 +418,7 @@
 
 
 def exchange(pieces, axis):
-    size = lax.axis_size(axis)
-    return [pieces[0]] + [
-        lax.ppermute(pieces[k], axis, [(i, i ^ k) for i in range(size)]) for k in range(1, size)
-    ]
-
-
-def swap(array, axes):
-    return lax.all_to_all(array, axes, split_axis=0, concat_axis=0, tiled=True)
+    return [pieces[0]] + hops(pieces[1:], axis, 1)
 
 
 def stack_kernel(places, *refs):
@@ -438,7 +426,7 @@
         refs[-1][index] = ref[place]
 
 
-def exchange_steps(even, odd, axis):
+def exchange_steps(even, odd, axis, carry=()):
     size = lax.axis_size(axis)
     held = [((even, odd)[k % 2], k // 2) for k in range(size)]
     step = 1
@@ -447,14 +435,17 @@
         sent = odd
         if step > 1:
             arrays, places = zip(*[held[k] for k in moving])
-            sent = call(
-                functools.partial(stack_kernel, places), shape(odd.shape, odd.dtype), *arrays
+            sent, *carry = call(
+                functools.partial(stack_kernel, places),
+                [shape(odd.shape, odd.dtype)],
+                *arrays,
+                carry=carry,
             )
         got = lax.ppermute(sent, axis, [(i, i ^ step) for i in range(size)])
         for index, k in enumerate(moving):
             held[k] = (got, index)
         step *= 2
-    return [array for array, _ in held], [place for _, place in held]
+    return [array for array, _ in held], [place for _, place in held], carry
 
 
 def double_kernel(own_ref, got_ref, out_ref):
@@ -472,6 +463,14 @@
         held = call(double_kernel, shape((2 * step,) + array.shape, array.dtype), held, got)
         step *= 2
     return held
+
+
+def hops(arrays, axis, first):
+    size = lax.axis_size(axis)
+    return [
+        lax.ppermute(array, axis, [(i, i ^ k) for i in range(size)])
+        for k, array in enumerate(arrays, first)
+    ]
 
 
 def share(array, axis):
@@ -496,39 +495,42 @@
     pad = -(-d_s // 128) * 128
 
     spatial = (key_s, patches, downs, adapters_b, query_s, value_s, cotangent)
-    send, *pieces = call(
+    pieces = call(
         functools.partial(pack_kernel, n_t, n_s, sub),
-        [shape((n_s, 3 * d_s, tokens), BF16)]
+        [shape((3 * d_s, tokens), BF16)] * n_s
         + [shape((2 * d_s + 2 * RANK, tokens), BF16)] * n_s
         + [shape((4, frames * sub, width), BF16)] * n_t,
         query_t, key_t, value_t, cotangent, *spatial,
-        scratch=[pltpu.VMEM(x.shape, BF16) for x in spatial]
+        scratch=[pltpu.VMEM(query_t.shape, BF16)] * 4
+        + [pltpu.VMEM(x.shape, BF16) for x in spatial]
         + [
             pltpu.VMEM((5, n_s, d_s, tokens), BF16),
             pltpu.VMEM((2 * RANK, tokens), BF16),
-            dma((7,)),
+            dma((11,)),
             dma((6 * n_s + 4 * frames * n_t,)),
         ],
         hbm=True, limit=54,
     )
-    time_pieces = exchange(pieces[n_s:], "tm")
-    packed = swap(send, "space")
-    sides = exchange(pieces[:n_s], "space")
+    firsts = exchange(pieces[:n_s], "space")
+    sides = pieces[n_s : 2 * n_s]
+    time_pieces = exchange(pieces[2 * n_s :], "tm")
     qkv, probs, *out_s = call(
-        functools.partial(space_forward_kernel, frames),
+        functools.partial(space_forward_kernel, frames, n_s),
         [shape((3, frames, d_s, total), BF16), shape((frames, d_s // HEAD_DIM, total, total), F32)]
         + [shape((d_s, tokens), BF16)] * n_s,
-        packed,
-        scratch=[pltpu.VMEM((n_s, d_s, tokens), BF16)],
+        *firsts,
+        after=[time_pieces[2]],
     )
     out_s = exchange(out_s, "space")
+    third = -(-(n_s - 1) // 3)
     hidden, *codes = call(
         functools.partial(hidden_kernel, n_t, n_s),
         [shape((tokens, width), BF16)] + [shape((8, 128), F32)] * n_t,
         *out_s, patches, downs,
+        carry=sides[1 : 1 + third],
         scratch=[pltpu.VMEM((n_s, d_s, tokens), BF16), pltpu.VMEM((tokens, 128), F32)],
     )
-    codes = exchange(codes, "tm")
+    codes, sides[1 : 1 + third] = exchange(codes[:n_t], "tm"), hops(codes[n_t:], "space", 1)
     turned = call(turn_kernel, shape((4, width, n_t * frames * sub), BF16), *time_pieces)
     timed = call(
         functools.partial(time_kernel, n_t, sub),
@@ -536,10 +538,13 @@
         + [shape((n_t // 2, 8, 128), F32)] * 2
         + [shape((2 * RANK, width), F32)],
         turned, adapters_b, *codes,
-        after=sides[1:],
-    )
-    out_t, (even, odd, time_grad_b) = timed[:n_t], timed[n_t:]
-    dcodes, places = exchange_steps(even, odd, "tm")
+        after=sides[1 : 1 + third],
+        carry=sides[1 + third : 1 + 2 * third],
+    )
+    out_t, (even, odd, time_grad_b) = timed[:n_t], timed[n_t : n_t + 3]
+    sides[1 + third : 1 + 2 * third] = hops(timed[n_t + 3 :], "space", 1 + third)
+    dcodes, places, rest = exchange_steps(even, odd, "tm", sides[1 + 2 * third :])
+    sides[1 + 2 * third :] = hops(rest, "space", 1 + 2 * third)
     dcodes = call(
         functools.partial(place_codes_kernel, frames, sub, places),
         shape((2 * RANK, tokens), BF16),
@@ -548,35 +553,30 @@
     )
     dcodes = share_steps(dcodes, "space")
 
-    def late(k):
-        return lax.ppermute(out_t[k], "tm", [(i, i ^ k) for i in range(n_t)])
-
-    out_t[1] = late(1)
+    out_t[1:2] = hops(out_t[1:2], "tm", 1)
     backward = call(
         functools.partial(space_backward_kernel, frames, n_s),
         [shape((2 * RANK, frames * total + 2 * pad), BF16)] * n_s + [shape((2 * RANK, d_s), F32)],
         qkv, probs, hidden, time_grad_b, dcodes, downs, downs_here, ups_here, *sides,
         scratch=[
             pltpu.VMEM((n_s, 2, 2 * RANK, pad), BF16),
-            pltpu.VMEM((n_s, d_s + 2 * RANK, tokens), BF16),
-            pltpu.VMEM((n_s, 2 * RANK, tokens), BF16),
         ],
         after=[out_t[1]],
         carry=[out_t[2]],
     )
     partial, part, out_t[2] = backward[:n_s], backward[n_s], backward[n_s + 1]
     partial = exchange(partial, "space")
-    out_t[2] = late(2)
+    out_t[2:3] = hops(out_t[2:3], "tm", 2)
     rows = 8 * RANK // n_d
     *sums, out_t[3] = call(
         functools.partial(merge_kernel, frames, n_s, n_d),
         [shape((rows, d_s), F32)] * n_d,
         part, *sides, *partial,
-        scratch=[pltpu.VMEM((n_d, rows, d_s), F32), pltpu.VMEM((n_s, d_s, tokens), BF16)],
+        scratch=[pltpu.VMEM((n_d, rows, d_s), F32)],
         after=[out_t[2]],
         carry=[out_t[3]],
     )
-    out_t[3] = late(3)
+    out_t[3:] = hops(out_t[3:], "tm", 3)
     sums = call(total_kernel, shape((rows, d_s), BF16), *exchange(sums, "dp"))
     sums = call(total_kernel, shape((rows, d_s), BF16), *share(sums, "tm"), after=[out_t[3]])
     sums = call(

time: 149 us -> 108 us (0.72)
  Pallas kernels: 51.2 us -> 18.4 us
  waiting for transfers between devices: 46.1 us -> 34 us
  starting transfers between devices: 44.4 us -> 48.6 us
    pallas_call x16, Pallas kernels: 51.2 us -> 18.4 us  [call(): pl.pallas_call(body, out_shape=outs + tuple((shape(x.shape, x.dtype) for...]
    ppermute x26 -> x29, starting transfers between devices: 32.6 us -> 44.2 us  [hops(): lax.ppermute(array, axis, [(i, i ^ k) for i in range(size)])]
    all_to_all x1 -> x0, waiting for transfers between devices: 11.3 us -> none  [swap(): return lax.all_to_all(array, axes, split_axis=0, concat_axis=0, tiled=True)]
    all_to_all x1 -> x0, starting transfers between devices: 5.18 us -> none  [swap(): return lax.all_to_all(array, axes, split_axis=0, concat_axis=0, tiled=True)]
    ppermute x2, starting transfers between devices: 4.94 us -> 2.82 us  [exchange_steps(): got = lax.ppermute(sent, axis, [(i, i ^ step) for i in range(size)])]
    ppermute x26 -> x29, waiting for transfers between devices: 28 us -> 27.4 us  [hops(): lax.ppermute(array, axis, [(i, i ^ k) for i in range(size)])]
    unnamed x26 -> x34, local copies, waits for them, and re-layouts: 6.25 us -> 6.14 us
  transfers between devices with their start and end apart: 31 -> 33, of which waited for: 16 -> 20; matrix products, arithmetic and copies ran while one was open for 0% -> 0% of each run, Pallas kernels for 3% -> 4%
where the time goes in v6:
time: 108 us
  starting transfers between devices  48.6 us (45%)
  waiting for transfers between devices  34 us (31%)
  Pallas kernels  18.4 us (17%)
  local copies, waits for them, and re-layouts  6.31 us (6%)
    ppermute x29, starting transfers between devices, hops(): lax.ppermute(array, axis, [(i, i ^ k) for i in range(size)])  44.2 us
    ppermute x29, waiting for transfers between devices, hops(): lax.ppermute(array, axis, [(i, i ^ k) for i in range(size)])  27.4 us
    pallas_call x16, Pallas kernels, call(): pl.pallas_call(body, out_shape=outs + tuple((shape(x.shape, x.dtype) for...  18.4 us
    unnamed x34, local copies, waits for them, and re-layouts  6.14 us
    ppermute x2, waiting for transfers between devices, share_steps(): got = lax.ppermute(held, axis, [(i, i ^ step) for i in range(size)])  3.97 us
    ppermute x2, starting transfers between devices, exchange_steps(): got = lax.ppermute(sent, axis, [(i, i ^ step) for i in range(size)])  2.82 us
    ppermute x2, waiting for transfers between devices, exchange_steps(): got = lax.ppermute(sent, axis, [(i, i ^ step) for i in range(size)])  2.66 us
  transfers between devices with their start and end apart: 33, of which 20 were waited for; matrix products, arithmetic and copies ran while one was open for 0% of the time, Pallas kernels for 4%

profile of v6, /device:TPU:0, one launch (start us, length us, event | category | flops | bytes accessed | tf_op | source)
XLA Modules:
  0.0 108.2 jit_solution(2170268477623117585)
XLA Ops:
  0.7 4.0 %shard_map.121 = (bf16[864,128]{1,0:T(8,128)(2,1)}, bf16[864,128]{1,0:T(8,128)(2,1)}, bf16[864,128]{1,0:T(8,128)(2,1)}, bf16[864,128]{1,0:T(8,128)(2,1)}, bf16[6...) custom-call(bf16[1,2,64,1152]{3,2,1,0:T(8,128)(2,1)} %refs_0_.1, ...), custom_call_target="tpu_custom_call" | custom-call | tf_op jit(solution)/shard_map/pallas_call | solution.py:36
  4.7 4.1 %collective-permute-start.3 = (bf16[4,32,1152]{2,1,0:T(8,128)(2,1)}, bf16[4,32,1152]{2,1,0:T(8,128)(2,1)S(1)}, u32[]{:S(2)}, u32[]{:S(2)}) collective-permute-start(bf16[4,32,1152]{2,1,0:T(8,128)(2,1)} %get-tuple-element.52), channel_id=1, source_target_pairs={{0,8},{4,12},{8,0},{12,4},{1,9},{5,13},{9,1},{13,5},{2,10},{6,14},... | collective-permute-start | bytes 884744 | tf_op jit(solution)/shard_map/ppermute | solution.py:471
  8.8 1.5 %collective-permute-start = (bf16[864,128]{1,0:T(8,128)(2,1)}, bf16[864,128]{1,0:T(8,128)(2,1)S(1)}, u32[]{:S(2)}, u32[]{:S(2)}) collective-permute-start(bf16[864,128]{1,0:T(8,128)(2,1)} %get-tuple-element.49), channel_id=1, source_target_pairs={{0,1},{1,0},{2,3},{3,2},{4,5},{5,4},{6,7},{7,6},{8,9},{9,8},{10,11... | collective-permute-start | bytes 663560 | tf_op jit(solution)/shard_map/ppermute | solution.py:471
  10.3 1.5 %collective-permute-start.1 = (bf16[864,128]{1,0:T(8,128)(2,1)}, bf16[864,128]{1,0:T(8,128)(2,1)S(1)}, u32[]{:S(2)}, u32[]{:S(2)}) collective-permute-start(bf16[864,128]{1,0:T(8,128)(2,1)} %get-tuple-element.50), channel_id=1, source_target_pairs={{0,2},{1,3},{2,0},{3,1},{4,6},{5,7},{6,4},{7,5},{8,10},{9,11},{10,... | collective-permute-start | bytes 663560 | tf_op jit(solution)/shard_map/ppermute | solution.py:471
  12.3 1.6 %collective-permute-start.7 = (bf16[4,32,1152]{2,1,0:T(8,128)(2,1)}, bf16[4,32,1152]{2,1,0:T(8,128)(2,1)S(1)}, u32[]{:S(2)}, u32[]{:S(2)}) collective-permute-start(bf16[4,32,1152]{2,1,0:T(8,128)(2,1)} %get-tuple-element.60), channel_id=1, source_target_pairs={{0,4},{4,0},{8,12},{12,8},{1,5},{5,1},{9,13},{13,9},{2,6},{6,2},{1... | collective-permute-start | bytes 884744 | tf_op jit(solution)/shard_map/ppermute | solution.py:471
  13.9 3.5 %collective-permute-done.refs_1_ = bf16[864,128]{1,0:T(8,128)(2,1)S(1)} collective-permute-done((bf16[864,128]{1,0:T(8,128)(2,1)}, bf16[864,128]{1,0:T(8,128)(2,1)S(1)}, u32[]{:S(2)}, u32[]{:S(2)}) %collective-permute-start) | collective-permute-done | bytes 221216 | tf_op jit(solution)/shard_map/ppermute | solution.py:471
  18.7 3.1 %collective-permute-done.1.refs_2_ = bf16[864,128]{1,0:T(8,128)(2,1)S(1)} collective-permute-done((bf16[864,128]{1,0:T(8,128)(2,1)}, bf16[864,128]{1,0:T(8,128)(2,1)S(1)}, u32[]{:S(2)}, u32[]{:S(2)}) %collective-permute-start.1) | collective-permute-done | bytes 221216 | tf_op jit(solution)/shard_map/ppermute | solution.py:471
  21.8 2.2 %collective-permute-done.3.refs_4_.refs_2_ = bf16[4,32,1152]{2,1,0:T(8,128)(2,1)S(1)} collective-permute-done((bf16[4,32,1152]{2,1,0:T(8,128)(2,1)}, bf16[4,32,1152]{2,1,0:T(8,128)(2,1)S(1)}, u32[]{:S(2)}, u32[]{:S(2)}) %collective-permute-start.3) | collective-permute-done | bytes 294944 | tf_op jit(solution)/shard_map/ppermute | solution.py:471
  25.0 2.9 %shard_map.122 = (bf16[3,2,288,256]{3,2,1,0:T(8,128)(2,1)S(1)}, f32[2,4,256,256]{3,2,1,0:T(8,128)S(1)}, bf16[288,128]{1,0:T(8,128)(2,1)S(1)}, bf16[288,128]{1,0:...) custom-call(bf16[864,128]{1,0:T(8,128)(2,1)S(1)} %copy-done.7, ...), custom_call_target="tpu_custom_call" | custom-call | tf_op jit(solution)/shard_map/pallas_call | solution.py:36
  28.9 7.3 %collective-permute-start.4 = (bf16[288,128]{1,0:T(8,128)(2,1)S(1)}, bf16[288,128]{1,0:T(8,128)(2,1)S(1)}, u32[]{:S(2)}, u32[]{:S(2)}) collective-permute-start(bf16[288,128]{1,0:T(8,128)(2,1)S(1)} %get-tuple-element.54), channel_id=1, source_target_pairs={{0,1},{1,0},{2,3},{3,2},{4,5},{5,4},{6,7},{7,6},{8,9},{9,8},{10,11... | collective-permute-start | bytes 221192 | tf_op jit(solution)/shard_map/ppermute | solution.py:471
  36.2 1.5 %collective-permute-start.5 = (bf16[288,128]{1,0:T(8,128)(2,1)S(1)}, bf16[288,128]{1,0:T(8,128)(2,1)S(1)}, u32[]{:S(2)}, u32[]{:S(2)}) collective-permute-start(bf16[288,128]{1,0:T(8,128)(2,1)S(1)} %get-tuple-element.55), channel_id=1, source_target_pairs={{0,2},{1,3},{2,0},{3,1},{4,6},{5,7},{6,4},{7,5},{8,10},{9,11},{10,... | collective-permute-start | bytes 221192 | tf_op jit(solution)/shard_map/ppermute | solution.py:471
  37.7 1.6 %collective-permute-done.4.refs_1_ = bf16[288,128]{1,0:T(8,128)(2,1)S(1)} collective-permute-done((bf16[288,128]{1,0:T(8,128)(2,1)S(1)}, bf16[288,128]{1,0:T(8,128)(2,1)S(1)}, u32[]{:S(2)}, u32[]{:S(2)}) %collective-permute-start.4) | collective-permute-done | bytes 73760 | tf_op jit(solution)/shard_map/ppermute | solution.py:471
  40.5 2.4 %collective-permute-done.6.refs_3_ = bf16[288,128]{1,0:T(8,128)(2,1)S(1)} collective-permute-done((bf16[288,128]{1,0:T(8,128)(2,1)S(1)}, bf16[288,128]{1,0:T(8,128)(2,1)S(1)}, u32[]{:S(2)}, u32[]{:S(2)}) %collective-permute-start.6) | collective-permute-done | bytes 73760 | tf_op jit(solution)/shard_map/ppermute | solution.py:471
  45.4 3.5 %collective-permute-start.9 = (f32[8,128]{1,0:T(8,128)S(1)}, f32[8,128]{1,0:T(8,128)S(1)}, u32[]{:S(2)}, u32[]{:S(2)}) collective-permute-start(f32[8,128]{1,0:T(8,128)S(1)} %get-tuple-element.63), channel_id=1, source_target_pairs={{0,4},{4,0},{8,12},{12,8},{1,5},{5,1},{9,13},{13,9},{2,6},{6,2},{1... | collective-permute-start | bytes 12296 | tf_op jit(solution)/shard_map/ppermute | solution.py:471
  50.9 5.0 %shard_map.125 = (bf16[32,1152]{1,0:T(8,128)(2,1)S(1)}, bf16[32,1152]{1,0:T(8,128)(2,1)S(1)}, bf16[32,1152]{1,0:T(8,128)(2,1)S(1)}, bf16[32,1152]{1,0:T(8,128)(2...) custom-call(bf16[4,1152,128]{2,1,0:T(8,128)(2,1)S(1)} %shard_map.124, ...), custom_call_target="tpu_custom_call", output_to_operand_aliasing={{7}: (7, {})} | custom-call | tf_op jit(solution)/shard_map/pallas_call | solution.py:36
  56.5 1.7 %collective-permute-start.14 = (f32[2,8,128]{2,1,0:T(8,128)S(1)}, f32[2,8,128]{2,1,0:T(8,128)S(1)}, u32[]{:S(2)}, u32[]{:S(2)}) collective-permute-start(f32[2,8,128]{2,1,0:T(8,128)S(1)} %get-tuple-element.74), channel_id=1, source_target_pairs={{0,4},{4,0},{8,12},{12,8},{1,5},{5,1},{9,13},{13,9},{2,6},{6,2},{1... | collective-permute-start | bytes 24584 | tf_op jit(solution)/shard_map/ppermute | solution.py:444
  58.1 2.0 %collective-permute-done.14.refs_1_ = f32[2,8,128]{2,1,0:T(8,128)S(1)} collective-permute-done((f32[2,8,128]{2,1,0:T(8,128)S(1)}, f32[2,8,128]{2,1,0:T(8,128)S(1)}, u32[]{:S(2)}, u32[]{:S(2)}) %collective-permute-start.14) | collective-permute-done | bytes 8224 | tf_op jit(solution)/shard_map/ppermute | solution.py:444
  61.9 2.9 %collective-permute-start.19 = (bf16[608,128]{1,0:T(8,128)(2,1)S(1)}, bf16[608,128]{1,0:T(8,128)(2,1)S(1)}, u32[]{:S(2)}, u32[]{:S(2)}) collective-permute-start(bf16[608,128]{1,0:T(8,128)(2,1)S(1)} %get-tuple-element.79), channel_id=1, source_target_pairs={{0,3},{1,2},{2,1},{3,0},{4,7},{5,6},{6,5},{7,4},{8,11},{9,10},{10,... | collective-permute-start | bytes 466952 | tf_op jit(solution)/shard_map/ppermute | solution.py:471
  65.6 1.5 %collective-permute-start.16 = (bf16[1,32,128]{2,1,0:T(8,128)(2,1)S(1)}, bf16[1,32,128]{2,1,0:T(8,128)(2,1)S(1)}, u32[]{:S(2)}, u32[]{:S(2)}) collective-permute-start(bf16[1,32,128]{2,1,0:T(8,128)(2,1)S(1)} %bitcast.8), channel_id=1, source_target_pairs={{0,1},{1,0},{2,3},{3,2},{4,5},{5,4},{6,7},{7,6},{8,9},{9,8},{10,11... | collective-permute-start | bytes 24584 | tf_op jit(solution)/shard_map/ppermute | solution.py:462
  67.3 1.8 %collective-permute-start.13 = (bf16[32,1152]{1,0:T(8,128)(2,1)}, bf16[32,1152]{1,0:T(8,128)(2,1)S(1)}, u32[]{:S(2)}, u32[]{:S(2)}) collective-permute-start(bf16[32,1152]{1,0:T(8,128)(2,1)} %copy-done.16), channel_id=1, source_target_pairs={{0,4},{4,0},{8,12},{12,8},{1,5},{5,1},{9,13},{13,9},{2,6},{6,2},{1... | collective-permute-start | bytes 221192 | tf_op jit(solution)/shard_map/ppermute | solution.py:471
  69.6 3.6 %collective-permute-done.17.refs_1_ = bf16[2,32,128]{2,1,0:T(8,128)(2,1)S(1)} collective-permute-done((bf16[2,32,128]{2,1,0:T(8,128)(2,1)S(1)}, bf16[2,32,128]{2,1,0:T(8,128)(2,1)S(1)}, u32[]{:S(2)}, u32[]{:S(2)}) %collective-permute-start.17) | collective-permute-done | bytes 16416 | tf_op jit(solution)/shard_map/ppermute | solution.py:462
  75.3 2.8 %shard_map.130 = (bf16[32,1280]{1,0:T(8,128)(2,1)S(1)}, bf16[32,1280]{1,0:T(8,128)(2,1)S(1)}, bf16[32,1280]{1,0:T(8,128)(2,1)S(1)}, bf16[32,1280]{1,0:T(8,128)(2...) custom-call(bf16[3,2,288,256]{3,2,1,0:T(8,128)(2,1)S(1)} %copy-done.3, ...), custom_call_target="tpu_custom_call", output_to_operand_aliasing={{5}: (13, {})} | custom-call | tf_op jit(solution)/shard_map/pallas_call | solution.py:36
  78.1 1.5 %collective-permute-start.21 = (bf16[32,1280]{1,0:T(8,128)(2,1)S(1)}, bf16[32,1280]{1,0:T(8,128)(2,1)S(1)}, u32[]{:S(2)}, u32[]{:S(2)}) collective-permute-start(bf16[32,1280]{1,0:T(8,128)(2,1)S(1)} %get-tuple-element.84), channel_id=1, source_target_pairs={{0,1},{1,0},{2,3},{3,2},{4,5},{5,4},{6,7},{7,6},{8,9},{9,8},{10,11... | collective-permute-start | bytes 245768 | tf_op jit(solution)/shard_map/ppermute | solution.py:471
  80.1 1.6 %collective-permute-start.23 = (bf16[32,1280]{1,0:T(8,128)(2,1)S(1)}, bf16[32,1280]{1,0:T(8,128)(2,1)S(1)}, u32[]{:S(2)}, u32[]{:S(2)}) collective-permute-start(bf16[32,1280]{1,0:T(8,128)(2,1)S(1)} %get-tuple-element.86), channel_id=1, source_target_pairs={{0,3},{1,2},{2,1},{3,0},{4,7},{5,6},{6,5},{7,4},{8,11},{9,10},{10,... | collective-permute-start | bytes 245768 | tf_op jit(solution)/shard_map/ppermute | solution.py:471
  82.9 4.0 %collective-permute-done.20.refs_9_.refs_3_ = bf16[32,1152]{1,0:T(8,128)(2,1)S(1)} collective-permute-done((bf16[32,1152]{1,0:T(8,128)(2,1)S(1)}, bf16[32,1152]{1,0:T(8,128)(2,1)S(1)}, u32[]{:S(2)}, u32[]{:S(2)}) %collective-permute-start.20) | collective-permute-done | bytes 73760 | tf_op jit(solution)/shard_map/ppermute | solution.py:471
  87.3 3.1 %collective-permute-start.24 = (bf16[32,1152]{1,0:T(8,128)(2,1)S(1)}, bf16[32,1152]{1,0:T(8,128)(2,1)S(1)}, u32[]{:S(2)}, u32[]{:S(2)}) collective-permute-start(bf16[32,1152]{1,0:T(8,128)(2,1)S(1)} %get-tuple-element.88), channel_id=1, source_target_pairs={{0,12},{4,8},{8,4},{12,0},{1,13},{5,9},{9,5},{13,1},{2,14},{6,10},... | collective-permute-start | bytes 221192 | tf_op jit(solution)/shard_map/ppermute | solution.py:471
  90.5 1.8 %collective-permute-start.27 = (bf16[64,288]{1,0:T(8,128)(2,1)S(1)}, bf16[64,288]{1,0:T(8,128)(2,1)S(1)}, u32[]{:S(2)}, u32[]{:S(2)}) collective-permute-start(bf16[64,288]{1,0:T(8,128)(2,1)S(1)} %shard_map.133.refs_0_), channel_id=1, source_target_pairs={{0,8},{4,12},{8,0},{12,4},{1,9},{5,13},{9,1},{13,5},{2,10},{6,14},... | collective-permute-start | bytes 110600 | tf_op jit(solution)/shard_map/ppermute | solution.py:471
  92.2 2.6 %collective-permute-start.28 = (bf16[64,288]{1,0:T(8,128)(2,1)S(1)}, bf16[64,288]{1,0:T(8,128)(2,1)S(1)}, u32[]{:S(2)}, u32[]{:S(2)}) collective-permute-start(bf16[64,288]{1,0:T(8,128)(2,1)S(1)} %shard_map.133.refs_0_), channel_id=1, source_target_pairs={{0,12},{4,8},{8,4},{12,0},{1,13},{5,9},{9,5},{13,1},{2,14},{6,10},... | collective-permute-start | bytes 110600 | tf_op jit(solution)/shard_map/ppermute | solution.py:471
  95.7 1.9 %collective-permute-done.27.refs_2_ = bf16[64,288]{1,0:T(8,128)(2,1)S(1)} collective-permute-done((bf16[64,288]{1,0:T(8,128)(2,1)S(1)}, bf16[64,288]{1,0:T(8,128)(2,1)S(1)}, u32[]{:S(2)}, u32[]{:S(2)}) %collective-permute-start.27) | collective-permute-done | bytes 36896 | tf_op jit(solution)/shard_map/ppermute | solution.py:471
  98.2 2.0 %collective-permute-start.29 = (bf16[64,288]{1,0:T(8,128)(2,1)S(1)}, bf16[64,288]{1,0:T(8,128)(2,1)S(1)}, u32[]{:S(2)}, u32[]{:S(2)}) collective-permute-start(bf16[64,288]{1,0:T(8,128)(2,1)S(1)} %shard_map.134.refs_0_), channel_id=1, source_target_pairs={{0,1},{1,0},{2,3},{3,2},{4,5},{5,4},{6,7},{7,6},{8,9},{9,8},{10,11... | collective-permute-start | bytes 110600 | tf_op jit(solution)/shard_map/ppermute | solution.py:471
  102.4 2.0 %collective-permute-done.30.refs_2_ = bf16[64,288]{1,0:T(8,128)(2,1)S(1)} collective-permute-done((bf16[64,288]{1,0:T(8,128)(2,1)S(1)}, bf16[64,288]{1,0:T(8,128)(2,1)S(1)}, u32[]{:S(2)}, u32[]{:S(2)}) %collective-permute-start.30) | collective-permute-done | bytes 36896 | tf_op jit(solution)/shard_map/ppermute | solution.py:471
  104.3 1.4 %collective-permute-done.31.refs_3_ = bf16[64,288]{1,0:T(8,128)(2,1)S(1)} collective-permute-done((bf16[64,288]{1,0:T(8,128)(2,1)S(1)}, bf16[64,288]{1,0:T(8,128)(2,1)S(1)}, u32[]{:S(2)}, u32[]{:S(2)}) %collective-permute-start.31) | collective-permute-done | bytes 36896 | tf_op jit(solution)/shard_map/ppermute | solution.py:471
  (86 shorter events, 23.5 us)
Async XLA Ops:
  4.7 19.4 %collective-permute-start.3 = (bf16[4,32,1152]{2,1,0:T(8,128)(2,1)}, bf16[4,32,1152]{2,1,0:T(8,128)(2,1)S(1)}, u32[]{:S(2)}, u32[]{:S(2)}) collective-permute-start(bf16[4,32,1152]{2,1,0:T(8,128)(2,1)} %get-tuple-element.52), channel_id=1, source_target_pairs={{0,8},{4,12},{8,0},{12,4},{1,9},{5,13},{9,1},{13,5},{2,10},{6,14},... | collective-permute-start | bytes 884744 | tf_op jit(solution)/shard_map/ppermute | solution.py:471
  8.8 8.6 %collective-permute-start = (bf16[864,128]{1,0:T(8,128)(2,1)}, bf16[864,128]{1,0:T(8,128)(2,1)S(1)}, u32[]{:S(2)}, u32[]{:S(2)}) collective-permute-start(bf16[864,128]{1,0:T(8,128)(2,1)} %get-tuple-element.49), channel_id=1, source_target_pairs={{0,1},{1,0},{2,3},{3,2},{4,5},{5,4},{6,7},{7,6},{8,9},{9,8},{10,11... | collective-permute-start | bytes 663560 | tf_op jit(solution)/shard_map/ppermute | solution.py:471
  10.3 11.6 %collective-permute-start.1 = (bf16[864,128]{1,0:T(8,128)(2,1)}, bf16[864,128]{1,0:T(8,128)(2,1)S(1)}, u32[]{:S(2)}, u32[]{:S(2)}) collective-permute-start(bf16[864,128]{1,0:T(8,128)(2,1)} %get-tuple-element.50), channel_id=1, source_target_pairs={{0,2},{1,3},{2,0},{3,1},{4,6},{5,7},{6,4},{7,5},{8,10},{9,11},{10,... | collective-permute-start | bytes 663560 | tf_op jit(solution)/shard_map/ppermute | solution.py:471
  11.8 10.0 %collective-permute-start.2 = (bf16[864,128]{1,0:T(8,128)(2,1)}, bf16[864,128]{1,0:T(8,128)(2,1)S(1)}, u32[]{:S(2)}, u32[]{:S(2)}) collective-permute-start(bf16[864,128]{1,0:T(8,128)(2,1)} %get-tuple-element.51), channel_id=1, source_target_pairs={{0,3},{1,2},{2,1},{3,0},{4,7},{5,6},{6,5},{7,4},{8,11},{9,10},{10,... | collective-permute-start | bytes 663560 | tf_op jit(solution)/shard_map/ppermute | solution.py:471
  12.3 33.1 %collective-permute-start.7 = (bf16[4,32,1152]{2,1,0:T(8,128)(2,1)}, bf16[4,32,1152]{2,1,0:T(8,128)(2,1)S(1)}, u32[]{:S(2)}, u32[]{:S(2)}) collective-permute-start(bf16[4,32,1152]{2,1,0:T(8,128)(2,1)} %get-tuple-element.60), channel_id=1, source_target_pairs={{0,4},{4,0},{8,12},{12,8},{1,5},{5,1},{9,13},{13,9},{2,6},{6,2},{1... | collective-permute-start | bytes 884744 | tf_op jit(solution)/shard_map/ppermute | solution.py:471
  17.4 31.6 %collective-permute-start.8 = (bf16[4,32,1152]{2,1,0:T(8,128)(2,1)}, bf16[4,32,1152]{2,1,0:T(8,128)(2,1)S(1)}, u32[]{:S(2)}, u32[]{:S(2)}) collective-permute-start(bf16[4,32,1152]{2,1,0:T(8,128)(2,1)} %get-tuple-element.61), channel_id=1, source_target_pairs={{0,12},{4,8},{8,4},{12,0},{1,13},{5,9},{9,5},{13,1},{2,14},{6,10},... | collective-permute-start | bytes 884744 | tf_op jit(solution)/shard_map/ppermute | solution.py:471
  28.9 10.5 %collective-permute-start.4 = (bf16[288,128]{1,0:T(8,128)(2,1)S(1)}, bf16[288,128]{1,0:T(8,128)(2,1)S(1)}, u32[]{:S(2)}, u32[]{:S(2)}) collective-permute-start(bf16[288,128]{1,0:T(8,128)(2,1)S(1)} %get-tuple-element.54), channel_id=1, source_target_pairs={{0,1},{1,0},{2,3},{3,2},{4,5},{5,4},{6,7},{7,6},{8,9},{9,8},{10,11... | collective-permute-start | bytes 221192 | tf_op jit(solution)/shard_map/ppermute | solution.py:471
  36.2 4.4 %collective-permute-start.5 = (bf16[288,128]{1,0:T(8,128)(2,1)S(1)}, bf16[288,128]{1,0:T(8,128)(2,1)S(1)}, u32[]{:S(2)}, u32[]{:S(2)}) collective-permute-start(bf16[288,128]{1,0:T(8,128)(2,1)S(1)} %get-tuple-element.55), channel_id=1, source_target_pairs={{0,2},{1,3},{2,0},{3,1},{4,6},{5,7},{6,4},{7,5},{8,10},{9,11},{10,... | collective-permute-start | bytes 221192 | tf_op jit(solution)/shard_map/ppermute | solution.py:471
  37.7 5.3 %collective-permute-start.6 = (bf16[288,128]{1,0:T(8,128)(2,1)S(1)}, bf16[288,128]{1,0:T(8,128)(2,1)S(1)}, u32[]{:S(2)}, u32[]{:S(2)}) collective-permute-start(bf16[288,128]{1,0:T(8,128)(2,1)S(1)} %get-tuple-element.56), channel_id=1, source_target_pairs={{0,3},{1,2},{2,1},{3,0},{4,7},{5,6},{6,5},{7,4},{8,11},{9,10},{10,... | collective-permute-start | bytes 221192 | tf_op jit(solution)/shard_map/ppermute | solution.py:471
  44.9 5.9 %collective-permute-start.12 = (bf16[608,128]{1,0:T(8,128)(2,1)}, bf16[608,128]{1,0:T(8,128)(2,1)S(1)}, u32[]{:S(2)}, u32[]{:S(2)}) collective-permute-start(bf16[608,128]{1,0:T(8,128)(2,1)} %copy-done.9), channel_id=1, source_target_pairs={{0,1},{1,0},{2,3},{3,2},{4,5},{5,4},{6,7},{7,6},{8,9},{9,8},{10,11... | collective-permute-start | bytes 466952 | tf_op jit(solution)/shard_map/ppermute | solution.py:471
  45.4 4.5 %collective-permute-start.10 = (f32[8,128]{1,0:T(8,128)S(1)}, f32[8,128]{1,0:T(8,128)S(1)}, u32[]{:S(2)}, u32[]{:S(2)}) collective-permute-start(f32[8,128]{1,0:T(8,128)S(1)} %get-tuple-element.64), channel_id=1, source_target_pairs={{0,8},{4,12},{8,0},{12,4},{1,9},{5,13},{9,1},{13,5},{2,10},{6,14},... | collective-permute-start | bytes 12296 | tf_op jit(solution)/shard_map/ppermute | solution.py:471
  45.4 5.4 %collective-permute-start.11 = (f32[8,128]{1,0:T(8,128)S(1)}, f32[8,128]{1,0:T(8,128)S(1)}, u32[]{:S(2)}, u32[]{:S(2)}) collective-permute-start(f32[8,128]{1,0:T(8,128)S(1)} %get-tuple-element.65), channel_id=1, source_target_pairs={{0,12},{4,8},{8,4},{12,0},{1,13},{5,9},{9,5},{13,1},{2,14},{6,10},... | collective-permute-start | bytes 12296 | tf_op jit(solution)/shard_map/ppermute | solution.py:471
  45.4 5.4 %collective-permute-start.9 = (f32[8,128]{1,0:T(8,128)S(1)}, f32[8,128]{1,0:T(8,128)S(1)}, u32[]{:S(2)}, u32[]{:S(2)}) collective-permute-start(f32[8,128]{1,0:T(8,128)S(1)} %get-tuple-element.63), channel_id=1, source_target_pairs={{0,4},{4,0},{8,12},{12,8},{1,5},{5,1},{9,13},{13,9},{2,6},{6,2},{1... | collective-permute-start | bytes 12296 | tf_op jit(solution)/shard_map/ppermute | solution.py:471
  56.5 3.7 %collective-permute-start.14 = (f32[2,8,128]{2,1,0:T(8,128)S(1)}, f32[2,8,128]{2,1,0:T(8,128)S(1)}, u32[]{:S(2)}, u32[]{:S(2)}) collective-permute-start(f32[2,8,128]{2,1,0:T(8,128)S(1)} %get-tuple-element.74), channel_id=1, source_target_pairs={{0,4},{4,0},{8,12},{12,8},{1,5},{5,1},{9,13},{13,9},{2,6},{6,2},{1... | collective-permute-start | bytes 24584 | tf_op jit(solution)/shard_map/ppermute | solution.py:444
  60.7 4.8 %collective-permute-start.15 = (f32[2,8,128]{2,1,0:T(8,128)}, f32[2,8,128]{2,1,0:T(8,128)S(1)}, u32[]{:S(2)}, u32[]{:S(2)}) collective-permute-start(f32[2,8,128]{2,1,0:T(8,128)} %get-tuple-element.76), channel_id=1, source_target_pairs={{0,8},{4,12},{8,0},{12,4},{1,9},{5,13},{9,1},{13,5},{2,10},{6,14},... | collective-permute-start | bytes 24584 | tf_op jit(solution)/shard_map/ppermute | solution.py:444
  61.9 11.3 %collective-permute-start.18 = (bf16[608,128]{1,0:T(8,128)(2,1)S(1)}, bf16[608,128]{1,0:T(8,128)(2,1)S(1)}, u32[]{:S(2)}, u32[]{:S(2)}) collective-permute-start(bf16[608,128]{1,0:T(8,128)(2,1)S(1)} %get-tuple-element.78), channel_id=1, source_target_pairs={{0,2},{1,3},{2,0},{3,1},{4,6},{5,7},{6,4},{7,5},{8,10},{9,11},{10,... | collective-permute-start | bytes 466952 | tf_op jit(solution)/shard_map/ppermute | solution.py:471
  61.9 11.3 %collective-permute-start.19 = (bf16[608,128]{1,0:T(8,128)(2,1)S(1)}, bf16[608,128]{1,0:T(8,128)(2,1)S(1)}, u32[]{:S(2)}, u32[]{:S(2)}) collective-permute-start(bf16[608,128]{1,0:T(8,128)(2,1)S(1)} %get-tuple-element.79), channel_id=1, source_target_pairs={{0,3},{1,2},{2,1},{3,0},{4,7},{5,6},{6,5},{7,4},{8,11},{9,10},{10,... | collective-permute-start | bytes 466952 | tf_op jit(solution)/shard_map/ppermute | solution.py:471
  65.6 3.8 %collective-permute-start.16 = (bf16[1,32,128]{2,1,0:T(8,128)(2,1)S(1)}, bf16[1,32,128]{2,1,0:T(8,128)(2,1)S(1)}, u32[]{:S(2)}, u32[]{:S(2)}) collective-permute-start(bf16[1,32,128]{2,1,0:T(8,128)(2,1)S(1)} %bitcast.8), channel_id=1, source_target_pairs={{0,1},{1,0},{2,3},{3,2},{4,5},{5,4},{6,7},{7,6},{8,9},{9,8},{10,11... | collective-permute-start | bytes 24584 | tf_op jit(solution)/shard_map/ppermute | solution.py:462
  67.3 5.9 %collective-permute-start.13 = (bf16[32,1152]{1,0:T(8,128)(2,1)}, bf16[32,1152]{1,0:T(8,128)(2,1)S(1)}, u32[]{:S(2)}, u32[]{:S(2)}) collective-permute-start(bf16[32,1152]{1,0:T(8,128)(2,1)} %copy-done.16), channel_id=1, source_target_pairs={{0,4},{4,0},{8,12},{12,8},{1,5},{5,1},{9,13},{13,9},{2,6},{6,2},{1... | collective-permute-start | bytes 221192 | tf_op jit(solution)/shard_map/ppermute | solution.py:471
  69.4 3.7 %collective-permute-start.17 = (bf16[2,32,128]{2,1,0:T(8,128)(2,1)S(1)}, bf16[2,32,128]{2,1,0:T(8,128)(2,1)S(1)}, u32[]{:S(2)}, u32[]{:S(2)}) collective-permute-start(bf16[2,32,128]{2,1,0:T(8,128)(2,1)S(1)} %shard_map.128.refs_0_), channel_id=1, source_target_pairs={{0,2},{1,3},{2,0},{3,1},{4,6},{5,7},{6,4},{7,5},{8,10},{9,11},{10,... | collective-permute-start | bytes 49160 | tf_op jit(solution)/shard_map/ppermute | solution.py:462
  78.1 8.8 %collective-permute-start.21 = (bf16[32,1280]{1,0:T(8,128)(2,1)S(1)}, bf16[32,1280]{1,0:T(8,128)(2,1)S(1)}, u32[]{:S(2)}, u32[]{:S(2)}) collective-permute-start(bf16[32,1280]{1,0:T(8,128)(2,1)S(1)} %get-tuple-element.84), channel_id=1, source_target_pairs={{0,1},{1,0},{2,3},{3,2},{4,5},{5,4},{6,7},{7,6},{8,9},{9,8},{10,11... | collective-permute-start | bytes 245768 | tf_op jit(solution)/shard_map/ppermute | solution.py:471
  79.6 7.3 %collective-permute-start.22 = (bf16[32,1280]{1,0:T(8,128)(2,1)S(1)}, bf16[32,1280]{1,0:T(8,128)(2,1)S(1)}, u32[]{:S(2)}, u32[]{:S(2)}) collective-permute-start(bf16[32,1280]{1,0:T(8,128)(2,1)S(1)} %get-tuple-element.85), channel_id=1, source_target_pairs={{0,2},{1,3},{2,0},{3,1},{4,6},{5,7},{6,4},{7,5},{8,10},{9,11},{10,... | collective-permute-start | bytes 245768 | tf_op jit(solution)/shard_map/ppermute | solution.py:471
  80.1 6.8 %collective-permute-start.23 = (bf16[32,1280]{1,0:T(8,128)(2,1)S(1)}, bf16[32,1280]{1,0:T(8,128)(2,1)S(1)}, u32[]{:S(2)}, u32[]{:S(2)}) collective-permute-start(bf16[32,1280]{1,0:T(8,128)(2,1)S(1)} %get-tuple-element.86), channel_id=1, source_target_pairs={{0,3},{1,2},{2,1},{3,0},{4,7},{5,6},{6,5},{7,4},{8,11},{9,10},{10,... | collective-permute-start | bytes 245768 | tf_op jit(solution)/shard_map/ppermute | solution.py:471
  81.6 5.3 %collective-permute-start.20 = (bf16[32,1152]{1,0:T(8,128)(2,1)S(1)}, bf16[32,1152]{1,0:T(8,128)(2,1)S(1)}, u32[]{:S(2)}, u32[]{:S(2)}) collective-permute-start(bf16[32,1152]{1,0:T(8,128)(2,1)S(1)} %get-tuple-element.81), channel_id=1, source_target_pairs={{0,8},{4,12},{8,0},{12,4},{1,9},{5,13},{9,1},{13,5},{2,10},{6,14},... | collective-permute-start | bytes 221192 | tf_op jit(solution)/shard_map/ppermute | solution.py:471
  87.2 3.2 %collective-permute-start.25 = (f32[64,288]{1,0:T(8,128)S(1)}, f32[64,288]{1,0:T(8,128)S(1)}, u32[]{:S(2)}, u32[]{:S(2)}) collective-permute-start(f32[64,288]{1,0:T(8,128)S(1)} %get-tuple-element.90), channel_id=1, source_target_pairs={{0,16},{16,0},{1,17},{17,1},{2,18},{18,2},{3,19},{19,3},{4,20},{20... | collective-permute-start | bytes 221192 | tf_op jit(solution)/shard_map/ppermute | solution.py:471
  87.3 7.6 %collective-permute-start.24 = (bf16[32,1152]{1,0:T(8,128)(2,1)S(1)}, bf16[32,1152]{1,0:T(8,128)(2,1)S(1)}, u32[]{:S(2)}, u32[]{:S(2)}) collective-permute-start(bf16[32,1152]{1,0:T(8,128)(2,1)S(1)} %get-tuple-element.88), channel_id=1, source_target_pairs={{0,12},{4,8},{8,4},{12,0},{1,13},{5,9},{9,5},{13,1},{2,14},{6,10},... | collective-permute-start | bytes 221192 | tf_op jit(solution)/shard_map/ppermute | solution.py:471
  90.4 5.3 %collective-permute-start.26 = (bf16[64,288]{1,0:T(8,128)(2,1)S(1)}, bf16[64,288]{1,0:T(8,128)(2,1)S(1)}, u32[]{:S(2)}, u32[]{:S(2)}) collective-permute-start(bf16[64,288]{1,0:T(8,128)(2,1)S(1)} %shard_map.133.refs_0_), channel_id=1, source_target_pairs={{0,4},{4,0},{8,12},{12,8},{1,5},{5,1},{9,13},{13,9},{2,6},{6,2},{1... | collective-permute-start | bytes 110600 | tf_op jit(solution)/shard_map/ppermute | solution.py:471
  90.5 7.1 %collective-permute-start.27 = (bf16[64,288]{1,0:T(8,128)(2,1)S(1)}, bf16[64,288]{1,0:T(8,128)(2,1)S(1)}, u32[]{:S(2)}, u32[]{:S(2)}) collective-permute-start(bf16[64,288]{1,0:T(8,128)(2,1)S(1)} %shard_map.133.refs_0_), channel_id=1, source_target_pairs={{0,8},{4,12},{8,0},{12,4},{1,9},{5,13},{9,1},{13,5},{2,10},{6,14},... | collective-permute-start | bytes 110600 | tf_op jit(solution)/shard_map/ppermute | solution.py:471
  92.2 5.9 %collective-permute-start.28 = (bf16[64,288]{1,0:T(8,128)(2,1)S(1)}, bf16[64,288]{1,0:T(8,128)(2,1)S(1)}, u32[]{:S(2)}, u32[]{:S(2)}) collective-permute-start(bf16[64,288]{1,0:T(8,128)(2,1)S(1)} %shard_map.133.refs_0_), channel_id=1, source_target_pairs={{0,12},{4,8},{8,4},{12,0},{1,13},{5,9},{9,5},{13,1},{2,14},{6,10},... | collective-permute-start | bytes 110600 | tf_op jit(solution)/shard_map/ppermute | solution.py:471
  98.2 4.2 %collective-permute-start.29 = (bf16[64,288]{1,0:T(8,128)(2,1)S(1)}, bf16[64,288]{1,0:T(8,128)(2,1)S(1)}, u32[]{:S(2)}, u32[]{:S(2)}) collective-permute-start(bf16[64,288]{1,0:T(8,128)(2,1)S(1)} %shard_map.134.refs_0_), channel_id=1, source_target_pairs={{0,1},{1,0},{2,3},{3,2},{4,5},{5,4},{6,7},{7,6},{8,9},{9,8},{10,11... | collective-permute-start | bytes 110600 | tf_op jit(solution)/shard_map/ppermute | solution.py:471
  100.2 4.1 %collective-permute-start.30 = (bf16[64,288]{1,0:T(8,128)(2,1)S(1)}, bf16[64,288]{1,0:T(8,128)(2,1)S(1)}, u32[]{:S(2)}, u32[]{:S(2)}) collective-permute-start(bf16[64,288]{1,0:T(8,128)(2,1)S(1)} %shard_map.134.refs_0_), channel_id=1, source_target_pairs={{0,2},{1,3},{2,0},{3,1},{4,6},{5,7},{6,4},{7,5},{8,10},{9,11},{10,... | collective-permute-start | bytes 110600 | tf_op jit(solution)/shard_map/ppermute | solution.py:471
  100.7 5.0 %collective-permute-start.31 = (bf16[64,288]{1,0:T(8,128)(2,1)S(1)}, bf16[64,288]{1,0:T(8,128)(2,1)S(1)}, u32[]{:S(2)}, u32[]{:S(2)}) collective-permute-start(bf16[64,288]{1,0:T(8,128)(2,1)S(1)} %shard_map.134.refs_0_), channel_id=1, source_target_pairs={{0,3},{1,2},{2,1},{3,0},{4,7},{5,6},{6,5},{7,4},{8,11},{9,10},{10,... | collective-permute-start | bytes 110600 | tf_op jit(solution)/shard_map/ppermute | solution.py:471
  (18 other events, 247.9 us)

commit v7 on v3

--- a/solution.py
+++ b/solution.py
@@ -41,7 +41,7 @@
         scratch_shapes=list(scratch),
         input_output_aliases={used + len(after) + i: len(outs) + i for i in range(len(carry))},
         compiler_params=pltpu.CompilerParams(vmem_limit_bytes=limit * 1024 * 1024),
-    )(*args, *after, *carry)
+    )(*(pltpu.with_memory_space_constraint(x, pltpu.HBM) if hbm else x for x in args), *after, *carry)
     return result[0] if single and not carry else list(result)
 
 
@@ -55,16 +55,10 @@
         scores = jnp.where(mask, scores, -1e30)
     peak = jnp.max(scores, axis=0, keepdims=True)
     weights = jnp.exp(scores - peak)
-    return weights / jnp.sum(weights, axis=0, keepdims=True)
-
-
-def head_forward(q_t, k_t, v_t, mask=None):
-    probs = probs_of(k_t.T, q_t, mask)
-    return mm(v_t, probs.astype(BF16))
-
-
-def head_backward(q_t, k_t, v_t, g_t, mask=None, forward=False):
-    probs = probs_of(k_t.T, q_t, mask)
+    return weights * (1.0 / jnp.sum(weights, axis=0, keepdims=True))
+
+
+def head_backward(probs, k_t, v_t, g_t, forward=False):
     low = probs.astype(BF16)
     dvals = mm(g_t, low, NT)
     dprob = mm(v_t.T, g_t)
@@ -156,7 +150,7 @@
 
 
 def space_forward_kernel(frames, n_s, *refs):
-    packed, qkv_ref, outs = refs[:n_s], refs[n_s], refs[n_s + 1 :]
+    packed, (qkv_ref, probs_ref, *outs) = refs[:n_s], refs[n_s:]
     d_s, tokens = outs[0].shape
     patch_dev = tokens // frames
     total = n_s * patch_dev
@@ -174,9 +168,11 @@
             k_h = rows_of(keys, h).astype(BF16)
             v_h = rows_of(vals, h).astype(BF16)
             q_h = rows_of(query, h).astype(BF16)
-            parts = [
-                head_forward(q_h[:, s : s + step], k_h, v_h) for s in range(0, total, step)
-            ]
+            parts = []
+            for s in range(0, total, step):
+                probs = probs_of(k_h.T, q_h[:, s : s + step], None)
+                probs_ref[f, h, :, s : s + step] = probs
+                parts.append(mm(v_h, probs.astype(BF16)))
             heads.append(parts[0] if len(parts) == 1 else jnp.concatenate(parts, axis=1))
         out = jnp.concatenate(heads, axis=0).astype(BF16)
         for k in range(n_s):
@@ -250,14 +246,10 @@
     mask = lax.rem(row, sub) == lax.rem(col, sub)
     outs_h, d_query, d_vals = [], [], []
     for h in range(width // HEAD_DIM):
-        dq, dv, out = head_backward(
-            rows_of(query, h).astype(BF16),
-            rows_of(keys, h).astype(BF16),
-            rows_of(vals, h).astype(BF16),
-            rows_of(grad, h).astype(BF16),
-            mask,
-            True,
-        )
+        k_h = rows_of(keys, h).astype(BF16)
+        v_h = rows_of(vals, h).astype(BF16)
+        probs = probs_of(k_h.T, rows_of(query, h).astype(BF16), mask)
+        dq, dv, out = head_backward(probs, k_h, v_h, rows_of(grad, h).astype(BF16), True)
         outs_h.append(out)
         d_query.append(dq)
         d_vals.append(dv)
@@ -286,7 +278,7 @@
     out_ref[...] = buf[...].T[: 2 * RANK].astype(BF16)
 
 
-def space_backward_kernel(frames, n_s, qkv_ref, hidden_ref, grad_b_ref, at_ref, at_here_ref, b_here_ref, *refs):
+def space_backward_kernel(frames, n_s, qkv_ref, probs_ref, hidden_ref, grad_b_ref, at_ref, at_here_ref, b_here_ref, *refs):
     packed, dcodes, sends = refs[:n_s], refs[n_s : 2 * n_s], refs[2 * n_s : 3 * n_s]
     part_ref, cut_buf = refs[3 * n_s :]
     d_s = part_ref.shape[1]
@@ -302,7 +294,6 @@
     grad_b_q = grad_b_v = None
     codes = [x[5 * d_s :] for x in packed]
     for f in range(frames):
-        query = qkv_ref[0, f].astype(F32)
         keys = qkv_ref[1, f].astype(F32)
         vals = qkv_ref[2, f].astype(F32)
         grad = frame_rows(grads, f, patch_dev).astype(F32)
@@ -310,11 +301,11 @@
         for h in range(d_s // HEAD_DIM):
             k_h = rows_of(keys, h).astype(BF16)
             v_h = rows_of(vals, h).astype(BF16)
-            q_h = rows_of(query, h).astype(BF16)
             g_h = rows_of(grad, h).astype(BF16)
             dq_parts, dv_sum = [], None
             for s in range(0, total, step):
-                dq, dv, _ = head_backward(q_h[:, s : s + step], k_h, v_h, g_h[:, s : s + step])
+                probs = probs_ref[f, h, :, s : s + step]
+                dq, dv, _ = head_backward(probs, k_h, v_h, g_h[:, s : s + step])
                 dq_parts.append(dq)
                 dv_sum = dv if dv_sum is None else dv_sum + dv
             d_query.append(
@@ -379,7 +370,10 @@
 
 
 def total_kernel(*refs):
-    refs[-1][...] = add_up([ref[...].astype(F32) for ref in refs[:-1]]).astype(refs[-1].dtype)
+    terms = [ref[...].astype(F32) for ref in refs[:-1]]
+    while len(terms) > 1:
+        terms = [terms[i] + terms[i + 1] for i in range(0, len(terms), 2)]
+    refs[-1][...] = terms[0].astype(refs[-1].dtype)
 
 
 def join_kernel(*refs):
@@ -418,11 +412,16 @@
     mixed_ref[0] = total.astype(BF16).reshape(frames, patch_dev, width)
 
 
+def hops(arrays, axis, first):
+    size = lax.axis_size(axis)
+    return [
+        lax.ppermute(array, axis, [(i, i ^ k) for i in range(size)])
+        for k, array in enumerate(arrays, first)
+    ]
+
+
 def exchange(pieces, axis):
-    size = lax.axis_size(axis)
-    return [pieces[0]] + [
-        lax.ppermute(pieces[k], axis, [(i, i ^ k) for i in range(size)]) for k in range(1, size)
-    ]
+    return [pieces[0]] + hops(pieces[1:], axis, 1)
 
 
 def share(array, axis):
@@ -451,7 +450,7 @@
         [shape((4, frames * sub, width), BF16)] * n_t,
         query_t, key_t, value_t, cotangent,
         scratch=[dma((4 * frames * n_t,))],
-        hbm=True, limit=54,
+        hbm=True, limit=48,
     )
     time_pieces = exchange(time_pieces, "tm")
     packed = call(
@@ -463,13 +462,15 @@
             for x in (patches, downs, adapters_b, query_s, value_s, key_s, cotangent)
         ]
         + [pltpu.VMEM((5, n_s, d_s, tokens), BF16), dma((7,))],
-        hbm=True, limit=54,
+        hbm=True, limit=48,
     )
     packed = exchange(packed, "space")
-    qkv, *out_s = call(
+    qkv, probs, *out_s = call(
         functools.partial(space_forward_kernel, frames, n_s),
-        [shape((3, frames, d_s, total), BF16)] + [shape((d_s, tokens), BF16)] * n_s,
+        [shape((3, frames, d_s, total), BF16), shape((frames, d_s // HEAD_DIM, total, total), F32)]
+        + [shape((d_s, tokens), BF16)] * n_s,
         *packed,
+        after=[time_pieces[1]],
     )
     out_s = exchange(out_s, "space")
     hidden, *codes = call(
@@ -489,6 +490,7 @@
     )
     out_t, dcodes, time_grad_b = timed[:n_t], timed[n_t : 2 * n_t], timed[2 * n_t]
     dcodes = exchange(dcodes, "tm")
+    out_t[1:2] = hops(out_t[1:2], "tm", 1)
     dcodes = call(
         functools.partial(place_codes_kernel, frames, sub),
         shape((2 * RANK, tokens), BF16),
@@ -499,13 +501,14 @@
     backward = call(
         functools.partial(space_backward_kernel, frames, n_s),
         [shape((2 * RANK, frames * total + 2 * pad), BF16)] * n_s + [shape((2 * RANK, d_s), F32)],
-        qkv, hidden, time_grad_b, downs, downs_here, ups_here, *packed, *dcodes,
+        qkv, probs, hidden, time_grad_b, downs, downs_here, ups_here, *packed, *dcodes,
         scratch=[pltpu.VMEM((n_s, 2, 2 * RANK, pad), BF16)],
-        carry=out_t,
-    )
-    partial, part, out_t = backward[:n_s], backward[n_s], backward[n_s + 1 :]
+        after=out_t[1:2],
+        carry=out_t[2:],
+    )
+    partial, part = backward[:n_s], backward[n_s]
     partial = exchange(partial, "space")
-    out_t = exchange(out_t, "tm")
+    out_t[2:] = hops(backward[n_s + 1 :], "tm", 2)
     rows = 8 * RANK // n_d
     sums = call(
         functools.partial(merge_kernel, frames, n_s, n_d),
@@ -513,12 +516,8 @@
         part, *packed, *partial,
         scratch=[pltpu.VMEM((n_d, rows, d_s), F32)],
     )
-    sums = call(total_kernel, shape((rows, d_s), BF16), *exchange(sums, "dp"), after=out_t[1:])
-    step = 1
-    while step < n_t:
-        other = lax.ppermute(sums, "tm", [(i, i ^ step) for i in range(n_t)])
-        sums = call(total_kernel, shape((rows, d_s), BF16), sums, other)
-        step *= 2
+    sums = call(total_kernel, shape((rows, d_s), BF16), *exchange(sums, "dp"), after=out_t[2:])
+    sums = call(total_kernel, shape((rows, d_s), BF16), *share(sums, "tm"))
     sums = call(
         join_kernel,
         shape((rows, width), BF16),

time: 104 us -> 97.4 us (0.937)
  waiting for transfers between devices: 37.6 us -> 32.5 us
  Pallas kernels: 23.5 us -> 19.8 us
  local copies, waits for them, and re-layouts: 0.2 us -> 2.64 us
    ppermute x31 -> x32, waiting for transfers between devices: 37.6 us -> 32.5 us  [hops(): lax.ppermute(array, axis, [(i, i ^ k) for i in range(size)])]
    pallas_call x15 -> x14, Pallas kernels: 23.5 us -> 19.8 us  [call(): pl.pallas_call(body, out_shape=outs + tuple((shape(x.shape, x.dtype) for...]
    unnamed x10 -> x14, local copies, waits for them, and re-layouts: 0.02 us -> 2.47 us
    ppermute x31 -> x32, starting transfers between devices: 41.5 us -> 41.4 us  [hops(): lax.ppermute(array, axis, [(i, i ^ k) for i in range(size)])]
  transfers between devices with their start and end apart: 31 -> 32, of which waited for: 19 -> 18; matrix products, arithmetic and copies ran while one was open for 0% -> 0% of each run, Pallas kernels for 8% -> 9%
where the time goes in v7:
time: 97.4 us; the launch traced here: 97.2 us
  starting transfers between devices  41.4 us (43%)
  waiting for transfers between devices  32.5 us (33%)
  Pallas kernels  19.8 us (20%)
  local copies, waits for them, and re-layouts  2.64 us (3%)
    ppermute x32, starting transfers between devices, hops(): lax.ppermute(array, axis, [(i, i ^ k) for i in range(size)])  41.4 us
    ppermute x32, waiting for transfers between devices, hops(): lax.ppermute(array, axis, [(i, i ^ k) for i in range(size)])  32.5 us
    pallas_call x14, Pallas kernels, call(): pl.pallas_call(body, out_shape=outs + tuple((shape(x.shape, x.dtype) for...  19.8 us
    unnamed x14, local copies, waits for them, and re-layouts  2.47 us
  transfers between devices with their start and end apart: 32, of which 18 were waited for; matrix products, arithmetic and copies ran while one was open for 0% of the time, Pallas kernels for 9%

profile of v7, /device:TPU:0, one launch (start us, length us, event | category | flops | bytes accessed | tf_op | source)
XLA Modules:
  0.0 97.2 jit_solution(1065313752833489951)
XLA Ops:
  0.7 2.4 %shard_map.122 = (bf16[4,32,1152]{2,1,0:T(8,128)(2,1)S(1)}, bf16[4,32,1152]{2,1,0:T(8,128)(2,1)S(1)}, bf16[4,32,1152]{2,1,0:T(8,128)(2,1)}, bf16[4,32,1152]{2,1,0:T(8,128)(2,1)}) custom-call(bf16[1,2,64,1152]{3,2,1,0:T(8,128)(2,1)} %refs_0_.3, bf16[1,2,64,1152]{3,2,1,0:T(8,128)(2,1)} %refs_1_.2, bf16[1,2,64,1152]{3,2,1,0:T(8,128)(2,1)} %refs_2_.3, ...), custom_call_target="tpu_custom_call" | custom-call | tf_op jit(solution)/shard_map/pallas_call | solution.py:36
  3.1 3.1 %collective-permute-start.3 = (bf16[4,32,1152]{2,1,0:T(8,128)(2,1)S(1)}, bf16[4,32,1152]{2,1,0:T(8,128)(2,1)S(1)}, u32[]{:S(2)}, u32[]{:S(2)}) collective-permute-start(bf16[4,32,1152]{2,1,0:T(8,128)(2,1)S(1)} %get-tuple-element.46), channel_id=1, source_target_pairs={{0,4},{4,0},{8,12},{12,8},{1,5},{5,1},{9,13},{13,9},{2,6},{6,2},{1... | collective-permute-start | bytes 884744 | tf_op jit(solution)/shard_map/ppermute | solution.py:418
  6.2 2.6 %shard_map.121 = (bf16[1472,128]{1,0:T(8,128)(2,1)S(1)}, bf16[1472,128]{1,0:T(8,128)(2,1)S(1)}, bf16[1472,128]{1,0:T(8,128)(2,1)S(1)}, bf16[1472,128]{1,0:T(8,128)(2,1)S(1)}) custom-call(bf16[1,2,64,1152]{3,2,1,0:T(8,128)(2,1)} %refs_4_.3, bf16[4,16,1152]{2,1,0:T(8,128)(2,1)} %bitcast.4, bf16[4,16,1152]{2,1,0:T(8,128)(2,1)} %refs_1_.3, ...), custom_call_target="tpu_custom_call" | custom-call | tf_op jit(solution)/shard_map/pallas_call | solution.py:36
  8.8 1.6 %collective-permute-start = (bf16[1472,128]{1,0:T(8,128)(2,1)S(1)}, bf16[1472,128]{1,0:T(8,128)(2,1)S(1)}, u32[]{:S(2)}, u32[]{:S(2)}) collective-permute-start(bf16[1472,128]{1,0:T(8,128)(2,1)S(1)} %get-tuple-element.43), channel_id=1, source_target_pairs={{0,1},{1,0},{2,3},{3,2},{4,5},{5,4},{6,7},{7,6},{8,9},{9,8},{10,11... | collective-permute-start | bytes 1130504 | tf_op jit(solution)/shard_map/ppermute | solution.py:418
  10.4 1.6 %collective-permute-start.1 = (bf16[1472,128]{1,0:T(8,128)(2,1)S(1)}, bf16[1472,128]{1,0:T(8,128)(2,1)S(1)}, u32[]{:S(2)}, u32[]{:S(2)}) collective-permute-start(bf16[1472,128]{1,0:T(8,128)(2,1)S(1)} %get-tuple-element.44), channel_id=1, source_target_pairs={{0,2},{1,3},{2,0},{3,1},{4,6},{5,7},{6,4},{7,5},{8,10},{9,11},{10,... | collective-permute-start | bytes 1130504 | tf_op jit(solution)/shard_map/ppermute | solution.py:418
  12.4 2.6 %collective-permute-start.7 = (bf16[4,32,1152]{2,1,0:T(8,128)(2,1)}, bf16[4,32,1152]{2,1,0:T(8,128)(2,1)}, u32[]{:S(2)}, u32[]{:S(2)}) collective-permute-start(bf16[4,32,1152]{2,1,0:T(8,128)(2,1)} %get-tuple-element.53), channel_id=1, source_target_pairs={{0,8},{4,12},{8,0},{12,4},{1,9},{5,13},{9,1},{13,5},{2,10},{6,14},... | collective-permute-start | bytes 884744 | tf_op jit(solution)/shard_map/ppermute | solution.py:418
  15.0 2.0 %collective-permute-start.8 = (bf16[4,32,1152]{2,1,0:T(8,128)(2,1)}, bf16[4,32,1152]{2,1,0:T(8,128)(2,1)}, u32[]{:S(2)}, u32[]{:S(2)}) collective-permute-start(bf16[4,32,1152]{2,1,0:T(8,128)(2,1)} %get-tuple-element.54), channel_id=1, source_target_pairs={{0,12},{4,8},{8,4},{12,0},{1,13},{5,9},{9,5},{13,1},{2,14},{6,10},... | collective-permute-start | bytes 884744 | tf_op jit(solution)/shard_map/ppermute | solution.py:418
  16.9 3.6 %collective-permute-done.refs_1_.refs_8_.refs_2_ = bf16[1472,128]{1,0:T(8,128)(2,1)S(1)} collective-permute-done((bf16[1472,128]{1,0:T(8,128)(2,1)S(1)}, bf16[1472,128]{1,0:T(8,128)(2,1)S(1)}, u32[]{:S(2)}, u32[]{:S(2)}) %collective-permute-start) | collective-permute-done | bytes 376864 | tf_op jit(solution)/shard_map/ppermute | solution.py:418
  20.6 7.8 %collective-permute-done.1.refs_2_.refs_9_.refs_3_ = bf16[1472,128]{1,0:T(8,128)(2,1)S(1)} collective-permute-done((bf16[1472,128]{1,0:T(8,128)(2,1)S(1)}, bf16[1472,128]{1,0:T(8,128)(2,1)S(1)}, u32[]{:S(2)}, u32[]{:S(2)}) %collective-permute-start.1) | collective-permute-done | bytes 376864 | tf_op jit(solution)/shard_map/ppermute | solution.py:418
  28.4 2.9 %shard_map.123 = (bf16[3,2,288,256]{3,2,1,0:T(8,128)(2,1)S(1)}, f32[2,4,256,256]{3,2,1,0:T(8,128)S(1)}, bf16[288,128]{1,0:T(8,128)(2,1)S(1)}, bf16[288,128]{1,0:...) custom-call(bf16[1472,128]{1,0:T(8,128)(2,1)S(1)} %get-tuple-element.42.refs_0_.refs_7_.refs_1_, ...), custom_call_target="tpu_custom_call" | custom-call | tf_op jit(solution)/shard_map/pallas_call | solution.py:36
  36.1 1.6 %collective-permute-done.4.refs_1_ = bf16[288,128]{1,0:T(8,128)(2,1)S(1)} collective-permute-done((bf16[288,128]{1,0:T(8,128)(2,1)S(1)}, bf16[288,128]{1,0:T(8,128)(2,1)S(1)}, u32[]{:S(2)}, u32[]{:S(2)}) %collective-permute-start.4) | collective-permute-done | bytes 73760 | tf_op jit(solution)/shard_map/ppermute | solution.py:418
  38.3 1.7 %collective-permute-done.6.refs_3_ = bf16[288,128]{1,0:T(8,128)(2,1)S(1)} collective-permute-done((bf16[288,128]{1,0:T(8,128)(2,1)S(1)}, bf16[288,128]{1,0:T(8,128)(2,1)S(1)}, u32[]{:S(2)}, u32[]{:S(2)}) %collective-permute-start.6) | collective-permute-done | bytes 73760 | tf_op jit(solution)/shard_map/ppermute | solution.py:418
  40.8 2.6 %collective-permute-start.10 = (f32[8,128]{1,0:T(8,128)S(1)}, f32[8,128]{1,0:T(8,128)S(1)}, u32[]{:S(2)}, u32[]{:S(2)}) collective-permute-start(f32[8,128]{1,0:T(8,128)S(1)} %get-tuple-element.57), channel_id=1, source_target_pairs={{0,8},{4,12},{8,0},{12,4},{1,9},{5,13},{9,1},{13,5},{2,10},{6,14},... | collective-permute-start | bytes 12296 | tf_op jit(solution)/shard_map/ppermute | solution.py:418
  47.3 1.5 %collective-permute-done.11.refs_5_ = f32[8,128]{1,0:T(8,128)S(1)} collective-permute-done((f32[8,128]{1,0:T(8,128)S(1)}, f32[8,128]{1,0:T(8,128)S(1)}, u32[]{:S(2)}, u32[]{:S(2)}) %collective-permute-start.11) | collective-permute-done | bytes 4128 | tf_op jit(solution)/shard_map/ppermute | solution.py:418
  48.8 4.9 %shard_map.126 = (bf16[32,1152]{1,0:T(8,128)(2,1)S(1)}, bf16[32,1152]{1,0:T(8,128)(2,1)S(1)}, bf16[32,1152]{1,0:T(8,128)(2,1)S(1)}, bf16[32,1152]{1,0:T(8,128)(2...) custom-call(bf16[4,1152,128]{2,1,0:T(8,128)(2,1)S(1)} %shard_map.125, ...), custom_call_target="tpu_custom_call" | custom-call | tf_op jit(solution)/shard_map/pallas_call | solution.py:36
  53.8 1.9 %collective-permute-start.14 = (f32[8,128]{1,0:T(8,128)S(1)}, f32[8,128]{1,0:T(8,128)S(1)}, u32[]{:S(2)}, u32[]{:S(2)}) collective-permute-start(f32[8,128]{1,0:T(8,128)S(1)} %get-tuple-element.66), channel_id=1, source_target_pairs={{0,8},{4,12},{8,0},{12,4},{1,9},{5,13},{9,1},{13,5},{2,10},{6,14},... | collective-permute-start | bytes 12296 | tf_op jit(solution)/shard_map/ppermute | solution.py:418
  55.7 2.5 %collective-permute-start.15 = (f32[8,128]{1,0:T(8,128)S(1)}, f32[8,128]{1,0:T(8,128)S(1)}, u32[]{:S(2)}, u32[]{:S(2)}) collective-permute-start(f32[8,128]{1,0:T(8,128)S(1)} %get-tuple-element.67), channel_id=1, source_target_pairs={{0,12},{4,8},{8,4},{12,0},{1,13},{5,9},{9,5},{13,1},{2,14},{6,10},... | collective-permute-start | bytes 12296 | tf_op jit(solution)/shard_map/ppermute | solution.py:418
  58.4 2.7 %collective-permute-done.15.refs_3_ = f32[8,128]{1,0:T(8,128)S(1)} collective-permute-done((f32[8,128]{1,0:T(8,128)S(1)}, f32[8,128]{1,0:T(8,128)S(1)}, u32[]{:S(2)}, u32[]{:S(2)}) %collective-permute-start.15) | collective-permute-done | bytes 4128 | tf_op jit(solution)/shard_map/ppermute | solution.py:418
  61.2 1.5 %collective-permute-start.18 = (bf16[32,128]{1,0:T(8,128)(2,1)S(1)}, bf16[32,128]{1,0:T(8,128)(2,1)S(1)}, u32[]{:S(2)}, u32[]{:S(2)}) collective-permute-start(bf16[32,128]{1,0:T(8,128)(2,1)S(1)} %shard_map.127.refs_11_), channel_id=1, source_target_pairs={{0,3},{1,2},{2,1},{3,0},{4,7},{5,6},{6,5},{7,4},{8,11},{9,10},{10,... | collective-permute-start | bytes 24584 | tf_op jit(solution)/shard_map/ppermute | solution.py:418
  62.7 1.6 %collective-permute-start.17 = (bf16[32,128]{1,0:T(8,128)(2,1)S(1)}, bf16[32,128]{1,0:T(8,128)(2,1)S(1)}, u32[]{:S(2)}, u32[]{:S(2)}) collective-permute-start(bf16[32,128]{1,0:T(8,128)(2,1)S(1)} %shard_map.127.refs_11_), channel_id=1, source_target_pairs={{0,2},{1,3},{2,0},{3,1},{4,6},{5,7},{6,4},{7,5},{8,10},{9,11},{10,... | collective-permute-start | bytes 24584 | tf_op jit(solution)/shard_map/ppermute | solution.py:418
  66.4 1.7 %collective-permute-done.16.refs_12_ = bf16[32,128]{1,0:T(8,128)(2,1)S(1)} collective-permute-done((bf16[32,128]{1,0:T(8,128)(2,1)S(1)}, bf16[32,128]{1,0:T(8,128)(2,1)S(1)}, u32[]{:S(2)}, u32[]{:S(2)}) %collective-permute-start.16) | collective-permute-done | bytes 8224 | tf_op jit(solution)/shard_map/ppermute | solution.py:418
  68.0 2.9 %shard_map.128 = (bf16[32,1280]{1,0:T(8,128)(2,1)S(1)}, bf16[32,1280]{1,0:T(8,128)(2,1)S(1)}, bf16[32,1280]{1,0:T(8,128)(2,1)S(1)}, bf16[32,1280]{1,0:T(8,128)(2...) custom-call(bf16[3,2,288,256]{3,2,1,0:T(8,128)(2,1)S(1)} %get-tuple-, ...), custom_call_target="tpu_custom_call", output_to_operand_aliasing={{5}: (16, {}), {6}: (17, {})} | custom-call | tf_op jit(solution)/shard_map/pallas_call | solution.py:36
  72.6 1.8 %collective-permute-start.23 = (bf16[32,1280]{1,0:T(8,128)(2,1)S(1)}, bf16[32,1280]{1,0:T(8,128)(2,1)S(1)}, u32[]{:S(2)}, u32[]{:S(2)}) collective-permute-start(bf16[32,1280]{1,0:T(8,128)(2,1)S(1)} %get-tuple-element.76), channel_id=1, source_target_pairs={{0,3},{1,2},{2,1},{3,0},{4,7},{5,6},{6,5},{7,4},{8,11},{9,10},{10,... | collective-permute-start | bytes 245768 | tf_op jit(solution)/shard_map/ppermute | solution.py:418
  74.4 2.5 %collective-permute-start.20 = (bf16[32,1152]{1,0:T(8,128)(2,1)S(1)}, bf16[32,1152]{1,0:T(8,128)(2,1)S(1)}, u32[]{:S(2)}, u32[]{:S(2)}) collective-permute-start(bf16[32,1152]{1,0:T(8,128)(2,1)S(1)} %get-tuple-element.71), channel_id=1, source_target_pairs={{0,12},{4,8},{8,4},{12,0},{1,13},{5,9},{9,5},{13,1},{2,14},{6,10},... | collective-permute-start | bytes 221192 | tf_op jit(solution)/shard_map/ppermute | solution.py:418
  78.3 2.5 %collective-permute-done.19.refs_3_.refs_2_ = bf16[32,1152]{1,0:T(8,128)(2,1)S(1)} collective-permute-done((bf16[32,1152]{1,0:T(8,128)(2,1)S(1)}, bf16[32,1152]{1,0:T(8,128)(2,1)S(1)}, u32[]{:S(2)}, u32[]{:S(2)}) %collective-permute-start.19) | collective-permute-done | bytes 73760 | tf_op jit(solution)/shard_map/ppermute | solution.py:418
  80.9 2.4 %collective-permute-start.27 = (bf16[64,288]{1,0:T(8,128)(2,1)S(1)}, bf16[64,288]{1,0:T(8,128)(2,1)S(1)}, u32[]{:S(2)}, u32[]{:S(2)}) collective-permute-start(bf16[64,288]{1,0:T(8,128)(2,1)S(1)} %shard_map.131.refs_0_), channel_id=1, source_target_pairs={{0,12},{4,8},{8,4},{12,0},{1,13},{5,9},{9,5},{13,1},{2,14},{6,10},... | collective-permute-start | bytes 110600 | tf_op jit(solution)/shard_map/ppermute | solution.py:418
  83.8 1.6 %collective-permute-start.25 = (bf16[64,288]{1,0:T(8,128)(2,1)S(1)}, bf16[64,288]{1,0:T(8,128)(2,1)S(1)}, u32[]{:S(2)}, u32[]{:S(2)}) collective-permute-start(bf16[64,288]{1,0:T(8,128)(2,1)S(1)} %shard_map.131.refs_0_), channel_id=1, source_target_pairs={{0,4},{4,0},{8,12},{12,8},{1,5},{5,1},{9,13},{13,9},{2,6},{6,2},{1... | collective-permute-start | bytes 110600 | tf_op jit(solution)/shard_map/ppermute | solution.py:418
  85.3 1.5 %collective-permute-done.27.refs_3_ = bf16[64,288]{1,0:T(8,128)(2,1)S(1)} collective-permute-done((bf16[64,288]{1,0:T(8,128)(2,1)S(1)}, bf16[64,288]{1,0:T(8,128)(2,1)S(1)}, u32[]{:S(2)}, u32[]{:S(2)}) %collective-permute-start.27) | collective-permute-done | bytes 36896 | tf_op jit(solution)/shard_map/ppermute | solution.py:418
  86.9 1.6 %collective-permute-done.26.refs_2_ = bf16[64,288]{1,0:T(8,128)(2,1)S(1)} collective-permute-done((bf16[64,288]{1,0:T(8,128)(2,1)S(1)}, bf16[64,288]{1,0:T(8,128)(2,1)S(1)}, u32[]{:S(2)}, u32[]{:S(2)}) %collective-permute-start.26) | collective-permute-done | bytes 36896 | tf_op jit(solution)/shard_map/ppermute | solution.py:418
  88.5 1.5 %collective-permute-start.30 = (bf16[64,288]{1,0:T(8,128)(2,1)S(1)}, bf16[64,288]{1,0:T(8,128)(2,1)S(1)}, u32[]{:S(2)}, u32[]{:S(2)}) collective-permute-start(bf16[64,288]{1,0:T(8,128)(2,1)S(1)} %shard_map.132.refs_0_), channel_id=1, source_target_pairs={{0,3},{1,2},{2,1},{3,0},{4,7},{5,6},{6,5},{7,4},{8,11},{9,10},{10,... | collective-permute-start | bytes 110600 | tf_op jit(solution)/shard_map/ppermute | solution.py:418
  90.6 1.4 %collective-permute-start.28 = (bf16[64,288]{1,0:T(8,128)(2,1)S(1)}, bf16[64,288]{1,0:T(8,128)(2,1)S(1)}, u32[]{:S(2)}, u32[]{:S(2)}) collective-permute-start(bf16[64,288]{1,0:T(8,128)(2,1)S(1)} %shard_map.132.refs_0_), channel_id=1, source_target_pairs={{0,1},{1,0},{2,3},{3,2},{4,5},{5,4},{6,7},{7,6},{8,9},{9,8},{10,11... | collective-permute-start | bytes 110600 | tf_op jit(solution)/shard_map/ppermute | solution.py:418
  92.1 1.5 %collective-permute-done.30.refs_3_ = bf16[64,288]{1,0:T(8,128)(2,1)S(1)} collective-permute-done((bf16[64,288]{1,0:T(8,128)(2,1)S(1)}, bf16[64,288]{1,0:T(8,128)(2,1)S(1)}, u32[]{:S(2)}, u32[]{:S(2)}) %collective-permute-start.30) | collective-permute-done | bytes 36896 | tf_op jit(solution)/shard_map/ppermute | solution.py:418
  (62 shorter events, 20.8 us)
Async XLA Ops:
  3.1 11.9 %collective-permute-start.3 = (bf16[4,32,1152]{2,1,0:T(8,128)(2,1)S(1)}, bf16[4,32,1152]{2,1,0:T(8,128)(2,1)S(1)}, u32[]{:S(2)}, u32[]{:S(2)}) collective-permute-start(bf16[4,32,1152]{2,1,0:T(8,128)(2,1)S(1)} %get-tuple-element.46), channel_id=1, source_target_pairs={{0,4},{4,0},{8,12},{12,8},{1,5},{5,1},{9,13},{13,9},{2,6},{6,2},{1... | collective-permute-start | bytes 884744 | tf_op jit(solution)/shard_map/ppermute | solution.py:418
  8.8 11.8 %collective-permute-start = (bf16[1472,128]{1,0:T(8,128)(2,1)S(1)}, bf16[1472,128]{1,0:T(8,128)(2,1)S(1)}, u32[]{:S(2)}, u32[]{:S(2)}) collective-permute-start(bf16[1472,128]{1,0:T(8,128)(2,1)S(1)} %get-tuple-element.43), channel_id=1, source_target_pairs={{0,1},{1,0},{2,3},{3,2},{4,5},{5,4},{6,7},{7,6},{8,9},{9,8},{10,11... | collective-permute-start | bytes 1130504 | tf_op jit(solution)/shard_map/ppermute | solution.py:418
  10.4 18.0 %collective-permute-start.1 = (bf16[1472,128]{1,0:T(8,128)(2,1)S(1)}, bf16[1472,128]{1,0:T(8,128)(2,1)S(1)}, u32[]{:S(2)}, u32[]{:S(2)}) collective-permute-start(bf16[1472,128]{1,0:T(8,128)(2,1)S(1)} %get-tuple-element.44), channel_id=1, source_target_pairs={{0,2},{1,3},{2,0},{3,1},{4,6},{5,7},{6,4},{7,5},{8,10},{9,11},{10,... | collective-permute-start | bytes 1130504 | tf_op jit(solution)/shard_map/ppermute | solution.py:418
  11.9 16.4 %collective-permute-start.2 = (bf16[1472,128]{1,0:T(8,128)(2,1)S(1)}, bf16[1472,128]{1,0:T(8,128)(2,1)S(1)}, u32[]{:S(2)}, u32[]{:S(2)}) collective-permute-start(bf16[1472,128]{1,0:T(8,128)(2,1)S(1)} %get-tuple-element.45), channel_id=1, source_target_pairs={{0,3},{1,2},{2,1},{3,0},{4,7},{5,6},{6,5},{7,4},{8,11},{9,10},{10,... | collective-permute-start | bytes 1130504 | tf_op jit(solution)/shard_map/ppermute | solution.py:418
  12.4 32.4 %collective-permute-start.7 = (bf16[4,32,1152]{2,1,0:T(8,128)(2,1)}, bf16[4,32,1152]{2,1,0:T(8,128)(2,1)}, u32[]{:S(2)}, u32[]{:S(2)}) collective-permute-start(bf16[4,32,1152]{2,1,0:T(8,128)(2,1)} %get-tuple-element.53), channel_id=1, source_target_pairs={{0,8},{4,12},{8,0},{12,4},{1,9},{5,13},{9,1},{13,5},{2,10},{6,14},... | collective-permute-start | bytes 884744 | tf_op jit(solution)/shard_map/ppermute | solution.py:418
  15.0 29.8 %collective-permute-start.8 = (bf16[4,32,1152]{2,1,0:T(8,128)(2,1)}, bf16[4,32,1152]{2,1,0:T(8,128)(2,1)}, u32[]{:S(2)}, u32[]{:S(2)}) collective-permute-start(bf16[4,32,1152]{2,1,0:T(8,128)(2,1)} %get-tuple-element.54), channel_id=1, source_target_pairs={{0,12},{4,8},{8,4},{12,0},{1,13},{5,9},{9,5},{13,1},{2,14},{6,10},... | collective-permute-start | bytes 884744 | tf_op jit(solution)/shard_map/ppermute | solution.py:418
  32.6 5.1 %collective-permute-start.4 = (bf16[288,128]{1,0:T(8,128)(2,1)S(1)}, bf16[288,128]{1,0:T(8,128)(2,1)S(1)}, u32[]{:S(2)}, u32[]{:S(2)}) collective-permute-start(bf16[288,128]{1,0:T(8,128)(2,1)S(1)} %get-tuple-element.48), channel_id=1, source_target_pairs={{0,1},{1,0},{2,3},{3,2},{4,5},{5,4},{6,7},{7,6},{8,9},{9,8},{10,11... | collective-permute-start | bytes 221192 | tf_op jit(solution)/shard_map/ppermute | solution.py:418
  33.9 4.4 %collective-permute-start.5 = (bf16[288,128]{1,0:T(8,128)(2,1)S(1)}, bf16[288,128]{1,0:T(8,128)(2,1)S(1)}, u32[]{:S(2)}, u32[]{:S(2)}) collective-permute-start(bf16[288,128]{1,0:T(8,128)(2,1)S(1)} %get-tuple-element.49), channel_id=1, source_target_pairs={{0,2},{1,3},{2,0},{3,1},{4,6},{5,7},{6,4},{7,5},{8,10},{9,11},{10,... | collective-permute-start | bytes 221192 | tf_op jit(solution)/shard_map/ppermute | solution.py:418
  34.7 5.3 %collective-permute-start.6 = (bf16[288,128]{1,0:T(8,128)(2,1)S(1)}, bf16[288,128]{1,0:T(8,128)(2,1)S(1)}, u32[]{:S(2)}, u32[]{:S(2)}) collective-permute-start(bf16[288,128]{1,0:T(8,128)(2,1)S(1)} %get-tuple-element.50), channel_id=1, source_target_pairs={{0,3},{1,2},{2,1},{3,0},{4,7},{5,6},{6,5},{7,4},{8,11},{9,10},{10,... | collective-permute-start | bytes 221192 | tf_op jit(solution)/shard_map/ppermute | solution.py:418
  40.3 7.0 %collective-permute-start.9 = (f32[8,128]{1,0:T(8,128)S(1)}, f32[8,128]{1,0:T(8,128)S(1)}, u32[]{:S(2)}, u32[]{:S(2)}) collective-permute-start(f32[8,128]{1,0:T(8,128)S(1)} %get-tuple-element.56), channel_id=1, source_target_pairs={{0,4},{4,0},{8,12},{12,8},{1,5},{5,1},{9,13},{13,9},{2,6},{6,2},{1... | collective-permute-start | bytes 12296 | tf_op jit(solution)/shard_map/ppermute | solution.py:418
  40.8 6.5 %collective-permute-start.10 = (f32[8,128]{1,0:T(8,128)S(1)}, f32[8,128]{1,0:T(8,128)S(1)}, u32[]{:S(2)}, u32[]{:S(2)}) collective-permute-start(f32[8,128]{1,0:T(8,128)S(1)} %get-tuple-element.57), channel_id=1, source_target_pairs={{0,8},{4,12},{8,0},{12,4},{1,9},{5,13},{9,1},{13,5},{2,10},{6,14},... | collective-permute-start | bytes 12296 | tf_op jit(solution)/shard_map/ppermute | solution.py:418
  43.4 5.4 %collective-permute-start.11 = (f32[8,128]{1,0:T(8,128)S(1)}, f32[8,128]{1,0:T(8,128)S(1)}, u32[]{:S(2)}, u32[]{:S(2)}) collective-permute-start(f32[8,128]{1,0:T(8,128)S(1)} %get-tuple-element.58), channel_id=1, source_target_pairs={{0,12},{4,8},{8,4},{12,0},{1,13},{5,9},{9,5},{13,1},{2,14},{6,10},... | collective-permute-start | bytes 12296 | tf_op jit(solution)/shard_map/ppermute | solution.py:418
  53.8 4.6 %collective-permute-start.13 = (f32[8,128]{1,0:T(8,128)S(1)}, f32[8,128]{1,0:T(8,128)S(1)}, u32[]{:S(2)}, u32[]{:S(2)}) collective-permute-start(f32[8,128]{1,0:T(8,128)S(1)} %get-tuple-element.65), channel_id=1, source_target_pairs={{0,4},{4,0},{8,12},{12,8},{1,5},{5,1},{9,13},{13,9},{2,6},{6,2},{1... | collective-permute-start | bytes 12296 | tf_op jit(solution)/shard_map/ppermute | solution.py:418
  53.8 4.6 %collective-permute-start.14 = (f32[8,128]{1,0:T(8,128)S(1)}, f32[8,128]{1,0:T(8,128)S(1)}, u32[]{:S(2)}, u32[]{:S(2)}) collective-permute-start(f32[8,128]{1,0:T(8,128)S(1)} %get-tuple-element.66), channel_id=1, source_target_pairs={{0,8},{4,12},{8,0},{12,4},{1,9},{5,13},{9,1},{13,5},{2,10},{6,14},... | collective-permute-start | bytes 12296 | tf_op jit(solution)/shard_map/ppermute | solution.py:418
  55.7 5.4 %collective-permute-start.15 = (f32[8,128]{1,0:T(8,128)S(1)}, f32[8,128]{1,0:T(8,128)S(1)}, u32[]{:S(2)}, u32[]{:S(2)}) collective-permute-start(f32[8,128]{1,0:T(8,128)S(1)} %get-tuple-element.67), channel_id=1, source_target_pairs={{0,12},{4,8},{8,4},{12,0},{1,13},{5,9},{9,5},{13,1},{2,14},{6,10},... | collective-permute-start | bytes 12296 | tf_op jit(solution)/shard_map/ppermute | solution.py:418
  58.3 9.8 %collective-permute-start.12 = (bf16[32,1152]{1,0:T(8,128)(2,1)S(1)}, bf16[32,1152]{1,0:T(8,128)(2,1)S(1)}, u32[]{:S(2)}, u32[]{:S(2)}) collective-permute-start(bf16[32,1152]{1,0:T(8,128)(2,1)S(1)} %get-tuple-element.60), channel_id=1, source_target_pairs={{0,4},{4,0},{8,12},{12,8},{1,5},{5,1},{9,13},{13,9},{2,6},{6,2},{1... | collective-permute-start | bytes 221192 | tf_op jit(solution)/shard_map/ppermute | solution.py:418
  61.2 4.6 %collective-permute-start.18 = (bf16[32,128]{1,0:T(8,128)(2,1)S(1)}, bf16[32,128]{1,0:T(8,128)(2,1)S(1)}, u32[]{:S(2)}, u32[]{:S(2)}) collective-permute-start(bf16[32,128]{1,0:T(8,128)(2,1)S(1)} %shard_map.127.refs_11_), channel_id=1, source_target_pairs={{0,3},{1,2},{2,1},{3,0},{4,7},{5,6},{6,5},{7,4},{8,11},{9,10},{10,... | collective-permute-start | bytes 24584 | tf_op jit(solution)/shard_map/ppermute | solution.py:418
  62.7 3.7 %collective-permute-start.17 = (bf16[32,128]{1,0:T(8,128)(2,1)S(1)}, bf16[32,128]{1,0:T(8,128)(2,1)S(1)}, u32[]{:S(2)}, u32[]{:S(2)}) collective-permute-start(bf16[32,128]{1,0:T(8,128)(2,1)S(1)} %shard_map.127.refs_11_), channel_id=1, source_target_pairs={{0,2},{1,3},{2,0},{3,1},{4,6},{5,7},{6,4},{7,5},{8,10},{9,11},{10,... | collective-permute-start | bytes 24584 | tf_op jit(solution)/shard_map/ppermute | solution.py:418
  64.3 3.7 %collective-permute-start.16 = (bf16[32,128]{1,0:T(8,128)(2,1)S(1)}, bf16[32,128]{1,0:T(8,128)(2,1)S(1)}, u32[]{:S(2)}, u32[]{:S(2)}) collective-permute-start(bf16[32,128]{1,0:T(8,128)(2,1)S(1)} %shard_map.127.refs_11_), channel_id=1, source_target_pairs={{0,1},{1,0},{2,3},{3,2},{4,5},{5,4},{6,7},{7,6},{8,9},{9,8},{10,11... | collective-permute-start | bytes 24584 | tf_op jit(solution)/shard_map/ppermute | solution.py:418
  70.9 6.1 %collective-permute-start.21 = (bf16[32,1280]{1,0:T(8,128)(2,1)S(1)}, bf16[32,1280]{1,0:T(8,128)(2,1)S(1)}, u32[]{:S(2)}, u32[]{:S(2)}) collective-permute-start(bf16[32,1280]{1,0:T(8,128)(2,1)S(1)} %get-tuple-element.74), channel_id=1, source_target_pairs={{0,1},{1,0},{2,3},{3,2},{4,5},{5,4},{6,7},{7,6},{8,9},{9,8},{10,11... | collective-permute-start | bytes 245768 | tf_op jit(solution)/shard_map/ppermute | solution.py:418
  71.4 5.6 %collective-permute-start.22 = (bf16[32,1280]{1,0:T(8,128)(2,1)S(1)}, bf16[32,1280]{1,0:T(8,128)(2,1)S(1)}, u32[]{:S(2)}, u32[]{:S(2)}) collective-permute-start(bf16[32,1280]{1,0:T(8,128)(2,1)S(1)} %get-tuple-element.75), channel_id=1, source_target_pairs={{0,2},{1,3},{2,0},{3,1},{4,6},{5,7},{6,4},{7,5},{8,10},{9,11},{10,... | collective-permute-start | bytes 245768 | tf_op jit(solution)/shard_map/ppermute | solution.py:418
  72.6 5.3 %collective-permute-start.23 = (bf16[32,1280]{1,0:T(8,128)(2,1)S(1)}, bf16[32,1280]{1,0:T(8,128)(2,1)S(1)}, u32[]{:S(2)}, u32[]{:S(2)}) collective-permute-start(bf16[32,1280]{1,0:T(8,128)(2,1)S(1)} %get-tuple-element.76), channel_id=1, source_target_pairs={{0,3},{1,2},{2,1},{3,0},{4,7},{5,6},{6,5},{7,4},{8,11},{9,10},{10,... | collective-permute-start | bytes 245768 | tf_op jit(solution)/shard_map/ppermute | solution.py:418
  74.4 6.4 %collective-permute-start.19 = (bf16[32,1152]{1,0:T(8,128)(2,1)S(1)}, bf16[32,1152]{1,0:T(8,128)(2,1)S(1)}, u32[]{:S(2)}, u32[]{:S(2)}) collective-permute-start(bf16[32,1152]{1,0:T(8,128)(2,1)S(1)} %get-tuple-element.70), channel_id=1, source_target_pairs={{0,8},{4,12},{8,0},{12,4},{1,9},{5,13},{9,1},{13,5},{2,10},{6,14},... | collective-permute-start | bytes 221192 | tf_op jit(solution)/shard_map/ppermute | solution.py:418
  74.4 6.4 %collective-permute-start.20 = (bf16[32,1152]{1,0:T(8,128)(2,1)S(1)}, bf16[32,1152]{1,0:T(8,128)(2,1)S(1)}, u32[]{:S(2)}, u32[]{:S(2)}) collective-permute-start(bf16[32,1152]{1,0:T(8,128)(2,1)S(1)} %get-tuple-element.71), channel_id=1, source_target_pairs={{0,12},{4,8},{8,4},{12,0},{1,13},{5,9},{9,5},{13,1},{2,14},{6,10},... | collective-permute-start | bytes 221192 | tf_op jit(solution)/shard_map/ppermute | solution.py:418
  78.2 2.6 %collective-permute-start.24 = (f32[64,288]{1,0:T(8,128)S(1)}, f32[64,288]{1,0:T(8,128)S(1)}, u32[]{:S(2)}, u32[]{:S(2)}) collective-permute-start(f32[64,288]{1,0:T(8,128)S(1)} %get-tuple-element.78), channel_id=1, source_target_pairs={{0,16},{16,0},{1,17},{17,1},{2,18},{18,2},{3,19},{19,3},{4,20},{20... | collective-permute-start | bytes 221192 | tf_op jit(solution)/shard_map/ppermute | solution.py:418
  80.9 6.0 %collective-permute-start.27 = (bf16[64,288]{1,0:T(8,128)(2,1)S(1)}, bf16[64,288]{1,0:T(8,128)(2,1)S(1)}, u32[]{:S(2)}, u32[]{:S(2)}) collective-permute-start(bf16[64,288]{1,0:T(8,128)(2,1)S(1)} %shard_map.131.refs_0_), channel_id=1, source_target_pairs={{0,12},{4,8},{8,4},{12,0},{1,13},{5,9},{9,5},{13,1},{2,14},{6,10},... | collective-permute-start | bytes 110600 | tf_op jit(solution)/shard_map/ppermute | solution.py:418
  83.3 5.2 %collective-permute-start.26 = (bf16[64,288]{1,0:T(8,128)(2,1)S(1)}, bf16[64,288]{1,0:T(8,128)(2,1)S(1)}, u32[]{:S(2)}, u32[]{:S(2)}) collective-permute-start(bf16[64,288]{1,0:T(8,128)(2,1)S(1)} %shard_map.131.refs_0_), channel_id=1, source_target_pairs={{0,8},{4,12},{8,0},{12,4},{1,9},{5,13},{9,1},{13,5},{2,10},{6,14},... | collective-permute-start | bytes 110600 | tf_op jit(solution)/shard_map/ppermute | solution.py:418
  83.8 4.7 %collective-permute-start.25 = (bf16[64,288]{1,0:T(8,128)(2,1)S(1)}, bf16[64,288]{1,0:T(8,128)(2,1)S(1)}, u32[]{:S(2)}, u32[]{:S(2)}) collective-permute-start(bf16[64,288]{1,0:T(8,128)(2,1)S(1)} %shard_map.131.refs_0_), channel_id=1, source_target_pairs={{0,4},{4,0},{8,12},{12,8},{1,5},{5,1},{9,13},{13,9},{2,6},{6,2},{1... | collective-permute-start | bytes 110600 | tf_op jit(solution)/shard_map/ppermute | solution.py:418
  88.5 5.1 %collective-permute-start.30 = (bf16[64,288]{1,0:T(8,128)(2,1)S(1)}, bf16[64,288]{1,0:T(8,128)(2,1)S(1)}, u32[]{:S(2)}, u32[]{:S(2)}) collective-permute-start(bf16[64,288]{1,0:T(8,128)(2,1)S(1)} %shard_map.132.refs_0_), channel_id=1, source_target_pairs={{0,3},{1,2},{2,1},{3,0},{4,7},{5,6},{6,5},{7,4},{8,11},{9,10},{10,... | collective-permute-start | bytes 110600 | tf_op jit(solution)/shard_map/ppermute | solution.py:418
  90.0 4.1 %collective-permute-start.29 = (bf16[64,288]{1,0:T(8,128)(2,1)S(1)}, bf16[64,288]{1,0:T(8,128)(2,1)S(1)}, u32[]{:S(2)}, u32[]{:S(2)}) collective-permute-start(bf16[64,288]{1,0:T(8,128)(2,1)S(1)} %shard_map.132.refs_0_), channel_id=1, source_target_pairs={{0,2},{1,3},{2,0},{3,1},{4,6},{5,7},{6,4},{7,5},{8,10},{9,11},{10,... | collective-permute-start | bytes 110600 | tf_op jit(solution)/shard_map/ppermute | solution.py:418
  90.6 4.1 %collective-permute-start.28 = (bf16[64,288]{1,0:T(8,128)(2,1)S(1)}, bf16[64,288]{1,0:T(8,128)(2,1)S(1)}, u32[]{:S(2)}, u32[]{:S(2)}) collective-permute-start(bf16[64,288]{1,0:T(8,128)(2,1)S(1)} %shard_map.132.refs_0_), channel_id=1, source_target_pairs={{0,1},{1,0},{2,3},{3,2},{4,5},{5,4},{6,7},{7,6},{8,9},{9,8},{10,11... | collective-permute-start | bytes 110600 | tf_op jit(solution)/shard_map/ppermute | solution.py:418
  94.9 1.4 %collective-permute-start.31 = (bf16[64,1152]{1,0:T(8,128)(2,1)S(1)}, bf16[64,1152]{1,0:T(8,128)(2,1)S(1)}, u32[]{:S(2)}, u32[]{:S(2)}) collective-permute-start(bf16[64,1152]{1,0:T(8,128)(2,1)S(1)} %shard_map.133.refs_0_), channel_id=1, source_target_pairs={{0,16},{16,0},{1,17},{17,1},{2,18},{18,2},{3,19},{19,3},{4,20},{20... | collective-permute-start | bytes 442376 | tf_op jit(solution)/shard_map/ppermute | solution.py:418
  (7 other events, 162.0 us)

commit v8 on v7

--- a/solution.py
+++ b/solution.py
@@ -21,10 +21,14 @@
     return lax.dot_general(a, b, dims, preferred_element_type=F32)
 
 
+def far(x):
+    return pltpu.with_memory_space_constraint(x, pltpu.HBM)
+
+
 def call(kernel, out_shape, *args, scratch=(), hbm=False, limit=48, after=(), carry=()):
     vmem = pl.BlockSpec(memory_space=pltpu.VMEM)
     anywhere = pl.BlockSpec(memory_space=pl.ANY)
-    main = pl.BlockSpec(memory_space=pltpu.HBM) if hbm else vmem
+    main = anywhere if hbm else vmem
     single = not isinstance(out_shape, (tuple, list))
     outs = (out_shape,) if single else tuple(out_shape)
     used, extra = len(args), len(after) + len(carry)
@@ -37,11 +41,12 @@
         body,
         out_shape=outs + tuple(shape(x.shape, x.dtype) for x in carry),
         in_specs=[main] * used + [anywhere] * extra,
-        out_specs=(vmem,) * len(outs) + (anywhere,) * len(carry),
+        out_specs=tuple(vmem if isinstance(o, jax.ShapeDtypeStruct) else anywhere for o in outs)
+        + (anywhere,) * len(carry),
         scratch_shapes=list(scratch),
         input_output_aliases={used + len(after) + i: len(outs) + i for i in range(len(carry))},
         compiler_params=pltpu.CompilerParams(vmem_limit_bytes=limit * 1024 * 1024),
-    )(*(pltpu.with_memory_space_constraint(x, pltpu.HBM) if hbm else x for x in args), *after, *carry)
+    )(*args, *after, *carry)
     return result[0] if single and not carry else list(result)
 
 
@@ -87,31 +92,15 @@
     return copies
 
 
-def pack_time_kernel(n_t, sub, q_ref, k_ref, v_ref, g_ref, *rest):
-    outs, sems = rest[:n_t], rest[n_t]
-    frames = q_ref.shape[1]
-    copies = []
-    for k in range(n_t):
-        start = pl.multiple_of(peer("tm", k) * sub, sub)
-        for index, ref in enumerate((q_ref, k_ref, v_ref, g_ref)):
-            for f in range(frames):
-                copy = pltpu.make_async_copy(
-                    ref.at[0, f, pl.ds(start, sub)],
-                    outs[k].at[index, f * sub : (f + 1) * sub],
-                    sems.at[len(copies)],
-                )
-                copy.start()
-                copies.append(copy)
-    for copy in copies:
-        copy.wait()
-
-
-def pack_space_kernel(n_s, *refs):
-    ins, refs = refs[:7], refs[7:]
-    outs, buffers, (turned_ref, sems) = refs[:n_s], refs[n_s : n_s + 7], refs[n_s + 7 :]
+def pack_kernel(n_s, n_t, sub, *refs):
+    ins, time_ins, refs = refs[:7], refs[7:11], refs[11:]
+    outs, time_outs, refs = refs[:n_s], refs[n_s : n_s + n_t - 1], refs[n_s + n_t - 1 :]
+    buffers, (time_buf, turned_ref, sems, time_sems) = refs[:7], refs[7:]
     p_buf, at_buf, b_buf, q_buf, v_buf, k_buf, g_buf = buffers
     copies = load_all(ins, buffers, sems)
+    time_copies = load_all(time_ins, [time_buf.at[index] for index in range(4)], time_sems)
     d_s, tokens = turned_ref.shape[2:]
+    frames = time_buf.shape[2]
 
     def flat(ref):
         return ref[0].reshape(tokens, ref.shape[3])
@@ -143,6 +132,14 @@
     send(flat(g_buf), 4)
     for k in range(n_s):
         outs[k][5 * d_s :] = codes_t
+    for index, copy in enumerate(time_copies):
+        copy.wait()
+        for k in range(1, n_t):
+            start = pl.multiple_of(peer("tm", k) * sub, sub)
+            for f in range(frames):
+                time_outs[k - 1][index, f * sub : (f + 1) * sub] = time_buf[
+                    index, 0, f, pl.ds(start, sub)
+                ]
 
 
 def frame_rows(pieces, f, patch_dev):
@@ -150,7 +147,9 @@
 
 
 def space_forward_kernel(frames, n_s, *refs):
-    packed, (qkv_ref, probs_ref, *outs) = refs[:n_s], refs[n_s:]
+    packed, (qkv_ref, probs_ref, *outs) = refs[:n_s], refs[n_s : 2 * n_s + 2]
+    probs_buf, sems = refs[2 * n_s + 2 :]
+    copies = []
     d_s, tokens = outs[0].shape
     patch_dev = tokens // frames
     total = n_s * patch_dev
@@ -171,14 +170,21 @@
             parts = []
             for s in range(0, total, step):
                 probs = probs_of(k_h.T, q_h[:, s : s + step], None)
-                probs_ref[f, h, :, s : s + step] = probs
+                probs_buf[f, h, :, s : s + step] = probs
                 parts.append(mm(v_h, probs.astype(BF16)))
             heads.append(parts[0] if len(parts) == 1 else jnp.concatenate(parts, axis=1))
+            copy = pltpu.make_async_copy(
+                probs_buf.at[f, h], probs_ref.at[f, h], sems.at[len(copies)]
+            )
+            copy.start()
+            copies.append(copy)
         out = jnp.concatenate(heads, axis=0).astype(BF16)
         for k in range(n_s):
             outs[k][:, f * patch_dev : (f + 1) * patch_dev] = out[
                 :, k * patch_dev : (k + 1) * patch_dev
             ]
+    for copy in copies:
+        copy.wait()
 
 
 def lane_block(rows):
@@ -223,11 +229,25 @@
         sends[k][...] = fold(jnp.concatenate(rows, axis=0))
 
 
-def turn_kernel(*refs):
-    pieces, out_ref = refs[:-1], refs[-1]
+def turn_kernel(frames, sub, q_ref, k_ref, v_ref, g_ref, *refs):
+    *pieces, out_ref, own_buf, piece_buf, own_sems, sems = refs
+    own = []
+    start = pl.multiple_of(peer("tm", 0) * sub, sub)
+    for index, ref in enumerate((q_ref, k_ref, v_ref, g_ref)):
+        for f in range(frames):
+            copy = pltpu.make_async_copy(
+                ref.at[0, f, pl.ds(start, sub)],
+                own_buf.at[index, f * sub : (f + 1) * sub],
+                own_sems.at[index * frames + f],
+            )
+            copy.start()
+            own.append(copy)
+    copies = load_all(pieces, [piece_buf.at[k] for k in range(len(pieces))], sems)
+    for copy in own + copies:
+        copy.wait()
     for index in range(4):
-        rows = jnp.concatenate([piece[index] for piece in pieces], axis=0)
-        out_ref[index] = rows.T
+        parts = [own_buf[index]] + [piece_buf[k, index] for k in range(len(pieces))]
+        out_ref[index] = jnp.concatenate(parts, axis=0).T
 
 
 def time_kernel(n_t, sub, x_ref, b_ref, *refs):
@@ -445,32 +465,34 @@
     dma = pltpu.SemaphoreType.DMA
     pad = -(-d_s // 128) * 128
 
-    time_pieces = call(
-        functools.partial(pack_time_kernel, n_t, sub),
-        [shape((4, frames * sub, width), BF16)] * n_t,
-        query_t, key_t, value_t, cotangent,
-        scratch=[dma((4 * frames * n_t,))],
-        hbm=True, limit=48,
-    )
-    time_pieces = exchange(time_pieces, "tm")
+    time_arrays = [far(x) for x in (query_t, key_t, value_t, cotangent)]
+    space_arrays = [
+        far(x) for x in (patches, downs, adapters_b, query_s, value_s, key_s, cotangent)
+    ]
     packed = call(
-        functools.partial(pack_space_kernel, n_s),
-        [shape((5 * d_s + 2 * RANK, tokens), BF16)] * n_s,
-        patches, downs, adapters_b, query_s, value_s, key_s, cotangent,
-        scratch=[
-            pltpu.VMEM(x.shape, BF16)
-            for x in (patches, downs, adapters_b, query_s, value_s, key_s, cotangent)
-        ]
-        + [pltpu.VMEM((5, n_s, d_s, tokens), BF16), dma((7,))],
-        hbm=True, limit=48,
-    )
-    packed = exchange(packed, "space")
+        functools.partial(pack_kernel, n_s, n_t, sub),
+        [shape((5 * d_s + 2 * RANK, tokens), BF16)] * n_s
+        + [shape((4, frames * sub, width), BF16)] * (n_t - 1),
+        *space_arrays, *time_arrays,
+        scratch=[pltpu.VMEM(x.shape, BF16) for x in space_arrays]
+        + [
+            pltpu.VMEM((4,) + query_t.shape, BF16),
+            pltpu.VMEM((5, n_s, d_s, tokens), BF16),
+            dma((7,)),
+            dma((4,)),
+        ],
+        hbm=True,
+    )
+    time_pieces = hops(packed[n_s:], "tm", 1)
+    packed = exchange(packed[:n_s], "space")
+    probs_dims = (frames, d_s // HEAD_DIM, total, total)
     qkv, probs, *out_s = call(
         functools.partial(space_forward_kernel, frames, n_s),
-        [shape((3, frames, d_s, total), BF16), shape((frames, d_s // HEAD_DIM, total, total), F32)]
+        [shape((3, frames, d_s, total), BF16), pltpu.HBM(probs_dims, F32)]
         + [shape((d_s, tokens), BF16)] * n_s,
         *packed,
-        after=[time_pieces[1]],
+        scratch=[pltpu.VMEM(probs_dims, F32), dma((probs_dims[0] * probs_dims[1],))],
+        after=time_pieces[:1],
     )
     out_s = exchange(out_s, "space")
     hidden, *codes = call(
@@ -480,7 +502,18 @@
         scratch=[pltpu.VMEM((n_s, d_s, tokens), BF16), pltpu.VMEM((tokens, 128), F32)],
     )
     codes = exchange(codes, "tm")
-    turned = call(turn_kernel, shape((4, width, n_t * frames * sub), BF16), *time_pieces)
+    turned = call(
+        functools.partial(turn_kernel, frames, sub),
+        shape((4, width, n_t * frames * sub), BF16),
+        *time_arrays, *time_pieces,
+        scratch=[
+            pltpu.VMEM((4, frames * sub, width), BF16),
+            pltpu.VMEM((n_t - 1, 4, frames * sub, width), BF16),
+            dma((4 * frames,)),
+            dma((n_t - 1,)),
+        ],
+        hbm=True,
+    )
     timed = call(
         functools.partial(time_kernel, n_t, sub),
         [shape((frames * sub, width), BF16)] * n_t

time: 97.4 us -> 95.1 us (0.976)
  local copies, waits for them, and re-layouts: 2.64 us -> 0.19 us
    unnamed x14 -> x8, local copies, waits for them, and re-layouts: 2.47 us -> 0.02 us
    pallas_call x14 -> x13, Pallas kernels: 19.8 us -> 19.3 us  [call(): pl.pallas_call(body, out_shape=outs + tuple((shape(x.shape, x.dtype) for...]
  transfers between devices with their start and end apart: 32 -> 32, of which waited for: 18 -> 18; matrix products, arithmetic and copies ran while one was open for 0% -> 0% of each run, Pallas kernels for 9% -> 7%
where the time goes in v8:
time: 95.1 us; the launch traced here: 94.9 us
  starting transfers between devices  42.3 us (44%)
  waiting for transfers between devices  32.3 us (34%)
  Pallas kernels  19.3 us (20%)
    ppermute x32, starting transfers between devices, hops(): lax.ppermute(array, axis, [(i, i ^ k) for i in range(size)])  42.3 us
    ppermute x32, waiting for transfers between devices, hops(): lax.ppermute(array, axis, [(i, i ^ k) for i in range(size)])  32.3 us
    pallas_call x13, Pallas kernels, call(): pl.pallas_call(body, out_shape=outs + tuple((shape(x.shape, x.dtype) for...  19.3 us
  transfers between devices with their start and end apart: 32, of which 18 were waited for; matrix products, arithmetic and copies ran while one was open for 0% of the time, Pallas kernels for 7%

profile of v8, /device:TPU:0, one launch (start us, length us, event | category | flops | bytes accessed | tf_op | source)
XLA Modules:
  0.0 94.9 jit_solution(5906662581482588134)
XLA Ops:
  0.7 3.6 %shard_map.121 = (bf16[1472,128]{1,0:T(8,128)(2,1)S(1)}, bf16[1472,128]{1,0:T(8,128)(2,1)S(1)}, bf16[1472,128]{1,0:T(8,128)(2,1)S(1)}, bf16[1472,128]{1,0:T(8,12...) custom-call(bf16[1,2,64,1152]{3,2,1,0:T(8,128)(2,1)} %refs_4_.3, ...), custom_call_target="tpu_custom_call" | custom-call | tf_op jit(solution)/shard_map/pallas_call | solution.py:40
  4.3 3.1 %collective-permute-start.3 = (bf16[4,32,1152]{2,1,0:T(8,128)(2,1)S(1)}, bf16[4,32,1152]{2,1,0:T(8,128)(2,1)S(1)}, u32[]{:S(2)}, u32[]{:S(2)}) collective-permute-start(bf16[4,32,1152]{2,1,0:T(8,128)(2,1)S(1)} %get-tuple-element.45), channel_id=1, source_target_pairs={{0,4},{4,0},{8,12},{12,8},{1,5},{5,1},{9,13},{13,9},{2,6},{6,2},{1... | collective-permute-start | bytes 884744 | tf_op jit(solution)/shard_map/ppermute | solution.py:438
  7.4 1.5 %collective-permute-start = (bf16[1472,128]{1,0:T(8,128)(2,1)S(1)}, bf16[1472,128]{1,0:T(8,128)(2,1)S(1)}, u32[]{:S(2)}, u32[]{:S(2)}) collective-permute-start(bf16[1472,128]{1,0:T(8,128)(2,1)S(1)} %get-tuple-element.42), channel_id=1, source_target_pairs={{0,1},{1,0},{2,3},{3,2},{4,5},{5,4},{6,7},{7,6},{8,9},{9,8},{10,11... | collective-permute-start | bytes 1130504 | tf_op jit(solution)/shard_map/ppermute | solution.py:438
  8.8 1.6 %collective-permute-start.1 = (bf16[1472,128]{1,0:T(8,128)(2,1)S(1)}, bf16[1472,128]{1,0:T(8,128)(2,1)S(1)}, u32[]{:S(2)}, u32[]{:S(2)}) collective-permute-start(bf16[1472,128]{1,0:T(8,128)(2,1)S(1)} %get-tuple-element.43), channel_id=1, source_target_pairs={{0,2},{1,3},{2,0},{3,1},{4,6},{5,7},{6,4},{7,5},{8,10},{9,11},{10,... | collective-permute-start | bytes 1130504 | tf_op jit(solution)/shard_map/ppermute | solution.py:438
  10.8 2.6 %collective-permute-start.7 = (bf16[4,32,1152]{2,1,0:T(8,128)(2,1)}, bf16[4,32,1152]{2,1,0:T(8,128)(2,1)}, u32[]{:S(2)}, u32[]{:S(2)}) collective-permute-start(bf16[4,32,1152]{2,1,0:T(8,128)(2,1)} %get-tuple-element.51), channel_id=1, source_target_pairs={{0,8},{4,12},{8,0},{12,4},{1,9},{5,13},{9,1},{13,5},{2,10},{6,14},... | collective-permute-start | bytes 884744 | tf_op jit(solution)/shard_map/ppermute | solution.py:438
  13.4 4.1 %collective-permute-done.3.refs_4_ = bf16[4,32,1152]{2,1,0:T(8,128)(2,1)S(1)} collective-permute-done((bf16[4,32,1152]{2,1,0:T(8,128)(2,1)S(1)}, bf16[4,32,1152]{2,1,0:T(8,128)(2,1)S(1)}, u32[]{:S(2)}, u32[]{:S(2)}) %collective-permute-start.3) | collective-permute-done | bytes 294944 | tf_op jit(solution)/shard_map/ppermute | solution.py:438
  17.5 2.8 %collective-permute-start.8 = (bf16[4,32,1152]{2,1,0:T(8,128)(2,1)}, bf16[4,32,1152]{2,1,0:T(8,128)(2,1)}, u32[]{:S(2)}, u32[]{:S(2)}) collective-permute-start(bf16[4,32,1152]{2,1,0:T(8,128)(2,1)} %get-tuple-element.52), channel_id=1, source_target_pairs={{0,12},{4,8},{8,4},{12,0},{1,13},{5,9},{9,5},{13,1},{2,14},{6,10},... | collective-permute-start | bytes 884744 | tf_op jit(solution)/shard_map/ppermute | solution.py:438
  20.3 6.5 %collective-permute-done.1.refs_2_.refs_9_.refs_3_ = bf16[1472,128]{1,0:T(8,128)(2,1)S(1)} collective-permute-done((bf16[1472,128]{1,0:T(8,128)(2,1)S(1)}, bf16[1472,128]{1,0:T(8,128)(2,1)S(1)}, u32[]{:S(2)}, u32[]{:S(2)}) %collective-permute-start.1) | collective-permute-done | bytes 376864 | tf_op jit(solution)/shard_map/ppermute | solution.py:438
  26.9 3.4 %shard_map.122 = (bf16[3,2,288,256]{3,2,1,0:T(8,128)(2,1)S(1)}, f32[2,4,256,256]{3,2,1,0:T(8,128)}, bf16[288,128]{1,0:T(8,128)(2,1)S(1)}, bf16[288,128]{1,0:T(8,...) custom-call(bf16[1472,128]{1,0:T(8,128)(2,1)S(1)} %get-tuple-element.41.refs_0_.refs_7_.refs_1_, ...), custom_call_target="tpu_custom_call" | custom-call | tf_op jit(solution)/shard_map/pallas_call | solution.py:40
  33.9 1.6 %collective-permute-done.4.refs_1_ = bf16[288,128]{1,0:T(8,128)(2,1)S(1)} collective-permute-done((bf16[288,128]{1,0:T(8,128)(2,1)S(1)}, bf16[288,128]{1,0:T(8,128)(2,1)S(1)}, u32[]{:S(2)}, u32[]{:S(2)}) %collective-permute-start.4) | collective-permute-done | bytes 73760 | tf_op jit(solution)/shard_map/ppermute | solution.py:438
  36.0 1.7 %collective-permute-done.6.refs_3_ = bf16[288,128]{1,0:T(8,128)(2,1)S(1)} collective-permute-done((bf16[288,128]{1,0:T(8,128)(2,1)S(1)}, bf16[288,128]{1,0:T(8,128)(2,1)S(1)}, u32[]{:S(2)}, u32[]{:S(2)}) %collective-permute-start.6) | collective-permute-done | bytes 73760 | tf_op jit(solution)/shard_map/ppermute | solution.py:438
  38.6 2.6 %collective-permute-start.10 = (f32[8,128]{1,0:T(8,128)S(1)}, f32[8,128]{1,0:T(8,128)S(1)}, u32[]{:S(2)}, u32[]{:S(2)}) collective-permute-start(f32[8,128]{1,0:T(8,128)S(1)} %get-tuple-element.55), channel_id=1, source_target_pairs={{0,8},{4,12},{8,0},{12,4},{1,9},{5,13},{9,1},{13,5},{2,10},{6,14},... | collective-permute-start | bytes 12296 | tf_op jit(solution)/shard_map/ppermute | solution.py:438
  42.5 1.8 %shard_map.124.refs_0_ = bf16[4,1152,128]{2,1,0:T(8,128)(2,1)S(1)} custom-call(bf16[1,2,64,1152]{3,2,1,0:T(8,128)(2,1)} %refs_0_.3, bf16[1,2,64,1152]{3,2,1,0:T(8,128)(2,1)} %refs_1_.2, bf16[1,2,64,1152]{3,2,1,0:T(8,128)(2,1)} %refs_2_.3, bf16[1,2,64,1152]{3,2,1,0:T(8,128)(2,1)} %refs_3_.3, bf16[4,32,1152]{2,1,0:T(8,128)(2,1)S(1)} %collective-permute-done.3.refs_4_, ...), custom_call_target="tpu_custom_call" | custom-call | tf_op jit(solution)/shard_map/pallas_call | solution.py:40
  44.4 2.2 %collective-permute-done.11.refs_5_ = f32[8,128]{1,0:T(8,128)S(1)} collective-permute-done((f32[8,128]{1,0:T(8,128)S(1)}, f32[8,128]{1,0:T(8,128)S(1)}, u32[]{:S(2)}, u32[]{:S(2)}) %collective-permute-start.11) | collective-permute-done | bytes 4128 | tf_op jit(solution)/shard_map/ppermute | solution.py:438
  46.6 4.9 %shard_map.125 = (bf16[32,1152]{1,0:T(8,128)(2,1)S(1)}, bf16[32,1152]{1,0:T(8,128)(2,1)S(1)}, bf16[32,1152]{1,0:T(8,128)(2,1)S(1)}, bf16[32,1152]{1,0:T(8,128)(2...) custom-call(bf16[4,1152,128]{2,1,0:T(8,128)(2,1)S(1)} %shard_map.124, ...), custom_call_target="tpu_custom_call" | custom-call | tf_op jit(solution)/shard_map/pallas_call | solution.py:40
  51.5 1.9 %collective-permute-start.14 = (f32[8,128]{1,0:T(8,128)S(1)}, f32[8,128]{1,0:T(8,128)S(1)}, u32[]{:S(2)}, u32[]{:S(2)}) collective-permute-start(f32[8,128]{1,0:T(8,128)S(1)} %get-tuple-element.64), channel_id=1, source_target_pairs={{0,8},{4,12},{8,0},{12,4},{1,9},{5,13},{9,1},{13,5},{2,10},{6,14},... | collective-permute-start | bytes 12296 | tf_op jit(solution)/shard_map/ppermute | solution.py:438
  53.4 2.5 %collective-permute-start.15 = (f32[8,128]{1,0:T(8,128)S(1)}, f32[8,128]{1,0:T(8,128)S(1)}, u32[]{:S(2)}, u32[]{:S(2)}) collective-permute-start(f32[8,128]{1,0:T(8,128)S(1)} %get-tuple-element.65), channel_id=1, source_target_pairs={{0,12},{4,8},{8,4},{12,0},{1,13},{5,9},{9,5},{13,1},{2,14},{6,10},... | collective-permute-start | bytes 12296 | tf_op jit(solution)/shard_map/ppermute | solution.py:438
  56.1 2.7 %collective-permute-done.15.refs_3_ = f32[8,128]{1,0:T(8,128)S(1)} collective-permute-done((f32[8,128]{1,0:T(8,128)S(1)}, f32[8,128]{1,0:T(8,128)S(1)}, u32[]{:S(2)}, u32[]{:S(2)}) %collective-permute-start.15) | collective-permute-done | bytes 4128 | tf_op jit(solution)/shard_map/ppermute | solution.py:438
  59.0 1.5 %collective-permute-start.18 = (bf16[32,128]{1,0:T(8,128)(2,1)S(1)}, bf16[32,128]{1,0:T(8,128)(2,1)S(1)}, u32[]{:S(2)}, u32[]{:S(2)}) collective-permute-start(bf16[32,128]{1,0:T(8,128)(2,1)S(1)} %shard_map.126.refs_11_), channel_id=1, source_target_pairs={{0,3},{1,2},{2,1},{3,0},{4,7},{5,6},{6,5},{7,4},{8,11},{9,10},{10,... | collective-permute-start | bytes 24584 | tf_op jit(solution)/shard_map/ppermute | solution.py:438
  60.5 1.6 %collective-permute-start.17 = (bf16[32,128]{1,0:T(8,128)(2,1)S(1)}, bf16[32,128]{1,0:T(8,128)(2,1)S(1)}, u32[]{:S(2)}, u32[]{:S(2)}) collective-permute-start(bf16[32,128]{1,0:T(8,128)(2,1)S(1)} %shard_map.126.refs_11_), channel_id=1, source_target_pairs={{0,2},{1,3},{2,0},{3,1},{4,6},{5,7},{6,4},{7,5},{8,10},{9,11},{10,... | collective-permute-start | bytes 24584 | tf_op jit(solution)/shard_map/ppermute | solution.py:438
  64.2 1.5 %collective-permute-done.16.refs_12_ = bf16[32,128]{1,0:T(8,128)(2,1)S(1)} collective-permute-done((bf16[32,128]{1,0:T(8,128)(2,1)S(1)}, bf16[32,128]{1,0:T(8,128)(2,1)S(1)}, u32[]{:S(2)}, u32[]{:S(2)}) %collective-permute-start.16) | collective-permute-done | bytes 8224 | tf_op jit(solution)/shard_map/ppermute | solution.py:438
  65.7 2.8 %shard_map.127 = (bf16[32,1280]{1,0:T(8,128)(2,1)S(1)}, bf16[32,1280]{1,0:T(8,128)(2,1)S(1)}, bf16[32,1280]{1,0:T(8,128)(2,1)S(1)}, bf16[32,1280]{1,0:T(8,128)(2...) custom-call(bf16[3,2,288,256]{3,2,1,0:T(8,128)(2,1)S(1)} %get-tuple-, ...), custom_call_target="tpu_custom_call", output_to_operand_aliasing={{5}: (16, {}), {6}: (17, {})} | custom-call | tf_op jit(solution)/shard_map/pallas_call | solution.py:40
  70.4 1.7 %collective-permute-start.23 = (bf16[32,1280]{1,0:T(8,128)(2,1)S(1)}, bf16[32,1280]{1,0:T(8,128)(2,1)S(1)}, u32[]{:S(2)}, u32[]{:S(2)}) collective-permute-start(bf16[32,1280]{1,0:T(8,128)(2,1)S(1)} %get-tuple-element.74), channel_id=1, source_target_pairs={{0,3},{1,2},{2,1},{3,0},{4,7},{5,6},{6,5},{7,4},{8,11},{9,10},{10,... | collective-permute-start | bytes 245768 | tf_op jit(solution)/shard_map/ppermute | solution.py:438
  72.1 2.6 %collective-permute-start.20 = (bf16[32,1152]{1,0:T(8,128)(2,1)S(1)}, bf16[32,1152]{1,0:T(8,128)(2,1)S(1)}, u32[]{:S(2)}, u32[]{:S(2)}) collective-permute-start(bf16[32,1152]{1,0:T(8,128)(2,1)S(1)} %get-tuple-element.69), channel_id=1, source_target_pairs={{0,12},{4,8},{8,4},{12,0},{1,13},{5,9},{9,5},{13,1},{2,14},{6,10},... | collective-permute-start | bytes 221192 | tf_op jit(solution)/shard_map/ppermute | solution.py:438
  76.2 2.5 %collective-permute-done.19.refs_3_.refs_2_ = bf16[32,1152]{1,0:T(8,128)(2,1)S(1)} collective-permute-done((bf16[32,1152]{1,0:T(8,128)(2,1)S(1)}, bf16[32,1152]{1,0:T(8,128)(2,1)S(1)}, u32[]{:S(2)}, u32[]{:S(2)}) %collective-permute-start.19) | collective-permute-done | bytes 73760 | tf_op jit(solution)/shard_map/ppermute | solution.py:438
  78.6 2.4 %collective-permute-start.27 = (bf16[64,288]{1,0:T(8,128)(2,1)S(1)}, bf16[64,288]{1,0:T(8,128)(2,1)S(1)}, u32[]{:S(2)}, u32[]{:S(2)}) collective-permute-start(bf16[64,288]{1,0:T(8,128)(2,1)S(1)} %shard_map.130.refs_0_), channel_id=1, source_target_pairs={{0,12},{4,8},{8,4},{12,0},{1,13},{5,9},{9,5},{13,1},{2,14},{6,10},... | collective-permute-start | bytes 110600 | tf_op jit(solution)/shard_map/ppermute | solution.py:438
  81.5 1.6 %collective-permute-start.25 = (bf16[64,288]{1,0:T(8,128)(2,1)S(1)}, bf16[64,288]{1,0:T(8,128)(2,1)S(1)}, u32[]{:S(2)}, u32[]{:S(2)}) collective-permute-start(bf16[64,288]{1,0:T(8,128)(2,1)S(1)} %shard_map.130.refs_0_), channel_id=1, source_target_pairs={{0,4},{4,0},{8,12},{12,8},{1,5},{5,1},{9,13},{13,9},{2,6},{6,2},{1... | collective-permute-start | bytes 110600 | tf_op jit(solution)/shard_map/ppermute | solution.py:438
  83.1 1.6 %collective-permute-done.27.refs_3_ = bf16[64,288]{1,0:T(8,128)(2,1)S(1)} collective-permute-done((bf16[64,288]{1,0:T(8,128)(2,1)S(1)}, bf16[64,288]{1,0:T(8,128)(2,1)S(1)}, u32[]{:S(2)}, u32[]{:S(2)}) %collective-permute-start.27) | collective-permute-done | bytes 36896 | tf_op jit(solution)/shard_map/ppermute | solution.py:438
  84.7 1.5 %collective-permute-done.26.refs_2_ = bf16[64,288]{1,0:T(8,128)(2,1)S(1)} collective-permute-done((bf16[64,288]{1,0:T(8,128)(2,1)S(1)}, bf16[64,288]{1,0:T(8,128)(2,1)S(1)}, u32[]{:S(2)}, u32[]{:S(2)}) %collective-permute-start.26) | collective-permute-done | bytes 36896 | tf_op jit(solution)/shard_map/ppermute | solution.py:438
  86.3 1.5 %collective-permute-start.30 = (bf16[64,288]{1,0:T(8,128)(2,1)S(1)}, bf16[64,288]{1,0:T(8,128)(2,1)S(1)}, u32[]{:S(2)}, u32[]{:S(2)}) collective-permute-start(bf16[64,288]{1,0:T(8,128)(2,1)S(1)} %shard_map.131.refs_0_), channel_id=1, source_target_pairs={{0,3},{1,2},{2,1},{3,0},{4,7},{5,6},{6,5},{7,4},{8,11},{9,10},{10,... | collective-permute-start | bytes 110600 | tf_op jit(solution)/shard_map/ppermute | solution.py:438
  88.4 1.4 %collective-permute-start.28 = (bf16[64,288]{1,0:T(8,128)(2,1)S(1)}, bf16[64,288]{1,0:T(8,128)(2,1)S(1)}, u32[]{:S(2)}, u32[]{:S(2)}) collective-permute-start(bf16[64,288]{1,0:T(8,128)(2,1)S(1)} %shard_map.131.refs_0_), channel_id=1, source_target_pairs={{0,1},{1,0},{2,3},{3,2},{4,5},{5,4},{6,7},{7,6},{8,9},{9,8},{10,11... | collective-permute-start | bytes 110600 | tf_op jit(solution)/shard_map/ppermute | solution.py:438
  89.8 1.5 %collective-permute-done.30.refs_3_ = bf16[64,288]{1,0:T(8,128)(2,1)S(1)} collective-permute-done((bf16[64,288]{1,0:T(8,128)(2,1)S(1)}, bf16[64,288]{1,0:T(8,128)(2,1)S(1)}, u32[]{:S(2)}, u32[]{:S(2)}) %collective-permute-start.30) | collective-permute-done | bytes 36896 | tf_op jit(solution)/shard_map/ppermute | solution.py:438
  (55 shorter events, 17.3 us)
Async XLA Ops:
  4.3 13.2 %collective-permute-start.3 = (bf16[4,32,1152]{2,1,0:T(8,128)(2,1)S(1)}, bf16[4,32,1152]{2,1,0:T(8,128)(2,1)S(1)}, u32[]{:S(2)}, u32[]{:S(2)}) collective-permute-start(bf16[4,32,1152]{2,1,0:T(8,128)(2,1)S(1)} %get-tuple-element.45), channel_id=1, source_target_pairs={{0,4},{4,0},{8,12},{12,8},{1,5},{5,1},{9,13},{13,9},{2,6},{6,2},{1... | collective-permute-start | bytes 884744 | tf_op jit(solution)/shard_map/ppermute | solution.py:438
  7.4 13.0 %collective-permute-start = (bf16[1472,128]{1,0:T(8,128)(2,1)S(1)}, bf16[1472,128]{1,0:T(8,128)(2,1)S(1)}, u32[]{:S(2)}, u32[]{:S(2)}) collective-permute-start(bf16[1472,128]{1,0:T(8,128)(2,1)S(1)} %get-tuple-element.42), channel_id=1, source_target_pairs={{0,1},{1,0},{2,3},{3,2},{4,5},{5,4},{6,7},{7,6},{8,9},{9,8},{10,11... | collective-permute-start | bytes 1130504 | tf_op jit(solution)/shard_map/ppermute | solution.py:438
  8.8 18.0 %collective-permute-start.1 = (bf16[1472,128]{1,0:T(8,128)(2,1)S(1)}, bf16[1472,128]{1,0:T(8,128)(2,1)S(1)}, u32[]{:S(2)}, u32[]{:S(2)}) collective-permute-start(bf16[1472,128]{1,0:T(8,128)(2,1)S(1)} %get-tuple-element.43), channel_id=1, source_target_pairs={{0,2},{1,3},{2,0},{3,1},{4,6},{5,7},{6,4},{7,5},{8,10},{9,11},{10,... | collective-permute-start | bytes 1130504 | tf_op jit(solution)/shard_map/ppermute | solution.py:438
  10.4 16.4 %collective-permute-start.2 = (bf16[1472,128]{1,0:T(8,128)(2,1)S(1)}, bf16[1472,128]{1,0:T(8,128)(2,1)S(1)}, u32[]{:S(2)}, u32[]{:S(2)}) collective-permute-start(bf16[1472,128]{1,0:T(8,128)(2,1)S(1)} %get-tuple-element.44), channel_id=1, source_target_pairs={{0,3},{1,2},{2,1},{3,0},{4,7},{5,6},{6,5},{7,4},{8,11},{9,10},{10,... | collective-permute-start | bytes 1130504 | tf_op jit(solution)/shard_map/ppermute | solution.py:438
  10.8 31.7 %collective-permute-start.7 = (bf16[4,32,1152]{2,1,0:T(8,128)(2,1)}, bf16[4,32,1152]{2,1,0:T(8,128)(2,1)}, u32[]{:S(2)}, u32[]{:S(2)}) collective-permute-start(bf16[4,32,1152]{2,1,0:T(8,128)(2,1)} %get-tuple-element.51), channel_id=1, source_target_pairs={{0,8},{4,12},{8,0},{12,4},{1,9},{5,13},{9,1},{13,5},{2,10},{6,14},... | collective-permute-start | bytes 884744 | tf_op jit(solution)/shard_map/ppermute | solution.py:438
  17.5 25.0 %collective-permute-start.8 = (bf16[4,32,1152]{2,1,0:T(8,128)(2,1)}, bf16[4,32,1152]{2,1,0:T(8,128)(2,1)}, u32[]{:S(2)}, u32[]{:S(2)}) collective-permute-start(bf16[4,32,1152]{2,1,0:T(8,128)(2,1)} %get-tuple-element.52), channel_id=1, source_target_pairs={{0,12},{4,8},{8,4},{12,0},{1,13},{5,9},{9,5},{13,1},{2,14},{6,10},... | collective-permute-start | bytes 884744 | tf_op jit(solution)/shard_map/ppermute | solution.py:438
  30.3 5.2 %collective-permute-start.4 = (bf16[288,128]{1,0:T(8,128)(2,1)S(1)}, bf16[288,128]{1,0:T(8,128)(2,1)S(1)}, u32[]{:S(2)}, u32[]{:S(2)}) collective-permute-start(bf16[288,128]{1,0:T(8,128)(2,1)S(1)} %get-tuple-element.47), channel_id=1, source_target_pairs={{0,1},{1,0},{2,3},{3,2},{4,5},{5,4},{6,7},{7,6},{8,9},{9,8},{10,11... | collective-permute-start | bytes 221192 | tf_op jit(solution)/shard_map/ppermute | solution.py:438
  31.7 4.4 %collective-permute-start.5 = (bf16[288,128]{1,0:T(8,128)(2,1)S(1)}, bf16[288,128]{1,0:T(8,128)(2,1)S(1)}, u32[]{:S(2)}, u32[]{:S(2)}) collective-permute-start(bf16[288,128]{1,0:T(8,128)(2,1)S(1)} %get-tuple-element.48), channel_id=1, source_target_pairs={{0,2},{1,3},{2,0},{3,1},{4,6},{5,7},{6,4},{7,5},{8,10},{9,11},{10,... | collective-permute-start | bytes 221192 | tf_op jit(solution)/shard_map/ppermute | solution.py:438
  32.4 5.3 %collective-permute-start.6 = (bf16[288,128]{1,0:T(8,128)(2,1)S(1)}, bf16[288,128]{1,0:T(8,128)(2,1)S(1)}, u32[]{:S(2)}, u32[]{:S(2)}) collective-permute-start(bf16[288,128]{1,0:T(8,128)(2,1)S(1)} %get-tuple-element.49), channel_id=1, source_target_pairs={{0,3},{1,2},{2,1},{3,0},{4,7},{5,6},{6,5},{7,4},{8,11},{9,10},{10,... | collective-permute-start | bytes 221192 | tf_op jit(solution)/shard_map/ppermute | solution.py:438
  38.0 6.3 %collective-permute-start.9 = (f32[8,128]{1,0:T(8,128)S(1)}, f32[8,128]{1,0:T(8,128)S(1)}, u32[]{:S(2)}, u32[]{:S(2)}) collective-permute-start(f32[8,128]{1,0:T(8,128)S(1)} %get-tuple-element.54), channel_id=1, source_target_pairs={{0,4},{4,0},{8,12},{12,8},{1,5},{5,1},{9,13},{13,9},{2,6},{6,2},{1... | collective-permute-start | bytes 12296 | tf_op jit(solution)/shard_map/ppermute | solution.py:438
  38.6 5.8 %collective-permute-start.10 = (f32[8,128]{1,0:T(8,128)S(1)}, f32[8,128]{1,0:T(8,128)S(1)}, u32[]{:S(2)}, u32[]{:S(2)}) collective-permute-start(f32[8,128]{1,0:T(8,128)S(1)} %get-tuple-element.55), channel_id=1, source_target_pairs={{0,8},{4,12},{8,0},{12,4},{1,9},{5,13},{9,1},{13,5},{2,10},{6,14},... | collective-permute-start | bytes 12296 | tf_op jit(solution)/shard_map/ppermute | solution.py:438
  41.2 5.4 %collective-permute-start.11 = (f32[8,128]{1,0:T(8,128)S(1)}, f32[8,128]{1,0:T(8,128)S(1)}, u32[]{:S(2)}, u32[]{:S(2)}) collective-permute-start(f32[8,128]{1,0:T(8,128)S(1)} %get-tuple-element.56), channel_id=1, source_target_pairs={{0,12},{4,8},{8,4},{12,0},{1,13},{5,9},{9,5},{13,1},{2,14},{6,10},... | collective-permute-start | bytes 12296 | tf_op jit(solution)/shard_map/ppermute | solution.py:438
  51.5 4.6 %collective-permute-start.13 = (f32[8,128]{1,0:T(8,128)S(1)}, f32[8,128]{1,0:T(8,128)S(1)}, u32[]{:S(2)}, u32[]{:S(2)}) collective-permute-start(f32[8,128]{1,0:T(8,128)S(1)} %get-tuple-element.63), channel_id=1, source_target_pairs={{0,4},{4,0},{8,12},{12,8},{1,5},{5,1},{9,13},{13,9},{2,6},{6,2},{1... | collective-permute-start | bytes 12296 | tf_op jit(solution)/shard_map/ppermute | solution.py:438
  51.5 4.6 %collective-permute-start.14 = (f32[8,128]{1,0:T(8,128)S(1)}, f32[8,128]{1,0:T(8,128)S(1)}, u32[]{:S(2)}, u32[]{:S(2)}) collective-permute-start(f32[8,128]{1,0:T(8,128)S(1)} %get-tuple-element.64), channel_id=1, source_target_pairs={{0,8},{4,12},{8,0},{12,4},{1,9},{5,13},{9,1},{13,5},{2,10},{6,14},... | collective-permute-start | bytes 12296 | tf_op jit(solution)/shard_map/ppermute | solution.py:438
  53.4 5.4 %collective-permute-start.15 = (f32[8,128]{1,0:T(8,128)S(1)}, f32[8,128]{1,0:T(8,128)S(1)}, u32[]{:S(2)}, u32[]{:S(2)}) collective-permute-start(f32[8,128]{1,0:T(8,128)S(1)} %get-tuple-element.65), channel_id=1, source_target_pairs={{0,12},{4,8},{8,4},{12,0},{1,13},{5,9},{9,5},{13,1},{2,14},{6,10},... | collective-permute-start | bytes 12296 | tf_op jit(solution)/shard_map/ppermute | solution.py:438
  56.0 9.7 %collective-permute-start.12 = (bf16[32,1152]{1,0:T(8,128)(2,1)S(1)}, bf16[32,1152]{1,0:T(8,128)(2,1)S(1)}, u32[]{:S(2)}, u32[]{:S(2)}) collective-permute-start(bf16[32,1152]{1,0:T(8,128)(2,1)S(1)} %get-tuple-element.58), channel_id=1, source_target_pairs={{0,4},{4,0},{8,12},{12,8},{1,5},{5,1},{9,13},{13,9},{2,6},{6,2},{1... | collective-permute-start | bytes 221192 | tf_op jit(solution)/shard_map/ppermute | solution.py:438
  59.0 4.6 %collective-permute-start.18 = (bf16[32,128]{1,0:T(8,128)(2,1)S(1)}, bf16[32,128]{1,0:T(8,128)(2,1)S(1)}, u32[]{:S(2)}, u32[]{:S(2)}) collective-permute-start(bf16[32,128]{1,0:T(8,128)(2,1)S(1)} %shard_map.126.refs_11_), channel_id=1, source_target_pairs={{0,3},{1,2},{2,1},{3,0},{4,7},{5,6},{6,5},{7,4},{8,11},{9,10},{10,... | collective-permute-start | bytes 24584 | tf_op jit(solution)/shard_map/ppermute | solution.py:438
  60.5 3.7 %collective-permute-start.17 = (bf16[32,128]{1,0:T(8,128)(2,1)S(1)}, bf16[32,128]{1,0:T(8,128)(2,1)S(1)}, u32[]{:S(2)}, u32[]{:S(2)}) collective-permute-start(bf16[32,128]{1,0:T(8,128)(2,1)S(1)} %shard_map.126.refs_11_), channel_id=1, source_target_pairs={{0,2},{1,3},{2,0},{3,1},{4,6},{5,7},{6,4},{7,5},{8,10},{9,11},{10,... | collective-permute-start | bytes 24584 | tf_op jit(solution)/shard_map/ppermute | solution.py:438
  62.0 3.7 %collective-permute-start.16 = (bf16[32,128]{1,0:T(8,128)(2,1)S(1)}, bf16[32,128]{1,0:T(8,128)(2,1)S(1)}, u32[]{:S(2)}, u32[]{:S(2)}) collective-permute-start(bf16[32,128]{1,0:T(8,128)(2,1)S(1)} %shard_map.126.refs_11_), channel_id=1, source_target_pairs={{0,1},{1,0},{2,3},{3,2},{4,5},{5,4},{6,7},{7,6},{8,9},{9,8},{10,11... | collective-permute-start | bytes 24584 | tf_op jit(solution)/shard_map/ppermute | solution.py:438
  68.6 6.1 %collective-permute-start.21 = (bf16[32,1280]{1,0:T(8,128)(2,1)S(1)}, bf16[32,1280]{1,0:T(8,128)(2,1)S(1)}, u32[]{:S(2)}, u32[]{:S(2)}) collective-permute-start(bf16[32,1280]{1,0:T(8,128)(2,1)S(1)} %get-tuple-element.72), channel_id=1, source_target_pairs={{0,1},{1,0},{2,3},{3,2},{4,5},{5,4},{6,7},{7,6},{8,9},{9,8},{10,11... | collective-permute-start | bytes 245768 | tf_op jit(solution)/shard_map/ppermute | solution.py:438
  69.1 5.6 %collective-permute-start.22 = (bf16[32,1280]{1,0:T(8,128)(2,1)S(1)}, bf16[32,1280]{1,0:T(8,128)(2,1)S(1)}, u32[]{:S(2)}, u32[]{:S(2)}) collective-permute-start(bf16[32,1280]{1,0:T(8,128)(2,1)S(1)} %get-tuple-element.73), channel_id=1, source_target_pairs={{0,2},{1,3},{2,0},{3,1},{4,6},{5,7},{6,4},{7,5},{8,10},{9,11},{10,... | collective-permute-start | bytes 245768 | tf_op jit(solution)/shard_map/ppermute | solution.py:438
  70.4 5.3 %collective-permute-start.23 = (bf16[32,1280]{1,0:T(8,128)(2,1)S(1)}, bf16[32,1280]{1,0:T(8,128)(2,1)S(1)}, u32[]{:S(2)}, u32[]{:S(2)}) collective-permute-start(bf16[32,1280]{1,0:T(8,128)(2,1)S(1)} %get-tuple-element.74), channel_id=1, source_target_pairs={{0,3},{1,2},{2,1},{3,0},{4,7},{5,6},{6,5},{7,4},{8,11},{9,10},{10,... | collective-permute-start | bytes 245768 | tf_op jit(solution)/shard_map/ppermute | solution.py:438
  72.1 6.5 %collective-permute-start.19 = (bf16[32,1152]{1,0:T(8,128)(2,1)S(1)}, bf16[32,1152]{1,0:T(8,128)(2,1)S(1)}, u32[]{:S(2)}, u32[]{:S(2)}) collective-permute-start(bf16[32,1152]{1,0:T(8,128)(2,1)S(1)} %get-tuple-element.68), channel_id=1, source_target_pairs={{0,8},{4,12},{8,0},{12,4},{1,9},{5,13},{9,1},{13,5},{2,10},{6,14},... | collective-permute-start | bytes 221192 | tf_op jit(solution)/shard_map/ppermute | solution.py:438
  72.1 6.5 %collective-permute-start.20 = (bf16[32,1152]{1,0:T(8,128)(2,1)S(1)}, bf16[32,1152]{1,0:T(8,128)(2,1)S(1)}, u32[]{:S(2)}, u32[]{:S(2)}) collective-permute-start(bf16[32,1152]{1,0:T(8,128)(2,1)S(1)} %get-tuple-element.69), channel_id=1, source_target_pairs={{0,12},{4,8},{8,4},{12,0},{1,13},{5,9},{9,5},{13,1},{2,14},{6,10},... | collective-permute-start | bytes 221192 | tf_op jit(solution)/shard_map/ppermute | solution.py:438
  76.1 2.5 %collective-permute-start.24 = (f32[64,288]{1,0:T(8,128)S(1)}, f32[64,288]{1,0:T(8,128)S(1)}, u32[]{:S(2)}, u32[]{:S(2)}) collective-permute-start(f32[64,288]{1,0:T(8,128)S(1)} %get-tuple-element.76), channel_id=1, source_target_pairs={{0,16},{16,0},{1,17},{17,1},{2,18},{18,2},{3,19},{19,3},{4,20},{20... | collective-permute-start | bytes 221192 | tf_op jit(solution)/shard_map/ppermute | solution.py:438
  78.6 6.1 %collective-permute-start.27 = (bf16[64,288]{1,0:T(8,128)(2,1)S(1)}, bf16[64,288]{1,0:T(8,128)(2,1)S(1)}, u32[]{:S(2)}, u32[]{:S(2)}) collective-permute-start(bf16[64,288]{1,0:T(8,128)(2,1)S(1)} %shard_map.130.refs_0_), channel_id=1, source_target_pairs={{0,12},{4,8},{8,4},{12,0},{1,13},{5,9},{9,5},{13,1},{2,14},{6,10},... | collective-permute-start | bytes 110600 | tf_op jit(solution)/shard_map/ppermute | solution.py:438
  81.0 5.2 %collective-permute-start.26 = (bf16[64,288]{1,0:T(8,128)(2,1)S(1)}, bf16[64,288]{1,0:T(8,128)(2,1)S(1)}, u32[]{:S(2)}, u32[]{:S(2)}) collective-permute-start(bf16[64,288]{1,0:T(8,128)(2,1)S(1)} %shard_map.130.refs_0_), channel_id=1, source_target_pairs={{0,8},{4,12},{8,0},{12,4},{1,9},{5,13},{9,1},{13,5},{2,10},{6,14},... | collective-permute-start | bytes 110600 | tf_op jit(solution)/shard_map/ppermute | solution.py:438
  81.5 4.7 %collective-permute-start.25 = (bf16[64,288]{1,0:T(8,128)(2,1)S(1)}, bf16[64,288]{1,0:T(8,128)(2,1)S(1)}, u32[]{:S(2)}, u32[]{:S(2)}) collective-permute-start(bf16[64,288]{1,0:T(8,128)(2,1)S(1)} %shard_map.130.refs_0_), channel_id=1, source_target_pairs={{0,4},{4,0},{8,12},{12,8},{1,5},{5,1},{9,13},{13,9},{2,6},{6,2},{1... | collective-permute-start | bytes 110600 | tf_op jit(solution)/shard_map/ppermute | solution.py:438
  86.3 5.1 %collective-permute-start.30 = (bf16[64,288]{1,0:T(8,128)(2,1)S(1)}, bf16[64,288]{1,0:T(8,128)(2,1)S(1)}, u32[]{:S(2)}, u32[]{:S(2)}) collective-permute-start(bf16[64,288]{1,0:T(8,128)(2,1)S(1)} %shard_map.131.refs_0_), channel_id=1, source_target_pairs={{0,3},{1,2},{2,1},{3,0},{4,7},{5,6},{6,5},{7,4},{8,11},{9,10},{10,... | collective-permute-start | bytes 110600 | tf_op jit(solution)/shard_map/ppermute | solution.py:438
  87.8 4.1 %collective-permute-start.29 = (bf16[64,288]{1,0:T(8,128)(2,1)S(1)}, bf16[64,288]{1,0:T(8,128)(2,1)S(1)}, u32[]{:S(2)}, u32[]{:S(2)}) collective-permute-start(bf16[64,288]{1,0:T(8,128)(2,1)S(1)} %shard_map.131.refs_0_), channel_id=1, source_target_pairs={{0,2},{1,3},{2,0},{3,1},{4,6},{5,7},{6,4},{7,5},{8,10},{9,11},{10,... | collective-permute-start | bytes 110600 | tf_op jit(solution)/shard_map/ppermute | solution.py:438
  88.4 4.1 %collective-permute-start.28 = (bf16[64,288]{1,0:T(8,128)(2,1)S(1)}, bf16[64,288]{1,0:T(8,128)(2,1)S(1)}, u32[]{:S(2)}, u32[]{:S(2)}) collective-permute-start(bf16[64,288]{1,0:T(8,128)(2,1)S(1)} %shard_map.131.refs_0_), channel_id=1, source_target_pairs={{0,1},{1,0},{2,3},{3,2},{4,5},{5,4},{6,7},{7,6},{8,9},{9,8},{10,11... | collective-permute-start | bytes 110600 | tf_op jit(solution)/shard_map/ppermute | solution.py:438
  92.6 1.4 %collective-permute-start.31 = (bf16[64,1152]{1,0:T(8,128)(2,1)S(1)}, bf16[64,1152]{1,0:T(8,128)(2,1)S(1)}, u32[]{:S(2)}, u32[]{:S(2)}) collective-permute-start(bf16[64,1152]{1,0:T(8,128)(2,1)S(1)} %shard_map.132.refs_0_), channel_id=1, source_target_pairs={{0,16},{16,0},{1,17},{17,1},{2,18},{18,2},{3,19},{19,3},{4,20},{20... | collective-permute-start | bytes 442376 | tf_op jit(solution)/shard_map/ppermute | solution.py:438
  (4 other events, 113.6 us)

commit v9 on v8

--- a/solution.py
+++ b/solution.py
@@ -25,7 +25,7 @@
     return pltpu.with_memory_space_constraint(x, pltpu.HBM)
 
 
-def call(kernel, out_shape, *args, scratch=(), hbm=False, limit=48, after=(), carry=()):
+def call(kernel, out_shape, *args, scratch=(), hbm=False, limit=48, after=(), carry=(), stay=False):
     vmem = pl.BlockSpec(memory_space=pltpu.VMEM)
     anywhere = pl.BlockSpec(memory_space=pl.ANY)
     main = anywhere if hbm else vmem
@@ -39,14 +39,14 @@
 
     result = pl.pallas_call(
         body,
-        out_shape=outs + tuple(shape(x.shape, x.dtype) for x in carry),
+        out_shape=outs + tuple((pltpu.HBM if stay else shape)(x.shape, x.dtype) for x in carry),
         in_specs=[main] * used + [anywhere] * extra,
         out_specs=tuple(vmem if isinstance(o, jax.ShapeDtypeStruct) else anywhere for o in outs)
         + (anywhere,) * len(carry),
         scratch_shapes=list(scratch),
         input_output_aliases={used + len(after) + i: len(outs) + i for i in range(len(carry))},
         compiler_params=pltpu.CompilerParams(vmem_limit_bytes=limit * 1024 * 1024),
-    )(*args, *after, *carry)
+    )(*args, *after, *(far(x) if stay else x for x in carry))
     return result[0] if single and not carry else list(result)
 
 
@@ -94,8 +94,9 @@
 
 def pack_kernel(n_s, n_t, sub, *refs):
     ins, time_ins, refs = refs[:7], refs[7:11], refs[11:]
-    outs, time_outs, refs = refs[:n_s], refs[n_s : n_s + n_t - 1], refs[n_s + n_t - 1 :]
-    buffers, (time_buf, turned_ref, sems, time_sems) = refs[:7], refs[7:]
+    outs, sides, refs = refs[:n_s], refs[n_s : 2 * n_s], refs[2 * n_s :]
+    time_outs, buffers, refs = refs[: n_t - 1], refs[n_t - 1 : n_t + 6], refs[n_t + 6 :]
+    time_buf, turned_ref, codes_ref, sems, time_sems, side_sems = refs
     p_buf, at_buf, b_buf, q_buf, v_buf, k_buf, g_buf = buffers
     copies = load_all(ins, buffers, sems)
     time_copies = load_all(time_ins, [time_buf.at[index] for index in range(4)], time_sems)
@@ -110,7 +111,18 @@
         for j in range(n_s):
             turned_ref[index, j] = turned[j * d_s : (j + 1) * d_s]
         for k in range(n_s):
-            outs[k][index * d_s : (index + 1) * d_s] = turned_ref[index, peer("space", k)]
+            source = turned_ref.at[index, peer("space", k)]
+            if index < 3:
+                outs[k][index * d_s : (index + 1) * d_s] = source[...]
+            else:
+                start_copy(source, sides[k].at[(index - 3) * d_s : (index - 2) * d_s])
+
+    sent = []
+
+    def start_copy(source, target):
+        copy = pltpu.make_async_copy(source, target, side_sems.at[len(sent)])
+        copy.start()
+        sent.append(copy)
 
     copies[0].wait()
     copies[1].wait()
@@ -118,7 +130,10 @@
     patches = flat(p_buf)
     codes_q = mm(patches, at_buf[0], NT).astype(BF16)
     codes_v = mm(patches, at_buf[1], NT).astype(BF16)
-    codes_t = jnp.concatenate([codes_q, codes_v], axis=1).T
+    codes_ref[...] = jnp.concatenate([codes_q, codes_v], axis=1).T
+    for k in range(n_s):
+        start_copy(codes_ref, sides[k].at[2 * d_s : 2 * d_s + 2 * RANK])
+    send(patches, 3)
     copies[3].wait()
     query = (flat(q_buf).astype(F32) + mm(codes_q, b_buf[0])).astype(BF16)
     send(query, 0)
@@ -127,11 +142,8 @@
     send(value, 2)
     copies[5].wait()
     send(flat(k_buf), 1)
-    send(patches, 3)
     copies[6].wait()
     send(flat(g_buf), 4)
-    for k in range(n_s):
-        outs[k][5 * d_s :] = codes_t
     for index, copy in enumerate(time_copies):
         copy.wait()
         for k in range(1, n_t):
@@ -140,6 +152,8 @@
                 time_outs[k - 1][index, f * sub : (f + 1) * sub] = time_buf[
                     index, 0, f, pl.ds(start, sub)
                 ]
+    for copy in sent:
+        copy.wait()
 
 
 def frame_rows(pieces, f, patch_dev):
@@ -299,7 +313,7 @@
 
 
 def space_backward_kernel(frames, n_s, qkv_ref, probs_ref, hidden_ref, grad_b_ref, at_ref, at_here_ref, b_here_ref, *refs):
-    packed, dcodes, sends = refs[:n_s], refs[n_s : 2 * n_s], refs[2 * n_s : 3 * n_s]
+    sides, dcodes, sends = refs[:n_s], refs[n_s : 2 * n_s], refs[2 * n_s : 3 * n_s]
     part_ref, cut_buf = refs[3 * n_s :]
     d_s = part_ref.shape[1]
     tokens = hidden_ref.shape[0]
@@ -309,10 +323,10 @@
     ups = jnp.concatenate([at_here_ref[2], at_here_ref[3]], axis=0).T
     grads = []
     for k in range(n_s):
-        cot = packed[k][4 * d_s : 5 * d_s].astype(F32)
+        cot = sides[k][d_s : 2 * d_s].astype(F32)
         grads.append((cot + mm(ups, dcodes[k][...])).astype(BF16))
     grad_b_q = grad_b_v = None
-    codes = [x[5 * d_s :] for x in packed]
+    codes = [x[2 * d_s :] for x in sides]
     for f in range(frames):
         keys = qkv_ref[1, f].astype(F32)
         vals = qkv_ref[2, f].astype(F32)
@@ -366,14 +380,14 @@
 
 
 def merge_kernel(frames, n_s, n_d, part_ref, *refs):
-    packed, recvs, refs = refs[:n_s], refs[n_s : 2 * n_s], refs[2 * n_s :]
+    sides, recvs, refs = refs[:n_s], refs[n_s : 2 * n_s], refs[2 * n_s :]
     sends, buf = refs[:n_d], refs[n_d]
     d_s = part_ref.shape[1]
-    tokens = packed[0].shape[1]
+    tokens = sides[0].shape[1]
     patch_dev = tokens // frames
     total = n_s * patch_dev
     pad = -(-d_s // 128) * 128
-    patches = [x[3 * d_s : 4 * d_s] for x in packed]
+    patches = [x[:d_s] for x in sides]
     terms = []
     for f in range(frames):
         codes = [recv[:, f * total : (f + 1) * total].astype(F32) for recv in recvs]
@@ -471,19 +485,22 @@
     ]
     packed = call(
         functools.partial(pack_kernel, n_s, n_t, sub),
-        [shape((5 * d_s + 2 * RANK, tokens), BF16)] * n_s
+        [shape((3 * d_s, tokens), BF16)] * n_s
+        + [pltpu.HBM((2 * d_s + 2 * RANK, tokens), BF16)] * n_s
         + [shape((4, frames * sub, width), BF16)] * (n_t - 1),
         *space_arrays, *time_arrays,
         scratch=[pltpu.VMEM(x.shape, BF16) for x in space_arrays]
         + [
             pltpu.VMEM((4,) + query_t.shape, BF16),
             pltpu.VMEM((5, n_s, d_s, tokens), BF16),
+            pltpu.VMEM((2 * RANK, tokens), BF16),
             dma((7,)),
             dma((4,)),
+            dma((3 * n_s,)),
         ],
         hbm=True,
     )
-    time_pieces = hops(packed[n_s:], "tm", 1)
+    sides, time_pieces = packed[n_s : 2 * n_s], hops(packed[2 * n_s :], "tm", 1)
     packed = exchange(packed[:n_s], "space")
     probs_dims = (frames, d_s // HEAD_DIM, total, total)
     qkv, probs, *out_s = call(
@@ -520,8 +537,11 @@
         + [shape((8, 128), F32)] * n_t
         + [shape((2 * RANK, width), F32)],
         turned, adapters_b, *codes,
+        carry=sides[1:],
+        stay=True,
     )
     out_t, dcodes, time_grad_b = timed[:n_t], timed[n_t : 2 * n_t], timed[2 * n_t]
+    sides[1:] = hops(timed[2 * n_t + 1 :], "space", 1)
     dcodes = exchange(dcodes, "tm")
     out_t[1:2] = hops(out_t[1:2], "tm", 1)
     dcodes = call(
@@ -534,7 +554,7 @@
     backward = call(
         functools.partial(space_backward_kernel, frames, n_s),
         [shape((2 * RANK, frames * total + 2 * pad), BF16)] * n_s + [shape((2 * RANK, d_s), F32)],
-        qkv, probs, hidden, time_grad_b, downs, downs_here, ups_here, *packed, *dcodes,
+        qkv, probs, hidden, time_grad_b, downs, downs_here, ups_here, *sides, *dcodes,
         scratch=[pltpu.VMEM((n_s, 2, 2 * RANK, pad), BF16)],
         after=out_t[1:2],
         carry=out_t[2:],
@@ -546,7 +566,7 @@
     sums = call(
         functools.partial(merge_kernel, frames, n_s, n_d),
         [shape((rows, d_s), F32)] * n_d,
-        part, *packed, *partial,
+        part, *sides, *partial,
         scratch=[pltpu.VMEM((n_d, rows, d_s), F32)],
     )
     sums = call(total_kernel, shape((rows, d_s), BF16), *exchange(sums, "dp"), after=out_t[2:])

time: 95.1 us -> 100 us (1.052)
  waiting for transfers between devices: 32.3 us -> 25.9 us
  starting transfers between devices: 42.3 us -> 48.4 us
  local copies, waits for them, and re-layouts: 0.19 us -> 5.64 us
    ppermute x32 -> x35, waiting for transfers between devices: 32.3 us -> 25.9 us  [hops(): lax.ppermute(array, axis, [(i, i ^ k) for i in range(size)])]
    ppermute x32 -> x35, starting transfers between devices: 42.3 us -> 48.4 us  [hops(): lax.ppermute(array, axis, [(i, i ^ k) for i in range(size)])]
    unnamed x8 -> x20, local copies, waits for them, and re-layouts: 0.02 us -> 4.64 us
  transfers between devices with their start and end apart: 32 -> 35, of which waited for: 18 -> 17; matrix products, arithmetic and copies ran while one was open for 0% -> 1% of each run, Pallas kernels for 7% -> 6%
where the time goes in v9:
time: 100 us
  starting transfers between devices  48.4 us (48%)
  waiting for transfers between devices  25.9 us (26%)
  Pallas kernels  19.3 us (19%)
  local copies, waits for them, and re-layouts  5.64 us (6%)
    ppermute x35, starting transfers between devices, hops(): lax.ppermute(array, axis, [(i, i ^ k) for i in range(size)])  48.4 us
    ppermute x35, waiting for transfers between devices, hops(): lax.ppermute(array, axis, [(i, i ^ k) for i in range(size)])  25.9 us
    pallas_call x13, Pallas kernels, call(): pl.pallas_call(body, out_shape=outs + tuple(((pltpu.HBM if stay else shap...  19.3 us
    unnamed x20, local copies, waits for them, and re-layouts  4.64 us
  transfers between devices with their start and end apart: 35, of which 17 were waited for; matrix products, arithmetic and copies ran while one was open for 1% of the time, Pallas kernels for 6%

profile of v9, /device:TPU:0, one launch (start us, length us, event | category | flops | bytes accessed | tf_op | source)
XLA Modules:
  0.0 100.1 jit_solution(9058986235861669070)
XLA Ops:
  0.7 3.4 %shard_map.121 = (bf16[864,128]{1,0:T(8,128)(2,1)S(1)}, bf16[864,128]{1,0:T(8,128)(2,1)S(1)}, bf16[864,128]{1,0:T(8,128)(2,1)S(1)}, bf16[864,128]{1,0:T(8,128)(2...) custom-call(bf16[1,2,64,1152]{3,2,1,0:T(8,128)(2,1)} %refs_4_.3, ...), custom_call_target="tpu_custom_call" | custom-call | tf_op jit(solution)/shard_map/pallas_call | solution.py:40
  4.1 3.0 %collective-permute-start = (bf16[864,128]{1,0:T(8,128)(2,1)S(1)}, bf16[864,128]{1,0:T(8,128)(2,1)S(1)}, u32[]{:S(2)}, u32[]{:S(2)}) collective-permute-start(bf16[864,128]{1,0:T(8,128)(2,1)S(1)} %get-tuple-element.49), channel_id=1, source_target_pairs={{0,1},{1,0},{2,3},{3,2},{4,5},{5,4},{6,7},{7,6},{8,9},{9,8},{10,11... | collective-permute-start | bytes 663560 | tf_op jit(solution)/shard_map/ppermute | solution.py:452
  7.1 1.6 %collective-permute-start.3 = (bf16[4,32,1152]{2,1,0:T(8,128)(2,1)S(1)}, bf16[4,32,1152]{2,1,0:T(8,128)(2,1)S(1)}, u32[]{:S(2)}, u32[]{:S(2)}) collective-permute-start(bf16[4,32,1152]{2,1,0:T(8,128)(2,1)S(1)} %get-tuple-element.52), channel_id=1, source_target_pairs={{0,4},{4,0},{8,12},{12,8},{1,5},{5,1},{9,13},{13,9},{2,6},{6,2},{1... | collective-permute-start | bytes 884744 | tf_op jit(solution)/shard_map/ppermute | solution.py:452
  8.7 1.6 %collective-permute-start.1 = (bf16[864,128]{1,0:T(8,128)(2,1)S(1)}, bf16[864,128]{1,0:T(8,128)(2,1)S(1)}, u32[]{:S(2)}, u32[]{:S(2)}) collective-permute-start(bf16[864,128]{1,0:T(8,128)(2,1)S(1)} %get-tuple-element.50), channel_id=1, source_target_pairs={{0,2},{1,3},{2,0},{3,1},{4,6},{5,7},{6,4},{7,5},{8,10},{9,11},{10,... | collective-permute-start | bytes 663560 | tf_op jit(solution)/shard_map/ppermute | solution.py:452
  10.7 2.6 %collective-permute-start.7 = (bf16[4,32,1152]{2,1,0:T(8,128)(2,1)S(1)}, bf16[4,32,1152]{2,1,0:T(8,128)(2,1)S(1)}, u32[]{:S(2)}, u32[]{:S(2)}) collective-permute-start(bf16[4,32,1152]{2,1,0:T(8,128)(2,1)S(1)} %get-tuple-element.58), channel_id=1, source_target_pairs={{0,8},{4,12},{8,0},{12,4},{1,9},{5,13},{9,1},{13,5},{2,10},{6,14},... | collective-permute-start | bytes 884744 | tf_op jit(solution)/shard_map/ppermute | solution.py:452
  13.3 4.3 %collective-permute-start.8 = (bf16[4,32,1152]{2,1,0:T(8,128)(2,1)S(1)}, bf16[4,32,1152]{2,1,0:T(8,128)(2,1)S(1)}, u32[]{:S(2)}, u32[]{:S(2)}) collective-permute-start(bf16[4,32,1152]{2,1,0:T(8,128)(2,1)S(1)} %get-tuple-element.59), channel_id=1, source_target_pairs={{0,12},{4,8},{8,4},{12,0},{1,13},{5,9},{9,5},{13,1},{2,14},{6,10},... | collective-permute-start | bytes 884744 | tf_op jit(solution)/shard_map/ppermute | solution.py:452
  17.5 2.5 %collective-permute-done.1.refs_2_ = bf16[864,128]{1,0:T(8,128)(2,1)S(1)} collective-permute-done((bf16[864,128]{1,0:T(8,128)(2,1)S(1)}, bf16[864,128]{1,0:T(8,128)(2,1)S(1)}, u32[]{:S(2)}, u32[]{:S(2)}) %collective-permute-start.1) | collective-permute-done | bytes 221216 | tf_op jit(solution)/shard_map/ppermute | solution.py:452
  20.0 3.5 %shard_map.122 = (bf16[3,2,288,256]{3,2,1,0:T(8,128)(2,1)S(1)}, f32[2,4,256,256]{3,2,1,0:T(8,128)}, bf16[288,128]{1,0:T(8,128)(2,1)S(1)}, bf16[288,128]{1,0:T(8,...) custom-call(bf16[864,128]{1,0:T(8,128)(2,1)S(1)} %get-tuple-element.48.refs_0_, ...), custom_call_target="tpu_custom_call" | custom-call | tf_op jit(solution)/shard_map/pallas_call | solution.py:40
  24.1 1.5 %collective-permute-start.5 = (bf16[288,128]{1,0:T(8,128)(2,1)S(1)}, bf16[288,128]{1,0:T(8,128)(2,1)S(1)}, u32[]{:S(2)}, u32[]{:S(2)}) collective-permute-start(bf16[288,128]{1,0:T(8,128)(2,1)S(1)} %get-tuple-element.55), channel_id=1, source_target_pairs={{0,2},{1,3},{2,0},{3,1},{4,6},{5,7},{6,4},{7,5},{8,10},{9,11},{10,... | collective-permute-start | bytes 221192 | tf_op jit(solution)/shard_map/ppermute | solution.py:452
  25.6 1.4 %collective-permute-start.6 = (bf16[288,128]{1,0:T(8,128)(2,1)S(1)}, bf16[288,128]{1,0:T(8,128)(2,1)S(1)}, u32[]{:S(2)}, u32[]{:S(2)}) collective-permute-start(bf16[288,128]{1,0:T(8,128)(2,1)S(1)} %get-tuple-element.56), channel_id=1, source_target_pairs={{0,3},{1,2},{2,1},{3,0},{4,7},{5,6},{6,5},{7,4},{8,11},{9,10},{10,... | collective-permute-start | bytes 221192 | tf_op jit(solution)/shard_map/ppermute | solution.py:452
  28.6 2.2 %collective-permute-done.6.refs_3_ = bf16[288,128]{1,0:T(8,128)(2,1)S(1)} collective-permute-done((bf16[288,128]{1,0:T(8,128)(2,1)S(1)}, bf16[288,128]{1,0:T(8,128)(2,1)S(1)}, u32[]{:S(2)}, u32[]{:S(2)}) %collective-permute-start.6) | collective-permute-done | bytes 73760 | tf_op jit(solution)/shard_map/ppermute | solution.py:452
  31.7 2.6 %collective-permute-start.10 = (f32[8,128]{1,0:T(8,128)S(1)}, f32[8,128]{1,0:T(8,128)S(1)}, u32[]{:S(2)}, u32[]{:S(2)}) collective-permute-start(f32[8,128]{1,0:T(8,128)S(1)} %get-tuple-element.62), channel_id=1, source_target_pairs={{0,8},{4,12},{8,0},{12,4},{1,9},{5,13},{9,1},{13,5},{2,10},{6,14},... | collective-permute-start | bytes 12296 | tf_op jit(solution)/shard_map/ppermute | solution.py:452
  34.3 1.3 %collective-permute-start.11 = (f32[8,128]{1,0:T(8,128)S(1)}, f32[8,128]{1,0:T(8,128)S(1)}, u32[]{:S(2)}, u32[]{:S(2)}) collective-permute-start(f32[8,128]{1,0:T(8,128)S(1)} %get-tuple-element.63), channel_id=1, source_target_pairs={{0,12},{4,8},{8,4},{12,0},{1,13},{5,9},{9,5},{13,1},{2,14},{6,10},... | collective-permute-start | bytes 12296 | tf_op jit(solution)/shard_map/ppermute | solution.py:452
  35.7 1.4 %shard_map.124.refs_0_ = bf16[4,1152,128]{2,1,0:T(8,128)(2,1)S(1)} custom-call(bf16[1,2,64,1152]{3,2,1,0:T(8,128)(2,1)} %refs_0_.3, bf16[1,2,64,1152]{3,2,1,0:T(8,128)(2,1)} %refs_1_.2, bf16[1,2,64,1152]{3,2,1,0:T(8,128)(2,1)} %refs_2_.3, bf16[1,2,64,1152]{3,2,1,0:T(8,128)(2,1)} %refs_3_.3, bf16[4,32,1152]{2,1,0:T(8,128)(2,1)S(1)} %collective-permute-done.3.refs_4_, ...), custom_call_target="tpu_custom_call" | custom-call | tf_op jit(solution)/shard_map/pallas_call | solution.py:40
  37.0 1.4 %collective-permute-done.10.refs_4_ = f32[8,128]{1,0:T(8,128)S(1)} collective-permute-done((f32[8,128]{1,0:T(8,128)S(1)}, f32[8,128]{1,0:T(8,128)S(1)}, u32[]{:S(2)}, u32[]{:S(2)}) %collective-permute-start.10) | collective-permute-done | bytes 4128 | tf_op jit(solution)/shard_map/ppermute | solution.py:452
  38.5 1.3 %collective-permute-done.11.refs_5_ = f32[8,128]{1,0:T(8,128)S(1)} collective-permute-done((f32[8,128]{1,0:T(8,128)S(1)}, f32[8,128]{1,0:T(8,128)S(1)}, u32[]{:S(2)}, u32[]{:S(2)}) %collective-permute-start.11) | collective-permute-done | bytes 4128 | tf_op jit(solution)/shard_map/ppermute | solution.py:452
  39.7 5.5 %shard_map.125 = (bf16[32,1152]{1,0:T(8,128)(2,1)S(1)}, bf16[32,1152]{1,0:T(8,128)(2,1)S(1)}, bf16[32,1152]{1,0:T(8,128)(2,1)}, bf16[32,1152]{1,0:T(8,128)(2,1)S...) custom-call(bf16[4,1152,128]{2,1,0:T(8,128)(2,1)S(1)} %shard_map.124, ...), custom_call_target="tpu_custom_call", output_to_operand_aliasing={{9}: (6, {}), {10}: (7, {}), {11}: (8, {})} | custom-call | tf_op jit(solution)/shard_map/pallas_call | solution.py:40
  49.1 2.5 %collective-permute-start.18 = (f32[8,128]{1,0:T(8,128)S(1)}, f32[8,128]{1,0:T(8,128)S(1)}, u32[]{:S(2)}, u32[]{:S(2)}) collective-permute-start(f32[8,128]{1,0:T(8,128)S(1)} %get-tuple-element.79), channel_id=1, source_target_pairs={{0,12},{4,8},{8,4},{12,0},{1,13},{5,9},{9,5},{13,1},{2,14},{6,10},... | collective-permute-start | bytes 12296 | tf_op jit(solution)/shard_map/ppermute | solution.py:452
  51.6 1.9 %collective-permute-start.13 = (bf16[608,128]{1,0:T(8,128)(2,1)}, bf16[608,128]{1,0:T(8,128)(2,1)S(1)}, u32[]{:S(2)}, u32[]{:S(2)}) collective-permute-start(bf16[608,128]{1,0:T(8,128)(2,1)} %get-tuple-element.73), channel_id=1, source_target_pairs={{0,1},{1,0},{2,3},{3,2},{4,5},{5,4},{6,7},{7,6},{8,9},{9,8},{10,11... | collective-permute-start | bytes 466952 | tf_op jit(solution)/shard_map/ppermute | solution.py:452
  55.2 1.9 %collective-permute-start.19 = (bf16[32,128]{1,0:T(8,128)(2,1)S(1)}, bf16[32,128]{1,0:T(8,128)(2,1)S(1)}, u32[]{:S(2)}, u32[]{:S(2)}) collective-permute-start(bf16[32,128]{1,0:T(8,128)(2,1)S(1)} %shard_map.126.refs_11_), channel_id=1, source_target_pairs={{0,1},{1,0},{2,3},{3,2},{4,5},{5,4},{6,7},{7,6},{8,9},{9,8},{10,11... | collective-permute-start | bytes 24584 | tf_op jit(solution)/shard_map/ppermute | solution.py:452
  57.7 2.8 %collective-permute-done.19.refs_12_ = bf16[32,128]{1,0:T(8,128)(2,1)S(1)} collective-permute-done((bf16[32,128]{1,0:T(8,128)(2,1)S(1)}, bf16[32,128]{1,0:T(8,128)(2,1)S(1)}, u32[]{:S(2)}, u32[]{:S(2)}) %collective-permute-start.19) | collective-permute-done | bytes 8224 | tf_op jit(solution)/shard_map/ppermute | solution.py:452
  62.6 2.8 %collective-permute-done.21.refs_14_ = bf16[32,128]{1,0:T(8,128)(2,1)S(1)} collective-permute-done((bf16[32,128]{1,0:T(8,128)(2,1)S(1)}, bf16[32,128]{1,0:T(8,128)(2,1)S(1)}, u32[]{:S(2)}, u32[]{:S(2)}) %collective-permute-start.21) | collective-permute-done | bytes 8224 | tf_op jit(solution)/shard_map/ppermute | solution.py:452
  68.1 2.9 %shard_map.127 = (bf16[32,1280]{1,0:T(8,128)(2,1)S(1)}, bf16[32,1280]{1,0:T(8,128)(2,1)S(1)}, bf16[32,1280]{1,0:T(8,128)(2,1)S(1)}, bf16[32,1280]{1,0:T(8,128)(2...) custom-call(bf16[3,2,288,256]{3,2,1,0:T(8,128)(2,1)S(1)} %get-tuple-, ...), custom_call_target="tpu_custom_call", output_to_operand_aliasing={{5}: (16, {}), {6}: (17, {})} | custom-call | tf_op jit(solution)/shard_map/pallas_call | solution.py:40
  72.4 2.1 %collective-permute-start.26 = (bf16[32,1280]{1,0:T(8,128)(2,1)S(1)}, bf16[32,1280]{1,0:T(8,128)(2,1)S(1)}, u32[]{:S(2)}, u32[]{:S(2)}) collective-permute-start(bf16[32,1280]{1,0:T(8,128)(2,1)S(1)} %get-tuple-element.88), channel_id=1, source_target_pairs={{0,3},{1,2},{2,1},{3,0},{4,7},{5,6},{6,5},{7,4},{8,11},{9,10},{10,... | collective-permute-start | bytes 245768 | tf_op jit(solution)/shard_map/ppermute | solution.py:452
  74.5 1.3 %collective-permute-start.22 = (bf16[32,1152]{1,0:T(8,128)(2,1)}, bf16[32,1152]{1,0:T(8,128)(2,1)S(1)}, u32[]{:S(2)}, u32[]{:S(2)}) collective-permute-start(bf16[32,1152]{1,0:T(8,128)(2,1)} %get-tuple-element.82), channel_id=1, source_target_pairs={{0,8},{4,12},{8,0},{12,4},{1,9},{5,13},{9,1},{13,5},{2,10},{6,14},... | collective-permute-start | bytes 221192 | tf_op jit(solution)/shard_map/ppermute | solution.py:452
  75.8 2.9 %collective-permute-start.23 = (bf16[32,1152]{1,0:T(8,128)(2,1)S(1)}, bf16[32,1152]{1,0:T(8,128)(2,1)S(1)}, u32[]{:S(2)}, u32[]{:S(2)}) collective-permute-start(bf16[32,1152]{1,0:T(8,128)(2,1)S(1)} %get-tuple-element.83), channel_id=1, source_target_pairs={{0,12},{4,8},{8,4},{12,0},{1,13},{5,9},{9,5},{13,1},{2,14},{6,10},... | collective-permute-start | bytes 221192 | tf_op jit(solution)/shard_map/ppermute | solution.py:452
  80.0 2.1 %collective-permute-done.23.refs_4_.refs_3_ = bf16[32,1152]{1,0:T(8,128)(2,1)S(1)} collective-permute-done((bf16[32,1152]{1,0:T(8,128)(2,1)S(1)}, bf16[32,1152]{1,0:T(8,128)(2,1)S(1)}, u32[]{:S(2)}, u32[]{:S(2)}) %collective-permute-start.23) | collective-permute-done | bytes 73760 | tf_op jit(solution)/shard_map/ppermute | solution.py:452
  83.0 2.5 %collective-permute-start.29 = (bf16[64,288]{1,0:T(8,128)(2,1)S(1)}, bf16[64,288]{1,0:T(8,128)(2,1)S(1)}, u32[]{:S(2)}, u32[]{:S(2)}) collective-permute-start(bf16[64,288]{1,0:T(8,128)(2,1)S(1)} %shard_map.130.refs_0_), channel_id=1, source_target_pairs={{0,8},{4,12},{8,0},{12,4},{1,9},{5,13},{9,1},{13,5},{2,10},{6,14},... | collective-permute-start | bytes 110600 | tf_op jit(solution)/shard_map/ppermute | solution.py:452
  86.6 1.4 %collective-permute-done.29.refs_2_ = bf16[64,288]{1,0:T(8,128)(2,1)S(1)} collective-permute-done((bf16[64,288]{1,0:T(8,128)(2,1)S(1)}, bf16[64,288]{1,0:T(8,128)(2,1)S(1)}, u32[]{:S(2)}, u32[]{:S(2)}) %collective-permute-start.29) | collective-permute-done | bytes 36896 | tf_op jit(solution)/shard_map/ppermute | solution.py:452
  88.0 3.4 %collective-permute-done.30.refs_3_ = bf16[64,288]{1,0:T(8,128)(2,1)S(1)} collective-permute-done((bf16[64,288]{1,0:T(8,128)(2,1)S(1)}, bf16[64,288]{1,0:T(8,128)(2,1)S(1)}, u32[]{:S(2)}, u32[]{:S(2)}) %collective-permute-start.30) | collective-permute-done | bytes 36896 | tf_op jit(solution)/shard_map/ppermute | solution.py:452
  92.7 2.3 %collective-permute-start.33 = (bf16[64,288]{1,0:T(8,128)(2,1)S(1)}, bf16[64,288]{1,0:T(8,128)(2,1)S(1)}, u32[]{:S(2)}, u32[]{:S(2)}) collective-permute-start(bf16[64,288]{1,0:T(8,128)(2,1)S(1)} %shard_map.131.refs_0_), channel_id=1, source_target_pairs={{0,3},{1,2},{2,1},{3,0},{4,7},{5,6},{6,5},{7,4},{8,11},{9,10},{10,... | collective-permute-start | bytes 110600 | tf_op jit(solution)/shard_map/ppermute | solution.py:452
  95.8 1.9 %collective-permute-done.33.refs_3_ = bf16[64,288]{1,0:T(8,128)(2,1)S(1)} collective-permute-done((bf16[64,288]{1,0:T(8,128)(2,1)S(1)}, bf16[64,288]{1,0:T(8,128)(2,1)S(1)}, u32[]{:S(2)}, u32[]{:S(2)}) %collective-permute-start.33) | collective-permute-done | bytes 36896 | tf_op jit(solution)/shard_map/ppermute | solution.py:452
  (73 shorter events, 23.7 us)
Async XLA Ops:
  4.1 9.2 %collective-permute-start = (bf16[864,128]{1,0:T(8,128)(2,1)S(1)}, bf16[864,128]{1,0:T(8,128)(2,1)S(1)}, u32[]{:S(2)}, u32[]{:S(2)}) collective-permute-start(bf16[864,128]{1,0:T(8,128)(2,1)S(1)} %get-tuple-element.49), channel_id=1, source_target_pairs={{0,1},{1,0},{2,3},{3,2},{4,5},{5,4},{6,7},{7,6},{8,9},{9,8},{10,11... | collective-permute-start | bytes 663560 | tf_op jit(solution)/shard_map/ppermute | solution.py:452
  7.1 12.9 %collective-permute-start.3 = (bf16[4,32,1152]{2,1,0:T(8,128)(2,1)S(1)}, bf16[4,32,1152]{2,1,0:T(8,128)(2,1)S(1)}, u32[]{:S(2)}, u32[]{:S(2)}) collective-permute-start(bf16[4,32,1152]{2,1,0:T(8,128)(2,1)S(1)} %get-tuple-element.52), channel_id=1, source_target_pairs={{0,4},{4,0},{8,12},{12,8},{1,5},{5,1},{9,13},{13,9},{2,6},{6,2},{1... | collective-permute-start | bytes 884744 | tf_op jit(solution)/shard_map/ppermute | solution.py:452
  8.7 11.3 %collective-permute-start.1 = (bf16[864,128]{1,0:T(8,128)(2,1)S(1)}, bf16[864,128]{1,0:T(8,128)(2,1)S(1)}, u32[]{:S(2)}, u32[]{:S(2)}) collective-permute-start(bf16[864,128]{1,0:T(8,128)(2,1)S(1)} %get-tuple-element.50), channel_id=1, source_target_pairs={{0,2},{1,3},{2,0},{3,1},{4,6},{5,7},{6,4},{7,5},{8,10},{9,11},{10,... | collective-permute-start | bytes 663560 | tf_op jit(solution)/shard_map/ppermute | solution.py:452
  10.2 9.8 %collective-permute-start.2 = (bf16[864,128]{1,0:T(8,128)(2,1)S(1)}, bf16[864,128]{1,0:T(8,128)(2,1)S(1)}, u32[]{:S(2)}, u32[]{:S(2)}) collective-permute-start(bf16[864,128]{1,0:T(8,128)(2,1)S(1)} %get-tuple-element.51), channel_id=1, source_target_pairs={{0,3},{1,2},{2,1},{3,0},{4,7},{5,6},{6,5},{7,4},{8,11},{9,10},{10,... | collective-permute-start | bytes 663560 | tf_op jit(solution)/shard_map/ppermute | solution.py:452
  10.7 25.0 %collective-permute-start.7 = (bf16[4,32,1152]{2,1,0:T(8,128)(2,1)S(1)}, bf16[4,32,1152]{2,1,0:T(8,128)(2,1)S(1)}, u32[]{:S(2)}, u32[]{:S(2)}) collective-permute-start(bf16[4,32,1152]{2,1,0:T(8,128)(2,1)S(1)} %get-tuple-element.58), channel_id=1, source_target_pairs={{0,8},{4,12},{8,0},{12,4},{1,9},{5,13},{9,1},{13,5},{2,10},{6,14},... | collective-permute-start | bytes 884744 | tf_op jit(solution)/shard_map/ppermute | solution.py:452
  13.3 22.4 %collective-permute-start.8 = (bf16[4,32,1152]{2,1,0:T(8,128)(2,1)S(1)}, bf16[4,32,1152]{2,1,0:T(8,128)(2,1)S(1)}, u32[]{:S(2)}, u32[]{:S(2)}) collective-permute-start(bf16[4,32,1152]{2,1,0:T(8,128)(2,1)S(1)} %get-tuple-element.59), channel_id=1, source_target_pairs={{0,12},{4,8},{8,4},{12,0},{1,13},{5,9},{9,5},{13,1},{2,14},{6,10},... | collective-permute-start | bytes 884744 | tf_op jit(solution)/shard_map/ppermute | solution.py:452
  23.5 4.4 %collective-permute-start.4 = (bf16[288,128]{1,0:T(8,128)(2,1)S(1)}, bf16[288,128]{1,0:T(8,128)(2,1)S(1)}, u32[]{:S(2)}, u32[]{:S(2)}) collective-permute-start(bf16[288,128]{1,0:T(8,128)(2,1)S(1)} %get-tuple-element.54), channel_id=1, source_target_pairs={{0,1},{1,0},{2,3},{3,2},{4,5},{5,4},{6,7},{7,6},{8,9},{9,8},{10,11... | collective-permute-start | bytes 221192 | tf_op jit(solution)/shard_map/ppermute | solution.py:452
  24.1 4.5 %collective-permute-start.5 = (bf16[288,128]{1,0:T(8,128)(2,1)S(1)}, bf16[288,128]{1,0:T(8,128)(2,1)S(1)}, u32[]{:S(2)}, u32[]{:S(2)}) collective-permute-start(bf16[288,128]{1,0:T(8,128)(2,1)S(1)} %get-tuple-element.55), channel_id=1, source_target_pairs={{0,2},{1,3},{2,0},{3,1},{4,6},{5,7},{6,4},{7,5},{8,10},{9,11},{10,... | collective-permute-start | bytes 221192 | tf_op jit(solution)/shard_map/ppermute | solution.py:452
  25.6 5.3 %collective-permute-start.6 = (bf16[288,128]{1,0:T(8,128)(2,1)S(1)}, bf16[288,128]{1,0:T(8,128)(2,1)S(1)}, u32[]{:S(2)}, u32[]{:S(2)}) collective-permute-start(bf16[288,128]{1,0:T(8,128)(2,1)S(1)} %get-tuple-element.56), channel_id=1, source_target_pairs={{0,3},{1,2},{2,1},{3,0},{4,7},{5,6},{6,5},{7,4},{8,11},{9,10},{10,... | collective-permute-start | bytes 221192 | tf_op jit(solution)/shard_map/ppermute | solution.py:452
  31.2 5.8 %collective-permute-start.9 = (f32[8,128]{1,0:T(8,128)S(1)}, f32[8,128]{1,0:T(8,128)S(1)}, u32[]{:S(2)}, u32[]{:S(2)}) collective-permute-start(f32[8,128]{1,0:T(8,128)S(1)} %get-tuple-element.61), channel_id=1, source_target_pairs={{0,4},{4,0},{8,12},{12,8},{1,5},{5,1},{9,13},{13,9},{2,6},{6,2},{1... | collective-permute-start | bytes 12296 | tf_op jit(solution)/shard_map/ppermute | solution.py:452
  31.7 6.7 %collective-permute-start.10 = (f32[8,128]{1,0:T(8,128)S(1)}, f32[8,128]{1,0:T(8,128)S(1)}, u32[]{:S(2)}, u32[]{:S(2)}) collective-permute-start(f32[8,128]{1,0:T(8,128)S(1)} %get-tuple-element.62), channel_id=1, source_target_pairs={{0,8},{4,12},{8,0},{12,4},{1,9},{5,13},{9,1},{13,5},{2,10},{6,14},... | collective-permute-start | bytes 12296 | tf_op jit(solution)/shard_map/ppermute | solution.py:452
  34.3 5.4 %collective-permute-start.11 = (f32[8,128]{1,0:T(8,128)S(1)}, f32[8,128]{1,0:T(8,128)S(1)}, u32[]{:S(2)}, u32[]{:S(2)}) collective-permute-start(f32[8,128]{1,0:T(8,128)S(1)} %get-tuple-element.63), channel_id=1, source_target_pairs={{0,12},{4,8},{8,4},{12,0},{1,13},{5,9},{9,5},{13,1},{2,14},{6,10},... | collective-permute-start | bytes 12296 | tf_op jit(solution)/shard_map/ppermute | solution.py:452
  47.2 6.7 %collective-permute-start.16 = (f32[8,128]{1,0:T(8,128)S(1)}, f32[8,128]{1,0:T(8,128)S(1)}, u32[]{:S(2)}, u32[]{:S(2)}) collective-permute-start(f32[8,128]{1,0:T(8,128)S(1)} %get-tuple-element.77), channel_id=1, source_target_pairs={{0,4},{4,0},{8,12},{12,8},{1,5},{5,1},{9,13},{13,9},{2,6},{6,2},{1... | collective-permute-start | bytes 12296 | tf_op jit(solution)/shard_map/ppermute | solution.py:452
  47.8 7.2 %collective-permute-start.17 = (f32[8,128]{1,0:T(8,128)S(1)}, f32[8,128]{1,0:T(8,128)S(1)}, u32[]{:S(2)}, u32[]{:S(2)}) collective-permute-start(f32[8,128]{1,0:T(8,128)S(1)} %get-tuple-element.78), channel_id=1, source_target_pairs={{0,8},{4,12},{8,0},{12,4},{1,9},{5,13},{9,1},{13,5},{2,10},{6,14},... | collective-permute-start | bytes 12296 | tf_op jit(solution)/shard_map/ppermute | solution.py:452
  49.1 6.0 %collective-permute-start.18 = (f32[8,128]{1,0:T(8,128)S(1)}, f32[8,128]{1,0:T(8,128)S(1)}, u32[]{:S(2)}, u32[]{:S(2)}) collective-permute-start(f32[8,128]{1,0:T(8,128)S(1)} %get-tuple-element.79), channel_id=1, source_target_pairs={{0,12},{4,8},{8,4},{12,0},{1,13},{5,9},{9,5},{13,1},{2,14},{6,10},... | collective-permute-start | bytes 12296 | tf_op jit(solution)/shard_map/ppermute | solution.py:452
  51.6 13.8 %collective-permute-start.13 = (bf16[608,128]{1,0:T(8,128)(2,1)}, bf16[608,128]{1,0:T(8,128)(2,1)S(1)}, u32[]{:S(2)}, u32[]{:S(2)}) collective-permute-start(bf16[608,128]{1,0:T(8,128)(2,1)} %get-tuple-element.73), channel_id=1, source_target_pairs={{0,1},{1,0},{2,3},{3,2},{4,5},{5,4},{6,7},{7,6},{8,9},{9,8},{10,11... | collective-permute-start | bytes 466952 | tf_op jit(solution)/shard_map/ppermute | solution.py:452
  53.5 11.9 %collective-permute-start.14 = (bf16[608,128]{1,0:T(8,128)(2,1)}, bf16[608,128]{1,0:T(8,128)(2,1)S(1)}, u32[]{:S(2)}, u32[]{:S(2)}) collective-permute-start(bf16[608,128]{1,0:T(8,128)(2,1)} %get-tuple-element.74), channel_id=1, source_target_pairs={{0,2},{1,3},{2,0},{3,1},{4,6},{5,7},{6,4},{7,5},{8,10},{9,11},{10,... | collective-permute-start | bytes 466952 | tf_op jit(solution)/shard_map/ppermute | solution.py:452
  53.9 11.5 %collective-permute-start.15 = (bf16[608,128]{1,0:T(8,128)(2,1)}, bf16[608,128]{1,0:T(8,128)(2,1)S(1)}, u32[]{:S(2)}, u32[]{:S(2)}) collective-permute-start(bf16[608,128]{1,0:T(8,128)(2,1)} %get-tuple-element.75), channel_id=1, source_target_pairs={{0,3},{1,2},{2,1},{3,0},{4,7},{5,6},{6,5},{7,4},{8,11},{9,10},{10,... | collective-permute-start | bytes 466952 | tf_op jit(solution)/shard_map/ppermute | solution.py:452
  55.2 5.3 %collective-permute-start.19 = (bf16[32,128]{1,0:T(8,128)(2,1)S(1)}, bf16[32,128]{1,0:T(8,128)(2,1)S(1)}, u32[]{:S(2)}, u32[]{:S(2)}) collective-permute-start(bf16[32,128]{1,0:T(8,128)(2,1)S(1)} %shard_map.126.refs_11_), channel_id=1, source_target_pairs={{0,1},{1,0},{2,3},{3,2},{4,5},{5,4},{6,7},{7,6},{8,9},{9,8},{10,11... | collective-permute-start | bytes 24584 | tf_op jit(solution)/shard_map/ppermute | solution.py:452
  60.5 4.8 %collective-permute-start.12 = (bf16[32,1152]{1,0:T(8,128)(2,1)}, bf16[32,1152]{1,0:T(8,128)(2,1)S(1)}, u32[]{:S(2)}, u32[]{:S(2)}) collective-permute-start(bf16[32,1152]{1,0:T(8,128)(2,1)} %copy-done.9), channel_id=1, source_target_pairs={{0,4},{4,0},{8,12},{12,8},{1,5},{5,1},{9,13},{13,9},{2,6},{6,2},{1... | collective-permute-start | bytes 221192 | tf_op jit(solution)/shard_map/ppermute | solution.py:452
  60.8 4.5 %collective-permute-start.21 = (bf16[32,128]{1,0:T(8,128)(2,1)S(1)}, bf16[32,128]{1,0:T(8,128)(2,1)S(1)}, u32[]{:S(2)}, u32[]{:S(2)}) collective-permute-start(bf16[32,128]{1,0:T(8,128)(2,1)S(1)} %shard_map.126.refs_11_), channel_id=1, source_target_pairs={{0,3},{1,2},{2,1},{3,0},{4,7},{5,6},{6,5},{7,4},{8,11},{9,10},{10,... | collective-permute-start | bytes 24584 | tf_op jit(solution)/shard_map/ppermute | solution.py:452
  70.9 7.7 %collective-permute-start.24 = (bf16[32,1280]{1,0:T(8,128)(2,1)S(1)}, bf16[32,1280]{1,0:T(8,128)(2,1)S(1)}, u32[]{:S(2)}, u32[]{:S(2)}) collective-permute-start(bf16[32,1280]{1,0:T(8,128)(2,1)S(1)} %get-tuple-element.86), channel_id=1, source_target_pairs={{0,1},{1,0},{2,3},{3,2},{4,5},{5,4},{6,7},{7,6},{8,9},{9,8},{10,11... | collective-permute-start | bytes 245768 | tf_op jit(solution)/shard_map/ppermute | solution.py:452
  71.4 7.2 %collective-permute-start.25 = (bf16[32,1280]{1,0:T(8,128)(2,1)S(1)}, bf16[32,1280]{1,0:T(8,128)(2,1)S(1)}, u32[]{:S(2)}, u32[]{:S(2)}) collective-permute-start(bf16[32,1280]{1,0:T(8,128)(2,1)S(1)} %get-tuple-element.87), channel_id=1, source_target_pairs={{0,2},{1,3},{2,0},{3,1},{4,6},{5,7},{6,4},{7,5},{8,10},{9,11},{10,... | collective-permute-start | bytes 245768 | tf_op jit(solution)/shard_map/ppermute | solution.py:452
  72.4 6.2 %collective-permute-start.26 = (bf16[32,1280]{1,0:T(8,128)(2,1)S(1)}, bf16[32,1280]{1,0:T(8,128)(2,1)S(1)}, u32[]{:S(2)}, u32[]{:S(2)}) collective-permute-start(bf16[32,1280]{1,0:T(8,128)(2,1)S(1)} %get-tuple-element.88), channel_id=1, source_target_pairs={{0,3},{1,2},{2,1},{3,0},{4,7},{5,6},{6,5},{7,4},{8,11},{9,10},{10,... | collective-permute-start | bytes 245768 | tf_op jit(solution)/shard_map/ppermute | solution.py:452
  74.5 5.5 %collective-permute-start.22 = (bf16[32,1152]{1,0:T(8,128)(2,1)}, bf16[32,1152]{1,0:T(8,128)(2,1)S(1)}, u32[]{:S(2)}, u32[]{:S(2)}) collective-permute-start(bf16[32,1152]{1,0:T(8,128)(2,1)} %get-tuple-element.82), channel_id=1, source_target_pairs={{0,8},{4,12},{8,0},{12,4},{1,9},{5,13},{9,1},{13,5},{2,10},{6,14},... | collective-permute-start | bytes 221192 | tf_op jit(solution)/shard_map/ppermute | solution.py:452
  75.8 6.3 %collective-permute-start.23 = (bf16[32,1152]{1,0:T(8,128)(2,1)S(1)}, bf16[32,1152]{1,0:T(8,128)(2,1)S(1)}, u32[]{:S(2)}, u32[]{:S(2)}) collective-permute-start(bf16[32,1152]{1,0:T(8,128)(2,1)S(1)} %get-tuple-element.83), channel_id=1, source_target_pairs={{0,12},{4,8},{8,4},{12,0},{1,13},{5,9},{9,5},{13,1},{2,14},{6,10},... | collective-permute-start | bytes 221192 | tf_op jit(solution)/shard_map/ppermute | solution.py:452
  82.1 4.5 %collective-permute-start.28 = (bf16[64,288]{1,0:T(8,128)(2,1)S(1)}, bf16[64,288]{1,0:T(8,128)(2,1)S(1)}, u32[]{:S(2)}, u32[]{:S(2)}) collective-permute-start(bf16[64,288]{1,0:T(8,128)(2,1)S(1)} %shard_map.130.refs_0_), channel_id=1, source_target_pairs={{0,4},{4,0},{8,12},{12,8},{1,5},{5,1},{9,13},{13,9},{2,6},{6,2},{1... | collective-permute-start | bytes 110600 | tf_op jit(solution)/shard_map/ppermute | solution.py:452
  83.0 5.0 %collective-permute-start.29 = (bf16[64,288]{1,0:T(8,128)(2,1)S(1)}, bf16[64,288]{1,0:T(8,128)(2,1)S(1)}, u32[]{:S(2)}, u32[]{:S(2)}) collective-permute-start(bf16[64,288]{1,0:T(8,128)(2,1)S(1)} %shard_map.130.refs_0_), channel_id=1, source_target_pairs={{0,8},{4,12},{8,0},{12,4},{1,9},{5,13},{9,1},{13,5},{2,10},{6,14},... | collective-permute-start | bytes 110600 | tf_op jit(solution)/shard_map/ppermute | solution.py:452
  85.5 5.9 %collective-permute-start.30 = (bf16[64,288]{1,0:T(8,128)(2,1)S(1)}, bf16[64,288]{1,0:T(8,128)(2,1)S(1)}, u32[]{:S(2)}, u32[]{:S(2)}) collective-permute-start(bf16[64,288]{1,0:T(8,128)(2,1)S(1)} %shard_map.130.refs_0_), channel_id=1, source_target_pairs={{0,12},{4,8},{8,4},{12,0},{1,13},{5,9},{9,5},{13,1},{2,14},{6,10},... | collective-permute-start | bytes 110600 | tf_op jit(solution)/shard_map/ppermute | solution.py:452
  91.4 4.2 %collective-permute-start.31 = (bf16[64,288]{1,0:T(8,128)(2,1)S(1)}, bf16[64,288]{1,0:T(8,128)(2,1)S(1)}, u32[]{:S(2)}, u32[]{:S(2)}) collective-permute-start(bf16[64,288]{1,0:T(8,128)(2,1)S(1)} %shard_map.131.refs_0_), channel_id=1, source_target_pairs={{0,1},{1,0},{2,3},{3,2},{4,5},{5,4},{6,7},{7,6},{8,9},{9,8},{10,11... | collective-permute-start | bytes 110600 | tf_op jit(solution)/shard_map/ppermute | solution.py:452
  91.7 4.1 %collective-permute-start.32 = (bf16[64,288]{1,0:T(8,128)(2,1)S(1)}, bf16[64,288]{1,0:T(8,128)(2,1)S(1)}, u32[]{:S(2)}, u32[]{:S(2)}) collective-permute-start(bf16[64,288]{1,0:T(8,128)(2,1)S(1)} %shard_map.131.refs_0_), channel_id=1, source_target_pairs={{0,2},{1,3},{2,0},{3,1},{4,6},{5,7},{6,4},{7,5},{8,10},{9,11},{10,... | collective-permute-start | bytes 110600 | tf_op jit(solution)/shard_map/ppermute | solution.py:452
  92.7 5.0 %collective-permute-start.33 = (bf16[64,288]{1,0:T(8,128)(2,1)S(1)}, bf16[64,288]{1,0:T(8,128)(2,1)S(1)}, u32[]{:S(2)}, u32[]{:S(2)}) collective-permute-start(bf16[64,288]{1,0:T(8,128)(2,1)S(1)} %shard_map.131.refs_0_), channel_id=1, source_target_pairs={{0,3},{1,2},{2,1},{3,0},{4,7},{5,6},{6,5},{7,4},{8,11},{9,10},{10,... | collective-permute-start | bytes 110600 | tf_op jit(solution)/shard_map/ppermute | solution.py:452
  (13 other events, 120.6 us)

commit v10 on v8

--- a/solution.py
+++ b/solution.py
@@ -63,15 +63,14 @@
     return weights * (1.0 / jnp.sum(weights, axis=0, keepdims=True))
 
 
-def head_backward(probs, k_t, v_t, g_t, forward=False):
+def head_backward(probs, k_t, v_t, g_t):
     low = probs.astype(BF16)
     dvals = mm(g_t, low, NT)
     dprob = mm(v_t.T, g_t)
     inner = jnp.sum(probs * dprob, axis=0, keepdims=True)
     dscore = (probs * (dprob - inner) * SCALE).astype(BF16)
     dquery = mm(k_t, dscore)
-    out = mm(v_t, low) if forward else None
-    return dquery, dvals, out
+    return dquery, dvals
 
 
 def rows_of(array, head):
@@ -261,18 +260,32 @@
     vals = (x_ref[2].astype(F32) + mm(b_ref[3], codes_v, TN)).astype(BF16).astype(F32)
     keys = x_ref[1].astype(F32)
     grad = x_ref[3].astype(F32)
-    row = lax.broadcasted_iota(jnp.int32, (tokens, tokens), 0)
-    col = lax.broadcasted_iota(jnp.int32, (tokens, tokens), 1)
+    row = lax.broadcasted_iota(jnp.int32, (tokens, 2 * tokens), 0)
+    col = lax.broadcasted_iota(jnp.int32, (tokens, 2 * tokens), 1)
     mask = lax.rem(row, sub) == lax.rem(col, sub)
+    top = lax.broadcasted_iota(jnp.int32, (2 * HEAD_DIM, tokens), 0) < HEAD_DIM
+
+    def spread(pair):
+        return jnp.concatenate(
+            [jnp.where(top, pair, 0.0), jnp.where(top, 0.0, pair)], axis=1
+        ).astype(BF16)
+
+    def pick(wide):
+        return jnp.concatenate([wide[:HEAD_DIM, :tokens], wide[HEAD_DIM:, tokens:]], axis=0)
+
     outs_h, d_query, d_vals = [], [], []
-    for h in range(width // HEAD_DIM):
-        k_h = rows_of(keys, h).astype(BF16)
-        v_h = rows_of(vals, h).astype(BF16)
-        probs = probs_of(k_h.T, rows_of(query, h).astype(BF16), mask)
-        dq, dv, out = head_backward(probs, k_h, v_h, rows_of(grad, h).astype(BF16), True)
-        outs_h.append(out)
-        d_query.append(dq)
-        d_vals.append(dv)
+    for h in range(0, width, 2 * HEAD_DIM):
+        pair = slice(h, h + 2 * HEAD_DIM)
+        k_h, v_h = keys[pair].astype(BF16), vals[pair].astype(BF16)
+        g_h = spread(grad[pair])
+        probs = probs_of(k_h.T, spread(query[pair]), mask)
+        low = probs.astype(BF16)
+        dprob = mm(v_h.T, g_h)
+        inner = jnp.sum(probs * dprob, axis=0, keepdims=True)
+        dscore = (probs * (dprob - inner) * SCALE).astype(BF16)
+        outs_h.append(pick(mm(v_h, low)))
+        d_vals.append(mm(g_h, low, NT))
+        d_query.append(pick(mm(k_h, dscore)))
     d_query = jnp.concatenate(d_query, axis=0).astype(BF16)
     d_vals = jnp.concatenate(d_vals, axis=0).astype(BF16)
     d_codes = jnp.concatenate([mm(b_ref[2], d_query), mm(b_ref[3], d_vals)] * 4, axis=0)
@@ -325,7 +338,7 @@
             dq_parts, dv_sum = [], None
             for s in range(0, total, step):
                 probs = probs_ref[f, h, :, s : s + step]
-                dq, dv, _ = head_backward(probs, k_h, v_h, g_h[:, s : s + step])
+                dq, dv = head_backward(probs, k_h, v_h, g_h[:, s : s + step])
                 dq_parts.append(dq)
                 dv_sum = dv if dv_sum is None else dv_sum + dv
             d_query.append(
@@ -348,14 +361,12 @@
     part_ref[:RANK] = grad_b_q
     part_ref[RANK:] = grad_b_v
     grad_a = mm(dcodes[0][...], hidden_ref[...])
-    pad = -(-d_s // 128) * 128
     for j in range(n_s):
-        cut_buf[j, 0, :, :d_s] = grad_a[:, j * d_s : (j + 1) * d_s].astype(BF16)
-        cut_buf[j, 1, :, :d_s] = grad_b_ref[:, j * d_s : (j + 1) * d_s].astype(BF16)
+        here = slice(j * d_s, (j + 1) * d_s)
+        cut_buf[j, :, :d_s] = grad_a[:, here].astype(BF16)
+        cut_buf[j, :, d_s:] = grad_b_ref[:, here].astype(BF16)
     for k in range(n_s):
-        for index in range(2):
-            start = frames * total + index * pad
-            sends[k][:, start : start + pad] = cut_buf[peer("space", k), index]
+        sends[k][:, frames * total :] = cut_buf[peer("space", k)]
 
 
 def add_up(terms):
@@ -372,7 +383,6 @@
     tokens = packed[0].shape[1]
     patch_dev = tokens // frames
     total = n_s * patch_dev
-    pad = -(-d_s // 128) * 128
     patches = [x[3 * d_s : 4 * d_s] for x in packed]
     terms = []
     for f in range(frames):
@@ -380,11 +390,12 @@
         terms.append(mm(add_up(codes).astype(BF16), frame_rows(patches, f, patch_dev), NT))
     start = frames * total
     time_a = add_up([recv[:, start : start + d_s].astype(F32) for recv in recvs])
-    time_b = add_up([recv[:, start + pad : start + pad + d_s].astype(F32) for recv in recvs])
+    time_b = add_up([recv[:, start + d_s : start + 2 * d_s].astype(F32) for recv in recvs])
     rows = jnp.concatenate([add_up(terms), time_a, part_ref[...], time_b], axis=0)
     per = rows.shape[0] // n_d
     for d in range(n_d):
-        buf[d] = rows[d * per : (d + 1) * per]
+        mine = rows[d * per : (d + 1) * per]
+        buf[d] = jnp.concatenate([mine[: per // 2], mine[per // 2 :]], axis=1)
     for k in range(n_d):
         sends[k][...] = buf[peer("dp", k)]
 
@@ -400,7 +411,10 @@
     pieces, (out_ref, buf) = refs[:-2], refs[-2:]
     for k, piece in enumerate(pieces):
         buf[peer("space", k)] = piece[...]
-    out_ref[...] = jnp.concatenate([buf[j] for j in range(len(pieces))], axis=1)
+    half, d_s = buf.shape[1], buf.shape[2] // 2
+    for h in range(2):
+        cuts = [buf[j, :, h * d_s : (h + 1) * d_s] for j in range(len(pieces))]
+        out_ref[h * half : (h + 1) * half] = jnp.concatenate(cuts, axis=1)
 
 
 def final_kernel(factor, n_d, *refs):
@@ -463,7 +477,6 @@
     downs_here = lax.dynamic_slice_in_dim(downs, here, d_s, 2)
     ups_here = lax.dynamic_slice_in_dim(adapters_b, here, d_s, 2)
     dma = pltpu.SemaphoreType.DMA
-    pad = -(-d_s // 128) * 128
 
     time_arrays = [far(x) for x in (query_t, key_t, value_t, cotangent)]
     space_arrays = [
@@ -523,7 +536,7 @@
     )
     out_t, dcodes, time_grad_b = timed[:n_t], timed[n_t : 2 * n_t], timed[2 * n_t]
     dcodes = exchange(dcodes, "tm")
-    out_t[1:2] = hops(out_t[1:2], "tm", 1)
+    out_t[1:3] = hops(out_t[1:3], "tm", 1)
     dcodes = call(
         functools.partial(place_codes_kernel, frames, sub),
         shape((2 * RANK, tokens), BF16),
@@ -533,29 +546,29 @@
     dcodes = share(dcodes, "space")
     backward = call(
         functools.partial(space_backward_kernel, frames, n_s),
-        [shape((2 * RANK, frames * total + 2 * pad), BF16)] * n_s + [shape((2 * RANK, d_s), F32)],
+        [shape((2 * RANK, frames * total + 2 * d_s), BF16)] * n_s + [shape((2 * RANK, d_s), F32)],
         qkv, probs, hidden, time_grad_b, downs, downs_here, ups_here, *packed, *dcodes,
-        scratch=[pltpu.VMEM((n_s, 2, 2 * RANK, pad), BF16)],
-        after=out_t[1:2],
-        carry=out_t[2:],
+        scratch=[pltpu.VMEM((n_s, 2 * RANK, 2 * d_s), BF16)],
+        after=out_t[1:3],
+        carry=out_t[3:],
     )
     partial, part = backward[:n_s], backward[n_s]
     partial = exchange(partial, "space")
-    out_t[2:] = hops(backward[n_s + 1 :], "tm", 2)
+    out_t[3:] = hops(backward[n_s + 1 :], "tm", 3)
     rows = 8 * RANK // n_d
     sums = call(
         functools.partial(merge_kernel, frames, n_s, n_d),
-        [shape((rows, d_s), F32)] * n_d,
+        [shape((rows // 2, 2 * d_s), F32)] * n_d,
         part, *packed, *partial,
-        scratch=[pltpu.VMEM((n_d, rows, d_s), F32)],
-    )
-    sums = call(total_kernel, shape((rows, d_s), BF16), *exchange(sums, "dp"), after=out_t[2:])
-    sums = call(total_kernel, shape((rows, d_s), BF16), *share(sums, "tm"))
+        scratch=[pltpu.VMEM((n_d, rows // 2, 2 * d_s), F32)],
+    )
+    sums = call(total_kernel, shape((rows // 2, 2 * d_s), BF16), *exchange(sums, "dp"), after=out_t[3:])
+    sums = call(total_kernel, shape((rows // 2, 2 * d_s), BF16), *share(sums, "tm"))
     sums = call(
         join_kernel,
         shape((rows, width), BF16),
         *share(sums, "space"),
-        scratch=[pltpu.VMEM((n_s, rows, d_s), BF16)],
+        scratch=[pltpu.VMEM((n_s, rows // 2, 2 * d_s), BF16)],
     )
     grads_a, grads_b = call(
         functools.partial(final_kernel, factor, n_d),

time: 95.1 us -> 92.6 us (0.974)
  waiting for transfers between devices: 32.3 us -> 29.8 us
  starting transfers between devices: 42.3 us -> 44.2 us
  Pallas kernels: 19.3 us -> 17.4 us
    ppermute x32, waiting for transfers between devices: 32.3 us -> 29.8 us  [hops(): lax.ppermute(array, axis, [(i, i ^ k) for i in range(size)])]
    ppermute x32, starting transfers between devices: 42.3 us -> 44.2 us  [hops(): lax.ppermute(array, axis, [(i, i ^ k) for i in range(size)])]
    pallas_call x13, Pallas kernels: 19.3 us -> 17.4 us  [call(): pl.pallas_call(body, out_shape=outs + tuple((shape(x.shape, x.dtype) for...]
where the time goes in v10:
time: 92.6 us; the launch traced here: 92.5 us
  starting transfers between devices  44.2 us (48%)
  waiting for transfers between devices  29.8 us (32%)
  Pallas kernels  17.4 us (19%)
    ppermute x32, starting transfers between devices, hops(): lax.ppermute(array, axis, [(i, i ^ k) for i in range(size)])  44.2 us
    ppermute x32, waiting for transfers between devices, hops(): lax.ppermute(array, axis, [(i, i ^ k) for i in range(size)])  29.8 us
    pallas_call x13, Pallas kernels, call(): pl.pallas_call(body, out_shape=outs + tuple((shape(x.shape, x.dtype) for...  17.4 us
  transfers between devices with their start and end apart: 32, of which 18 were waited for; matrix products, arithmetic and copies ran while one was open for 0% of the time, Pallas kernels for 7%

profile of v10, /device:TPU:0, one launch (start us, length us, event | category | flops | bytes accessed | tf_op | source)
XLA Modules:
  0.0 92.5 jit_solution(11834570998191581836)
XLA Ops:
  0.7 3.6 %shard_map.121 = (bf16[1472,128]{1,0:T(8,128)(2,1)S(1)}, bf16[1472,128]{1,0:T(8,128)(2,1)S(1)}, bf16[1472,128]{1,0:T(8,128)(2,1)S(1)}, bf16[1472,128]{1,0:T(8,12...) custom-call(bf16[1,2,64,1152]{3,2,1,0:T(8,128)(2,1)} %refs_4_.3, ...), custom_call_target="tpu_custom_call" | custom-call | tf_op jit(solution)/shard_map/pallas_call | solution.py:40
  4.3 3.1 %collective-permute-start.3 = (bf16[4,32,1152]{2,1,0:T(8,128)(2,1)S(1)}, bf16[4,32,1152]{2,1,0:T(8,128)(2,1)S(1)}, u32[]{:S(2)}, u32[]{:S(2)}) collective-permute-start(bf16[4,32,1152]{2,1,0:T(8,128)(2,1)S(1)} %get-tuple-element.44), channel_id=1, source_target_pairs={{0,4},{4,0},{8,12},{12,8},{1,5},{5,1},{9,13},{13,9},{2,6},{6,2},{1... | collective-permute-start | bytes 884744 | tf_op jit(solution)/shard_map/ppermute | solution.py:452
  7.4 1.5 %collective-permute-start = (bf16[1472,128]{1,0:T(8,128)(2,1)S(1)}, bf16[1472,128]{1,0:T(8,128)(2,1)S(1)}, u32[]{:S(2)}, u32[]{:S(2)}) collective-permute-start(bf16[1472,128]{1,0:T(8,128)(2,1)S(1)} %get-tuple-element.41), channel_id=1, source_target_pairs={{0,1},{1,0},{2,3},{3,2},{4,5},{5,4},{6,7},{7,6},{8,9},{9,8},{10,11... | collective-permute-start | bytes 1130504 | tf_op jit(solution)/shard_map/ppermute | solution.py:452
  8.8 1.6 %collective-permute-start.1 = (bf16[1472,128]{1,0:T(8,128)(2,1)S(1)}, bf16[1472,128]{1,0:T(8,128)(2,1)S(1)}, u32[]{:S(2)}, u32[]{:S(2)}) collective-permute-start(bf16[1472,128]{1,0:T(8,128)(2,1)S(1)} %get-tuple-element.42), channel_id=1, source_target_pairs={{0,2},{1,3},{2,0},{3,1},{4,6},{5,7},{6,4},{7,5},{8,10},{9,11},{10,... | collective-permute-start | bytes 1130504 | tf_op jit(solution)/shard_map/ppermute | solution.py:452
  10.8 2.6 %collective-permute-start.7 = (bf16[4,32,1152]{2,1,0:T(8,128)(2,1)}, bf16[4,32,1152]{2,1,0:T(8,128)(2,1)}, u32[]{:S(2)}, u32[]{:S(2)}) collective-permute-start(bf16[4,32,1152]{2,1,0:T(8,128)(2,1)} %get-tuple-element.50), channel_id=1, source_target_pairs={{0,8},{4,12},{8,0},{12,4},{1,9},{5,13},{9,1},{13,5},{2,10},{6,14},... | collective-permute-start | bytes 884744 | tf_op jit(solution)/shard_map/ppermute | solution.py:452
  13.4 4.1 %collective-permute-done.3.refs_4_ = bf16[4,32,1152]{2,1,0:T(8,128)(2,1)S(1)} collective-permute-done((bf16[4,32,1152]{2,1,0:T(8,128)(2,1)S(1)}, bf16[4,32,1152]{2,1,0:T(8,128)(2,1)S(1)}, u32[]{:S(2)}, u32[]{:S(2)}) %collective-permute-start.3) | collective-permute-done | bytes 294944 | tf_op jit(solution)/shard_map/ppermute | solution.py:452
  17.5 2.8 %collective-permute-start.8 = (bf16[4,32,1152]{2,1,0:T(8,128)(2,1)}, bf16[4,32,1152]{2,1,0:T(8,128)(2,1)}, u32[]{:S(2)}, u32[]{:S(2)}) collective-permute-start(bf16[4,32,1152]{2,1,0:T(8,128)(2,1)} %get-tuple-element.51), channel_id=1, source_target_pairs={{0,12},{4,8},{8,4},{12,0},{1,13},{5,9},{9,5},{13,1},{2,14},{6,10},... | collective-permute-start | bytes 884744 | tf_op jit(solution)/shard_map/ppermute | solution.py:452
  20.3 6.5 %collective-permute-done.1.refs_2_.refs_9_.refs_3_ = bf16[1472,128]{1,0:T(8,128)(2,1)S(1)} collective-permute-done((bf16[1472,128]{1,0:T(8,128)(2,1)S(1)}, bf16[1472,128]{1,0:T(8,128)(2,1)S(1)}, u32[]{:S(2)}, u32[]{:S(2)}) %collective-permute-start.1) | collective-permute-done | bytes 376864 | tf_op jit(solution)/shard_map/ppermute | solution.py:452
  26.9 3.4 %shard_map.122 = (bf16[3,2,288,256]{3,2,1,0:T(8,128)(2,1)S(1)}, f32[2,4,256,256]{3,2,1,0:T(8,128)}, bf16[288,128]{1,0:T(8,128)(2,1)S(1)}, bf16[288,128]{1,0:T(8,...) custom-call(bf16[1472,128]{1,0:T(8,128)(2,1)S(1)} %get-tuple-element.40.refs_0_.refs_7_.refs_1_, ...), custom_call_target="tpu_custom_call" | custom-call | tf_op jit(solution)/shard_map/pallas_call | solution.py:40
  32.4 1.4 %collective-permute-start.6 = (bf16[288,128]{1,0:T(8,128)(2,1)S(1)}, bf16[288,128]{1,0:T(8,128)(2,1)S(1)}, u32[]{:S(2)}, u32[]{:S(2)}) collective-permute-start(bf16[288,128]{1,0:T(8,128)(2,1)S(1)} %get-tuple-element.48), channel_id=1, source_target_pairs={{0,3},{1,2},{2,1},{3,0},{4,7},{5,6},{6,5},{7,4},{8,11},{9,10},{10,... | collective-permute-start | bytes 221192 | tf_op jit(solution)/shard_map/ppermute | solution.py:452
  33.9 1.6 %collective-permute-done.4.refs_1_ = bf16[288,128]{1,0:T(8,128)(2,1)S(1)} collective-permute-done((bf16[288,128]{1,0:T(8,128)(2,1)S(1)}, bf16[288,128]{1,0:T(8,128)(2,1)S(1)}, u32[]{:S(2)}, u32[]{:S(2)}) %collective-permute-start.4) | collective-permute-done | bytes 73760 | tf_op jit(solution)/shard_map/ppermute | solution.py:452
  36.0 1.7 %collective-permute-done.6.refs_3_ = bf16[288,128]{1,0:T(8,128)(2,1)S(1)} collective-permute-done((bf16[288,128]{1,0:T(8,128)(2,1)S(1)}, bf16[288,128]{1,0:T(8,128)(2,1)S(1)}, u32[]{:S(2)}, u32[]{:S(2)}) %collective-permute-start.6) | collective-permute-done | bytes 73760 | tf_op jit(solution)/shard_map/ppermute | solution.py:452
  38.6 2.6 %collective-permute-start.10 = (f32[8,128]{1,0:T(8,128)S(1)}, f32[8,128]{1,0:T(8,128)S(1)}, u32[]{:S(2)}, u32[]{:S(2)}) collective-permute-start(f32[8,128]{1,0:T(8,128)S(1)} %get-tuple-element.54), channel_id=1, source_target_pairs={{0,8},{4,12},{8,0},{12,4},{1,9},{5,13},{9,1},{13,5},{2,10},{6,14},... | collective-permute-start | bytes 12296 | tf_op jit(solution)/shard_map/ppermute | solution.py:452
  42.5 1.8 %shard_map.124.refs_0_ = bf16[4,1152,128]{2,1,0:T(8,128)(2,1)S(1)} custom-call(bf16[1,2,64,1152]{3,2,1,0:T(8,128)(2,1)} %refs_0_.3, bf16[1,2,64,1152]{3,2,1,0:T(8,128)(2,1)} %refs_1_.2, bf16[1,2,64,1152]{3,2,1,0:T(8,128)(2,1)} %refs_2_.3, bf16[1,2,64,1152]{3,2,1,0:T(8,128)(2,1)} %refs_3_.3, bf16[4,32,1152]{2,1,0:T(8,128)(2,1)S(1)} %collective-permute-done.3.refs_4_, ...), custom_call_target="tpu_custom_call" | custom-call | tf_op jit(solution)/shard_map/pallas_call | solution.py:40
  44.4 2.2 %collective-permute-done.11.refs_5_ = f32[8,128]{1,0:T(8,128)S(1)} collective-permute-done((f32[8,128]{1,0:T(8,128)S(1)}, f32[8,128]{1,0:T(8,128)S(1)}, u32[]{:S(2)}, u32[]{:S(2)}) %collective-permute-start.11) | collective-permute-done | bytes 4128 | tf_op jit(solution)/shard_map/ppermute | solution.py:452
  46.6 3.1 %shard_map.125 = (bf16[32,1152]{1,0:T(8,128)(2,1)S(1)}, bf16[32,1152]{1,0:T(8,128)(2,1)S(1)}, bf16[32,1152]{1,0:T(8,128)(2,1)S(1)}, bf16[32,1152]{1,0:T(8,128)(2...) custom-call(bf16[4,1152,128]{2,1,0:T(8,128)(2,1)S(1)} %shard_map.124, ...), custom_call_target="tpu_custom_call" | custom-call | tf_op jit(solution)/shard_map/pallas_call | solution.py:40
  49.7 1.9 %collective-permute-start.15 = (f32[8,128]{1,0:T(8,128)S(1)}, f32[8,128]{1,0:T(8,128)S(1)}, u32[]{:S(2)}, u32[]{:S(2)}) collective-permute-start(f32[8,128]{1,0:T(8,128)S(1)} %get-tuple-element.64), channel_id=1, source_target_pairs={{0,8},{4,12},{8,0},{12,4},{1,9},{5,13},{9,1},{13,5},{2,10},{6,14},... | collective-permute-start | bytes 12296 | tf_op jit(solution)/shard_map/ppermute | solution.py:452
  51.6 2.5 %collective-permute-start.16 = (f32[8,128]{1,0:T(8,128)S(1)}, f32[8,128]{1,0:T(8,128)S(1)}, u32[]{:S(2)}, u32[]{:S(2)}) collective-permute-start(f32[8,128]{1,0:T(8,128)S(1)} %get-tuple-element.65), channel_id=1, source_target_pairs={{0,12},{4,8},{8,4},{12,0},{1,13},{5,9},{9,5},{13,1},{2,14},{6,10},... | collective-permute-start | bytes 12296 | tf_op jit(solution)/shard_map/ppermute | solution.py:452
  54.2 1.9 %collective-permute-start.13 = (bf16[32,1152]{1,0:T(8,128)(2,1)S(1)}, bf16[32,1152]{1,0:T(8,128)(2,1)S(1)}, u32[]{:S(2)}, u32[]{:S(2)}) collective-permute-start(bf16[32,1152]{1,0:T(8,128)(2,1)S(1)} %get-tuple-element.58), channel_id=1, source_target_pairs={{0,8},{4,12},{8,0},{12,4},{1,9},{5,13},{9,1},{13,5},{2,10},{6,14},... | collective-permute-start | bytes 221192 | tf_op jit(solution)/shard_map/ppermute | solution.py:452
  57.1 1.5 %collective-permute-start.19 = (bf16[32,128]{1,0:T(8,128)(2,1)S(1)}, bf16[32,128]{1,0:T(8,128)(2,1)S(1)}, u32[]{:S(2)}, u32[]{:S(2)}) collective-permute-start(bf16[32,128]{1,0:T(8,128)(2,1)S(1)} %shard_map.126.refs_11_), channel_id=1, source_target_pairs={{0,3},{1,2},{2,1},{3,0},{4,7},{5,6},{6,5},{7,4},{8,11},{9,10},{10,... | collective-permute-start | bytes 24584 | tf_op jit(solution)/shard_map/ppermute | solution.py:452
  58.6 1.6 %collective-permute-start.18 = (bf16[32,128]{1,0:T(8,128)(2,1)S(1)}, bf16[32,128]{1,0:T(8,128)(2,1)S(1)}, u32[]{:S(2)}, u32[]{:S(2)}) collective-permute-start(bf16[32,128]{1,0:T(8,128)(2,1)S(1)} %shard_map.126.refs_11_), channel_id=1, source_target_pairs={{0,2},{1,3},{2,0},{3,1},{4,6},{5,7},{6,4},{7,5},{8,10},{9,11},{10,... | collective-permute-start | bytes 24584 | tf_op jit(solution)/shard_map/ppermute | solution.py:452
  62.4 1.5 %collective-permute-done.17.refs_12_ = bf16[32,128]{1,0:T(8,128)(2,1)S(1)} collective-permute-done((bf16[32,128]{1,0:T(8,128)(2,1)S(1)}, bf16[32,128]{1,0:T(8,128)(2,1)S(1)}, u32[]{:S(2)}, u32[]{:S(2)}) %collective-permute-start.17) | collective-permute-done | bytes 8224 | tf_op jit(solution)/shard_map/ppermute | solution.py:452
  63.9 2.8 %shard_map.127 = (bf16[32,1088]{1,0:T(8,128)(2,1)S(1)}, bf16[32,1088]{1,0:T(8,128)(2,1)S(1)}, bf16[32,1088]{1,0:T(8,128)(2,1)S(1)}, bf16[32,1088]{1,0:T(8,128)(2...) custom-call(bf16[3,2,288,256]{3,2,1,0:T(8,128)(2,1)S(1)} %get-tuple-element.59.refs, ...), custom_call_target="tpu_custom_call", output_to_operand_aliasing={{5}: (17, {})} | custom-call | tf_op jit(solution)/shard_map/pallas_call | solution.py:40
  68.6 1.7 %collective-permute-start.23 = (bf16[32,1088]{1,0:T(8,128)(2,1)S(1)}, bf16[32,1088]{1,0:T(8,128)(2,1)S(1)}, u32[]{:S(2)}, u32[]{:S(2)}) collective-permute-start(bf16[32,1088]{1,0:T(8,128)(2,1)S(1)} %get-tuple-element.72), channel_id=1, source_target_pairs={{0,3},{1,2},{2,1},{3,0},{4,7},{5,6},{6,5},{7,4},{8,11},{9,10},{10,... | collective-permute-start | bytes 208904 | tf_op jit(solution)/shard_map/ppermute | solution.py:452
  70.3 2.6 %collective-permute-start.20 = (bf16[32,1152]{1,0:T(8,128)(2,1)S(1)}, bf16[32,1152]{1,0:T(8,128)(2,1)S(1)}, u32[]{:S(2)}, u32[]{:S(2)}) collective-permute-start(bf16[32,1152]{1,0:T(8,128)(2,1)S(1)} %get-tuple-element.67), channel_id=1, source_target_pairs={{0,12},{4,8},{8,4},{12,0},{1,13},{5,9},{9,5},{13,1},{2,14},{6,10},... | collective-permute-start | bytes 221192 | tf_op jit(solution)/shard_map/ppermute | solution.py:452
  74.2 2.2 %collective-permute-done.20.refs_4_.refs_2_ = bf16[32,1152]{1,0:T(8,128)(2,1)S(1)} collective-permute-done((bf16[32,1152]{1,0:T(8,128)(2,1)S(1)}, bf16[32,1152]{1,0:T(8,128)(2,1)S(1)}, u32[]{:S(2)}, u32[]{:S(2)}) %collective-permute-start.20) | collective-permute-done | bytes 73760 | tf_op jit(solution)/shard_map/ppermute | solution.py:452
  76.4 2.7 %collective-permute-start.27 = (bf16[32,576]{1,0:T(8,128)(2,1)S(1)}, bf16[32,576]{1,0:T(8,128)(2,1)S(1)}, u32[]{:S(2)}, u32[]{:S(2)}) collective-permute-start(bf16[32,576]{1,0:T(8,128)(2,1)S(1)} %shard_map.130.refs_0_), channel_id=1, source_target_pairs={{0,12},{4,8},{8,4},{12,0},{1,13},{5,9},{9,5},{13,1},{2,14},{6,10},... | collective-permute-start | bytes 110600 | tf_op jit(solution)/shard_map/ppermute | solution.py:452
  79.1 1.8 %collective-permute-start.25 = (bf16[32,576]{1,0:T(8,128)(2,1)S(1)}, bf16[32,576]{1,0:T(8,128)(2,1)S(1)}, u32[]{:S(2)}, u32[]{:S(2)}) collective-permute-start(bf16[32,576]{1,0:T(8,128)(2,1)S(1)} %shard_map.130.refs_0_), channel_id=1, source_target_pairs={{0,4},{4,0},{8,12},{12,8},{1,5},{5,1},{9,13},{13,9},{2,6},{6,2},{1... | collective-permute-start | bytes 110600 | tf_op jit(solution)/shard_map/ppermute | solution.py:452
  80.9 1.5 %collective-permute-done.27.refs_3_ = bf16[32,576]{1,0:T(8,128)(2,1)S(1)} collective-permute-done((bf16[32,576]{1,0:T(8,128)(2,1)S(1)}, bf16[32,576]{1,0:T(8,128)(2,1)S(1)}, u32[]{:S(2)}, u32[]{:S(2)}) %collective-permute-start.27) | collective-permute-done | bytes 36896 | tf_op jit(solution)/shard_map/ppermute | solution.py:452
  82.4 1.6 %collective-permute-done.26.refs_2_ = bf16[32,576]{1,0:T(8,128)(2,1)S(1)} collective-permute-done((bf16[32,576]{1,0:T(8,128)(2,1)S(1)}, bf16[32,576]{1,0:T(8,128)(2,1)S(1)}, u32[]{:S(2)}, u32[]{:S(2)}) %collective-permute-start.26) | collective-permute-done | bytes 36896 | tf_op jit(solution)/shard_map/ppermute | solution.py:452
  86.0 1.6 %collective-permute-start.28 = (bf16[32,576]{1,0:T(8,128)(2,1)S(1)}, bf16[32,576]{1,0:T(8,128)(2,1)S(1)}, u32[]{:S(2)}, u32[]{:S(2)}) collective-permute-start(bf16[32,576]{1,0:T(8,128)(2,1)S(1)} %shard_map.131.refs_0_), channel_id=1, source_target_pairs={{0,1},{1,0},{2,3},{3,2},{4,5},{5,4},{6,7},{7,6},{8,9},{9,8},{10,11... | collective-permute-start | bytes 110600 | tf_op jit(solution)/shard_map/ppermute | solution.py:452
  87.6 1.4 %collective-permute-done.30.refs_3_ = bf16[32,576]{1,0:T(8,128)(2,1)S(1)} collective-permute-done((bf16[32,576]{1,0:T(8,128)(2,1)S(1)}, bf16[32,576]{1,0:T(8,128)(2,1)S(1)}, u32[]{:S(2)}, u32[]{:S(2)}) %collective-permute-start.30) | collective-permute-done | bytes 36896 | tf_op jit(solution)/shard_map/ppermute | solution.py:452
  (55 shorter events, 17.4 us)
Async XLA Ops:
  4.3 13.2 %collective-permute-start.3 = (bf16[4,32,1152]{2,1,0:T(8,128)(2,1)S(1)}, bf16[4,32,1152]{2,1,0:T(8,128)(2,1)S(1)}, u32[]{:S(2)}, u32[]{:S(2)}) collective-permute-start(bf16[4,32,1152]{2,1,0:T(8,128)(2,1)S(1)} %get-tuple-element.44), channel_id=1, source_target_pairs={{0,4},{4,0},{8,12},{12,8},{1,5},{5,1},{9,13},{13,9},{2,6},{6,2},{1... | collective-permute-start | bytes 884744 | tf_op jit(solution)/shard_map/ppermute | solution.py:452
  7.4 13.0 %collective-permute-start = (bf16[1472,128]{1,0:T(8,128)(2,1)S(1)}, bf16[1472,128]{1,0:T(8,128)(2,1)S(1)}, u32[]{:S(2)}, u32[]{:S(2)}) collective-permute-start(bf16[1472,128]{1,0:T(8,128)(2,1)S(1)} %get-tuple-element.41), channel_id=1, source_target_pairs={{0,1},{1,0},{2,3},{3,2},{4,5},{5,4},{6,7},{7,6},{8,9},{9,8},{10,11... | collective-permute-start | bytes 1130504 | tf_op jit(solution)/shard_map/ppermute | solution.py:452
  8.8 18.0 %collective-permute-start.1 = (bf16[1472,128]{1,0:T(8,128)(2,1)S(1)}, bf16[1472,128]{1,0:T(8,128)(2,1)S(1)}, u32[]{:S(2)}, u32[]{:S(2)}) collective-permute-start(bf16[1472,128]{1,0:T(8,128)(2,1)S(1)} %get-tuple-element.42), channel_id=1, source_target_pairs={{0,2},{1,3},{2,0},{3,1},{4,6},{5,7},{6,4},{7,5},{8,10},{9,11},{10,... | collective-permute-start | bytes 1130504 | tf_op jit(solution)/shard_map/ppermute | solution.py:452
  10.4 16.4 %collective-permute-start.2 = (bf16[1472,128]{1,0:T(8,128)(2,1)S(1)}, bf16[1472,128]{1,0:T(8,128)(2,1)S(1)}, u32[]{:S(2)}, u32[]{:S(2)}) collective-permute-start(bf16[1472,128]{1,0:T(8,128)(2,1)S(1)} %get-tuple-element.43), channel_id=1, source_target_pairs={{0,3},{1,2},{2,1},{3,0},{4,7},{5,6},{6,5},{7,4},{8,11},{9,10},{10,... | collective-permute-start | bytes 1130504 | tf_op jit(solution)/shard_map/ppermute | solution.py:452
  10.8 31.7 %collective-permute-start.7 = (bf16[4,32,1152]{2,1,0:T(8,128)(2,1)}, bf16[4,32,1152]{2,1,0:T(8,128)(2,1)}, u32[]{:S(2)}, u32[]{:S(2)}) collective-permute-start(bf16[4,32,1152]{2,1,0:T(8,128)(2,1)} %get-tuple-element.50), channel_id=1, source_target_pairs={{0,8},{4,12},{8,0},{12,4},{1,9},{5,13},{9,1},{13,5},{2,10},{6,14},... | collective-permute-start | bytes 884744 | tf_op jit(solution)/shard_map/ppermute | solution.py:452
  17.5 25.0 %collective-permute-start.8 = (bf16[4,32,1152]{2,1,0:T(8,128)(2,1)}, bf16[4,32,1152]{2,1,0:T(8,128)(2,1)}, u32[]{:S(2)}, u32[]{:S(2)}) collective-permute-start(bf16[4,32,1152]{2,1,0:T(8,128)(2,1)} %get-tuple-element.51), channel_id=1, source_target_pairs={{0,12},{4,8},{8,4},{12,0},{1,13},{5,9},{9,5},{13,1},{2,14},{6,10},... | collective-permute-start | bytes 884744 | tf_op jit(solution)/shard_map/ppermute | solution.py:452
  30.3 5.2 %collective-permute-start.4 = (bf16[288,128]{1,0:T(8,128)(2,1)S(1)}, bf16[288,128]{1,0:T(8,128)(2,1)S(1)}, u32[]{:S(2)}, u32[]{:S(2)}) collective-permute-start(bf16[288,128]{1,0:T(8,128)(2,1)S(1)} %get-tuple-element.46), channel_id=1, source_target_pairs={{0,1},{1,0},{2,3},{3,2},{4,5},{5,4},{6,7},{7,6},{8,9},{9,8},{10,11... | collective-permute-start | bytes 221192 | tf_op jit(solution)/shard_map/ppermute | solution.py:452
  31.7 4.4 %collective-permute-start.5 = (bf16[288,128]{1,0:T(8,128)(2,1)S(1)}, bf16[288,128]{1,0:T(8,128)(2,1)S(1)}, u32[]{:S(2)}, u32[]{:S(2)}) collective-permute-start(bf16[288,128]{1,0:T(8,128)(2,1)S(1)} %get-tuple-element.47), channel_id=1, source_target_pairs={{0,2},{1,3},{2,0},{3,1},{4,6},{5,7},{6,4},{7,5},{8,10},{9,11},{10,... | collective-permute-start | bytes 221192 | tf_op jit(solution)/shard_map/ppermute | solution.py:452
  32.4 5.3 %collective-permute-start.6 = (bf16[288,128]{1,0:T(8,128)(2,1)S(1)}, bf16[288,128]{1,0:T(8,128)(2,1)S(1)}, u32[]{:S(2)}, u32[]{:S(2)}) collective-permute-start(bf16[288,128]{1,0:T(8,128)(2,1)S(1)} %get-tuple-element.48), channel_id=1, source_target_pairs={{0,3},{1,2},{2,1},{3,0},{4,7},{5,6},{6,5},{7,4},{8,11},{9,10},{10,... | collective-permute-start | bytes 221192 | tf_op jit(solution)/shard_map/ppermute | solution.py:452
  38.0 6.3 %collective-permute-start.9 = (f32[8,128]{1,0:T(8,128)S(1)}, f32[8,128]{1,0:T(8,128)S(1)}, u32[]{:S(2)}, u32[]{:S(2)}) collective-permute-start(f32[8,128]{1,0:T(8,128)S(1)} %get-tuple-element.53), channel_id=1, source_target_pairs={{0,4},{4,0},{8,12},{12,8},{1,5},{5,1},{9,13},{13,9},{2,6},{6,2},{1... | collective-permute-start | bytes 12296 | tf_op jit(solution)/shard_map/ppermute | solution.py:452
  38.6 5.8 %collective-permute-start.10 = (f32[8,128]{1,0:T(8,128)S(1)}, f32[8,128]{1,0:T(8,128)S(1)}, u32[]{:S(2)}, u32[]{:S(2)}) collective-permute-start(f32[8,128]{1,0:T(8,128)S(1)} %get-tuple-element.54), channel_id=1, source_target_pairs={{0,8},{4,12},{8,0},{12,4},{1,9},{5,13},{9,1},{13,5},{2,10},{6,14},... | collective-permute-start | bytes 12296 | tf_op jit(solution)/shard_map/ppermute | solution.py:452
  41.2 5.4 %collective-permute-start.11 = (f32[8,128]{1,0:T(8,128)S(1)}, f32[8,128]{1,0:T(8,128)S(1)}, u32[]{:S(2)}, u32[]{:S(2)}) collective-permute-start(f32[8,128]{1,0:T(8,128)S(1)} %get-tuple-element.55), channel_id=1, source_target_pairs={{0,12},{4,8},{8,4},{12,0},{1,13},{5,9},{9,5},{13,1},{2,14},{6,10},... | collective-permute-start | bytes 12296 | tf_op jit(solution)/shard_map/ppermute | solution.py:452
  49.7 6.5 %collective-permute-start.14 = (f32[8,128]{1,0:T(8,128)S(1)}, f32[8,128]{1,0:T(8,128)S(1)}, u32[]{:S(2)}, u32[]{:S(2)}) collective-permute-start(f32[8,128]{1,0:T(8,128)S(1)} %get-tuple-element.63), channel_id=1, source_target_pairs={{0,4},{4,0},{8,12},{12,8},{1,5},{5,1},{9,13},{13,9},{2,6},{6,2},{1... | collective-permute-start | bytes 12296 | tf_op jit(solution)/shard_map/ppermute | solution.py:452
  49.7 6.4 %collective-permute-start.15 = (f32[8,128]{1,0:T(8,128)S(1)}, f32[8,128]{1,0:T(8,128)S(1)}, u32[]{:S(2)}, u32[]{:S(2)}) collective-permute-start(f32[8,128]{1,0:T(8,128)S(1)} %get-tuple-element.64), channel_id=1, source_target_pairs={{0,8},{4,12},{8,0},{12,4},{1,9},{5,13},{9,1},{13,5},{2,10},{6,14},... | collective-permute-start | bytes 12296 | tf_op jit(solution)/shard_map/ppermute | solution.py:452
  51.6 5.4 %collective-permute-start.16 = (f32[8,128]{1,0:T(8,128)S(1)}, f32[8,128]{1,0:T(8,128)S(1)}, u32[]{:S(2)}, u32[]{:S(2)}) collective-permute-start(f32[8,128]{1,0:T(8,128)S(1)} %get-tuple-element.65), channel_id=1, source_target_pairs={{0,12},{4,8},{8,4},{12,0},{1,13},{5,9},{9,5},{13,1},{2,14},{6,10},... | collective-permute-start | bytes 12296 | tf_op jit(solution)/shard_map/ppermute | solution.py:452
  54.2 9.7 %collective-permute-start.12 = (bf16[32,1152]{1,0:T(8,128)(2,1)S(1)}, bf16[32,1152]{1,0:T(8,128)(2,1)S(1)}, u32[]{:S(2)}, u32[]{:S(2)}) collective-permute-start(bf16[32,1152]{1,0:T(8,128)(2,1)S(1)} %get-tuple-element.57), channel_id=1, source_target_pairs={{0,4},{4,0},{8,12},{12,8},{1,5},{5,1},{9,13},{13,9},{2,6},{6,2},{1... | collective-permute-start | bytes 221192 | tf_op jit(solution)/shard_map/ppermute | solution.py:452
  54.2 9.6 %collective-permute-start.13 = (bf16[32,1152]{1,0:T(8,128)(2,1)S(1)}, bf16[32,1152]{1,0:T(8,128)(2,1)S(1)}, u32[]{:S(2)}, u32[]{:S(2)}) collective-permute-start(bf16[32,1152]{1,0:T(8,128)(2,1)S(1)} %get-tuple-element.58), channel_id=1, source_target_pairs={{0,8},{4,12},{8,0},{12,4},{1,9},{5,13},{9,1},{13,5},{2,10},{6,14},... | collective-permute-start | bytes 221192 | tf_op jit(solution)/shard_map/ppermute | solution.py:452
  57.1 4.6 %collective-permute-start.19 = (bf16[32,128]{1,0:T(8,128)(2,1)S(1)}, bf16[32,128]{1,0:T(8,128)(2,1)S(1)}, u32[]{:S(2)}, u32[]{:S(2)}) collective-permute-start(bf16[32,128]{1,0:T(8,128)(2,1)S(1)} %shard_map.126.refs_11_), channel_id=1, source_target_pairs={{0,3},{1,2},{2,1},{3,0},{4,7},{5,6},{6,5},{7,4},{8,11},{9,10},{10,... | collective-permute-start | bytes 24584 | tf_op jit(solution)/shard_map/ppermute | solution.py:452
  58.6 3.7 %collective-permute-start.18 = (bf16[32,128]{1,0:T(8,128)(2,1)S(1)}, bf16[32,128]{1,0:T(8,128)(2,1)S(1)}, u32[]{:S(2)}, u32[]{:S(2)}) collective-permute-start(bf16[32,128]{1,0:T(8,128)(2,1)S(1)} %shard_map.126.refs_11_), channel_id=1, source_target_pairs={{0,2},{1,3},{2,0},{3,1},{4,6},{5,7},{6,4},{7,5},{8,10},{9,11},{10,... | collective-permute-start | bytes 24584 | tf_op jit(solution)/shard_map/ppermute | solution.py:452
  60.2 3.7 %collective-permute-start.17 = (bf16[32,128]{1,0:T(8,128)(2,1)S(1)}, bf16[32,128]{1,0:T(8,128)(2,1)S(1)}, u32[]{:S(2)}, u32[]{:S(2)}) collective-permute-start(bf16[32,128]{1,0:T(8,128)(2,1)S(1)} %shard_map.126.refs_11_), channel_id=1, source_target_pairs={{0,1},{1,0},{2,3},{3,2},{4,5},{5,4},{6,7},{7,6},{8,9},{9,8},{10,11... | collective-permute-start | bytes 24584 | tf_op jit(solution)/shard_map/ppermute | solution.py:452
  66.7 6.1 %collective-permute-start.21 = (bf16[32,1088]{1,0:T(8,128)(2,1)S(1)}, bf16[32,1088]{1,0:T(8,128)(2,1)S(1)}, u32[]{:S(2)}, u32[]{:S(2)}) collective-permute-start(bf16[32,1088]{1,0:T(8,128)(2,1)S(1)} %get-tuple-element.70), channel_id=1, source_target_pairs={{0,1},{1,0},{2,3},{3,2},{4,5},{5,4},{6,7},{7,6},{8,9},{9,8},{10,11... | collective-permute-start | bytes 208904 | tf_op jit(solution)/shard_map/ppermute | solution.py:452
  67.3 5.6 %collective-permute-start.22 = (bf16[32,1088]{1,0:T(8,128)(2,1)S(1)}, bf16[32,1088]{1,0:T(8,128)(2,1)S(1)}, u32[]{:S(2)}, u32[]{:S(2)}) collective-permute-start(bf16[32,1088]{1,0:T(8,128)(2,1)S(1)} %get-tuple-element.71), channel_id=1, source_target_pairs={{0,2},{1,3},{2,0},{3,1},{4,6},{5,7},{6,4},{7,5},{8,10},{9,11},{10,... | collective-permute-start | bytes 208904 | tf_op jit(solution)/shard_map/ppermute | solution.py:452
  68.6 5.3 %collective-permute-start.23 = (bf16[32,1088]{1,0:T(8,128)(2,1)S(1)}, bf16[32,1088]{1,0:T(8,128)(2,1)S(1)}, u32[]{:S(2)}, u32[]{:S(2)}) collective-permute-start(bf16[32,1088]{1,0:T(8,128)(2,1)S(1)} %get-tuple-element.72), channel_id=1, source_target_pairs={{0,3},{1,2},{2,1},{3,0},{4,7},{5,6},{6,5},{7,4},{8,11},{9,10},{10,... | collective-permute-start | bytes 208904 | tf_op jit(solution)/shard_map/ppermute | solution.py:452
  70.3 6.2 %collective-permute-start.20 = (bf16[32,1152]{1,0:T(8,128)(2,1)S(1)}, bf16[32,1152]{1,0:T(8,128)(2,1)S(1)}, u32[]{:S(2)}, u32[]{:S(2)}) collective-permute-start(bf16[32,1152]{1,0:T(8,128)(2,1)S(1)} %get-tuple-element.67), channel_id=1, source_target_pairs={{0,12},{4,8},{8,4},{12,0},{1,13},{5,9},{9,5},{13,1},{2,14},{6,10},... | collective-permute-start | bytes 221192 | tf_op jit(solution)/shard_map/ppermute | solution.py:452
  74.2 2.3 %collective-permute-start.24 = (f32[32,576]{1,0:T(8,128)S(1)}, f32[32,576]{1,0:T(8,128)S(1)}, u32[]{:S(2)}, u32[]{:S(2)}) collective-permute-start(f32[32,576]{1,0:T(8,128)S(1)} %get-tuple-element.74), channel_id=1, source_target_pairs={{0,16},{16,0},{1,17},{17,1},{2,18},{18,2},{3,19},{19,3},{4,20},{20... | collective-permute-start | bytes 221192 | tf_op jit(solution)/shard_map/ppermute | solution.py:452
  76.4 5.9 %collective-permute-start.27 = (bf16[32,576]{1,0:T(8,128)(2,1)S(1)}, bf16[32,576]{1,0:T(8,128)(2,1)S(1)}, u32[]{:S(2)}, u32[]{:S(2)}) collective-permute-start(bf16[32,576]{1,0:T(8,128)(2,1)S(1)} %shard_map.130.refs_0_), channel_id=1, source_target_pairs={{0,12},{4,8},{8,4},{12,0},{1,13},{5,9},{9,5},{13,1},{2,14},{6,10},... | collective-permute-start | bytes 110600 | tf_op jit(solution)/shard_map/ppermute | solution.py:452
  79.1 4.9 %collective-permute-start.26 = (bf16[32,576]{1,0:T(8,128)(2,1)S(1)}, bf16[32,576]{1,0:T(8,128)(2,1)S(1)}, u32[]{:S(2)}, u32[]{:S(2)}) collective-permute-start(bf16[32,576]{1,0:T(8,128)(2,1)S(1)} %shard_map.130.refs_0_), channel_id=1, source_target_pairs={{0,8},{4,12},{8,0},{12,4},{1,9},{5,13},{9,1},{13,5},{2,10},{6,14},... | collective-permute-start | bytes 110600 | tf_op jit(solution)/shard_map/ppermute | solution.py:452
  79.1 4.9 %collective-permute-start.25 = (bf16[32,576]{1,0:T(8,128)(2,1)S(1)}, bf16[32,576]{1,0:T(8,128)(2,1)S(1)}, u32[]{:S(2)}, u32[]{:S(2)}) collective-permute-start(bf16[32,576]{1,0:T(8,128)(2,1)S(1)} %shard_map.130.refs_0_), channel_id=1, source_target_pairs={{0,4},{4,0},{8,12},{12,8},{1,5},{5,1},{9,13},{13,9},{2,6},{6,2},{1... | collective-permute-start | bytes 110600 | tf_op jit(solution)/shard_map/ppermute | solution.py:452
  84.0 5.0 %collective-permute-start.30 = (bf16[32,576]{1,0:T(8,128)(2,1)S(1)}, bf16[32,576]{1,0:T(8,128)(2,1)S(1)}, u32[]{:S(2)}, u32[]{:S(2)}) collective-permute-start(bf16[32,576]{1,0:T(8,128)(2,1)S(1)} %shard_map.131.refs_0_), channel_id=1, source_target_pairs={{0,3},{1,2},{2,1},{3,0},{4,7},{5,6},{6,5},{7,4},{8,11},{9,10},{10,... | collective-permute-start | bytes 110600 | tf_op jit(solution)/shard_map/ppermute | solution.py:452
  85.3 4.1 %collective-permute-start.29 = (bf16[32,576]{1,0:T(8,128)(2,1)S(1)}, bf16[32,576]{1,0:T(8,128)(2,1)S(1)}, u32[]{:S(2)}, u32[]{:S(2)}) collective-permute-start(bf16[32,576]{1,0:T(8,128)(2,1)S(1)} %shard_map.131.refs_0_), channel_id=1, source_target_pairs={{0,2},{1,3},{2,0},{3,1},{4,6},{5,7},{6,4},{7,5},{8,10},{9,11},{10,... | collective-permute-start | bytes 110600 | tf_op jit(solution)/shard_map/ppermute | solution.py:452
  86.0 4.0 %collective-permute-start.28 = (bf16[32,576]{1,0:T(8,128)(2,1)S(1)}, bf16[32,576]{1,0:T(8,128)(2,1)S(1)}, u32[]{:S(2)}, u32[]{:S(2)}) collective-permute-start(bf16[32,576]{1,0:T(8,128)(2,1)S(1)} %shard_map.131.refs_0_), channel_id=1, source_target_pairs={{0,1},{1,0},{2,3},{3,2},{4,5},{5,4},{6,7},{7,6},{8,9},{9,8},{10,11... | collective-permute-start | bytes 110600 | tf_op jit(solution)/shard_map/ppermute | solution.py:452
  90.2 1.4 %collective-permute-start.31 = (bf16[64,1152]{1,0:T(8,128)(2,1)S(1)}, bf16[64,1152]{1,0:T(8,128)(2,1)S(1)}, u32[]{:S(2)}, u32[]{:S(2)}) collective-permute-start(bf16[64,1152]{1,0:T(8,128)(2,1)S(1)} %shard_map.132.refs_0_), channel_id=1, source_target_pairs={{0,16},{16,0},{1,17},{17,1},{2,18},{18,2},{3,19},{19,3},{4,20},{20... | collective-permute-start | bytes 442376 | tf_op jit(solution)/shard_map/ppermute | solution.py:452
  (4 other events, 111.7 us)

commit v11 on v10

--- a/solution.py
+++ b/solution.py
@@ -537,24 +537,24 @@
     out_t, dcodes, time_grad_b = timed[:n_t], timed[n_t : 2 * n_t], timed[2 * n_t]
     dcodes = exchange(dcodes, "tm")
     out_t[1:3] = hops(out_t[1:3], "tm", 1)
-    dcodes = call(
+    dcodes, *rest = call(
         functools.partial(place_codes_kernel, frames, sub),
         shape((2 * RANK, tokens), BF16),
         *dcodes,
         scratch=[pltpu.VMEM((tokens, 128), F32)],
+        after=out_t[1:2],
+        carry=out_t[3:],
     )
     dcodes = share(dcodes, "space")
+    out_t[3:] = hops(rest, "tm", 3)
     backward = call(
         functools.partial(space_backward_kernel, frames, n_s),
         [shape((2 * RANK, frames * total + 2 * d_s), BF16)] * n_s + [shape((2 * RANK, d_s), F32)],
         qkv, probs, hidden, time_grad_b, downs, downs_here, ups_here, *packed, *dcodes,
         scratch=[pltpu.VMEM((n_s, 2 * RANK, 2 * d_s), BF16)],
-        after=out_t[1:3],
-        carry=out_t[3:],
-    )
-    partial, part = backward[:n_s], backward[n_s]
-    partial = exchange(partial, "space")
-    out_t[3:] = hops(backward[n_s + 1 :], "tm", 3)
+        after=out_t[2:],
+    )
+    partial, part = exchange(backward[:n_s], "space"), backward[n_s]
     rows = 8 * RANK // n_d
     sums = call(
         functools.partial(merge_kernel, frames, n_s, n_d),
@@ -562,7 +562,7 @@
         part, *packed, *partial,
         scratch=[pltpu.VMEM((n_d, rows // 2, 2 * d_s), F32)],
     )
-    sums = call(total_kernel, shape((rows // 2, 2 * d_s), BF16), *exchange(sums, "dp"), after=out_t[3:])
+    sums = call(total_kernel, shape((rows // 2, 2 * d_s), BF16), *exchange(sums, "dp"))
     sums = call(total_kernel, shape((rows // 2, 2 * d_s), BF16), *share(sums, "tm"))
     sums = call(
         join_kernel,

time: 92.6 us -> 96.7 us (1.044)
  waiting for transfers between devices: 29.8 us -> 35.1 us
  starting transfers between devices: 44.2 us -> 43 us
    ppermute x32, waiting for transfers between devices: 29.8 us -> 35.1 us  [hops(): lax.ppermute(array, axis, [(i, i ^ k) for i in range(size)])]
    ppermute x32, starting transfers between devices: 44.2 us -> 43 us  [hops(): lax.ppermute(array, axis, [(i, i ^ k) for i in range(size)])]
  transfers between devices with their start and end apart: 32 -> 32, of which waited for: 18 -> 21; matrix products, arithmetic and copies ran while one was open for 0% -> 0% of each run, Pallas kernels for 7% -> 7%
where the time goes in v11:
time: 96.7 us; the launch traced here: 96.6 us
  starting transfers between devices  43 us (44%)
  waiting for transfers between devices  35.1 us (36%)
  Pallas kernels  17.4 us (18%)
    ppermute x32, starting transfers between devices, hops(): lax.ppermute(array, axis, [(i, i ^ k) for i in range(size)])  43 us
    ppermute x32, waiting for transfers between devices, hops(): lax.ppermute(array, axis, [(i, i ^ k) for i in range(size)])  35.1 us
    pallas_call x13, Pallas kernels, call(): pl.pallas_call(body, out_shape=outs + tuple((shape(x.shape, x.dtype) for...  17.4 us
  transfers between devices with their start and end apart: 32, of which 21 were waited for; matrix products, arithmetic and copies ran while one was open for 0% of the time, Pallas kernels for 7%

profile of v11, /device:TPU:0, one launch (start us, length us, event | category | flops | bytes accessed | tf_op | source)
XLA Modules:
  0.0 96.6 jit_solution(9940464786226400904)
XLA Ops:
  0.7 3.6 %shard_map.121 = (bf16[1472,128]{1,0:T(8,128)(2,1)S(1)}, bf16[1472,128]{1,0:T(8,128)(2,1)S(1)}, bf16[1472,128]{1,0:T(8,128)(2,1)S(1)}, bf16[1472,128]{1,0:T(8,12...) custom-call(bf16[1,2,64,1152]{3,2,1,0:T(8,128)(2,1)} %refs_4_.3, ...), custom_call_target="tpu_custom_call" | custom-call | tf_op jit(solution)/shard_map/pallas_call | solution.py:40
  4.3 3.1 %collective-permute-start.3 = (bf16[4,32,1152]{2,1,0:T(8,128)(2,1)S(1)}, bf16[4,32,1152]{2,1,0:T(8,128)(2,1)S(1)}, u32[]{:S(2)}, u32[]{:S(2)}) collective-permute-start(bf16[4,32,1152]{2,1,0:T(8,128)(2,1)S(1)} %get-tuple-element.45), channel_id=1, source_target_pairs={{0,4},{4,0},{8,12},{12,8},{1,5},{5,1},{9,13},{13,9},{2,6},{6,2},{1... | collective-permute-start | bytes 884744 | tf_op jit(solution)/shard_map/ppermute | solution.py:452
  7.4 1.5 %collective-permute-start = (bf16[1472,128]{1,0:T(8,128)(2,1)S(1)}, bf16[1472,128]{1,0:T(8,128)(2,1)S(1)}, u32[]{:S(2)}, u32[]{:S(2)}) collective-permute-start(bf16[1472,128]{1,0:T(8,128)(2,1)S(1)} %get-tuple-element.42), channel_id=1, source_target_pairs={{0,1},{1,0},{2,3},{3,2},{4,5},{5,4},{6,7},{7,6},{8,9},{9,8},{10,11... | collective-permute-start | bytes 1130504 | tf_op jit(solution)/shard_map/ppermute | solution.py:452
  8.8 1.6 %collective-permute-start.1 = (bf16[1472,128]{1,0:T(8,128)(2,1)S(1)}, bf16[1472,128]{1,0:T(8,128)(2,1)S(1)}, u32[]{:S(2)}, u32[]{:S(2)}) collective-permute-start(bf16[1472,128]{1,0:T(8,128)(2,1)S(1)} %get-tuple-element.43), channel_id=1, source_target_pairs={{0,2},{1,3},{2,0},{3,1},{4,6},{5,7},{6,4},{7,5},{8,10},{9,11},{10,... | collective-permute-start | bytes 1130504 | tf_op jit(solution)/shard_map/ppermute | solution.py:452
  10.8 2.6 %collective-permute-start.7 = (bf16[4,32,1152]{2,1,0:T(8,128)(2,1)}, bf16[4,32,1152]{2,1,0:T(8,128)(2,1)}, u32[]{:S(2)}, u32[]{:S(2)}) collective-permute-start(bf16[4,32,1152]{2,1,0:T(8,128)(2,1)} %get-tuple-element.51), channel_id=1, source_target_pairs={{0,8},{4,12},{8,0},{12,4},{1,9},{5,13},{9,1},{13,5},{2,10},{6,14},... | collective-permute-start | bytes 884744 | tf_op jit(solution)/shard_map/ppermute | solution.py:452
  13.4 4.1 %collective-permute-done.3.refs_4_ = bf16[4,32,1152]{2,1,0:T(8,128)(2,1)S(1)} collective-permute-done((bf16[4,32,1152]{2,1,0:T(8,128)(2,1)S(1)}, bf16[4,32,1152]{2,1,0:T(8,128)(2,1)S(1)}, u32[]{:S(2)}, u32[]{:S(2)}) %collective-permute-start.3) | collective-permute-done | bytes 294944 | tf_op jit(solution)/shard_map/ppermute | solution.py:452
  17.5 2.8 %collective-permute-start.8 = (bf16[4,32,1152]{2,1,0:T(8,128)(2,1)}, bf16[4,32,1152]{2,1,0:T(8,128)(2,1)}, u32[]{:S(2)}, u32[]{:S(2)}) collective-permute-start(bf16[4,32,1152]{2,1,0:T(8,128)(2,1)} %get-tuple-element.52), channel_id=1, source_target_pairs={{0,12},{4,8},{8,4},{12,0},{1,13},{5,9},{9,5},{13,1},{2,14},{6,10},... | collective-permute-start | bytes 884744 | tf_op jit(solution)/shard_map/ppermute | solution.py:452
  20.3 6.5 %collective-permute-done.1.refs_2_.refs_9_.refs_3_ = bf16[1472,128]{1,0:T(8,128)(2,1)S(1)} collective-permute-done((bf16[1472,128]{1,0:T(8,128)(2,1)S(1)}, bf16[1472,128]{1,0:T(8,128)(2,1)S(1)}, u32[]{:S(2)}, u32[]{:S(2)}) %collective-permute-start.1) | collective-permute-done | bytes 376864 | tf_op jit(solution)/shard_map/ppermute | solution.py:452
  26.9 3.4 %shard_map.122 = (bf16[3,2,288,256]{3,2,1,0:T(8,128)(2,1)S(1)}, f32[2,4,256,256]{3,2,1,0:T(8,128)}, bf16[288,128]{1,0:T(8,128)(2,1)S(1)}, bf16[288,128]{1,0:T(8,...) custom-call(bf16[1472,128]{1,0:T(8,128)(2,1)S(1)} %get-tuple-element.41.refs_0_.refs_7_.refs_1_, ...), custom_call_target="tpu_custom_call" | custom-call | tf_op jit(solution)/shard_map/pallas_call | solution.py:40
  32.4 1.4 %collective-permute-start.6 = (bf16[288,128]{1,0:T(8,128)(2,1)S(1)}, bf16[288,128]{1,0:T(8,128)(2,1)S(1)}, u32[]{:S(2)}, u32[]{:S(2)}) collective-permute-start(bf16[288,128]{1,0:T(8,128)(2,1)S(1)} %get-tuple-element.49), channel_id=1, source_target_pairs={{0,3},{1,2},{2,1},{3,0},{4,7},{5,6},{6,5},{7,4},{8,11},{9,10},{10,... | collective-permute-start | bytes 221192 | tf_op jit(solution)/shard_map/ppermute | solution.py:452
  33.9 1.6 %collective-permute-done.4.refs_1_ = bf16[288,128]{1,0:T(8,128)(2,1)S(1)} collective-permute-done((bf16[288,128]{1,0:T(8,128)(2,1)S(1)}, bf16[288,128]{1,0:T(8,128)(2,1)S(1)}, u32[]{:S(2)}, u32[]{:S(2)}) %collective-permute-start.4) | collective-permute-done | bytes 73760 | tf_op jit(solution)/shard_map/ppermute | solution.py:452
  36.0 1.7 %collective-permute-done.6.refs_3_ = bf16[288,128]{1,0:T(8,128)(2,1)S(1)} collective-permute-done((bf16[288,128]{1,0:T(8,128)(2,1)S(1)}, bf16[288,128]{1,0:T(8,128)(2,1)S(1)}, u32[]{:S(2)}, u32[]{:S(2)}) %collective-permute-start.6) | collective-permute-done | bytes 73760 | tf_op jit(solution)/shard_map/ppermute | solution.py:452
  38.5 2.6 %collective-permute-start.10 = (f32[8,128]{1,0:T(8,128)S(1)}, f32[8,128]{1,0:T(8,128)S(1)}, u32[]{:S(2)}, u32[]{:S(2)}) collective-permute-start(f32[8,128]{1,0:T(8,128)S(1)} %get-tuple-element.55), channel_id=1, source_target_pairs={{0,8},{4,12},{8,0},{12,4},{1,9},{5,13},{9,1},{13,5},{2,10},{6,14},... | collective-permute-start | bytes 12296 | tf_op jit(solution)/shard_map/ppermute | solution.py:452
  42.5 1.8 %shard_map.124.refs_0_ = bf16[4,1152,128]{2,1,0:T(8,128)(2,1)S(1)} custom-call(bf16[1,2,64,1152]{3,2,1,0:T(8,128)(2,1)} %refs_0_.3, bf16[1,2,64,1152]{3,2,1,0:T(8,128)(2,1)} %refs_1_.2, bf16[1,2,64,1152]{3,2,1,0:T(8,128)(2,1)} %refs_2_.3, bf16[1,2,64,1152]{3,2,1,0:T(8,128)(2,1)} %refs_3_.3, bf16[4,32,1152]{2,1,0:T(8,128)(2,1)S(1)} %collective-permute-done.3.refs_4_, ...), custom_call_target="tpu_custom_call" | custom-call | tf_op jit(solution)/shard_map/pallas_call | solution.py:40
  44.3 2.2 %collective-permute-done.11.refs_5_ = f32[8,128]{1,0:T(8,128)S(1)} collective-permute-done((f32[8,128]{1,0:T(8,128)S(1)}, f32[8,128]{1,0:T(8,128)S(1)}, u32[]{:S(2)}, u32[]{:S(2)}) %collective-permute-start.11) | collective-permute-done | bytes 4128 | tf_op jit(solution)/shard_map/ppermute | solution.py:452
  46.5 3.1 %shard_map.125 = (bf16[32,1152]{1,0:T(8,128)(2,1)S(1)}, bf16[32,1152]{1,0:T(8,128)(2,1)S(1)}, bf16[32,1152]{1,0:T(8,128)(2,1)S(1)}, bf16[32,1152]{1,0:T(8,128)(2...) custom-call(bf16[4,1152,128]{2,1,0:T(8,128)(2,1)S(1)} %shard_map.124, ...), custom_call_target="tpu_custom_call" | custom-call | tf_op jit(solution)/shard_map/pallas_call | solution.py:40
  49.7 1.9 %collective-permute-start.15 = (f32[8,128]{1,0:T(8,128)S(1)}, f32[8,128]{1,0:T(8,128)S(1)}, u32[]{:S(2)}, u32[]{:S(2)}) collective-permute-start(f32[8,128]{1,0:T(8,128)S(1)} %get-tuple-element.62), channel_id=1, source_target_pairs={{0,8},{4,12},{8,0},{12,4},{1,9},{5,13},{9,1},{13,5},{2,10},{6,14},... | collective-permute-start | bytes 12296 | tf_op jit(solution)/shard_map/ppermute | solution.py:452
  51.6 2.5 %collective-permute-start.16 = (f32[8,128]{1,0:T(8,128)S(1)}, f32[8,128]{1,0:T(8,128)S(1)}, u32[]{:S(2)}, u32[]{:S(2)}) collective-permute-start(f32[8,128]{1,0:T(8,128)S(1)} %get-tuple-element.63), channel_id=1, source_target_pairs={{0,12},{4,8},{8,4},{12,0},{1,13},{5,9},{9,5},{13,1},{2,14},{6,10},... | collective-permute-start | bytes 12296 | tf_op jit(solution)/shard_map/ppermute | solution.py:452
  54.2 2.0 %collective-permute-start.13 = (bf16[32,1152]{1,0:T(8,128)(2,1)S(1)}, bf16[32,1152]{1,0:T(8,128)(2,1)S(1)}, u32[]{:S(2)}, u32[]{:S(2)}) collective-permute-start(bf16[32,1152]{1,0:T(8,128)(2,1)S(1)} %get-tuple-element.59), channel_id=1, source_target_pairs={{0,8},{4,12},{8,0},{12,4},{1,9},{5,13},{9,1},{13,5},{2,10},{6,14},... | collective-permute-start | bytes 221192 | tf_op jit(solution)/shard_map/ppermute | solution.py:452
  57.0 1.4 %collective-permute-done.12.refs_4_.refs_2_ = bf16[32,1152]{1,0:T(8,128)(2,1)S(1)} collective-permute-done((bf16[32,1152]{1,0:T(8,128)(2,1)S(1)}, bf16[32,1152]{1,0:T(8,128)(2,1)S(1)}, u32[]{:S(2)}, u32[]{:S(2)}) %collective-permute-start.12) | collective-permute-done | bytes 73760 | tf_op jit(solution)/shard_map/ppermute | solution.py:452
  58.5 1.5 %collective-permute-start.20 = (bf16[32,128]{1,0:T(8,128)(2,1)S(1)}, bf16[32,128]{1,0:T(8,128)(2,1)S(1)}, u32[]{:S(2)}, u32[]{:S(2)}) collective-permute-start(bf16[32,128]{1,0:T(8,128)(2,1)S(1)} %get-tuple-element.69.refs_11_), channel_id=1, source_target_pairs={{0,3},{1,2},{2,1},{3,0},{4,7},{5,6},{6,5},{7,4},{8,11},{9,10},{10,... | collective-permute-start | bytes 24584 | tf_op jit(solution)/shard_map/ppermute | solution.py:452
  60.0 1.6 %collective-permute-start.19 = (bf16[32,128]{1,0:T(8,128)(2,1)S(1)}, bf16[32,128]{1,0:T(8,128)(2,1)S(1)}, u32[]{:S(2)}, u32[]{:S(2)}) collective-permute-start(bf16[32,128]{1,0:T(8,128)(2,1)S(1)} %get-tuple-element.69.refs_11_), channel_id=1, source_target_pairs={{0,2},{1,3},{2,0},{3,1},{4,6},{5,7},{6,4},{7,5},{8,10},{9,11},{10,... | collective-permute-start | bytes 24584 | tf_op jit(solution)/shard_map/ppermute | solution.py:452
  63.7 1.6 %collective-permute-done.18.refs_12_ = bf16[32,128]{1,0:T(8,128)(2,1)S(1)} collective-permute-done((bf16[32,128]{1,0:T(8,128)(2,1)S(1)}, bf16[32,128]{1,0:T(8,128)(2,1)S(1)}, u32[]{:S(2)}, u32[]{:S(2)}) %collective-permute-start.18) | collective-permute-done | bytes 8224 | tf_op jit(solution)/shard_map/ppermute | solution.py:452
  65.3 3.0 %collective-permute-done.17.refs_4_.refs_16_ = bf16[32,1152]{1,0:T(8,128)(2,1)S(1)} collective-permute-done((bf16[32,1152]{1,0:T(8,128)(2,1)S(1)}, bf16[32,1152]{1,0:T(8,128)(2,1)S(1)}, u32[]{:S(2)}, u32[]{:S(2)}) %collective-permute-start.17) | collective-permute-done | bytes 73760 | tf_op jit(solution)/shard_map/ppermute | solution.py:452
  68.2 2.8 %shard_map.128 = (bf16[32,1088]{1,0:T(8,128)(2,1)S(1)}, bf16[32,1088]{1,0:T(8,128)(2,1)S(1)}, bf16[32,1088]{1,0:T(8,128)(2,1)S(1)}, bf16[32,1088]{1,0:T(8,128)(2,1)S(1)}, f32[32,288]{1,0:T(8,128)S(1)}) custom-call(bf16[3,2,288,256]{3,2,1,0:T(8,128)(2,1)S(1)} %get-tuple-element.66.refs_0_, f32[2,4,256,256]{3,2,1,0:T(8,128)S(1)} %copy-done, ...), custom_call_target="tpu_custom_call" | custom-call | tf_op jit(solution)/shard_map/pallas_call | solution.py:40
  71.1 1.6 %collective-permute-start.21 = (bf16[32,1088]{1,0:T(8,128)(2,1)S(1)}, bf16[32,1088]{1,0:T(8,128)(2,1)S(1)}, u32[]{:S(2)}, u32[]{:S(2)}) collective-permute-start(bf16[32,1088]{1,0:T(8,128)(2,1)S(1)} %get-tuple-element.72), channel_id=1, source_target_pairs={{0,1},{1,0},{2,3},{3,2},{4,5},{5,4},{6,7},{7,6},{8,9},{9,8},{10,11... | collective-permute-start | bytes 208904 | tf_op jit(solution)/shard_map/ppermute | solution.py:452
  73.1 1.5 %collective-permute-start.23 = (bf16[32,1088]{1,0:T(8,128)(2,1)S(1)}, bf16[32,1088]{1,0:T(8,128)(2,1)S(1)}, u32[]{:S(2)}, u32[]{:S(2)}) collective-permute-start(bf16[32,1088]{1,0:T(8,128)(2,1)S(1)} %get-tuple-element.74), channel_id=1, source_target_pairs={{0,3},{1,2},{2,1},{3,0},{4,7},{5,6},{6,5},{7,4},{8,11},{9,10},{10,... | collective-permute-start | bytes 208904 | tf_op jit(solution)/shard_map/ppermute | solution.py:452
  75.5 1.6 %collective-permute-done.22.refs_7_ = bf16[32,1088]{1,0:T(8,128)(2,1)S(1)} collective-permute-done((bf16[32,1088]{1,0:T(8,128)(2,1)S(1)}, bf16[32,1088]{1,0:T(8,128)(2,1)S(1)}, u32[]{:S(2)}, u32[]{:S(2)}) %collective-permute-start.22) | collective-permute-done | bytes 69664 | tf_op jit(solution)/shard_map/ppermute | solution.py:452
  80.0 1.5 %collective-permute-start.27 = (bf16[32,576]{1,0:T(8,128)(2,1)S(1)}, bf16[32,576]{1,0:T(8,128)(2,1)S(1)}, u32[]{:S(2)}, u32[]{:S(2)}) collective-permute-start(bf16[32,576]{1,0:T(8,128)(2,1)S(1)} %shard_map.130.refs_0_), channel_id=1, source_target_pairs={{0,12},{4,8},{8,4},{12,0},{1,13},{5,9},{9,5},{13,1},{2,14},{6,10},... | collective-permute-start | bytes 110600 | tf_op jit(solution)/shard_map/ppermute | solution.py:452
  81.5 3.0 %collective-permute-start.25 = (bf16[32,576]{1,0:T(8,128)(2,1)S(1)}, bf16[32,576]{1,0:T(8,128)(2,1)S(1)}, u32[]{:S(2)}, u32[]{:S(2)}) collective-permute-start(bf16[32,576]{1,0:T(8,128)(2,1)S(1)} %shard_map.130.refs_0_), channel_id=1, source_target_pairs={{0,4},{4,0},{8,12},{12,8},{1,5},{5,1},{9,13},{13,9},{2,6},{6,2},{1... | collective-permute-start | bytes 110600 | tf_op jit(solution)/shard_map/ppermute | solution.py:452
  84.5 1.6 %collective-permute-done.27.refs_3_ = bf16[32,576]{1,0:T(8,128)(2,1)S(1)} collective-permute-done((bf16[32,576]{1,0:T(8,128)(2,1)S(1)}, bf16[32,576]{1,0:T(8,128)(2,1)S(1)}, u32[]{:S(2)}, u32[]{:S(2)}) %collective-permute-start.27) | collective-permute-done | bytes 36896 | tf_op jit(solution)/shard_map/ppermute | solution.py:452
  87.3 1.6 %collective-permute-start.30 = (bf16[32,576]{1,0:T(8,128)(2,1)S(1)}, bf16[32,576]{1,0:T(8,128)(2,1)S(1)}, u32[]{:S(2)}, u32[]{:S(2)}) collective-permute-start(bf16[32,576]{1,0:T(8,128)(2,1)S(1)} %shard_map.131.refs_0_), channel_id=1, source_target_pairs={{0,3},{1,2},{2,1},{3,0},{4,7},{5,6},{6,5},{7,4},{8,11},{9,10},{10,... | collective-permute-start | bytes 110600 | tf_op jit(solution)/shard_map/ppermute | solution.py:452
  (55 shorter events, 21.7 us)
Async XLA Ops:
  4.3 13.2 %collective-permute-start.3 = (bf16[4,32,1152]{2,1,0:T(8,128)(2,1)S(1)}, bf16[4,32,1152]{2,1,0:T(8,128)(2,1)S(1)}, u32[]{:S(2)}, u32[]{:S(2)}) collective-permute-start(bf16[4,32,1152]{2,1,0:T(8,128)(2,1)S(1)} %get-tuple-element.45), channel_id=1, source_target_pairs={{0,4},{4,0},{8,12},{12,8},{1,5},{5,1},{9,13},{13,9},{2,6},{6,2},{1... | collective-permute-start | bytes 884744 | tf_op jit(solution)/shard_map/ppermute | solution.py:452
  7.4 13.0 %collective-permute-start = (bf16[1472,128]{1,0:T(8,128)(2,1)S(1)}, bf16[1472,128]{1,0:T(8,128)(2,1)S(1)}, u32[]{:S(2)}, u32[]{:S(2)}) collective-permute-start(bf16[1472,128]{1,0:T(8,128)(2,1)S(1)} %get-tuple-element.42), channel_id=1, source_target_pairs={{0,1},{1,0},{2,3},{3,2},{4,5},{5,4},{6,7},{7,6},{8,9},{9,8},{10,11... | collective-permute-start | bytes 1130504 | tf_op jit(solution)/shard_map/ppermute | solution.py:452
  8.8 18.0 %collective-permute-start.1 = (bf16[1472,128]{1,0:T(8,128)(2,1)S(1)}, bf16[1472,128]{1,0:T(8,128)(2,1)S(1)}, u32[]{:S(2)}, u32[]{:S(2)}) collective-permute-start(bf16[1472,128]{1,0:T(8,128)(2,1)S(1)} %get-tuple-element.43), channel_id=1, source_target_pairs={{0,2},{1,3},{2,0},{3,1},{4,6},{5,7},{6,4},{7,5},{8,10},{9,11},{10,... | collective-permute-start | bytes 1130504 | tf_op jit(solution)/shard_map/ppermute | solution.py:452
  10.4 16.4 %collective-permute-start.2 = (bf16[1472,128]{1,0:T(8,128)(2,1)S(1)}, bf16[1472,128]{1,0:T(8,128)(2,1)S(1)}, u32[]{:S(2)}, u32[]{:S(2)}) collective-permute-start(bf16[1472,128]{1,0:T(8,128)(2,1)S(1)} %get-tuple-element.44), channel_id=1, source_target_pairs={{0,3},{1,2},{2,1},{3,0},{4,7},{5,6},{6,5},{7,4},{8,11},{9,10},{10,... | collective-permute-start | bytes 1130504 | tf_op jit(solution)/shard_map/ppermute | solution.py:452
  10.8 31.6 %collective-permute-start.7 = (bf16[4,32,1152]{2,1,0:T(8,128)(2,1)}, bf16[4,32,1152]{2,1,0:T(8,128)(2,1)}, u32[]{:S(2)}, u32[]{:S(2)}) collective-permute-start(bf16[4,32,1152]{2,1,0:T(8,128)(2,1)} %get-tuple-element.51), channel_id=1, source_target_pairs={{0,8},{4,12},{8,0},{12,4},{1,9},{5,13},{9,1},{13,5},{2,10},{6,14},... | collective-permute-start | bytes 884744 | tf_op jit(solution)/shard_map/ppermute | solution.py:452
  17.5 25.0 %collective-permute-start.8 = (bf16[4,32,1152]{2,1,0:T(8,128)(2,1)}, bf16[4,32,1152]{2,1,0:T(8,128)(2,1)}, u32[]{:S(2)}, u32[]{:S(2)}) collective-permute-start(bf16[4,32,1152]{2,1,0:T(8,128)(2,1)} %get-tuple-element.52), channel_id=1, source_target_pairs={{0,12},{4,8},{8,4},{12,0},{1,13},{5,9},{9,5},{13,1},{2,14},{6,10},... | collective-permute-start | bytes 884744 | tf_op jit(solution)/shard_map/ppermute | solution.py:452
  30.3 5.2 %collective-permute-start.4 = (bf16[288,128]{1,0:T(8,128)(2,1)S(1)}, bf16[288,128]{1,0:T(8,128)(2,1)S(1)}, u32[]{:S(2)}, u32[]{:S(2)}) collective-permute-start(bf16[288,128]{1,0:T(8,128)(2,1)S(1)} %get-tuple-element.47), channel_id=1, source_target_pairs={{0,1},{1,0},{2,3},{3,2},{4,5},{5,4},{6,7},{7,6},{8,9},{9,8},{10,11... | collective-permute-start | bytes 221192 | tf_op jit(solution)/shard_map/ppermute | solution.py:452
  31.7 4.4 %collective-permute-start.5 = (bf16[288,128]{1,0:T(8,128)(2,1)S(1)}, bf16[288,128]{1,0:T(8,128)(2,1)S(1)}, u32[]{:S(2)}, u32[]{:S(2)}) collective-permute-start(bf16[288,128]{1,0:T(8,128)(2,1)S(1)} %get-tuple-element.48), channel_id=1, source_target_pairs={{0,2},{1,3},{2,0},{3,1},{4,6},{5,7},{6,4},{7,5},{8,10},{9,11},{10,... | collective-permute-start | bytes 221192 | tf_op jit(solution)/shard_map/ppermute | solution.py:452
  32.4 5.3 %collective-permute-start.6 = (bf16[288,128]{1,0:T(8,128)(2,1)S(1)}, bf16[288,128]{1,0:T(8,128)(2,1)S(1)}, u32[]{:S(2)}, u32[]{:S(2)}) collective-permute-start(bf16[288,128]{1,0:T(8,128)(2,1)S(1)} %get-tuple-element.49), channel_id=1, source_target_pairs={{0,3},{1,2},{2,1},{3,0},{4,7},{5,6},{6,5},{7,4},{8,11},{9,10},{10,... | collective-permute-start | bytes 221192 | tf_op jit(solution)/shard_map/ppermute | solution.py:452
  38.0 6.3 %collective-permute-start.9 = (f32[8,128]{1,0:T(8,128)S(1)}, f32[8,128]{1,0:T(8,128)S(1)}, u32[]{:S(2)}, u32[]{:S(2)}) collective-permute-start(f32[8,128]{1,0:T(8,128)S(1)} %get-tuple-element.54), channel_id=1, source_target_pairs={{0,4},{4,0},{8,12},{12,8},{1,5},{5,1},{9,13},{13,9},{2,6},{6,2},{1... | collective-permute-start | bytes 12296 | tf_op jit(solution)/shard_map/ppermute | solution.py:452
  38.5 5.8 %collective-permute-start.10 = (f32[8,128]{1,0:T(8,128)S(1)}, f32[8,128]{1,0:T(8,128)S(1)}, u32[]{:S(2)}, u32[]{:S(2)}) collective-permute-start(f32[8,128]{1,0:T(8,128)S(1)} %get-tuple-element.55), channel_id=1, source_target_pairs={{0,8},{4,12},{8,0},{12,4},{1,9},{5,13},{9,1},{13,5},{2,10},{6,14},... | collective-permute-start | bytes 12296 | tf_op jit(solution)/shard_map/ppermute | solution.py:452
  41.1 5.4 %collective-permute-start.11 = (f32[8,128]{1,0:T(8,128)S(1)}, f32[8,128]{1,0:T(8,128)S(1)}, u32[]{:S(2)}, u32[]{:S(2)}) collective-permute-start(f32[8,128]{1,0:T(8,128)S(1)} %get-tuple-element.56), channel_id=1, source_target_pairs={{0,12},{4,8},{8,4},{12,0},{1,13},{5,9},{9,5},{13,1},{2,14},{6,10},... | collective-permute-start | bytes 12296 | tf_op jit(solution)/shard_map/ppermute | solution.py:452
  49.6 6.5 %collective-permute-start.14 = (f32[8,128]{1,0:T(8,128)S(1)}, f32[8,128]{1,0:T(8,128)S(1)}, u32[]{:S(2)}, u32[]{:S(2)}) collective-permute-start(f32[8,128]{1,0:T(8,128)S(1)} %get-tuple-element.61), channel_id=1, source_target_pairs={{0,4},{4,0},{8,12},{12,8},{1,5},{5,1},{9,13},{13,9},{2,6},{6,2},{1... | collective-permute-start | bytes 12296 | tf_op jit(solution)/shard_map/ppermute | solution.py:452
  49.7 6.4 %collective-permute-start.15 = (f32[8,128]{1,0:T(8,128)S(1)}, f32[8,128]{1,0:T(8,128)S(1)}, u32[]{:S(2)}, u32[]{:S(2)}) collective-permute-start(f32[8,128]{1,0:T(8,128)S(1)} %get-tuple-element.62), channel_id=1, source_target_pairs={{0,8},{4,12},{8,0},{12,4},{1,9},{5,13},{9,1},{13,5},{2,10},{6,14},... | collective-permute-start | bytes 12296 | tf_op jit(solution)/shard_map/ppermute | solution.py:452
  51.6 5.4 %collective-permute-start.16 = (f32[8,128]{1,0:T(8,128)S(1)}, f32[8,128]{1,0:T(8,128)S(1)}, u32[]{:S(2)}, u32[]{:S(2)}) collective-permute-start(f32[8,128]{1,0:T(8,128)S(1)} %get-tuple-element.63), channel_id=1, source_target_pairs={{0,12},{4,8},{8,4},{12,0},{1,13},{5,9},{9,5},{13,1},{2,14},{6,10},... | collective-permute-start | bytes 12296 | tf_op jit(solution)/shard_map/ppermute | solution.py:452
  54.1 4.4 %collective-permute-start.12 = (bf16[32,1152]{1,0:T(8,128)(2,1)S(1)}, bf16[32,1152]{1,0:T(8,128)(2,1)S(1)}, u32[]{:S(2)}, u32[]{:S(2)}) collective-permute-start(bf16[32,1152]{1,0:T(8,128)(2,1)S(1)} %get-tuple-element.58), channel_id=1, source_target_pairs={{0,4},{4,0},{8,12},{12,8},{1,5},{5,1},{9,13},{13,9},{2,6},{6,2},{1... | collective-permute-start | bytes 221192 | tf_op jit(solution)/shard_map/ppermute | solution.py:452
  54.2 9.4 %collective-permute-start.13 = (bf16[32,1152]{1,0:T(8,128)(2,1)S(1)}, bf16[32,1152]{1,0:T(8,128)(2,1)S(1)}, u32[]{:S(2)}, u32[]{:S(2)}) collective-permute-start(bf16[32,1152]{1,0:T(8,128)(2,1)S(1)} %get-tuple-element.59), channel_id=1, source_target_pairs={{0,8},{4,12},{8,0},{12,4},{1,9},{5,13},{9,1},{13,5},{2,10},{6,14},... | collective-permute-start | bytes 221192 | tf_op jit(solution)/shard_map/ppermute | solution.py:452
  58.5 5.0 %collective-permute-start.20 = (bf16[32,128]{1,0:T(8,128)(2,1)S(1)}, bf16[32,128]{1,0:T(8,128)(2,1)S(1)}, u32[]{:S(2)}, u32[]{:S(2)}) collective-permute-start(bf16[32,128]{1,0:T(8,128)(2,1)S(1)} %get-tuple-element.69.refs_11_), channel_id=1, source_target_pairs={{0,3},{1,2},{2,1},{3,0},{4,7},{5,6},{6,5},{7,4},{8,11},{9,10},{10,... | collective-permute-start | bytes 24584 | tf_op jit(solution)/shard_map/ppermute | solution.py:452
  60.0 3.7 %collective-permute-start.19 = (bf16[32,128]{1,0:T(8,128)(2,1)S(1)}, bf16[32,128]{1,0:T(8,128)(2,1)S(1)}, u32[]{:S(2)}, u32[]{:S(2)}) collective-permute-start(bf16[32,128]{1,0:T(8,128)(2,1)S(1)} %get-tuple-element.69.refs_11_), channel_id=1, source_target_pairs={{0,2},{1,3},{2,0},{3,1},{4,6},{5,7},{6,4},{7,5},{8,10},{9,11},{10,... | collective-permute-start | bytes 24584 | tf_op jit(solution)/shard_map/ppermute | solution.py:452
  61.6 3.7 %collective-permute-start.18 = (bf16[32,128]{1,0:T(8,128)(2,1)S(1)}, bf16[32,128]{1,0:T(8,128)(2,1)S(1)}, u32[]{:S(2)}, u32[]{:S(2)}) collective-permute-start(bf16[32,128]{1,0:T(8,128)(2,1)S(1)} %get-tuple-element.69.refs_11_), channel_id=1, source_target_pairs={{0,1},{1,0},{2,3},{3,2},{4,5},{5,4},{6,7},{7,6},{8,9},{9,8},{10,11... | collective-permute-start | bytes 24584 | tf_op jit(solution)/shard_map/ppermute | solution.py:452
  62.1 6.2 %collective-permute-start.17 = (bf16[32,1152]{1,0:T(8,128)(2,1)S(1)}, bf16[32,1152]{1,0:T(8,128)(2,1)S(1)}, u32[]{:S(2)}, u32[]{:S(2)}) collective-permute-start(bf16[32,1152]{1,0:T(8,128)(2,1)S(1)} %get-tuple-element.65), channel_id=1, source_target_pairs={{0,12},{4,8},{8,4},{12,0},{1,13},{5,9},{9,5},{13,1},{2,14},{6,10},... | collective-permute-start | bytes 221192 | tf_op jit(solution)/shard_map/ppermute | solution.py:452
  71.1 4.4 %collective-permute-start.21 = (bf16[32,1088]{1,0:T(8,128)(2,1)S(1)}, bf16[32,1088]{1,0:T(8,128)(2,1)S(1)}, u32[]{:S(2)}, u32[]{:S(2)}) collective-permute-start(bf16[32,1088]{1,0:T(8,128)(2,1)S(1)} %get-tuple-element.72), channel_id=1, source_target_pairs={{0,1},{1,0},{2,3},{3,2},{4,5},{5,4},{6,7},{7,6},{8,9},{9,8},{10,11... | collective-permute-start | bytes 208904 | tf_op jit(solution)/shard_map/ppermute | solution.py:452
  72.7 4.4 %collective-permute-start.22 = (bf16[32,1088]{1,0:T(8,128)(2,1)S(1)}, bf16[32,1088]{1,0:T(8,128)(2,1)S(1)}, u32[]{:S(2)}, u32[]{:S(2)}) collective-permute-start(bf16[32,1088]{1,0:T(8,128)(2,1)S(1)} %get-tuple-element.73), channel_id=1, source_target_pairs={{0,2},{1,3},{2,0},{3,1},{4,6},{5,7},{6,4},{7,5},{8,10},{9,11},{10,... | collective-permute-start | bytes 208904 | tf_op jit(solution)/shard_map/ppermute | solution.py:452
  73.1 5.3 %collective-permute-start.23 = (bf16[32,1088]{1,0:T(8,128)(2,1)S(1)}, bf16[32,1088]{1,0:T(8,128)(2,1)S(1)}, u32[]{:S(2)}, u32[]{:S(2)}) collective-permute-start(bf16[32,1088]{1,0:T(8,128)(2,1)S(1)} %get-tuple-element.74), channel_id=1, source_target_pairs={{0,3},{1,2},{2,1},{3,0},{4,7},{5,6},{6,5},{7,4},{8,11},{9,10},{10,... | collective-permute-start | bytes 208904 | tf_op jit(solution)/shard_map/ppermute | solution.py:452
  78.7 1.3 %collective-permute-start.24 = (f32[32,576]{1,0:T(8,128)S(1)}, f32[32,576]{1,0:T(8,128)S(1)}, u32[]{:S(2)}, u32[]{:S(2)}) collective-permute-start(f32[32,576]{1,0:T(8,128)S(1)} %get-tuple-element.76), channel_id=1, source_target_pairs={{0,16},{16,0},{1,17},{17,1},{2,18},{18,2},{3,19},{19,3},{4,20},{20... | collective-permute-start | bytes 221192 | tf_op jit(solution)/shard_map/ppermute | solution.py:452
  80.0 6.0 %collective-permute-start.27 = (bf16[32,576]{1,0:T(8,128)(2,1)S(1)}, bf16[32,576]{1,0:T(8,128)(2,1)S(1)}, u32[]{:S(2)}, u32[]{:S(2)}) collective-permute-start(bf16[32,576]{1,0:T(8,128)(2,1)S(1)} %shard_map.130.refs_0_), channel_id=1, source_target_pairs={{0,12},{4,8},{8,4},{12,0},{1,13},{5,9},{9,5},{13,1},{2,14},{6,10},... | collective-permute-start | bytes 110600 | tf_op jit(solution)/shard_map/ppermute | solution.py:452
  81.5 5.8 %collective-permute-start.26 = (bf16[32,576]{1,0:T(8,128)(2,1)S(1)}, bf16[32,576]{1,0:T(8,128)(2,1)S(1)}, u32[]{:S(2)}, u32[]{:S(2)}) collective-permute-start(bf16[32,576]{1,0:T(8,128)(2,1)S(1)} %shard_map.130.refs_0_), channel_id=1, source_target_pairs={{0,8},{4,12},{8,0},{12,4},{1,9},{5,13},{9,1},{13,5},{2,10},{6,14},... | collective-permute-start | bytes 110600 | tf_op jit(solution)/shard_map/ppermute | solution.py:452
  81.5 5.8 %collective-permute-start.25 = (bf16[32,576]{1,0:T(8,128)(2,1)S(1)}, bf16[32,576]{1,0:T(8,128)(2,1)S(1)}, u32[]{:S(2)}, u32[]{:S(2)}) collective-permute-start(bf16[32,576]{1,0:T(8,128)(2,1)S(1)} %shard_map.130.refs_0_), channel_id=1, source_target_pairs={{0,4},{4,0},{8,12},{12,8},{1,5},{5,1},{9,13},{13,9},{2,6},{6,2},{1... | collective-permute-start | bytes 110600 | tf_op jit(solution)/shard_map/ppermute | solution.py:452
  87.3 5.0 %collective-permute-start.30 = (bf16[32,576]{1,0:T(8,128)(2,1)S(1)}, bf16[32,576]{1,0:T(8,128)(2,1)S(1)}, u32[]{:S(2)}, u32[]{:S(2)}) collective-permute-start(bf16[32,576]{1,0:T(8,128)(2,1)S(1)} %shard_map.131.refs_0_), channel_id=1, source_target_pairs={{0,3},{1,2},{2,1},{3,0},{4,7},{5,6},{6,5},{7,4},{8,11},{9,10},{10,... | collective-permute-start | bytes 110600 | tf_op jit(solution)/shard_map/ppermute | solution.py:452
  88.9 4.0 %collective-permute-start.29 = (bf16[32,576]{1,0:T(8,128)(2,1)S(1)}, bf16[32,576]{1,0:T(8,128)(2,1)S(1)}, u32[]{:S(2)}, u32[]{:S(2)}) collective-permute-start(bf16[32,576]{1,0:T(8,128)(2,1)S(1)} %shard_map.131.refs_0_), channel_id=1, source_target_pairs={{0,2},{1,3},{2,0},{3,1},{4,6},{5,7},{6,4},{7,5},{8,10},{9,11},{10,... | collective-permute-start | bytes 110600 | tf_op jit(solution)/shard_map/ppermute | solution.py:452
  90.1 4.0 %collective-permute-start.28 = (bf16[32,576]{1,0:T(8,128)(2,1)S(1)}, bf16[32,576]{1,0:T(8,128)(2,1)S(1)}, u32[]{:S(2)}, u32[]{:S(2)}) collective-permute-start(bf16[32,576]{1,0:T(8,128)(2,1)S(1)} %shard_map.131.refs_0_), channel_id=1, source_target_pairs={{0,1},{1,0},{2,3},{3,2},{4,5},{5,4},{6,7},{7,6},{8,9},{9,8},{10,11... | collective-permute-start | bytes 110600 | tf_op jit(solution)/shard_map/ppermute | solution.py:452
  94.3 1.4 %collective-permute-start.31 = (bf16[64,1152]{1,0:T(8,128)(2,1)S(1)}, bf16[64,1152]{1,0:T(8,128)(2,1)S(1)}, u32[]{:S(2)}, u32[]{:S(2)}) collective-permute-start(bf16[64,1152]{1,0:T(8,128)(2,1)S(1)} %shard_map.132.refs_0_), channel_id=1, source_target_pairs={{0,16},{16,0},{1,17},{17,1},{2,18},{18,2},{3,19},{19,3},{4,20},{20... | collective-permute-start | bytes 442376 | tf_op jit(solution)/shard_map/ppermute | solution.py:452
  (4 other events, 116.1 us)

commit v12 on v10

--- a/solution.py
+++ b/solution.py
@@ -1,4 +1,5 @@
 import functools
+import math
 
 import jax
 import jax.numpy as jnp
@@ -126,11 +127,10 @@
     send(value, 2)
     copies[5].wait()
     send(flat(k_buf), 1)
-    send(patches, 3)
     copies[6].wait()
-    send(flat(g_buf), 4)
+    send(flat(g_buf), 3)
     for k in range(n_s):
-        outs[k][5 * d_s :] = codes_t
+        outs[k][4 * d_s :] = codes_t
     for index, copy in enumerate(time_copies):
         copy.wait()
         for k in range(1, n_t):
@@ -322,10 +322,10 @@
     ups = jnp.concatenate([at_here_ref[2], at_here_ref[3]], axis=0).T
     grads = []
     for k in range(n_s):
-        cot = packed[k][4 * d_s : 5 * d_s].astype(F32)
+        cot = packed[k][3 * d_s : 4 * d_s].astype(F32)
         grads.append((cot + mm(ups, dcodes[k][...])).astype(BF16))
     grad_b_q = grad_b_v = None
-    codes = [x[5 * d_s :] for x in packed]
+    codes = [x[4 * d_s :] for x in packed]
     for f in range(frames):
         keys = qkv_ref[1, f].astype(F32)
         vals = qkv_ref[2, f].astype(F32)
@@ -348,11 +348,9 @@
         d_query = jnp.concatenate(d_query, axis=0).astype(BF16)
         d_vals = jnp.concatenate(d_vals, axis=0).astype(BF16)
         partial = jnp.concatenate([mm(b_here_ref[0], d_query), mm(b_here_ref[1], d_vals)], axis=0)
-        partial = partial.astype(BF16)
-        blocks = [partial[:, m * patch_dev : (m + 1) * patch_dev] for m in range(n_s)]
         for k in range(n_s):
-            turned = jnp.concatenate([blocks[m ^ k] for m in range(n_s)], axis=1)
-            sends[k][:, f * total : (f + 1) * total] = turned
+            place = slice(f * patch_dev, (f + 1) * patch_dev)
+            sends[k][:, place] = partial[:, k * patch_dev : (k + 1) * patch_dev].astype(BF16)
         frame_codes = frame_rows(codes, f, patch_dev)
         term_q = mm(frame_codes[:RANK], d_query, NT)
         term_v = mm(frame_codes[RANK:], d_vals, NT)
@@ -366,7 +364,7 @@
         cut_buf[j, :, :d_s] = grad_a[:, here].astype(BF16)
         cut_buf[j, :, d_s:] = grad_b_ref[:, here].astype(BF16)
     for k in range(n_s):
-        sends[k][:, frames * total :] = cut_buf[peer("space", k)]
+        sends[k][:, tokens:] = cut_buf[peer("space", k)]
 
 
 def add_up(terms):
@@ -376,26 +374,23 @@
     return result
 
 
-def merge_kernel(frames, n_s, n_d, part_ref, *refs):
-    packed, recvs, refs = refs[:n_s], refs[n_s : 2 * n_s], refs[2 * n_s :]
-    sends, buf = refs[:n_d], refs[n_d]
+def merge_kernel(n_s, n_d, part_ref, patches_ref, *refs):
+    recvs, sends, buf = refs[:n_s], refs[n_s : n_s + n_d], refs[n_s + n_d]
     d_s = part_ref.shape[1]
-    tokens = packed[0].shape[1]
-    patch_dev = tokens // frames
-    total = n_s * patch_dev
-    patches = [x[3 * d_s : 4 * d_s] for x in packed]
-    terms = []
-    for f in range(frames):
-        codes = [recv[:, f * total : (f + 1) * total].astype(F32) for recv in recvs]
-        terms.append(mm(add_up(codes).astype(BF16), frame_rows(patches, f, patch_dev), NT))
-    start = frames * total
-    time_a = add_up([recv[:, start : start + d_s].astype(F32) for recv in recvs])
-    time_b = add_up([recv[:, start + d_s : start + 2 * d_s].astype(F32) for recv in recvs])
-    rows = jnp.concatenate([add_up(terms), time_a, part_ref[...], time_b], axis=0)
-    per = rows.shape[0] // n_d
+    tokens = recvs[0].shape[1] - 2 * d_s
+    codes = add_up([recv[:, :tokens].astype(F32) for recv in recvs]).astype(BF16)
+    full = mm(codes, patches_ref[0].reshape(tokens, n_s * d_s))
+    time_a = add_up([recv[:, tokens : tokens + d_s].astype(F32) for recv in recvs])
+    time_b = add_up([recv[:, tokens + d_s :].astype(F32) for recv in recvs])
+    split = jnp.concatenate([time_a, part_ref[...], time_b], axis=0)
+    per, per_full = split.shape[0] // n_d, full.shape[0] // n_d
     for d in range(n_d):
-        mine = rows[d * per : (d + 1) * per]
-        buf[d] = jnp.concatenate([mine[: per // 2], mine[per // 2 :]], axis=1)
+        mine = [split[d * per : (d + 1) * per]]
+        rows = full[d * per_full : (d + 1) * per_full]
+        mine += [rows[:, j * d_s : (j + 1) * d_s] for j in range(n_s)]
+        mine = jnp.concatenate(mine, axis=0)
+        half = mine.shape[0] // 2
+        buf[d] = jnp.concatenate([mine[:half], mine[half:]], axis=1)
     for k in range(n_d):
         sends[k][...] = buf[peer("dp", k)]
 
@@ -407,29 +402,34 @@
     refs[-1][...] = terms[0].astype(refs[-1].dtype)
 
 
-def join_kernel(*refs):
+def join_kernel(n_full, *refs):
     pieces, (out_ref, buf) = refs[:-2], refs[-2:]
+    n_s, d_s = len(pieces), buf.shape[2] // 2
     for k, piece in enumerate(pieces):
         buf[peer("space", k)] = piece[...]
-    half, d_s = buf.shape[1], buf.shape[2] // 2
-    for h in range(2):
-        cuts = [buf[j, :, h * d_s : (h + 1) * d_s] for j in range(len(pieces))]
-        out_ref[h * half : (h + 1) * half] = jnp.concatenate(cuts, axis=1)
-
-
-def final_kernel(factor, n_d, *refs):
+    rows = [
+        jnp.concatenate([buf[j, :, :d_s], buf[j, :, d_s:]], axis=0).astype(F32) for j in range(n_s)
+    ]
+    n_split = rows[0].shape[0] - n_s * n_full
+    out_ref[n_full:] = jnp.concatenate([x[:n_split] for x in rows], axis=1).astype(BF16)
+    full = add_up([x[n_split:] for x in rows])
+    cuts = [full[j * n_full : (j + 1) * n_full] for j in range(n_s)]
+    out_ref[:n_full] = jnp.concatenate(cuts, axis=1).astype(BF16)
+
+
+def final_kernel(factor, n_d, n_full, *refs):
     pieces, (a_ref, b_ref, buf) = refs[:n_d], refs[n_d:]
     for k, piece in enumerate(pieces):
         buf[peer("dp", k)] = piece[...]
-    per = pieces[0].shape[0]
-    half = n_d // 2
+    n_split = pieces[0].shape[0] - n_full
+    size = math.gcd(n_full, n_split, RANK)
     for d in range(n_d):
         rows = buf[d].astype(F32) * factor
-        target = a_ref if d < half else b_ref
-        for r in range(0, per, min(per, RANK)):
-            start = (d % half) * per + r
-            size = min(per, RANK)
-            target[start // RANK, start % RANK : start % RANK + size] = rows[r : r + size]
+        for r in range(0, n_full + n_split, size):
+            row = d * n_full + r if r < n_full else 2 * RANK + d * n_split + r - n_full
+            target = a_ref if row < 4 * RANK else b_ref
+            row %= 4 * RANK
+            target[row // RANK, row % RANK : row % RANK + size] = rows[r : r + size]
 
 
 def mixed_kernel(frames, hidden_ref, *refs):
@@ -484,13 +484,13 @@
     ]
     packed = call(
         functools.partial(pack_kernel, n_s, n_t, sub),
-        [shape((5 * d_s + 2 * RANK, tokens), BF16)] * n_s
+        [shape((4 * d_s + 2 * RANK, tokens), BF16)] * n_s
         + [shape((4, frames * sub, width), BF16)] * (n_t - 1),
         *space_arrays, *time_arrays,
         scratch=[pltpu.VMEM(x.shape, BF16) for x in space_arrays]
         + [
             pltpu.VMEM((4,) + query_t.shape, BF16),
-            pltpu.VMEM((5, n_s, d_s, tokens), BF16),
+            pltpu.VMEM((4, n_s, d_s, tokens), BF16),
             dma((7,)),
             dma((4,)),
         ],
@@ -546,7 +546,7 @@
     dcodes = share(dcodes, "space")
     backward = call(
         functools.partial(space_backward_kernel, frames, n_s),
-        [shape((2 * RANK, frames * total + 2 * d_s), BF16)] * n_s + [shape((2 * RANK, d_s), F32)],
+        [shape((2 * RANK, tokens + 2 * d_s), BF16)] * n_s + [shape((2 * RANK, d_s), F32)],
         qkv, probs, hidden, time_grad_b, downs, downs_here, ups_here, *packed, *dcodes,
         scratch=[pltpu.VMEM((n_s, 2 * RANK, 2 * d_s), BF16)],
         after=out_t[1:3],
@@ -555,26 +555,28 @@
     partial, part = backward[:n_s], backward[n_s]
     partial = exchange(partial, "space")
     out_t[3:] = hops(backward[n_s + 1 :], "tm", 3)
-    rows = 8 * RANK // n_d
+    n_full, n_split = 2 * RANK // n_d, 6 * RANK // n_d
+    dims = ((n_s * n_full + n_split) // 2, 2 * d_s)
     sums = call(
-        functools.partial(merge_kernel, frames, n_s, n_d),
-        [shape((rows // 2, 2 * d_s), F32)] * n_d,
-        part, *packed, *partial,
-        scratch=[pltpu.VMEM((n_d, rows // 2, 2 * d_s), F32)],
-    )
-    sums = call(total_kernel, shape((rows // 2, 2 * d_s), BF16), *exchange(sums, "dp"), after=out_t[3:])
-    sums = call(total_kernel, shape((rows // 2, 2 * d_s), BF16), *share(sums, "tm"))
+        functools.partial(merge_kernel, n_s, n_d),
+        [shape(dims, F32)] * n_d,
+        part, patches, *partial,
+        scratch=[pltpu.VMEM((n_d,) + dims, F32)],
+        after=out_t[3:],
+    )
+    sums = call(total_kernel, shape(dims, BF16), *exchange(sums, "dp"))
+    sums = call(total_kernel, shape(dims, BF16), *share(sums, "tm"))
     sums = call(
-        join_kernel,
-        shape((rows, width), BF16),
+        functools.partial(join_kernel, n_full),
+        shape((n_full + n_split, width), BF16),
         *share(sums, "space"),
-        scratch=[pltpu.VMEM((n_s, rows // 2, 2 * d_s), BF16)],
+        scratch=[pltpu.VMEM((n_s,) + dims, BF16)],
     )
     grads_a, grads_b = call(
-        functools.partial(final_kernel, factor, n_d),
+        functools.partial(final_kernel, factor, n_d, n_full),
         [shape((4, RANK, width), F32)] * 2,
         *share(sums, "dp"),
-        scratch=[pltpu.VMEM((n_d, rows, width), BF16)],
+        scratch=[pltpu.VMEM((n_d, n_full + n_split, width), BF16)],
     )
     mixed = call(
         functools.partial(mixed_kernel, frames),

time: 92.6 us -> 93.3 us (level)
  transfers between devices with their start and end apart: 32 -> 32, of which waited for: 18 -> 19; matrix products, arithmetic and copies ran while one was open for 0% -> 0% of each run, Pallas kernels for 7% -> 7%
where the time goes in v12:
time: 93.3 us; the launch traced here: 93.1 us
  starting transfers between devices  44.2 us (47%)
  waiting for transfers between devices  30.4 us (33%)
  Pallas kernels  17.5 us (19%)
    ppermute x32, starting transfers between devices, hops(): lax.ppermute(array, axis, [(i, i ^ k) for i in range(size)])  44.2 us
    ppermute x32, waiting for transfers between devices, hops(): lax.ppermute(array, axis, [(i, i ^ k) for i in range(size)])  30.4 us
    pallas_call x13, Pallas kernels, call(): pl.pallas_call(body, out_shape=outs + tuple((shape(x.shape, x.dtype) for...  17.5 us
  transfers between devices with their start and end apart: 32, of which 19 were waited for; matrix products, arithmetic and copies ran while one was open for 0% of the time, Pallas kernels for 7%

profile of v12, /device:TPU:0, one launch (start us, length us, event | category | flops | bytes accessed | tf_op | source)
XLA Modules:
  0.0 93.1 jit_solution(9359572415094887895)
XLA Ops:
  0.7 3.5 %shard_map.121 = (bf16[1184,128]{1,0:T(8,128)(2,1)S(1)}, bf16[1184,128]{1,0:T(8,128)(2,1)S(1)}, bf16[1184,128]{1,0:T(8,128)(2,1)S(1)}, bf16[1184,128]{1,0:T(8,12...) custom-call(bf16[1,2,64,1152]{3,2,1,0:T(8,128)(2,1)} %refs_1_.5, ...), custom_call_target="tpu_custom_call" | custom-call | tf_op jit(solution)/shard_map/pallas_call | solution.py:41
  4.1 3.1 %collective-permute-start.3 = (bf16[4,32,1152]{2,1,0:T(8,128)(2,1)S(1)}, bf16[4,32,1152]{2,1,0:T(8,128)(2,1)S(1)}, u32[]{:S(2)}, u32[]{:S(2)}) collective-permute-start(bf16[4,32,1152]{2,1,0:T(8,128)(2,1)S(1)} %get-tuple-element.44), channel_id=1, source_target_pairs={{0,4},{4,0},{8,12},{12,8},{1,5},{5,1},{9,13},{13,9},{2,6},{6,2},{1... | collective-permute-start | bytes 884744 | tf_op jit(solution)/shard_map/ppermute | solution.py:452
  7.2 1.5 %collective-permute-start = (bf16[1184,128]{1,0:T(8,128)(2,1)S(1)}, bf16[1184,128]{1,0:T(8,128)(2,1)S(1)}, u32[]{:S(2)}, u32[]{:S(2)}) collective-permute-start(bf16[1184,128]{1,0:T(8,128)(2,1)S(1)} %get-tuple-element.41), channel_id=1, source_target_pairs={{0,1},{1,0},{2,3},{3,2},{4,5},{5,4},{6,7},{7,6},{8,9},{9,8},{10,11... | collective-permute-start | bytes 909320 | tf_op jit(solution)/shard_map/ppermute | solution.py:452
  8.7 1.6 %collective-permute-start.1 = (bf16[1184,128]{1,0:T(8,128)(2,1)S(1)}, bf16[1184,128]{1,0:T(8,128)(2,1)S(1)}, u32[]{:S(2)}, u32[]{:S(2)}) collective-permute-start(bf16[1184,128]{1,0:T(8,128)(2,1)S(1)} %get-tuple-element.42), channel_id=1, source_target_pairs={{0,2},{1,3},{2,0},{3,1},{4,6},{5,7},{6,4},{7,5},{8,10},{9,11},{10,... | collective-permute-start | bytes 909320 | tf_op jit(solution)/shard_map/ppermute | solution.py:452
  10.7 2.6 %collective-permute-start.7 = (bf16[4,32,1152]{2,1,0:T(8,128)(2,1)}, bf16[4,32,1152]{2,1,0:T(8,128)(2,1)}, u32[]{:S(2)}, u32[]{:S(2)}) collective-permute-start(bf16[4,32,1152]{2,1,0:T(8,128)(2,1)} %get-tuple-element.50), channel_id=1, source_target_pairs={{0,8},{4,12},{8,0},{12,4},{1,9},{5,13},{9,1},{13,5},{2,10},{6,14},... | collective-permute-start | bytes 884744 | tf_op jit(solution)/shard_map/ppermute | solution.py:452
  13.3 4.1 %collective-permute-done.3.refs_4_ = bf16[4,32,1152]{2,1,0:T(8,128)(2,1)S(1)} collective-permute-done((bf16[4,32,1152]{2,1,0:T(8,128)(2,1)S(1)}, bf16[4,32,1152]{2,1,0:T(8,128)(2,1)S(1)}, u32[]{:S(2)}, u32[]{:S(2)}) %collective-permute-start.3) | collective-permute-done | bytes 294944 | tf_op jit(solution)/shard_map/ppermute | solution.py:452
  17.4 2.9 %collective-permute-start.8 = (bf16[4,32,1152]{2,1,0:T(8,128)(2,1)}, bf16[4,32,1152]{2,1,0:T(8,128)(2,1)}, u32[]{:S(2)}, u32[]{:S(2)}) collective-permute-start(bf16[4,32,1152]{2,1,0:T(8,128)(2,1)} %get-tuple-element.51), channel_id=1, source_target_pairs={{0,12},{4,8},{8,4},{12,0},{1,13},{5,9},{9,5},{13,1},{2,14},{6,10},... | collective-permute-start | bytes 884744 | tf_op jit(solution)/shard_map/ppermute | solution.py:452
  20.2 3.4 %collective-permute-done.1.refs_2_.refs_9_ = bf16[1184,128]{1,0:T(8,128)(2,1)S(1)} collective-permute-done((bf16[1184,128]{1,0:T(8,128)(2,1)S(1)}, bf16[1184,128]{1,0:T(8,128)(2,1)S(1)}, u32[]{:S(2)}, u32[]{:S(2)}) %collective-permute-start.1) | collective-permute-done | bytes 303136 | tf_op jit(solution)/shard_map/ppermute | solution.py:452
  23.6 3.4 %shard_map.122 = (bf16[3,2,288,256]{3,2,1,0:T(8,128)(2,1)S(1)}, f32[2,4,256,256]{3,2,1,0:T(8,128)}, bf16[288,128]{1,0:T(8,128)(2,1)S(1)}, bf16[288,128]{1,0:T(8,...) custom-call(bf16[1184,128]{1,0:T(8,128)(2,1)S(1)} %get-tuple-element.40.refs_0_.refs_7_, ...), custom_call_target="tpu_custom_call" | custom-call | tf_op jit(solution)/shard_map/pallas_call | solution.py:41
  27.1 1.4 %collective-permute-start.4 = (bf16[288,128]{1,0:T(8,128)(2,1)S(1)}, bf16[288,128]{1,0:T(8,128)(2,1)S(1)}, u32[]{:S(2)}, u32[]{:S(2)}) collective-permute-start(bf16[288,128]{1,0:T(8,128)(2,1)S(1)} %get-tuple-element.46), channel_id=1, source_target_pairs={{0,1},{1,0},{2,3},{3,2},{4,5},{5,4},{6,7},{7,6},{8,9},{9,8},{10,11... | collective-permute-start | bytes 221192 | tf_op jit(solution)/shard_map/ppermute | solution.py:452
  29.2 1.4 %collective-permute-start.6 = (bf16[288,128]{1,0:T(8,128)(2,1)S(1)}, bf16[288,128]{1,0:T(8,128)(2,1)S(1)}, u32[]{:S(2)}, u32[]{:S(2)}) collective-permute-start(bf16[288,128]{1,0:T(8,128)(2,1)S(1)} %get-tuple-element.48), channel_id=1, source_target_pairs={{0,3},{1,2},{2,1},{3,0},{4,7},{5,6},{6,5},{7,4},{8,11},{9,10},{10,... | collective-permute-start | bytes 221192 | tf_op jit(solution)/shard_map/ppermute | solution.py:452
  30.6 1.6 %collective-permute-done.4.refs_1_ = bf16[288,128]{1,0:T(8,128)(2,1)S(1)} collective-permute-done((bf16[288,128]{1,0:T(8,128)(2,1)S(1)}, bf16[288,128]{1,0:T(8,128)(2,1)S(1)}, u32[]{:S(2)}, u32[]{:S(2)}) %collective-permute-start.4) | collective-permute-done | bytes 73760 | tf_op jit(solution)/shard_map/ppermute | solution.py:452
  32.8 1.7 %collective-permute-done.6.refs_3_ = bf16[288,128]{1,0:T(8,128)(2,1)S(1)} collective-permute-done((bf16[288,128]{1,0:T(8,128)(2,1)S(1)}, bf16[288,128]{1,0:T(8,128)(2,1)S(1)}, u32[]{:S(2)}, u32[]{:S(2)}) %collective-permute-start.6) | collective-permute-done | bytes 73760 | tf_op jit(solution)/shard_map/ppermute | solution.py:452
  35.3 2.6 %collective-permute-start.10 = (f32[8,128]{1,0:T(8,128)S(1)}, f32[8,128]{1,0:T(8,128)S(1)}, u32[]{:S(2)}, u32[]{:S(2)}) collective-permute-start(f32[8,128]{1,0:T(8,128)S(1)} %get-tuple-element.54), channel_id=1, source_target_pairs={{0,8},{4,12},{8,0},{12,4},{1,9},{5,13},{9,1},{13,5},{2,10},{6,14},... | collective-permute-start | bytes 12296 | tf_op jit(solution)/shard_map/ppermute | solution.py:452
  39.2 1.8 %shard_map.124.refs_0_ = bf16[4,1152,128]{2,1,0:T(8,128)(2,1)S(1)} custom-call(bf16[1,2,64,1152]{3,2,1,0:T(8,128)(2,1)} %refs_0_.3, bf16[1,2,64,1152]{3,2,1,0:T(8,128)(2,1)} %refs_1_.3, bf16[1,2,64,1152]{3,2,1,0:T(8,128)(2,1)} %refs_2_.3, bf16[1,2,64,1152]{3,2,1,0:T(8,128)(2,1)} %refs_3_.3, bf16[4,32,1152]{2,1,0:T(8,128)(2,1)S(1)} %collective-permute-done.3.refs_4_, ...), custom_call_target="tpu_custom_call" | custom-call | tf_op jit(solution)/shard_map/pallas_call | solution.py:41
  41.1 2.2 %collective-permute-done.11.refs_5_ = f32[8,128]{1,0:T(8,128)S(1)} collective-permute-done((f32[8,128]{1,0:T(8,128)S(1)}, f32[8,128]{1,0:T(8,128)S(1)}, u32[]{:S(2)}, u32[]{:S(2)}) %collective-permute-start.11) | collective-permute-done | bytes 4128 | tf_op jit(solution)/shard_map/ppermute | solution.py:452
  43.3 3.1 %shard_map.125 = (bf16[32,1152]{1,0:T(8,128)(2,1)S(1)}, bf16[32,1152]{1,0:T(8,128)(2,1)S(1)}, bf16[32,1152]{1,0:T(8,128)(2,1)S(1)}, bf16[32,1152]{1,0:T(8,128)(2...) custom-call(bf16[4,1152,128]{2,1,0:T(8,128)(2,1)S(1)} %shard_map.124, ...), custom_call_target="tpu_custom_call" | custom-call | tf_op jit(solution)/shard_map/pallas_call | solution.py:41
  46.4 1.9 %collective-permute-start.15 = (f32[8,128]{1,0:T(8,128)S(1)}, f32[8,128]{1,0:T(8,128)S(1)}, u32[]{:S(2)}, u32[]{:S(2)}) collective-permute-start(f32[8,128]{1,0:T(8,128)S(1)} %get-tuple-element.64), channel_id=1, source_target_pairs={{0,8},{4,12},{8,0},{12,4},{1,9},{5,13},{9,1},{13,5},{2,10},{6,14},... | collective-permute-start | bytes 12296 | tf_op jit(solution)/shard_map/ppermute | solution.py:452
  48.3 2.5 %collective-permute-start.16 = (f32[8,128]{1,0:T(8,128)S(1)}, f32[8,128]{1,0:T(8,128)S(1)}, u32[]{:S(2)}, u32[]{:S(2)}) collective-permute-start(f32[8,128]{1,0:T(8,128)S(1)} %get-tuple-element.65), channel_id=1, source_target_pairs={{0,12},{4,8},{8,4},{12,0},{1,13},{5,9},{9,5},{13,1},{2,14},{6,10},... | collective-permute-start | bytes 12296 | tf_op jit(solution)/shard_map/ppermute | solution.py:452
  51.0 1.9 %collective-permute-start.13 = (bf16[32,1152]{1,0:T(8,128)(2,1)S(1)}, bf16[32,1152]{1,0:T(8,128)(2,1)S(1)}, u32[]{:S(2)}, u32[]{:S(2)}) collective-permute-start(bf16[32,1152]{1,0:T(8,128)(2,1)S(1)} %get-tuple-element.58), channel_id=1, source_target_pairs={{0,8},{4,12},{8,0},{12,4},{1,9},{5,13},{9,1},{13,5},{2,10},{6,14},... | collective-permute-start | bytes 221192 | tf_op jit(solution)/shard_map/ppermute | solution.py:452
  53.9 1.5 %collective-permute-start.19 = (bf16[32,128]{1,0:T(8,128)(2,1)S(1)}, bf16[32,128]{1,0:T(8,128)(2,1)S(1)}, u32[]{:S(2)}, u32[]{:S(2)}) collective-permute-start(bf16[32,128]{1,0:T(8,128)(2,1)S(1)} %shard_map.126.refs_11_), channel_id=1, source_target_pairs={{0,3},{1,2},{2,1},{3,0},{4,7},{5,6},{6,5},{7,4},{8,11},{9,10},{10,... | collective-permute-start | bytes 24584 | tf_op jit(solution)/shard_map/ppermute | solution.py:452
  55.3 1.6 %collective-permute-start.18 = (bf16[32,128]{1,0:T(8,128)(2,1)S(1)}, bf16[32,128]{1,0:T(8,128)(2,1)S(1)}, u32[]{:S(2)}, u32[]{:S(2)}) collective-permute-start(bf16[32,128]{1,0:T(8,128)(2,1)S(1)} %shard_map.126.refs_11_), channel_id=1, source_target_pairs={{0,2},{1,3},{2,0},{3,1},{4,6},{5,7},{6,4},{7,5},{8,10},{9,11},{10,... | collective-permute-start | bytes 24584 | tf_op jit(solution)/shard_map/ppermute | solution.py:452
  59.0 1.6 %collective-permute-done.17.refs_12_ = bf16[32,128]{1,0:T(8,128)(2,1)S(1)} collective-permute-done((bf16[32,128]{1,0:T(8,128)(2,1)S(1)}, bf16[32,128]{1,0:T(8,128)(2,1)S(1)}, u32[]{:S(2)}, u32[]{:S(2)}) %collective-permute-start.17) | collective-permute-done | bytes 8224 | tf_op jit(solution)/shard_map/ppermute | solution.py:452
  60.6 2.9 %shard_map.127 = (bf16[32,704]{1,0:T(8,128)(2,1)S(1)}, bf16[32,704]{1,0:T(8,128)(2,1)S(1)}, bf16[32,704]{1,0:T(8,128)(2,1)S(1)}, bf16[32,704]{1,0:T(8,128)(2,1)S...) custom-call(bf16[3,2,288,256]{3,2,1,0:T(8,128)(2,1)S(1)} %get-tuple-element.59.refs_0_,, ...), custom_call_target="tpu_custom_call", output_to_operand_aliasing={{5}: (17, {})} | custom-call | tf_op jit(solution)/shard_map/pallas_call | solution.py:41
  63.4 2.7 %collective-permute-start.20 = (bf16[32,1152]{1,0:T(8,128)(2,1)S(1)}, bf16[32,1152]{1,0:T(8,128)(2,1)S(1)}, u32[]{:S(2)}, u32[]{:S(2)}) collective-permute-start(bf16[32,1152]{1,0:T(8,128)(2,1)S(1)} %get-tuple-element.67), channel_id=1, source_target_pairs={{0,12},{4,8},{8,4},{12,0},{1,13},{5,9},{9,5},{13,1},{2,14},{6,10},... | collective-permute-start | bytes 221192 | tf_op jit(solution)/shard_map/ppermute | solution.py:452
  67.9 1.7 %collective-permute-start.23 = (bf16[32,704]{1,0:T(8,128)(2,1)S(1)}, bf16[32,704]{1,0:T(8,128)(2,1)S(1)}, u32[]{:S(2)}, u32[]{:S(2)}) collective-permute-start(bf16[32,704]{1,0:T(8,128)(2,1)S(1)} %get-tuple-element.72), channel_id=1, source_target_pairs={{0,3},{1,2},{2,1},{3,0},{4,7},{5,6},{6,5},{7,4},{8,11},{9,10},{10,... | collective-permute-start | bytes 135176 | tf_op jit(solution)/shard_map/ppermute | solution.py:452
  70.7 2.2 %collective-permute-done.23.refs_5_ = bf16[32,704]{1,0:T(8,128)(2,1)S(1)} collective-permute-done((bf16[32,704]{1,0:T(8,128)(2,1)S(1)}, bf16[32,704]{1,0:T(8,128)(2,1)S(1)}, u32[]{:S(2)}, u32[]{:S(2)}) %collective-permute-start.23) | collective-permute-done | bytes 45088 | tf_op jit(solution)/shard_map/ppermute | solution.py:452
  75.9 3.2 %collective-permute-start.25 = (bf16[56,576]{1,0:T(8,128)(2,1)S(1)}, bf16[56,576]{1,0:T(8,128)(2,1)S(1)}, u32[]{:S(2)}, u32[]{:S(2)}) collective-permute-start(bf16[56,576]{1,0:T(8,128)(2,1)S(1)} %shard_map.130.refs_0_), channel_id=1, source_target_pairs={{0,4},{4,0},{8,12},{12,8},{1,5},{5,1},{9,13},{13,9},{2,6},{6,2},{1... | collective-permute-start | bytes 193544 | tf_op jit(solution)/shard_map/ppermute | solution.py:452
  79.2 2.6 %collective-permute-done.27.refs_3_ = bf16[56,576]{1,0:T(8,128)(2,1)S(1)} collective-permute-done((bf16[56,576]{1,0:T(8,128)(2,1)S(1)}, bf16[56,576]{1,0:T(8,128)(2,1)S(1)}, u32[]{:S(2)}, u32[]{:S(2)}) %collective-permute-start.27) | collective-permute-done | bytes 64544 | tf_op jit(solution)/shard_map/ppermute | solution.py:452
  81.7 2.2 %collective-permute-done.26.refs_2_ = bf16[56,576]{1,0:T(8,128)(2,1)S(1)} collective-permute-done((bf16[56,576]{1,0:T(8,128)(2,1)S(1)}, bf16[56,576]{1,0:T(8,128)(2,1)S(1)}, u32[]{:S(2)}, u32[]{:S(2)}) %collective-permute-start.26) | collective-permute-done | bytes 64544 | tf_op jit(solution)/shard_map/ppermute | solution.py:452
  84.0 1.8 %collective-permute-start.30 = (bf16[56,576]{1,0:T(8,128)(2,1)S(1)}, bf16[56,576]{1,0:T(8,128)(2,1)S(1)}, u32[]{:S(2)}, u32[]{:S(2)}) collective-permute-start(bf16[56,576]{1,0:T(8,128)(2,1)S(1)} %shard_map.131.refs_0_), channel_id=1, source_target_pairs={{0,3},{1,2},{2,1},{3,0},{4,7},{5,6},{6,5},{7,4},{8,11},{9,10},{10,... | collective-permute-start | bytes 193544 | tf_op jit(solution)/shard_map/ppermute | solution.py:452
  87.5 1.8 %collective-permute-done.30.refs_3_ = bf16[56,576]{1,0:T(8,128)(2,1)S(1)} collective-permute-done((bf16[56,576]{1,0:T(8,128)(2,1)S(1)}, bf16[56,576]{1,0:T(8,128)(2,1)S(1)}, u32[]{:S(2)}, u32[]{:S(2)}) %collective-permute-start.30) | collective-permute-done | bytes 64544 | tf_op jit(solution)/shard_map/ppermute | solution.py:452
  (55 shorter events, 18.8 us)
Async XLA Ops:
  4.1 13.2 %collective-permute-start.3 = (bf16[4,32,1152]{2,1,0:T(8,128)(2,1)S(1)}, bf16[4,32,1152]{2,1,0:T(8,128)(2,1)S(1)}, u32[]{:S(2)}, u32[]{:S(2)}) collective-permute-start(bf16[4,32,1152]{2,1,0:T(8,128)(2,1)S(1)} %get-tuple-element.44), channel_id=1, source_target_pairs={{0,4},{4,0},{8,12},{12,8},{1,5},{5,1},{9,13},{13,9},{2,6},{6,2},{1... | collective-permute-start | bytes 884744 | tf_op jit(solution)/shard_map/ppermute | solution.py:452
  7.2 13.0 %collective-permute-start = (bf16[1184,128]{1,0:T(8,128)(2,1)S(1)}, bf16[1184,128]{1,0:T(8,128)(2,1)S(1)}, u32[]{:S(2)}, u32[]{:S(2)}) collective-permute-start(bf16[1184,128]{1,0:T(8,128)(2,1)S(1)} %get-tuple-element.41), channel_id=1, source_target_pairs={{0,1},{1,0},{2,3},{3,2},{4,5},{5,4},{6,7},{7,6},{8,9},{9,8},{10,11... | collective-permute-start | bytes 909320 | tf_op jit(solution)/shard_map/ppermute | solution.py:452
  8.7 14.9 %collective-permute-start.1 = (bf16[1184,128]{1,0:T(8,128)(2,1)S(1)}, bf16[1184,128]{1,0:T(8,128)(2,1)S(1)}, u32[]{:S(2)}, u32[]{:S(2)}) collective-permute-start(bf16[1184,128]{1,0:T(8,128)(2,1)S(1)} %get-tuple-element.42), channel_id=1, source_target_pairs={{0,2},{1,3},{2,0},{3,1},{4,6},{5,7},{6,4},{7,5},{8,10},{9,11},{10,... | collective-permute-start | bytes 909320 | tf_op jit(solution)/shard_map/ppermute | solution.py:452
  10.3 13.3 %collective-permute-start.2 = (bf16[1184,128]{1,0:T(8,128)(2,1)S(1)}, bf16[1184,128]{1,0:T(8,128)(2,1)S(1)}, u32[]{:S(2)}, u32[]{:S(2)}) collective-permute-start(bf16[1184,128]{1,0:T(8,128)(2,1)S(1)} %get-tuple-element.43), channel_id=1, source_target_pairs={{0,3},{1,2},{2,1},{3,0},{4,7},{5,6},{6,5},{7,4},{8,11},{9,10},{10,... | collective-permute-start | bytes 909320 | tf_op jit(solution)/shard_map/ppermute | solution.py:452
  10.7 28.5 %collective-permute-start.7 = (bf16[4,32,1152]{2,1,0:T(8,128)(2,1)}, bf16[4,32,1152]{2,1,0:T(8,128)(2,1)}, u32[]{:S(2)}, u32[]{:S(2)}) collective-permute-start(bf16[4,32,1152]{2,1,0:T(8,128)(2,1)} %get-tuple-element.50), channel_id=1, source_target_pairs={{0,8},{4,12},{8,0},{12,4},{1,9},{5,13},{9,1},{13,5},{2,10},{6,14},... | collective-permute-start | bytes 884744 | tf_op jit(solution)/shard_map/ppermute | solution.py:452
  17.4 21.9 %collective-permute-start.8 = (bf16[4,32,1152]{2,1,0:T(8,128)(2,1)}, bf16[4,32,1152]{2,1,0:T(8,128)(2,1)}, u32[]{:S(2)}, u32[]{:S(2)}) collective-permute-start(bf16[4,32,1152]{2,1,0:T(8,128)(2,1)} %get-tuple-element.51), channel_id=1, source_target_pairs={{0,12},{4,8},{8,4},{12,0},{1,13},{5,9},{9,5},{13,1},{2,14},{6,10},... | collective-permute-start | bytes 884744 | tf_op jit(solution)/shard_map/ppermute | solution.py:452
  27.1 5.2 %collective-permute-start.4 = (bf16[288,128]{1,0:T(8,128)(2,1)S(1)}, bf16[288,128]{1,0:T(8,128)(2,1)S(1)}, u32[]{:S(2)}, u32[]{:S(2)}) collective-permute-start(bf16[288,128]{1,0:T(8,128)(2,1)S(1)} %get-tuple-element.46), channel_id=1, source_target_pairs={{0,1},{1,0},{2,3},{3,2},{4,5},{5,4},{6,7},{7,6},{8,9},{9,8},{10,11... | collective-permute-start | bytes 221192 | tf_op jit(solution)/shard_map/ppermute | solution.py:452
  28.4 4.4 %collective-permute-start.5 = (bf16[288,128]{1,0:T(8,128)(2,1)S(1)}, bf16[288,128]{1,0:T(8,128)(2,1)S(1)}, u32[]{:S(2)}, u32[]{:S(2)}) collective-permute-start(bf16[288,128]{1,0:T(8,128)(2,1)S(1)} %get-tuple-element.47), channel_id=1, source_target_pairs={{0,2},{1,3},{2,0},{3,1},{4,6},{5,7},{6,4},{7,5},{8,10},{9,11},{10,... | collective-permute-start | bytes 221192 | tf_op jit(solution)/shard_map/ppermute | solution.py:452
  29.2 5.3 %collective-permute-start.6 = (bf16[288,128]{1,0:T(8,128)(2,1)S(1)}, bf16[288,128]{1,0:T(8,128)(2,1)S(1)}, u32[]{:S(2)}, u32[]{:S(2)}) collective-permute-start(bf16[288,128]{1,0:T(8,128)(2,1)S(1)} %get-tuple-element.48), channel_id=1, source_target_pairs={{0,3},{1,2},{2,1},{3,0},{4,7},{5,6},{6,5},{7,4},{8,11},{9,10},{10,... | collective-permute-start | bytes 221192 | tf_op jit(solution)/shard_map/ppermute | solution.py:452
  34.8 6.3 %collective-permute-start.9 = (f32[8,128]{1,0:T(8,128)S(1)}, f32[8,128]{1,0:T(8,128)S(1)}, u32[]{:S(2)}, u32[]{:S(2)}) collective-permute-start(f32[8,128]{1,0:T(8,128)S(1)} %get-tuple-element.53), channel_id=1, source_target_pairs={{0,4},{4,0},{8,12},{12,8},{1,5},{5,1},{9,13},{13,9},{2,6},{6,2},{1... | collective-permute-start | bytes 12296 | tf_op jit(solution)/shard_map/ppermute | solution.py:452
  35.3 5.8 %collective-permute-start.10 = (f32[8,128]{1,0:T(8,128)S(1)}, f32[8,128]{1,0:T(8,128)S(1)}, u32[]{:S(2)}, u32[]{:S(2)}) collective-permute-start(f32[8,128]{1,0:T(8,128)S(1)} %get-tuple-element.54), channel_id=1, source_target_pairs={{0,8},{4,12},{8,0},{12,4},{1,9},{5,13},{9,1},{13,5},{2,10},{6,14},... | collective-permute-start | bytes 12296 | tf_op jit(solution)/shard_map/ppermute | solution.py:452
  37.9 5.4 %collective-permute-start.11 = (f32[8,128]{1,0:T(8,128)S(1)}, f32[8,128]{1,0:T(8,128)S(1)}, u32[]{:S(2)}, u32[]{:S(2)}) collective-permute-start(f32[8,128]{1,0:T(8,128)S(1)} %get-tuple-element.55), channel_id=1, source_target_pairs={{0,12},{4,8},{8,4},{12,0},{1,13},{5,9},{9,5},{13,1},{2,14},{6,10},... | collective-permute-start | bytes 12296 | tf_op jit(solution)/shard_map/ppermute | solution.py:452
  46.4 6.5 %collective-permute-start.14 = (f32[8,128]{1,0:T(8,128)S(1)}, f32[8,128]{1,0:T(8,128)S(1)}, u32[]{:S(2)}, u32[]{:S(2)}) collective-permute-start(f32[8,128]{1,0:T(8,128)S(1)} %get-tuple-element.63), channel_id=1, source_target_pairs={{0,4},{4,0},{8,12},{12,8},{1,5},{5,1},{9,13},{13,9},{2,6},{6,2},{1... | collective-permute-start | bytes 12296 | tf_op jit(solution)/shard_map/ppermute | solution.py:452
  46.4 6.4 %collective-permute-start.15 = (f32[8,128]{1,0:T(8,128)S(1)}, f32[8,128]{1,0:T(8,128)S(1)}, u32[]{:S(2)}, u32[]{:S(2)}) collective-permute-start(f32[8,128]{1,0:T(8,128)S(1)} %get-tuple-element.64), channel_id=1, source_target_pairs={{0,8},{4,12},{8,0},{12,4},{1,9},{5,13},{9,1},{13,5},{2,10},{6,14},... | collective-permute-start | bytes 12296 | tf_op jit(solution)/shard_map/ppermute | solution.py:452
  48.3 5.4 %collective-permute-start.16 = (f32[8,128]{1,0:T(8,128)S(1)}, f32[8,128]{1,0:T(8,128)S(1)}, u32[]{:S(2)}, u32[]{:S(2)}) collective-permute-start(f32[8,128]{1,0:T(8,128)S(1)} %get-tuple-element.65), channel_id=1, source_target_pairs={{0,12},{4,8},{8,4},{12,0},{1,13},{5,9},{9,5},{13,1},{2,14},{6,10},... | collective-permute-start | bytes 12296 | tf_op jit(solution)/shard_map/ppermute | solution.py:452
  50.9 9.7 %collective-permute-start.12 = (bf16[32,1152]{1,0:T(8,128)(2,1)S(1)}, bf16[32,1152]{1,0:T(8,128)(2,1)S(1)}, u32[]{:S(2)}, u32[]{:S(2)}) collective-permute-start(bf16[32,1152]{1,0:T(8,128)(2,1)S(1)} %get-tuple-element.57), channel_id=1, source_target_pairs={{0,4},{4,0},{8,12},{12,8},{1,5},{5,1},{9,13},{13,9},{2,6},{6,2},{1... | collective-permute-start | bytes 221192 | tf_op jit(solution)/shard_map/ppermute | solution.py:452
  51.0 9.6 %collective-permute-start.13 = (bf16[32,1152]{1,0:T(8,128)(2,1)S(1)}, bf16[32,1152]{1,0:T(8,128)(2,1)S(1)}, u32[]{:S(2)}, u32[]{:S(2)}) collective-permute-start(bf16[32,1152]{1,0:T(8,128)(2,1)S(1)} %get-tuple-element.58), channel_id=1, source_target_pairs={{0,8},{4,12},{8,0},{12,4},{1,9},{5,13},{9,1},{13,5},{2,10},{6,14},... | collective-permute-start | bytes 221192 | tf_op jit(solution)/shard_map/ppermute | solution.py:452
  53.9 4.6 %collective-permute-start.19 = (bf16[32,128]{1,0:T(8,128)(2,1)S(1)}, bf16[32,128]{1,0:T(8,128)(2,1)S(1)}, u32[]{:S(2)}, u32[]{:S(2)}) collective-permute-start(bf16[32,128]{1,0:T(8,128)(2,1)S(1)} %shard_map.126.refs_11_), channel_id=1, source_target_pairs={{0,3},{1,2},{2,1},{3,0},{4,7},{5,6},{6,5},{7,4},{8,11},{9,10},{10,... | collective-permute-start | bytes 24584 | tf_op jit(solution)/shard_map/ppermute | solution.py:452
  55.3 3.7 %collective-permute-start.18 = (bf16[32,128]{1,0:T(8,128)(2,1)S(1)}, bf16[32,128]{1,0:T(8,128)(2,1)S(1)}, u32[]{:S(2)}, u32[]{:S(2)}) collective-permute-start(bf16[32,128]{1,0:T(8,128)(2,1)S(1)} %shard_map.126.refs_11_), channel_id=1, source_target_pairs={{0,2},{1,3},{2,0},{3,1},{4,6},{5,7},{6,4},{7,5},{8,10},{9,11},{10,... | collective-permute-start | bytes 24584 | tf_op jit(solution)/shard_map/ppermute | solution.py:452
  56.9 3.7 %collective-permute-start.17 = (bf16[32,128]{1,0:T(8,128)(2,1)S(1)}, bf16[32,128]{1,0:T(8,128)(2,1)S(1)}, u32[]{:S(2)}, u32[]{:S(2)}) collective-permute-start(bf16[32,128]{1,0:T(8,128)(2,1)S(1)} %shard_map.126.refs_11_), channel_id=1, source_target_pairs={{0,1},{1,0},{2,3},{3,2},{4,5},{5,4},{6,7},{7,6},{8,9},{9,8},{10,11... | collective-permute-start | bytes 24584 | tf_op jit(solution)/shard_map/ppermute | solution.py:452
  63.4 9.4 %collective-permute-start.20 = (bf16[32,1152]{1,0:T(8,128)(2,1)S(1)}, bf16[32,1152]{1,0:T(8,128)(2,1)S(1)}, u32[]{:S(2)}, u32[]{:S(2)}) collective-permute-start(bf16[32,1152]{1,0:T(8,128)(2,1)S(1)} %get-tuple-element.67), channel_id=1, source_target_pairs={{0,12},{4,8},{8,4},{12,0},{1,13},{5,9},{9,5},{13,1},{2,14},{6,10},... | collective-permute-start | bytes 221192 | tf_op jit(solution)/shard_map/ppermute | solution.py:452
  66.1 4.1 %collective-permute-start.21 = (bf16[32,704]{1,0:T(8,128)(2,1)S(1)}, bf16[32,704]{1,0:T(8,128)(2,1)S(1)}, u32[]{:S(2)}, u32[]{:S(2)}) collective-permute-start(bf16[32,704]{1,0:T(8,128)(2,1)S(1)} %get-tuple-element.70), channel_id=1, source_target_pairs={{0,1},{1,0},{2,3},{3,2},{4,5},{5,4},{6,7},{7,6},{8,9},{9,8},{10,11... | collective-permute-start | bytes 135176 | tf_op jit(solution)/shard_map/ppermute | solution.py:452
  66.6 4.1 %collective-permute-start.22 = (bf16[32,704]{1,0:T(8,128)(2,1)S(1)}, bf16[32,704]{1,0:T(8,128)(2,1)S(1)}, u32[]{:S(2)}, u32[]{:S(2)}) collective-permute-start(bf16[32,704]{1,0:T(8,128)(2,1)S(1)} %get-tuple-element.71), channel_id=1, source_target_pairs={{0,2},{1,3},{2,0},{3,1},{4,6},{5,7},{6,4},{7,5},{8,10},{9,11},{10,... | collective-permute-start | bytes 135176 | tf_op jit(solution)/shard_map/ppermute | solution.py:452
  67.9 5.0 %collective-permute-start.23 = (bf16[32,704]{1,0:T(8,128)(2,1)S(1)}, bf16[32,704]{1,0:T(8,128)(2,1)S(1)}, u32[]{:S(2)}, u32[]{:S(2)}) collective-permute-start(bf16[32,704]{1,0:T(8,128)(2,1)S(1)} %get-tuple-element.72), channel_id=1, source_target_pairs={{0,3},{1,2},{2,1},{3,0},{4,7},{5,6},{6,5},{7,4},{8,11},{9,10},{10,... | collective-permute-start | bytes 135176 | tf_op jit(solution)/shard_map/ppermute | solution.py:452
  73.3 1.4 %collective-permute-start.24 = (f32[56,576]{1,0:T(8,128)S(1)}, f32[56,576]{1,0:T(8,128)S(1)}, u32[]{:S(2)}, u32[]{:S(2)}) collective-permute-start(f32[56,576]{1,0:T(8,128)S(1)} %get-tuple-element.74), channel_id=1, source_target_pairs={{0,16},{16,0},{1,17},{17,1},{2,18},{18,2},{3,19},{19,3},{4,20},{20... | collective-permute-start | bytes 387080 | tf_op jit(solution)/shard_map/ppermute | solution.py:452
  74.7 7.0 %collective-permute-start.27 = (bf16[56,576]{1,0:T(8,128)(2,1)S(1)}, bf16[56,576]{1,0:T(8,128)(2,1)S(1)}, u32[]{:S(2)}, u32[]{:S(2)}) collective-permute-start(bf16[56,576]{1,0:T(8,128)(2,1)S(1)} %shard_map.130.refs_0_), channel_id=1, source_target_pairs={{0,12},{4,8},{8,4},{12,0},{1,13},{5,9},{9,5},{13,1},{2,14},{6,10},... | collective-permute-start | bytes 193544 | tf_op jit(solution)/shard_map/ppermute | solution.py:452
  75.9 8.0 %collective-permute-start.26 = (bf16[56,576]{1,0:T(8,128)(2,1)S(1)}, bf16[56,576]{1,0:T(8,128)(2,1)S(1)}, u32[]{:S(2)}, u32[]{:S(2)}) collective-permute-start(bf16[56,576]{1,0:T(8,128)(2,1)S(1)} %shard_map.130.refs_0_), channel_id=1, source_target_pairs={{0,8},{4,12},{8,0},{12,4},{1,9},{5,13},{9,1},{13,5},{2,10},{6,14},... | collective-permute-start | bytes 193544 | tf_op jit(solution)/shard_map/ppermute | solution.py:452
  75.9 8.0 %collective-permute-start.25 = (bf16[56,576]{1,0:T(8,128)(2,1)S(1)}, bf16[56,576]{1,0:T(8,128)(2,1)S(1)}, u32[]{:S(2)}, u32[]{:S(2)}) collective-permute-start(bf16[56,576]{1,0:T(8,128)(2,1)S(1)} %shard_map.130.refs_0_), channel_id=1, source_target_pairs={{0,4},{4,0},{8,12},{12,8},{1,5},{5,1},{9,13},{13,9},{2,6},{6,2},{1... | collective-permute-start | bytes 193544 | tf_op jit(solution)/shard_map/ppermute | solution.py:452
  84.0 5.4 %collective-permute-start.30 = (bf16[56,576]{1,0:T(8,128)(2,1)S(1)}, bf16[56,576]{1,0:T(8,128)(2,1)S(1)}, u32[]{:S(2)}, u32[]{:S(2)}) collective-permute-start(bf16[56,576]{1,0:T(8,128)(2,1)S(1)} %shard_map.131.refs_0_), channel_id=1, source_target_pairs={{0,3},{1,2},{2,1},{3,0},{4,7},{5,6},{6,5},{7,4},{8,11},{9,10},{10,... | collective-permute-start | bytes 193544 | tf_op jit(solution)/shard_map/ppermute | solution.py:452
  85.7 4.9 %collective-permute-start.29 = (bf16[56,576]{1,0:T(8,128)(2,1)S(1)}, bf16[56,576]{1,0:T(8,128)(2,1)S(1)}, u32[]{:S(2)}, u32[]{:S(2)}) collective-permute-start(bf16[56,576]{1,0:T(8,128)(2,1)S(1)} %shard_map.131.refs_0_), channel_id=1, source_target_pairs={{0,2},{1,3},{2,0},{3,1},{4,6},{5,7},{6,4},{7,5},{8,10},{9,11},{10,... | collective-permute-start | bytes 193544 | tf_op jit(solution)/shard_map/ppermute | solution.py:452
  86.2 4.4 %collective-permute-start.28 = (bf16[56,576]{1,0:T(8,128)(2,1)S(1)}, bf16[56,576]{1,0:T(8,128)(2,1)S(1)}, u32[]{:S(2)}, u32[]{:S(2)}) collective-permute-start(bf16[56,576]{1,0:T(8,128)(2,1)S(1)} %shard_map.131.refs_0_), channel_id=1, source_target_pairs={{0,1},{1,0},{2,3},{3,2},{4,5},{5,4},{6,7},{7,6},{8,9},{9,8},{10,11... | collective-permute-start | bytes 193544 | tf_op jit(solution)/shard_map/ppermute | solution.py:452
  90.8 1.4 %collective-permute-start.31 = (bf16[64,1152]{1,0:T(8,128)(2,1)S(1)}, bf16[64,1152]{1,0:T(8,128)(2,1)S(1)}, u32[]{:S(2)}, u32[]{:S(2)}) collective-permute-start(bf16[64,1152]{1,0:T(8,128)(2,1)S(1)} %shard_map.132.refs_0_), channel_id=1, source_target_pairs={{0,16},{16,0},{1,17},{17,1},{2,18},{18,2},{3,19},{19,3},{4,20},{20... | collective-permute-start | bytes 442376 | tf_op jit(solution)/shard_map/ppermute | solution.py:452
  (4 other events, 105.2 us)

commit v13 on v12

--- a/solution.py
+++ b/solution.py
@@ -390,7 +390,7 @@
         mine += [rows[:, j * d_s : (j + 1) * d_s] for j in range(n_s)]
         mine = jnp.concatenate(mine, axis=0)
         half = mine.shape[0] // 2
-        buf[d] = jnp.concatenate([mine[:half], mine[half:]], axis=1)
+        buf[d] = jnp.concatenate([mine[:half], mine[half:]], axis=1).astype(BF16)
     for k in range(n_d):
         sends[k][...] = buf[peer("dp", k)]
 
@@ -559,12 +559,11 @@
     dims = ((n_s * n_full + n_split) // 2, 2 * d_s)
     sums = call(
         functools.partial(merge_kernel, n_s, n_d),
-        [shape(dims, F32)] * n_d,
+        [shape(dims, BF16)] * n_d,
         part, patches, *partial,
-        scratch=[pltpu.VMEM((n_d,) + dims, F32)],
-        after=out_t[3:],
-    )
-    sums = call(total_kernel, shape(dims, BF16), *exchange(sums, "dp"))
+        scratch=[pltpu.VMEM((n_d,) + dims, BF16)],
+    )
+    sums = call(total_kernel, shape(dims, BF16), *exchange(sums, "dp"), after=out_t[3:])
     sums = call(total_kernel, shape(dims, BF16), *share(sums, "tm"))
     sums = call(
         functools.partial(join_kernel, n_full),

time: 93.3 us -> 90.6 us (0.971)
  waiting for transfers between devices: 30.4 us -> 27.6 us
    ppermute x32, waiting for transfers between devices: 30.4 us -> 27.6 us  [hops(): lax.ppermute(array, axis, [(i, i ^ k) for i in range(size)])]
  transfers between devices with their start and end apart: 32 -> 32, of which waited for: 19 -> 17; matrix products, arithmetic and copies ran while one was open for 0% -> 0% of each run, Pallas kernels for 7% -> 8%
where the time goes in v13:
time: 90.6 us; the launch traced here: 90.4 us
  starting transfers between devices  44.2 us (49%)
  waiting for transfers between devices  27.6 us (30%)
  Pallas kernels  17.5 us (19%)
    ppermute x32, starting transfers between devices, hops(): lax.ppermute(array, axis, [(i, i ^ k) for i in range(size)])  44.2 us
    ppermute x32, waiting for transfers between devices, hops(): lax.ppermute(array, axis, [(i, i ^ k) for i in range(size)])  27.6 us
    pallas_call x13, Pallas kernels, call(): pl.pallas_call(body, out_shape=outs + tuple((shape(x.shape, x.dtype) for...  17.5 us
  transfers between devices with their start and end apart: 32, of which 17 were waited for; matrix products, arithmetic and copies ran while one was open for 0% of the time, Pallas kernels for 8%

profile of v13, /device:TPU:0, one launch (start us, length us, event | category | flops | bytes accessed | tf_op | source)
XLA Modules:
  0.0 90.4 jit_solution(12379215284896849319)
XLA Ops:
  0.7 3.5 %shard_map.121 = (bf16[1184,128]{1,0:T(8,128)(2,1)S(1)}, bf16[1184,128]{1,0:T(8,128)(2,1)S(1)}, bf16[1184,128]{1,0:T(8,128)(2,1)S(1)}, bf16[1184,128]{1,0:T(8,12...) custom-call(bf16[1,2,64,1152]{3,2,1,0:T(8,128)(2,1)} %refs_1_.5, ...), custom_call_target="tpu_custom_call" | custom-call | tf_op jit(solution)/shard_map/pallas_call | solution.py:41
  4.1 3.1 %collective-permute-start.3 = (bf16[4,32,1152]{2,1,0:T(8,128)(2,1)S(1)}, bf16[4,32,1152]{2,1,0:T(8,128)(2,1)S(1)}, u32[]{:S(2)}, u32[]{:S(2)}) collective-permute-start(bf16[4,32,1152]{2,1,0:T(8,128)(2,1)S(1)} %get-tuple-element.44), channel_id=1, source_target_pairs={{0,4},{4,0},{8,12},{12,8},{1,5},{5,1},{9,13},{13,9},{2,6},{6,2},{1... | collective-permute-start | bytes 884744 | tf_op jit(solution)/shard_map/ppermute | solution.py:452
  7.2 1.5 %collective-permute-start = (bf16[1184,128]{1,0:T(8,128)(2,1)S(1)}, bf16[1184,128]{1,0:T(8,128)(2,1)S(1)}, u32[]{:S(2)}, u32[]{:S(2)}) collective-permute-start(bf16[1184,128]{1,0:T(8,128)(2,1)S(1)} %get-tuple-element.41), channel_id=1, source_target_pairs={{0,1},{1,0},{2,3},{3,2},{4,5},{5,4},{6,7},{7,6},{8,9},{9,8},{10,11... | collective-permute-start | bytes 909320 | tf_op jit(solution)/shard_map/ppermute | solution.py:452
  8.7 1.6 %collective-permute-start.1 = (bf16[1184,128]{1,0:T(8,128)(2,1)S(1)}, bf16[1184,128]{1,0:T(8,128)(2,1)S(1)}, u32[]{:S(2)}, u32[]{:S(2)}) collective-permute-start(bf16[1184,128]{1,0:T(8,128)(2,1)S(1)} %get-tuple-element.42), channel_id=1, source_target_pairs={{0,2},{1,3},{2,0},{3,1},{4,6},{5,7},{6,4},{7,5},{8,10},{9,11},{10,... | collective-permute-start | bytes 909320 | tf_op jit(solution)/shard_map/ppermute | solution.py:452
  10.7 2.6 %collective-permute-start.7 = (bf16[4,32,1152]{2,1,0:T(8,128)(2,1)}, bf16[4,32,1152]{2,1,0:T(8,128)(2,1)}, u32[]{:S(2)}, u32[]{:S(2)}) collective-permute-start(bf16[4,32,1152]{2,1,0:T(8,128)(2,1)} %get-tuple-element.50), channel_id=1, source_target_pairs={{0,8},{4,12},{8,0},{12,4},{1,9},{5,13},{9,1},{13,5},{2,10},{6,14},... | collective-permute-start | bytes 884744 | tf_op jit(solution)/shard_map/ppermute | solution.py:452
  13.3 4.1 %collective-permute-done.3.refs_4_ = bf16[4,32,1152]{2,1,0:T(8,128)(2,1)S(1)} collective-permute-done((bf16[4,32,1152]{2,1,0:T(8,128)(2,1)S(1)}, bf16[4,32,1152]{2,1,0:T(8,128)(2,1)S(1)}, u32[]{:S(2)}, u32[]{:S(2)}) %collective-permute-start.3) | collective-permute-done | bytes 294944 | tf_op jit(solution)/shard_map/ppermute | solution.py:452
  17.4 2.9 %collective-permute-start.8 = (bf16[4,32,1152]{2,1,0:T(8,128)(2,1)}, bf16[4,32,1152]{2,1,0:T(8,128)(2,1)}, u32[]{:S(2)}, u32[]{:S(2)}) collective-permute-start(bf16[4,32,1152]{2,1,0:T(8,128)(2,1)} %get-tuple-element.51), channel_id=1, source_target_pairs={{0,12},{4,8},{8,4},{12,0},{1,13},{5,9},{9,5},{13,1},{2,14},{6,10},... | collective-permute-start | bytes 884744 | tf_op jit(solution)/shard_map/ppermute | solution.py:452
  20.2 3.4 %collective-permute-done.1.refs_2_.refs_9_ = bf16[1184,128]{1,0:T(8,128)(2,1)S(1)} collective-permute-done((bf16[1184,128]{1,0:T(8,128)(2,1)S(1)}, bf16[1184,128]{1,0:T(8,128)(2,1)S(1)}, u32[]{:S(2)}, u32[]{:S(2)}) %collective-permute-start.1) | collective-permute-done | bytes 303136 | tf_op jit(solution)/shard_map/ppermute | solution.py:452
  23.6 3.4 %shard_map.122 = (bf16[3,2,288,256]{3,2,1,0:T(8,128)(2,1)S(1)}, f32[2,4,256,256]{3,2,1,0:T(8,128)}, bf16[288,128]{1,0:T(8,128)(2,1)S(1)}, bf16[288,128]{1,0:T(8,...) custom-call(bf16[1184,128]{1,0:T(8,128)(2,1)S(1)} %get-tuple-element.40.refs_0_.refs_7_, ...), custom_call_target="tpu_custom_call" | custom-call | tf_op jit(solution)/shard_map/pallas_call | solution.py:41
  29.2 1.4 %collective-permute-start.6 = (bf16[288,128]{1,0:T(8,128)(2,1)S(1)}, bf16[288,128]{1,0:T(8,128)(2,1)S(1)}, u32[]{:S(2)}, u32[]{:S(2)}) collective-permute-start(bf16[288,128]{1,0:T(8,128)(2,1)S(1)} %get-tuple-element.48), channel_id=1, source_target_pairs={{0,3},{1,2},{2,1},{3,0},{4,7},{5,6},{6,5},{7,4},{8,11},{9,10},{10,... | collective-permute-start | bytes 221192 | tf_op jit(solution)/shard_map/ppermute | solution.py:452
  30.6 1.6 %collective-permute-done.4.refs_1_ = bf16[288,128]{1,0:T(8,128)(2,1)S(1)} collective-permute-done((bf16[288,128]{1,0:T(8,128)(2,1)S(1)}, bf16[288,128]{1,0:T(8,128)(2,1)S(1)}, u32[]{:S(2)}, u32[]{:S(2)}) %collective-permute-start.4) | collective-permute-done | bytes 73760 | tf_op jit(solution)/shard_map/ppermute | solution.py:452
  32.8 1.7 %collective-permute-done.6.refs_3_ = bf16[288,128]{1,0:T(8,128)(2,1)S(1)} collective-permute-done((bf16[288,128]{1,0:T(8,128)(2,1)S(1)}, bf16[288,128]{1,0:T(8,128)(2,1)S(1)}, u32[]{:S(2)}, u32[]{:S(2)}) %collective-permute-start.6) | collective-permute-done | bytes 73760 | tf_op jit(solution)/shard_map/ppermute | solution.py:452
  35.3 2.6 %collective-permute-start.10 = (f32[8,128]{1,0:T(8,128)S(1)}, f32[8,128]{1,0:T(8,128)S(1)}, u32[]{:S(2)}, u32[]{:S(2)}) collective-permute-start(f32[8,128]{1,0:T(8,128)S(1)} %get-tuple-element.54), channel_id=1, source_target_pairs={{0,8},{4,12},{8,0},{12,4},{1,9},{5,13},{9,1},{13,5},{2,10},{6,14},... | collective-permute-start | bytes 12296 | tf_op jit(solution)/shard_map/ppermute | solution.py:452
  39.2 1.8 %shard_map.124.refs_0_ = bf16[4,1152,128]{2,1,0:T(8,128)(2,1)S(1)} custom-call(bf16[1,2,64,1152]{3,2,1,0:T(8,128)(2,1)} %refs_0_.3, bf16[1,2,64,1152]{3,2,1,0:T(8,128)(2,1)} %refs_1_.3, bf16[1,2,64,1152]{3,2,1,0:T(8,128)(2,1)} %refs_2_.3, bf16[1,2,64,1152]{3,2,1,0:T(8,128)(2,1)} %refs_3_.3, bf16[4,32,1152]{2,1,0:T(8,128)(2,1)S(1)} %collective-permute-done.3.refs_4_, ...), custom_call_target="tpu_custom_call" | custom-call | tf_op jit(solution)/shard_map/pallas_call | solution.py:41
  41.1 2.2 %collective-permute-done.11.refs_5_ = f32[8,128]{1,0:T(8,128)S(1)} collective-permute-done((f32[8,128]{1,0:T(8,128)S(1)}, f32[8,128]{1,0:T(8,128)S(1)}, u32[]{:S(2)}, u32[]{:S(2)}) %collective-permute-start.11) | collective-permute-done | bytes 4128 | tf_op jit(solution)/shard_map/ppermute | solution.py:452
  43.3 3.1 %shard_map.125 = (bf16[32,1152]{1,0:T(8,128)(2,1)S(1)}, bf16[32,1152]{1,0:T(8,128)(2,1)S(1)}, bf16[32,1152]{1,0:T(8,128)(2,1)S(1)}, bf16[32,1152]{1,0:T(8,128)(2...) custom-call(bf16[4,1152,128]{2,1,0:T(8,128)(2,1)S(1)} %shard_map.124, ...), custom_call_target="tpu_custom_call" | custom-call | tf_op jit(solution)/shard_map/pallas_call | solution.py:41
  46.4 1.9 %collective-permute-start.15 = (f32[8,128]{1,0:T(8,128)S(1)}, f32[8,128]{1,0:T(8,128)S(1)}, u32[]{:S(2)}, u32[]{:S(2)}) collective-permute-start(f32[8,128]{1,0:T(8,128)S(1)} %get-tuple-element.64), channel_id=1, source_target_pairs={{0,8},{4,12},{8,0},{12,4},{1,9},{5,13},{9,1},{13,5},{2,10},{6,14},... | collective-permute-start | bytes 12296 | tf_op jit(solution)/shard_map/ppermute | solution.py:452
  48.3 2.5 %collective-permute-start.16 = (f32[8,128]{1,0:T(8,128)S(1)}, f32[8,128]{1,0:T(8,128)S(1)}, u32[]{:S(2)}, u32[]{:S(2)}) collective-permute-start(f32[8,128]{1,0:T(8,128)S(1)} %get-tuple-element.65), channel_id=1, source_target_pairs={{0,12},{4,8},{8,4},{12,0},{1,13},{5,9},{9,5},{13,1},{2,14},{6,10},... | collective-permute-start | bytes 12296 | tf_op jit(solution)/shard_map/ppermute | solution.py:452
  51.0 1.9 %collective-permute-start.13 = (bf16[32,1152]{1,0:T(8,128)(2,1)S(1)}, bf16[32,1152]{1,0:T(8,128)(2,1)S(1)}, u32[]{:S(2)}, u32[]{:S(2)}) collective-permute-start(bf16[32,1152]{1,0:T(8,128)(2,1)S(1)} %get-tuple-element.58), channel_id=1, source_target_pairs={{0,8},{4,12},{8,0},{12,4},{1,9},{5,13},{9,1},{13,5},{2,10},{6,14},... | collective-permute-start | bytes 221192 | tf_op jit(solution)/shard_map/ppermute | solution.py:452
  53.9 1.5 %collective-permute-start.19 = (bf16[32,128]{1,0:T(8,128)(2,1)S(1)}, bf16[32,128]{1,0:T(8,128)(2,1)S(1)}, u32[]{:S(2)}, u32[]{:S(2)}) collective-permute-start(bf16[32,128]{1,0:T(8,128)(2,1)S(1)} %shard_map.126.refs_11_), channel_id=1, source_target_pairs={{0,3},{1,2},{2,1},{3,0},{4,7},{5,6},{6,5},{7,4},{8,11},{9,10},{10,... | collective-permute-start | bytes 24584 | tf_op jit(solution)/shard_map/ppermute | solution.py:452
  55.3 1.6 %collective-permute-start.18 = (bf16[32,128]{1,0:T(8,128)(2,1)S(1)}, bf16[32,128]{1,0:T(8,128)(2,1)S(1)}, u32[]{:S(2)}, u32[]{:S(2)}) collective-permute-start(bf16[32,128]{1,0:T(8,128)(2,1)S(1)} %shard_map.126.refs_11_), channel_id=1, source_target_pairs={{0,2},{1,3},{2,0},{3,1},{4,6},{5,7},{6,4},{7,5},{8,10},{9,11},{10,... | collective-permute-start | bytes 24584 | tf_op jit(solution)/shard_map/ppermute | solution.py:452
  59.0 1.7 %collective-permute-done.17.refs_12_ = bf16[32,128]{1,0:T(8,128)(2,1)S(1)} collective-permute-done((bf16[32,128]{1,0:T(8,128)(2,1)S(1)}, bf16[32,128]{1,0:T(8,128)(2,1)S(1)}, u32[]{:S(2)}, u32[]{:S(2)}) %collective-permute-start.17) | collective-permute-done | bytes 8224 | tf_op jit(solution)/shard_map/ppermute | solution.py:452
  60.7 2.9 %shard_map.127 = (bf16[32,704]{1,0:T(8,128)(2,1)S(1)}, bf16[32,704]{1,0:T(8,128)(2,1)S(1)}, bf16[32,704]{1,0:T(8,128)(2,1)S(1)}, bf16[32,704]{1,0:T(8,128)(2,1)S...) custom-call(bf16[3,2,288,256]{3,2,1,0:T(8,128)(2,1)S(1)} %get-tuple-element.59.refs_0_,, ...), custom_call_target="tpu_custom_call", output_to_operand_aliasing={{5}: (17, {})} | custom-call | tf_op jit(solution)/shard_map/pallas_call | solution.py:41
  65.2 1.8 %collective-permute-start.23 = (bf16[32,704]{1,0:T(8,128)(2,1)S(1)}, bf16[32,704]{1,0:T(8,128)(2,1)S(1)}, u32[]{:S(2)}, u32[]{:S(2)}) collective-permute-start(bf16[32,704]{1,0:T(8,128)(2,1)S(1)} %get-tuple-element.72), channel_id=1, source_target_pairs={{0,3},{1,2},{2,1},{3,0},{4,7},{5,6},{6,5},{7,4},{8,11},{9,10},{10,... | collective-permute-start | bytes 135176 | tf_op jit(solution)/shard_map/ppermute | solution.py:452
  67.1 2.6 %collective-permute-start.20 = (bf16[32,1152]{1,0:T(8,128)(2,1)S(1)}, bf16[32,1152]{1,0:T(8,128)(2,1)S(1)}, u32[]{:S(2)}, u32[]{:S(2)}) collective-permute-start(bf16[32,1152]{1,0:T(8,128)(2,1)S(1)} %get-tuple-element.67), channel_id=1, source_target_pairs={{0,12},{4,8},{8,4},{12,0},{1,13},{5,9},{9,5},{13,1},{2,14},{6,10},... | collective-permute-start | bytes 221192 | tf_op jit(solution)/shard_map/ppermute | solution.py:452
  70.7 2.6 %collective-permute-done.20.refs_4_.refs_2_ = bf16[32,1152]{1,0:T(8,128)(2,1)S(1)} collective-permute-done((bf16[32,1152]{1,0:T(8,128)(2,1)S(1)}, bf16[32,1152]{1,0:T(8,128)(2,1)S(1)}, u32[]{:S(2)}, u32[]{:S(2)}) %collective-permute-start.20) | collective-permute-done | bytes 73760 | tf_op jit(solution)/shard_map/ppermute | solution.py:452
  73.3 2.6 %collective-permute-start.27 = (bf16[56,576]{1,0:T(8,128)(2,1)S(1)}, bf16[56,576]{1,0:T(8,128)(2,1)S(1)}, u32[]{:S(2)}, u32[]{:S(2)}) collective-permute-start(bf16[56,576]{1,0:T(8,128)(2,1)S(1)} %shard_map.130.refs_0_), channel_id=1, source_target_pairs={{0,12},{4,8},{8,4},{12,0},{1,13},{5,9},{9,5},{13,1},{2,14},{6,10},... | collective-permute-start | bytes 193544 | tf_op jit(solution)/shard_map/ppermute | solution.py:452
  75.9 1.8 %collective-permute-start.25 = (bf16[56,576]{1,0:T(8,128)(2,1)S(1)}, bf16[56,576]{1,0:T(8,128)(2,1)S(1)}, u32[]{:S(2)}, u32[]{:S(2)}) collective-permute-start(bf16[56,576]{1,0:T(8,128)(2,1)S(1)} %shard_map.130.refs_0_), channel_id=1, source_target_pairs={{0,4},{4,0},{8,12},{12,8},{1,5},{5,1},{9,13},{13,9},{2,6},{6,2},{1... | collective-permute-start | bytes 193544 | tf_op jit(solution)/shard_map/ppermute | solution.py:452
  77.7 2.1 %collective-permute-done.27.refs_3_ = bf16[56,576]{1,0:T(8,128)(2,1)S(1)} collective-permute-done((bf16[56,576]{1,0:T(8,128)(2,1)S(1)}, bf16[56,576]{1,0:T(8,128)(2,1)S(1)}, u32[]{:S(2)}, u32[]{:S(2)}) %collective-permute-start.27) | collective-permute-done | bytes 64544 | tf_op jit(solution)/shard_map/ppermute | solution.py:452
  79.8 1.8 %collective-permute-done.26.refs_2_ = bf16[56,576]{1,0:T(8,128)(2,1)S(1)} collective-permute-done((bf16[56,576]{1,0:T(8,128)(2,1)S(1)}, bf16[56,576]{1,0:T(8,128)(2,1)S(1)}, u32[]{:S(2)}, u32[]{:S(2)}) %collective-permute-start.26) | collective-permute-done | bytes 64544 | tf_op jit(solution)/shard_map/ppermute | solution.py:452
  83.5 1.7 %collective-permute-start.28 = (bf16[56,576]{1,0:T(8,128)(2,1)S(1)}, bf16[56,576]{1,0:T(8,128)(2,1)S(1)}, u32[]{:S(2)}, u32[]{:S(2)}) collective-permute-start(bf16[56,576]{1,0:T(8,128)(2,1)S(1)} %shard_map.131.refs_0_), channel_id=1, source_target_pairs={{0,1},{1,0},{2,3},{3,2},{4,5},{5,4},{6,7},{7,6},{8,9},{9,8},{10,11... | collective-permute-start | bytes 193544 | tf_op jit(solution)/shard_map/ppermute | solution.py:452
  85.2 2.3 %collective-permute-done.30.refs_3_ = bf16[56,576]{1,0:T(8,128)(2,1)S(1)} collective-permute-done((bf16[56,576]{1,0:T(8,128)(2,1)S(1)}, bf16[56,576]{1,0:T(8,128)(2,1)S(1)}, u32[]{:S(2)}, u32[]{:S(2)}) %collective-permute-start.30) | collective-permute-done | bytes 64544 | tf_op jit(solution)/shard_map/ppermute | solution.py:452
  (55 shorter events, 16.1 us)
Async XLA Ops:
  4.1 13.2 %collective-permute-start.3 = (bf16[4,32,1152]{2,1,0:T(8,128)(2,1)S(1)}, bf16[4,32,1152]{2,1,0:T(8,128)(2,1)S(1)}, u32[]{:S(2)}, u32[]{:S(2)}) collective-permute-start(bf16[4,32,1152]{2,1,0:T(8,128)(2,1)S(1)} %get-tuple-element.44), channel_id=1, source_target_pairs={{0,4},{4,0},{8,12},{12,8},{1,5},{5,1},{9,13},{13,9},{2,6},{6,2},{1... | collective-permute-start | bytes 884744 | tf_op jit(solution)/shard_map/ppermute | solution.py:452
  7.2 13.0 %collective-permute-start = (bf16[1184,128]{1,0:T(8,128)(2,1)S(1)}, bf16[1184,128]{1,0:T(8,128)(2,1)S(1)}, u32[]{:S(2)}, u32[]{:S(2)}) collective-permute-start(bf16[1184,128]{1,0:T(8,128)(2,1)S(1)} %get-tuple-element.41), channel_id=1, source_target_pairs={{0,1},{1,0},{2,3},{3,2},{4,5},{5,4},{6,7},{7,6},{8,9},{9,8},{10,11... | collective-permute-start | bytes 909320 | tf_op jit(solution)/shard_map/ppermute | solution.py:452
  8.7 14.9 %collective-permute-start.1 = (bf16[1184,128]{1,0:T(8,128)(2,1)S(1)}, bf16[1184,128]{1,0:T(8,128)(2,1)S(1)}, u32[]{:S(2)}, u32[]{:S(2)}) collective-permute-start(bf16[1184,128]{1,0:T(8,128)(2,1)S(1)} %get-tuple-element.42), channel_id=1, source_target_pairs={{0,2},{1,3},{2,0},{3,1},{4,6},{5,7},{6,4},{7,5},{8,10},{9,11},{10,... | collective-permute-start | bytes 909320 | tf_op jit(solution)/shard_map/ppermute | solution.py:452
  10.3 13.3 %collective-permute-start.2 = (bf16[1184,128]{1,0:T(8,128)(2,1)S(1)}, bf16[1184,128]{1,0:T(8,128)(2,1)S(1)}, u32[]{:S(2)}, u32[]{:S(2)}) collective-permute-start(bf16[1184,128]{1,0:T(8,128)(2,1)S(1)} %get-tuple-element.43), channel_id=1, source_target_pairs={{0,3},{1,2},{2,1},{3,0},{4,7},{5,6},{6,5},{7,4},{8,11},{9,10},{10,... | collective-permute-start | bytes 909320 | tf_op jit(solution)/shard_map/ppermute | solution.py:452
  10.7 28.5 %collective-permute-start.7 = (bf16[4,32,1152]{2,1,0:T(8,128)(2,1)}, bf16[4,32,1152]{2,1,0:T(8,128)(2,1)}, u32[]{:S(2)}, u32[]{:S(2)}) collective-permute-start(bf16[4,32,1152]{2,1,0:T(8,128)(2,1)} %get-tuple-element.50), channel_id=1, source_target_pairs={{0,8},{4,12},{8,0},{12,4},{1,9},{5,13},{9,1},{13,5},{2,10},{6,14},... | collective-permute-start | bytes 884744 | tf_op jit(solution)/shard_map/ppermute | solution.py:452
  17.4 21.9 %collective-permute-start.8 = (bf16[4,32,1152]{2,1,0:T(8,128)(2,1)}, bf16[4,32,1152]{2,1,0:T(8,128)(2,1)}, u32[]{:S(2)}, u32[]{:S(2)}) collective-permute-start(bf16[4,32,1152]{2,1,0:T(8,128)(2,1)} %get-tuple-element.51), channel_id=1, source_target_pairs={{0,12},{4,8},{8,4},{12,0},{1,13},{5,9},{9,5},{13,1},{2,14},{6,10},... | collective-permute-start | bytes 884744 | tf_op jit(solution)/shard_map/ppermute | solution.py:452
  27.1 5.2 %collective-permute-start.4 = (bf16[288,128]{1,0:T(8,128)(2,1)S(1)}, bf16[288,128]{1,0:T(8,128)(2,1)S(1)}, u32[]{:S(2)}, u32[]{:S(2)}) collective-permute-start(bf16[288,128]{1,0:T(8,128)(2,1)S(1)} %get-tuple-element.46), channel_id=1, source_target_pairs={{0,1},{1,0},{2,3},{3,2},{4,5},{5,4},{6,7},{7,6},{8,9},{9,8},{10,11... | collective-permute-start | bytes 221192 | tf_op jit(solution)/shard_map/ppermute | solution.py:452
  28.4 4.4 %collective-permute-start.5 = (bf16[288,128]{1,0:T(8,128)(2,1)S(1)}, bf16[288,128]{1,0:T(8,128)(2,1)S(1)}, u32[]{:S(2)}, u32[]{:S(2)}) collective-permute-start(bf16[288,128]{1,0:T(8,128)(2,1)S(1)} %get-tuple-element.47), channel_id=1, source_target_pairs={{0,2},{1,3},{2,0},{3,1},{4,6},{5,7},{6,4},{7,5},{8,10},{9,11},{10,... | collective-permute-start | bytes 221192 | tf_op jit(solution)/shard_map/ppermute | solution.py:452
  29.2 5.3 %collective-permute-start.6 = (bf16[288,128]{1,0:T(8,128)(2,1)S(1)}, bf16[288,128]{1,0:T(8,128)(2,1)S(1)}, u32[]{:S(2)}, u32[]{:S(2)}) collective-permute-start(bf16[288,128]{1,0:T(8,128)(2,1)S(1)} %get-tuple-element.48), channel_id=1, source_target_pairs={{0,3},{1,2},{2,1},{3,0},{4,7},{5,6},{6,5},{7,4},{8,11},{9,10},{10,... | collective-permute-start | bytes 221192 | tf_op jit(solution)/shard_map/ppermute | solution.py:452
  34.8 6.3 %collective-permute-start.9 = (f32[8,128]{1,0:T(8,128)S(1)}, f32[8,128]{1,0:T(8,128)S(1)}, u32[]{:S(2)}, u32[]{:S(2)}) collective-permute-start(f32[8,128]{1,0:T(8,128)S(1)} %get-tuple-element.53), channel_id=1, source_target_pairs={{0,4},{4,0},{8,12},{12,8},{1,5},{5,1},{9,13},{13,9},{2,6},{6,2},{1... | collective-permute-start | bytes 12296 | tf_op jit(solution)/shard_map/ppermute | solution.py:452
  35.3 5.8 %collective-permute-start.10 = (f32[8,128]{1,0:T(8,128)S(1)}, f32[8,128]{1,0:T(8,128)S(1)}, u32[]{:S(2)}, u32[]{:S(2)}) collective-permute-start(f32[8,128]{1,0:T(8,128)S(1)} %get-tuple-element.54), channel_id=1, source_target_pairs={{0,8},{4,12},{8,0},{12,4},{1,9},{5,13},{9,1},{13,5},{2,10},{6,14},... | collective-permute-start | bytes 12296 | tf_op jit(solution)/shard_map/ppermute | solution.py:452
  37.9 5.4 %collective-permute-start.11 = (f32[8,128]{1,0:T(8,128)S(1)}, f32[8,128]{1,0:T(8,128)S(1)}, u32[]{:S(2)}, u32[]{:S(2)}) collective-permute-start(f32[8,128]{1,0:T(8,128)S(1)} %get-tuple-element.55), channel_id=1, source_target_pairs={{0,12},{4,8},{8,4},{12,0},{1,13},{5,9},{9,5},{13,1},{2,14},{6,10},... | collective-permute-start | bytes 12296 | tf_op jit(solution)/shard_map/ppermute | solution.py:452
  46.4 6.5 %collective-permute-start.14 = (f32[8,128]{1,0:T(8,128)S(1)}, f32[8,128]{1,0:T(8,128)S(1)}, u32[]{:S(2)}, u32[]{:S(2)}) collective-permute-start(f32[8,128]{1,0:T(8,128)S(1)} %get-tuple-element.63), channel_id=1, source_target_pairs={{0,4},{4,0},{8,12},{12,8},{1,5},{5,1},{9,13},{13,9},{2,6},{6,2},{1... | collective-permute-start | bytes 12296 | tf_op jit(solution)/shard_map/ppermute | solution.py:452
  46.4 6.4 %collective-permute-start.15 = (f32[8,128]{1,0:T(8,128)S(1)}, f32[8,128]{1,0:T(8,128)S(1)}, u32[]{:S(2)}, u32[]{:S(2)}) collective-permute-start(f32[8,128]{1,0:T(8,128)S(1)} %get-tuple-element.64), channel_id=1, source_target_pairs={{0,8},{4,12},{8,0},{12,4},{1,9},{5,13},{9,1},{13,5},{2,10},{6,14},... | collective-permute-start | bytes 12296 | tf_op jit(solution)/shard_map/ppermute | solution.py:452
  48.3 5.4 %collective-permute-start.16 = (f32[8,128]{1,0:T(8,128)S(1)}, f32[8,128]{1,0:T(8,128)S(1)}, u32[]{:S(2)}, u32[]{:S(2)}) collective-permute-start(f32[8,128]{1,0:T(8,128)S(1)} %get-tuple-element.65), channel_id=1, source_target_pairs={{0,12},{4,8},{8,4},{12,0},{1,13},{5,9},{9,5},{13,1},{2,14},{6,10},... | collective-permute-start | bytes 12296 | tf_op jit(solution)/shard_map/ppermute | solution.py:452
  50.9 9.8 %collective-permute-start.12 = (bf16[32,1152]{1,0:T(8,128)(2,1)S(1)}, bf16[32,1152]{1,0:T(8,128)(2,1)S(1)}, u32[]{:S(2)}, u32[]{:S(2)}) collective-permute-start(bf16[32,1152]{1,0:T(8,128)(2,1)S(1)} %get-tuple-element.57), channel_id=1, source_target_pairs={{0,4},{4,0},{8,12},{12,8},{1,5},{5,1},{9,13},{13,9},{2,6},{6,2},{1... | collective-permute-start | bytes 221192 | tf_op jit(solution)/shard_map/ppermute | solution.py:452
  51.0 9.7 %collective-permute-start.13 = (bf16[32,1152]{1,0:T(8,128)(2,1)S(1)}, bf16[32,1152]{1,0:T(8,128)(2,1)S(1)}, u32[]{:S(2)}, u32[]{:S(2)}) collective-permute-start(bf16[32,1152]{1,0:T(8,128)(2,1)S(1)} %get-tuple-element.58), channel_id=1, source_target_pairs={{0,8},{4,12},{8,0},{12,4},{1,9},{5,13},{9,1},{13,5},{2,10},{6,14},... | collective-permute-start | bytes 221192 | tf_op jit(solution)/shard_map/ppermute | solution.py:452
  53.9 4.6 %collective-permute-start.19 = (bf16[32,128]{1,0:T(8,128)(2,1)S(1)}, bf16[32,128]{1,0:T(8,128)(2,1)S(1)}, u32[]{:S(2)}, u32[]{:S(2)}) collective-permute-start(bf16[32,128]{1,0:T(8,128)(2,1)S(1)} %shard_map.126.refs_11_), channel_id=1, source_target_pairs={{0,3},{1,2},{2,1},{3,0},{4,7},{5,6},{6,5},{7,4},{8,11},{9,10},{10,... | collective-permute-start | bytes 24584 | tf_op jit(solution)/shard_map/ppermute | solution.py:452
  55.3 3.7 %collective-permute-start.18 = (bf16[32,128]{1,0:T(8,128)(2,1)S(1)}, bf16[32,128]{1,0:T(8,128)(2,1)S(1)}, u32[]{:S(2)}, u32[]{:S(2)}) collective-permute-start(bf16[32,128]{1,0:T(8,128)(2,1)S(1)} %shard_map.126.refs_11_), channel_id=1, source_target_pairs={{0,2},{1,3},{2,0},{3,1},{4,6},{5,7},{6,4},{7,5},{8,10},{9,11},{10,... | collective-permute-start | bytes 24584 | tf_op jit(solution)/shard_map/ppermute | solution.py:452
  56.9 3.7 %collective-permute-start.17 = (bf16[32,128]{1,0:T(8,128)(2,1)S(1)}, bf16[32,128]{1,0:T(8,128)(2,1)S(1)}, u32[]{:S(2)}, u32[]{:S(2)}) collective-permute-start(bf16[32,128]{1,0:T(8,128)(2,1)S(1)} %shard_map.126.refs_11_), channel_id=1, source_target_pairs={{0,1},{1,0},{2,3},{3,2},{4,5},{5,4},{6,7},{7,6},{8,9},{9,8},{10,11... | collective-permute-start | bytes 24584 | tf_op jit(solution)/shard_map/ppermute | solution.py:452
  63.5 6.1 %collective-permute-start.21 = (bf16[32,704]{1,0:T(8,128)(2,1)S(1)}, bf16[32,704]{1,0:T(8,128)(2,1)S(1)}, u32[]{:S(2)}, u32[]{:S(2)}) collective-permute-start(bf16[32,704]{1,0:T(8,128)(2,1)S(1)} %get-tuple-element.70), channel_id=1, source_target_pairs={{0,1},{1,0},{2,3},{3,2},{4,5},{5,4},{6,7},{7,6},{8,9},{9,8},{10,11... | collective-permute-start | bytes 135176 | tf_op jit(solution)/shard_map/ppermute | solution.py:452
  64.0 5.7 %collective-permute-start.22 = (bf16[32,704]{1,0:T(8,128)(2,1)S(1)}, bf16[32,704]{1,0:T(8,128)(2,1)S(1)}, u32[]{:S(2)}, u32[]{:S(2)}) collective-permute-start(bf16[32,704]{1,0:T(8,128)(2,1)S(1)} %get-tuple-element.71), channel_id=1, source_target_pairs={{0,2},{1,3},{2,0},{3,1},{4,6},{5,7},{6,4},{7,5},{8,10},{9,11},{10,... | collective-permute-start | bytes 135176 | tf_op jit(solution)/shard_map/ppermute | solution.py:452
  65.2 5.0 %collective-permute-start.23 = (bf16[32,704]{1,0:T(8,128)(2,1)S(1)}, bf16[32,704]{1,0:T(8,128)(2,1)S(1)}, u32[]{:S(2)}, u32[]{:S(2)}) collective-permute-start(bf16[32,704]{1,0:T(8,128)(2,1)S(1)} %get-tuple-element.72), channel_id=1, source_target_pairs={{0,3},{1,2},{2,1},{3,0},{4,7},{5,6},{6,5},{7,4},{8,11},{9,10},{10,... | collective-permute-start | bytes 135176 | tf_op jit(solution)/shard_map/ppermute | solution.py:452
  67.1 6.2 %collective-permute-start.20 = (bf16[32,1152]{1,0:T(8,128)(2,1)S(1)}, bf16[32,1152]{1,0:T(8,128)(2,1)S(1)}, u32[]{:S(2)}, u32[]{:S(2)}) collective-permute-start(bf16[32,1152]{1,0:T(8,128)(2,1)S(1)} %get-tuple-element.67), channel_id=1, source_target_pairs={{0,12},{4,8},{8,4},{12,0},{1,13},{5,9},{9,5},{13,1},{2,14},{6,10},... | collective-permute-start | bytes 221192 | tf_op jit(solution)/shard_map/ppermute | solution.py:452
  70.6 2.7 %collective-permute-start.24 = (bf16[56,576]{1,0:T(8,128)(2,1)S(1)}, bf16[56,576]{1,0:T(8,128)(2,1)S(1)}, u32[]{:S(2)}, u32[]{:S(2)}) collective-permute-start(bf16[56,576]{1,0:T(8,128)(2,1)S(1)} %get-tuple-element.74), channel_id=1, source_target_pairs={{0,16},{16,0},{1,17},{17,1},{2,18},{18,2},{3,19},{19,3},{4,20},{20... | collective-permute-start | bytes 193544 | tf_op jit(solution)/shard_map/ppermute | solution.py:452
  73.3 6.6 %collective-permute-start.27 = (bf16[56,576]{1,0:T(8,128)(2,1)S(1)}, bf16[56,576]{1,0:T(8,128)(2,1)S(1)}, u32[]{:S(2)}, u32[]{:S(2)}) collective-permute-start(bf16[56,576]{1,0:T(8,128)(2,1)S(1)} %shard_map.130.refs_0_), channel_id=1, source_target_pairs={{0,12},{4,8},{8,4},{12,0},{1,13},{5,9},{9,5},{13,1},{2,14},{6,10},... | collective-permute-start | bytes 193544 | tf_op jit(solution)/shard_map/ppermute | solution.py:452
  75.9 5.7 %collective-permute-start.26 = (bf16[56,576]{1,0:T(8,128)(2,1)S(1)}, bf16[56,576]{1,0:T(8,128)(2,1)S(1)}, u32[]{:S(2)}, u32[]{:S(2)}) collective-permute-start(bf16[56,576]{1,0:T(8,128)(2,1)S(1)} %shard_map.130.refs_0_), channel_id=1, source_target_pairs={{0,8},{4,12},{8,0},{12,4},{1,9},{5,13},{9,1},{13,5},{2,10},{6,14},... | collective-permute-start | bytes 193544 | tf_op jit(solution)/shard_map/ppermute | solution.py:452
  75.9 5.7 %collective-permute-start.25 = (bf16[56,576]{1,0:T(8,128)(2,1)S(1)}, bf16[56,576]{1,0:T(8,128)(2,1)S(1)}, u32[]{:S(2)}, u32[]{:S(2)}) collective-permute-start(bf16[56,576]{1,0:T(8,128)(2,1)S(1)} %shard_map.130.refs_0_), channel_id=1, source_target_pairs={{0,4},{4,0},{8,12},{12,8},{1,5},{5,1},{9,13},{13,9},{2,6},{6,2},{1... | collective-permute-start | bytes 193544 | tf_op jit(solution)/shard_map/ppermute | solution.py:452
  81.7 5.8 %collective-permute-start.30 = (bf16[56,576]{1,0:T(8,128)(2,1)S(1)}, bf16[56,576]{1,0:T(8,128)(2,1)S(1)}, u32[]{:S(2)}, u32[]{:S(2)}) collective-permute-start(bf16[56,576]{1,0:T(8,128)(2,1)S(1)} %shard_map.131.refs_0_), channel_id=1, source_target_pairs={{0,3},{1,2},{2,1},{3,0},{4,7},{5,6},{6,5},{7,4},{8,11},{9,10},{10,... | collective-permute-start | bytes 193544 | tf_op jit(solution)/shard_map/ppermute | solution.py:452
  83.1 4.7 %collective-permute-start.29 = (bf16[56,576]{1,0:T(8,128)(2,1)S(1)}, bf16[56,576]{1,0:T(8,128)(2,1)S(1)}, u32[]{:S(2)}, u32[]{:S(2)}) collective-permute-start(bf16[56,576]{1,0:T(8,128)(2,1)S(1)} %shard_map.131.refs_0_), channel_id=1, source_target_pairs={{0,2},{1,3},{2,0},{3,1},{4,6},{5,7},{6,4},{7,5},{8,10},{9,11},{10,... | collective-permute-start | bytes 193544 | tf_op jit(solution)/shard_map/ppermute | solution.py:452
  83.5 4.3 %collective-permute-start.28 = (bf16[56,576]{1,0:T(8,128)(2,1)S(1)}, bf16[56,576]{1,0:T(8,128)(2,1)S(1)}, u32[]{:S(2)}, u32[]{:S(2)}) collective-permute-start(bf16[56,576]{1,0:T(8,128)(2,1)S(1)} %shard_map.131.refs_0_), channel_id=1, source_target_pairs={{0,1},{1,0},{2,3},{3,2},{4,5},{5,4},{6,7},{7,6},{8,9},{9,8},{10,11... | collective-permute-start | bytes 193544 | tf_op jit(solution)/shard_map/ppermute | solution.py:452
  88.1 1.4 %collective-permute-start.31 = (bf16[64,1152]{1,0:T(8,128)(2,1)S(1)}, bf16[64,1152]{1,0:T(8,128)(2,1)S(1)}, u32[]{:S(2)}, u32[]{:S(2)}) collective-permute-start(bf16[64,1152]{1,0:T(8,128)(2,1)S(1)} %shard_map.132.refs_0_), channel_id=1, source_target_pairs={{0,16},{16,0},{1,17},{17,1},{2,18},{18,2},{3,19},{19,3},{4,20},{20... | collective-permute-start | bytes 442376 | tf_op jit(solution)/shard_map/ppermute | solution.py:452
  (4 other events, 105.3 us)

commit v14 on v13

--- a/solution.py
+++ b/solution.py
@@ -93,10 +93,10 @@
 
 
 def pack_kernel(n_s, n_t, sub, *refs):
-    ins, time_ins, refs = refs[:7], refs[7:11], refs[11:]
+    ins, time_ins, refs = refs[:6], refs[6:10], refs[10:]
     outs, time_outs, refs = refs[:n_s], refs[n_s : n_s + n_t - 1], refs[n_s + n_t - 1 :]
-    buffers, (time_buf, turned_ref, sems, time_sems) = refs[:7], refs[7:]
-    p_buf, at_buf, b_buf, q_buf, v_buf, k_buf, g_buf = buffers
+    buffers, (time_buf, turned_ref, sems, time_sems) = refs[:6], refs[6:]
+    p_buf, at_buf, b_buf, q_buf, v_buf, k_buf = buffers
     copies = load_all(ins, buffers, sems)
     time_copies = load_all(time_ins, [time_buf.at[index] for index in range(4)], time_sems)
     d_s, tokens = turned_ref.shape[2:]
@@ -127,10 +127,8 @@
     send(value, 2)
     copies[5].wait()
     send(flat(k_buf), 1)
-    copies[6].wait()
-    send(flat(g_buf), 3)
     for k in range(n_s):
-        outs[k][4 * d_s :] = codes_t
+        outs[k][3 * d_s :] = codes_t
     for index, copy in enumerate(time_copies):
         copy.wait()
         for k in range(1, n_t):
@@ -300,32 +298,38 @@
     grad_b_ref[RANK:] = mm(codes_v, d_vals, NT)
 
 
-def place_codes_kernel(frames, sub, *refs):
-    pieces, (out_ref, buf) = refs[:-2], refs[-2:]
+def hidden_grad_kernel(frames, n_s, sub, g_ref, at_ref, *refs):
+    *pieces, codes_ref = refs[: -n_s - 2]
+    outs, (buf, turned_ref) = refs[-n_s - 2 : -2], refs[-2:]
     patch_dev = sub * len(pieces)
+    _, d_s, tokens = turned_ref.shape
     for k, piece in enumerate(pieces):
         rows = unfold(piece[...])
         for f in range(frames):
             start = pl.multiple_of(f * patch_dev + peer("tm", k) * sub, sub)
             buf[pl.ds(start, sub)] = rows[f * sub : (f + 1) * sub]
-    out_ref[...] = buf[...].T[: 2 * RANK].astype(BF16)
-
-
-def space_backward_kernel(frames, n_s, qkv_ref, probs_ref, hidden_ref, grad_b_ref, at_ref, at_here_ref, b_here_ref, *refs):
-    packed, dcodes, sends = refs[:n_s], refs[n_s : 2 * n_s], refs[2 * n_s : 3 * n_s]
+    codes = buf[:, : 2 * RANK].astype(BF16)
+    codes_ref[...] = buf[...].T[: 2 * RANK].astype(BF16)
+    downs = jnp.concatenate([at_ref[2], at_ref[3]], axis=0)
+    grad = g_ref[0].reshape(tokens, n_s * d_s).astype(F32) + mm(codes, downs)
+    turned = grad.astype(BF16).T
+    for j in range(n_s):
+        turned_ref[j] = turned[j * d_s : (j + 1) * d_s]
+    for k in range(n_s):
+        outs[k][...] = turned_ref[peer("space", k)]
+
+
+def space_backward_kernel(frames, n_s, qkv_ref, probs_ref, hidden_ref, grad_b_ref, dcodes_ref, b_here_ref, *refs):
+    packed, grads, sends = refs[:n_s], refs[n_s : 2 * n_s], refs[2 * n_s : 3 * n_s]
     part_ref, cut_buf = refs[3 * n_s :]
     d_s = part_ref.shape[1]
     tokens = hidden_ref.shape[0]
     patch_dev = tokens // frames
     total = n_s * patch_dev
     step = min(total, 256)
-    ups = jnp.concatenate([at_here_ref[2], at_here_ref[3]], axis=0).T
-    grads = []
-    for k in range(n_s):
-        cot = packed[k][3 * d_s : 4 * d_s].astype(F32)
-        grads.append((cot + mm(ups, dcodes[k][...])).astype(BF16))
+    grads = [x[...] for x in grads]
     grad_b_q = grad_b_v = None
-    codes = [x[4 * d_s :] for x in packed]
+    codes = [x[3 * d_s :] for x in packed]
     for f in range(frames):
         keys = qkv_ref[1, f].astype(F32)
         vals = qkv_ref[2, f].astype(F32)
@@ -358,7 +362,7 @@
         grad_b_v = term_v if grad_b_v is None else grad_b_v + term_v
     part_ref[:RANK] = grad_b_q
     part_ref[RANK:] = grad_b_v
-    grad_a = mm(dcodes[0][...], hidden_ref[...])
+    grad_a = mm(dcodes_ref[...], hidden_ref[...])
     for j in range(n_s):
         here = slice(j * d_s, (j + 1) * d_s)
         cut_buf[j, :, :d_s] = grad_a[:, here].astype(BF16)
@@ -474,24 +478,23 @@
     factor = (tokens * n_d * n_t * n_s) ** (-0.5)
     here = lax.axis_index("space") * d_s
     downs = jnp.swapaxes(adapters_a, 1, 2)
-    downs_here = lax.dynamic_slice_in_dim(downs, here, d_s, 2)
     ups_here = lax.dynamic_slice_in_dim(adapters_b, here, d_s, 2)
     dma = pltpu.SemaphoreType.DMA
 
     time_arrays = [far(x) for x in (query_t, key_t, value_t, cotangent)]
     space_arrays = [
-        far(x) for x in (patches, downs, adapters_b, query_s, value_s, key_s, cotangent)
+        far(x) for x in (patches, downs, adapters_b, query_s, value_s, key_s)
     ]
     packed = call(
         functools.partial(pack_kernel, n_s, n_t, sub),
-        [shape((4 * d_s + 2 * RANK, tokens), BF16)] * n_s
+        [shape((3 * d_s + 2 * RANK, tokens), BF16)] * n_s
         + [shape((4, frames * sub, width), BF16)] * (n_t - 1),
         *space_arrays, *time_arrays,
         scratch=[pltpu.VMEM(x.shape, BF16) for x in space_arrays]
         + [
             pltpu.VMEM((4,) + query_t.shape, BF16),
-            pltpu.VMEM((4, n_s, d_s, tokens), BF16),
-            dma((7,)),
+            pltpu.VMEM((3, n_s, d_s, tokens), BF16),
+            dma((6,)),
             dma((4,)),
         ],
         hbm=True,
@@ -537,19 +540,18 @@
     out_t, dcodes, time_grad_b = timed[:n_t], timed[n_t : 2 * n_t], timed[2 * n_t]
     dcodes = exchange(dcodes, "tm")
     out_t[1:3] = hops(out_t[1:3], "tm", 1)
-    dcodes = call(
-        functools.partial(place_codes_kernel, frames, sub),
-        shape((2 * RANK, tokens), BF16),
-        *dcodes,
-        scratch=[pltpu.VMEM((tokens, 128), F32)],
-    )
-    dcodes = share(dcodes, "space")
+    dcodes, *grads = call(
+        functools.partial(hidden_grad_kernel, frames, n_s, sub),
+        [shape((2 * RANK, tokens), BF16)] + [shape((d_s, tokens), BF16)] * n_s,
+        cotangent, downs, *dcodes,
+        scratch=[pltpu.VMEM((tokens, 128), F32), pltpu.VMEM((n_s, d_s, tokens), BF16)],
+    )
+    grads = exchange(grads, "space")
     backward = call(
         functools.partial(space_backward_kernel, frames, n_s),
         [shape((2 * RANK, tokens + 2 * d_s), BF16)] * n_s + [shape((2 * RANK, d_s), F32)],
-        qkv, probs, hidden, time_grad_b, downs, downs_here, ups_here, *packed, *dcodes,
+        qkv, probs, hidden, time_grad_b, dcodes, ups_here, *packed, *grads,
         scratch=[pltpu.VMEM((n_s, 2 * RANK, 2 * d_s), BF16)],
-        after=out_t[1:3],
         carry=out_t[3:],
     )
     partial, part = backward[:n_s], backward[n_s]
@@ -562,6 +564,7 @@
         [shape(dims, BF16)] * n_d,
         part, patches, *partial,
         scratch=[pltpu.VMEM((n_d,) + dims, BF16)],
+        after=out_t[1:3],
     )
     sums = call(total_kernel, shape(dims, BF16), *exchange(sums, "dp"), after=out_t[3:])
     sums = call(total_kernel, shape(dims, BF16), *share(sums, "tm"))

time: 90.6 us -> 97 us (1.071)
  local copies, waits for them, and re-layouts: 0.19 us -> 8.73 us
  waiting for transfers between devices: 27.6 us -> 25.4 us
  Pallas kernels: 17.5 us -> 16.2 us
  starting transfers between devices: 44.2 us -> 45.4 us
    unnamed x8 -> x42, local copies, waits for them, and re-layouts: 0.02 us -> 8.64 us
    ppermute x32, waiting for transfers between devices: 27.6 us -> 25.4 us  [hops(): lax.ppermute(array, axis, [(i, i ^ k) for i in range(size)])]
    pallas_call x13, Pallas kernels: 17.5 us -> 16.2 us  [call(): pl.pallas_call(body, out_shape=outs + tuple((shape(x.shape, x.dtype) for...]
    ppermute x32, starting transfers between devices: 44.2 us -> 45.4 us  [hops(): lax.ppermute(array, axis, [(i, i ^ k) for i in range(size)])]
  transfers between devices with their start and end apart: 32 -> 32, of which waited for: 17 -> 19; matrix products, arithmetic and copies ran while one was open for 0% -> 0% of each run, Pallas kernels for 8% -> 10%
where the time goes in v14:
time: 97 us; the launch traced here: 96.6 us
  starting transfers between devices  45.4 us (47%)
  waiting for transfers between devices  25.4 us (26%)
  Pallas kernels  16.2 us (17%)
  local copies, waits for them, and re-layouts  8.73 us (9%)
    ppermute x32, starting transfers between devices, hops(): lax.ppermute(array, axis, [(i, i ^ k) for i in range(size)])  45.4 us
    ppermute x32, waiting for transfers between devices, hops(): lax.ppermute(array, axis, [(i, i ^ k) for i in range(size)])  25.4 us
    pallas_call x13, Pallas kernels, call(): pl.pallas_call(body, out_shape=outs + tuple((shape(x.shape, x.dtype) for...  16.2 us
    unnamed x42, local copies, waits for them, and re-layouts  8.64 us
  transfers between devices with their start and end apart: 32, of which 19 were waited for; matrix products, arithmetic and copies ran while one was open for 0% of the time, Pallas kernels for 10%

profile of v14, /device:TPU:0, one launch (start us, length us, event | category | flops | bytes accessed | tf_op | source)
XLA Modules:
  0.0 96.6 jit_solution(13474198832934957268)
XLA Ops:
  0.7 2.6 %shard_map.121 = (bf16[896,128]{1,0:T(8,128)(2,1)S(1)}, bf16[896,128]{1,0:T(8,128)(2,1)S(1)}, bf16[896,128]{1,0:T(8,128)(2,1)S(1)}, bf16[896,128]{1,0:T(8,128)(2...) custom-call(bf16[1,2,64,1152]{3,2,1,0:T(8,128)(2,1)} %refs_1_.5, ...), custom_call_target="tpu_custom_call" | custom-call | tf_op jit(solution)/shard_map/pallas_call | solution.py:41
  3.2 3.0 %collective-permute-start = (bf16[896,128]{1,0:T(8,128)(2,1)S(1)}, bf16[896,128]{1,0:T(8,128)(2,1)S(1)}, u32[]{:S(2)}, u32[]{:S(2)}) collective-permute-start(bf16[896,128]{1,0:T(8,128)(2,1)S(1)} %get-tuple-element.46), channel_id=1, source_target_pairs={{0,1},{1,0},{2,3},{3,2},{4,5},{5,4},{6,7},{7,6},{8,9},{9,8},{10,11... | collective-permute-start | bytes 688136 | tf_op jit(solution)/shard_map/ppermute | solution.py:456
  6.2 1.6 %collective-permute-start.3 = (bf16[4,32,1152]{2,1,0:T(8,128)(2,1)S(1)}, bf16[4,32,1152]{2,1,0:T(8,128)(2,1)S(1)}, u32[]{:S(2)}, u32[]{:S(2)}) collective-permute-start(bf16[4,32,1152]{2,1,0:T(8,128)(2,1)S(1)} %get-tuple-element.49), channel_id=1, source_target_pairs={{0,4},{4,0},{8,12},{12,8},{1,5},{5,1},{9,13},{13,9},{2,6},{6,2},{1... | collective-permute-start | bytes 884744 | tf_op jit(solution)/shard_map/ppermute | solution.py:456
  7.8 1.6 %collective-permute-start.1 = (bf16[896,128]{1,0:T(8,128)(2,1)S(1)}, bf16[896,128]{1,0:T(8,128)(2,1)S(1)}, u32[]{:S(2)}, u32[]{:S(2)}) collective-permute-start(bf16[896,128]{1,0:T(8,128)(2,1)S(1)} %get-tuple-element.47), channel_id=1, source_target_pairs={{0,2},{1,3},{2,0},{3,1},{4,6},{5,7},{6,4},{7,5},{8,10},{9,11},{10,... | collective-permute-start | bytes 688136 | tf_op jit(solution)/shard_map/ppermute | solution.py:456
  9.8 2.6 %collective-permute-start.7 = (bf16[4,32,1152]{2,1,0:T(8,128)(2,1)S(1)}, bf16[4,32,1152]{2,1,0:T(8,128)(2,1)S(1)}, u32[]{:S(2)}, u32[]{:S(2)}) collective-permute-start(bf16[4,32,1152]{2,1,0:T(8,128)(2,1)S(1)} %get-tuple-element.55), channel_id=1, source_target_pairs={{0,8},{4,12},{8,0},{12,4},{1,9},{5,13},{9,1},{13,5},{2,10},{6,14},... | collective-permute-start | bytes 884744 | tf_op jit(solution)/shard_map/ppermute | solution.py:456
  12.7 4.2 %collective-permute-start.8 = (bf16[4,32,1152]{2,1,0:T(8,128)(2,1)S(1)}, bf16[4,32,1152]{2,1,0:T(8,128)(2,1)S(1)}, u32[]{:S(2)}, u32[]{:S(2)}) collective-permute-start(bf16[4,32,1152]{2,1,0:T(8,128)(2,1)S(1)} %get-tuple-element.56), channel_id=1, source_target_pairs={{0,12},{4,8},{8,4},{12,0},{1,13},{5,9},{9,5},{13,1},{2,14},{6,10},... | collective-permute-start | bytes 884744 | tf_op jit(solution)/shard_map/ppermute | solution.py:456
  16.8 2.7 %collective-permute-done.1.refs_2_.refs_8_ = bf16[896,128]{1,0:T(8,128)(2,1)S(1)} collective-permute-done((bf16[896,128]{1,0:T(8,128)(2,1)S(1)}, bf16[896,128]{1,0:T(8,128)(2,1)S(1)}, u32[]{:S(2)}, u32[]{:S(2)}) %collective-permute-start.1) | collective-permute-done | bytes 229408 | tf_op jit(solution)/shard_map/ppermute | solution.py:456
  19.5 3.4 %shard_map.122 = (bf16[3,2,288,256]{3,2,1,0:T(8,128)(2,1)S(1)}, f32[2,4,256,256]{3,2,1,0:T(8,128)}, bf16[288,128]{1,0:T(8,128)(2,1)S(1)}, bf16[288,128]{1,0:T(8,...) custom-call(bf16[896,128]{1,0:T(8,128)(2,1)S(1)} %get-tuple-element.45.refs_0_.refs_6_, ...), custom_call_target="tpu_custom_call" | custom-call | tf_op jit(solution)/shard_map/pallas_call | solution.py:41
  24.4 1.5 %collective-permute-start.5 = (bf16[288,128]{1,0:T(8,128)(2,1)S(1)}, bf16[288,128]{1,0:T(8,128)(2,1)S(1)}, u32[]{:S(2)}, u32[]{:S(2)}) collective-permute-start(bf16[288,128]{1,0:T(8,128)(2,1)S(1)} %get-tuple-element.52), channel_id=1, source_target_pairs={{0,2},{1,3},{2,0},{3,1},{4,6},{5,7},{6,4},{7,5},{8,10},{9,11},{10,... | collective-permute-start | bytes 221192 | tf_op jit(solution)/shard_map/ppermute | solution.py:456
  25.9 1.4 %collective-permute-start.6 = (bf16[288,128]{1,0:T(8,128)(2,1)S(1)}, bf16[288,128]{1,0:T(8,128)(2,1)S(1)}, u32[]{:S(2)}, u32[]{:S(2)}) collective-permute-start(bf16[288,128]{1,0:T(8,128)(2,1)S(1)} %get-tuple-element.53), channel_id=1, source_target_pairs={{0,3},{1,2},{2,1},{3,0},{4,7},{5,6},{6,5},{7,4},{8,11},{9,10},{10,... | collective-permute-start | bytes 221192 | tf_op jit(solution)/shard_map/ppermute | solution.py:456
  28.8 2.4 %collective-permute-done.6.refs_3_ = bf16[288,128]{1,0:T(8,128)(2,1)S(1)} collective-permute-done((bf16[288,128]{1,0:T(8,128)(2,1)S(1)}, bf16[288,128]{1,0:T(8,128)(2,1)S(1)}, u32[]{:S(2)}, u32[]{:S(2)}) %collective-permute-start.6) | collective-permute-done | bytes 73760 | tf_op jit(solution)/shard_map/ppermute | solution.py:456
  32.1 2.6 %collective-permute-start.10 = (f32[8,128]{1,0:T(8,128)S(1)}, f32[8,128]{1,0:T(8,128)S(1)}, u32[]{:S(2)}, u32[]{:S(2)}) collective-permute-start(f32[8,128]{1,0:T(8,128)S(1)} %get-tuple-element.59), channel_id=1, source_target_pairs={{0,8},{4,12},{8,0},{12,4},{1,9},{5,13},{9,1},{13,5},{2,10},{6,14},... | collective-permute-start | bytes 12296 | tf_op jit(solution)/shard_map/ppermute | solution.py:456
  37.5 2.5 %collective-permute-done.11.refs_5_ = f32[8,128]{1,0:T(8,128)S(1)} collective-permute-done((f32[8,128]{1,0:T(8,128)S(1)}, f32[8,128]{1,0:T(8,128)S(1)}, u32[]{:S(2)}, u32[]{:S(2)}) %collective-permute-start.11) | collective-permute-done | bytes 4128 | tf_op jit(solution)/shard_map/ppermute | solution.py:456
  40.1 3.1 %shard_map.125 = (bf16[32,1152]{1,0:T(8,128)(2,1)S(1)}, bf16[32,1152]{1,0:T(8,128)(2,1)S(1)}, bf16[32,1152]{1,0:T(8,128)(2,1)S(1)}, bf16[32,1152]{1,0:T(8,128)(2...) custom-call(bf16[4,1152,128]{2,1,0:T(8,128)(2,1)S(1)} %shard_map.124, ...), custom_call_target="tpu_custom_call" | custom-call | tf_op jit(solution)/shard_map/pallas_call | solution.py:41
  45.1 1.9 %collective-permute-start.15 = (f32[8,128]{1,0:T(8,128)S(1)}, f32[8,128]{1,0:T(8,128)S(1)}, u32[]{:S(2)}, u32[]{:S(2)}) collective-permute-start(f32[8,128]{1,0:T(8,128)S(1)} %get-tuple-element.69), channel_id=1, source_target_pairs={{0,8},{4,12},{8,0},{12,4},{1,9},{5,13},{9,1},{13,5},{2,10},{6,14},... | collective-permute-start | bytes 12296 | tf_op jit(solution)/shard_map/ppermute | solution.py:456
  47.0 2.5 %collective-permute-start.16 = (f32[8,128]{1,0:T(8,128)S(1)}, f32[8,128]{1,0:T(8,128)S(1)}, u32[]{:S(2)}, u32[]{:S(2)}) collective-permute-start(f32[8,128]{1,0:T(8,128)S(1)} %get-tuple-element.70), channel_id=1, source_target_pairs={{0,12},{4,8},{8,4},{12,0},{1,13},{5,9},{9,5},{13,1},{2,14},{6,10},... | collective-permute-start | bytes 12296 | tf_op jit(solution)/shard_map/ppermute | solution.py:456
  49.5 1.9 %collective-permute-start.13 = (bf16[32,1152]{1,0:T(8,128)(2,1)}, bf16[32,1152]{1,0:T(8,128)(2,1)S(1)}, u32[]{:S(2)}, u32[]{:S(2)}) collective-permute-start(bf16[32,1152]{1,0:T(8,128)(2,1)} %copy-done.19), channel_id=1, source_target_pairs={{0,8},{4,12},{8,0},{12,4},{1,9},{5,13},{9,1},{13,5},{2,10},{6,14},... | collective-permute-start | bytes 221192 | tf_op jit(solution)/shard_map/ppermute | solution.py:456
  52.8 1.6 %collective-permute-start.17 = (bf16[288,128]{1,0:T(8,128)(2,1)S(1)}, bf16[288,128]{1,0:T(8,128)(2,1)S(1)}, u32[]{:S(2)}, u32[]{:S(2)}) collective-permute-start(bf16[288,128]{1,0:T(8,128)(2,1)S(1)} %get-tuple-element.73), channel_id=1, source_target_pairs={{0,1},{1,0},{2,3},{3,2},{4,5},{5,4},{6,7},{7,6},{8,9},{9,8},{10,11... | collective-permute-start | bytes 221192 | tf_op jit(solution)/shard_map/ppermute | solution.py:456
  54.9 1.5 %collective-permute-start.19 = (bf16[288,128]{1,0:T(8,128)(2,1)S(1)}, bf16[288,128]{1,0:T(8,128)(2,1)S(1)}, u32[]{:S(2)}, u32[]{:S(2)}) collective-permute-start(bf16[288,128]{1,0:T(8,128)(2,1)S(1)} %get-tuple-element.75), channel_id=1, source_target_pairs={{0,3},{1,2},{2,1},{3,0},{4,7},{5,6},{6,5},{7,4},{8,11},{9,10},{10,... | collective-permute-start | bytes 221192 | tf_op jit(solution)/shard_map/ppermute | solution.py:456
  57.3 1.5 %collective-permute-done.18.refs_12_ = bf16[288,128]{1,0:T(8,128)(2,1)S(1)} collective-permute-done((bf16[288,128]{1,0:T(8,128)(2,1)S(1)}, bf16[288,128]{1,0:T(8,128)(2,1)S(1)}, u32[]{:S(2)}, u32[]{:S(2)}) %collective-permute-start.18) | collective-permute-done | bytes 73760 | tf_op jit(solution)/shard_map/ppermute | solution.py:456
  66.0 2.6 %shard_map.127 = (bf16[32,704]{1,0:T(8,128)(2,1)S(1)}, bf16[32,704]{1,0:T(8,128)(2,1)S(1)}, bf16[32,704]{1,0:T(8,128)(2,1)S(1)}, bf16[32,704]{1,0:T(8,128)(2,1)S...) custom-call(bf16[3,2,288,256]{3,2,1,0:T(8,128)(2,1)S(1)} %copy-done.11, ...), custom_call_target="tpu_custom_call", output_to_operand_aliasing={{5}: (14, {})} | custom-call | tf_op jit(solution)/shard_map/pallas_call | solution.py:41
  69.1 1.5 %collective-permute-start.22 = (bf16[32,704]{1,0:T(8,128)(2,1)S(1)}, bf16[32,704]{1,0:T(8,128)(2,1)S(1)}, u32[]{:S(2)}, u32[]{:S(2)}) collective-permute-start(bf16[32,704]{1,0:T(8,128)(2,1)S(1)} %get-tuple-element.81), channel_id=1, source_target_pairs={{0,2},{1,3},{2,0},{3,1},{4,6},{5,7},{6,4},{7,5},{8,10},{9,11},{10,... | collective-permute-start | bytes 135176 | tf_op jit(solution)/shard_map/ppermute | solution.py:456
  70.7 1.4 %collective-permute-start.23 = (bf16[32,704]{1,0:T(8,128)(2,1)S(1)}, bf16[32,704]{1,0:T(8,128)(2,1)S(1)}, u32[]{:S(2)}, u32[]{:S(2)}) collective-permute-start(bf16[32,704]{1,0:T(8,128)(2,1)S(1)} %get-tuple-element.82), channel_id=1, source_target_pairs={{0,3},{1,2},{2,1},{3,0},{4,7},{5,6},{6,5},{7,4},{8,11},{9,10},{10,... | collective-permute-start | bytes 135176 | tf_op jit(solution)/shard_map/ppermute | solution.py:456
  72.1 2.6 %collective-permute-start.20 = (bf16[32,1152]{1,0:T(8,128)(2,1)S(1)}, bf16[32,1152]{1,0:T(8,128)(2,1)S(1)}, u32[]{:S(2)}, u32[]{:S(2)}) collective-permute-start(bf16[32,1152]{1,0:T(8,128)(2,1)S(1)} %get-tuple-element.77), channel_id=1, source_target_pairs={{0,12},{4,8},{8,4},{12,0},{1,13},{5,9},{9,5},{13,1},{2,14},{6,10},... | collective-permute-start | bytes 221192 | tf_op jit(solution)/shard_map/ppermute | solution.py:456
  76.1 2.2 %collective-permute-done.20.refs_4_.refs_2_ = bf16[32,1152]{1,0:T(8,128)(2,1)S(1)} collective-permute-done((bf16[32,1152]{1,0:T(8,128)(2,1)S(1)}, bf16[32,1152]{1,0:T(8,128)(2,1)S(1)}, u32[]{:S(2)}, u32[]{:S(2)}) %collective-permute-start.20) | collective-permute-done | bytes 73760 | tf_op jit(solution)/shard_map/ppermute | solution.py:456
  78.3 2.6 %collective-permute-start.27 = (bf16[56,576]{1,0:T(8,128)(2,1)S(1)}, bf16[56,576]{1,0:T(8,128)(2,1)S(1)}, u32[]{:S(2)}, u32[]{:S(2)}) collective-permute-start(bf16[56,576]{1,0:T(8,128)(2,1)S(1)} %shard_map.130.refs_0_), channel_id=1, source_target_pairs={{0,12},{4,8},{8,4},{12,0},{1,13},{5,9},{9,5},{13,1},{2,14},{6,10},... | collective-permute-start | bytes 193544 | tf_op jit(solution)/shard_map/ppermute | solution.py:456
  80.9 1.8 %collective-permute-start.25 = (bf16[56,576]{1,0:T(8,128)(2,1)S(1)}, bf16[56,576]{1,0:T(8,128)(2,1)S(1)}, u32[]{:S(2)}, u32[]{:S(2)}) collective-permute-start(bf16[56,576]{1,0:T(8,128)(2,1)S(1)} %shard_map.130.refs_0_), channel_id=1, source_target_pairs={{0,4},{4,0},{8,12},{12,8},{1,5},{5,1},{9,13},{13,9},{2,6},{6,2},{1... | collective-permute-start | bytes 193544 | tf_op jit(solution)/shard_map/ppermute | solution.py:456
  82.7 1.7 %collective-permute-done.27.refs_3_ = bf16[56,576]{1,0:T(8,128)(2,1)S(1)} collective-permute-done((bf16[56,576]{1,0:T(8,128)(2,1)S(1)}, bf16[56,576]{1,0:T(8,128)(2,1)S(1)}, u32[]{:S(2)}, u32[]{:S(2)}) %collective-permute-start.27) | collective-permute-done | bytes 64544 | tf_op jit(solution)/shard_map/ppermute | solution.py:456
  84.5 2.1 %collective-permute-done.26.refs_2_ = bf16[56,576]{1,0:T(8,128)(2,1)S(1)} collective-permute-done((bf16[56,576]{1,0:T(8,128)(2,1)S(1)}, bf16[56,576]{1,0:T(8,128)(2,1)S(1)}, u32[]{:S(2)}, u32[]{:S(2)}) %collective-permute-start.26) | collective-permute-done | bytes 64544 | tf_op jit(solution)/shard_map/ppermute | solution.py:456
  86.6 1.5 %collective-permute-start.30 = (bf16[56,576]{1,0:T(8,128)(2,1)S(1)}, bf16[56,576]{1,0:T(8,128)(2,1)S(1)}, u32[]{:S(2)}, u32[]{:S(2)}) collective-permute-start(bf16[56,576]{1,0:T(8,128)(2,1)S(1)} %shard_map.131.refs_0_), channel_id=1, source_target_pairs={{0,3},{1,2},{2,1},{3,0},{4,7},{5,6},{6,5},{7,4},{8,11},{9,10},{10,... | collective-permute-start | bytes 193544 | tf_op jit(solution)/shard_map/ppermute | solution.py:456
  88.1 1.6 %collective-permute-start.29 = (bf16[56,576]{1,0:T(8,128)(2,1)S(1)}, bf16[56,576]{1,0:T(8,128)(2,1)S(1)}, u32[]{:S(2)}, u32[]{:S(2)}) collective-permute-start(bf16[56,576]{1,0:T(8,128)(2,1)S(1)} %shard_map.131.refs_0_), channel_id=1, source_target_pairs={{0,2},{1,3},{2,0},{3,1},{4,6},{5,7},{6,4},{7,5},{8,10},{9,11},{10,... | collective-permute-start | bytes 193544 | tf_op jit(solution)/shard_map/ppermute | solution.py:456
  90.2 2.2 %collective-permute-done.30.refs_3_ = bf16[56,576]{1,0:T(8,128)(2,1)S(1)} collective-permute-done((bf16[56,576]{1,0:T(8,128)(2,1)S(1)}, bf16[56,576]{1,0:T(8,128)(2,1)S(1)}, u32[]{:S(2)}, u32[]{:S(2)}) %collective-permute-start.30) | collective-permute-done | bytes 64544 | tf_op jit(solution)/shard_map/ppermute | solution.py:456
  (88 shorter events, 25.8 us)
Async XLA Ops:
  3.2 9.4 %collective-permute-start = (bf16[896,128]{1,0:T(8,128)(2,1)S(1)}, bf16[896,128]{1,0:T(8,128)(2,1)S(1)}, u32[]{:S(2)}, u32[]{:S(2)}) collective-permute-start(bf16[896,128]{1,0:T(8,128)(2,1)S(1)} %get-tuple-element.46), channel_id=1, source_target_pairs={{0,1},{1,0},{2,3},{3,2},{4,5},{5,4},{6,7},{7,6},{8,9},{9,8},{10,11... | collective-permute-start | bytes 688136 | tf_op jit(solution)/shard_map/ppermute | solution.py:456
  6.2 13.3 %collective-permute-start.3 = (bf16[4,32,1152]{2,1,0:T(8,128)(2,1)S(1)}, bf16[4,32,1152]{2,1,0:T(8,128)(2,1)S(1)}, u32[]{:S(2)}, u32[]{:S(2)}) collective-permute-start(bf16[4,32,1152]{2,1,0:T(8,128)(2,1)S(1)} %get-tuple-element.49), channel_id=1, source_target_pairs={{0,4},{4,0},{8,12},{12,8},{1,5},{5,1},{9,13},{13,9},{2,6},{6,2},{1... | collective-permute-start | bytes 884744 | tf_op jit(solution)/shard_map/ppermute | solution.py:456
  7.8 11.7 %collective-permute-start.1 = (bf16[896,128]{1,0:T(8,128)(2,1)S(1)}, bf16[896,128]{1,0:T(8,128)(2,1)S(1)}, u32[]{:S(2)}, u32[]{:S(2)}) collective-permute-start(bf16[896,128]{1,0:T(8,128)(2,1)S(1)} %get-tuple-element.47), channel_id=1, source_target_pairs={{0,2},{1,3},{2,0},{3,1},{4,6},{5,7},{6,4},{7,5},{8,10},{9,11},{10,... | collective-permute-start | bytes 688136 | tf_op jit(solution)/shard_map/ppermute | solution.py:456
  9.4 10.1 %collective-permute-start.2 = (bf16[896,128]{1,0:T(8,128)(2,1)S(1)}, bf16[896,128]{1,0:T(8,128)(2,1)S(1)}, u32[]{:S(2)}, u32[]{:S(2)}) collective-permute-start(bf16[896,128]{1,0:T(8,128)(2,1)S(1)} %get-tuple-element.48), channel_id=1, source_target_pairs={{0,3},{1,2},{2,1},{3,0},{4,7},{5,6},{6,5},{7,4},{8,11},{9,10},{10,... | collective-permute-start | bytes 688136 | tf_op jit(solution)/shard_map/ppermute | solution.py:456
  9.8 26.2 %collective-permute-start.7 = (bf16[4,32,1152]{2,1,0:T(8,128)(2,1)S(1)}, bf16[4,32,1152]{2,1,0:T(8,128)(2,1)S(1)}, u32[]{:S(2)}, u32[]{:S(2)}) collective-permute-start(bf16[4,32,1152]{2,1,0:T(8,128)(2,1)S(1)} %get-tuple-element.55), channel_id=1, source_target_pairs={{0,8},{4,12},{8,0},{12,4},{1,9},{5,13},{9,1},{13,5},{2,10},{6,14},... | collective-permute-start | bytes 884744 | tf_op jit(solution)/shard_map/ppermute | solution.py:456
  12.7 23.4 %collective-permute-start.8 = (bf16[4,32,1152]{2,1,0:T(8,128)(2,1)S(1)}, bf16[4,32,1152]{2,1,0:T(8,128)(2,1)S(1)}, u32[]{:S(2)}, u32[]{:S(2)}) collective-permute-start(bf16[4,32,1152]{2,1,0:T(8,128)(2,1)S(1)} %get-tuple-element.56), channel_id=1, source_target_pairs={{0,12},{4,8},{8,4},{12,0},{1,13},{5,9},{9,5},{13,1},{2,14},{6,10},... | collective-permute-start | bytes 884744 | tf_op jit(solution)/shard_map/ppermute | solution.py:456
  23.9 4.4 %collective-permute-start.4 = (bf16[288,128]{1,0:T(8,128)(2,1)S(1)}, bf16[288,128]{1,0:T(8,128)(2,1)S(1)}, u32[]{:S(2)}, u32[]{:S(2)}) collective-permute-start(bf16[288,128]{1,0:T(8,128)(2,1)S(1)} %get-tuple-element.51), channel_id=1, source_target_pairs={{0,1},{1,0},{2,3},{3,2},{4,5},{5,4},{6,7},{7,6},{8,9},{9,8},{10,11... | collective-permute-start | bytes 221192 | tf_op jit(solution)/shard_map/ppermute | solution.py:456
  24.4 4.4 %collective-permute-start.5 = (bf16[288,128]{1,0:T(8,128)(2,1)S(1)}, bf16[288,128]{1,0:T(8,128)(2,1)S(1)}, u32[]{:S(2)}, u32[]{:S(2)}) collective-permute-start(bf16[288,128]{1,0:T(8,128)(2,1)S(1)} %get-tuple-element.52), channel_id=1, source_target_pairs={{0,2},{1,3},{2,0},{3,1},{4,6},{5,7},{6,4},{7,5},{8,10},{9,11},{10,... | collective-permute-start | bytes 221192 | tf_op jit(solution)/shard_map/ppermute | solution.py:456
  25.9 5.3 %collective-permute-start.6 = (bf16[288,128]{1,0:T(8,128)(2,1)S(1)}, bf16[288,128]{1,0:T(8,128)(2,1)S(1)}, u32[]{:S(2)}, u32[]{:S(2)}) collective-permute-start(bf16[288,128]{1,0:T(8,128)(2,1)S(1)} %get-tuple-element.53), channel_id=1, source_target_pairs={{0,3},{1,2},{2,1},{3,0},{4,7},{5,6},{6,5},{7,4},{8,11},{9,10},{10,... | collective-permute-start | bytes 221192 | tf_op jit(solution)/shard_map/ppermute | solution.py:456
  31.6 5.8 %collective-permute-start.9 = (f32[8,128]{1,0:T(8,128)S(1)}, f32[8,128]{1,0:T(8,128)S(1)}, u32[]{:S(2)}, u32[]{:S(2)}) collective-permute-start(f32[8,128]{1,0:T(8,128)S(1)} %get-tuple-element.58), channel_id=1, source_target_pairs={{0,4},{4,0},{8,12},{12,8},{1,5},{5,1},{9,13},{13,9},{2,6},{6,2},{1... | collective-permute-start | bytes 12296 | tf_op jit(solution)/shard_map/ppermute | solution.py:456
  32.1 5.5 %collective-permute-start.10 = (f32[8,128]{1,0:T(8,128)S(1)}, f32[8,128]{1,0:T(8,128)S(1)}, u32[]{:S(2)}, u32[]{:S(2)}) collective-permute-start(f32[8,128]{1,0:T(8,128)S(1)} %get-tuple-element.59), channel_id=1, source_target_pairs={{0,8},{4,12},{8,0},{12,4},{1,9},{5,13},{9,1},{13,5},{2,10},{6,14},... | collective-permute-start | bytes 12296 | tf_op jit(solution)/shard_map/ppermute | solution.py:456
  34.7 5.4 %collective-permute-start.11 = (f32[8,128]{1,0:T(8,128)S(1)}, f32[8,128]{1,0:T(8,128)S(1)}, u32[]{:S(2)}, u32[]{:S(2)}) collective-permute-start(f32[8,128]{1,0:T(8,128)S(1)} %get-tuple-element.60), channel_id=1, source_target_pairs={{0,12},{4,8},{8,4},{12,0},{1,13},{5,9},{9,5},{13,1},{2,14},{6,10},... | collective-permute-start | bytes 12296 | tf_op jit(solution)/shard_map/ppermute | solution.py:456
  45.1 6.3 %collective-permute-start.14 = (f32[8,128]{1,0:T(8,128)S(1)}, f32[8,128]{1,0:T(8,128)S(1)}, u32[]{:S(2)}, u32[]{:S(2)}) collective-permute-start(f32[8,128]{1,0:T(8,128)S(1)} %get-tuple-element.68), channel_id=1, source_target_pairs={{0,4},{4,0},{8,12},{12,8},{1,5},{5,1},{9,13},{13,9},{2,6},{6,2},{1... | collective-permute-start | bytes 12296 | tf_op jit(solution)/shard_map/ppermute | solution.py:456
  45.1 6.3 %collective-permute-start.15 = (f32[8,128]{1,0:T(8,128)S(1)}, f32[8,128]{1,0:T(8,128)S(1)}, u32[]{:S(2)}, u32[]{:S(2)}) collective-permute-start(f32[8,128]{1,0:T(8,128)S(1)} %get-tuple-element.69), channel_id=1, source_target_pairs={{0,8},{4,12},{8,0},{12,4},{1,9},{5,13},{9,1},{13,5},{2,10},{6,14},... | collective-permute-start | bytes 12296 | tf_op jit(solution)/shard_map/ppermute | solution.py:456
  47.0 5.4 %collective-permute-start.16 = (f32[8,128]{1,0:T(8,128)S(1)}, f32[8,128]{1,0:T(8,128)S(1)}, u32[]{:S(2)}, u32[]{:S(2)}) collective-permute-start(f32[8,128]{1,0:T(8,128)S(1)} %get-tuple-element.70), channel_id=1, source_target_pairs={{0,12},{4,8},{8,4},{12,0},{1,13},{5,9},{9,5},{13,1},{2,14},{6,10},... | collective-permute-start | bytes 12296 | tf_op jit(solution)/shard_map/ppermute | solution.py:456
  49.5 22.6 %collective-permute-start.12 = (bf16[32,1152]{1,0:T(8,128)(2,1)}, bf16[32,1152]{1,0:T(8,128)(2,1)S(1)}, u32[]{:S(2)}, u32[]{:S(2)}) collective-permute-start(bf16[32,1152]{1,0:T(8,128)(2,1)} %copy-done.20), channel_id=1, source_target_pairs={{0,4},{4,0},{8,12},{12,8},{1,5},{5,1},{9,13},{13,9},{2,6},{6,2},{1... | collective-permute-start | bytes 221192 | tf_op jit(solution)/shard_map/ppermute | solution.py:456
  49.5 25.2 %collective-permute-start.13 = (bf16[32,1152]{1,0:T(8,128)(2,1)}, bf16[32,1152]{1,0:T(8,128)(2,1)S(1)}, u32[]{:S(2)}, u32[]{:S(2)}) collective-permute-start(bf16[32,1152]{1,0:T(8,128)(2,1)} %copy-done.19), channel_id=1, source_target_pairs={{0,8},{4,12},{8,0},{12,4},{1,9},{5,13},{9,1},{13,5},{2,10},{6,14},... | collective-permute-start | bytes 221192 | tf_op jit(solution)/shard_map/ppermute | solution.py:456
  52.8 4.4 %collective-permute-start.17 = (bf16[288,128]{1,0:T(8,128)(2,1)S(1)}, bf16[288,128]{1,0:T(8,128)(2,1)S(1)}, u32[]{:S(2)}, u32[]{:S(2)}) collective-permute-start(bf16[288,128]{1,0:T(8,128)(2,1)S(1)} %get-tuple-element.73), channel_id=1, source_target_pairs={{0,1},{1,0},{2,3},{3,2},{4,5},{5,4},{6,7},{7,6},{8,9},{9,8},{10,11... | collective-permute-start | bytes 221192 | tf_op jit(solution)/shard_map/ppermute | solution.py:456
  54.4 4.4 %collective-permute-start.18 = (bf16[288,128]{1,0:T(8,128)(2,1)S(1)}, bf16[288,128]{1,0:T(8,128)(2,1)S(1)}, u32[]{:S(2)}, u32[]{:S(2)}) collective-permute-start(bf16[288,128]{1,0:T(8,128)(2,1)S(1)} %get-tuple-element.74), channel_id=1, source_target_pairs={{0,2},{1,3},{2,0},{3,1},{4,6},{5,7},{6,4},{7,5},{8,10},{9,11},{10,... | collective-permute-start | bytes 221192 | tf_op jit(solution)/shard_map/ppermute | solution.py:456
  54.9 5.3 %collective-permute-start.19 = (bf16[288,128]{1,0:T(8,128)(2,1)S(1)}, bf16[288,128]{1,0:T(8,128)(2,1)S(1)}, u32[]{:S(2)}, u32[]{:S(2)}) collective-permute-start(bf16[288,128]{1,0:T(8,128)(2,1)S(1)} %get-tuple-element.75), channel_id=1, source_target_pairs={{0,3},{1,2},{2,1},{3,0},{4,7},{5,6},{6,5},{7,4},{8,11},{9,10},{10,... | collective-permute-start | bytes 221192 | tf_op jit(solution)/shard_map/ppermute | solution.py:456
  68.5 6.1 %collective-permute-start.21 = (bf16[32,704]{1,0:T(8,128)(2,1)S(1)}, bf16[32,704]{1,0:T(8,128)(2,1)S(1)}, u32[]{:S(2)}, u32[]{:S(2)}) collective-permute-start(bf16[32,704]{1,0:T(8,128)(2,1)S(1)} %get-tuple-element.80), channel_id=1, source_target_pairs={{0,1},{1,0},{2,3},{3,2},{4,5},{5,4},{6,7},{7,6},{8,9},{9,8},{10,11... | collective-permute-start | bytes 135176 | tf_op jit(solution)/shard_map/ppermute | solution.py:456
  69.1 5.6 %collective-permute-start.22 = (bf16[32,704]{1,0:T(8,128)(2,1)S(1)}, bf16[32,704]{1,0:T(8,128)(2,1)S(1)}, u32[]{:S(2)}, u32[]{:S(2)}) collective-permute-start(bf16[32,704]{1,0:T(8,128)(2,1)S(1)} %get-tuple-element.81), channel_id=1, source_target_pairs={{0,2},{1,3},{2,0},{3,1},{4,6},{5,7},{6,4},{7,5},{8,10},{9,11},{10,... | collective-permute-start | bytes 135176 | tf_op jit(solution)/shard_map/ppermute | solution.py:456
  70.7 5.0 %collective-permute-start.23 = (bf16[32,704]{1,0:T(8,128)(2,1)S(1)}, bf16[32,704]{1,0:T(8,128)(2,1)S(1)}, u32[]{:S(2)}, u32[]{:S(2)}) collective-permute-start(bf16[32,704]{1,0:T(8,128)(2,1)S(1)} %get-tuple-element.82), channel_id=1, source_target_pairs={{0,3},{1,2},{2,1},{3,0},{4,7},{5,6},{6,5},{7,4},{8,11},{9,10},{10,... | collective-permute-start | bytes 135176 | tf_op jit(solution)/shard_map/ppermute | solution.py:456
  72.1 6.2 %collective-permute-start.20 = (bf16[32,1152]{1,0:T(8,128)(2,1)S(1)}, bf16[32,1152]{1,0:T(8,128)(2,1)S(1)}, u32[]{:S(2)}, u32[]{:S(2)}) collective-permute-start(bf16[32,1152]{1,0:T(8,128)(2,1)S(1)} %get-tuple-element.77), channel_id=1, source_target_pairs={{0,12},{4,8},{8,4},{12,0},{1,13},{5,9},{9,5},{13,1},{2,14},{6,10},... | collective-permute-start | bytes 221192 | tf_op jit(solution)/shard_map/ppermute | solution.py:456
  76.0 2.3 %collective-permute-start.24 = (bf16[56,576]{1,0:T(8,128)(2,1)S(1)}, bf16[56,576]{1,0:T(8,128)(2,1)S(1)}, u32[]{:S(2)}, u32[]{:S(2)}) collective-permute-start(bf16[56,576]{1,0:T(8,128)(2,1)S(1)} %get-tuple-element.84), channel_id=1, source_target_pairs={{0,16},{16,0},{1,17},{17,1},{2,18},{18,2},{3,19},{19,3},{4,20},{20... | collective-permute-start | bytes 193544 | tf_op jit(solution)/shard_map/ppermute | solution.py:456
  78.3 6.2 %collective-permute-start.27 = (bf16[56,576]{1,0:T(8,128)(2,1)S(1)}, bf16[56,576]{1,0:T(8,128)(2,1)S(1)}, u32[]{:S(2)}, u32[]{:S(2)}) collective-permute-start(bf16[56,576]{1,0:T(8,128)(2,1)S(1)} %shard_map.130.refs_0_), channel_id=1, source_target_pairs={{0,12},{4,8},{8,4},{12,0},{1,13},{5,9},{9,5},{13,1},{2,14},{6,10},... | collective-permute-start | bytes 193544 | tf_op jit(solution)/shard_map/ppermute | solution.py:456
  80.9 5.7 %collective-permute-start.26 = (bf16[56,576]{1,0:T(8,128)(2,1)S(1)}, bf16[56,576]{1,0:T(8,128)(2,1)S(1)}, u32[]{:S(2)}, u32[]{:S(2)}) collective-permute-start(bf16[56,576]{1,0:T(8,128)(2,1)S(1)} %shard_map.130.refs_0_), channel_id=1, source_target_pairs={{0,8},{4,12},{8,0},{12,4},{1,9},{5,13},{9,1},{13,5},{2,10},{6,14},... | collective-permute-start | bytes 193544 | tf_op jit(solution)/shard_map/ppermute | solution.py:456
  80.9 5.7 %collective-permute-start.25 = (bf16[56,576]{1,0:T(8,128)(2,1)S(1)}, bf16[56,576]{1,0:T(8,128)(2,1)S(1)}, u32[]{:S(2)}, u32[]{:S(2)}) collective-permute-start(bf16[56,576]{1,0:T(8,128)(2,1)S(1)} %shard_map.130.refs_0_), channel_id=1, source_target_pairs={{0,4},{4,0},{8,12},{12,8},{1,5},{5,1},{9,13},{13,9},{2,6},{6,2},{1... | collective-permute-start | bytes 193544 | tf_op jit(solution)/shard_map/ppermute | solution.py:456
  86.6 5.8 %collective-permute-start.30 = (bf16[56,576]{1,0:T(8,128)(2,1)S(1)}, bf16[56,576]{1,0:T(8,128)(2,1)S(1)}, u32[]{:S(2)}, u32[]{:S(2)}) collective-permute-start(bf16[56,576]{1,0:T(8,128)(2,1)S(1)} %shard_map.131.refs_0_), channel_id=1, source_target_pairs={{0,3},{1,2},{2,1},{3,0},{4,7},{5,6},{6,5},{7,4},{8,11},{9,10},{10,... | collective-permute-start | bytes 193544 | tf_op jit(solution)/shard_map/ppermute | solution.py:456
  88.1 4.7 %collective-permute-start.29 = (bf16[56,576]{1,0:T(8,128)(2,1)S(1)}, bf16[56,576]{1,0:T(8,128)(2,1)S(1)}, u32[]{:S(2)}, u32[]{:S(2)}) collective-permute-start(bf16[56,576]{1,0:T(8,128)(2,1)S(1)} %shard_map.131.refs_0_), channel_id=1, source_target_pairs={{0,2},{1,3},{2,0},{3,1},{4,6},{5,7},{6,4},{7,5},{8,10},{9,11},{10,... | collective-permute-start | bytes 193544 | tf_op jit(solution)/shard_map/ppermute | solution.py:456
  89.7 4.3 %collective-permute-start.28 = (bf16[56,576]{1,0:T(8,128)(2,1)S(1)}, bf16[56,576]{1,0:T(8,128)(2,1)S(1)}, u32[]{:S(2)}, u32[]{:S(2)}) collective-permute-start(bf16[56,576]{1,0:T(8,128)(2,1)S(1)} %shard_map.131.refs_0_), channel_id=1, source_target_pairs={{0,1},{1,0},{2,3},{3,2},{4,5},{5,4},{6,7},{7,6},{8,9},{9,8},{10,11... | collective-permute-start | bytes 193544 | tf_op jit(solution)/shard_map/ppermute | solution.py:456
  94.2 1.4 %collective-permute-start.31 = (bf16[64,1152]{1,0:T(8,128)(2,1)S(1)}, bf16[64,1152]{1,0:T(8,128)(2,1)S(1)}, u32[]{:S(2)}, u32[]{:S(2)}) collective-permute-start(bf16[64,1152]{1,0:T(8,128)(2,1)S(1)} %shard_map.132.refs_0_), channel_id=1, source_target_pairs={{0,16},{16,0},{1,17},{17,1},{2,18},{18,2},{3,19},{19,3},{4,20},{20... | collective-permute-start | bytes 442376 | tf_op jit(solution)/shard_map/ppermute | solution.py:456
  (21 other events, 209.6 us)

commit v15 on v14

--- a/solution.py
+++ b/solution.py
@@ -94,8 +94,9 @@
 
 def pack_kernel(n_s, n_t, sub, *refs):
     ins, time_ins, refs = refs[:6], refs[6:10], refs[10:]
-    outs, time_outs, refs = refs[:n_s], refs[n_s : n_s + n_t - 1], refs[n_s + n_t - 1 :]
-    buffers, (time_buf, turned_ref, sems, time_sems) = refs[:6], refs[6:]
+    outs, here_ref, refs = refs[:n_s], refs[n_s], refs[n_s + 1 :]
+    time_outs, refs = refs[: n_t - 1], refs[n_t - 1 :]
+    buffers, (time_buf, turned_ref, maps_ref, sems, time_sems) = refs[:6], refs[6:]
     p_buf, at_buf, b_buf, q_buf, v_buf, k_buf = buffers
     copies = load_all(ins, buffers, sems)
     time_copies = load_all(time_ins, [time_buf.at[index] for index in range(4)], time_sems)
@@ -119,6 +120,10 @@
     codes_q = mm(patches, at_buf[0], NT).astype(BF16)
     codes_v = mm(patches, at_buf[1], NT).astype(BF16)
     codes_t = jnp.concatenate([codes_q, codes_v], axis=1).T
+    maps = jnp.concatenate([b_buf[0], b_buf[1]], axis=0).T
+    for j in range(n_s):
+        maps_ref[j] = maps[j * d_s : (j + 1) * d_s]
+    here_ref[...] = maps_ref[peer("space", 0)]
     copies[3].wait()
     query = (flat(q_buf).astype(F32) + mm(codes_q, b_buf[0])).astype(BF16)
     send(query, 0)
@@ -319,7 +324,7 @@
         outs[k][...] = turned_ref[peer("space", k)]
 
 
-def space_backward_kernel(frames, n_s, qkv_ref, probs_ref, hidden_ref, grad_b_ref, dcodes_ref, b_here_ref, *refs):
+def space_backward_kernel(frames, n_s, qkv_ref, probs_ref, hidden_ref, grad_b_ref, dcodes_ref, here_ref, *refs):
     packed, grads, sends = refs[:n_s], refs[n_s : 2 * n_s], refs[2 * n_s : 3 * n_s]
     part_ref, cut_buf = refs[3 * n_s :]
     d_s = part_ref.shape[1]
@@ -327,6 +332,7 @@
     patch_dev = tokens // frames
     total = n_s * patch_dev
     step = min(total, 256)
+    b_here = here_ref[...].T
     grads = [x[...] for x in grads]
     grad_b_q = grad_b_v = None
     codes = [x[3 * d_s :] for x in packed]
@@ -351,7 +357,7 @@
             d_vals.append(dv_sum)
         d_query = jnp.concatenate(d_query, axis=0).astype(BF16)
         d_vals = jnp.concatenate(d_vals, axis=0).astype(BF16)
-        partial = jnp.concatenate([mm(b_here_ref[0], d_query), mm(b_here_ref[1], d_vals)], axis=0)
+        partial = jnp.concatenate([mm(b_here[:RANK], d_query), mm(b_here[RANK:], d_vals)], axis=0)
         for k in range(n_s):
             place = slice(f * patch_dev, (f + 1) * patch_dev)
             sends[k][:, place] = partial[:, k * patch_dev : (k + 1) * patch_dev].astype(BF16)
@@ -476,9 +482,7 @@
     d_s = width // n_s
     total = n_s * patch_dev
     factor = (tokens * n_d * n_t * n_s) ** (-0.5)
-    here = lax.axis_index("space") * d_s
     downs = jnp.swapaxes(adapters_a, 1, 2)
-    ups_here = lax.dynamic_slice_in_dim(adapters_b, here, d_s, 2)
     dma = pltpu.SemaphoreType.DMA
 
     time_arrays = [far(x) for x in (query_t, key_t, value_t, cotangent)]
@@ -488,18 +492,20 @@
     packed = call(
         functools.partial(pack_kernel, n_s, n_t, sub),
         [shape((3 * d_s + 2 * RANK, tokens), BF16)] * n_s
+        + [shape((d_s, 2 * RANK), BF16)]
         + [shape((4, frames * sub, width), BF16)] * (n_t - 1),
         *space_arrays, *time_arrays,
         scratch=[pltpu.VMEM(x.shape, BF16) for x in space_arrays]
         + [
             pltpu.VMEM((4,) + query_t.shape, BF16),
             pltpu.VMEM((3, n_s, d_s, tokens), BF16),
+            pltpu.VMEM((n_s, d_s, 2 * RANK), BF16),
             dma((6,)),
             dma((4,)),
         ],
         hbm=True,
     )
-    time_pieces = hops(packed[n_s:], "tm", 1)
+    here, time_pieces = packed[n_s], hops(packed[n_s + 1 :], "tm", 1)
     packed = exchange(packed[:n_s], "space")
     probs_dims = (frames, d_s // HEAD_DIM, total, total)
     qkv, probs, *out_s = call(
@@ -550,7 +556,7 @@
     backward = call(
         functools.partial(space_backward_kernel, frames, n_s),
         [shape((2 * RANK, tokens + 2 * d_s), BF16)] * n_s + [shape((2 * RANK, d_s), F32)],
-        qkv, probs, hidden, time_grad_b, dcodes, ups_here, *packed, *grads,
+        qkv, probs, hidden, time_grad_b, dcodes, here, *packed, *grads,
         scratch=[pltpu.VMEM((n_s, 2 * RANK, 2 * d_s), BF16)],
         carry=out_t[3:],
     )

time: 97 us -> 88.4 us (0.911)
  local copies, waits for them, and re-layouts: 8.73 us -> 0.02 us
    unnamed x42 -> x10, local copies, waits for them, and re-layouts: 8.64 us -> 0.02 us
  transfers between devices with their start and end apart: 32 -> 32, of which waited for: 19 -> 18; matrix products, arithmetic and copies ran while one was open for 0% -> 0% of each run, Pallas kernels for 10% -> 10%
where the time goes in v15:
time: 88.4 us; the launch traced here: 88.2 us
  starting transfers between devices  46.3 us (52%)
  waiting for transfers between devices  24.8 us (28%)
  Pallas kernels  16.3 us (18%)
    ppermute x32, starting transfers between devices, hops(): lax.ppermute(array, axis, [(i, i ^ k) for i in range(size)])  46.3 us
    ppermute x32, waiting for transfers between devices, hops(): lax.ppermute(array, axis, [(i, i ^ k) for i in range(size)])  24.8 us
    pallas_call x13, Pallas kernels, call(): pl.pallas_call(body, out_shape=outs + tuple((shape(x.shape, x.dtype) for...  16.3 us
  transfers between devices with their start and end apart: 32, of which 18 were waited for; matrix products, arithmetic and copies ran while one was open for 0% of the time, Pallas kernels for 10%

profile of v15, /device:TPU:0, one launch (start us, length us, event | category | flops | bytes accessed | tf_op | source)
XLA Modules:
  0.0 88.2 jit_solution(10506186490460959194)
XLA Ops:
  0.7 2.6 %shard_map.121 = (bf16[896,128]{1,0:T(8,128)(2,1)S(1)}, bf16[896,128]{1,0:T(8,128)(2,1)S(1)}, bf16[896,128]{1,0:T(8,128)(2,1)S(1)}, bf16[896,128]{1,0:T(8,128)(2...) custom-call(bf16[1,2,64,1152]{3,2,1,0:T(8,128)(2,1)} %refs_1_.5, ...), custom_call_target="tpu_custom_call" | custom-call | tf_op jit(solution)/shard_map/pallas_call | solution.py:41
  3.3 3.0 %collective-permute-start = (bf16[896,128]{1,0:T(8,128)(2,1)S(1)}, bf16[896,128]{1,0:T(8,128)(2,1)S(1)}, u32[]{:S(2)}, u32[]{:S(2)}) collective-permute-start(bf16[896,128]{1,0:T(8,128)(2,1)S(1)} %get-tuple-element.47), channel_id=1, source_target_pairs={{0,1},{1,0},{2,3},{3,2},{4,5},{5,4},{6,7},{7,6},{8,9},{9,8},{10,11... | collective-permute-start | bytes 688136 | tf_op jit(solution)/shard_map/ppermute | solution.py:462
  6.3 1.6 %collective-permute-start.3 = (bf16[4,32,1152]{2,1,0:T(8,128)(2,1)S(1)}, bf16[4,32,1152]{2,1,0:T(8,128)(2,1)S(1)}, u32[]{:S(2)}, u32[]{:S(2)}) collective-permute-start(bf16[4,32,1152]{2,1,0:T(8,128)(2,1)S(1)} %get-tuple-element.50), channel_id=1, source_target_pairs={{0,4},{4,0},{8,12},{12,8},{1,5},{5,1},{9,13},{13,9},{2,6},{6,2},{1... | collective-permute-start | bytes 884744 | tf_op jit(solution)/shard_map/ppermute | solution.py:462
  7.9 1.6 %collective-permute-start.1 = (bf16[896,128]{1,0:T(8,128)(2,1)S(1)}, bf16[896,128]{1,0:T(8,128)(2,1)S(1)}, u32[]{:S(2)}, u32[]{:S(2)}) collective-permute-start(bf16[896,128]{1,0:T(8,128)(2,1)S(1)} %get-tuple-element.48), channel_id=1, source_target_pairs={{0,2},{1,3},{2,0},{3,1},{4,6},{5,7},{6,4},{7,5},{8,10},{9,11},{10,... | collective-permute-start | bytes 688136 | tf_op jit(solution)/shard_map/ppermute | solution.py:462
  9.9 2.6 %collective-permute-start.7 = (bf16[4,32,1152]{2,1,0:T(8,128)(2,1)S(1)}, bf16[4,32,1152]{2,1,0:T(8,128)(2,1)S(1)}, u32[]{:S(2)}, u32[]{:S(2)}) collective-permute-start(bf16[4,32,1152]{2,1,0:T(8,128)(2,1)S(1)} %get-tuple-element.56), channel_id=1, source_target_pairs={{0,8},{4,12},{8,0},{12,4},{1,9},{5,13},{9,1},{13,5},{2,10},{6,14},... | collective-permute-start | bytes 884744 | tf_op jit(solution)/shard_map/ppermute | solution.py:462
  12.7 4.2 %collective-permute-start.8 = (bf16[4,32,1152]{2,1,0:T(8,128)(2,1)S(1)}, bf16[4,32,1152]{2,1,0:T(8,128)(2,1)S(1)}, u32[]{:S(2)}, u32[]{:S(2)}) collective-permute-start(bf16[4,32,1152]{2,1,0:T(8,128)(2,1)S(1)} %get-tuple-element.57), channel_id=1, source_target_pairs={{0,12},{4,8},{8,4},{12,0},{1,13},{5,9},{9,5},{13,1},{2,14},{6,10},... | collective-permute-start | bytes 884744 | tf_op jit(solution)/shard_map/ppermute | solution.py:462
  16.9 2.7 %collective-permute-done.1.refs_2_.refs_8_ = bf16[896,128]{1,0:T(8,128)(2,1)S(1)} collective-permute-done((bf16[896,128]{1,0:T(8,128)(2,1)S(1)}, bf16[896,128]{1,0:T(8,128)(2,1)S(1)}, u32[]{:S(2)}, u32[]{:S(2)}) %collective-permute-start.1) | collective-permute-done | bytes 229408 | tf_op jit(solution)/shard_map/ppermute | solution.py:462
  19.6 3.5 %shard_map.122 = (bf16[3,2,288,256]{3,2,1,0:T(8,128)(2,1)S(1)}, f32[2,4,256,256]{3,2,1,0:T(8,128)}, bf16[288,128]{1,0:T(8,128)(2,1)S(1)}, bf16[288,128]{1,0:T(8,...) custom-call(bf16[896,128]{1,0:T(8,128)(2,1)S(1)} %get-tuple-element.46.refs_0_.refs_6_, ...), custom_call_target="tpu_custom_call" | custom-call | tf_op jit(solution)/shard_map/pallas_call | solution.py:41
  23.7 1.5 %collective-permute-start.5 = (bf16[288,128]{1,0:T(8,128)(2,1)S(1)}, bf16[288,128]{1,0:T(8,128)(2,1)S(1)}, u32[]{:S(2)}, u32[]{:S(2)}) collective-permute-start(bf16[288,128]{1,0:T(8,128)(2,1)S(1)} %get-tuple-element.53), channel_id=1, source_target_pairs={{0,2},{1,3},{2,0},{3,1},{4,6},{5,7},{6,4},{7,5},{8,10},{9,11},{10,... | collective-permute-start | bytes 221192 | tf_op jit(solution)/shard_map/ppermute | solution.py:462
  25.2 1.4 %collective-permute-start.6 = (bf16[288,128]{1,0:T(8,128)(2,1)S(1)}, bf16[288,128]{1,0:T(8,128)(2,1)S(1)}, u32[]{:S(2)}, u32[]{:S(2)}) collective-permute-start(bf16[288,128]{1,0:T(8,128)(2,1)S(1)} %get-tuple-element.54), channel_id=1, source_target_pairs={{0,3},{1,2},{2,1},{3,0},{4,7},{5,6},{6,5},{7,4},{8,11},{9,10},{10,... | collective-permute-start | bytes 221192 | tf_op jit(solution)/shard_map/ppermute | solution.py:462
  28.2 2.3 %collective-permute-done.6.refs_3_ = bf16[288,128]{1,0:T(8,128)(2,1)S(1)} collective-permute-done((bf16[288,128]{1,0:T(8,128)(2,1)S(1)}, bf16[288,128]{1,0:T(8,128)(2,1)S(1)}, u32[]{:S(2)}, u32[]{:S(2)}) %collective-permute-start.6) | collective-permute-done | bytes 73760 | tf_op jit(solution)/shard_map/ppermute | solution.py:462
  31.3 2.6 %collective-permute-start.10 = (f32[8,128]{1,0:T(8,128)S(1)}, f32[8,128]{1,0:T(8,128)S(1)}, u32[]{:S(2)}, u32[]{:S(2)}) collective-permute-start(f32[8,128]{1,0:T(8,128)S(1)} %get-tuple-element.60), channel_id=1, source_target_pairs={{0,8},{4,12},{8,0},{12,4},{1,9},{5,13},{9,1},{13,5},{2,10},{6,14},... | collective-permute-start | bytes 12296 | tf_op jit(solution)/shard_map/ppermute | solution.py:462
  33.9 1.3 %collective-permute-start.11 = (f32[8,128]{1,0:T(8,128)S(1)}, f32[8,128]{1,0:T(8,128)S(1)}, u32[]{:S(2)}, u32[]{:S(2)}) collective-permute-start(f32[8,128]{1,0:T(8,128)S(1)} %get-tuple-element.61), channel_id=1, source_target_pairs={{0,12},{4,8},{8,4},{12,0},{1,13},{5,9},{9,5},{13,1},{2,14},{6,10},... | collective-permute-start | bytes 12296 | tf_op jit(solution)/shard_map/ppermute | solution.py:462
  35.2 1.4 %shard_map.124.refs_0_ = bf16[4,1152,128]{2,1,0:T(8,128)(2,1)S(1)} custom-call(bf16[1,2,64,1152]{3,2,1,0:T(8,128)(2,1)} %refs_0_.4, bf16[1,2,64,1152]{3,2,1,0:T(8,128)(2,1)} %refs_1_.3, bf16[1,2,64,1152]{3,2,1,0:T(8,128)(2,1)} %refs_2_.3, bf16[1,2,64,1152]{3,2,1,0:T(8,128)(2,1)} %refs_0_.5, bf16[4,32,1152]{2,1,0:T(8,128)(2,1)S(1)} %collective-permute-done.3.refs_4_, ...), custom_call_target="tpu_custom_call" | custom-call | tf_op jit(solution)/shard_map/pallas_call | solution.py:41
  37.7 1.6 %collective-permute-done.11.refs_5_ = f32[8,128]{1,0:T(8,128)S(1)} collective-permute-done((f32[8,128]{1,0:T(8,128)S(1)}, f32[8,128]{1,0:T(8,128)S(1)}, u32[]{:S(2)}, u32[]{:S(2)}) %collective-permute-start.11) | collective-permute-done | bytes 4128 | tf_op jit(solution)/shard_map/ppermute | solution.py:462
  39.3 3.1 %shard_map.125 = (bf16[32,1152]{1,0:T(8,128)(2,1)S(1)}, bf16[32,1152]{1,0:T(8,128)(2,1)S(1)}, bf16[32,1152]{1,0:T(8,128)(2,1)S(1)}, bf16[32,1152]{1,0:T(8,128)(2...) custom-call(bf16[4,1152,128]{2,1,0:T(8,128)(2,1)S(1)} %shard_map.124, ...), custom_call_target="tpu_custom_call" | custom-call | tf_op jit(solution)/shard_map/pallas_call | solution.py:41
  42.7 1.6 %collective-permute-start.15 = (f32[8,128]{1,0:T(8,128)S(1)}, f32[8,128]{1,0:T(8,128)S(1)}, u32[]{:S(2)}, u32[]{:S(2)}) collective-permute-start(f32[8,128]{1,0:T(8,128)S(1)} %get-tuple-element.70), channel_id=1, source_target_pairs={{0,8},{4,12},{8,0},{12,4},{1,9},{5,13},{9,1},{13,5},{2,10},{6,14},... | collective-permute-start | bytes 12296 | tf_op jit(solution)/shard_map/ppermute | solution.py:462
  44.3 2.5 %collective-permute-start.16 = (f32[8,128]{1,0:T(8,128)S(1)}, f32[8,128]{1,0:T(8,128)S(1)}, u32[]{:S(2)}, u32[]{:S(2)}) collective-permute-start(f32[8,128]{1,0:T(8,128)S(1)} %get-tuple-element.71), channel_id=1, source_target_pairs={{0,12},{4,8},{8,4},{12,0},{1,13},{5,9},{9,5},{13,1},{2,14},{6,10},... | collective-permute-start | bytes 12296 | tf_op jit(solution)/shard_map/ppermute | solution.py:462
  47.2 2.5 %collective-permute-done.16.refs_5_ = f32[8,128]{1,0:T(8,128)S(1)} collective-permute-done((f32[8,128]{1,0:T(8,128)S(1)}, f32[8,128]{1,0:T(8,128)S(1)}, u32[]{:S(2)}, u32[]{:S(2)}) %collective-permute-start.16) | collective-permute-done | bytes 4128 | tf_op jit(solution)/shard_map/ppermute | solution.py:462
  50.2 1.6 %collective-permute-start.17 = (bf16[288,128]{1,0:T(8,128)(2,1)S(1)}, bf16[288,128]{1,0:T(8,128)(2,1)S(1)}, u32[]{:S(2)}, u32[]{:S(2)}) collective-permute-start(bf16[288,128]{1,0:T(8,128)(2,1)S(1)} %get-tuple-element.75), channel_id=1, source_target_pairs={{0,1},{1,0},{2,3},{3,2},{4,5},{5,4},{6,7},{7,6},{8,9},{9,8},{10,11... | collective-permute-start | bytes 221192 | tf_op jit(solution)/shard_map/ppermute | solution.py:462
  53.7 3.0 %collective-permute-start.13 = (bf16[32,1152]{1,0:T(8,128)(2,1)S(1)}, bf16[32,1152]{1,0:T(8,128)(2,1)S(1)}, u32[]{:S(2)}, u32[]{:S(2)}) collective-permute-start(bf16[32,1152]{1,0:T(8,128)(2,1)S(1)} %get-tuple-element.64), channel_id=1, source_target_pairs={{0,8},{4,12},{8,0},{12,4},{1,9},{5,13},{9,1},{13,5},{2,10},{6,14},... | collective-permute-start | bytes 221192 | tf_op jit(solution)/shard_map/ppermute | solution.py:462
  56.8 1.3 %collective-permute-done.19.refs_13_ = bf16[288,128]{1,0:T(8,128)(2,1)S(1)} collective-permute-done((bf16[288,128]{1,0:T(8,128)(2,1)S(1)}, bf16[288,128]{1,0:T(8,128)(2,1)S(1)}, u32[]{:S(2)}, u32[]{:S(2)}) %collective-permute-start.19) | collective-permute-done | bytes 73760 | tf_op jit(solution)/shard_map/ppermute | solution.py:462
  58.1 2.6 %shard_map.127 = (bf16[32,704]{1,0:T(8,128)(2,1)S(1)}, bf16[32,704]{1,0:T(8,128)(2,1)S(1)}, bf16[32,704]{1,0:T(8,128)(2,1)S(1)}, bf16[32,704]{1,0:T(8,128)(2,1)S...) custom-call(bf16[3,2,288,256]{3,2,1,0:T(8,128)(2,1)S(1)} %get-tuple-element.65.refs_0_,, ...), custom_call_target="tpu_custom_call", output_to_operand_aliasing={{5}: (14, {})} | custom-call | tf_op jit(solution)/shard_map/pallas_call | solution.py:41
  62.2 2.1 %collective-permute-start.23 = (bf16[32,704]{1,0:T(8,128)(2,1)S(1)}, bf16[32,704]{1,0:T(8,128)(2,1)S(1)}, u32[]{:S(2)}, u32[]{:S(2)}) collective-permute-start(bf16[32,704]{1,0:T(8,128)(2,1)S(1)} %get-tuple-element.84), channel_id=1, source_target_pairs={{0,3},{1,2},{2,1},{3,0},{4,7},{5,6},{6,5},{7,4},{8,11},{9,10},{10,... | collective-permute-start | bytes 135176 | tf_op jit(solution)/shard_map/ppermute | solution.py:462
  64.3 2.2 %collective-permute-start.20 = (bf16[32,1152]{1,0:T(8,128)(2,1)S(1)}, bf16[32,1152]{1,0:T(8,128)(2,1)S(1)}, u32[]{:S(2)}, u32[]{:S(2)}) collective-permute-start(bf16[32,1152]{1,0:T(8,128)(2,1)S(1)} %get-tuple-element.79), channel_id=1, source_target_pairs={{0,12},{4,8},{8,4},{12,0},{1,13},{5,9},{9,5},{13,1},{2,14},{6,10},... | collective-permute-start | bytes 221192 | tf_op jit(solution)/shard_map/ppermute | solution.py:462
  67.7 2.8 %collective-permute-done.20.refs_4_.refs_2_ = bf16[32,1152]{1,0:T(8,128)(2,1)S(1)} collective-permute-done((bf16[32,1152]{1,0:T(8,128)(2,1)S(1)}, bf16[32,1152]{1,0:T(8,128)(2,1)S(1)}, u32[]{:S(2)}, u32[]{:S(2)}) %collective-permute-start.20) | collective-permute-done | bytes 73760 | tf_op jit(solution)/shard_map/ppermute | solution.py:462
  70.5 2.3 %collective-permute-start.27 = (bf16[56,576]{1,0:T(8,128)(2,1)S(1)}, bf16[56,576]{1,0:T(8,128)(2,1)S(1)}, u32[]{:S(2)}, u32[]{:S(2)}) collective-permute-start(bf16[56,576]{1,0:T(8,128)(2,1)S(1)} %shard_map.130.refs_0_), channel_id=1, source_target_pairs={{0,12},{4,8},{8,4},{12,0},{1,13},{5,9},{9,5},{13,1},{2,14},{6,10},... | collective-permute-start | bytes 193544 | tf_op jit(solution)/shard_map/ppermute | solution.py:462
  72.8 2.2 %collective-permute-start.25 = (bf16[56,576]{1,0:T(8,128)(2,1)S(1)}, bf16[56,576]{1,0:T(8,128)(2,1)S(1)}, u32[]{:S(2)}, u32[]{:S(2)}) collective-permute-start(bf16[56,576]{1,0:T(8,128)(2,1)S(1)} %shard_map.130.refs_0_), channel_id=1, source_target_pairs={{0,4},{4,0},{8,12},{12,8},{1,5},{5,1},{9,13},{13,9},{2,6},{6,2},{1... | collective-permute-start | bytes 193544 | tf_op jit(solution)/shard_map/ppermute | solution.py:462
  74.9 2.0 %collective-permute-done.27.refs_3_ = bf16[56,576]{1,0:T(8,128)(2,1)S(1)} collective-permute-done((bf16[56,576]{1,0:T(8,128)(2,1)S(1)}, bf16[56,576]{1,0:T(8,128)(2,1)S(1)}, u32[]{:S(2)}, u32[]{:S(2)}) %collective-permute-start.27) | collective-permute-done | bytes 64544 | tf_op jit(solution)/shard_map/ppermute | solution.py:462
  77.0 1.7 %collective-permute-done.26.refs_2_ = bf16[56,576]{1,0:T(8,128)(2,1)S(1)} collective-permute-done((bf16[56,576]{1,0:T(8,128)(2,1)S(1)}, bf16[56,576]{1,0:T(8,128)(2,1)S(1)}, u32[]{:S(2)}, u32[]{:S(2)}) %collective-permute-start.26) | collective-permute-done | bytes 64544 | tf_op jit(solution)/shard_map/ppermute | solution.py:462
  78.7 1.6 %collective-permute-start.30 = (bf16[56,576]{1,0:T(8,128)(2,1)S(1)}, bf16[56,576]{1,0:T(8,128)(2,1)S(1)}, u32[]{:S(2)}, u32[]{:S(2)}) collective-permute-start(bf16[56,576]{1,0:T(8,128)(2,1)S(1)} %shard_map.131.refs_0_), channel_id=1, source_target_pairs={{0,3},{1,2},{2,1},{3,0},{4,7},{5,6},{6,5},{7,4},{8,11},{9,10},{10,... | collective-permute-start | bytes 193544 | tf_op jit(solution)/shard_map/ppermute | solution.py:462
  82.2 2.3 %collective-permute-done.30.refs_3_ = bf16[56,576]{1,0:T(8,128)(2,1)S(1)} collective-permute-done((bf16[56,576]{1,0:T(8,128)(2,1)S(1)}, bf16[56,576]{1,0:T(8,128)(2,1)S(1)}, u32[]{:S(2)}, u32[]{:S(2)}) %collective-permute-start.30) | collective-permute-done | bytes 64544 | tf_op jit(solution)/shard_map/ppermute | solution.py:462
  (55 shorter events, 16.1 us)
Async XLA Ops:
  3.3 9.4 %collective-permute-start = (bf16[896,128]{1,0:T(8,128)(2,1)S(1)}, bf16[896,128]{1,0:T(8,128)(2,1)S(1)}, u32[]{:S(2)}, u32[]{:S(2)}) collective-permute-start(bf16[896,128]{1,0:T(8,128)(2,1)S(1)} %get-tuple-element.47), channel_id=1, source_target_pairs={{0,1},{1,0},{2,3},{3,2},{4,5},{5,4},{6,7},{7,6},{8,9},{9,8},{10,11... | collective-permute-start | bytes 688136 | tf_op jit(solution)/shard_map/ppermute | solution.py:462
  6.3 13.3 %collective-permute-start.3 = (bf16[4,32,1152]{2,1,0:T(8,128)(2,1)S(1)}, bf16[4,32,1152]{2,1,0:T(8,128)(2,1)S(1)}, u32[]{:S(2)}, u32[]{:S(2)}) collective-permute-start(bf16[4,32,1152]{2,1,0:T(8,128)(2,1)S(1)} %get-tuple-element.50), channel_id=1, source_target_pairs={{0,4},{4,0},{8,12},{12,8},{1,5},{5,1},{9,13},{13,9},{2,6},{6,2},{1... | collective-permute-start | bytes 884744 | tf_op jit(solution)/shard_map/ppermute | solution.py:462
  7.9 11.7 %collective-permute-start.1 = (bf16[896,128]{1,0:T(8,128)(2,1)S(1)}, bf16[896,128]{1,0:T(8,128)(2,1)S(1)}, u32[]{:S(2)}, u32[]{:S(2)}) collective-permute-start(bf16[896,128]{1,0:T(8,128)(2,1)S(1)} %get-tuple-element.48), channel_id=1, source_target_pairs={{0,2},{1,3},{2,0},{3,1},{4,6},{5,7},{6,4},{7,5},{8,10},{9,11},{10,... | collective-permute-start | bytes 688136 | tf_op jit(solution)/shard_map/ppermute | solution.py:462
  9.4 10.1 %collective-permute-start.2 = (bf16[896,128]{1,0:T(8,128)(2,1)S(1)}, bf16[896,128]{1,0:T(8,128)(2,1)S(1)}, u32[]{:S(2)}, u32[]{:S(2)}) collective-permute-start(bf16[896,128]{1,0:T(8,128)(2,1)S(1)} %get-tuple-element.49), channel_id=1, source_target_pairs={{0,3},{1,2},{2,1},{3,0},{4,7},{5,6},{6,5},{7,4},{8,11},{9,10},{10,... | collective-permute-start | bytes 688136 | tf_op jit(solution)/shard_map/ppermute | solution.py:462
  9.9 25.4 %collective-permute-start.7 = (bf16[4,32,1152]{2,1,0:T(8,128)(2,1)S(1)}, bf16[4,32,1152]{2,1,0:T(8,128)(2,1)S(1)}, u32[]{:S(2)}, u32[]{:S(2)}) collective-permute-start(bf16[4,32,1152]{2,1,0:T(8,128)(2,1)S(1)} %get-tuple-element.56), channel_id=1, source_target_pairs={{0,8},{4,12},{8,0},{12,4},{1,9},{5,13},{9,1},{13,5},{2,10},{6,14},... | collective-permute-start | bytes 884744 | tf_op jit(solution)/shard_map/ppermute | solution.py:462
  12.7 22.5 %collective-permute-start.8 = (bf16[4,32,1152]{2,1,0:T(8,128)(2,1)S(1)}, bf16[4,32,1152]{2,1,0:T(8,128)(2,1)S(1)}, u32[]{:S(2)}, u32[]{:S(2)}) collective-permute-start(bf16[4,32,1152]{2,1,0:T(8,128)(2,1)S(1)} %get-tuple-element.57), channel_id=1, source_target_pairs={{0,12},{4,8},{8,4},{12,0},{1,13},{5,9},{9,5},{13,1},{2,14},{6,10},... | collective-permute-start | bytes 884744 | tf_op jit(solution)/shard_map/ppermute | solution.py:462
  23.1 4.4 %collective-permute-start.4 = (bf16[288,128]{1,0:T(8,128)(2,1)S(1)}, bf16[288,128]{1,0:T(8,128)(2,1)S(1)}, u32[]{:S(2)}, u32[]{:S(2)}) collective-permute-start(bf16[288,128]{1,0:T(8,128)(2,1)S(1)} %get-tuple-element.52), channel_id=1, source_target_pairs={{0,1},{1,0},{2,3},{3,2},{4,5},{5,4},{6,7},{7,6},{8,9},{9,8},{10,11... | collective-permute-start | bytes 221192 | tf_op jit(solution)/shard_map/ppermute | solution.py:462
  23.7 4.5 %collective-permute-start.5 = (bf16[288,128]{1,0:T(8,128)(2,1)S(1)}, bf16[288,128]{1,0:T(8,128)(2,1)S(1)}, u32[]{:S(2)}, u32[]{:S(2)}) collective-permute-start(bf16[288,128]{1,0:T(8,128)(2,1)S(1)} %get-tuple-element.53), channel_id=1, source_target_pairs={{0,2},{1,3},{2,0},{3,1},{4,6},{5,7},{6,4},{7,5},{8,10},{9,11},{10,... | collective-permute-start | bytes 221192 | tf_op jit(solution)/shard_map/ppermute | solution.py:462
  25.2 5.3 %collective-permute-start.6 = (bf16[288,128]{1,0:T(8,128)(2,1)S(1)}, bf16[288,128]{1,0:T(8,128)(2,1)S(1)}, u32[]{:S(2)}, u32[]{:S(2)}) collective-permute-start(bf16[288,128]{1,0:T(8,128)(2,1)S(1)} %get-tuple-element.54), channel_id=1, source_target_pairs={{0,3},{1,2},{2,1},{3,0},{4,7},{5,6},{6,5},{7,4},{8,11},{9,10},{10,... | collective-permute-start | bytes 221192 | tf_op jit(solution)/shard_map/ppermute | solution.py:462
  30.8 5.8 %collective-permute-start.9 = (f32[8,128]{1,0:T(8,128)S(1)}, f32[8,128]{1,0:T(8,128)S(1)}, u32[]{:S(2)}, u32[]{:S(2)}) collective-permute-start(f32[8,128]{1,0:T(8,128)S(1)} %get-tuple-element.59), channel_id=1, source_target_pairs={{0,4},{4,0},{8,12},{12,8},{1,5},{5,1},{9,13},{13,9},{2,6},{6,2},{1... | collective-permute-start | bytes 12296 | tf_op jit(solution)/shard_map/ppermute | solution.py:462
  31.3 6.4 %collective-permute-start.10 = (f32[8,128]{1,0:T(8,128)S(1)}, f32[8,128]{1,0:T(8,128)S(1)}, u32[]{:S(2)}, u32[]{:S(2)}) collective-permute-start(f32[8,128]{1,0:T(8,128)S(1)} %get-tuple-element.60), channel_id=1, source_target_pairs={{0,8},{4,12},{8,0},{12,4},{1,9},{5,13},{9,1},{13,5},{2,10},{6,14},... | collective-permute-start | bytes 12296 | tf_op jit(solution)/shard_map/ppermute | solution.py:462
  33.9 5.4 %collective-permute-start.11 = (f32[8,128]{1,0:T(8,128)S(1)}, f32[8,128]{1,0:T(8,128)S(1)}, u32[]{:S(2)}, u32[]{:S(2)}) collective-permute-start(f32[8,128]{1,0:T(8,128)S(1)} %get-tuple-element.61), channel_id=1, source_target_pairs={{0,12},{4,8},{8,4},{12,0},{1,13},{5,9},{9,5},{13,1},{2,14},{6,10},... | collective-permute-start | bytes 12296 | tf_op jit(solution)/shard_map/ppermute | solution.py:462
  42.4 4.4 %collective-permute-start.14 = (f32[8,128]{1,0:T(8,128)S(1)}, f32[8,128]{1,0:T(8,128)S(1)}, u32[]{:S(2)}, u32[]{:S(2)}) collective-permute-start(f32[8,128]{1,0:T(8,128)S(1)} %get-tuple-element.69), channel_id=1, source_target_pairs={{0,4},{4,0},{8,12},{12,8},{1,5},{5,1},{9,13},{13,9},{2,6},{6,2},{1... | collective-permute-start | bytes 12296 | tf_op jit(solution)/shard_map/ppermute | solution.py:462
  42.7 4.5 %collective-permute-start.15 = (f32[8,128]{1,0:T(8,128)S(1)}, f32[8,128]{1,0:T(8,128)S(1)}, u32[]{:S(2)}, u32[]{:S(2)}) collective-permute-start(f32[8,128]{1,0:T(8,128)S(1)} %get-tuple-element.70), channel_id=1, source_target_pairs={{0,8},{4,12},{8,0},{12,4},{1,9},{5,13},{9,1},{13,5},{2,10},{6,14},... | collective-permute-start | bytes 12296 | tf_op jit(solution)/shard_map/ppermute | solution.py:462
  44.3 5.4 %collective-permute-start.16 = (f32[8,128]{1,0:T(8,128)S(1)}, f32[8,128]{1,0:T(8,128)S(1)}, u32[]{:S(2)}, u32[]{:S(2)}) collective-permute-start(f32[8,128]{1,0:T(8,128)S(1)} %get-tuple-element.71), channel_id=1, source_target_pairs={{0,12},{4,8},{8,4},{12,0},{1,13},{5,9},{9,5},{13,1},{2,14},{6,10},... | collective-permute-start | bytes 12296 | tf_op jit(solution)/shard_map/ppermute | solution.py:462
  50.2 6.6 %collective-permute-start.17 = (bf16[288,128]{1,0:T(8,128)(2,1)S(1)}, bf16[288,128]{1,0:T(8,128)(2,1)S(1)}, u32[]{:S(2)}, u32[]{:S(2)}) collective-permute-start(bf16[288,128]{1,0:T(8,128)(2,1)S(1)} %get-tuple-element.75), channel_id=1, source_target_pairs={{0,1},{1,0},{2,3},{3,2},{4,5},{5,4},{6,7},{7,6},{8,9},{9,8},{10,11... | collective-permute-start | bytes 221192 | tf_op jit(solution)/shard_map/ppermute | solution.py:462
  51.8 5.0 %collective-permute-start.18 = (bf16[288,128]{1,0:T(8,128)(2,1)S(1)}, bf16[288,128]{1,0:T(8,128)(2,1)S(1)}, u32[]{:S(2)}, u32[]{:S(2)}) collective-permute-start(bf16[288,128]{1,0:T(8,128)(2,1)S(1)} %get-tuple-element.76), channel_id=1, source_target_pairs={{0,2},{1,3},{2,0},{3,1},{4,6},{5,7},{6,4},{7,5},{8,10},{9,11},{10,... | collective-permute-start | bytes 221192 | tf_op jit(solution)/shard_map/ppermute | solution.py:462
  52.9 5.3 %collective-permute-start.19 = (bf16[288,128]{1,0:T(8,128)(2,1)S(1)}, bf16[288,128]{1,0:T(8,128)(2,1)S(1)}, u32[]{:S(2)}, u32[]{:S(2)}) collective-permute-start(bf16[288,128]{1,0:T(8,128)(2,1)S(1)} %get-tuple-element.77), channel_id=1, source_target_pairs={{0,3},{1,2},{2,1},{3,0},{4,7},{5,6},{6,5},{7,4},{8,11},{9,10},{10,... | collective-permute-start | bytes 221192 | tf_op jit(solution)/shard_map/ppermute | solution.py:462
  53.7 10.6 %collective-permute-start.12 = (bf16[32,1152]{1,0:T(8,128)(2,1)S(1)}, bf16[32,1152]{1,0:T(8,128)(2,1)S(1)}, u32[]{:S(2)}, u32[]{:S(2)}) collective-permute-start(bf16[32,1152]{1,0:T(8,128)(2,1)S(1)} %get-tuple-element.63), channel_id=1, source_target_pairs={{0,4},{4,0},{8,12},{12,8},{1,5},{5,1},{9,13},{13,9},{2,6},{6,2},{1... | collective-permute-start | bytes 221192 | tf_op jit(solution)/shard_map/ppermute | solution.py:462
  53.7 12.8 %collective-permute-start.13 = (bf16[32,1152]{1,0:T(8,128)(2,1)S(1)}, bf16[32,1152]{1,0:T(8,128)(2,1)S(1)}, u32[]{:S(2)}, u32[]{:S(2)}) collective-permute-start(bf16[32,1152]{1,0:T(8,128)(2,1)S(1)} %get-tuple-element.64), channel_id=1, source_target_pairs={{0,8},{4,12},{8,0},{12,4},{1,9},{5,13},{9,1},{13,5},{2,10},{6,14},... | collective-permute-start | bytes 221192 | tf_op jit(solution)/shard_map/ppermute | solution.py:462
  60.7 5.8 %collective-permute-start.21 = (bf16[32,704]{1,0:T(8,128)(2,1)S(1)}, bf16[32,704]{1,0:T(8,128)(2,1)S(1)}, u32[]{:S(2)}, u32[]{:S(2)}) collective-permute-start(bf16[32,704]{1,0:T(8,128)(2,1)S(1)} %get-tuple-element.82), channel_id=1, source_target_pairs={{0,1},{1,0},{2,3},{3,2},{4,5},{5,4},{6,7},{7,6},{8,9},{9,8},{10,11... | collective-permute-start | bytes 135176 | tf_op jit(solution)/shard_map/ppermute | solution.py:462
  61.3 5.2 %collective-permute-start.22 = (bf16[32,704]{1,0:T(8,128)(2,1)S(1)}, bf16[32,704]{1,0:T(8,128)(2,1)S(1)}, u32[]{:S(2)}, u32[]{:S(2)}) collective-permute-start(bf16[32,704]{1,0:T(8,128)(2,1)S(1)} %get-tuple-element.83), channel_id=1, source_target_pairs={{0,2},{1,3},{2,0},{3,1},{4,6},{5,7},{6,4},{7,5},{8,10},{9,11},{10,... | collective-permute-start | bytes 135176 | tf_op jit(solution)/shard_map/ppermute | solution.py:462
  62.2 5.0 %collective-permute-start.23 = (bf16[32,704]{1,0:T(8,128)(2,1)S(1)}, bf16[32,704]{1,0:T(8,128)(2,1)S(1)}, u32[]{:S(2)}, u32[]{:S(2)}) collective-permute-start(bf16[32,704]{1,0:T(8,128)(2,1)S(1)} %get-tuple-element.84), channel_id=1, source_target_pairs={{0,3},{1,2},{2,1},{3,0},{4,7},{5,6},{6,5},{7,4},{8,11},{9,10},{10,... | collective-permute-start | bytes 135176 | tf_op jit(solution)/shard_map/ppermute | solution.py:462
  64.3 6.2 %collective-permute-start.20 = (bf16[32,1152]{1,0:T(8,128)(2,1)S(1)}, bf16[32,1152]{1,0:T(8,128)(2,1)S(1)}, u32[]{:S(2)}, u32[]{:S(2)}) collective-permute-start(bf16[32,1152]{1,0:T(8,128)(2,1)S(1)} %get-tuple-element.79), channel_id=1, source_target_pairs={{0,12},{4,8},{8,4},{12,0},{1,13},{5,9},{9,5},{13,1},{2,14},{6,10},... | collective-permute-start | bytes 221192 | tf_op jit(solution)/shard_map/ppermute | solution.py:462
  67.6 2.9 %collective-permute-start.24 = (bf16[56,576]{1,0:T(8,128)(2,1)S(1)}, bf16[56,576]{1,0:T(8,128)(2,1)S(1)}, u32[]{:S(2)}, u32[]{:S(2)}) collective-permute-start(bf16[56,576]{1,0:T(8,128)(2,1)S(1)} %get-tuple-element.86), channel_id=1, source_target_pairs={{0,16},{16,0},{1,17},{17,1},{2,18},{18,2},{3,19},{19,3},{4,20},{20... | collective-permute-start | bytes 193544 | tf_op jit(solution)/shard_map/ppermute | solution.py:462
  70.5 6.5 %collective-permute-start.27 = (bf16[56,576]{1,0:T(8,128)(2,1)S(1)}, bf16[56,576]{1,0:T(8,128)(2,1)S(1)}, u32[]{:S(2)}, u32[]{:S(2)}) collective-permute-start(bf16[56,576]{1,0:T(8,128)(2,1)S(1)} %shard_map.130.refs_0_), channel_id=1, source_target_pairs={{0,12},{4,8},{8,4},{12,0},{1,13},{5,9},{9,5},{13,1},{2,14},{6,10},... | collective-permute-start | bytes 193544 | tf_op jit(solution)/shard_map/ppermute | solution.py:462
  72.8 5.9 %collective-permute-start.26 = (bf16[56,576]{1,0:T(8,128)(2,1)S(1)}, bf16[56,576]{1,0:T(8,128)(2,1)S(1)}, u32[]{:S(2)}, u32[]{:S(2)}) collective-permute-start(bf16[56,576]{1,0:T(8,128)(2,1)S(1)} %shard_map.130.refs_0_), channel_id=1, source_target_pairs={{0,8},{4,12},{8,0},{12,4},{1,9},{5,13},{9,1},{13,5},{2,10},{6,14},... | collective-permute-start | bytes 193544 | tf_op jit(solution)/shard_map/ppermute | solution.py:462
  72.8 5.9 %collective-permute-start.25 = (bf16[56,576]{1,0:T(8,128)(2,1)S(1)}, bf16[56,576]{1,0:T(8,128)(2,1)S(1)}, u32[]{:S(2)}, u32[]{:S(2)}) collective-permute-start(bf16[56,576]{1,0:T(8,128)(2,1)S(1)} %shard_map.130.refs_0_), channel_id=1, source_target_pairs={{0,4},{4,0},{8,12},{12,8},{1,5},{5,1},{9,13},{13,9},{2,6},{6,2},{1... | collective-permute-start | bytes 193544 | tf_op jit(solution)/shard_map/ppermute | solution.py:462
  78.7 5.9 %collective-permute-start.30 = (bf16[56,576]{1,0:T(8,128)(2,1)S(1)}, bf16[56,576]{1,0:T(8,128)(2,1)S(1)}, u32[]{:S(2)}, u32[]{:S(2)}) collective-permute-start(bf16[56,576]{1,0:T(8,128)(2,1)S(1)} %shard_map.131.refs_0_), channel_id=1, source_target_pairs={{0,3},{1,2},{2,1},{3,0},{4,7},{5,6},{6,5},{7,4},{8,11},{9,10},{10,... | collective-permute-start | bytes 193544 | tf_op jit(solution)/shard_map/ppermute | solution.py:462
  80.3 4.7 %collective-permute-start.29 = (bf16[56,576]{1,0:T(8,128)(2,1)S(1)}, bf16[56,576]{1,0:T(8,128)(2,1)S(1)}, u32[]{:S(2)}, u32[]{:S(2)}) collective-permute-start(bf16[56,576]{1,0:T(8,128)(2,1)S(1)} %shard_map.131.refs_0_), channel_id=1, source_target_pairs={{0,2},{1,3},{2,0},{3,1},{4,6},{5,7},{6,4},{7,5},{8,10},{9,11},{10,... | collective-permute-start | bytes 193544 | tf_op jit(solution)/shard_map/ppermute | solution.py:462
  81.3 4.3 %collective-permute-start.28 = (bf16[56,576]{1,0:T(8,128)(2,1)S(1)}, bf16[56,576]{1,0:T(8,128)(2,1)S(1)}, u32[]{:S(2)}, u32[]{:S(2)}) collective-permute-start(bf16[56,576]{1,0:T(8,128)(2,1)S(1)} %shard_map.131.refs_0_), channel_id=1, source_target_pairs={{0,1},{1,0},{2,3},{3,2},{4,5},{5,4},{6,7},{7,6},{8,9},{9,8},{10,11... | collective-permute-start | bytes 193544 | tf_op jit(solution)/shard_map/ppermute | solution.py:462
  85.8 1.4 %collective-permute-start.31 = (bf16[64,1152]{1,0:T(8,128)(2,1)S(1)}, bf16[64,1152]{1,0:T(8,128)(2,1)S(1)}, u32[]{:S(2)}, u32[]{:S(2)}) collective-permute-start(bf16[64,1152]{1,0:T(8,128)(2,1)S(1)} %shard_map.132.refs_0_), channel_id=1, source_target_pairs={{0,16},{16,0},{1,17},{17,1},{2,18},{18,2},{3,19},{19,3},{4,20},{20... | collective-permute-start | bytes 442376 | tf_op jit(solution)/shard_map/ppermute | solution.py:462
  (5 other events, 115.9 us)

commit v16 on v15

--- a/solution.py
+++ b/solution.py
@@ -209,7 +209,7 @@
 
 
 def hidden_kernel(n_t, n_s, *refs):
-    pieces, refs = refs[:n_s], refs[n_s:]
+    pieces, refs = refs[:n_s][::-1], refs[n_s:]
     p_ref, at_ref, hidden_ref = refs[:3]
     sends = refs[3 : 3 + n_t]
     out_buf, codes_buf = refs[3 + n_t :]
@@ -253,7 +253,7 @@
 
 
 def time_kernel(n_t, sub, x_ref, b_ref, *refs):
-    codes_refs, refs = refs[:n_t], refs[n_t:]
+    codes_refs, refs = refs[:n_t][::-1], refs[n_t:]
     outs, sends, grad_b_ref = refs[:n_t], refs[n_t : 2 * n_t], refs[2 * n_t]
     _, width, tokens = x_ref.shape
     codes = jnp.concatenate([unfold(ref[...]) for ref in codes_refs], axis=0).T
@@ -305,6 +305,7 @@
 
 def hidden_grad_kernel(frames, n_s, sub, g_ref, at_ref, *refs):
     *pieces, codes_ref = refs[: -n_s - 2]
+    pieces = pieces[::-1]
     outs, (buf, turned_ref) = refs[-n_s - 2 : -2], refs[-2:]
     patch_dev = sub * len(pieces)
     _, d_s, tokens = turned_ref.shape
@@ -325,7 +326,7 @@
 
 
 def space_backward_kernel(frames, n_s, qkv_ref, probs_ref, hidden_ref, grad_b_ref, dcodes_ref, here_ref, *refs):
-    packed, grads, sends = refs[:n_s], refs[n_s : 2 * n_s], refs[2 * n_s : 3 * n_s]
+    packed, grads, sends = refs[:n_s], refs[n_s : 2 * n_s][::-1], refs[2 * n_s : 3 * n_s]
     part_ref, cut_buf = refs[3 * n_s :]
     d_s = part_ref.shape[1]
     tokens = hidden_ref.shape[0]
@@ -385,7 +386,7 @@
 
 
 def merge_kernel(n_s, n_d, part_ref, patches_ref, *refs):
-    recvs, sends, buf = refs[:n_s], refs[n_s : n_s + n_d], refs[n_s + n_d]
+    recvs, sends, buf = refs[:n_s][::-1], refs[n_s : n_s + n_d], refs[n_s + n_d]
     d_s = part_ref.shape[1]
     tokens = recvs[0].shape[1] - 2 * d_s
     codes = add_up([recv[:, :tokens].astype(F32) for recv in recvs]).astype(BF16)
@@ -520,7 +521,7 @@
     hidden, *codes = call(
         functools.partial(hidden_kernel, n_t, n_s),
         [shape((tokens, width), BF16)] + [shape((8, 128), F32)] * n_t,
-        *out_s, patches, downs,
+        *out_s[::-1], patches, downs,
         scratch=[pltpu.VMEM((n_s, d_s, tokens), BF16), pltpu.VMEM((tokens, 128), F32)],
     )
     codes = exchange(codes, "tm")
@@ -541,38 +542,38 @@
         [shape((frames * sub, width), BF16)] * n_t
         + [shape((8, 128), F32)] * n_t
         + [shape((2 * RANK, width), F32)],
-        turned, adapters_b, *codes,
+        turned, adapters_b, *codes[::-1],
     )
     out_t, dcodes, time_grad_b = timed[:n_t], timed[n_t : 2 * n_t], timed[2 * n_t]
     dcodes = exchange(dcodes, "tm")
-    out_t[1:3] = hops(out_t[1:3], "tm", 1)
+    out_t[2:] = hops(out_t[2:], "tm", 2)
     dcodes, *grads = call(
         functools.partial(hidden_grad_kernel, frames, n_s, sub),
         [shape((2 * RANK, tokens), BF16)] + [shape((d_s, tokens), BF16)] * n_s,
-        cotangent, downs, *dcodes,
+        cotangent, downs, *dcodes[::-1],
         scratch=[pltpu.VMEM((tokens, 128), F32), pltpu.VMEM((n_s, d_s, tokens), BF16)],
     )
     grads = exchange(grads, "space")
     backward = call(
         functools.partial(space_backward_kernel, frames, n_s),
         [shape((2 * RANK, tokens + 2 * d_s), BF16)] * n_s + [shape((2 * RANK, d_s), F32)],
-        qkv, probs, hidden, time_grad_b, dcodes, here, *packed, *grads,
+        qkv, probs, hidden, time_grad_b, dcodes, here, *packed, *grads[::-1],
         scratch=[pltpu.VMEM((n_s, 2 * RANK, 2 * d_s), BF16)],
-        carry=out_t[3:],
+        carry=out_t[1:2],
     )
     partial, part = backward[:n_s], backward[n_s]
     partial = exchange(partial, "space")
-    out_t[3:] = hops(backward[n_s + 1 :], "tm", 3)
+    out_t[1:2] = hops(backward[n_s + 1 :], "tm", 1)
     n_full, n_split = 2 * RANK // n_d, 6 * RANK // n_d
     dims = ((n_s * n_full + n_split) // 2, 2 * d_s)
     sums = call(
         functools.partial(merge_kernel, n_s, n_d),
         [shape(dims, BF16)] * n_d,
-        part, patches, *partial,
+        part, patches, *partial[::-1],
         scratch=[pltpu.VMEM((n_d,) + dims, BF16)],
-        after=out_t[1:3],
-    )
-    sums = call(total_kernel, shape(dims, BF16), *exchange(sums, "dp"), after=out_t[3:])
+        after=out_t[2:],
+    )
+    sums = call(total_kernel, shape(dims, BF16), *exchange(sums, "dp"), after=out_t[1:2])
     sums = call(total_kernel, shape(dims, BF16), *share(sums, "tm"))
     sums = call(
         functools.partial(join_kernel, n_full),

time: 88.4 us -> 85.8 us (0.971)
  waiting for transfers between devices: 24.8 us -> 23.1 us
  starting transfers between devices: 46.3 us -> 45.4 us
    ppermute x32, waiting for transfers between devices: 24.8 us -> 23.1 us  [hops(): lax.ppermute(array, axis, [(i, i ^ k) for i in range(size)])]
  transfers between devices with their start and end apart: 32 -> 32, of which waited for: 18 -> 20; matrix products, arithmetic and copies ran while one was open for 0% -> 0% of each run, Pallas kernels for 10% -> 10%
where the time goes in v16:
time: 85.8 us; the launch traced here: 85.6 us
  starting transfers between devices  45.4 us (53%)
  waiting for transfers between devices  23.1 us (27%)
  Pallas kernels  16.3 us (19%)
    ppermute x32, starting transfers between devices, hops(): lax.ppermute(array, axis, [(i, i ^ k) for i in range(size)])  45.4 us
    ppermute x32, waiting for transfers between devices, hops(): lax.ppermute(array, axis, [(i, i ^ k) for i in range(size)])  23.1 us
    pallas_call x13, Pallas kernels, call(): pl.pallas_call(body, out_shape=outs + tuple((shape(x.shape, x.dtype) for...  16.3 us
  transfers between devices with their start and end apart: 32, of which 20 were waited for; matrix products, arithmetic and copies ran while one was open for 0% of the time, Pallas kernels for 10%

profile of v16, /device:TPU:0, one launch (start us, length us, event | category | flops | bytes accessed | tf_op | source)
XLA Modules:
  0.0 85.6 jit_solution(6427046821084550086)
XLA Ops:
  0.7 2.6 %shard_map.121 = (bf16[896,128]{1,0:T(8,128)(2,1)S(1)}, bf16[896,128]{1,0:T(8,128)(2,1)S(1)}, bf16[896,128]{1,0:T(8,128)(2,1)S(1)}, bf16[896,128]{1,0:T(8,128)(2...) custom-call(bf16[1,2,64,1152]{3,2,1,0:T(8,128)(2,1)} %refs_1_.5, ...), custom_call_target="tpu_custom_call" | custom-call | tf_op jit(solution)/shard_map/pallas_call | solution.py:41
  3.3 3.0 %collective-permute-start = (bf16[896,128]{1,0:T(8,128)(2,1)S(1)}, bf16[896,128]{1,0:T(8,128)(2,1)S(1)}, u32[]{:S(2)}, u32[]{:S(2)}) collective-permute-start(bf16[896,128]{1,0:T(8,128)(2,1)S(1)} %get-tuple-element.47), channel_id=1, source_target_pairs={{0,1},{1,0},{2,3},{3,2},{4,5},{5,4},{6,7},{7,6},{8,9},{9,8},{10,11... | collective-permute-start | bytes 688136 | tf_op jit(solution)/shard_map/ppermute | solution.py:463
  6.3 1.6 %collective-permute-start.3 = (bf16[4,32,1152]{2,1,0:T(8,128)(2,1)S(1)}, bf16[4,32,1152]{2,1,0:T(8,128)(2,1)S(1)}, u32[]{:S(2)}, u32[]{:S(2)}) collective-permute-start(bf16[4,32,1152]{2,1,0:T(8,128)(2,1)S(1)} %get-tuple-element.50), channel_id=1, source_target_pairs={{0,4},{4,0},{8,12},{12,8},{1,5},{5,1},{9,13},{13,9},{2,6},{6,2},{1... | collective-permute-start | bytes 884744 | tf_op jit(solution)/shard_map/ppermute | solution.py:463
  7.9 1.6 %collective-permute-start.1 = (bf16[896,128]{1,0:T(8,128)(2,1)S(1)}, bf16[896,128]{1,0:T(8,128)(2,1)S(1)}, u32[]{:S(2)}, u32[]{:S(2)}) collective-permute-start(bf16[896,128]{1,0:T(8,128)(2,1)S(1)} %get-tuple-element.48), channel_id=1, source_target_pairs={{0,2},{1,3},{2,0},{3,1},{4,6},{5,7},{6,4},{7,5},{8,10},{9,11},{10,... | collective-permute-start | bytes 688136 | tf_op jit(solution)/shard_map/ppermute | solution.py:463
  9.9 2.6 %collective-permute-start.7 = (bf16[4,32,1152]{2,1,0:T(8,128)(2,1)S(1)}, bf16[4,32,1152]{2,1,0:T(8,128)(2,1)S(1)}, u32[]{:S(2)}, u32[]{:S(2)}) collective-permute-start(bf16[4,32,1152]{2,1,0:T(8,128)(2,1)S(1)} %get-tuple-element.56), channel_id=1, source_target_pairs={{0,8},{4,12},{8,0},{12,4},{1,9},{5,13},{9,1},{13,5},{2,10},{6,14},... | collective-permute-start | bytes 884744 | tf_op jit(solution)/shard_map/ppermute | solution.py:463
  12.7 4.2 %collective-permute-start.8 = (bf16[4,32,1152]{2,1,0:T(8,128)(2,1)S(1)}, bf16[4,32,1152]{2,1,0:T(8,128)(2,1)S(1)}, u32[]{:S(2)}, u32[]{:S(2)}) collective-permute-start(bf16[4,32,1152]{2,1,0:T(8,128)(2,1)S(1)} %get-tuple-element.57), channel_id=1, source_target_pairs={{0,12},{4,8},{8,4},{12,0},{1,13},{5,9},{9,5},{13,1},{2,14},{6,10},... | collective-permute-start | bytes 884744 | tf_op jit(solution)/shard_map/ppermute | solution.py:463
  16.9 2.7 %collective-permute-done.1.refs_2_.refs_8_ = bf16[896,128]{1,0:T(8,128)(2,1)S(1)} collective-permute-done((bf16[896,128]{1,0:T(8,128)(2,1)S(1)}, bf16[896,128]{1,0:T(8,128)(2,1)S(1)}, u32[]{:S(2)}, u32[]{:S(2)}) %collective-permute-start.1) | collective-permute-done | bytes 229408 | tf_op jit(solution)/shard_map/ppermute | solution.py:463
  19.6 3.5 %shard_map.122 = (bf16[3,2,288,256]{3,2,1,0:T(8,128)(2,1)S(1)}, f32[2,4,256,256]{3,2,1,0:T(8,128)}, bf16[288,128]{1,0:T(8,128)(2,1)S(1)}, bf16[288,128]{1,0:T(8,...) custom-call(bf16[896,128]{1,0:T(8,128)(2,1)S(1)} %get-tuple-element.46.refs_0_.refs_6_, ...), custom_call_target="tpu_custom_call" | custom-call | tf_op jit(solution)/shard_map/pallas_call | solution.py:41
  23.1 1.6 %collective-permute-start.4 = (bf16[288,128]{1,0:T(8,128)(2,1)S(1)}, bf16[288,128]{1,0:T(8,128)(2,1)S(1)}, u32[]{:S(2)}, u32[]{:S(2)}) collective-permute-start(bf16[288,128]{1,0:T(8,128)(2,1)S(1)} %get-tuple-element.51), channel_id=1, source_target_pairs={{0,3},{1,2},{2,1},{3,0},{4,7},{5,6},{6,5},{7,4},{8,11},{9,10},{10,... | collective-permute-start | bytes 221192 | tf_op jit(solution)/shard_map/ppermute | solution.py:463
  25.1 1.5 %collective-permute-start.6 = (bf16[288,128]{1,0:T(8,128)(2,1)S(1)}, bf16[288,128]{1,0:T(8,128)(2,1)S(1)}, u32[]{:S(2)}, u32[]{:S(2)}) collective-permute-start(bf16[288,128]{1,0:T(8,128)(2,1)S(1)} %get-tuple-element.53), channel_id=1, source_target_pairs={{0,1},{1,0},{2,3},{3,2},{4,5},{5,4},{6,7},{7,6},{8,9},{9,8},{10,11... | collective-permute-start | bytes 221192 | tf_op jit(solution)/shard_map/ppermute | solution.py:463
  26.6 1.8 %collective-permute-done.4.refs_0_ = bf16[288,128]{1,0:T(8,128)(2,1)S(1)} collective-permute-done((bf16[288,128]{1,0:T(8,128)(2,1)S(1)}, bf16[288,128]{1,0:T(8,128)(2,1)S(1)}, u32[]{:S(2)}, u32[]{:S(2)}) %collective-permute-start.4) | collective-permute-done | bytes 73760 | tf_op jit(solution)/shard_map/ppermute | solution.py:463
  29.8 3.1 %collective-permute-start.9 = (f32[8,128]{1,0:T(8,128)S(1)}, f32[8,128]{1,0:T(8,128)S(1)}, u32[]{:S(2)}, u32[]{:S(2)}) collective-permute-start(f32[8,128]{1,0:T(8,128)S(1)} %get-tuple-element.58), channel_id=1, source_target_pairs={{0,12},{4,8},{8,4},{12,0},{1,13},{5,9},{9,5},{13,1},{2,14},{6,10},... | collective-permute-start | bytes 12296 | tf_op jit(solution)/shard_map/ppermute | solution.py:463
  33.0 1.3 %collective-permute-start.11 = (f32[8,128]{1,0:T(8,128)S(1)}, f32[8,128]{1,0:T(8,128)S(1)}, u32[]{:S(2)}, u32[]{:S(2)}) collective-permute-start(f32[8,128]{1,0:T(8,128)S(1)} %get-tuple-element.60), channel_id=1, source_target_pairs={{0,4},{4,0},{8,12},{12,8},{1,5},{5,1},{9,13},{13,9},{2,6},{6,2},{1... | collective-permute-start | bytes 12296 | tf_op jit(solution)/shard_map/ppermute | solution.py:463
  34.3 1.4 %shard_map.124.refs_0_ = bf16[4,1152,128]{2,1,0:T(8,128)(2,1)S(1)} custom-call(bf16[1,2,64,1152]{3,2,1,0:T(8,128)(2,1)} %refs_0_.4, bf16[1,2,64,1152]{3,2,1,0:T(8,128)(2,1)} %refs_1_.3, bf16[1,2,64,1152]{3,2,1,0:T(8,128)(2,1)} %refs_2_.3, bf16[1,2,64,1152]{3,2,1,0:T(8,128)(2,1)} %refs_0_.5, bf16[4,32,1152]{2,1,0:T(8,128)(2,1)S(1)} %collective-permute-done.3.refs_4_, ...), custom_call_target="tpu_custom_call" | custom-call | tf_op jit(solution)/shard_map/pallas_call | solution.py:41
  35.7 2.1 %collective-permute-done.10.refs_3_ = f32[8,128]{1,0:T(8,128)S(1)} collective-permute-done((f32[8,128]{1,0:T(8,128)S(1)}, f32[8,128]{1,0:T(8,128)S(1)}, u32[]{:S(2)}, u32[]{:S(2)}) %collective-permute-start.10) | collective-permute-done | bytes 4128 | tf_op jit(solution)/shard_map/ppermute | solution.py:463
  37.8 3.1 %shard_map.125 = (bf16[32,1152]{1,0:T(8,128)(2,1)S(1)}, bf16[32,1152]{1,0:T(8,128)(2,1)S(1)}, bf16[32,1152]{1,0:T(8,128)(2,1)S(1)}, bf16[32,1152]{1,0:T(8,128)(2...) custom-call(bf16[4,1152,128]{2,1,0:T(8,128)(2,1)S(1)} %shard_map.124, ...), custom_call_target="tpu_custom_call" | custom-call | tf_op jit(solution)/shard_map/pallas_call | solution.py:41
  40.9 2.5 %collective-permute-start.12 = (f32[8,128]{1,0:T(8,128)S(1)}, f32[8,128]{1,0:T(8,128)S(1)}, u32[]{:S(2)}, u32[]{:S(2)}) collective-permute-start(f32[8,128]{1,0:T(8,128)S(1)} %get-tuple-element.66), channel_id=1, source_target_pairs={{0,12},{4,8},{8,4},{12,0},{1,13},{5,9},{9,5},{13,1},{2,14},{6,10},... | collective-permute-start | bytes 12296 | tf_op jit(solution)/shard_map/ppermute | solution.py:463
  44.2 1.1 %collective-permute-start.14 = (f32[8,128]{1,0:T(8,128)S(1)}, f32[8,128]{1,0:T(8,128)S(1)}, u32[]{:S(2)}, u32[]{:S(2)}) collective-permute-start(f32[8,128]{1,0:T(8,128)S(1)} %get-tuple-element.68), channel_id=1, source_target_pairs={{0,4},{4,0},{8,12},{12,8},{1,5},{5,1},{9,13},{13,9},{2,6},{6,2},{1... | collective-permute-start | bytes 12296 | tf_op jit(solution)/shard_map/ppermute | solution.py:463
  46.3 1.6 %collective-permute-done.13.refs_3_ = f32[8,128]{1,0:T(8,128)S(1)} collective-permute-done((f32[8,128]{1,0:T(8,128)S(1)}, f32[8,128]{1,0:T(8,128)S(1)}, u32[]{:S(2)}, u32[]{:S(2)}) %collective-permute-start.13) | collective-permute-done | bytes 4128 | tf_op jit(solution)/shard_map/ppermute | solution.py:463
  48.3 2.6 %collective-permute-start.15 = (bf16[288,128]{1,0:T(8,128)(2,1)S(1)}, bf16[288,128]{1,0:T(8,128)(2,1)S(1)}, u32[]{:S(2)}, u32[]{:S(2)}) collective-permute-start(bf16[288,128]{1,0:T(8,128)(2,1)S(1)} %get-tuple-element.72), channel_id=1, source_target_pairs={{0,3},{1,2},{2,1},{3,0},{4,7},{5,6},{6,5},{7,4},{8,11},{9,10},{10,... | collective-permute-start | bytes 221192 | tf_op jit(solution)/shard_map/ppermute | solution.py:463
  51.9 2.0 %collective-permute-start.19 = (bf16[32,1152]{1,0:T(8,128)(2,1)S(1)}, bf16[32,1152]{1,0:T(8,128)(2,1)S(1)}, u32[]{:S(2)}, u32[]{:S(2)}) collective-permute-start(bf16[32,1152]{1,0:T(8,128)(2,1)S(1)} %get-tuple-element.78), channel_id=1, source_target_pairs={{0,8},{4,12},{8,0},{12,4},{1,9},{5,13},{9,1},{13,5},{2,10},{6,14},... | collective-permute-start | bytes 221192 | tf_op jit(solution)/shard_map/ppermute | solution.py:463
  53.9 1.4 %collective-permute-start.20 = (bf16[32,1152]{1,0:T(8,128)(2,1)S(1)}, bf16[32,1152]{1,0:T(8,128)(2,1)S(1)}, u32[]{:S(2)}, u32[]{:S(2)}) collective-permute-start(bf16[32,1152]{1,0:T(8,128)(2,1)S(1)} %get-tuple-element.79), channel_id=1, source_target_pairs={{0,12},{4,8},{8,4},{12,0},{1,13},{5,9},{9,5},{13,1},{2,14},{6,10},... | collective-permute-start | bytes 221192 | tf_op jit(solution)/shard_map/ppermute | solution.py:463
  55.7 2.6 %shard_map.127 = (bf16[32,704]{1,0:T(8,128)(2,1)S(1)}, bf16[32,704]{1,0:T(8,128)(2,1)S(1)}, bf16[32,704]{1,0:T(8,128)(2,1)S(1)}, bf16[32,704]{1,0:T(8,128)(2,1)S...) custom-call(bf16[3,2,288,256]{3,2,1,0:T(8,128)(2,1)S(1)} %get-tuple-element.63.refs_0_,, ...), custom_call_target="tpu_custom_call", output_to_operand_aliasing={{5}: (14, {})} | custom-call | tf_op jit(solution)/shard_map/pallas_call | solution.py:41
  58.3 2.2 %collective-permute-start.21 = (bf16[32,704]{1,0:T(8,128)(2,1)S(1)}, bf16[32,704]{1,0:T(8,128)(2,1)S(1)}, u32[]{:S(2)}, u32[]{:S(2)}) collective-permute-start(bf16[32,704]{1,0:T(8,128)(2,1)S(1)} %get-tuple-element.81), channel_id=1, source_target_pairs={{0,3},{1,2},{2,1},{3,0},{4,7},{5,6},{6,5},{7,4},{8,11},{9,10},{10,... | collective-permute-start | bytes 135176 | tf_op jit(solution)/shard_map/ppermute | solution.py:463
  63.4 1.2 %collective-permute-done.22.refs_3_ = bf16[32,704]{1,0:T(8,128)(2,1)S(1)} collective-permute-done((bf16[32,704]{1,0:T(8,128)(2,1)S(1)}, bf16[32,704]{1,0:T(8,128)(2,1)S(1)}, u32[]{:S(2)}, u32[]{:S(2)}) %collective-permute-start.22) | collective-permute-done | bytes 45088 | tf_op jit(solution)/shard_map/ppermute | solution.py:463
  66.7 2.5 %collective-permute-start.27 = (bf16[56,576]{1,0:T(8,128)(2,1)S(1)}, bf16[56,576]{1,0:T(8,128)(2,1)S(1)}, u32[]{:S(2)}, u32[]{:S(2)}) collective-permute-start(bf16[56,576]{1,0:T(8,128)(2,1)S(1)} %shard_map.130.refs_0_), channel_id=1, source_target_pairs={{0,12},{4,8},{8,4},{12,0},{1,13},{5,9},{9,5},{13,1},{2,14},{6,10},... | collective-permute-start | bytes 193544 | tf_op jit(solution)/shard_map/ppermute | solution.py:463
  69.2 1.9 %collective-permute-start.25 = (bf16[56,576]{1,0:T(8,128)(2,1)S(1)}, bf16[56,576]{1,0:T(8,128)(2,1)S(1)}, u32[]{:S(2)}, u32[]{:S(2)}) collective-permute-start(bf16[56,576]{1,0:T(8,128)(2,1)S(1)} %shard_map.130.refs_0_), channel_id=1, source_target_pairs={{0,4},{4,0},{8,12},{12,8},{1,5},{5,1},{9,13},{13,9},{2,6},{6,2},{1... | collective-permute-start | bytes 193544 | tf_op jit(solution)/shard_map/ppermute | solution.py:463
  71.1 2.6 %collective-permute-done.27.refs_3_ = bf16[56,576]{1,0:T(8,128)(2,1)S(1)} collective-permute-done((bf16[56,576]{1,0:T(8,128)(2,1)S(1)}, bf16[56,576]{1,0:T(8,128)(2,1)S(1)}, u32[]{:S(2)}, u32[]{:S(2)}) %collective-permute-start.27) | collective-permute-done | bytes 64544 | tf_op jit(solution)/shard_map/ppermute | solution.py:463
  73.7 2.2 %collective-permute-done.26.refs_2_ = bf16[56,576]{1,0:T(8,128)(2,1)S(1)} collective-permute-done((bf16[56,576]{1,0:T(8,128)(2,1)S(1)}, bf16[56,576]{1,0:T(8,128)(2,1)S(1)}, u32[]{:S(2)}, u32[]{:S(2)}) %collective-permute-start.26) | collective-permute-done | bytes 64544 | tf_op jit(solution)/shard_map/ppermute | solution.py:463
  76.0 2.3 %collective-permute-start.30 = (bf16[56,576]{1,0:T(8,128)(2,1)S(1)}, bf16[56,576]{1,0:T(8,128)(2,1)S(1)}, u32[]{:S(2)}, u32[]{:S(2)}) collective-permute-start(bf16[56,576]{1,0:T(8,128)(2,1)S(1)} %shard_map.131.refs_0_), channel_id=1, source_target_pairs={{0,3},{1,2},{2,1},{3,0},{4,7},{5,6},{6,5},{7,4},{8,11},{9,10},{10,... | collective-permute-start | bytes 193544 | tf_op jit(solution)/shard_map/ppermute | solution.py:463
  79.5 1.8 %collective-permute-done.30.refs_3_ = bf16[56,576]{1,0:T(8,128)(2,1)S(1)} collective-permute-done((bf16[56,576]{1,0:T(8,128)(2,1)S(1)}, bf16[56,576]{1,0:T(8,128)(2,1)S(1)}, u32[]{:S(2)}, u32[]{:S(2)}) %collective-permute-start.30) | collective-permute-done | bytes 64544 | tf_op jit(solution)/shard_map/ppermute | solution.py:463
  81.3 1.5 %collective-permute-done.29.refs_2_ = bf16[56,576]{1,0:T(8,128)(2,1)S(1)} collective-permute-done((bf16[56,576]{1,0:T(8,128)(2,1)S(1)}, bf16[56,576]{1,0:T(8,128)(2,1)S(1)}, u32[]{:S(2)}, u32[]{:S(2)}) %collective-permute-start.29) | collective-permute-done | bytes 64544 | tf_op jit(solution)/shard_map/ppermute | solution.py:463
  (55 shorter events, 15.4 us)
Async XLA Ops:
  3.3 9.4 %collective-permute-start = (bf16[896,128]{1,0:T(8,128)(2,1)S(1)}, bf16[896,128]{1,0:T(8,128)(2,1)S(1)}, u32[]{:S(2)}, u32[]{:S(2)}) collective-permute-start(bf16[896,128]{1,0:T(8,128)(2,1)S(1)} %get-tuple-element.47), channel_id=1, source_target_pairs={{0,1},{1,0},{2,3},{3,2},{4,5},{5,4},{6,7},{7,6},{8,9},{9,8},{10,11... | collective-permute-start | bytes 688136 | tf_op jit(solution)/shard_map/ppermute | solution.py:463
  6.3 13.3 %collective-permute-start.3 = (bf16[4,32,1152]{2,1,0:T(8,128)(2,1)S(1)}, bf16[4,32,1152]{2,1,0:T(8,128)(2,1)S(1)}, u32[]{:S(2)}, u32[]{:S(2)}) collective-permute-start(bf16[4,32,1152]{2,1,0:T(8,128)(2,1)S(1)} %get-tuple-element.50), channel_id=1, source_target_pairs={{0,4},{4,0},{8,12},{12,8},{1,5},{5,1},{9,13},{13,9},{2,6},{6,2},{1... | collective-permute-start | bytes 884744 | tf_op jit(solution)/shard_map/ppermute | solution.py:463
  7.9 11.7 %collective-permute-start.1 = (bf16[896,128]{1,0:T(8,128)(2,1)S(1)}, bf16[896,128]{1,0:T(8,128)(2,1)S(1)}, u32[]{:S(2)}, u32[]{:S(2)}) collective-permute-start(bf16[896,128]{1,0:T(8,128)(2,1)S(1)} %get-tuple-element.48), channel_id=1, source_target_pairs={{0,2},{1,3},{2,0},{3,1},{4,6},{5,7},{6,4},{7,5},{8,10},{9,11},{10,... | collective-permute-start | bytes 688136 | tf_op jit(solution)/shard_map/ppermute | solution.py:463
  9.4 10.1 %collective-permute-start.2 = (bf16[896,128]{1,0:T(8,128)(2,1)S(1)}, bf16[896,128]{1,0:T(8,128)(2,1)S(1)}, u32[]{:S(2)}, u32[]{:S(2)}) collective-permute-start(bf16[896,128]{1,0:T(8,128)(2,1)S(1)} %get-tuple-element.49), channel_id=1, source_target_pairs={{0,3},{1,2},{2,1},{3,0},{4,7},{5,6},{6,5},{7,4},{8,11},{9,10},{10,... | collective-permute-start | bytes 688136 | tf_op jit(solution)/shard_map/ppermute | solution.py:463
  9.9 24.4 %collective-permute-start.7 = (bf16[4,32,1152]{2,1,0:T(8,128)(2,1)S(1)}, bf16[4,32,1152]{2,1,0:T(8,128)(2,1)S(1)}, u32[]{:S(2)}, u32[]{:S(2)}) collective-permute-start(bf16[4,32,1152]{2,1,0:T(8,128)(2,1)S(1)} %get-tuple-element.56), channel_id=1, source_target_pairs={{0,8},{4,12},{8,0},{12,4},{1,9},{5,13},{9,1},{13,5},{2,10},{6,14},... | collective-permute-start | bytes 884744 | tf_op jit(solution)/shard_map/ppermute | solution.py:463
  12.7 21.6 %collective-permute-start.8 = (bf16[4,32,1152]{2,1,0:T(8,128)(2,1)S(1)}, bf16[4,32,1152]{2,1,0:T(8,128)(2,1)S(1)}, u32[]{:S(2)}, u32[]{:S(2)}) collective-permute-start(bf16[4,32,1152]{2,1,0:T(8,128)(2,1)S(1)} %get-tuple-element.57), channel_id=1, source_target_pairs={{0,12},{4,8},{8,4},{12,0},{1,13},{5,9},{9,5},{13,1},{2,14},{6,10},... | collective-permute-start | bytes 884744 | tf_op jit(solution)/shard_map/ppermute | solution.py:463
  23.1 5.3 %collective-permute-start.4 = (bf16[288,128]{1,0:T(8,128)(2,1)S(1)}, bf16[288,128]{1,0:T(8,128)(2,1)S(1)}, u32[]{:S(2)}, u32[]{:S(2)}) collective-permute-start(bf16[288,128]{1,0:T(8,128)(2,1)S(1)} %get-tuple-element.51), channel_id=1, source_target_pairs={{0,3},{1,2},{2,1},{3,0},{4,7},{5,6},{6,5},{7,4},{8,11},{9,10},{10,... | collective-permute-start | bytes 221192 | tf_op jit(solution)/shard_map/ppermute | solution.py:463
  24.6 4.5 %collective-permute-start.5 = (bf16[288,128]{1,0:T(8,128)(2,1)S(1)}, bf16[288,128]{1,0:T(8,128)(2,1)S(1)}, u32[]{:S(2)}, u32[]{:S(2)}) collective-permute-start(bf16[288,128]{1,0:T(8,128)(2,1)S(1)} %get-tuple-element.52), channel_id=1, source_target_pairs={{0,2},{1,3},{2,0},{3,1},{4,6},{5,7},{6,4},{7,5},{8,10},{9,11},{10,... | collective-permute-start | bytes 221192 | tf_op jit(solution)/shard_map/ppermute | solution.py:463
  25.1 4.4 %collective-permute-start.6 = (bf16[288,128]{1,0:T(8,128)(2,1)S(1)}, bf16[288,128]{1,0:T(8,128)(2,1)S(1)}, u32[]{:S(2)}, u32[]{:S(2)}) collective-permute-start(bf16[288,128]{1,0:T(8,128)(2,1)S(1)} %get-tuple-element.53), channel_id=1, source_target_pairs={{0,1},{1,0},{2,3},{3,2},{4,5},{5,4},{6,7},{7,6},{8,9},{9,8},{10,11... | collective-permute-start | bytes 221192 | tf_op jit(solution)/shard_map/ppermute | solution.py:463
  29.8 5.8 %collective-permute-start.9 = (f32[8,128]{1,0:T(8,128)S(1)}, f32[8,128]{1,0:T(8,128)S(1)}, u32[]{:S(2)}, u32[]{:S(2)}) collective-permute-start(f32[8,128]{1,0:T(8,128)S(1)} %get-tuple-element.58), channel_id=1, source_target_pairs={{0,12},{4,8},{8,4},{12,0},{1,13},{5,9},{9,5},{13,1},{2,14},{6,10},... | collective-permute-start | bytes 12296 | tf_op jit(solution)/shard_map/ppermute | solution.py:463
  33.0 4.8 %collective-permute-start.10 = (f32[8,128]{1,0:T(8,128)S(1)}, f32[8,128]{1,0:T(8,128)S(1)}, u32[]{:S(2)}, u32[]{:S(2)}) collective-permute-start(f32[8,128]{1,0:T(8,128)S(1)} %get-tuple-element.59), channel_id=1, source_target_pairs={{0,8},{4,12},{8,0},{12,4},{1,9},{5,13},{9,1},{13,5},{2,10},{6,14},... | collective-permute-start | bytes 12296 | tf_op jit(solution)/shard_map/ppermute | solution.py:463
  33.0 4.8 %collective-permute-start.11 = (f32[8,128]{1,0:T(8,128)S(1)}, f32[8,128]{1,0:T(8,128)S(1)}, u32[]{:S(2)}, u32[]{:S(2)}) collective-permute-start(f32[8,128]{1,0:T(8,128)S(1)} %get-tuple-element.60), channel_id=1, source_target_pairs={{0,4},{4,0},{8,12},{12,8},{1,5},{5,1},{9,13},{13,9},{2,6},{6,2},{1... | collective-permute-start | bytes 12296 | tf_op jit(solution)/shard_map/ppermute | solution.py:463
  40.9 5.4 %collective-permute-start.12 = (f32[8,128]{1,0:T(8,128)S(1)}, f32[8,128]{1,0:T(8,128)S(1)}, u32[]{:S(2)}, u32[]{:S(2)}) collective-permute-start(f32[8,128]{1,0:T(8,128)S(1)} %get-tuple-element.66), channel_id=1, source_target_pairs={{0,12},{4,8},{8,4},{12,0},{1,13},{5,9},{9,5},{13,1},{2,14},{6,10},... | collective-permute-start | bytes 12296 | tf_op jit(solution)/shard_map/ppermute | solution.py:463
  43.4 4.5 %collective-permute-start.13 = (f32[8,128]{1,0:T(8,128)S(1)}, f32[8,128]{1,0:T(8,128)S(1)}, u32[]{:S(2)}, u32[]{:S(2)}) collective-permute-start(f32[8,128]{1,0:T(8,128)S(1)} %get-tuple-element.67), channel_id=1, source_target_pairs={{0,8},{4,12},{8,0},{12,4},{1,9},{5,13},{9,1},{13,5},{2,10},{6,14},... | collective-permute-start | bytes 12296 | tf_op jit(solution)/shard_map/ppermute | solution.py:463
  44.2 3.7 %collective-permute-start.14 = (f32[8,128]{1,0:T(8,128)S(1)}, f32[8,128]{1,0:T(8,128)S(1)}, u32[]{:S(2)}, u32[]{:S(2)}) collective-permute-start(f32[8,128]{1,0:T(8,128)S(1)} %get-tuple-element.68), channel_id=1, source_target_pairs={{0,4},{4,0},{8,12},{12,8},{1,5},{5,1},{9,13},{13,9},{2,6},{6,2},{1... | collective-permute-start | bytes 12296 | tf_op jit(solution)/shard_map/ppermute | solution.py:463
  48.3 6.9 %collective-permute-start.15 = (bf16[288,128]{1,0:T(8,128)(2,1)S(1)}, bf16[288,128]{1,0:T(8,128)(2,1)S(1)}, u32[]{:S(2)}, u32[]{:S(2)}) collective-permute-start(bf16[288,128]{1,0:T(8,128)(2,1)S(1)} %get-tuple-element.72), channel_id=1, source_target_pairs={{0,3},{1,2},{2,1},{3,0},{4,7},{5,6},{6,5},{7,4},{8,11},{9,10},{10,... | collective-permute-start | bytes 221192 | tf_op jit(solution)/shard_map/ppermute | solution.py:463
  50.9 4.4 %collective-permute-start.16 = (bf16[288,128]{1,0:T(8,128)(2,1)S(1)}, bf16[288,128]{1,0:T(8,128)(2,1)S(1)}, u32[]{:S(2)}, u32[]{:S(2)}) collective-permute-start(bf16[288,128]{1,0:T(8,128)(2,1)S(1)} %get-tuple-element.73), channel_id=1, source_target_pairs={{0,2},{1,3},{2,0},{3,1},{4,6},{5,7},{6,4},{7,5},{8,10},{9,11},{10,... | collective-permute-start | bytes 221192 | tf_op jit(solution)/shard_map/ppermute | solution.py:463
  51.3 4.4 %collective-permute-start.17 = (bf16[288,128]{1,0:T(8,128)(2,1)S(1)}, bf16[288,128]{1,0:T(8,128)(2,1)S(1)}, u32[]{:S(2)}, u32[]{:S(2)}) collective-permute-start(bf16[288,128]{1,0:T(8,128)(2,1)S(1)} %get-tuple-element.74), channel_id=1, source_target_pairs={{0,1},{1,0},{2,3},{3,2},{4,5},{5,4},{6,7},{7,6},{8,9},{9,8},{10,11... | collective-permute-start | bytes 221192 | tf_op jit(solution)/shard_map/ppermute | solution.py:463
  51.9 10.0 %collective-permute-start.19 = (bf16[32,1152]{1,0:T(8,128)(2,1)S(1)}, bf16[32,1152]{1,0:T(8,128)(2,1)S(1)}, u32[]{:S(2)}, u32[]{:S(2)}) collective-permute-start(bf16[32,1152]{1,0:T(8,128)(2,1)S(1)} %get-tuple-element.78), channel_id=1, source_target_pairs={{0,8},{4,12},{8,0},{12,4},{1,9},{5,13},{9,1},{13,5},{2,10},{6,14},... | collective-permute-start | bytes 221192 | tf_op jit(solution)/shard_map/ppermute | solution.py:463
  53.9 9.0 %collective-permute-start.20 = (bf16[32,1152]{1,0:T(8,128)(2,1)S(1)}, bf16[32,1152]{1,0:T(8,128)(2,1)S(1)}, u32[]{:S(2)}, u32[]{:S(2)}) collective-permute-start(bf16[32,1152]{1,0:T(8,128)(2,1)S(1)} %get-tuple-element.79), channel_id=1, source_target_pairs={{0,12},{4,8},{8,4},{12,0},{1,13},{5,9},{9,5},{13,1},{2,14},{6,10},... | collective-permute-start | bytes 221192 | tf_op jit(solution)/shard_map/ppermute | solution.py:463
  58.3 5.1 %collective-permute-start.21 = (bf16[32,704]{1,0:T(8,128)(2,1)S(1)}, bf16[32,704]{1,0:T(8,128)(2,1)S(1)}, u32[]{:S(2)}, u32[]{:S(2)}) collective-permute-start(bf16[32,704]{1,0:T(8,128)(2,1)S(1)} %get-tuple-element.81), channel_id=1, source_target_pairs={{0,3},{1,2},{2,1},{3,0},{4,7},{5,6},{6,5},{7,4},{8,11},{9,10},{10,... | collective-permute-start | bytes 135176 | tf_op jit(solution)/shard_map/ppermute | solution.py:463
  60.5 4.1 %collective-permute-start.22 = (bf16[32,704]{1,0:T(8,128)(2,1)S(1)}, bf16[32,704]{1,0:T(8,128)(2,1)S(1)}, u32[]{:S(2)}, u32[]{:S(2)}) collective-permute-start(bf16[32,704]{1,0:T(8,128)(2,1)S(1)} %get-tuple-element.82), channel_id=1, source_target_pairs={{0,2},{1,3},{2,0},{3,1},{4,6},{5,7},{6,4},{7,5},{8,10},{9,11},{10,... | collective-permute-start | bytes 135176 | tf_op jit(solution)/shard_map/ppermute | solution.py:463
  60.9 4.1 %collective-permute-start.23 = (bf16[32,704]{1,0:T(8,128)(2,1)S(1)}, bf16[32,704]{1,0:T(8,128)(2,1)S(1)}, u32[]{:S(2)}, u32[]{:S(2)}) collective-permute-start(bf16[32,704]{1,0:T(8,128)(2,1)S(1)} %get-tuple-element.83), channel_id=1, source_target_pairs={{0,1},{1,0},{2,3},{3,2},{4,5},{5,4},{6,7},{7,6},{8,9},{9,8},{10,11... | collective-permute-start | bytes 135176 | tf_op jit(solution)/shard_map/ppermute | solution.py:463
  61.9 4.4 %collective-permute-start.18 = (bf16[32,1152]{1,0:T(8,128)(2,1)S(1)}, bf16[32,1152]{1,0:T(8,128)(2,1)S(1)}, u32[]{:S(2)}, u32[]{:S(2)}) collective-permute-start(bf16[32,1152]{1,0:T(8,128)(2,1)S(1)} %get-tuple-element.77), channel_id=1, source_target_pairs={{0,4},{4,0},{8,12},{12,8},{1,5},{5,1},{9,13},{13,9},{2,6},{6,2},{1... | collective-permute-start | bytes 221192 | tf_op jit(solution)/shard_map/ppermute | solution.py:463
  65.3 1.3 %collective-permute-start.24 = (bf16[56,576]{1,0:T(8,128)(2,1)S(1)}, bf16[56,576]{1,0:T(8,128)(2,1)S(1)}, u32[]{:S(2)}, u32[]{:S(2)}) collective-permute-start(bf16[56,576]{1,0:T(8,128)(2,1)S(1)} %get-tuple-element.86), channel_id=1, source_target_pairs={{0,16},{16,0},{1,17},{17,1},{2,18},{18,2},{3,19},{19,3},{4,20},{20... | collective-permute-start | bytes 193544 | tf_op jit(solution)/shard_map/ppermute | solution.py:463
  66.7 7.0 %collective-permute-start.27 = (bf16[56,576]{1,0:T(8,128)(2,1)S(1)}, bf16[56,576]{1,0:T(8,128)(2,1)S(1)}, u32[]{:S(2)}, u32[]{:S(2)}) collective-permute-start(bf16[56,576]{1,0:T(8,128)(2,1)S(1)} %shard_map.130.refs_0_), channel_id=1, source_target_pairs={{0,12},{4,8},{8,4},{12,0},{1,13},{5,9},{9,5},{13,1},{2,14},{6,10},... | collective-permute-start | bytes 193544 | tf_op jit(solution)/shard_map/ppermute | solution.py:463
  69.2 6.7 %collective-permute-start.26 = (bf16[56,576]{1,0:T(8,128)(2,1)S(1)}, bf16[56,576]{1,0:T(8,128)(2,1)S(1)}, u32[]{:S(2)}, u32[]{:S(2)}) collective-permute-start(bf16[56,576]{1,0:T(8,128)(2,1)S(1)} %shard_map.130.refs_0_), channel_id=1, source_target_pairs={{0,8},{4,12},{8,0},{12,4},{1,9},{5,13},{9,1},{13,5},{2,10},{6,14},... | collective-permute-start | bytes 193544 | tf_op jit(solution)/shard_map/ppermute | solution.py:463
  69.2 6.7 %collective-permute-start.25 = (bf16[56,576]{1,0:T(8,128)(2,1)S(1)}, bf16[56,576]{1,0:T(8,128)(2,1)S(1)}, u32[]{:S(2)}, u32[]{:S(2)}) collective-permute-start(bf16[56,576]{1,0:T(8,128)(2,1)S(1)} %shard_map.130.refs_0_), channel_id=1, source_target_pairs={{0,4},{4,0},{8,12},{12,8},{1,5},{5,1},{9,13},{13,9},{2,6},{6,2},{1... | collective-permute-start | bytes 193544 | tf_op jit(solution)/shard_map/ppermute | solution.py:463
  76.0 5.4 %collective-permute-start.30 = (bf16[56,576]{1,0:T(8,128)(2,1)S(1)}, bf16[56,576]{1,0:T(8,128)(2,1)S(1)}, u32[]{:S(2)}, u32[]{:S(2)}) collective-permute-start(bf16[56,576]{1,0:T(8,128)(2,1)S(1)} %shard_map.131.refs_0_), channel_id=1, source_target_pairs={{0,3},{1,2},{2,1},{3,0},{4,7},{5,6},{6,5},{7,4},{8,11},{9,10},{10,... | collective-permute-start | bytes 193544 | tf_op jit(solution)/shard_map/ppermute | solution.py:463
  78.3 4.5 %collective-permute-start.29 = (bf16[56,576]{1,0:T(8,128)(2,1)S(1)}, bf16[56,576]{1,0:T(8,128)(2,1)S(1)}, u32[]{:S(2)}, u32[]{:S(2)}) collective-permute-start(bf16[56,576]{1,0:T(8,128)(2,1)S(1)} %shard_map.131.refs_0_), channel_id=1, source_target_pairs={{0,2},{1,3},{2,0},{3,1},{4,6},{5,7},{6,4},{7,5},{8,10},{9,11},{10,... | collective-permute-start | bytes 193544 | tf_op jit(solution)/shard_map/ppermute | solution.py:463
  78.7 4.3 %collective-permute-start.28 = (bf16[56,576]{1,0:T(8,128)(2,1)S(1)}, bf16[56,576]{1,0:T(8,128)(2,1)S(1)}, u32[]{:S(2)}, u32[]{:S(2)}) collective-permute-start(bf16[56,576]{1,0:T(8,128)(2,1)S(1)} %shard_map.131.refs_0_), channel_id=1, source_target_pairs={{0,1},{1,0},{2,3},{3,2},{4,5},{5,4},{6,7},{7,6},{8,9},{9,8},{10,11... | collective-permute-start | bytes 193544 | tf_op jit(solution)/shard_map/ppermute | solution.py:463
  83.2 1.4 %collective-permute-start.31 = (bf16[64,1152]{1,0:T(8,128)(2,1)S(1)}, bf16[64,1152]{1,0:T(8,128)(2,1)S(1)}, u32[]{:S(2)}, u32[]{:S(2)}) collective-permute-start(bf16[64,1152]{1,0:T(8,128)(2,1)S(1)} %shard_map.132.refs_0_), channel_id=1, source_target_pairs={{0,16},{16,0},{1,17},{17,1},{2,18},{18,2},{3,19},{19,3},{4,20},{20... | collective-permute-start | bytes 442376 | tf_op jit(solution)/shard_map/ppermute | solution.py:463
  (5 other events, 110.1 us)

commit v17 on v16

--- a/solution.py
+++ b/solution.py
@@ -97,7 +97,7 @@
     outs, here_ref, refs = refs[:n_s], refs[n_s], refs[n_s + 1 :]
     time_outs, refs = refs[: n_t - 1], refs[n_t - 1 :]
     buffers, (time_buf, turned_ref, maps_ref, sems, time_sems) = refs[:6], refs[6:]
-    p_buf, at_buf, b_buf, q_buf, v_buf, k_buf = buffers
+    k_buf, p_buf, at_buf, b_buf, q_buf, v_buf = buffers
     copies = load_all(ins, buffers, sems)
     time_copies = load_all(time_ins, [time_buf.at[index] for index in range(4)], time_sems)
     d_s, tokens = turned_ref.shape[2:]
@@ -114,24 +114,23 @@
             outs[k][index * d_s : (index + 1) * d_s] = turned_ref[index, peer("space", k)]
 
     copies[0].wait()
-    copies[1].wait()
-    copies[2].wait()
+    send(flat(k_buf), 1)
+    for copy in copies[1:4]:
+        copy.wait()
     patches = flat(p_buf)
     codes_q = mm(patches, at_buf[0], NT).astype(BF16)
     codes_v = mm(patches, at_buf[1], NT).astype(BF16)
     codes_t = jnp.concatenate([codes_q, codes_v], axis=1).T
+    copies[4].wait()
+    query = (flat(q_buf).astype(F32) + mm(codes_q, b_buf[0])).astype(BF16)
+    send(query, 0)
+    copies[5].wait()
+    value = (flat(v_buf).astype(F32) + mm(codes_v, b_buf[1])).astype(BF16)
+    send(value, 2)
     maps = jnp.concatenate([b_buf[0], b_buf[1]], axis=0).T
     for j in range(n_s):
         maps_ref[j] = maps[j * d_s : (j + 1) * d_s]
     here_ref[...] = maps_ref[peer("space", 0)]
-    copies[3].wait()
-    query = (flat(q_buf).astype(F32) + mm(codes_q, b_buf[0])).astype(BF16)
-    send(query, 0)
-    copies[4].wait()
-    value = (flat(v_buf).astype(F32) + mm(codes_v, b_buf[1])).astype(BF16)
-    send(value, 2)
-    copies[5].wait()
-    send(flat(k_buf), 1)
     for k in range(n_s):
         outs[k][3 * d_s :] = codes_t
     for index, copy in enumerate(time_copies):
@@ -149,7 +148,7 @@
 
 
 def space_forward_kernel(frames, n_s, *refs):
-    packed, (qkv_ref, probs_ref, *outs) = refs[:n_s], refs[n_s : 2 * n_s + 2]
+    packed, (qkv_ref, probs_ref, *outs) = refs[:n_s][::-1], refs[n_s : 2 * n_s + 2]
     probs_buf, sems = refs[2 * n_s + 2 :]
     copies = []
     d_s, tokens = outs[0].shape
@@ -326,7 +325,7 @@
 
 
 def space_backward_kernel(frames, n_s, qkv_ref, probs_ref, hidden_ref, grad_b_ref, dcodes_ref, here_ref, *refs):
-    packed, grads, sends = refs[:n_s], refs[n_s : 2 * n_s][::-1], refs[2 * n_s : 3 * n_s]
+    packed, grads, sends = refs[:n_s][::-1], refs[n_s : 2 * n_s][::-1], refs[2 * n_s : 3 * n_s]
     part_ref, cut_buf = refs[3 * n_s :]
     d_s = part_ref.shape[1]
     tokens = hidden_ref.shape[0]
@@ -429,18 +428,25 @@
 
 
 def final_kernel(factor, n_d, n_full, *refs):
-    pieces, (a_ref, b_ref, buf) = refs[:n_d], refs[n_d:]
+    pieces, (a_ref, b_ref, buf, out_buf, sems) = refs[:n_d], refs[n_d:]
     for k, piece in enumerate(pieces):
         buf[peer("dp", k)] = piece[...]
     n_split = pieces[0].shape[0] - n_full
     size = math.gcd(n_full, n_split, RANK)
+    filled, copies = [0] * 8, []
     for d in range(n_d):
         rows = buf[d].astype(F32) * factor
         for r in range(0, n_full + n_split, size):
             row = d * n_full + r if r < n_full else 2 * RANK + d * n_split + r - n_full
-            target = a_ref if row < 4 * RANK else b_ref
-            row %= 4 * RANK
-            target[row // RANK, row % RANK : row % RANK + size] = rows[r : r + size]
+            index = row // RANK
+            out_buf[index, row % RANK : row % RANK + size] = rows[r : r + size]
+            filled[index] += size
+            if filled[index] == RANK:
+                target = (a_ref if index < 4 else b_ref).at[index % 4]
+                copies.append(pltpu.make_async_copy(out_buf.at[index], target, sems.at[index]))
+                copies[-1].start()
+    for copy in copies:
+        copy.wait()
 
 
 def mixed_kernel(frames, hidden_ref, *refs):
@@ -488,7 +494,7 @@
 
     time_arrays = [far(x) for x in (query_t, key_t, value_t, cotangent)]
     space_arrays = [
-        far(x) for x in (patches, downs, adapters_b, query_s, value_s, key_s)
+        far(x) for x in (key_s, patches, downs, adapters_b, query_s, value_s)
     ]
     packed = call(
         functools.partial(pack_kernel, n_s, n_t, sub),
@@ -513,7 +519,7 @@
         functools.partial(space_forward_kernel, frames, n_s),
         [shape((3, frames, d_s, total), BF16), pltpu.HBM(probs_dims, F32)]
         + [shape((d_s, tokens), BF16)] * n_s,
-        *packed,
+        *packed[::-1],
         scratch=[pltpu.VMEM(probs_dims, F32), dma((probs_dims[0] * probs_dims[1],))],
         after=time_pieces[:1],
     )
@@ -557,7 +563,7 @@
     backward = call(
         functools.partial(space_backward_kernel, frames, n_s),
         [shape((2 * RANK, tokens + 2 * d_s), BF16)] * n_s + [shape((2 * RANK, d_s), F32)],
-        qkv, probs, hidden, time_grad_b, dcodes, here, *packed, *grads[::-1],
+        qkv, probs, hidden, time_grad_b, dcodes, here, *packed[::-1], *grads[::-1],
         scratch=[pltpu.VMEM((n_s, 2 * RANK, 2 * d_s), BF16)],
         carry=out_t[1:2],
     )
@@ -583,9 +589,13 @@
     )
     grads_a, grads_b = call(
         functools.partial(final_kernel, factor, n_d, n_full),
-        [shape((4, RANK, width), F32)] * 2,
+        [pltpu.HBM((4, RANK, width), F32)] * 2,
         *share(sums, "dp"),
-        scratch=[pltpu.VMEM((n_d, n_full + n_split, width), BF16)],
+        scratch=[
+            pltpu.VMEM((n_d, n_full + n_split, width), BF16),
+            pltpu.VMEM((8, RANK, width), F32),
+            dma((8,)),
+        ],
     )
     mixed = call(
         functools.partial(mixed_kernel, frames),

time: 85.8 us -> 86.4 us (level)
  starting transfers between devices: 45.4 us -> 46.4 us
    ppermute x32, starting transfers between devices: 45.4 us -> 46.4 us  [hops(): lax.ppermute(array, axis, [(i, i ^ k) for i in range(size)])]
  transfers between devices with their start and end apart: 32 -> 32, of which waited for: 20 -> 18; matrix products, arithmetic and copies ran while one was open for 0% -> 0% of each run, Pallas kernels for 10% -> 10%
where the time goes in v17:
time: 86.4 us; the launch traced here: 86.2 us
  starting transfers between devices  46.4 us (54%)
  waiting for transfers between devices  22.8 us (26%)
  Pallas kernels  16.2 us (19%)
    ppermute x32, starting transfers between devices, hops(): lax.ppermute(array, axis, [(i, i ^ k) for i in range(size)])  46.4 us
    ppermute x32, waiting for transfers between devices, hops(): lax.ppermute(array, axis, [(i, i ^ k) for i in range(size)])  22.8 us
    pallas_call x13, Pallas kernels, call(): pl.pallas_call(body, out_shape=outs + tuple((shape(x.shape, x.dtype) for...  16.2 us
  transfers between devices with their start and end apart: 32, of which 18 were waited for; matrix products, arithmetic and copies ran while one was open for 0% of the time, Pallas kernels for 10%

profile of v17, /device:TPU:0, one launch (start us, length us, event | category | flops | bytes accessed | tf_op | source)
XLA Modules:
  0.0 86.2 jit_solution(3711779245812614772)
XLA Ops:
  0.7 2.5 %shard_map.121 = (bf16[896,128]{1,0:T(8,128)(2,1)S(1)}, bf16[896,128]{1,0:T(8,128)(2,1)S(1)}, bf16[896,128]{1,0:T(8,128)(2,1)S(1)}, bf16[896,128]{1,0:T(8,128)(2...) custom-call(bf16[1,2,64,1152]{3,2,1,0:T(8,128)(2,1)} %refs_0_.3, ...), custom_call_target="tpu_custom_call" | custom-call | tf_op jit(solution)/shard_map/pallas_call | solution.py:41
  3.2 4.0 %collective-permute-start = (bf16[896,128]{1,0:T(8,128)(2,1)S(1)}, bf16[896,128]{1,0:T(8,128)(2,1)S(1)}, u32[]{:S(2)}, u32[]{:S(2)}) collective-permute-start(bf16[896,128]{1,0:T(8,128)(2,1)S(1)} %get-tuple-element.46), channel_id=1, source_target_pairs={{0,3},{1,2},{2,1},{3,0},{4,7},{5,6},{6,5},{7,4},{8,11},{9,10},{10,... | collective-permute-start | bytes 688136 | tf_op jit(solution)/shard_map/ppermute | solution.py:469
  7.2 1.6 %collective-permute-start.3 = (bf16[4,32,1152]{2,1,0:T(8,128)(2,1)S(1)}, bf16[4,32,1152]{2,1,0:T(8,128)(2,1)S(1)}, u32[]{:S(2)}, u32[]{:S(2)}) collective-permute-start(bf16[4,32,1152]{2,1,0:T(8,128)(2,1)S(1)} %get-tuple-element.50), channel_id=1, source_target_pairs={{0,4},{4,0},{8,12},{12,8},{1,5},{5,1},{9,13},{13,9},{2,6},{6,2},{1... | collective-permute-start | bytes 884744 | tf_op jit(solution)/shard_map/ppermute | solution.py:469
  9.8 2.6 %collective-permute-start.7 = (bf16[4,32,1152]{2,1,0:T(8,128)(2,1)S(1)}, bf16[4,32,1152]{2,1,0:T(8,128)(2,1)S(1)}, u32[]{:S(2)}, u32[]{:S(2)}) collective-permute-start(bf16[4,32,1152]{2,1,0:T(8,128)(2,1)S(1)} %get-tuple-element.56), channel_id=1, source_target_pairs={{0,8},{4,12},{8,0},{12,4},{1,9},{5,13},{9,1},{13,5},{2,10},{6,14},... | collective-permute-start | bytes 884744 | tf_op jit(solution)/shard_map/ppermute | solution.py:469
  12.3 1.3 %collective-permute-done.refs_0_.refs_6_ = bf16[896,128]{1,0:T(8,128)(2,1)S(1)} collective-permute-done((bf16[896,128]{1,0:T(8,128)(2,1)S(1)}, bf16[896,128]{1,0:T(8,128)(2,1)S(1)}, u32[]{:S(2)}, u32[]{:S(2)}) %collective-permute-start) | collective-permute-done | bytes 229408 | tf_op jit(solution)/shard_map/ppermute | solution.py:469
  13.6 4.1 %collective-permute-start.8 = (bf16[4,32,1152]{2,1,0:T(8,128)(2,1)S(1)}, bf16[4,32,1152]{2,1,0:T(8,128)(2,1)S(1)}, u32[]{:S(2)}, u32[]{:S(2)}) collective-permute-start(bf16[4,32,1152]{2,1,0:T(8,128)(2,1)S(1)} %get-tuple-element.57), channel_id=1, source_target_pairs={{0,12},{4,8},{8,4},{12,0},{1,13},{5,9},{9,5},{13,1},{2,14},{6,10},... | collective-permute-start | bytes 884744 | tf_op jit(solution)/shard_map/ppermute | solution.py:469
  17.9 2.6 %collective-permute-done.3.refs_4_ = bf16[4,32,1152]{2,1,0:T(8,128)(2,1)S(1)} collective-permute-done((bf16[4,32,1152]{2,1,0:T(8,128)(2,1)S(1)}, bf16[4,32,1152]{2,1,0:T(8,128)(2,1)S(1)}, u32[]{:S(2)}, u32[]{:S(2)}) %collective-permute-start.3) | collective-permute-done | bytes 294944 | tf_op jit(solution)/shard_map/ppermute | solution.py:469
  20.5 3.5 %shard_map.122 = (bf16[3,2,288,256]{3,2,1,0:T(8,128)(2,1)S(1)}, f32[2,4,256,256]{3,2,1,0:T(8,128)}, bf16[288,128]{1,0:T(8,128)(2,1)S(1)}, bf16[288,128]{1,0:T(8,...) custom-call(bf16[896,128]{1,0:T(8,128)(2,1)S(1)} %collective-permute-done.refs_0_.refs_6_, ...), custom_call_target="tpu_custom_call" | custom-call | tf_op jit(solution)/shard_map/pallas_call | solution.py:41
  24.1 1.5 %collective-permute-start.5 = (bf16[288,128]{1,0:T(8,128)(2,1)S(1)}, bf16[288,128]{1,0:T(8,128)(2,1)S(1)}, u32[]{:S(2)}, u32[]{:S(2)}) collective-permute-start(bf16[288,128]{1,0:T(8,128)(2,1)S(1)} %get-tuple-element.52), channel_id=1, source_target_pairs={{0,2},{1,3},{2,0},{3,1},{4,6},{5,7},{6,4},{7,5},{8,10},{9,11},{10,... | collective-permute-start | bytes 221192 | tf_op jit(solution)/shard_map/ppermute | solution.py:469
  25.6 2.0 %collective-permute-start.6 = (bf16[288,128]{1,0:T(8,128)(2,1)S(1)}, bf16[288,128]{1,0:T(8,128)(2,1)S(1)}, u32[]{:S(2)}, u32[]{:S(2)}) collective-permute-start(bf16[288,128]{1,0:T(8,128)(2,1)S(1)} %get-tuple-element.53), channel_id=1, source_target_pairs={{0,1},{1,0},{2,3},{3,2},{4,5},{5,4},{6,7},{7,6},{8,9},{9,8},{10,11... | collective-permute-start | bytes 221192 | tf_op jit(solution)/shard_map/ppermute | solution.py:469
  27.6 1.8 %collective-permute-done.4.refs_0_ = bf16[288,128]{1,0:T(8,128)(2,1)S(1)} collective-permute-done((bf16[288,128]{1,0:T(8,128)(2,1)S(1)}, bf16[288,128]{1,0:T(8,128)(2,1)S(1)}, u32[]{:S(2)}, u32[]{:S(2)}) %collective-permute-start.4) | collective-permute-done | bytes 73760 | tf_op jit(solution)/shard_map/ppermute | solution.py:469
  30.3 3.1 %collective-permute-start.9 = (f32[8,128]{1,0:T(8,128)S(1)}, f32[8,128]{1,0:T(8,128)S(1)}, u32[]{:S(2)}, u32[]{:S(2)}) collective-permute-start(f32[8,128]{1,0:T(8,128)S(1)} %get-tuple-element.58), channel_id=1, source_target_pairs={{0,12},{4,8},{8,4},{12,0},{1,13},{5,9},{9,5},{13,1},{2,14},{6,10},... | collective-permute-start | bytes 12296 | tf_op jit(solution)/shard_map/ppermute | solution.py:469
  33.4 1.3 %collective-permute-start.11 = (f32[8,128]{1,0:T(8,128)S(1)}, f32[8,128]{1,0:T(8,128)S(1)}, u32[]{:S(2)}, u32[]{:S(2)}) collective-permute-start(f32[8,128]{1,0:T(8,128)S(1)} %get-tuple-element.60), channel_id=1, source_target_pairs={{0,4},{4,0},{8,12},{12,8},{1,5},{5,1},{9,13},{13,9},{2,6},{6,2},{1... | collective-permute-start | bytes 12296 | tf_op jit(solution)/shard_map/ppermute | solution.py:469
  34.7 1.4 %shard_map.124.refs_0_ = bf16[4,1152,128]{2,1,0:T(8,128)(2,1)S(1)} custom-call(bf16[1,2,64,1152]{3,2,1,0:T(8,128)(2,1)} %refs_0_.4, bf16[1,2,64,1152]{3,2,1,0:T(8,128)(2,1)} %refs_1_.5, bf16[1,2,64,1152]{3,2,1,0:T(8,128)(2,1)} %refs_2_.1, bf16[1,2,64,1152]{3,2,1,0:T(8,128)(2,1)} %refs_0_.5, bf16[4,32,1152]{2,1,0:T(8,128)(2,1)S(1)} %collective-permute-done.3.refs_4_, ...), custom_call_target="tpu_custom_call" | custom-call | tf_op jit(solution)/shard_map/pallas_call | solution.py:41
  36.1 1.8 %collective-permute-done.10.refs_3_ = f32[8,128]{1,0:T(8,128)S(1)} collective-permute-done((f32[8,128]{1,0:T(8,128)S(1)}, f32[8,128]{1,0:T(8,128)S(1)}, u32[]{:S(2)}, u32[]{:S(2)}) %collective-permute-start.10) | collective-permute-done | bytes 4128 | tf_op jit(solution)/shard_map/ppermute | solution.py:469
  37.9 3.1 %shard_map.125 = (bf16[32,1152]{1,0:T(8,128)(2,1)S(1)}, bf16[32,1152]{1,0:T(8,128)(2,1)S(1)}, bf16[32,1152]{1,0:T(8,128)(2,1)S(1)}, bf16[32,1152]{1,0:T(8,128)(2...) custom-call(bf16[4,1152,128]{2,1,0:T(8,128)(2,1)S(1)} %shard_map.124, ...), custom_call_target="tpu_custom_call" | custom-call | tf_op jit(solution)/shard_map/pallas_call | solution.py:41
  41.0 2.3 %collective-permute-start.12 = (f32[8,128]{1,0:T(8,128)S(1)}, f32[8,128]{1,0:T(8,128)S(1)}, u32[]{:S(2)}, u32[]{:S(2)}) collective-permute-start(f32[8,128]{1,0:T(8,128)S(1)} %get-tuple-element.66), channel_id=1, source_target_pairs={{0,12},{4,8},{8,4},{12,0},{1,13},{5,9},{9,5},{13,1},{2,14},{6,10},... | collective-permute-start | bytes 12296 | tf_op jit(solution)/shard_map/ppermute | solution.py:469
  44.1 1.3 %collective-permute-start.14 = (f32[8,128]{1,0:T(8,128)S(1)}, f32[8,128]{1,0:T(8,128)S(1)}, u32[]{:S(2)}, u32[]{:S(2)}) collective-permute-start(f32[8,128]{1,0:T(8,128)S(1)} %get-tuple-element.68), channel_id=1, source_target_pairs={{0,4},{4,0},{8,12},{12,8},{1,5},{5,1},{9,13},{13,9},{2,6},{6,2},{1... | collective-permute-start | bytes 12296 | tf_op jit(solution)/shard_map/ppermute | solution.py:469
  46.4 1.3 %collective-permute-done.13.refs_3_ = f32[8,128]{1,0:T(8,128)S(1)} collective-permute-done((f32[8,128]{1,0:T(8,128)S(1)}, f32[8,128]{1,0:T(8,128)S(1)}, u32[]{:S(2)}, u32[]{:S(2)}) %collective-permute-start.13) | collective-permute-done | bytes 4128 | tf_op jit(solution)/shard_map/ppermute | solution.py:469
  48.2 2.6 %collective-permute-start.15 = (bf16[288,128]{1,0:T(8,128)(2,1)S(1)}, bf16[288,128]{1,0:T(8,128)(2,1)S(1)}, u32[]{:S(2)}, u32[]{:S(2)}) collective-permute-start(bf16[288,128]{1,0:T(8,128)(2,1)S(1)} %get-tuple-element.72), channel_id=1, source_target_pairs={{0,3},{1,2},{2,1},{3,0},{4,7},{5,6},{6,5},{7,4},{8,11},{9,10},{10,... | collective-permute-start | bytes 221192 | tf_op jit(solution)/shard_map/ppermute | solution.py:469
  51.7 2.0 %collective-permute-start.19 = (bf16[32,1152]{1,0:T(8,128)(2,1)S(1)}, bf16[32,1152]{1,0:T(8,128)(2,1)S(1)}, u32[]{:S(2)}, u32[]{:S(2)}) collective-permute-start(bf16[32,1152]{1,0:T(8,128)(2,1)S(1)} %get-tuple-element.78), channel_id=1, source_target_pairs={{0,8},{4,12},{8,0},{12,4},{1,9},{5,13},{9,1},{13,5},{2,10},{6,14},... | collective-permute-start | bytes 221192 | tf_op jit(solution)/shard_map/ppermute | solution.py:469
  53.8 1.6 %collective-permute-start.20 = (bf16[32,1152]{1,0:T(8,128)(2,1)S(1)}, bf16[32,1152]{1,0:T(8,128)(2,1)S(1)}, u32[]{:S(2)}, u32[]{:S(2)}) collective-permute-start(bf16[32,1152]{1,0:T(8,128)(2,1)S(1)} %get-tuple-element.79), channel_id=1, source_target_pairs={{0,12},{4,8},{8,4},{12,0},{1,13},{5,9},{9,5},{13,1},{2,14},{6,10},... | collective-permute-start | bytes 221192 | tf_op jit(solution)/shard_map/ppermute | solution.py:469
  55.6 2.6 %shard_map.127 = (bf16[32,704]{1,0:T(8,128)(2,1)S(1)}, bf16[32,704]{1,0:T(8,128)(2,1)S(1)}, bf16[32,704]{1,0:T(8,128)(2,1)S(1)}, bf16[32,704]{1,0:T(8,128)(2,1)S...) custom-call(bf16[3,2,288,256]{3,2,1,0:T(8,128)(2,1)S(1)} %get-tuple-element.63.refs_0_,, ...), custom_call_target="tpu_custom_call", output_to_operand_aliasing={{5}: (14, {})} | custom-call | tf_op jit(solution)/shard_map/pallas_call | solution.py:41
  58.2 2.1 %collective-permute-start.21 = (bf16[32,704]{1,0:T(8,128)(2,1)S(1)}, bf16[32,704]{1,0:T(8,128)(2,1)S(1)}, u32[]{:S(2)}, u32[]{:S(2)}) collective-permute-start(bf16[32,704]{1,0:T(8,128)(2,1)S(1)} %get-tuple-element.81), channel_id=1, source_target_pairs={{0,3},{1,2},{2,1},{3,0},{4,7},{5,6},{6,5},{7,4},{8,11},{9,10},{10,... | collective-permute-start | bytes 135176 | tf_op jit(solution)/shard_map/ppermute | solution.py:469
  61.7 1.8 %collective-permute-start.18 = (bf16[32,1152]{1,0:T(8,128)(2,1)S(1)}, bf16[32,1152]{1,0:T(8,128)(2,1)S(1)}, u32[]{:S(2)}, u32[]{:S(2)}) collective-permute-start(bf16[32,1152]{1,0:T(8,128)(2,1)S(1)} %get-tuple-element.77), channel_id=1, source_target_pairs={{0,4},{4,0},{8,12},{12,8},{1,5},{5,1},{9,13},{13,9},{2,6},{6,2},{1... | collective-permute-start | bytes 221192 | tf_op jit(solution)/shard_map/ppermute | solution.py:469
  66.1 1.2 %collective-permute-done.24.refs_1_ = bf16[56,576]{1,0:T(8,128)(2,1)S(1)} collective-permute-done((bf16[56,576]{1,0:T(8,128)(2,1)S(1)}, bf16[56,576]{1,0:T(8,128)(2,1)S(1)}, u32[]{:S(2)}, u32[]{:S(2)}) %collective-permute-start.24) | collective-permute-done | bytes 64544 | tf_op jit(solution)/shard_map/ppermute | solution.py:469
  67.4 1.8 %collective-permute-start.27 = (bf16[56,576]{1,0:T(8,128)(2,1)S(1)}, bf16[56,576]{1,0:T(8,128)(2,1)S(1)}, u32[]{:S(2)}, u32[]{:S(2)}) collective-permute-start(bf16[56,576]{1,0:T(8,128)(2,1)S(1)} %shard_map.130.refs_0_), channel_id=1, source_target_pairs={{0,12},{4,8},{8,4},{12,0},{1,13},{5,9},{9,5},{13,1},{2,14},{6,10},... | collective-permute-start | bytes 193544 | tf_op jit(solution)/shard_map/ppermute | solution.py:469
  69.4 2.4 %collective-permute-start.25 = (bf16[56,576]{1,0:T(8,128)(2,1)S(1)}, bf16[56,576]{1,0:T(8,128)(2,1)S(1)}, u32[]{:S(2)}, u32[]{:S(2)}) collective-permute-start(bf16[56,576]{1,0:T(8,128)(2,1)S(1)} %shard_map.130.refs_0_), channel_id=1, source_target_pairs={{0,4},{4,0},{8,12},{12,8},{1,5},{5,1},{9,13},{13,9},{2,6},{6,2},{1... | collective-permute-start | bytes 193544 | tf_op jit(solution)/shard_map/ppermute | solution.py:469
  71.8 2.6 %collective-permute-done.27.refs_3_ = bf16[56,576]{1,0:T(8,128)(2,1)S(1)} collective-permute-done((bf16[56,576]{1,0:T(8,128)(2,1)S(1)}, bf16[56,576]{1,0:T(8,128)(2,1)S(1)}, u32[]{:S(2)}, u32[]{:S(2)}) %collective-permute-start.27) | collective-permute-done | bytes 64544 | tf_op jit(solution)/shard_map/ppermute | solution.py:469
  74.4 2.2 %collective-permute-done.26.refs_2_ = bf16[56,576]{1,0:T(8,128)(2,1)S(1)} collective-permute-done((bf16[56,576]{1,0:T(8,128)(2,1)S(1)}, bf16[56,576]{1,0:T(8,128)(2,1)S(1)}, u32[]{:S(2)}, u32[]{:S(2)}) %collective-permute-start.26) | collective-permute-done | bytes 64544 | tf_op jit(solution)/shard_map/ppermute | solution.py:469
  76.6 1.6 %collective-permute-start.30 = (bf16[56,576]{1,0:T(8,128)(2,1)S(1)}, bf16[56,576]{1,0:T(8,128)(2,1)S(1)}, u32[]{:S(2)}, u32[]{:S(2)}) collective-permute-start(bf16[56,576]{1,0:T(8,128)(2,1)S(1)} %shard_map.131.refs_0_), channel_id=1, source_target_pairs={{0,3},{1,2},{2,1},{3,0},{4,7},{5,6},{6,5},{7,4},{8,11},{9,10},{10,... | collective-permute-start | bytes 193544 | tf_op jit(solution)/shard_map/ppermute | solution.py:469
  80.2 2.1 %collective-permute-done.30.refs_3_ = bf16[56,576]{1,0:T(8,128)(2,1)S(1)} collective-permute-done((bf16[56,576]{1,0:T(8,128)(2,1)S(1)}, bf16[56,576]{1,0:T(8,128)(2,1)S(1)}, u32[]{:S(2)}, u32[]{:S(2)}) %collective-permute-start.30) | collective-permute-done | bytes 64544 | tf_op jit(solution)/shard_map/ppermute | solution.py:469
  (55 shorter events, 16.0 us)
Async XLA Ops:
  3.2 10.4 %collective-permute-start = (bf16[896,128]{1,0:T(8,128)(2,1)S(1)}, bf16[896,128]{1,0:T(8,128)(2,1)S(1)}, u32[]{:S(2)}, u32[]{:S(2)}) collective-permute-start(bf16[896,128]{1,0:T(8,128)(2,1)S(1)} %get-tuple-element.46), channel_id=1, source_target_pairs={{0,3},{1,2},{2,1},{3,0},{4,7},{5,6},{6,5},{7,4},{8,11},{9,10},{10,... | collective-permute-start | bytes 688136 | tf_op jit(solution)/shard_map/ppermute | solution.py:469
  7.2 13.4 %collective-permute-start.3 = (bf16[4,32,1152]{2,1,0:T(8,128)(2,1)S(1)}, bf16[4,32,1152]{2,1,0:T(8,128)(2,1)S(1)}, u32[]{:S(2)}, u32[]{:S(2)}) collective-permute-start(bf16[4,32,1152]{2,1,0:T(8,128)(2,1)S(1)} %get-tuple-element.50), channel_id=1, source_target_pairs={{0,4},{4,0},{8,12},{12,8},{1,5},{5,1},{9,13},{13,9},{2,6},{6,2},{1... | collective-permute-start | bytes 884744 | tf_op jit(solution)/shard_map/ppermute | solution.py:469
  8.7 9.0 %collective-permute-start.1 = (bf16[896,128]{1,0:T(8,128)(2,1)S(1)}, bf16[896,128]{1,0:T(8,128)(2,1)S(1)}, u32[]{:S(2)}, u32[]{:S(2)}) collective-permute-start(bf16[896,128]{1,0:T(8,128)(2,1)S(1)} %get-tuple-element.47), channel_id=1, source_target_pairs={{0,2},{1,3},{2,0},{3,1},{4,6},{5,7},{6,4},{7,5},{8,10},{9,11},{10,... | collective-permute-start | bytes 688136 | tf_op jit(solution)/shard_map/ppermute | solution.py:469
  9.2 8.7 %collective-permute-start.2 = (bf16[896,128]{1,0:T(8,128)(2,1)S(1)}, bf16[896,128]{1,0:T(8,128)(2,1)S(1)}, u32[]{:S(2)}, u32[]{:S(2)}) collective-permute-start(bf16[896,128]{1,0:T(8,128)(2,1)S(1)} %get-tuple-element.48), channel_id=1, source_target_pairs={{0,1},{1,0},{2,3},{3,2},{4,5},{5,4},{6,7},{7,6},{8,9},{9,8},{10,11... | collective-permute-start | bytes 688136 | tf_op jit(solution)/shard_map/ppermute | solution.py:469
  9.8 25.0 %collective-permute-start.7 = (bf16[4,32,1152]{2,1,0:T(8,128)(2,1)S(1)}, bf16[4,32,1152]{2,1,0:T(8,128)(2,1)S(1)}, u32[]{:S(2)}, u32[]{:S(2)}) collective-permute-start(bf16[4,32,1152]{2,1,0:T(8,128)(2,1)S(1)} %get-tuple-element.56), channel_id=1, source_target_pairs={{0,8},{4,12},{8,0},{12,4},{1,9},{5,13},{9,1},{13,5},{2,10},{6,14},... | collective-permute-start | bytes 884744 | tf_op jit(solution)/shard_map/ppermute | solution.py:469
  13.6 21.1 %collective-permute-start.8 = (bf16[4,32,1152]{2,1,0:T(8,128)(2,1)S(1)}, bf16[4,32,1152]{2,1,0:T(8,128)(2,1)S(1)}, u32[]{:S(2)}, u32[]{:S(2)}) collective-permute-start(bf16[4,32,1152]{2,1,0:T(8,128)(2,1)S(1)} %get-tuple-element.57), channel_id=1, source_target_pairs={{0,12},{4,8},{8,4},{12,0},{1,13},{5,9},{9,5},{13,1},{2,14},{6,10},... | collective-permute-start | bytes 884744 | tf_op jit(solution)/shard_map/ppermute | solution.py:469
  24.0 5.3 %collective-permute-start.4 = (bf16[288,128]{1,0:T(8,128)(2,1)S(1)}, bf16[288,128]{1,0:T(8,128)(2,1)S(1)}, u32[]{:S(2)}, u32[]{:S(2)}) collective-permute-start(bf16[288,128]{1,0:T(8,128)(2,1)S(1)} %get-tuple-element.51), channel_id=1, source_target_pairs={{0,3},{1,2},{2,1},{3,0},{4,7},{5,6},{6,5},{7,4},{8,11},{9,10},{10,... | collective-permute-start | bytes 221192 | tf_op jit(solution)/shard_map/ppermute | solution.py:469
  24.1 5.2 %collective-permute-start.5 = (bf16[288,128]{1,0:T(8,128)(2,1)S(1)}, bf16[288,128]{1,0:T(8,128)(2,1)S(1)}, u32[]{:S(2)}, u32[]{:S(2)}) collective-permute-start(bf16[288,128]{1,0:T(8,128)(2,1)S(1)} %get-tuple-element.52), channel_id=1, source_target_pairs={{0,2},{1,3},{2,0},{3,1},{4,6},{5,7},{6,4},{7,5},{8,10},{9,11},{10,... | collective-permute-start | bytes 221192 | tf_op jit(solution)/shard_map/ppermute | solution.py:469
  25.6 4.4 %collective-permute-start.6 = (bf16[288,128]{1,0:T(8,128)(2,1)S(1)}, bf16[288,128]{1,0:T(8,128)(2,1)S(1)}, u32[]{:S(2)}, u32[]{:S(2)}) collective-permute-start(bf16[288,128]{1,0:T(8,128)(2,1)S(1)} %get-tuple-element.53), channel_id=1, source_target_pairs={{0,1},{1,0},{2,3},{3,2},{4,5},{5,4},{6,7},{7,6},{8,9},{9,8},{10,11... | collective-permute-start | bytes 221192 | tf_op jit(solution)/shard_map/ppermute | solution.py:469
  30.3 5.8 %collective-permute-start.9 = (f32[8,128]{1,0:T(8,128)S(1)}, f32[8,128]{1,0:T(8,128)S(1)}, u32[]{:S(2)}, u32[]{:S(2)}) collective-permute-start(f32[8,128]{1,0:T(8,128)S(1)} %get-tuple-element.58), channel_id=1, source_target_pairs={{0,12},{4,8},{8,4},{12,0},{1,13},{5,9},{9,5},{13,1},{2,14},{6,10},... | collective-permute-start | bytes 12296 | tf_op jit(solution)/shard_map/ppermute | solution.py:469
  33.4 4.5 %collective-permute-start.10 = (f32[8,128]{1,0:T(8,128)S(1)}, f32[8,128]{1,0:T(8,128)S(1)}, u32[]{:S(2)}, u32[]{:S(2)}) collective-permute-start(f32[8,128]{1,0:T(8,128)S(1)} %get-tuple-element.59), channel_id=1, source_target_pairs={{0,8},{4,12},{8,0},{12,4},{1,9},{5,13},{9,1},{13,5},{2,10},{6,14},... | collective-permute-start | bytes 12296 | tf_op jit(solution)/shard_map/ppermute | solution.py:469
  33.4 4.5 %collective-permute-start.11 = (f32[8,128]{1,0:T(8,128)S(1)}, f32[8,128]{1,0:T(8,128)S(1)}, u32[]{:S(2)}, u32[]{:S(2)}) collective-permute-start(f32[8,128]{1,0:T(8,128)S(1)} %get-tuple-element.60), channel_id=1, source_target_pairs={{0,4},{4,0},{8,12},{12,8},{1,5},{5,1},{9,13},{13,9},{2,6},{6,2},{1... | collective-permute-start | bytes 12296 | tf_op jit(solution)/shard_map/ppermute | solution.py:469
  41.0 5.4 %collective-permute-start.12 = (f32[8,128]{1,0:T(8,128)S(1)}, f32[8,128]{1,0:T(8,128)S(1)}, u32[]{:S(2)}, u32[]{:S(2)}) collective-permute-start(f32[8,128]{1,0:T(8,128)S(1)} %get-tuple-element.66), channel_id=1, source_target_pairs={{0,12},{4,8},{8,4},{12,0},{1,13},{5,9},{9,5},{13,1},{2,14},{6,10},... | collective-permute-start | bytes 12296 | tf_op jit(solution)/shard_map/ppermute | solution.py:469
  43.2 4.5 %collective-permute-start.13 = (f32[8,128]{1,0:T(8,128)S(1)}, f32[8,128]{1,0:T(8,128)S(1)}, u32[]{:S(2)}, u32[]{:S(2)}) collective-permute-start(f32[8,128]{1,0:T(8,128)S(1)} %get-tuple-element.67), channel_id=1, source_target_pairs={{0,8},{4,12},{8,0},{12,4},{1,9},{5,13},{9,1},{13,5},{2,10},{6,14},... | collective-permute-start | bytes 12296 | tf_op jit(solution)/shard_map/ppermute | solution.py:469
  44.1 3.7 %collective-permute-start.14 = (f32[8,128]{1,0:T(8,128)S(1)}, f32[8,128]{1,0:T(8,128)S(1)}, u32[]{:S(2)}, u32[]{:S(2)}) collective-permute-start(f32[8,128]{1,0:T(8,128)S(1)} %get-tuple-element.68), channel_id=1, source_target_pairs={{0,4},{4,0},{8,12},{12,8},{1,5},{5,1},{9,13},{13,9},{2,6},{6,2},{1... | collective-permute-start | bytes 12296 | tf_op jit(solution)/shard_map/ppermute | solution.py:469
  48.2 7.2 %collective-permute-start.15 = (bf16[288,128]{1,0:T(8,128)(2,1)S(1)}, bf16[288,128]{1,0:T(8,128)(2,1)S(1)}, u32[]{:S(2)}, u32[]{:S(2)}) collective-permute-start(bf16[288,128]{1,0:T(8,128)(2,1)S(1)} %get-tuple-element.72), channel_id=1, source_target_pairs={{0,3},{1,2},{2,1},{3,0},{4,7},{5,6},{6,5},{7,4},{8,11},{9,10},{10,... | collective-permute-start | bytes 221192 | tf_op jit(solution)/shard_map/ppermute | solution.py:469
  50.8 4.6 %collective-permute-start.16 = (bf16[288,128]{1,0:T(8,128)(2,1)S(1)}, bf16[288,128]{1,0:T(8,128)(2,1)S(1)}, u32[]{:S(2)}, u32[]{:S(2)}) collective-permute-start(bf16[288,128]{1,0:T(8,128)(2,1)S(1)} %get-tuple-element.73), channel_id=1, source_target_pairs={{0,2},{1,3},{2,0},{3,1},{4,6},{5,7},{6,4},{7,5},{8,10},{9,11},{10,... | collective-permute-start | bytes 221192 | tf_op jit(solution)/shard_map/ppermute | solution.py:469
  51.2 4.4 %collective-permute-start.17 = (bf16[288,128]{1,0:T(8,128)(2,1)S(1)}, bf16[288,128]{1,0:T(8,128)(2,1)S(1)}, u32[]{:S(2)}, u32[]{:S(2)}) collective-permute-start(bf16[288,128]{1,0:T(8,128)(2,1)S(1)} %get-tuple-element.74), channel_id=1, source_target_pairs={{0,1},{1,0},{2,3},{3,2},{4,5},{5,4},{6,7},{7,6},{8,9},{9,8},{10,11... | collective-permute-start | bytes 221192 | tf_op jit(solution)/shard_map/ppermute | solution.py:469
  51.7 10.0 %collective-permute-start.19 = (bf16[32,1152]{1,0:T(8,128)(2,1)S(1)}, bf16[32,1152]{1,0:T(8,128)(2,1)S(1)}, u32[]{:S(2)}, u32[]{:S(2)}) collective-permute-start(bf16[32,1152]{1,0:T(8,128)(2,1)S(1)} %get-tuple-element.78), channel_id=1, source_target_pairs={{0,8},{4,12},{8,0},{12,4},{1,9},{5,13},{9,1},{13,5},{2,10},{6,14},... | collective-permute-start | bytes 221192 | tf_op jit(solution)/shard_map/ppermute | solution.py:469
  53.8 9.8 %collective-permute-start.20 = (bf16[32,1152]{1,0:T(8,128)(2,1)S(1)}, bf16[32,1152]{1,0:T(8,128)(2,1)S(1)}, u32[]{:S(2)}, u32[]{:S(2)}) collective-permute-start(bf16[32,1152]{1,0:T(8,128)(2,1)S(1)} %get-tuple-element.79), channel_id=1, source_target_pairs={{0,12},{4,8},{8,4},{12,0},{1,13},{5,9},{9,5},{13,1},{2,14},{6,10},... | collective-permute-start | bytes 221192 | tf_op jit(solution)/shard_map/ppermute | solution.py:469
  58.2 5.3 %collective-permute-start.21 = (bf16[32,704]{1,0:T(8,128)(2,1)S(1)}, bf16[32,704]{1,0:T(8,128)(2,1)S(1)}, u32[]{:S(2)}, u32[]{:S(2)}) collective-permute-start(bf16[32,704]{1,0:T(8,128)(2,1)S(1)} %get-tuple-element.81), channel_id=1, source_target_pairs={{0,3},{1,2},{2,1},{3,0},{4,7},{5,6},{6,5},{7,4},{8,11},{9,10},{10,... | collective-permute-start | bytes 135176 | tf_op jit(solution)/shard_map/ppermute | solution.py:469
  60.3 4.1 %collective-permute-start.22 = (bf16[32,704]{1,0:T(8,128)(2,1)S(1)}, bf16[32,704]{1,0:T(8,128)(2,1)S(1)}, u32[]{:S(2)}, u32[]{:S(2)}) collective-permute-start(bf16[32,704]{1,0:T(8,128)(2,1)S(1)} %get-tuple-element.82), channel_id=1, source_target_pairs={{0,2},{1,3},{2,0},{3,1},{4,6},{5,7},{6,4},{7,5},{8,10},{9,11},{10,... | collective-permute-start | bytes 135176 | tf_op jit(solution)/shard_map/ppermute | solution.py:469
  61.6 4.1 %collective-permute-start.23 = (bf16[32,704]{1,0:T(8,128)(2,1)S(1)}, bf16[32,704]{1,0:T(8,128)(2,1)S(1)}, u32[]{:S(2)}, u32[]{:S(2)}) collective-permute-start(bf16[32,704]{1,0:T(8,128)(2,1)S(1)} %get-tuple-element.83), channel_id=1, source_target_pairs={{0,1},{1,0},{2,3},{3,2},{4,5},{5,4},{6,7},{7,6},{8,9},{9,8},{10,11... | collective-permute-start | bytes 135176 | tf_op jit(solution)/shard_map/ppermute | solution.py:469
  61.7 4.4 %collective-permute-start.18 = (bf16[32,1152]{1,0:T(8,128)(2,1)S(1)}, bf16[32,1152]{1,0:T(8,128)(2,1)S(1)}, u32[]{:S(2)}, u32[]{:S(2)}) collective-permute-start(bf16[32,1152]{1,0:T(8,128)(2,1)S(1)} %get-tuple-element.77), channel_id=1, source_target_pairs={{0,4},{4,0},{8,12},{12,8},{1,5},{5,1},{9,13},{13,9},{2,6},{6,2},{1... | collective-permute-start | bytes 221192 | tf_op jit(solution)/shard_map/ppermute | solution.py:469
  66.0 1.3 %collective-permute-start.24 = (bf16[56,576]{1,0:T(8,128)(2,1)S(1)}, bf16[56,576]{1,0:T(8,128)(2,1)S(1)}, u32[]{:S(2)}, u32[]{:S(2)}) collective-permute-start(bf16[56,576]{1,0:T(8,128)(2,1)S(1)} %get-tuple-element.86), channel_id=1, source_target_pairs={{0,16},{16,0},{1,17},{17,1},{2,18},{18,2},{3,19},{19,3},{4,20},{20... | collective-permute-start | bytes 193544 | tf_op jit(solution)/shard_map/ppermute | solution.py:469
  67.4 7.0 %collective-permute-start.27 = (bf16[56,576]{1,0:T(8,128)(2,1)S(1)}, bf16[56,576]{1,0:T(8,128)(2,1)S(1)}, u32[]{:S(2)}, u32[]{:S(2)}) collective-permute-start(bf16[56,576]{1,0:T(8,128)(2,1)S(1)} %shard_map.130.refs_0_), channel_id=1, source_target_pairs={{0,12},{4,8},{8,4},{12,0},{1,13},{5,9},{9,5},{13,1},{2,14},{6,10},... | collective-permute-start | bytes 193544 | tf_op jit(solution)/shard_map/ppermute | solution.py:469
  69.1 7.5 %collective-permute-start.26 = (bf16[56,576]{1,0:T(8,128)(2,1)S(1)}, bf16[56,576]{1,0:T(8,128)(2,1)S(1)}, u32[]{:S(2)}, u32[]{:S(2)}) collective-permute-start(bf16[56,576]{1,0:T(8,128)(2,1)S(1)} %shard_map.130.refs_0_), channel_id=1, source_target_pairs={{0,8},{4,12},{8,0},{12,4},{1,9},{5,13},{9,1},{13,5},{2,10},{6,14},... | collective-permute-start | bytes 193544 | tf_op jit(solution)/shard_map/ppermute | solution.py:469
  69.4 7.1 %collective-permute-start.25 = (bf16[56,576]{1,0:T(8,128)(2,1)S(1)}, bf16[56,576]{1,0:T(8,128)(2,1)S(1)}, u32[]{:S(2)}, u32[]{:S(2)}) collective-permute-start(bf16[56,576]{1,0:T(8,128)(2,1)S(1)} %shard_map.130.refs_0_), channel_id=1, source_target_pairs={{0,4},{4,0},{8,12},{12,8},{1,5},{5,1},{9,13},{13,9},{2,6},{6,2},{1... | collective-permute-start | bytes 193544 | tf_op jit(solution)/shard_map/ppermute | solution.py:469
  76.6 5.6 %collective-permute-start.30 = (bf16[56,576]{1,0:T(8,128)(2,1)S(1)}, bf16[56,576]{1,0:T(8,128)(2,1)S(1)}, u32[]{:S(2)}, u32[]{:S(2)}) collective-permute-start(bf16[56,576]{1,0:T(8,128)(2,1)S(1)} %shard_map.131.refs_0_), channel_id=1, source_target_pairs={{0,3},{1,2},{2,1},{3,0},{4,7},{5,6},{6,5},{7,4},{8,11},{9,10},{10,... | collective-permute-start | bytes 193544 | tf_op jit(solution)/shard_map/ppermute | solution.py:469
  78.2 5.0 %collective-permute-start.29 = (bf16[56,576]{1,0:T(8,128)(2,1)S(1)}, bf16[56,576]{1,0:T(8,128)(2,1)S(1)}, u32[]{:S(2)}, u32[]{:S(2)}) collective-permute-start(bf16[56,576]{1,0:T(8,128)(2,1)S(1)} %shard_map.131.refs_0_), channel_id=1, source_target_pairs={{0,2},{1,3},{2,0},{3,1},{4,6},{5,7},{6,4},{7,5},{8,10},{9,11},{10,... | collective-permute-start | bytes 193544 | tf_op jit(solution)/shard_map/ppermute | solution.py:469
  79.3 4.3 %collective-permute-start.28 = (bf16[56,576]{1,0:T(8,128)(2,1)S(1)}, bf16[56,576]{1,0:T(8,128)(2,1)S(1)}, u32[]{:S(2)}, u32[]{:S(2)}) collective-permute-start(bf16[56,576]{1,0:T(8,128)(2,1)S(1)} %shard_map.131.refs_0_), channel_id=1, source_target_pairs={{0,1},{1,0},{2,3},{3,2},{4,5},{5,4},{6,7},{7,6},{8,9},{9,8},{10,11... | collective-permute-start | bytes 193544 | tf_op jit(solution)/shard_map/ppermute | solution.py:469
  83.9 1.4 %collective-permute-start.31 = (bf16[64,1152]{1,0:T(8,128)(2,1)S(1)}, bf16[64,1152]{1,0:T(8,128)(2,1)S(1)}, u32[]{:S(2)}, u32[]{:S(2)}) collective-permute-start(bf16[64,1152]{1,0:T(8,128)(2,1)S(1)} %shard_map.132.refs_0_), channel_id=1, source_target_pairs={{0,16},{16,0},{1,17},{17,1},{2,18},{18,2},{3,19},{19,3},{4,20},{20... | collective-permute-start | bytes 442376 | tf_op jit(solution)/shard_map/ppermute | solution.py:469
  (5 other events, 109.0 us)

commit v18 on v16

--- a/solution.py
+++ b/solution.py
@@ -149,9 +149,7 @@
 
 
 def space_forward_kernel(frames, n_s, *refs):
-    packed, (qkv_ref, probs_ref, *outs) = refs[:n_s], refs[n_s : 2 * n_s + 2]
-    probs_buf, sems = refs[2 * n_s + 2 :]
-    copies = []
+    packed, (qkv_ref, probs_ref, *outs) = refs[:n_s], refs[n_s:]
     d_s, tokens = outs[0].shape
     patch_dev = tokens // frames
     total = n_s * patch_dev
@@ -172,21 +170,14 @@
             parts = []
             for s in range(0, total, step):
                 probs = probs_of(k_h.T, q_h[:, s : s + step], None)
-                probs_buf[f, h, :, s : s + step] = probs
+                probs_ref[f, h, :, s : s + step] = probs
                 parts.append(mm(v_h, probs.astype(BF16)))
             heads.append(parts[0] if len(parts) == 1 else jnp.concatenate(parts, axis=1))
-            copy = pltpu.make_async_copy(
-                probs_buf.at[f, h], probs_ref.at[f, h], sems.at[len(copies)]
-            )
-            copy.start()
-            copies.append(copy)
         out = jnp.concatenate(heads, axis=0).astype(BF16)
         for k in range(n_s):
             outs[k][:, f * patch_dev : (f + 1) * patch_dev] = out[
                 :, k * patch_dev : (k + 1) * patch_dev
             ]
-    for copy in copies:
-        copy.wait()
 
 
 def lane_block(rows):
@@ -511,10 +502,9 @@
     probs_dims = (frames, d_s // HEAD_DIM, total, total)
     qkv, probs, *out_s = call(
         functools.partial(space_forward_kernel, frames, n_s),
-        [shape((3, frames, d_s, total), BF16), pltpu.HBM(probs_dims, F32)]
+        [shape((3, frames, d_s, total), BF16), shape(probs_dims, F32)]
         + [shape((d_s, tokens), BF16)] * n_s,
         *packed,
-        scratch=[pltpu.VMEM(probs_dims, F32), dma((probs_dims[0] * probs_dims[1],))],
         after=time_pieces[:1],
     )
     out_s = exchange(out_s, "space")

time: 85.8 us -> 85.7 us (level)
  no operation moved by 1% of the time
where the time goes in v18:
time: 85.7 us; the launch traced here: 85.5 us
  starting transfers between devices  45.4 us (53%)
  waiting for transfers between devices  23.6 us (28%)
  Pallas kernels  15.7 us (18%)
    ppermute x32, starting transfers between devices, hops(): lax.ppermute(array, axis, [(i, i ^ k) for i in range(size)])  45.4 us
    ppermute x32, waiting for transfers between devices, hops(): lax.ppermute(array, axis, [(i, i ^ k) for i in range(size)])  23.6 us
    pallas_call x13, Pallas kernels, call(): pl.pallas_call(body, out_shape=outs + tuple((shape(x.shape, x.dtype) for...  15.7 us
  transfers between devices with their start and end apart: 32, of which 20 were waited for; matrix products, arithmetic and copies ran while one was open for 0% of the time, Pallas kernels for 10%

profile of v18, /device:TPU:0, one launch (start us, length us, event | category | flops | bytes accessed | tf_op | source)
XLA Modules:
  0.0 85.5 jit_solution(297878756098293378)
XLA Ops:
  0.7 2.6 %shard_map.121 = (bf16[896,128]{1,0:T(8,128)(2,1)S(1)}, bf16[896,128]{1,0:T(8,128)(2,1)S(1)}, bf16[896,128]{1,0:T(8,128)(2,1)S(1)}, bf16[896,128]{1,0:T(8,128)(2...) custom-call(bf16[1,2,64,1152]{3,2,1,0:T(8,128)(2,1)} %refs_1_.5, ...), custom_call_target="tpu_custom_call" | custom-call | tf_op jit(solution)/shard_map/pallas_call | solution.py:41
  3.3 3.0 %collective-permute-start = (bf16[896,128]{1,0:T(8,128)(2,1)S(1)}, bf16[896,128]{1,0:T(8,128)(2,1)S(1)}, u32[]{:S(2)}, u32[]{:S(2)}) collective-permute-start(bf16[896,128]{1,0:T(8,128)(2,1)S(1)} %get-tuple-element.47), channel_id=1, source_target_pairs={{0,1},{1,0},{2,3},{3,2},{4,5},{5,4},{6,7},{7,6},{8,9},{9,8},{10,11... | collective-permute-start | bytes 688136 | tf_op jit(solution)/shard_map/ppermute | solution.py:454
  6.3 1.6 %collective-permute-start.3 = (bf16[4,32,1152]{2,1,0:T(8,128)(2,1)S(1)}, bf16[4,32,1152]{2,1,0:T(8,128)(2,1)S(1)}, u32[]{:S(2)}, u32[]{:S(2)}) collective-permute-start(bf16[4,32,1152]{2,1,0:T(8,128)(2,1)S(1)} %get-tuple-element.50), channel_id=1, source_target_pairs={{0,4},{4,0},{8,12},{12,8},{1,5},{5,1},{9,13},{13,9},{2,6},{6,2},{1... | collective-permute-start | bytes 884744 | tf_op jit(solution)/shard_map/ppermute | solution.py:454
  7.8 1.6 %collective-permute-start.1 = (bf16[896,128]{1,0:T(8,128)(2,1)S(1)}, bf16[896,128]{1,0:T(8,128)(2,1)S(1)}, u32[]{:S(2)}, u32[]{:S(2)}) collective-permute-start(bf16[896,128]{1,0:T(8,128)(2,1)S(1)} %get-tuple-element.48), channel_id=1, source_target_pairs={{0,2},{1,3},{2,0},{3,1},{4,6},{5,7},{6,4},{7,5},{8,10},{9,11},{10,... | collective-permute-start | bytes 688136 | tf_op jit(solution)/shard_map/ppermute | solution.py:454
  9.8 2.6 %collective-permute-start.7 = (bf16[4,32,1152]{2,1,0:T(8,128)(2,1)S(1)}, bf16[4,32,1152]{2,1,0:T(8,128)(2,1)S(1)}, u32[]{:S(2)}, u32[]{:S(2)}) collective-permute-start(bf16[4,32,1152]{2,1,0:T(8,128)(2,1)S(1)} %get-tuple-element.56), channel_id=1, source_target_pairs={{0,8},{4,12},{8,0},{12,4},{1,9},{5,13},{9,1},{13,5},{2,10},{6,14},... | collective-permute-start | bytes 884744 | tf_op jit(solution)/shard_map/ppermute | solution.py:454
  12.7 4.2 %collective-permute-start.8 = (bf16[4,32,1152]{2,1,0:T(8,128)(2,1)S(1)}, bf16[4,32,1152]{2,1,0:T(8,128)(2,1)S(1)}, u32[]{:S(2)}, u32[]{:S(2)}) collective-permute-start(bf16[4,32,1152]{2,1,0:T(8,128)(2,1)S(1)} %get-tuple-element.57), channel_id=1, source_target_pairs={{0,12},{4,8},{8,4},{12,0},{1,13},{5,9},{9,5},{13,1},{2,14},{6,10},... | collective-permute-start | bytes 884744 | tf_op jit(solution)/shard_map/ppermute | solution.py:454
  16.9 2.7 %collective-permute-done.1.refs_2_.refs_8_ = bf16[896,128]{1,0:T(8,128)(2,1)S(1)} collective-permute-done((bf16[896,128]{1,0:T(8,128)(2,1)S(1)}, bf16[896,128]{1,0:T(8,128)(2,1)S(1)}, u32[]{:S(2)}, u32[]{:S(2)}) %collective-permute-start.1) | collective-permute-done | bytes 229408 | tf_op jit(solution)/shard_map/ppermute | solution.py:454
  19.5 2.9 %shard_map.122 = (bf16[3,2,288,256]{3,2,1,0:T(8,128)(2,1)S(1)}, f32[2,4,256,256]{3,2,1,0:T(8,128)S(1)}, bf16[288,128]{1,0:T(8,128)(2,1)S(1)}, bf16[288,128]{1,0:...) custom-call(bf16[896,128]{1,0:T(8,128)(2,1)S(1)} %get-tuple-element.46.refs_0_.refs_6_, ...), custom_call_target="tpu_custom_call" | custom-call | tf_op jit(solution)/shard_map/pallas_call | solution.py:41
  22.5 1.6 %collective-permute-start.4 = (bf16[288,128]{1,0:T(8,128)(2,1)S(1)}, bf16[288,128]{1,0:T(8,128)(2,1)S(1)}, u32[]{:S(2)}, u32[]{:S(2)}) collective-permute-start(bf16[288,128]{1,0:T(8,128)(2,1)S(1)} %get-tuple-element.51), channel_id=1, source_target_pairs={{0,3},{1,2},{2,1},{3,0},{4,7},{5,6},{6,5},{7,4},{8,11},{9,10},{10,... | collective-permute-start | bytes 221192 | tf_op jit(solution)/shard_map/ppermute | solution.py:454
  24.5 1.5 %collective-permute-start.6 = (bf16[288,128]{1,0:T(8,128)(2,1)S(1)}, bf16[288,128]{1,0:T(8,128)(2,1)S(1)}, u32[]{:S(2)}, u32[]{:S(2)}) collective-permute-start(bf16[288,128]{1,0:T(8,128)(2,1)S(1)} %get-tuple-element.53), channel_id=1, source_target_pairs={{0,1},{1,0},{2,3},{3,2},{4,5},{5,4},{6,7},{7,6},{8,9},{9,8},{10,11... | collective-permute-start | bytes 221192 | tf_op jit(solution)/shard_map/ppermute | solution.py:454
  26.0 1.8 %collective-permute-done.4.refs_0_ = bf16[288,128]{1,0:T(8,128)(2,1)S(1)} collective-permute-done((bf16[288,128]{1,0:T(8,128)(2,1)S(1)}, bf16[288,128]{1,0:T(8,128)(2,1)S(1)}, u32[]{:S(2)}, u32[]{:S(2)}) %collective-permute-start.4) | collective-permute-done | bytes 73760 | tf_op jit(solution)/shard_map/ppermute | solution.py:454
  29.2 3.1 %collective-permute-start.9 = (f32[8,128]{1,0:T(8,128)S(1)}, f32[8,128]{1,0:T(8,128)S(1)}, u32[]{:S(2)}, u32[]{:S(2)}) collective-permute-start(f32[8,128]{1,0:T(8,128)S(1)} %get-tuple-element.58), channel_id=1, source_target_pairs={{0,12},{4,8},{8,4},{12,0},{1,13},{5,9},{9,5},{13,1},{2,14},{6,10},... | collective-permute-start | bytes 12296 | tf_op jit(solution)/shard_map/ppermute | solution.py:454
  32.4 1.3 %collective-permute-start.11 = (f32[8,128]{1,0:T(8,128)S(1)}, f32[8,128]{1,0:T(8,128)S(1)}, u32[]{:S(2)}, u32[]{:S(2)}) collective-permute-start(f32[8,128]{1,0:T(8,128)S(1)} %get-tuple-element.60), channel_id=1, source_target_pairs={{0,4},{4,0},{8,12},{12,8},{1,5},{5,1},{9,13},{13,9},{2,6},{6,2},{1... | collective-permute-start | bytes 12296 | tf_op jit(solution)/shard_map/ppermute | solution.py:454
  33.7 1.4 %shard_map.124.refs_0_ = bf16[4,1152,128]{2,1,0:T(8,128)(2,1)S(1)} custom-call(bf16[1,2,64,1152]{3,2,1,0:T(8,128)(2,1)} %refs_0_.4, bf16[1,2,64,1152]{3,2,1,0:T(8,128)(2,1)} %refs_1_.3, bf16[1,2,64,1152]{3,2,1,0:T(8,128)(2,1)} %refs_2_.3, bf16[1,2,64,1152]{3,2,1,0:T(8,128)(2,1)} %refs_0_.5, bf16[4,32,1152]{2,1,0:T(8,128)(2,1)S(1)} %collective-permute-done.3.refs_4_, ...), custom_call_target="tpu_custom_call" | custom-call | tf_op jit(solution)/shard_map/pallas_call | solution.py:41
  35.1 2.7 %collective-permute-done.10.refs_3_ = f32[8,128]{1,0:T(8,128)S(1)} collective-permute-done((f32[8,128]{1,0:T(8,128)S(1)}, f32[8,128]{1,0:T(8,128)S(1)}, u32[]{:S(2)}, u32[]{:S(2)}) %collective-permute-start.10) | collective-permute-done | bytes 4128 | tf_op jit(solution)/shard_map/ppermute | solution.py:454
  37.7 3.1 %shard_map.125 = (bf16[32,1152]{1,0:T(8,128)(2,1)S(1)}, bf16[32,1152]{1,0:T(8,128)(2,1)S(1)}, bf16[32,1152]{1,0:T(8,128)(2,1)S(1)}, bf16[32,1152]{1,0:T(8,128)(2...) custom-call(bf16[4,1152,128]{2,1,0:T(8,128)(2,1)S(1)} %shard_map.124, ...), custom_call_target="tpu_custom_call" | custom-call | tf_op jit(solution)/shard_map/pallas_call | solution.py:41
  40.8 2.5 %collective-permute-start.12 = (f32[8,128]{1,0:T(8,128)S(1)}, f32[8,128]{1,0:T(8,128)S(1)}, u32[]{:S(2)}, u32[]{:S(2)}) collective-permute-start(f32[8,128]{1,0:T(8,128)S(1)} %get-tuple-element.66), channel_id=1, source_target_pairs={{0,12},{4,8},{8,4},{12,0},{1,13},{5,9},{9,5},{13,1},{2,14},{6,10},... | collective-permute-start | bytes 12296 | tf_op jit(solution)/shard_map/ppermute | solution.py:454
  44.2 1.1 %collective-permute-start.14 = (f32[8,128]{1,0:T(8,128)S(1)}, f32[8,128]{1,0:T(8,128)S(1)}, u32[]{:S(2)}, u32[]{:S(2)}) collective-permute-start(f32[8,128]{1,0:T(8,128)S(1)} %get-tuple-element.68), channel_id=1, source_target_pairs={{0,4},{4,0},{8,12},{12,8},{1,5},{5,1},{9,13},{13,9},{2,6},{6,2},{1... | collective-permute-start | bytes 12296 | tf_op jit(solution)/shard_map/ppermute | solution.py:454
  46.3 1.6 %collective-permute-done.13.refs_3_ = f32[8,128]{1,0:T(8,128)S(1)} collective-permute-done((f32[8,128]{1,0:T(8,128)S(1)}, f32[8,128]{1,0:T(8,128)S(1)}, u32[]{:S(2)}, u32[]{:S(2)}) %collective-permute-start.13) | collective-permute-done | bytes 4128 | tf_op jit(solution)/shard_map/ppermute | solution.py:454
  48.3 2.6 %collective-permute-start.15 = (bf16[288,128]{1,0:T(8,128)(2,1)S(1)}, bf16[288,128]{1,0:T(8,128)(2,1)S(1)}, u32[]{:S(2)}, u32[]{:S(2)}) collective-permute-start(bf16[288,128]{1,0:T(8,128)(2,1)S(1)} %get-tuple-element.72), channel_id=1, source_target_pairs={{0,3},{1,2},{2,1},{3,0},{4,7},{5,6},{6,5},{7,4},{8,11},{9,10},{10,... | collective-permute-start | bytes 221192 | tf_op jit(solution)/shard_map/ppermute | solution.py:454
  51.8 2.0 %collective-permute-start.19 = (bf16[32,1152]{1,0:T(8,128)(2,1)S(1)}, bf16[32,1152]{1,0:T(8,128)(2,1)S(1)}, u32[]{:S(2)}, u32[]{:S(2)}) collective-permute-start(bf16[32,1152]{1,0:T(8,128)(2,1)S(1)} %get-tuple-element.78), channel_id=1, source_target_pairs={{0,8},{4,12},{8,0},{12,4},{1,9},{5,13},{9,1},{13,5},{2,10},{6,14},... | collective-permute-start | bytes 221192 | tf_op jit(solution)/shard_map/ppermute | solution.py:454
  53.9 1.3 %collective-permute-start.20 = (bf16[32,1152]{1,0:T(8,128)(2,1)S(1)}, bf16[32,1152]{1,0:T(8,128)(2,1)S(1)}, u32[]{:S(2)}, u32[]{:S(2)}) collective-permute-start(bf16[32,1152]{1,0:T(8,128)(2,1)S(1)} %get-tuple-element.79), channel_id=1, source_target_pairs={{0,12},{4,8},{8,4},{12,0},{1,13},{5,9},{9,5},{13,1},{2,14},{6,10},... | collective-permute-start | bytes 221192 | tf_op jit(solution)/shard_map/ppermute | solution.py:454
  55.6 2.6 %shard_map.127 = (bf16[32,704]{1,0:T(8,128)(2,1)S(1)}, bf16[32,704]{1,0:T(8,128)(2,1)S(1)}, bf16[32,704]{1,0:T(8,128)(2,1)S(1)}, bf16[32,704]{1,0:T(8,128)(2,1)S...) custom-call(bf16[3,2,288,256]{3,2,1,0:T(8,128)(2,1)S(1)} %get-tuple-element.63.refs_0_,, ...), custom_call_target="tpu_custom_call", output_to_operand_aliasing={{5}: (14, {})} | custom-call | tf_op jit(solution)/shard_map/pallas_call | solution.py:41
  58.3 2.2 %collective-permute-start.21 = (bf16[32,704]{1,0:T(8,128)(2,1)S(1)}, bf16[32,704]{1,0:T(8,128)(2,1)S(1)}, u32[]{:S(2)}, u32[]{:S(2)}) collective-permute-start(bf16[32,704]{1,0:T(8,128)(2,1)S(1)} %get-tuple-element.81), channel_id=1, source_target_pairs={{0,3},{1,2},{2,1},{3,0},{4,7},{5,6},{6,5},{7,4},{8,11},{9,10},{10,... | collective-permute-start | bytes 135176 | tf_op jit(solution)/shard_map/ppermute | solution.py:454
  63.3 1.2 %collective-permute-done.22.refs_3_ = bf16[32,704]{1,0:T(8,128)(2,1)S(1)} collective-permute-done((bf16[32,704]{1,0:T(8,128)(2,1)S(1)}, bf16[32,704]{1,0:T(8,128)(2,1)S(1)}, u32[]{:S(2)}, u32[]{:S(2)}) %collective-permute-start.22) | collective-permute-done | bytes 45088 | tf_op jit(solution)/shard_map/ppermute | solution.py:454
  66.6 2.5 %collective-permute-start.27 = (bf16[56,576]{1,0:T(8,128)(2,1)S(1)}, bf16[56,576]{1,0:T(8,128)(2,1)S(1)}, u32[]{:S(2)}, u32[]{:S(2)}) collective-permute-start(bf16[56,576]{1,0:T(8,128)(2,1)S(1)} %shard_map.130.refs_0_), channel_id=1, source_target_pairs={{0,12},{4,8},{8,4},{12,0},{1,13},{5,9},{9,5},{13,1},{2,14},{6,10},... | collective-permute-start | bytes 193544 | tf_op jit(solution)/shard_map/ppermute | solution.py:454
  69.2 1.9 %collective-permute-start.25 = (bf16[56,576]{1,0:T(8,128)(2,1)S(1)}, bf16[56,576]{1,0:T(8,128)(2,1)S(1)}, u32[]{:S(2)}, u32[]{:S(2)}) collective-permute-start(bf16[56,576]{1,0:T(8,128)(2,1)S(1)} %shard_map.130.refs_0_), channel_id=1, source_target_pairs={{0,4},{4,0},{8,12},{12,8},{1,5},{5,1},{9,13},{13,9},{2,6},{6,2},{1... | collective-permute-start | bytes 193544 | tf_op jit(solution)/shard_map/ppermute | solution.py:454
  71.1 2.6 %collective-permute-done.27.refs_3_ = bf16[56,576]{1,0:T(8,128)(2,1)S(1)} collective-permute-done((bf16[56,576]{1,0:T(8,128)(2,1)S(1)}, bf16[56,576]{1,0:T(8,128)(2,1)S(1)}, u32[]{:S(2)}, u32[]{:S(2)}) %collective-permute-start.27) | collective-permute-done | bytes 64544 | tf_op jit(solution)/shard_map/ppermute | solution.py:454
  73.7 2.2 %collective-permute-done.26.refs_2_ = bf16[56,576]{1,0:T(8,128)(2,1)S(1)} collective-permute-done((bf16[56,576]{1,0:T(8,128)(2,1)S(1)}, bf16[56,576]{1,0:T(8,128)(2,1)S(1)}, u32[]{:S(2)}, u32[]{:S(2)}) %collective-permute-start.26) | collective-permute-done | bytes 64544 | tf_op jit(solution)/shard_map/ppermute | solution.py:454
  75.9 2.3 %collective-permute-start.30 = (bf16[56,576]{1,0:T(8,128)(2,1)S(1)}, bf16[56,576]{1,0:T(8,128)(2,1)S(1)}, u32[]{:S(2)}, u32[]{:S(2)}) collective-permute-start(bf16[56,576]{1,0:T(8,128)(2,1)S(1)} %shard_map.131.refs_0_), channel_id=1, source_target_pairs={{0,3},{1,2},{2,1},{3,0},{4,7},{5,6},{6,5},{7,4},{8,11},{9,10},{10,... | collective-permute-start | bytes 193544 | tf_op jit(solution)/shard_map/ppermute | solution.py:454
  79.5 1.8 %collective-permute-done.30.refs_3_ = bf16[56,576]{1,0:T(8,128)(2,1)S(1)} collective-permute-done((bf16[56,576]{1,0:T(8,128)(2,1)S(1)}, bf16[56,576]{1,0:T(8,128)(2,1)S(1)}, u32[]{:S(2)}, u32[]{:S(2)}) %collective-permute-start.30) | collective-permute-done | bytes 64544 | tf_op jit(solution)/shard_map/ppermute | solution.py:454
  81.3 1.5 %collective-permute-done.29.refs_2_ = bf16[56,576]{1,0:T(8,128)(2,1)S(1)} collective-permute-done((bf16[56,576]{1,0:T(8,128)(2,1)S(1)}, bf16[56,576]{1,0:T(8,128)(2,1)S(1)}, u32[]{:S(2)}, u32[]{:S(2)}) %collective-permute-start.29) | collective-permute-done | bytes 64544 | tf_op jit(solution)/shard_map/ppermute | solution.py:454
  (53 shorter events, 15.4 us)
Async XLA Ops:
  3.3 9.4 %collective-permute-start = (bf16[896,128]{1,0:T(8,128)(2,1)S(1)}, bf16[896,128]{1,0:T(8,128)(2,1)S(1)}, u32[]{:S(2)}, u32[]{:S(2)}) collective-permute-start(bf16[896,128]{1,0:T(8,128)(2,1)S(1)} %get-tuple-element.47), channel_id=1, source_target_pairs={{0,1},{1,0},{2,3},{3,2},{4,5},{5,4},{6,7},{7,6},{8,9},{9,8},{10,11... | collective-permute-start | bytes 688136 | tf_op jit(solution)/shard_map/ppermute | solution.py:454
  6.3 13.3 %collective-permute-start.3 = (bf16[4,32,1152]{2,1,0:T(8,128)(2,1)S(1)}, bf16[4,32,1152]{2,1,0:T(8,128)(2,1)S(1)}, u32[]{:S(2)}, u32[]{:S(2)}) collective-permute-start(bf16[4,32,1152]{2,1,0:T(8,128)(2,1)S(1)} %get-tuple-element.50), channel_id=1, source_target_pairs={{0,4},{4,0},{8,12},{12,8},{1,5},{5,1},{9,13},{13,9},{2,6},{6,2},{1... | collective-permute-start | bytes 884744 | tf_op jit(solution)/shard_map/ppermute | solution.py:454
  7.8 11.7 %collective-permute-start.1 = (bf16[896,128]{1,0:T(8,128)(2,1)S(1)}, bf16[896,128]{1,0:T(8,128)(2,1)S(1)}, u32[]{:S(2)}, u32[]{:S(2)}) collective-permute-start(bf16[896,128]{1,0:T(8,128)(2,1)S(1)} %get-tuple-element.48), channel_id=1, source_target_pairs={{0,2},{1,3},{2,0},{3,1},{4,6},{5,7},{6,4},{7,5},{8,10},{9,11},{10,... | collective-permute-start | bytes 688136 | tf_op jit(solution)/shard_map/ppermute | solution.py:454
  9.4 10.1 %collective-permute-start.2 = (bf16[896,128]{1,0:T(8,128)(2,1)S(1)}, bf16[896,128]{1,0:T(8,128)(2,1)S(1)}, u32[]{:S(2)}, u32[]{:S(2)}) collective-permute-start(bf16[896,128]{1,0:T(8,128)(2,1)S(1)} %get-tuple-element.49), channel_id=1, source_target_pairs={{0,3},{1,2},{2,1},{3,0},{4,7},{5,6},{6,5},{7,4},{8,11},{9,10},{10,... | collective-permute-start | bytes 688136 | tf_op jit(solution)/shard_map/ppermute | solution.py:454
  9.8 23.9 %collective-permute-start.7 = (bf16[4,32,1152]{2,1,0:T(8,128)(2,1)S(1)}, bf16[4,32,1152]{2,1,0:T(8,128)(2,1)S(1)}, u32[]{:S(2)}, u32[]{:S(2)}) collective-permute-start(bf16[4,32,1152]{2,1,0:T(8,128)(2,1)S(1)} %get-tuple-element.56), channel_id=1, source_target_pairs={{0,8},{4,12},{8,0},{12,4},{1,9},{5,13},{9,1},{13,5},{2,10},{6,14},... | collective-permute-start | bytes 884744 | tf_op jit(solution)/shard_map/ppermute | solution.py:454
  12.7 21.0 %collective-permute-start.8 = (bf16[4,32,1152]{2,1,0:T(8,128)(2,1)S(1)}, bf16[4,32,1152]{2,1,0:T(8,128)(2,1)S(1)}, u32[]{:S(2)}, u32[]{:S(2)}) collective-permute-start(bf16[4,32,1152]{2,1,0:T(8,128)(2,1)S(1)} %get-tuple-element.57), channel_id=1, source_target_pairs={{0,12},{4,8},{8,4},{12,0},{1,13},{5,9},{9,5},{13,1},{2,14},{6,10},... | collective-permute-start | bytes 884744 | tf_op jit(solution)/shard_map/ppermute | solution.py:454
  22.5 5.3 %collective-permute-start.4 = (bf16[288,128]{1,0:T(8,128)(2,1)S(1)}, bf16[288,128]{1,0:T(8,128)(2,1)S(1)}, u32[]{:S(2)}, u32[]{:S(2)}) collective-permute-start(bf16[288,128]{1,0:T(8,128)(2,1)S(1)} %get-tuple-element.51), channel_id=1, source_target_pairs={{0,3},{1,2},{2,1},{3,0},{4,7},{5,6},{6,5},{7,4},{8,11},{9,10},{10,... | collective-permute-start | bytes 221192 | tf_op jit(solution)/shard_map/ppermute | solution.py:454
  24.0 4.5 %collective-permute-start.5 = (bf16[288,128]{1,0:T(8,128)(2,1)S(1)}, bf16[288,128]{1,0:T(8,128)(2,1)S(1)}, u32[]{:S(2)}, u32[]{:S(2)}) collective-permute-start(bf16[288,128]{1,0:T(8,128)(2,1)S(1)} %get-tuple-element.52), channel_id=1, source_target_pairs={{0,2},{1,3},{2,0},{3,1},{4,6},{5,7},{6,4},{7,5},{8,10},{9,11},{10,... | collective-permute-start | bytes 221192 | tf_op jit(solution)/shard_map/ppermute | solution.py:454
  24.5 4.4 %collective-permute-start.6 = (bf16[288,128]{1,0:T(8,128)(2,1)S(1)}, bf16[288,128]{1,0:T(8,128)(2,1)S(1)}, u32[]{:S(2)}, u32[]{:S(2)}) collective-permute-start(bf16[288,128]{1,0:T(8,128)(2,1)S(1)} %get-tuple-element.53), channel_id=1, source_target_pairs={{0,1},{1,0},{2,3},{3,2},{4,5},{5,4},{6,7},{7,6},{8,9},{9,8},{10,11... | collective-permute-start | bytes 221192 | tf_op jit(solution)/shard_map/ppermute | solution.py:454
  29.2 5.8 %collective-permute-start.9 = (f32[8,128]{1,0:T(8,128)S(1)}, f32[8,128]{1,0:T(8,128)S(1)}, u32[]{:S(2)}, u32[]{:S(2)}) collective-permute-start(f32[8,128]{1,0:T(8,128)S(1)} %get-tuple-element.58), channel_id=1, source_target_pairs={{0,12},{4,8},{8,4},{12,0},{1,13},{5,9},{9,5},{13,1},{2,14},{6,10},... | collective-permute-start | bytes 12296 | tf_op jit(solution)/shard_map/ppermute | solution.py:454
  32.4 5.4 %collective-permute-start.10 = (f32[8,128]{1,0:T(8,128)S(1)}, f32[8,128]{1,0:T(8,128)S(1)}, u32[]{:S(2)}, u32[]{:S(2)}) collective-permute-start(f32[8,128]{1,0:T(8,128)S(1)} %get-tuple-element.59), channel_id=1, source_target_pairs={{0,8},{4,12},{8,0},{12,4},{1,9},{5,13},{9,1},{13,5},{2,10},{6,14},... | collective-permute-start | bytes 12296 | tf_op jit(solution)/shard_map/ppermute | solution.py:454
  32.4 5.4 %collective-permute-start.11 = (f32[8,128]{1,0:T(8,128)S(1)}, f32[8,128]{1,0:T(8,128)S(1)}, u32[]{:S(2)}, u32[]{:S(2)}) collective-permute-start(f32[8,128]{1,0:T(8,128)S(1)} %get-tuple-element.60), channel_id=1, source_target_pairs={{0,4},{4,0},{8,12},{12,8},{1,5},{5,1},{9,13},{13,9},{2,6},{6,2},{1... | collective-permute-start | bytes 12296 | tf_op jit(solution)/shard_map/ppermute | solution.py:454
  40.8 5.4 %collective-permute-start.12 = (f32[8,128]{1,0:T(8,128)S(1)}, f32[8,128]{1,0:T(8,128)S(1)}, u32[]{:S(2)}, u32[]{:S(2)}) collective-permute-start(f32[8,128]{1,0:T(8,128)S(1)} %get-tuple-element.66), channel_id=1, source_target_pairs={{0,12},{4,8},{8,4},{12,0},{1,13},{5,9},{9,5},{13,1},{2,14},{6,10},... | collective-permute-start | bytes 12296 | tf_op jit(solution)/shard_map/ppermute | solution.py:454
  43.3 4.5 %collective-permute-start.13 = (f32[8,128]{1,0:T(8,128)S(1)}, f32[8,128]{1,0:T(8,128)S(1)}, u32[]{:S(2)}, u32[]{:S(2)}) collective-permute-start(f32[8,128]{1,0:T(8,128)S(1)} %get-tuple-element.67), channel_id=1, source_target_pairs={{0,8},{4,12},{8,0},{12,4},{1,9},{5,13},{9,1},{13,5},{2,10},{6,14},... | collective-permute-start | bytes 12296 | tf_op jit(solution)/shard_map/ppermute | solution.py:454
  44.2 3.7 %collective-permute-start.14 = (f32[8,128]{1,0:T(8,128)S(1)}, f32[8,128]{1,0:T(8,128)S(1)}, u32[]{:S(2)}, u32[]{:S(2)}) collective-permute-start(f32[8,128]{1,0:T(8,128)S(1)} %get-tuple-element.68), channel_id=1, source_target_pairs={{0,4},{4,0},{8,12},{12,8},{1,5},{5,1},{9,13},{13,9},{2,6},{6,2},{1... | collective-permute-start | bytes 12296 | tf_op jit(solution)/shard_map/ppermute | solution.py:454
  48.3 6.9 %collective-permute-start.15 = (bf16[288,128]{1,0:T(8,128)(2,1)S(1)}, bf16[288,128]{1,0:T(8,128)(2,1)S(1)}, u32[]{:S(2)}, u32[]{:S(2)}) collective-permute-start(bf16[288,128]{1,0:T(8,128)(2,1)S(1)} %get-tuple-element.72), channel_id=1, source_target_pairs={{0,3},{1,2},{2,1},{3,0},{4,7},{5,6},{6,5},{7,4},{8,11},{9,10},{10,... | collective-permute-start | bytes 221192 | tf_op jit(solution)/shard_map/ppermute | solution.py:454
  50.9 4.4 %collective-permute-start.16 = (bf16[288,128]{1,0:T(8,128)(2,1)S(1)}, bf16[288,128]{1,0:T(8,128)(2,1)S(1)}, u32[]{:S(2)}, u32[]{:S(2)}) collective-permute-start(bf16[288,128]{1,0:T(8,128)(2,1)S(1)} %get-tuple-element.73), channel_id=1, source_target_pairs={{0,2},{1,3},{2,0},{3,1},{4,6},{5,7},{6,4},{7,5},{8,10},{9,11},{10,... | collective-permute-start | bytes 221192 | tf_op jit(solution)/shard_map/ppermute | solution.py:454
  51.3 4.4 %collective-permute-start.17 = (bf16[288,128]{1,0:T(8,128)(2,1)S(1)}, bf16[288,128]{1,0:T(8,128)(2,1)S(1)}, u32[]{:S(2)}, u32[]{:S(2)}) collective-permute-start(bf16[288,128]{1,0:T(8,128)(2,1)S(1)} %get-tuple-element.74), channel_id=1, source_target_pairs={{0,1},{1,0},{2,3},{3,2},{4,5},{5,4},{6,7},{7,6},{8,9},{9,8},{10,11... | collective-permute-start | bytes 221192 | tf_op jit(solution)/shard_map/ppermute | solution.py:454
  51.8 10.0 %collective-permute-start.19 = (bf16[32,1152]{1,0:T(8,128)(2,1)S(1)}, bf16[32,1152]{1,0:T(8,128)(2,1)S(1)}, u32[]{:S(2)}, u32[]{:S(2)}) collective-permute-start(bf16[32,1152]{1,0:T(8,128)(2,1)S(1)} %get-tuple-element.78), channel_id=1, source_target_pairs={{0,8},{4,12},{8,0},{12,4},{1,9},{5,13},{9,1},{13,5},{2,10},{6,14},... | collective-permute-start | bytes 221192 | tf_op jit(solution)/shard_map/ppermute | solution.py:454
  53.9 9.0 %collective-permute-start.20 = (bf16[32,1152]{1,0:T(8,128)(2,1)S(1)}, bf16[32,1152]{1,0:T(8,128)(2,1)S(1)}, u32[]{:S(2)}, u32[]{:S(2)}) collective-permute-start(bf16[32,1152]{1,0:T(8,128)(2,1)S(1)} %get-tuple-element.79), channel_id=1, source_target_pairs={{0,12},{4,8},{8,4},{12,0},{1,13},{5,9},{9,5},{13,1},{2,14},{6,10},... | collective-permute-start | bytes 221192 | tf_op jit(solution)/shard_map/ppermute | solution.py:454
  58.3 5.1 %collective-permute-start.21 = (bf16[32,704]{1,0:T(8,128)(2,1)S(1)}, bf16[32,704]{1,0:T(8,128)(2,1)S(1)}, u32[]{:S(2)}, u32[]{:S(2)}) collective-permute-start(bf16[32,704]{1,0:T(8,128)(2,1)S(1)} %get-tuple-element.81), channel_id=1, source_target_pairs={{0,3},{1,2},{2,1},{3,0},{4,7},{5,6},{6,5},{7,4},{8,11},{9,10},{10,... | collective-permute-start | bytes 135176 | tf_op jit(solution)/shard_map/ppermute | solution.py:454
  60.4 4.1 %collective-permute-start.22 = (bf16[32,704]{1,0:T(8,128)(2,1)S(1)}, bf16[32,704]{1,0:T(8,128)(2,1)S(1)}, u32[]{:S(2)}, u32[]{:S(2)}) collective-permute-start(bf16[32,704]{1,0:T(8,128)(2,1)S(1)} %get-tuple-element.82), channel_id=1, source_target_pairs={{0,2},{1,3},{2,0},{3,1},{4,6},{5,7},{6,4},{7,5},{8,10},{9,11},{10,... | collective-permute-start | bytes 135176 | tf_op jit(solution)/shard_map/ppermute | solution.py:454
  60.9 4.1 %collective-permute-start.23 = (bf16[32,704]{1,0:T(8,128)(2,1)S(1)}, bf16[32,704]{1,0:T(8,128)(2,1)S(1)}, u32[]{:S(2)}, u32[]{:S(2)}) collective-permute-start(bf16[32,704]{1,0:T(8,128)(2,1)S(1)} %get-tuple-element.83), channel_id=1, source_target_pairs={{0,1},{1,0},{2,3},{3,2},{4,5},{5,4},{6,7},{7,6},{8,9},{9,8},{10,11... | collective-permute-start | bytes 135176 | tf_op jit(solution)/shard_map/ppermute | solution.py:454
  61.8 4.4 %collective-permute-start.18 = (bf16[32,1152]{1,0:T(8,128)(2,1)S(1)}, bf16[32,1152]{1,0:T(8,128)(2,1)S(1)}, u32[]{:S(2)}, u32[]{:S(2)}) collective-permute-start(bf16[32,1152]{1,0:T(8,128)(2,1)S(1)} %get-tuple-element.77), channel_id=1, source_target_pairs={{0,4},{4,0},{8,12},{12,8},{1,5},{5,1},{9,13},{13,9},{2,6},{6,2},{1... | collective-permute-start | bytes 221192 | tf_op jit(solution)/shard_map/ppermute | solution.py:454
  65.3 1.3 %collective-permute-start.24 = (bf16[56,576]{1,0:T(8,128)(2,1)S(1)}, bf16[56,576]{1,0:T(8,128)(2,1)S(1)}, u32[]{:S(2)}, u32[]{:S(2)}) collective-permute-start(bf16[56,576]{1,0:T(8,128)(2,1)S(1)} %get-tuple-element.86), channel_id=1, source_target_pairs={{0,16},{16,0},{1,17},{17,1},{2,18},{18,2},{3,19},{19,3},{4,20},{20... | collective-permute-start | bytes 193544 | tf_op jit(solution)/shard_map/ppermute | solution.py:454
  66.6 7.0 %collective-permute-start.27 = (bf16[56,576]{1,0:T(8,128)(2,1)S(1)}, bf16[56,576]{1,0:T(8,128)(2,1)S(1)}, u32[]{:S(2)}, u32[]{:S(2)}) collective-permute-start(bf16[56,576]{1,0:T(8,128)(2,1)S(1)} %shard_map.130.refs_0_), channel_id=1, source_target_pairs={{0,12},{4,8},{8,4},{12,0},{1,13},{5,9},{9,5},{13,1},{2,14},{6,10},... | collective-permute-start | bytes 193544 | tf_op jit(solution)/shard_map/ppermute | solution.py:454
  69.2 6.7 %collective-permute-start.26 = (bf16[56,576]{1,0:T(8,128)(2,1)S(1)}, bf16[56,576]{1,0:T(8,128)(2,1)S(1)}, u32[]{:S(2)}, u32[]{:S(2)}) collective-permute-start(bf16[56,576]{1,0:T(8,128)(2,1)S(1)} %shard_map.130.refs_0_), channel_id=1, source_target_pairs={{0,8},{4,12},{8,0},{12,4},{1,9},{5,13},{9,1},{13,5},{2,10},{6,14},... | collective-permute-start | bytes 193544 | tf_op jit(solution)/shard_map/ppermute | solution.py:454
  69.2 6.7 %collective-permute-start.25 = (bf16[56,576]{1,0:T(8,128)(2,1)S(1)}, bf16[56,576]{1,0:T(8,128)(2,1)S(1)}, u32[]{:S(2)}, u32[]{:S(2)}) collective-permute-start(bf16[56,576]{1,0:T(8,128)(2,1)S(1)} %shard_map.130.refs_0_), channel_id=1, source_target_pairs={{0,4},{4,0},{8,12},{12,8},{1,5},{5,1},{9,13},{13,9},{2,6},{6,2},{1... | collective-permute-start | bytes 193544 | tf_op jit(solution)/shard_map/ppermute | solution.py:454
  75.9 5.4 %collective-permute-start.30 = (bf16[56,576]{1,0:T(8,128)(2,1)S(1)}, bf16[56,576]{1,0:T(8,128)(2,1)S(1)}, u32[]{:S(2)}, u32[]{:S(2)}) collective-permute-start(bf16[56,576]{1,0:T(8,128)(2,1)S(1)} %shard_map.131.refs_0_), channel_id=1, source_target_pairs={{0,3},{1,2},{2,1},{3,0},{4,7},{5,6},{6,5},{7,4},{8,11},{9,10},{10,... | collective-permute-start | bytes 193544 | tf_op jit(solution)/shard_map/ppermute | solution.py:454
  78.2 4.5 %collective-permute-start.29 = (bf16[56,576]{1,0:T(8,128)(2,1)S(1)}, bf16[56,576]{1,0:T(8,128)(2,1)S(1)}, u32[]{:S(2)}, u32[]{:S(2)}) collective-permute-start(bf16[56,576]{1,0:T(8,128)(2,1)S(1)} %shard_map.131.refs_0_), channel_id=1, source_target_pairs={{0,2},{1,3},{2,0},{3,1},{4,6},{5,7},{6,4},{7,5},{8,10},{9,11},{10,... | collective-permute-start | bytes 193544 | tf_op jit(solution)/shard_map/ppermute | solution.py:454
  78.6 4.3 %collective-permute-start.28 = (bf16[56,576]{1,0:T(8,128)(2,1)S(1)}, bf16[56,576]{1,0:T(8,128)(2,1)S(1)}, u32[]{:S(2)}, u32[]{:S(2)}) collective-permute-start(bf16[56,576]{1,0:T(8,128)(2,1)S(1)} %shard_map.131.refs_0_), channel_id=1, source_target_pairs={{0,1},{1,0},{2,3},{3,2},{4,5},{5,4},{6,7},{7,6},{8,9},{9,8},{10,11... | collective-permute-start | bytes 193544 | tf_op jit(solution)/shard_map/ppermute | solution.py:454
  83.2 1.4 %collective-permute-start.31 = (bf16[64,1152]{1,0:T(8,128)(2,1)S(1)}, bf16[64,1152]{1,0:T(8,128)(2,1)S(1)}, u32[]{:S(2)}, u32[]{:S(2)}) collective-permute-start(bf16[64,1152]{1,0:T(8,128)(2,1)S(1)} %shard_map.132.refs_0_), channel_id=1, source_target_pairs={{0,16},{16,0},{1,17},{17,1},{2,18},{18,2},{3,19},{19,3},{4,20},{20... | collective-permute-start | bytes 442376 | tf_op jit(solution)/shard_map/ppermute | solution.py:454
  (4 other events, 87.3 us)

commit v19 on v18

--- a/solution.py
+++ b/solution.py
@@ -289,7 +289,8 @@
         sends[k][...] = fold(d_codes[k * per : (k + 1) * per])
     out = jnp.concatenate(outs_h, axis=0).astype(BF16).T
     for k in range(n_t):
-        outs[k][...] = out[k * per : (k + 1) * per]
+        rows = [out[k * per : (k + 1) * per], jnp.zeros((8, width), BF16)]
+        outs[k][...] = jnp.concatenate(rows, axis=0)
     grad_b_ref[:RANK] = mm(codes_q, d_query, NT)
     grad_b_ref[RANK:] = mm(codes_v, d_vals, NT)
 
@@ -529,7 +530,7 @@
     )
     timed = call(
         functools.partial(time_kernel, n_t, sub),
-        [shape((frames * sub, width), BF16)] * n_t
+        [shape((frames * sub + 8, width), BF16)] * n_t
         + [shape((8, 128), F32)] * n_t
         + [shape((2 * RANK, width), F32)],
         turned, adapters_b, *codes[::-1],

time: 85.7 us -> 85.7 us (level)
  starting transfers between devices: 45.4 us -> 46.5 us
  waiting for transfers between devices: 23.6 us -> 22.5 us
    ppermute x32, waiting for transfers between devices: 23.6 us -> 22.5 us  [hops(): lax.ppermute(array, axis, [(i, i ^ k) for i in range(size)])]
    ppermute x32, starting transfers between devices: 45.4 us -> 46.5 us  [hops(): lax.ppermute(array, axis, [(i, i ^ k) for i in range(size)])]
  transfers between devices with their start and end apart: 32 -> 32, of which waited for: 20 -> 19; matrix products, arithmetic and copies ran while one was open for 0% -> 0% of each run, Pallas kernels for 10% -> 10%
where the time goes in v19:
time: 85.7 us; the launch traced here: 85.5 us
  starting transfers between devices  46.5 us (54%)
  waiting for transfers between devices  22.5 us (26%)
  Pallas kernels  15.7 us (18%)
    ppermute x32, starting transfers between devices, hops(): lax.ppermute(array, axis, [(i, i ^ k) for i in range(size)])  46.5 us
    ppermute x32, waiting for transfers between devices, hops(): lax.ppermute(array, axis, [(i, i ^ k) for i in range(size)])  22.5 us
    pallas_call x13, Pallas kernels, call(): pl.pallas_call(body, out_shape=outs + tuple((shape(x.shape, x.dtype) for...  15.7 us
  transfers between devices with their start and end apart: 32, of which 19 were waited for; matrix products, arithmetic and copies ran while one was open for 0% of the time, Pallas kernels for 10%

profile of v19, /device:TPU:0, one launch (start us, length us, event | category | flops | bytes accessed | tf_op | source)
XLA Modules:
  0.0 85.5 jit_solution(9318612785637727472)
XLA Ops:
  0.7 2.6 %shard_map.121 = (bf16[896,128]{1,0:T(8,128)(2,1)S(1)}, bf16[896,128]{1,0:T(8,128)(2,1)S(1)}, bf16[896,128]{1,0:T(8,128)(2,1)S(1)}, bf16[896,128]{1,0:T(8,128)(2...) custom-call(bf16[1,2,64,1152]{3,2,1,0:T(8,128)(2,1)} %refs_1_.5, ...), custom_call_target="tpu_custom_call" | custom-call | tf_op jit(solution)/shard_map/pallas_call | solution.py:41
  3.3 3.0 %collective-permute-start = (bf16[896,128]{1,0:T(8,128)(2,1)S(1)}, bf16[896,128]{1,0:T(8,128)(2,1)S(1)}, u32[]{:S(2)}, u32[]{:S(2)}) collective-permute-start(bf16[896,128]{1,0:T(8,128)(2,1)S(1)} %get-tuple-element.47), channel_id=1, source_target_pairs={{0,1},{1,0},{2,3},{3,2},{4,5},{5,4},{6,7},{7,6},{8,9},{9,8},{10,11... | collective-permute-start | bytes 688136 | tf_op jit(solution)/shard_map/ppermute | solution.py:455
  6.3 1.6 %collective-permute-start.3 = (bf16[4,32,1152]{2,1,0:T(8,128)(2,1)S(1)}, bf16[4,32,1152]{2,1,0:T(8,128)(2,1)S(1)}, u32[]{:S(2)}, u32[]{:S(2)}) collective-permute-start(bf16[4,32,1152]{2,1,0:T(8,128)(2,1)S(1)} %get-tuple-element.50), channel_id=1, source_target_pairs={{0,4},{4,0},{8,12},{12,8},{1,5},{5,1},{9,13},{13,9},{2,6},{6,2},{1... | collective-permute-start | bytes 884744 | tf_op jit(solution)/shard_map/ppermute | solution.py:455
  7.8 1.6 %collective-permute-start.1 = (bf16[896,128]{1,0:T(8,128)(2,1)S(1)}, bf16[896,128]{1,0:T(8,128)(2,1)S(1)}, u32[]{:S(2)}, u32[]{:S(2)}) collective-permute-start(bf16[896,128]{1,0:T(8,128)(2,1)S(1)} %get-tuple-element.48), channel_id=1, source_target_pairs={{0,2},{1,3},{2,0},{3,1},{4,6},{5,7},{6,4},{7,5},{8,10},{9,11},{10,... | collective-permute-start | bytes 688136 | tf_op jit(solution)/shard_map/ppermute | solution.py:455
  9.8 2.6 %collective-permute-start.7 = (bf16[4,32,1152]{2,1,0:T(8,128)(2,1)S(1)}, bf16[4,32,1152]{2,1,0:T(8,128)(2,1)S(1)}, u32[]{:S(2)}, u32[]{:S(2)}) collective-permute-start(bf16[4,32,1152]{2,1,0:T(8,128)(2,1)S(1)} %get-tuple-element.56), channel_id=1, source_target_pairs={{0,8},{4,12},{8,0},{12,4},{1,9},{5,13},{9,1},{13,5},{2,10},{6,14},... | collective-permute-start | bytes 884744 | tf_op jit(solution)/shard_map/ppermute | solution.py:455
  12.7 4.2 %collective-permute-start.8 = (bf16[4,32,1152]{2,1,0:T(8,128)(2,1)S(1)}, bf16[4,32,1152]{2,1,0:T(8,128)(2,1)S(1)}, u32[]{:S(2)}, u32[]{:S(2)}) collective-permute-start(bf16[4,32,1152]{2,1,0:T(8,128)(2,1)S(1)} %get-tuple-element.57), channel_id=1, source_target_pairs={{0,12},{4,8},{8,4},{12,0},{1,13},{5,9},{9,5},{13,1},{2,14},{6,10},... | collective-permute-start | bytes 884744 | tf_op jit(solution)/shard_map/ppermute | solution.py:455
  16.9 2.7 %collective-permute-done.1.refs_2_.refs_8_ = bf16[896,128]{1,0:T(8,128)(2,1)S(1)} collective-permute-done((bf16[896,128]{1,0:T(8,128)(2,1)S(1)}, bf16[896,128]{1,0:T(8,128)(2,1)S(1)}, u32[]{:S(2)}, u32[]{:S(2)}) %collective-permute-start.1) | collective-permute-done | bytes 229408 | tf_op jit(solution)/shard_map/ppermute | solution.py:455
  19.5 2.9 %shard_map.122 = (bf16[3,2,288,256]{3,2,1,0:T(8,128)(2,1)S(1)}, f32[2,4,256,256]{3,2,1,0:T(8,128)S(1)}, bf16[288,128]{1,0:T(8,128)(2,1)S(1)}, bf16[288,128]{1,0:...) custom-call(bf16[896,128]{1,0:T(8,128)(2,1)S(1)} %get-tuple-element.46.refs_0_.refs_6_, ...), custom_call_target="tpu_custom_call" | custom-call | tf_op jit(solution)/shard_map/pallas_call | solution.py:41
  22.5 1.6 %collective-permute-start.4 = (bf16[288,128]{1,0:T(8,128)(2,1)S(1)}, bf16[288,128]{1,0:T(8,128)(2,1)S(1)}, u32[]{:S(2)}, u32[]{:S(2)}) collective-permute-start(bf16[288,128]{1,0:T(8,128)(2,1)S(1)} %get-tuple-element.51), channel_id=1, source_target_pairs={{0,3},{1,2},{2,1},{3,0},{4,7},{5,6},{6,5},{7,4},{8,11},{9,10},{10,... | collective-permute-start | bytes 221192 | tf_op jit(solution)/shard_map/ppermute | solution.py:455
  24.5 1.5 %collective-permute-start.6 = (bf16[288,128]{1,0:T(8,128)(2,1)S(1)}, bf16[288,128]{1,0:T(8,128)(2,1)S(1)}, u32[]{:S(2)}, u32[]{:S(2)}) collective-permute-start(bf16[288,128]{1,0:T(8,128)(2,1)S(1)} %get-tuple-element.53), channel_id=1, source_target_pairs={{0,1},{1,0},{2,3},{3,2},{4,5},{5,4},{6,7},{7,6},{8,9},{9,8},{10,11... | collective-permute-start | bytes 221192 | tf_op jit(solution)/shard_map/ppermute | solution.py:455
  26.0 1.8 %collective-permute-done.4.refs_0_ = bf16[288,128]{1,0:T(8,128)(2,1)S(1)} collective-permute-done((bf16[288,128]{1,0:T(8,128)(2,1)S(1)}, bf16[288,128]{1,0:T(8,128)(2,1)S(1)}, u32[]{:S(2)}, u32[]{:S(2)}) %collective-permute-start.4) | collective-permute-done | bytes 73760 | tf_op jit(solution)/shard_map/ppermute | solution.py:455
  29.2 3.1 %collective-permute-start.9 = (f32[8,128]{1,0:T(8,128)S(1)}, f32[8,128]{1,0:T(8,128)S(1)}, u32[]{:S(2)}, u32[]{:S(2)}) collective-permute-start(f32[8,128]{1,0:T(8,128)S(1)} %get-tuple-element.58), channel_id=1, source_target_pairs={{0,12},{4,8},{8,4},{12,0},{1,13},{5,9},{9,5},{13,1},{2,14},{6,10},... | collective-permute-start | bytes 12296 | tf_op jit(solution)/shard_map/ppermute | solution.py:455
  32.4 1.3 %collective-permute-start.11 = (f32[8,128]{1,0:T(8,128)S(1)}, f32[8,128]{1,0:T(8,128)S(1)}, u32[]{:S(2)}, u32[]{:S(2)}) collective-permute-start(f32[8,128]{1,0:T(8,128)S(1)} %get-tuple-element.60), channel_id=1, source_target_pairs={{0,4},{4,0},{8,12},{12,8},{1,5},{5,1},{9,13},{13,9},{2,6},{6,2},{1... | collective-permute-start | bytes 12296 | tf_op jit(solution)/shard_map/ppermute | solution.py:455
  33.7 1.4 %shard_map.124.refs_0_ = bf16[4,1152,128]{2,1,0:T(8,128)(2,1)S(1)} custom-call(bf16[1,2,64,1152]{3,2,1,0:T(8,128)(2,1)} %refs_0_.4, bf16[1,2,64,1152]{3,2,1,0:T(8,128)(2,1)} %refs_1_.3, bf16[1,2,64,1152]{3,2,1,0:T(8,128)(2,1)} %refs_2_.3, bf16[1,2,64,1152]{3,2,1,0:T(8,128)(2,1)} %refs_0_.5, bf16[4,32,1152]{2,1,0:T(8,128)(2,1)S(1)} %collective-permute-done.3.refs_4_, ...), custom_call_target="tpu_custom_call" | custom-call | tf_op jit(solution)/shard_map/pallas_call | solution.py:41
  35.1 2.7 %collective-permute-done.10.refs_3_ = f32[8,128]{1,0:T(8,128)S(1)} collective-permute-done((f32[8,128]{1,0:T(8,128)S(1)}, f32[8,128]{1,0:T(8,128)S(1)}, u32[]{:S(2)}, u32[]{:S(2)}) %collective-permute-start.10) | collective-permute-done | bytes 4128 | tf_op jit(solution)/shard_map/ppermute | solution.py:455
  37.7 3.1 %shard_map.125 = (bf16[40,1152]{1,0:T(8,128)(2,1)S(1)}, bf16[40,1152]{1,0:T(8,128)(2,1)S(1)}, bf16[40,1152]{1,0:T(8,128)(2,1)S(1)}, bf16[40,1152]{1,0:T(8,128)(2...) custom-call(bf16[4,1152,128]{2,1,0:T(8,128)(2,1)S(1)} %shard_map.124, ...), custom_call_target="tpu_custom_call" | custom-call | tf_op jit(solution)/shard_map/pallas_call | solution.py:41
  40.8 2.5 %collective-permute-start.12 = (f32[8,128]{1,0:T(8,128)S(1)}, f32[8,128]{1,0:T(8,128)S(1)}, u32[]{:S(2)}, u32[]{:S(2)}) collective-permute-start(f32[8,128]{1,0:T(8,128)S(1)} %get-tuple-element.66), channel_id=1, source_target_pairs={{0,12},{4,8},{8,4},{12,0},{1,13},{5,9},{9,5},{13,1},{2,14},{6,10},... | collective-permute-start | bytes 12296 | tf_op jit(solution)/shard_map/ppermute | solution.py:455
  44.2 1.1 %collective-permute-start.14 = (f32[8,128]{1,0:T(8,128)S(1)}, f32[8,128]{1,0:T(8,128)S(1)}, u32[]{:S(2)}, u32[]{:S(2)}) collective-permute-start(f32[8,128]{1,0:T(8,128)S(1)} %get-tuple-element.68), channel_id=1, source_target_pairs={{0,4},{4,0},{8,12},{12,8},{1,5},{5,1},{9,13},{13,9},{2,6},{6,2},{1... | collective-permute-start | bytes 12296 | tf_op jit(solution)/shard_map/ppermute | solution.py:455
  45.2 2.0 %collective-permute-start.19 = (bf16[40,1152]{1,0:T(8,128)(2,1)S(1)}, bf16[40,1152]{1,0:T(8,128)(2,1)S(1)}, u32[]{:S(2)}, u32[]{:S(2)}) collective-permute-start(bf16[40,1152]{1,0:T(8,128)(2,1)S(1)} %get-tuple-element.78), channel_id=1, source_target_pairs={{0,8},{4,12},{8,0},{12,4},{1,9},{5,13},{9,1},{13,5},{2,10},{6,14},... | collective-permute-start | bytes 276488 | tf_op jit(solution)/shard_map/ppermute | solution.py:455
  48.3 2.6 %collective-permute-start.15 = (bf16[288,128]{1,0:T(8,128)(2,1)S(1)}, bf16[288,128]{1,0:T(8,128)(2,1)S(1)}, u32[]{:S(2)}, u32[]{:S(2)}) collective-permute-start(bf16[288,128]{1,0:T(8,128)(2,1)S(1)} %get-tuple-element.72), channel_id=1, source_target_pairs={{0,3},{1,2},{2,1},{3,0},{4,7},{5,6},{6,5},{7,4},{8,11},{9,10},{10,... | collective-permute-start | bytes 221192 | tf_op jit(solution)/shard_map/ppermute | solution.py:455
  51.8 2.5 %collective-permute-start.20 = (bf16[40,1152]{1,0:T(8,128)(2,1)S(1)}, bf16[40,1152]{1,0:T(8,128)(2,1)S(1)}, u32[]{:S(2)}, u32[]{:S(2)}) collective-permute-start(bf16[40,1152]{1,0:T(8,128)(2,1)S(1)} %get-tuple-element.79), channel_id=1, source_target_pairs={{0,12},{4,8},{8,4},{12,0},{1,13},{5,9},{9,5},{13,1},{2,14},{6,10},... | collective-permute-start | bytes 276488 | tf_op jit(solution)/shard_map/ppermute | solution.py:455
  55.6 2.6 %shard_map.127 = (bf16[32,704]{1,0:T(8,128)(2,1)S(1)}, bf16[32,704]{1,0:T(8,128)(2,1)S(1)}, bf16[32,704]{1,0:T(8,128)(2,1)S(1)}, bf16[32,704]{1,0:T(8,128)(2,1)S...) custom-call(bf16[3,2,288,256]{3,2,1,0:T(8,128)(2,1)S(1)} %get-tuple-element.63.refs_0_,, ...), custom_call_target="tpu_custom_call", output_to_operand_aliasing={{5}: (14, {})} | custom-call | tf_op jit(solution)/shard_map/pallas_call | solution.py:41
  58.3 1.6 %collective-permute-start.21 = (bf16[32,704]{1,0:T(8,128)(2,1)S(1)}, bf16[32,704]{1,0:T(8,128)(2,1)S(1)}, u32[]{:S(2)}, u32[]{:S(2)}) collective-permute-start(bf16[32,704]{1,0:T(8,128)(2,1)S(1)} %get-tuple-element.81), channel_id=1, source_target_pairs={{0,3},{1,2},{2,1},{3,0},{4,7},{5,6},{6,5},{7,4},{8,11},{9,10},{10,... | collective-permute-start | bytes 135176 | tf_op jit(solution)/shard_map/ppermute | solution.py:455
  60.3 1.5 %collective-permute-start.23 = (bf16[32,704]{1,0:T(8,128)(2,1)S(1)}, bf16[32,704]{1,0:T(8,128)(2,1)S(1)}, u32[]{:S(2)}, u32[]{:S(2)}) collective-permute-start(bf16[32,704]{1,0:T(8,128)(2,1)S(1)} %get-tuple-element.83), channel_id=1, source_target_pairs={{0,1},{1,0},{2,3},{3,2},{4,5},{5,4},{6,7},{7,6},{8,9},{9,8},{10,11... | collective-permute-start | bytes 135176 | tf_op jit(solution)/shard_map/ppermute | solution.py:455
  64.9 1.5 %collective-permute-done.18.refs_2_ = bf16[40,1152]{1,0:T(8,128)(2,1)S(1)} collective-permute-done((bf16[40,1152]{1,0:T(8,128)(2,1)S(1)}, bf16[40,1152]{1,0:T(8,128)(2,1)S(1)}, u32[]{:S(2)}, u32[]{:S(2)}) %collective-permute-start.18) | collective-permute-done | bytes 92192 | tf_op jit(solution)/shard_map/ppermute | solution.py:455
  66.4 2.8 %collective-permute-start.27 = (bf16[56,576]{1,0:T(8,128)(2,1)S(1)}, bf16[56,576]{1,0:T(8,128)(2,1)S(1)}, u32[]{:S(2)}, u32[]{:S(2)}) collective-permute-start(bf16[56,576]{1,0:T(8,128)(2,1)S(1)} %shard_map.130.refs_0_), channel_id=1, source_target_pairs={{0,12},{4,8},{8,4},{12,0},{1,13},{5,9},{9,5},{13,1},{2,14},{6,10},... | collective-permute-start | bytes 193544 | tf_op jit(solution)/shard_map/ppermute | solution.py:455
  69.2 1.6 %collective-permute-start.25 = (bf16[56,576]{1,0:T(8,128)(2,1)S(1)}, bf16[56,576]{1,0:T(8,128)(2,1)S(1)}, u32[]{:S(2)}, u32[]{:S(2)}) collective-permute-start(bf16[56,576]{1,0:T(8,128)(2,1)S(1)} %shard_map.130.refs_0_), channel_id=1, source_target_pairs={{0,4},{4,0},{8,12},{12,8},{1,5},{5,1},{9,13},{13,9},{2,6},{6,2},{1... | collective-permute-start | bytes 193544 | tf_op jit(solution)/shard_map/ppermute | solution.py:455
  70.9 2.3 %collective-permute-done.27.refs_3_ = bf16[56,576]{1,0:T(8,128)(2,1)S(1)} collective-permute-done((bf16[56,576]{1,0:T(8,128)(2,1)S(1)}, bf16[56,576]{1,0:T(8,128)(2,1)S(1)}, u32[]{:S(2)}, u32[]{:S(2)}) %collective-permute-start.27) | collective-permute-done | bytes 64544 | tf_op jit(solution)/shard_map/ppermute | solution.py:455
  73.2 2.7 %collective-permute-done.26.refs_2_ = bf16[56,576]{1,0:T(8,128)(2,1)S(1)} collective-permute-done((bf16[56,576]{1,0:T(8,128)(2,1)S(1)}, bf16[56,576]{1,0:T(8,128)(2,1)S(1)}, u32[]{:S(2)}, u32[]{:S(2)}) %collective-permute-start.26) | collective-permute-done | bytes 64544 | tf_op jit(solution)/shard_map/ppermute | solution.py:455
  75.9 2.3 %collective-permute-start.30 = (bf16[56,576]{1,0:T(8,128)(2,1)S(1)}, bf16[56,576]{1,0:T(8,128)(2,1)S(1)}, u32[]{:S(2)}, u32[]{:S(2)}) collective-permute-start(bf16[56,576]{1,0:T(8,128)(2,1)S(1)} %shard_map.131.refs_0_), channel_id=1, source_target_pairs={{0,3},{1,2},{2,1},{3,0},{4,7},{5,6},{6,5},{7,4},{8,11},{9,10},{10,... | collective-permute-start | bytes 193544 | tf_op jit(solution)/shard_map/ppermute | solution.py:455
  79.5 1.8 %collective-permute-done.30.refs_3_ = bf16[56,576]{1,0:T(8,128)(2,1)S(1)} collective-permute-done((bf16[56,576]{1,0:T(8,128)(2,1)S(1)}, bf16[56,576]{1,0:T(8,128)(2,1)S(1)}, u32[]{:S(2)}, u32[]{:S(2)}) %collective-permute-start.30) | collective-permute-done | bytes 64544 | tf_op jit(solution)/shard_map/ppermute | solution.py:455
  81.3 1.5 %collective-permute-done.29.refs_2_ = bf16[56,576]{1,0:T(8,128)(2,1)S(1)} collective-permute-done((bf16[56,576]{1,0:T(8,128)(2,1)S(1)}, bf16[56,576]{1,0:T(8,128)(2,1)S(1)}, u32[]{:S(2)}, u32[]{:S(2)}) %collective-permute-start.29) | collective-permute-done | bytes 64544 | tf_op jit(solution)/shard_map/ppermute | solution.py:455
  (53 shorter events, 14.4 us)
Async XLA Ops:
  3.3 9.4 %collective-permute-start = (bf16[896,128]{1,0:T(8,128)(2,1)S(1)}, bf16[896,128]{1,0:T(8,128)(2,1)S(1)}, u32[]{:S(2)}, u32[]{:S(2)}) collective-permute-start(bf16[896,128]{1,0:T(8,128)(2,1)S(1)} %get-tuple-element.47), channel_id=1, source_target_pairs={{0,1},{1,0},{2,3},{3,2},{4,5},{5,4},{6,7},{7,6},{8,9},{9,8},{10,11... | collective-permute-start | bytes 688136 | tf_op jit(solution)/shard_map/ppermute | solution.py:455
  6.3 13.3 %collective-permute-start.3 = (bf16[4,32,1152]{2,1,0:T(8,128)(2,1)S(1)}, bf16[4,32,1152]{2,1,0:T(8,128)(2,1)S(1)}, u32[]{:S(2)}, u32[]{:S(2)}) collective-permute-start(bf16[4,32,1152]{2,1,0:T(8,128)(2,1)S(1)} %get-tuple-element.50), channel_id=1, source_target_pairs={{0,4},{4,0},{8,12},{12,8},{1,5},{5,1},{9,13},{13,9},{2,6},{6,2},{1... | collective-permute-start | bytes 884744 | tf_op jit(solution)/shard_map/ppermute | solution.py:455
  7.8 11.7 %collective-permute-start.1 = (bf16[896,128]{1,0:T(8,128)(2,1)S(1)}, bf16[896,128]{1,0:T(8,128)(2,1)S(1)}, u32[]{:S(2)}, u32[]{:S(2)}) collective-permute-start(bf16[896,128]{1,0:T(8,128)(2,1)S(1)} %get-tuple-element.48), channel_id=1, source_target_pairs={{0,2},{1,3},{2,0},{3,1},{4,6},{5,7},{6,4},{7,5},{8,10},{9,11},{10,... | collective-permute-start | bytes 688136 | tf_op jit(solution)/shard_map/ppermute | solution.py:455
  9.4 10.1 %collective-permute-start.2 = (bf16[896,128]{1,0:T(8,128)(2,1)S(1)}, bf16[896,128]{1,0:T(8,128)(2,1)S(1)}, u32[]{:S(2)}, u32[]{:S(2)}) collective-permute-start(bf16[896,128]{1,0:T(8,128)(2,1)S(1)} %get-tuple-element.49), channel_id=1, source_target_pairs={{0,3},{1,2},{2,1},{3,0},{4,7},{5,6},{6,5},{7,4},{8,11},{9,10},{10,... | collective-permute-start | bytes 688136 | tf_op jit(solution)/shard_map/ppermute | solution.py:455
  9.8 23.9 %collective-permute-start.7 = (bf16[4,32,1152]{2,1,0:T(8,128)(2,1)S(1)}, bf16[4,32,1152]{2,1,0:T(8,128)(2,1)S(1)}, u32[]{:S(2)}, u32[]{:S(2)}) collective-permute-start(bf16[4,32,1152]{2,1,0:T(8,128)(2,1)S(1)} %get-tuple-element.56), channel_id=1, source_target_pairs={{0,8},{4,12},{8,0},{12,4},{1,9},{5,13},{9,1},{13,5},{2,10},{6,14},... | collective-permute-start | bytes 884744 | tf_op jit(solution)/shard_map/ppermute | solution.py:455
  12.7 21.0 %collective-permute-start.8 = (bf16[4,32,1152]{2,1,0:T(8,128)(2,1)S(1)}, bf16[4,32,1152]{2,1,0:T(8,128)(2,1)S(1)}, u32[]{:S(2)}, u32[]{:S(2)}) collective-permute-start(bf16[4,32,1152]{2,1,0:T(8,128)(2,1)S(1)} %get-tuple-element.57), channel_id=1, source_target_pairs={{0,12},{4,8},{8,4},{12,0},{1,13},{5,9},{9,5},{13,1},{2,14},{6,10},... | collective-permute-start | bytes 884744 | tf_op jit(solution)/shard_map/ppermute | solution.py:455
  22.5 5.3 %collective-permute-start.4 = (bf16[288,128]{1,0:T(8,128)(2,1)S(1)}, bf16[288,128]{1,0:T(8,128)(2,1)S(1)}, u32[]{:S(2)}, u32[]{:S(2)}) collective-permute-start(bf16[288,128]{1,0:T(8,128)(2,1)S(1)} %get-tuple-element.51), channel_id=1, source_target_pairs={{0,3},{1,2},{2,1},{3,0},{4,7},{5,6},{6,5},{7,4},{8,11},{9,10},{10,... | collective-permute-start | bytes 221192 | tf_op jit(solution)/shard_map/ppermute | solution.py:455
  24.0 4.5 %collective-permute-start.5 = (bf16[288,128]{1,0:T(8,128)(2,1)S(1)}, bf16[288,128]{1,0:T(8,128)(2,1)S(1)}, u32[]{:S(2)}, u32[]{:S(2)}) collective-permute-start(bf16[288,128]{1,0:T(8,128)(2,1)S(1)} %get-tuple-element.52), channel_id=1, source_target_pairs={{0,2},{1,3},{2,0},{3,1},{4,6},{5,7},{6,4},{7,5},{8,10},{9,11},{10,... | collective-permute-start | bytes 221192 | tf_op jit(solution)/shard_map/ppermute | solution.py:455
  24.5 4.4 %collective-permute-start.6 = (bf16[288,128]{1,0:T(8,128)(2,1)S(1)}, bf16[288,128]{1,0:T(8,128)(2,1)S(1)}, u32[]{:S(2)}, u32[]{:S(2)}) collective-permute-start(bf16[288,128]{1,0:T(8,128)(2,1)S(1)} %get-tuple-element.53), channel_id=1, source_target_pairs={{0,1},{1,0},{2,3},{3,2},{4,5},{5,4},{6,7},{7,6},{8,9},{9,8},{10,11... | collective-permute-start | bytes 221192 | tf_op jit(solution)/shard_map/ppermute | solution.py:455
  29.2 5.8 %collective-permute-start.9 = (f32[8,128]{1,0:T(8,128)S(1)}, f32[8,128]{1,0:T(8,128)S(1)}, u32[]{:S(2)}, u32[]{:S(2)}) collective-permute-start(f32[8,128]{1,0:T(8,128)S(1)} %get-tuple-element.58), channel_id=1, source_target_pairs={{0,12},{4,8},{8,4},{12,0},{1,13},{5,9},{9,5},{13,1},{2,14},{6,10},... | collective-permute-start | bytes 12296 | tf_op jit(solution)/shard_map/ppermute | solution.py:455
  32.4 5.4 %collective-permute-start.10 = (f32[8,128]{1,0:T(8,128)S(1)}, f32[8,128]{1,0:T(8,128)S(1)}, u32[]{:S(2)}, u32[]{:S(2)}) collective-permute-start(f32[8,128]{1,0:T(8,128)S(1)} %get-tuple-element.59), channel_id=1, source_target_pairs={{0,8},{4,12},{8,0},{12,4},{1,9},{5,13},{9,1},{13,5},{2,10},{6,14},... | collective-permute-start | bytes 12296 | tf_op jit(solution)/shard_map/ppermute | solution.py:455
  32.4 5.4 %collective-permute-start.11 = (f32[8,128]{1,0:T(8,128)S(1)}, f32[8,128]{1,0:T(8,128)S(1)}, u32[]{:S(2)}, u32[]{:S(2)}) collective-permute-start(f32[8,128]{1,0:T(8,128)S(1)} %get-tuple-element.60), channel_id=1, source_target_pairs={{0,4},{4,0},{8,12},{12,8},{1,5},{5,1},{9,13},{13,9},{2,6},{6,2},{1... | collective-permute-start | bytes 12296 | tf_op jit(solution)/shard_map/ppermute | solution.py:455
  40.8 6.4 %collective-permute-start.12 = (f32[8,128]{1,0:T(8,128)S(1)}, f32[8,128]{1,0:T(8,128)S(1)}, u32[]{:S(2)}, u32[]{:S(2)}) collective-permute-start(f32[8,128]{1,0:T(8,128)S(1)} %get-tuple-element.66), channel_id=1, source_target_pairs={{0,12},{4,8},{8,4},{12,0},{1,13},{5,9},{9,5},{13,1},{2,14},{6,10},... | collective-permute-start | bytes 12296 | tf_op jit(solution)/shard_map/ppermute | solution.py:455
  43.3 4.5 %collective-permute-start.13 = (f32[8,128]{1,0:T(8,128)S(1)}, f32[8,128]{1,0:T(8,128)S(1)}, u32[]{:S(2)}, u32[]{:S(2)}) collective-permute-start(f32[8,128]{1,0:T(8,128)S(1)} %get-tuple-element.67), channel_id=1, source_target_pairs={{0,8},{4,12},{8,0},{12,4},{1,9},{5,13},{9,1},{13,5},{2,10},{6,14},... | collective-permute-start | bytes 12296 | tf_op jit(solution)/shard_map/ppermute | solution.py:455
  44.2 3.7 %collective-permute-start.14 = (f32[8,128]{1,0:T(8,128)S(1)}, f32[8,128]{1,0:T(8,128)S(1)}, u32[]{:S(2)}, u32[]{:S(2)}) collective-permute-start(f32[8,128]{1,0:T(8,128)S(1)} %get-tuple-element.68), channel_id=1, source_target_pairs={{0,4},{4,0},{8,12},{12,8},{1,5},{5,1},{9,13},{13,9},{2,6},{6,2},{1... | collective-permute-start | bytes 12296 | tf_op jit(solution)/shard_map/ppermute | solution.py:455
  45.2 16.6 %collective-permute-start.19 = (bf16[40,1152]{1,0:T(8,128)(2,1)S(1)}, bf16[40,1152]{1,0:T(8,128)(2,1)S(1)}, u32[]{:S(2)}, u32[]{:S(2)}) collective-permute-start(bf16[40,1152]{1,0:T(8,128)(2,1)S(1)} %get-tuple-element.78), channel_id=1, source_target_pairs={{0,8},{4,12},{8,0},{12,4},{1,9},{5,13},{9,1},{13,5},{2,10},{6,14},... | collective-permute-start | bytes 276488 | tf_op jit(solution)/shard_map/ppermute | solution.py:455
  48.3 6.0 %collective-permute-start.15 = (bf16[288,128]{1,0:T(8,128)(2,1)S(1)}, bf16[288,128]{1,0:T(8,128)(2,1)S(1)}, u32[]{:S(2)}, u32[]{:S(2)}) collective-permute-start(bf16[288,128]{1,0:T(8,128)(2,1)S(1)} %get-tuple-element.72), channel_id=1, source_target_pairs={{0,3},{1,2},{2,1},{3,0},{4,7},{5,6},{6,5},{7,4},{8,11},{9,10},{10,... | collective-permute-start | bytes 221192 | tf_op jit(solution)/shard_map/ppermute | solution.py:455
  50.9 4.4 %collective-permute-start.16 = (bf16[288,128]{1,0:T(8,128)(2,1)S(1)}, bf16[288,128]{1,0:T(8,128)(2,1)S(1)}, u32[]{:S(2)}, u32[]{:S(2)}) collective-permute-start(bf16[288,128]{1,0:T(8,128)(2,1)S(1)} %get-tuple-element.73), channel_id=1, source_target_pairs={{0,2},{1,3},{2,0},{3,1},{4,6},{5,7},{6,4},{7,5},{8,10},{9,11},{10,... | collective-permute-start | bytes 221192 | tf_op jit(solution)/shard_map/ppermute | solution.py:455
  51.3 4.4 %collective-permute-start.17 = (bf16[288,128]{1,0:T(8,128)(2,1)S(1)}, bf16[288,128]{1,0:T(8,128)(2,1)S(1)}, u32[]{:S(2)}, u32[]{:S(2)}) collective-permute-start(bf16[288,128]{1,0:T(8,128)(2,1)S(1)} %get-tuple-element.74), channel_id=1, source_target_pairs={{0,1},{1,0},{2,3},{3,2},{4,5},{5,4},{6,7},{7,6},{8,9},{9,8},{10,11... | collective-permute-start | bytes 221192 | tf_op jit(solution)/shard_map/ppermute | solution.py:455
  51.8 11.0 %collective-permute-start.20 = (bf16[40,1152]{1,0:T(8,128)(2,1)S(1)}, bf16[40,1152]{1,0:T(8,128)(2,1)S(1)}, u32[]{:S(2)}, u32[]{:S(2)}) collective-permute-start(bf16[40,1152]{1,0:T(8,128)(2,1)S(1)} %get-tuple-element.79), channel_id=1, source_target_pairs={{0,12},{4,8},{8,4},{12,0},{1,13},{5,9},{9,5},{13,1},{2,14},{6,10},... | collective-permute-start | bytes 276488 | tf_op jit(solution)/shard_map/ppermute | solution.py:455
  58.3 5.1 %collective-permute-start.21 = (bf16[32,704]{1,0:T(8,128)(2,1)S(1)}, bf16[32,704]{1,0:T(8,128)(2,1)S(1)}, u32[]{:S(2)}, u32[]{:S(2)}) collective-permute-start(bf16[32,704]{1,0:T(8,128)(2,1)S(1)} %get-tuple-element.81), channel_id=1, source_target_pairs={{0,3},{1,2},{2,1},{3,0},{4,7},{5,6},{6,5},{7,4},{8,11},{9,10},{10,... | collective-permute-start | bytes 135176 | tf_op jit(solution)/shard_map/ppermute | solution.py:455
  59.9 4.1 %collective-permute-start.22 = (bf16[32,704]{1,0:T(8,128)(2,1)S(1)}, bf16[32,704]{1,0:T(8,128)(2,1)S(1)}, u32[]{:S(2)}, u32[]{:S(2)}) collective-permute-start(bf16[32,704]{1,0:T(8,128)(2,1)S(1)} %get-tuple-element.82), channel_id=1, source_target_pairs={{0,2},{1,3},{2,0},{3,1},{4,6},{5,7},{6,4},{7,5},{8,10},{9,11},{10,... | collective-permute-start | bytes 135176 | tf_op jit(solution)/shard_map/ppermute | solution.py:455
  60.3 4.1 %collective-permute-start.23 = (bf16[32,704]{1,0:T(8,128)(2,1)S(1)}, bf16[32,704]{1,0:T(8,128)(2,1)S(1)}, u32[]{:S(2)}, u32[]{:S(2)}) collective-permute-start(bf16[32,704]{1,0:T(8,128)(2,1)S(1)} %get-tuple-element.83), channel_id=1, source_target_pairs={{0,1},{1,0},{2,3},{3,2},{4,5},{5,4},{6,7},{7,6},{8,9},{9,8},{10,11... | collective-permute-start | bytes 135176 | tf_op jit(solution)/shard_map/ppermute | solution.py:455
  61.8 4.6 %collective-permute-start.18 = (bf16[40,1152]{1,0:T(8,128)(2,1)S(1)}, bf16[40,1152]{1,0:T(8,128)(2,1)S(1)}, u32[]{:S(2)}, u32[]{:S(2)}) collective-permute-start(bf16[40,1152]{1,0:T(8,128)(2,1)S(1)} %get-tuple-element.77), channel_id=1, source_target_pairs={{0,4},{4,0},{8,12},{12,8},{1,5},{5,1},{9,13},{13,9},{2,6},{6,2},{1... | collective-permute-start | bytes 276488 | tf_op jit(solution)/shard_map/ppermute | solution.py:455
  64.8 1.6 %collective-permute-start.24 = (bf16[56,576]{1,0:T(8,128)(2,1)S(1)}, bf16[56,576]{1,0:T(8,128)(2,1)S(1)}, u32[]{:S(2)}, u32[]{:S(2)}) collective-permute-start(bf16[56,576]{1,0:T(8,128)(2,1)S(1)} %get-tuple-element.86), channel_id=1, source_target_pairs={{0,16},{16,0},{1,17},{17,1},{2,18},{18,2},{3,19},{19,3},{4,20},{20... | collective-permute-start | bytes 193544 | tf_op jit(solution)/shard_map/ppermute | solution.py:455
  66.4 6.8 %collective-permute-start.27 = (bf16[56,576]{1,0:T(8,128)(2,1)S(1)}, bf16[56,576]{1,0:T(8,128)(2,1)S(1)}, u32[]{:S(2)}, u32[]{:S(2)}) collective-permute-start(bf16[56,576]{1,0:T(8,128)(2,1)S(1)} %shard_map.130.refs_0_), channel_id=1, source_target_pairs={{0,12},{4,8},{8,4},{12,0},{1,13},{5,9},{9,5},{13,1},{2,14},{6,10},... | collective-permute-start | bytes 193544 | tf_op jit(solution)/shard_map/ppermute | solution.py:455
  69.2 6.6 %collective-permute-start.26 = (bf16[56,576]{1,0:T(8,128)(2,1)S(1)}, bf16[56,576]{1,0:T(8,128)(2,1)S(1)}, u32[]{:S(2)}, u32[]{:S(2)}) collective-permute-start(bf16[56,576]{1,0:T(8,128)(2,1)S(1)} %shard_map.130.refs_0_), channel_id=1, source_target_pairs={{0,8},{4,12},{8,0},{12,4},{1,9},{5,13},{9,1},{13,5},{2,10},{6,14},... | collective-permute-start | bytes 193544 | tf_op jit(solution)/shard_map/ppermute | solution.py:455
  69.2 6.6 %collective-permute-start.25 = (bf16[56,576]{1,0:T(8,128)(2,1)S(1)}, bf16[56,576]{1,0:T(8,128)(2,1)S(1)}, u32[]{:S(2)}, u32[]{:S(2)}) collective-permute-start(bf16[56,576]{1,0:T(8,128)(2,1)S(1)} %shard_map.130.refs_0_), channel_id=1, source_target_pairs={{0,4},{4,0},{8,12},{12,8},{1,5},{5,1},{9,13},{13,9},{2,6},{6,2},{1... | collective-permute-start | bytes 193544 | tf_op jit(solution)/shard_map/ppermute | solution.py:455
  75.9 5.4 %collective-permute-start.30 = (bf16[56,576]{1,0:T(8,128)(2,1)S(1)}, bf16[56,576]{1,0:T(8,128)(2,1)S(1)}, u32[]{:S(2)}, u32[]{:S(2)}) collective-permute-start(bf16[56,576]{1,0:T(8,128)(2,1)S(1)} %shard_map.131.refs_0_), channel_id=1, source_target_pairs={{0,3},{1,2},{2,1},{3,0},{4,7},{5,6},{6,5},{7,4},{8,11},{9,10},{10,... | collective-permute-start | bytes 193544 | tf_op jit(solution)/shard_map/ppermute | solution.py:455
  78.2 4.5 %collective-permute-start.29 = (bf16[56,576]{1,0:T(8,128)(2,1)S(1)}, bf16[56,576]{1,0:T(8,128)(2,1)S(1)}, u32[]{:S(2)}, u32[]{:S(2)}) collective-permute-start(bf16[56,576]{1,0:T(8,128)(2,1)S(1)} %shard_map.131.refs_0_), channel_id=1, source_target_pairs={{0,2},{1,3},{2,0},{3,1},{4,6},{5,7},{6,4},{7,5},{8,10},{9,11},{10,... | collective-permute-start | bytes 193544 | tf_op jit(solution)/shard_map/ppermute | solution.py:455
  78.6 4.3 %collective-permute-start.28 = (bf16[56,576]{1,0:T(8,128)(2,1)S(1)}, bf16[56,576]{1,0:T(8,128)(2,1)S(1)}, u32[]{:S(2)}, u32[]{:S(2)}) collective-permute-start(bf16[56,576]{1,0:T(8,128)(2,1)S(1)} %shard_map.131.refs_0_), channel_id=1, source_target_pairs={{0,1},{1,0},{2,3},{3,2},{4,5},{5,4},{6,7},{7,6},{8,9},{9,8},{10,11... | collective-permute-start | bytes 193544 | tf_op jit(solution)/shard_map/ppermute | solution.py:455
  83.2 1.4 %collective-permute-start.31 = (bf16[64,1152]{1,0:T(8,128)(2,1)S(1)}, bf16[64,1152]{1,0:T(8,128)(2,1)S(1)}, u32[]{:S(2)}, u32[]{:S(2)}) collective-permute-start(bf16[64,1152]{1,0:T(8,128)(2,1)S(1)} %shard_map.132.refs_0_), channel_id=1, source_target_pairs={{0,16},{16,0},{1,17},{17,1},{2,18},{18,2},{3,19},{19,3},{4,20},{20... | collective-permute-start | bytes 442376 | tf_op jit(solution)/shard_map/ppermute | solution.py:455
  (4 other events, 87.3 us)
